TPU v7x, 32 devices: a whole 2x2x4 slice. The times are simulated.
32 devices in a mesh: parts: 2 (over y), dp: 2 (over core), tensor: 8 (over z, x).
Axes of the slice: x: 2, y: 2, z: 4, core: 2. Of those that a mesh axis runs over, the one named last changes fastest.
Arguments:
- tokens: bfloat16 [4096, 5120], P(('parts', 'dp', 'tensor')), parts along dimension 0, may hold values from -6 to 6
- cotangent: bfloat16 [4096, 1024], P(('parts', 'dp', 'tensor')), parts along dimension 0, may hold values from -0.119628906 to 0.119628906
- frozen_value: bfloat16 [5120, 1024], P('tensor', 'dp'), may hold values from -0.078125 to 0.078125
- down_store: bfloat16 [512, 327680], P('parts', 'tensor'), parts along dimension 0, may hold values from -0.078125 to 0.078125
- up_store: bfloat16 [512, 65536], P('parts', 'tensor'), parts along dimension 0, may hold values from -0.75 to 0.75
- block_adapter: int32 [32], P(('parts', 'dp', 'tensor')), parts along dimension 0, may hold values from 0 to 255
- adapter_slot: int32 [512], P('parts'), parts along dimension 0, may hold values from 0 to 255, each once
Outputs:
- mixed: bfloat16 [4096, 1024], P(('parts', 'dp', 'tensor')), parts along dimension 0
- grad_down: float32 [512, 327680], P(('parts', 'dp'), 'tensor'), parts along dimension 0
- grad_up: float32 [512, 65536], P(('parts', 'dp'), 'tensor'), parts along dimension 0
There are 2 independent parts, one for each index of `parts`. A program takes and returns all parts, laid end to end along the dimension named above; an argument that names none is the same for every part. Nothing has to cross between parts.
Inputs may be any that keep to these rules, and one draw needn't show every extreme that they name: `adapter_slot`: each store row holds exactly one adapter.
All inputs are finite; a program needn't handle non-finite values.
Results may differ from a plain program's by a relative error of at most 0.0046.
Values may be sent and summed in bfloat16 or wider, within the bound.
No kernel may reach another device: no remote copies, remote signals or barrier semaphores. Data moves between devices by JAX's collectives and lax.ppermute only.
A program may use at most 256 MiB of HBM per device.

v0:
```python
import jax
import jax.numpy as jnp
from jax import lax
from jax.sharding import PartitionSpec as P

D = 5120
VALUE_OUTPUTS = 1024
R = 64
ADAPTERS = 256


adapter_scale = 2.0


def fold_rows(left, piece):
    return jnp.dot(left, piece, preferred_element_type=jnp.float32)


def store_rows(requests, adapter_slot):
    table = jnp.arange(adapter_slot.shape[0], dtype=jnp.int32)
    return jnp.sum(jnp.where(requests[:, None] == table[None, :], adapter_slot[None, :], 0), axis=1)


def body(tokens, cotangent, frozen_value, down_store, up_store, block_adapter, adapter_slot):
    token_rows = tokens.shape[0]
    blocks_here = block_adapter.shape[0]
    block_rows = token_rows // blocks_here
    group = lax.axis_size("tensor")
    columns = lax.all_gather(frozen_value, "dp", axis=1, tiled=True)
    frozen_output = fold_rows(tokens, lax.all_gather(columns, "tensor", axis=0, tiled=True))
    requests = lax.all_gather(block_adapter, "tensor", axis=0, tiled=True)
    stored = store_rows(requests, adapter_slot)
    order = stored.reshape(group, blocks_here).T.reshape(-1)
    down_send = jnp.take(down_store, order, axis=0).reshape(blocks_here, group, -1)
    up_send = jnp.take(up_store, order, axis=0).reshape(blocks_here, group, -1)
    down_got, up_got = (
        lax.all_to_all(down_send, "tensor", split_axis=1, concat_axis=1, tiled=True),
        lax.all_to_all(up_send, "tensor", split_axis=1, concat_axis=1, tiled=True),
    )
    down_panel = down_got.reshape(blocks_here, D, R)
    up_panel = up_got.reshape(blocks_here, R, VALUE_OUTPUTS)
    token_blocks = tokens.reshape(blocks_here, block_rows, D)
    grad_blocks = cotangent.reshape(blocks_here, block_rows, VALUE_OUTPUTS)
    down_projected = jnp.einsum(
        "jtd,jdr->jtr", token_blocks, down_panel, preferred_element_type=jnp.float32
    ).astype(jnp.bfloat16)
    up_projected = jnp.einsum(
        "jtr,jrk->jtk", down_projected, up_panel, preferred_element_type=jnp.float32
    )
    mixed = (
        frozen_output + adapter_scale * up_projected.reshape(token_rows, VALUE_OUTPUTS)
    ).astype(jnp.bfloat16)
    down_projected_gradient = (
        adapter_scale
        * jnp.einsum("jtk,jrk->jtr", grad_blocks, up_panel, preferred_element_type=jnp.float32)
    ).astype(jnp.bfloat16)
    down_term = jnp.einsum(
        "jtd,jtr->jdr", token_blocks, down_projected_gradient, preferred_element_type=jnp.float32
    )
    up_weight_gradient = adapter_scale * jnp.einsum(
        "jtr,jtk->jrk", down_projected, grad_blocks, preferred_element_type=jnp.float32
    )
    down_back, up_back = (
        lax.all_to_all(
            down_term.reshape(blocks_here, group, -1),
            "tensor",
            split_axis=1,
            concat_axis=1,
            tiled=True,
        ),
        lax.all_to_all(
            up_weight_gradient.reshape(blocks_here, group, -1),
            "tensor",
            split_axis=1,
            concat_axis=1,
            tiled=True,
        ),
    )
    down_flat = down_back.reshape(blocks_here * group, -1)
    up_flat = up_back.reshape(blocks_here * group, -1)
    down_table = jax.ops.segment_sum(down_flat, order, num_segments=ADAPTERS)
    up_table = jax.ops.segment_sum(up_flat, order, num_segments=ADAPTERS)
    grad_down, grad_up = (
        lax.psum_scatter(down_table, "dp", scatter_dimension=0, tiled=True),
        lax.psum_scatter(up_table, "dp", scatter_dimension=0, tiled=True),
    )
    return (mixed, grad_down, grad_up)


def solution(mesh):
    placed = (
        P(("parts", "dp", "tensor"), None),
        P(("parts", "dp", "tensor"), None),
        P("tensor", "dp"),
        P("parts", "tensor"),
        P("parts", "tensor"),
        P(("parts", "dp", "tensor")),
        P("parts"),
    )
    return jax.shard_map(
        body,
        mesh=mesh,
        in_specs=placed,
        out_specs=(
            P(("parts", "dp", "tensor"), None),
            P(("parts", "dp"), "tensor"),
            P(("parts", "dp"), "tensor"),
        ),
        check_vma=False,
    )
```

profile of v0, /device:TPU:0, one launch (start us, length us, event | category | flops | bytes accessed | tf_op | source)
XLA Modules:
  0.0 306.9 jit_solution(8069221660928475528)
XLA Ops:
  7.2 0.0 copy-start
  7.2 0.0 copy-start.3
  7.2 0.0 copy-start.2
  7.2 0.0 all-gather.3.cloned.1.call-start
  7.2 0.7 all-gather.3.cloned.1.call-update
  7.9 0.0 all-gather.5.cloned.1.call-start
  8.0 13.8 %all-gather.3.cloned.1.call-done = bf16[640,1024]{1,0:T(8,128)(2,1)} async-done(((bf16[640,512]{1,0:T(8,128)(2,1)}), bf16[640,1024]{1,0:T(8,128)(2,1)}) %all-gather.3.cloned.1.call-update) | async-done | bytes 1310736 | tf_op jit(solution)/shard_map/all_gather | solution.py:29
  21.7 0.0 all-gather.5.cloned.1.call-update
  21.8 0.0 reduce-scatter.6.cloned.1.call-start
  22.5 0.0 copy-done.3
  22.5 0.6 dynamic-slice
  23.0 0.8 dynamic-update-slice
  23.8 11.6 %all-reduce = s32[8]{0:T(128)S(1)} all-reduce(s32[8]{0:T(128)S(1)} %dynamic-update-slice), channel_id=1, replica_groups=mesh['parts'=2,'dp'=2,'tensor'=8] {'tensor'}, use_global_device_ids=true, to_apply=%add | all-reduce | flops 8 | bytes 64
  35.4 0.0 copy-done.2
  35.4 0.2 select_reduce_fusion
  35.6 11.2 %gather_fusion = bf16[8,40960]{1,0:T(8,128)(2,1)S(1)} fusion(bf16[256,40960]{1,0:T(8,128)(2,1)} %param.10, s32[1024]{0:T(1024)S(1)} %pad_clamp_fusion), kind=kCustom, calls=%fused_computation | custom fusion | bytes 1310752 | tf_op jit(solution)/shard_map/jit(_take)/gather | solution.py:34
  46.9 0.1 bitcast_select_fusion
  47.0 1.0 copy.36
  48.0 0.5 broadcast.100
  48.5 4.6 %reduce.4 = bf16[8,40960]{1,0:T(8,128)(2,1)S(1)} reduce(bf16[8,1,40960]{2,1,0:T(2,128)(2,1)S(1)} %bitcast.40, bf16[]{:T(256)} %broadcast.100), dimensions={1}, to_apply=%bitcast.37.reduce_sub_computation | reduce | bytes 1310722
  53.2 0.5 reshape.179
  53.7 37.9 %all_to_all.20 = bf16[8,2,20480]{2,1,0:T(2,128)(2,1)S(1)} all-to-all(bf16[8,2,20480]{2,1,0:T(2,128)(2,1)S(1)} %reshape.179), channel_id=1, replica_groups=mesh['parts'=2,'dp'=2,'tensor'=8] {'tensor'}, dimensions={0} | all-to-all | bytes 1310720 | tf_op jit(solution)/shard_map/all_to_all | solution.py:37
  91.5 0.6 reshape.180
  92.2 3.7 %bitcast_reduce_fusion = bf16[8,40960]{1,0:T(8,128)(2,1)S(1)} fusion(bf16[8,1,40960]{2,1,0:T(2,128)(2,1)S(1)} %reshape.180), kind=kLoop, calls=%fused_computation.28 | loop fusion | bytes 1310720 | tf_op jit(solution)/shard_map/all_to_all | solution.py:37
  95.9 1.4 reshape.127
  97.3 0.0 copy-done
  97.3 0.0 copy-start.1
  97.3 0.6 convolution_convert_fusion
  98.0 0.3 copy-done.1
  98.3 0.2 convolution_multiply_fusion.1
  98.5 0.3 reshape.173
  98.8 20.0 %all_to_all.21 = f32[1,8,8192]{2,0,1:T(1,128)S(1)} all-to-all(f32[1,8,8192]{2,0,1:T(1,128)S(1)} %reshape.173), channel_id=1, replica_groups=mesh['parts'=2,'dp'=2,'tensor'=8] {'tensor'}, dimensions={1} | all-to-all | bytes 524288 | tf_op jit(solution)/shard_map/all_to_all | solution.py:71
  118.8 4.9 %scatter_custom_fusion.1 = f32[256,8192]{1,0:T(8,128)} fusion(s32[8]{0:T(128)S(1)} %select_reduce_fusion, f32[]{:T(128)} %constant.23.clone.1, f32[1,8,8192]{2,0,1:T(1,128)S(1)} %all_to_all.21), kind=kCustom, calls=%fused_computation.5 | custom fusion | flops 65536 | bytes 8650756 | tf_op jit(solution)/shard_map/scatter-add | solution.py:82
  123.7 0.0 reduce-scatter.6.cloned.1.call-update
  123.7 0.0 reduce-scatter.8.cloned.1.call-start
  123.8 3.5 %gather_fusion.1 = bf16[8,8192]{1,0:T(8,128)(2,1)S(1)} fusion(bf16[256,8192]{1,0:T(8,128)(2,1)} %param.11, s32[1024]{0:T(1024)S(1)} %pad_clamp_fusion), kind=kCustom, calls=%fused_computation.1 | custom fusion | bytes 262176 | tf_op jit(solution)/shard_map/jit(_take)/gather | solution.py:35
  127.2 0.1 bitcast_select_fusion.1
  127.3 0.2 copy.37
  127.5 1.4 reduce.5
  129.0 0.1 reshape.181
  129.0 14.1 %all_to_all.22 = bf16[8,2,4096]{2,1,0:T(2,128)(2,1)S(1)} all-to-all(bf16[8,2,4096]{2,1,0:T(2,128)(2,1)S(1)} %reshape.181), channel_id=1, replica_groups=mesh['parts'=2,'dp'=2,'tensor'=8] {'tensor'}, dimensions={0} | all-to-all | bytes 262144 | tf_op jit(solution)/shard_map/all_to_all | solution.py:38
  143.1 0.1 reshape.182
  143.2 0.7 bitcast_reduce_fusion.1
  144.0 0.1 reshape.128
  144.0 0.6 convolution_bitcast_fusion
  144.7 2.0 copy.23
  146.7 3.4 %reshape.172 = f32[1,8,40960]{2,0,1:T(1,128)S(1)} reshape(f32[5120,64]{1,0:T(8,128)} %copy.23) | data formatting | bytes 2621440 | tf_op jit(solution)/shard_map/reshape | solution.py:65
  150.1 66.6 %all_to_all.23 = f32[1,8,40960]{2,0,1:T(1,128)S(1)} all-to-all(f32[1,8,40960]{2,0,1:T(1,128)S(1)} %reshape.172), channel_id=1, replica_groups=mesh['parts'=2,'dp'=2,'tensor'=8] {'tensor'}, dimensions={1} | all-to-all | bytes 2621440 | tf_op jit(solution)/shard_map/all_to_all | solution.py:64
  216.7 0.8 copy.35
  217.5 13.8 %broadcast_in_dim.47 = f32[256,40960]{1,0:T(8,128)} broadcast(f32[]{:T(128)} %constant.23.clone.1), dimensions={} | broadcast | bytes 41943044 | tf_op jit(solution)/shard_map/broadcast_in_dim | solution.py:81
  231.3 15.5 %scatter_fusion = f32[256,40960]{1,0:T(8,128)} fusion(f32[256,40960]{1,0:T(8,128)} %broadcast_in_dim.47, s32[8]{0:T(128)S(1)} %select_reduce_fusion, f32[8,40960]{1,0:T(8,128)S(1)} %bitcast.39), kind=kCustom, calls=%fused_computation.2 | custom fusion | flops 327680 | bytes 3932192 | tf_op jit(solution)/shard_map/scatter-add | solution.py:81
  246.8 0.0 reduce-scatter.8.cloned.1.call-update
  246.8 0.0 all-gather.5.cloned.1.call-done
  246.8 5.5 %fusion.10 = f32[128,1024]{1,0:T(8,128)S(1)} fusion(bf16[128,5120]{1,0:T(8,128)(2,1)S(1)} %copy-done, bf16[5120,1024]{1,0:T(8,128)(2,1)} %all-gather.5.cloned.1.call-done), kind=kOutput, calls=%fused_computation.32 | convolution fusion | flops 1342177280 | bytes 12320768 | tf_op jit(solution)/shard_map/dot_general | solution.py:16
  252.3 1.0 fusion.3
  253.3 0.0 reduce-scatter.6.cloned.1.call-done
  253.3 47.1 %reduce-scatter.8.cloned.1.call-done = f32[128,40960]{1,0:T(8,128)} async-done(((f32[256,40960]{1,0:T(8,128)}), f32[128,40960]{1,0:T(8,128)}) %reduce-scatter.8.cloned.1.call-update) | async-done | bytes 20971536
  (4 shorter events, 0.0 us)
Async XLA Ops:
  7.2 90.2 %copy-start = (bf16[128,5120]{1,0:T(8,128)(2,1)S(1)}, bf16[128,5120]{1,0:T(8,128)(2,1)}, u32[]{:S(2)}) copy-start(bf16[128,5120]{1,0:T(8,128)(2,1)} %param.7) | copy-start | bytes 3932164
  7.2 15.3 %copy-start.3 = (u32[32]{0:T(128)S(1)}, u32[32]{0:T(128)}, u32[]{:S(2)}) copy-start(u32[32]{0:T(128)} %constant.39) | copy-start | bytes 388
  7.2 28.2 %copy-start.2 = (s32[256]{0:T(256)S(1)}, s32[256]{0:T(256)}, u32[]{:S(2)}) copy-start(s32[256]{0:T(256)} %param.13) | copy-start | bytes 3076
  7.2 14.5 %all-gather.3.cloned.1.call-start = ((), (), s32[]{:S(2)}) async-start(), calls=%async_computation.6 | async-start | bytes 1966080 | tf_op jit(solution)/shard_map/all_gather | solution.py:29
  7.9 238.9 %all-gather.5.cloned.1.call-start = ((), (), s32[]{:S(2)}) async-start(), calls=%async_computation.7 | async-start | bytes 11796480 | tf_op jit(solution)/shard_map/all_gather | solution.py:30
  21.8 231.5 %reduce-scatter.6.cloned.1.call-start = ((), (), s32[]{:S(2)}) async-start(), calls=%async_computation.8 | async-start | bytes 12582912 | tf_op jit(solution)/shard_map/reduce_scatter | solution.py:85
  97.3 1.0 copy-start.1
  123.7 176.7 %reduce-scatter.8.cloned.1.call-start = ((), (), s32[]{:S(2)}) async-start(), calls=%async_computation.9 | async-start | bytes 62914560
Sparse Core Ops, SparseCore 0:
  9.6 12.1 all-gather.2
  23.9 199.6 all-gather.4
  226.4 15.8 reduce-scatter.5
  246.9 53.4 reduce-scatter.7
where the time goes:
time: 307 us
  blocking collectives  150 us (49%)
  waiting for transfers between devices  61.6 us (20%)
  local copies, waits for them, and re-layouts  45.7 us (15%)
  other arithmetic  26.8 us (9%)
  between operations  14.6 us (5%)
  matrix products  7.88 us (3%)
    all_to_all x1, blocking collectives, body(): lax.all_to_all(down_term.reshape(blocks_here, group, -1), 'tensor', split...  66.6 us
    unnamed x5, waiting for transfers between devices  47.8 us
    all_to_all x1, blocking collectives, body(): lax.all_to_all(down_send, 'tensor', split_axis=1, concat_axis=1, tiled=True)  37.9 us
    all_to_all x1, blocking collectives, body(): lax.all_to_all(up_weight_gradient.reshape(blocks_here, group, -1), 'tenso...  20 us
    scatter-add x1, other arithmetic, body(): down_table = jax.ops.segment_sum(down_flat, order, num_segments=ADAPTERS)  15.5 us
    all_to_all x1, blocking collectives, body(): lax.all_to_all(up_send, 'tensor', split_axis=1, concat_axis=1, tiled=True)  14.1 us
    broadcast_in_dim x1, local copies, waits for them, and re-layouts, body(): down_table = jax.ops.segment_sum(down_flat, order, num_segments=ADAPTERS)  13.8 us
    all_gather x1, waiting for transfers between devices, body(): columns = lax.all_gather(frozen_value, 'dp', axis=1, tiled=True)  13.8 us
  transfers between devices with their start and end apart: 4, of which 2 were waited for; matrix products, arithmetic and copies ran while one was open for 26% of the time, Pallas kernels for 0%

commit v1 on v0

--- a/solution.py
+++ b/solution.py
@@ -1,15 +1,36 @@
+import functools
+
 import jax
 import jax.numpy as jnp
 from jax import lax
+from jax.experimental import pallas as pl
+from jax.experimental.pallas import tpu as pltpu
 from jax.sharding import PartitionSpec as P
 
 D = 5120
 VALUE_OUTPUTS = 1024
 R = 64
 ADAPTERS = 256
-
+LANES = 128
+GROUP_ROWS = 16
 
 adapter_scale = 2.0
+VMEM = pl.BlockSpec(memory_space=pltpu.VMEM)
+SMEM = pl.BlockSpec(memory_space=pltpu.SMEM)
+ANY = pl.BlockSpec(memory_space=pl.ANY)
+LIMIT = pltpu.CompilerParams(vmem_limit_bytes=40 * 1024 * 1024)
+
+
+def dot(a, b):
+    return jnp.dot(a, b, preferred_element_type=jnp.float32)
+
+
+def dot_t(a, b):
+    return lax.dot_general(a, b, (((1,), (1,)), ((), ())), preferred_element_type=jnp.float32)
+
+
+def t_dot(a, b):
+    return lax.dot_general(a, b, (((0,), (0,)), ((), ())), preferred_element_type=jnp.float32)
 
 
 def fold_rows(left, piece):
@@ -21,7 +42,7 @@
     return jnp.sum(jnp.where(requests[:, None] == table[None, :], adapter_slot[None, :], 0), axis=1)
 
 
-def body(tokens, cotangent, frozen_value, down_store, up_store, block_adapter, adapter_slot):
+def plain_body(tokens, cotangent, frozen_value, down_store, up_store, block_adapter, adapter_slot):
     token_rows = tokens.shape[0]
     blocks_here = block_adapter.shape[0]
     block_rows = token_rows // blocks_here
@@ -33,10 +54,8 @@
     order = stored.reshape(group, blocks_here).T.reshape(-1)
     down_send = jnp.take(down_store, order, axis=0).reshape(blocks_here, group, -1)
     up_send = jnp.take(up_store, order, axis=0).reshape(blocks_here, group, -1)
-    down_got, up_got = (
-        lax.all_to_all(down_send, "tensor", split_axis=1, concat_axis=1, tiled=True),
-        lax.all_to_all(up_send, "tensor", split_axis=1, concat_axis=1, tiled=True),
-    )
+    down_got = lax.all_to_all(down_send, "tensor", split_axis=1, concat_axis=1, tiled=True)
+    up_got = lax.all_to_all(up_send, "tensor", split_axis=1, concat_axis=1, tiled=True)
     down_panel = down_got.reshape(blocks_here, D, R)
     up_panel = up_got.reshape(blocks_here, R, VALUE_OUTPUTS)
     token_blocks = tokens.reshape(blocks_here, block_rows, D)
@@ -60,31 +79,356 @@
     up_weight_gradient = adapter_scale * jnp.einsum(
         "jtr,jtk->jrk", down_projected, grad_blocks, preferred_element_type=jnp.float32
     )
-    down_back, up_back = (
-        lax.all_to_all(
-            down_term.reshape(blocks_here, group, -1),
-            "tensor",
-            split_axis=1,
-            concat_axis=1,
-            tiled=True,
-        ),
-        lax.all_to_all(
-            up_weight_gradient.reshape(blocks_here, group, -1),
-            "tensor",
-            split_axis=1,
-            concat_axis=1,
-            tiled=True,
-        ),
+    down_back = lax.all_to_all(
+        down_term.reshape(blocks_here, group, -1), "tensor", split_axis=1, concat_axis=1, tiled=True
+    )
+    up_back = lax.all_to_all(
+        up_weight_gradient.reshape(blocks_here, group, -1), "tensor", split_axis=1, concat_axis=1, tiled=True
     )
     down_flat = down_back.reshape(blocks_here * group, -1)
     up_flat = up_back.reshape(blocks_here * group, -1)
     down_table = jax.ops.segment_sum(down_flat, order, num_segments=ADAPTERS)
     up_table = jax.ops.segment_sum(up_flat, order, num_segments=ADAPTERS)
-    grad_down, grad_up = (
-        lax.psum_scatter(down_table, "dp", scatter_dimension=0, tiled=True),
-        lax.psum_scatter(up_table, "dp", scatter_dimension=0, tiled=True),
-    )
-    return (mixed, grad_down, grad_up)
+    grad_down = lax.psum_scatter(down_table, "dp", scatter_dimension=0, tiled=True)
+    grad_up = lax.psum_scatter(up_table, "dp", scatter_dimension=0, tiled=True)
+    return mixed, grad_down, grad_up
+
+
+def split_kernel(where, x_ref, mine_ref, theirs_ref):
+    inner = where[0]
+    outer, rows, width = mine_ref.shape
+    for k in range(outer):
+        own = pl.multiple_of((2 * k + inner) * width, LANES)
+        other = pl.multiple_of((2 * k + 1 - inner) * width, LANES)
+        mine_ref[k] = x_ref[:, pl.ds(own, width)]
+        theirs_ref[k] = x_ref[:, pl.ds(other, width)]
+
+
+def interleave_kernel(x_ref, xs_ref):
+    group, rows2, half = xs_ref.shape
+    rows, width = rows2 // 2, 2 * half
+    source = lax.broadcasted_iota(jnp.int32, (width, half), 0)
+    target = lax.broadcasted_iota(jnp.int32, (width, half), 1)
+    even = (source == 2 * target).astype(jnp.bfloat16)
+    odd = (source == 2 * target + 1).astype(jnp.bfloat16)
+    for k in range(group):
+        x = x_ref[:, k * width:(k + 1) * width]
+        xs_ref[k, :rows] = dot(x, even).astype(jnp.bfloat16)
+        xs_ref[k, rows:] = dot(x, odd).astype(jnp.bfloat16)
+
+
+def gather_kernel(count, down_chunks, up_chunks, rows, down_ref, up_ref, *rest):
+    outs, (down_buf, up_buf, flat, sems) = rest[:count], rest[count:]
+    copies = []
+    for s in range(count):
+        start = pl.multiple_of((rows[s] // GROUP_ROWS) * GROUP_ROWS, GROUP_ROWS)
+        a = pltpu.make_async_copy(down_ref.at[pl.ds(start, GROUP_ROWS)], down_buf.at[s], sems.at[2 * s])
+        b = pltpu.make_async_copy(up_ref.at[pl.ds(start, GROUP_ROWS)], up_buf.at[s], sems.at[2 * s + 1])
+        a.start()
+        b.start()
+        copies.append((a, b))
+    step = 8
+    for s in range(count):
+        row = rows[s] % GROUP_ROWS
+        upper = row >= 8
+        sub = row % 8
+        copies[s][0].wait()
+        copies[s][1].wait()
+
+        def pick(buf, lane):
+            tile = buf[s, :, pl.ds(pl.multiple_of(lane, LANES), LANES)].astype(jnp.float32)
+            return jnp.where(upper, tile[8:], tile[:8])
+
+        def some(i, carry):
+            for u in range(step):
+                j = i * step + u
+                flat[pl.ds(pl.multiple_of(j * 8, 8), 8), :] = pick(down_buf, j * LANES)
+            return carry
+
+        lax.fori_loop(0, down_chunks // step, some, 0)
+        outs[s][:down_chunks] = flat[pl.ds(sub, down_chunks, stride=8), :].astype(jnp.bfloat16)
+        across = up_chunks // 8
+        for j in range(up_chunks):
+            place = (j % across) * 8 + j // across
+            flat[place * 8:place * 8 + 8, :] = pick(up_buf, j * LANES)
+        outs[s][down_chunks:] = flat[pl.ds(sub, up_chunks, stride=8), :].astype(jnp.bfloat16)
+
+
+def zero_kernel(after_ref, down_ref, up_ref, zeros, sems):
+    del after_ref
+    zeros[...] = jnp.zeros_like(zeros)
+    part = zeros.shape[0]
+    copies = []
+    for ref, sem in ((down_ref, sems.at[0]), (up_ref, sems.at[1])):
+        for g in range(ref.shape[0]):
+            for c in range(ref.shape[1] // part):
+                copies.append(pltpu.make_async_copy(zeros, ref.at[g, pl.ds(c * part, part)], sem))
+    for c in copies:
+        c.start()
+    for c in copies:
+        c.wait()
+
+
+def adapter_kernel(count, down_chunks, where, xs_ref, g_ref, *rest):
+    pieces, outs, (lifted_ref, up_panel) = rest[:count], rest[count:2 * count], rest[2 * count:]
+    me = where[0]
+    rows = g_ref.shape[0]
+    across = g_ref.shape[1] // LANES
+    total = jnp.zeros((2 * rows, LANES), jnp.float32)
+    for s in range(count):
+        owner = me ^ s
+        total += dot(xs_ref[owner], pieces[s][:down_chunks])
+        at = pl.multiple_of(owner * 8, 8)
+        for c in range(across):
+            block = pieces[s][down_chunks + 8 * c:down_chunks + 8 * c + 8, :].astype(jnp.float32)
+            up_panel[pl.ds(at, 8), c * LANES:(c + 1) * LANES] = block
+            up_panel[pl.ds(R + at, 8), c * LANES:(c + 1) * LANES] = block
+    panel = up_panel[...].astype(jnp.bfloat16)
+    left = lax.broadcasted_iota(jnp.int32, (rows, LANES), 1) < R
+    inner = total[:rows] + pltpu.roll(total[rows:], R, 1)
+    inner = jnp.where(left, inner, 0.0).astype(jnp.bfloat16)
+    g = g_ref[...]
+    lifted_ref[...] = adapter_scale * dot(inner, panel)
+    inner_grad = adapter_scale * dot_t(g, panel)
+    diagonal = jnp.concatenate(
+        [jnp.where(left, inner_grad, 0.0), jnp.where(left, 0.0, inner_grad)], axis=0
+    ).astype(jnp.bfloat16)
+    up_term = adapter_scale * t_dot(inner, g)
+    up_panel[...] = up_term
+    for s in range(count):
+        owner = me ^ s
+        outs[s][:down_chunks] = t_dot(xs_ref[owner], diagonal).astype(jnp.bfloat16)
+        at = pl.multiple_of(owner * 8, 8)
+        rows_here = up_panel[pl.ds(at, 8), :]
+        up_part = jnp.concatenate(
+            [rows_here[:, c * LANES:(c + 1) * LANES] for c in range(across)], axis=0
+        )
+        outs[s][down_chunks:] = up_part.astype(jnp.bfloat16)
+
+
+def scatter_kernel(count, down_chunks, up_chunks, first_row, rows, *rest):
+    pieces = rest[:count]
+    down_out, up_out = rest[count + 2:count + 4]
+    down_sum, up_sum, ordered, sem = rest[count + 4:]
+    owned_rows = down_out.shape[0] * 8
+    across = up_chunks // 8
+    slots = []
+    for b in range(count):
+        slot = jnp.int32(b)
+        for e in range(b - 1, -1, -1):
+            slot = jnp.where(rows[e] == rows[b], e, slot)
+        slots.append(slot)
+        down = pieces[b][:down_chunks].astype(jnp.float32).reshape(down_chunks, 1, LANES)
+        for c in range(across):
+            ordered[pl.ds(c, 8, stride=across), :] = pieces[b][
+                down_chunks + 8 * c:down_chunks + 8 * c + 8
+            ].astype(jnp.float32)
+        up = ordered[...].reshape(up_chunks, 1, LANES)
+
+        @pl.when(slot == b)
+        def _():
+            down_sum[b] = down
+            up_sum[b] = up
+
+        @pl.when(slot != b)
+        def _():
+            down_sum[slot] += down
+            up_sum[slot] += up
+
+    def copies(b):
+        local = rows[b] - first_row[0]
+        return (
+            pltpu.make_async_copy(down_sum.at[b], down_out.at[local // 8, :, local % 8], sem),
+            pltpu.make_async_copy(up_sum.at[b], up_out.at[local // 8, :, local % 8], sem),
+        )
+
+    def mine(b):
+        local = rows[b] - first_row[0]
+        return (slots[b] == b) & (local >= 0) & (local < owned_rows)
+
+    for b in range(count):
+        @pl.when(mine(b))
+        def _():
+            for copy in copies(b):
+                copy.start()
+    for b in range(count):
+        @pl.when(mine(b))
+        def _():
+            for copy in copies(b):
+                copy.wait()
+
+
+def base_kernel(outer, where, x_refs, w_ref, arrivals, own_ref, other_ref, acc):
+    z, half = where[0], where[1]
+    width = arrivals[0][3].shape[1]
+
+    def left(block):
+        return jnp.concatenate([ref[block] for ref in x_refs], axis=0)
+
+    acc[...] = dot(left(z), w_ref[...])
+    for direction, distance, crossed, ref in arrivals:
+        source = z - direction * distance
+
+        @pl.when((source >= 0) & (source < outer))
+        def _():
+            at = pl.multiple_of((half if not crossed else 1 - half) * width, LANES)
+            acc[:, pl.ds(at, width)] += dot(left(source), ref[...])
+
+    rows = own_ref.shape[0]
+    own_ref[...] = acc[:rows]
+    other_ref[...] = acc[rows:]
+
+
+def fast_body(tokens, cotangent, frozen_value, down_store, up_store, block_adapter, adapter_slot):
+    group, parts = lax.axis_size("tensor"), lax.axis_size("parts")
+    outer = group // 2
+    token_rows = tokens.shape[0]
+    slice_width = D // group
+    down_chunks = down_store.shape[1] // LANES
+    up_chunks = up_store.shape[1] // LANES
+    piece = jax.ShapeDtypeStruct((down_chunks + up_chunks, LANES), jnp.bfloat16)
+    me, part, core = lax.axis_index("tensor"), lax.axis_index("parts"), lax.axis_index("dp")
+    z, x = me // 2, me % 2
+    here = jnp.stack([me, x, z, part])
+
+    def exchange(value, s):
+        return lax.ppermute(value, "tensor", [(t, t ^ s) for t in range(group)])
+
+    def other_core(value):
+        return lax.ppermute(value, "dp", [(0, 1), (1, 0)])
+
+    row = store_rows(block_adapter, adapter_slot)
+    rows = jnp.concatenate([row] + [exchange(row, s) for s in range(1, group)])
+    rows_core = other_core(rows)
+
+    width = frozen_value.shape[1] // parts
+    half = lax.dynamic_slice_in_dim(frozen_value, part * width, width, axis=1)
+    arrivals = []
+    for direction in (1, -1):
+        moving = half
+        for distance in range(1, outer):
+            steps = [
+                (t, t + 2 * direction)
+                for t in range(group)
+                if 0 <= t // 2 + direction < outer and 0 <= t // 2 - direction * (distance - 1) < outer
+            ]
+            moving = lax.ppermute(moving, "tensor", steps)
+            arrivals.append((direction, distance, False, moving))
+            crossing = [
+                (a * group + t, (1 - a) * group + t)
+                for a in range(parts)
+                for t in range(group)
+                if 0 <= t // 2 - direction * distance < outer
+            ]
+            arrivals.append(
+                (direction, distance, True, lax.ppermute(moving, ("parts", "tensor"), crossing))
+            )
+
+    block = jax.ShapeDtypeStruct((outer, token_rows, slice_width), jnp.bfloat16)
+    x_mine, x_theirs = pl.pallas_call(
+        split_kernel, out_shape=(block, block), in_specs=[SMEM, VMEM], out_specs=(VMEM, VMEM),
+        name="split_tokens",
+    )(x[None], tokens)
+    x_far = exchange(x_theirs, 1)
+    x_blocks = (x_mine, other_core(x_mine), x_far, other_core(x_far))
+
+    xs = pl.pallas_call(
+        interleave_kernel,
+        out_shape=jax.ShapeDtypeStruct((group, 2 * token_rows, slice_width // 2), jnp.bfloat16),
+        in_specs=[VMEM], out_specs=VMEM, name="pair_columns", compiler_params=LIMIT,
+    )(tokens)
+
+    sent = pl.pallas_call(
+        functools.partial(gather_kernel, group, down_chunks, up_chunks),
+        out_shape=[piece] * group,
+        in_specs=[SMEM, ANY, ANY],
+        out_specs=[VMEM] * group,
+        scratch_shapes=[
+            pltpu.VMEM((group, GROUP_ROWS, down_store.shape[1]), jnp.bfloat16),
+            pltpu.VMEM((group, GROUP_ROWS, up_store.shape[1]), jnp.bfloat16),
+            pltpu.VMEM((down_chunks * 8, LANES), jnp.float32),
+            pltpu.SemaphoreType.DMA((2 * group,)),
+        ],
+        compiler_params=LIMIT,
+        name="pick_panels",
+    )(rows, down_store, up_store)
+    panels = [sent[0]] + [exchange(sent[s], s) for s in range(1, group)]
+
+    owned_groups = ADAPTERS // lax.axis_size("dp") // 8
+    down_shape = jax.ShapeDtypeStruct((owned_groups, down_chunks, 8, 1, LANES), jnp.float32)
+    up_shape = jax.ShapeDtypeStruct((owned_groups, up_chunks, 8, 1, LANES), jnp.float32)
+    down_zero, up_zero = pl.pallas_call(
+        zero_kernel, out_shape=(down_shape, up_shape), in_specs=[ANY], out_specs=(ANY, ANY),
+        scratch_shapes=[pltpu.VMEM((up_chunks, 8, 1, LANES), jnp.float32), pltpu.SemaphoreType.DMA((2,))],
+        compiler_params=LIMIT, name="clear_rows",
+    )(sent[0])
+
+    results = pl.pallas_call(
+        functools.partial(adapter_kernel, group, down_chunks),
+        out_shape=[piece] * group + [jax.ShapeDtypeStruct((token_rows, VALUE_OUTPUTS), jnp.float32)],
+        in_specs=[SMEM] + [VMEM] * (2 + group),
+        out_specs=[VMEM] * (group + 1),
+        scratch_shapes=[pltpu.VMEM((2 * R, VALUE_OUTPUTS), jnp.float32)],
+        compiler_params=LIMIT,
+        name="adapter",
+    )(here, xs, cotangent, *panels)
+    terms, lifted = results[:group], results[group]
+    back = [terms[0]] + [exchange(terms[s], s) for s in range(1, group)]
+    back_core = [other_core(term) for term in back]
+
+    grad_down, grad_up = pl.pallas_call(
+        functools.partial(scatter_kernel, 2 * group, down_chunks, up_chunks),
+        out_shape=(down_shape, up_shape),
+        in_specs=[SMEM, SMEM] + [VMEM] * (2 * group) + [ANY, ANY],
+        out_specs=(ANY, ANY),
+        input_output_aliases={2 + 2 * group: 0, 3 + 2 * group: 1},
+        scratch_shapes=[
+            pltpu.VMEM((2 * group, down_chunks, 1, LANES), jnp.float32),
+            pltpu.VMEM((2 * group, up_chunks, 1, LANES), jnp.float32),
+            pltpu.VMEM((up_chunks, LANES), jnp.float32),
+            pltpu.SemaphoreType.DMA(()),
+        ],
+        compiler_params=LIMIT,
+        name="place_rows",
+    )((core * (ADAPTERS // lax.axis_size("dp")))[None], jnp.concatenate([rows, rows_core]), *back, *back_core,
+      down_zero, up_zero)
+    grad_down = grad_down.reshape(owned_groups, down_chunks, 8, LANES).transpose(0, 2, 1, 3)
+    grad_up = grad_up.reshape(owned_groups, up_chunks, 8, LANES).transpose(0, 2, 1, 3)
+
+    def base(where, *refs):
+        x_refs, w_ref, got = refs[:4], refs[4], refs[5:5 + len(arrivals)]
+        tagged = [a[:3] + (ref,) for a, ref in zip(arrivals, got)]
+        base_kernel(outer, where, x_refs, w_ref, tagged, *refs[5 + len(arrivals):])
+
+    sums = jax.ShapeDtypeStruct((2 * token_rows, frozen_value.shape[1]), jnp.float32)
+    own, other = pl.pallas_call(
+        base,
+        out_shape=(sums, sums),
+        in_specs=[SMEM] + [VMEM] * (5 + len(arrivals)),
+        out_specs=(VMEM, VMEM),
+        scratch_shapes=[pltpu.VMEM((4 * token_rows, frozen_value.shape[1]), jnp.float32)],
+        compiler_params=LIMIT,
+        name="frozen_part",
+    )(jnp.stack([z, part]), *x_blocks, frozen_value, *[a[3] for a in arrivals])
+    columns = own + exchange(other, 1)
+    kept, gone = columns[:token_rows], columns[token_rows:]
+    got = other_core(gone)
+    frozen_output = jnp.where(
+        core == 0, jnp.concatenate([kept, got], axis=1), jnp.concatenate([got, kept], axis=1)
+    )
+    mixed = (frozen_output + lifted).astype(jnp.bfloat16)
+    return mixed, grad_down.reshape(owned_groups * 8, -1), grad_up.reshape(owned_groups * 8, -1)
+
+
+def fits(mesh):
+    group, cores, parts = mesh.shape["tensor"], mesh.shape["dp"], mesh.shape["parts"]
+    return cores == 2 and parts == 2 and group <= 8 and group & (group - 1) == 0 and R == 8 * group
+
+
+def body(mesh, tokens, *rest):
+    block_adapter = rest[4]
+    one_block = block_adapter.shape[0] == 1
+    return (fast_body if fits(mesh) and one_block else plain_body)(tokens, *rest)
 
 
 def solution(mesh):
@@ -98,7 +442,7 @@
         P("parts"),
     )
     return jax.shard_map(
-        body,
+        functools.partial(body, mesh),
         mesh=mesh,
         in_specs=placed,
         out_specs=(

time: 307 us -> 164 us (0.53)
  blocking collectives: 150 us -> 0 us
  starting transfers between devices: 0.16 us -> 70.7 us
  Pallas kernels: 0 us -> 33.3 us
  waiting for transfers between devices: 61.6 us -> 33.9 us
  other arithmetic: 26.8 us -> 1.73 us
  local copies, waits for them, and re-layouts: 45.7 us -> 20.7 us
  between operations: 14.6 us -> 1.61 us
  matrix products: 7.88 us -> 0 us
    all_to_all x4 -> x0, blocking collectives: 139 us -> none  [the longest x1 66.6 us: body(): lax.all_to_all(down_term.reshape(blocks_here, group, -1), 'tensor', split...]
    ppermute x0 -> x47, starting transfers between devices: none -> 70.7 us  [the longest x23 43.2 us: exchange(): return lax.ppermute(value, 'tensor', [(t, t ^ s) for t in range(group)])]
    unnamed x5 -> x0, waiting for transfers between devices: 47.8 us -> none
    ppermute x0 -> x47, waiting for transfers between devices: none -> 33.9 us  [the longest x23 16.9 us: exchange(): return lax.ppermute(value, 'tensor', [(t, t ^ s) for t in range(group)])]
    pallas_call x0 -> x7, Pallas kernels: none -> 33.3 us  [the longest x1 8.42 us: fast_body(): pl.pallas_call(zero_kernel, out_shape=(down_shape, up_shape), in_specs=[A...]
    scatter-add x2 -> x0, other arithmetic: 20.4 us -> none  [the longest x1 15.5 us: body(): down_table = jax.ops.segment_sum(down_flat, order, num_segments=ADAPTERS)]
    gather x2 -> x0, local copies, waits for them, and re-layouts: 14.7 us -> none  [the longest x1 11.2 us: body(): jnp.take(down_store, order, axis=0).reshape(blocks_here, group, -1)]
    broadcast_in_dim x1 -> x0, local copies, waits for them, and re-layouts: 13.8 us -> none  [body(): down_table = jax.ops.segment_sum(down_flat, order, num_segments=ADAPTERS)]
  transfers between devices with their start and end apart: 4 -> 47, of which waited for: 2 -> 14; matrix products, arithmetic and copies ran while one was open for 26% -> 7% of each run, Pallas kernels for 0% -> 18%
where the time goes in v1:
time: 164 us; the launch traced here: 162 us
  starting transfers between devices  70.7 us (43%)
  waiting for transfers between devices  33.9 us (21%)
  Pallas kernels  33.3 us (20%)
  local copies, waits for them, and re-layouts  20.7 us (13%)
  other arithmetic  1.73 us (1%)
    ppermute x23, starting transfers between devices, exchange(): return lax.ppermute(value, 'tensor', [(t, t ^ s) for t in range(group)])  43.2 us
    ppermute x23, waiting for transfers between devices, exchange(): return lax.ppermute(value, 'tensor', [(t, t ^ s) for t in range(group)])  16.9 us
    ppermute x6, starting transfers between devices, fast_body(): lax.ppermute(moving, ('parts', 'tensor'), crossing)  14.2 us
    ppermute x6, starting transfers between devices, fast_body(): moving = lax.ppermute(moving, 'tensor', steps)  11.5 us
    unnamed x24, local copies, waits for them, and re-layouts  9.47 us
    ppermute x6, waiting for transfers between devices, fast_body(): moving = lax.ppermute(moving, 'tensor', steps)  8.87 us
    pallas_call x1, Pallas kernels, fast_body(): pl.pallas_call(zero_kernel, out_shape=(down_shape, up_shape), in_specs=[A...  8.42 us
    ppermute x6, waiting for transfers between devices, fast_body(): lax.ppermute(moving, ('parts', 'tensor'), crossing)  7.83 us
  transfers between devices with their start and end apart: 47, of which 14 were waited for; matrix products, arithmetic and copies ran while one was open for 7% of the time, Pallas kernels for 18%

profile of v1, /device:TPU:0, one launch (start us, length us, event | category | flops | bytes accessed | tf_op | source)
XLA Modules:
  0.0 162.0 jit_solution(6443032225079110405)
XLA Ops:
  0.6 1.0 constant_dynamic-slice_fusion
  1.6 1.3 collective-permute-start.9
  2.9 5.6 %collective-permute-start.3 = (bf16[640,256]{1,0:T(8,128)(2,1)S(1)}, bf16[640,256]{1,0:T(8,128)(2,1)S(1)}, u32[]{:S(2)}, u32[]{:S(2)}) collective-permute-start(bf16[640,256]{1,0:T(8,128)(2,1)S(1)} %constant_dynamic-slice_fusion), channel_id=1, source_target_pairs={{0,2},{1,3},{2,4},{3,5},{4,6},{5,7},{8,10},{9,11},{10,12},{11,13},... | collective-permute-start | bytes 983048 | tf_op jit(solution)/shard_map/ppermute | solution.py:315
  8.5 2.5 %split_tokens.1 = (bf16[4,128,640]{2,1,0:T(8,128)(2,1)}, bf16[4,128,640]{2,1,0:T(8,128)(2,1)}) custom-call(s32[1]{0:T(128)} %bitcast.2.where, bf16[128,5120]{1,0:T(8,128)(2,1)} %x_ref.3), custom_call_target="tpu_custom_call" | custom-call | tf_op jit(solution)/shard_map/split_tokens/pallas_call | solution.py:328
  11.0 1.9 %collective-permute-start.1 = (bf16[4,128,640]{2,1,0:T(8,128)(2,1)}, bf16[4,128,640]{2,1,0:T(8,128)(2,1)S(1)}, u32[]{:S(2)}, u32[]{:S(2)}) collective-permute-start(bf16[4,128,640]{2,1,0:T(8,128)(2,1)} %get-tuple-element.29), channel_id=1, source_target_pairs={{0,1},{1,0},{2,3},{3,2},{4,5},{5,4},{6,7},{7,6},{8,9},{9,8},{10,11... | collective-permute-start | bytes 1966088 | tf_op jit(solution)/shard_map/ppermute | solution.py:295
  13.0 1.3 collective-permute-done.9.refs_11_
  14.3 1.3 collective-permute-start.11
  15.6 3.6 %collective-permute-start.10 = (bf16[640,256]{1,0:T(8,128)(2,1)S(1)}, bf16[640,256]{1,0:T(8,128)(2,1)S(1)}, u32[]{:S(2)}, u32[]{:S(2)}) collective-permute-start(bf16[640,256]{1,0:T(8,128)(2,1)S(1)} %collective-permute-done.9.refs_11_), channel_id=1, source_target_pairs={{0,16},{1,17},{2,18},{3,19},{4,20},{5,21},{16,0},{17,1},{18,2},{19... | collective-permute-start | bytes 983048 | tf_op jit(solution)/shard_map/ppermute | solution.py:324
  19.2 0.7 collective-permute-start.5
  19.9 5.1 %collective-permute-done.11.refs_13_ = bf16[640,256]{1,0:T(8,128)(2,1)S(1)} collective-permute-done((bf16[640,256]{1,0:T(8,128)(2,1)S(1)}, bf16[640,256]{1,0:T(8,128)(2,1)S(1)}, u32[]{:S(2)}, u32[]{:S(2)}) %collective-permute-start.11) | collective-permute-done | bytes 327712 | tf_op jit(solution)/shard_map/ppermute | solution.py:315
  25.1 0.7 collective-permute-start.4
  25.7 1.9 %collective-permute-done.10.refs_12_ = bf16[640,256]{1,0:T(8,128)(2,1)S(1)} collective-permute-done((bf16[640,256]{1,0:T(8,128)(2,1)S(1)}, bf16[640,256]{1,0:T(8,128)(2,1)S(1)}, u32[]{:S(2)}, u32[]{:S(2)}) %collective-permute-start.10) | collective-permute-done | bytes 327712 | tf_op jit(solution)/shard_map/ppermute | solution.py:324
  27.6 0.7 copy-done.4
  28.4 1.3 collective-permute-start.13
  29.7 1.4 collective-permute-start.7
  31.1 0.7 copy-done.8
  31.8 3.6 %collective-permute-start.12 = (bf16[640,256]{1,0:T(8,128)(2,1)S(1)}, bf16[640,256]{1,0:T(8,128)(2,1)}, u32[]{:S(2)}, u32[]{:S(2)}) collective-permute-start(bf16[640,256]{1,0:T(8,128)(2,1)S(1)} %collective-permute-done.11.refs_13_), channel_id=1, source_target_pairs={{0,16},{1,17},{2,18},{3,19},{16,0},{17,1},{18,2},{19,3},{8,24},{9,... | collective-permute-start | bytes 983048 | tf_op jit(solution)/shard_map/ppermute | solution.py:324
  35.4 1.4 collective-permute-start.6
  36.8 0.7 copy-done.6
  37.5 2.4 %collective-permute-done.13.refs_15_ = bf16[640,256]{1,0:T(8,128)(2,1)} collective-permute-done((bf16[640,256]{1,0:T(8,128)(2,1)S(1)}, bf16[640,256]{1,0:T(8,128)(2,1)}, u32[]{:S(2)}, u32[]{:S(2)}) %collective-permute-start.13) | collective-permute-done | bytes 327712 | tf_op jit(solution)/shard_map/ppermute | solution.py:315
  40.0 3.6 %collective-permute-start.14 = (bf16[640,256]{1,0:T(8,128)(2,1)}, bf16[640,256]{1,0:T(8,128)(2,1)}, u32[]{:S(2)}, u32[]{:S(2)}) collective-permute-start(bf16[640,256]{1,0:T(8,128)(2,1)} %collective-permute-done.13.refs_15_), channel_id=1, source_target_pairs={{0,16},{1,17},{16,0},{17,1},{8,24},{9,25},{24,8},{25,9}} | collective-permute-start | bytes 983048 | tf_op jit(solution)/shard_map/ppermute | solution.py:324
  43.5 1.4 collective-permute-start.8
  45.0 5.9 %collective-permute-done.14.refs_16_ = bf16[640,256]{1,0:T(8,128)(2,1)} collective-permute-done((bf16[640,256]{1,0:T(8,128)(2,1)}, bf16[640,256]{1,0:T(8,128)(2,1)}, u32[]{:S(2)}, u32[]{:S(2)}) %collective-permute-start.14) | collective-permute-done | bytes 327712 | tf_op jit(solution)/shard_map/ppermute | solution.py:324
  50.9 1.1 copy-done.2
  52.0 1.1 copy-done.3
  53.1 1.0 copy-done.5
  54.1 1.0 copy-done.7
  55.1 1.0 copy-done.9
  56.0 5.0 %frozen_part.1 = (f32[256,512]{1,0:T(8,128)S(1)}, f32[256,512]{1,0:T(8,128)}) custom-call(s32[2]{0:T(128)S(1)} %pad_add_fusion.where, bf16[4,128,640]{2,1,0:T(8,128)(2,1)S(1)} %copy-done.3, bf16[4,128,640]{2,1,0:T(8,128)(2,1)S(1)} %collective-permute-done.refs_1_, bf16[4,128,640]{2,1,0:T(8,128)(2,1)S(1)} %collective-permute-done.1.refs_2_, ...), custom_call_target="tpu_custom_call" | custom-call | tf_op jit(solution)/shard_map/frozen_part/pallas_call | solution.py:404
  61.0 1.7 %collective-permute-start.15 = (f32[256,512]{1,0:T(8,128)}, f32[256,512]{1,0:T(8,128)S(1)}, u32[]{:S(2)}, u32[]{:S(2)}) collective-permute-start(f32[256,512]{1,0:T(8,128)} %get-tuple-element.31), channel_id=1, source_target_pairs={{0,1},{1,0},{2,3},{3,2},{4,5},{5,4},{6,7},{7,6},{8,9},{9,8},{10,11... | collective-permute-start | bytes 1572872 | tf_op jit(solution)/shard_map/ppermute | solution.py:295
  63.3 0.7 fusion.2
  64.0 5.9 %collective-permute-start.23 = (s32[1]{0:T(128)}, s32[1]{0:T(128)}, u32[]{:S(2)}, u32[]{:S(2)}) collective-permute-start(s32[1]{0:T(128)} %bitcast.5), channel_id=1, source_target_pairs={{0,7},{1,6},{2,5},{3,4},{4,3},{5,2},{6,1},{7,0},{8,15},{9,14},{10,... | collective-permute-start | bytes 20 | tf_op jit(solution)/shard_map/ppermute | solution.py:295
  69.9 3.8 %collective-permute-start.20 = (s32[1]{0:T(128)}, s32[1]{0:T(128)}, u32[]{:S(2)}, u32[]{:S(2)}) collective-permute-start(s32[1]{0:T(128)} %bitcast.5), channel_id=1, source_target_pairs={{0,4},{1,5},{2,6},{3,7},{4,0},{5,1},{6,2},{7,3},{8,12},{9,13},{10,... | collective-permute-start | bytes 20 | tf_op jit(solution)/shard_map/ppermute | solution.py:295
  73.7 1.5 collective-permute-start.19
  75.2 0.5 collective-permute-start.18
  75.8 1.5 collective-permute-start.17
  77.2 0.9 collective-permute-done.19
  78.2 0.8 collective-permute-done.18
  79.0 0.5 collective-permute-done.17
  79.5 5.1 %concatenate.15.rows = s32[8]{0:T(128)S(1)} concatenate(s32[1]{0:T(128)} %bitcast.5, s32[1]{0:T(128)} %collective-permute-done.17, s32[1]{0:T(128)} %collective-permute-done.18, s32[1]{0:T(128)} %collective-permute-done.19, s32[1]{0:T(128)} %collective-permute-done.20, s32[1]{0:T(128)} %collective-permute-done.21, s32[1]{0:T(128)} %collective-permute-done.22, ...), dimensions={0} | concatenate | bytes 64 | tf_op jit(solution)/shard_map/concatenate | solution.py:301
  84.6 2.2 %copy-done.1 = bf16[256,8192]{1,0:T(8,128)(2,1)S(1)} copy-done((bf16[256,8192]{1,0:T(8,128)(2,1)S(1)}, bf16[256,8192]{1,0:T(8,128)(2,1)}, u32[]{:S(2)}) %copy-start.1) | copy-done | bytes 4194328
  86.8 7.4 %pick_panels.1 = (bf16[384,128]{1,0:T(8,128)(2,1)S(1)}, bf16[384,128]{1,0:T(8,128)(2,1)S(1)}, bf16[384,128]{1,0:T(8,128)(2,1)S(1)}, bf16[384,128]{1,0:T(8,128)(2...) custom-call(s32[8]{0:T(128)S(1)} %concatenate.15.rows, ...), custom_call_target="tpu_custom_call" | custom-call | tf_op jit(solution)/shard_map/pick_panels/pallas_call | solution.py:341
  94.2 1.5 collective-permute-start.24
  95.7 1.9 %collective-permute-start.25 = (bf16[384,128]{1,0:T(8,128)(2,1)S(1)}, bf16[384,128]{1,0:T(8,128)(2,1)S(1)}, u32[]{:S(2)}, u32[]{:S(2)}) collective-permute-start(bf16[384,128]{1,0:T(8,128)(2,1)S(1)} %get-tuple-element.34), channel_id=1, source_target_pairs={{0,2},{1,3},{2,0},{3,1},{4,6},{5,7},{6,4},{7,5},{8,10},{9,11},{10,... | collective-permute-start | bytes 294920 | tf_op jit(solution)/shard_map/ppermute | solution.py:295
  97.7 1.8 %pair_columns.1.xs_ref = bf16[8,256,320]{2,1,0:T(8,128)(2,1)S(1)} custom-call(bf16[128,5120]{1,0:T(8,128)(2,1)S(1)} %copy-done), custom_call_target="tpu_custom_call" | custom-call | tf_op jit(solution)/shard_map/pair_columns/pallas_call | solution.py:335
  99.5 2.9 %collective-permute-start.27 = (bf16[384,128]{1,0:T(8,128)(2,1)S(1)}, bf16[384,128]{1,0:T(8,128)(2,1)S(1)}, u32[]{:S(2)}, u32[]{:S(2)}) collective-permute-start(bf16[384,128]{1,0:T(8,128)(2,1)S(1)} %get-tuple-element.36), channel_id=1, source_target_pairs={{0,4},{1,5},{2,6},{3,7},{4,0},{5,1},{6,2},{7,3},{8,12},{9,13},{10,... | collective-permute-start | bytes 294920 | tf_op jit(solution)/shard_map/ppermute | solution.py:295
  102.5 1.0 collective-permute-start.28
  103.5 4.2 %collective-permute-start.29 = (bf16[384,128]{1,0:T(8,128)(2,1)S(1)}, bf16[384,128]{1,0:T(8,128)(2,1)S(1)}, u32[]{:S(2)}, u32[]{:S(2)}) collective-permute-start(bf16[384,128]{1,0:T(8,128)(2,1)S(1)} %get-tuple-element.38), channel_id=1, source_target_pairs={{0,6},{1,7},{2,4},{3,5},{4,2},{5,3},{6,0},{7,1},{8,14},{9,15},{10,... | collective-permute-start | bytes 294920 | tf_op jit(solution)/shard_map/ppermute | solution.py:295
  107.7 2.4 %collective-permute-start.30 = (bf16[384,128]{1,0:T(8,128)(2,1)S(1)}, bf16[384,128]{1,0:T(8,128)(2,1)S(1)}, u32[]{:S(2)}, u32[]{:S(2)}) collective-permute-start(bf16[384,128]{1,0:T(8,128)(2,1)S(1)} %get-tuple-element.39), channel_id=1, source_target_pairs={{0,7},{1,6},{2,5},{3,4},{4,3},{5,2},{6,1},{7,0},{8,15},{9,14},{10,... | collective-permute-start | bytes 294920 | tf_op jit(solution)/shard_map/ppermute | solution.py:295
  110.2 1.8 %collective-permute-done.27.rest_4_ = bf16[384,128]{1,0:T(8,128)(2,1)S(1)} collective-permute-done((bf16[384,128]{1,0:T(8,128)(2,1)S(1)}, bf16[384,128]{1,0:T(8,128)(2,1)S(1)}, u32[]{:S(2)}, u32[]{:S(2)}) %collective-permute-start.27) | collective-permute-done | bytes 98336 | tf_op jit(solution)/shard_map/ppermute | solution.py:295
  111.9 1.8 %collective-permute-done.28.rest_5_ = bf16[384,128]{1,0:T(8,128)(2,1)S(1)} collective-permute-done((bf16[384,128]{1,0:T(8,128)(2,1)S(1)}, bf16[384,128]{1,0:T(8,128)(2,1)S(1)}, u32[]{:S(2)}, u32[]{:S(2)}) %collective-permute-start.28) | collective-permute-done | bytes 98336 | tf_op jit(solution)/shard_map/ppermute | solution.py:295
  113.7 1.4 collective-permute-done.30.rest_7_
  115.2 2.0 %adapter.1 = (bf16[384,128]{1,0:T(8,128)(2,1)S(1)}, bf16[384,128]{1,0:T(8,128)(2,1)S(1)}, bf16[384,128]{1,0:T(8,128)(2,1)S(1)}, bf16[384,128]{1,0:T(8,128)(2,1)S...) custom-call(s32[4]{0:T(128)S(1)} %pad_add_fusion.1.where, ...), custom_call_target="tpu_custom_call" | custom-call | tf_op jit(solution)/shard_map/adapter/pallas_call | solution.py:366
  117.2 1.1 collective-permute-start.32
  118.3 2.5 %collective-permute-start.33 = (bf16[384,128]{1,0:T(8,128)(2,1)S(1)}, bf16[384,128]{1,0:T(8,128)(2,1)S(1)}, u32[]{:S(2)}, u32[]{:S(2)}) collective-permute-start(bf16[384,128]{1,0:T(8,128)(2,1)S(1)} %get-tuple-element.43), channel_id=1, source_target_pairs={{0,2},{1,3},{2,0},{3,1},{4,6},{5,7},{6,4},{7,5},{8,10},{9,11},{10,... | collective-permute-start | bytes 294920 | tf_op jit(solution)/shard_map/ppermute | solution.py:295
  120.9 3.9 %collective-permute-start.35 = (bf16[384,128]{1,0:T(8,128)(2,1)S(1)}, bf16[384,128]{1,0:T(8,128)(2,1)S(1)}, u32[]{:S(2)}, u32[]{:S(2)}) collective-permute-start(bf16[384,128]{1,0:T(8,128)(2,1)S(1)} %get-tuple-element.45), channel_id=1, source_target_pairs={{0,4},{1,5},{2,6},{3,7},{4,0},{5,1},{6,2},{7,3},{8,12},{9,13},{10,... | collective-permute-start | bytes 294920 | tf_op jit(solution)/shard_map/ppermute | solution.py:295
  124.9 2.4 %collective-permute-start.37 = (bf16[384,128]{1,0:T(8,128)(2,1)S(1)}, bf16[384,128]{1,0:T(8,128)(2,1)S(1)}, u32[]{:S(2)}, u32[]{:S(2)}) collective-permute-start(bf16[384,128]{1,0:T(8,128)(2,1)S(1)} %get-tuple-element.47), channel_id=1, source_target_pairs={{0,6},{1,7},{2,4},{3,5},{4,2},{5,3},{6,0},{7,1},{8,14},{9,15},{10,... | collective-permute-start | bytes 294920 | tf_op jit(solution)/shard_map/ppermute | solution.py:295
  127.4 2.3 %collective-permute-start.38 = (bf16[384,128]{1,0:T(8,128)(2,1)S(1)}, bf16[384,128]{1,0:T(8,128)(2,1)S(1)}, u32[]{:S(2)}, u32[]{:S(2)}) collective-permute-start(bf16[384,128]{1,0:T(8,128)(2,1)S(1)} %get-tuple-element.48), channel_id=1, source_target_pairs={{0,7},{1,6},{2,5},{3,4},{4,3},{5,2},{6,1},{7,0},{8,15},{9,14},{10,... | collective-permute-start | bytes 294920 | tf_op jit(solution)/shard_map/ppermute | solution.py:295
  129.8 6.8 %collective-permute-done.35.rest_4_ = bf16[384,128]{1,0:T(8,128)(2,1)S(1)} collective-permute-done((bf16[384,128]{1,0:T(8,128)(2,1)S(1)}, bf16[384,128]{1,0:T(8,128)(2,1)S(1)}, u32[]{:S(2)}, u32[]{:S(2)}) %collective-permute-start.35) | collective-permute-done | bytes 98336 | tf_op jit(solution)/shard_map/ppermute | solution.py:295
  136.6 2.8 %collective-permute-done.36.rest_5_ = bf16[384,128]{1,0:T(8,128)(2,1)S(1)} collective-permute-done((bf16[384,128]{1,0:T(8,128)(2,1)S(1)}, bf16[384,128]{1,0:T(8,128)(2,1)S(1)}, u32[]{:S(2)}, u32[]{:S(2)}) %collective-permute-start.36) | collective-permute-done | bytes 98336 | tf_op jit(solution)/shard_map/ppermute | solution.py:295
  141.3 8.4 %clear_rows.1 = (f32[16,320,8,1,128]{4,3,2,1,0:T(1,128)}, f32[16,64,8,1,128]{4,3,2,1,0:T(1,128)}) custom-call(bf16[384,128]{1,0:T(8,128)(2,1)S(1)} %get-tuple-element.32.rest_0_.after_ref), custom_call_target="tpu_custom_call" | custom-call | tf_op jit(solution)/shard_map/clear_rows/pallas_call | solution.py:360
  149.7 5.1 %concatenate.16.rows = s32[16]{0:T(128)S(1)} concatenate(s32[1]{0:T(128)} %bitcast.5, s32[1]{0:T(128)} %collective-permute-done.17, s32[1]{0:T(128)} %collective-permute-done.18, s32[1]{0:T(128)} %collective-permute-done.19, s32[1]{0:T(128)} %collective-permute-done.20, s32[1]{0:T(128)} %collective-permute-done.21, s32[1]{0:T(128)} %collective-permute-done.22, ...), dimensions={0} | concatenate | bytes 128 | tf_op jit(solution)/shard_map/concatenate | solution.py:393
  154.9 6.3 %place_rows.1 = (f32[16,320,8,1,128]{4,3,2,1,0:T(1,128)}, f32[16,64,8,1,128]{4,3,2,1,0:T(1,128)}) custom-call(s32[1]{0:T(128)} %bitcast.6.first_row, s32[16]{0:T(128)S(1)} %concatenate.16.rows, bf16[384,128]{1,0:T(8,128)(2,1)S(1)} %get-tuple-element.41.rest_0_, ...), custom_call_target="tpu_custom_call", output_to_operand_aliasing={{0}: (18, {}), {1}: (19, {})} | custom-call | tf_op jit(solution)/shard_map/place_rows/pallas_call | solution.py:379
  161.2 0.8 fusion.1
  (70 shorter events, 2.8 us)
Async XLA Ops:
  1.6 12.6 %collective-permute-start.9 = (bf16[640,256]{1,0:T(8,128)(2,1)S(1)}, bf16[640,256]{1,0:T(8,128)(2,1)S(1)}, u32[]{:S(2)}, u32[]{:S(2)}) collective-permute-start(bf16[640,256]{1,0:T(8,128)(2,1)S(1)} %constant_dynamic-slice_fusion), channel_id=1, source_target_pairs={{2,0},{3,1},{4,2},{5,3},{6,4},{7,5},{10,8},{11,9},{12,10},{13,11},... | collective-permute-start | bytes 983048 | tf_op jit(solution)/shard_map/ppermute | solution.py:315
  2.9 16.3 %collective-permute-start.3 = (bf16[640,256]{1,0:T(8,128)(2,1)S(1)}, bf16[640,256]{1,0:T(8,128)(2,1)S(1)}, u32[]{:S(2)}, u32[]{:S(2)}) collective-permute-start(bf16[640,256]{1,0:T(8,128)(2,1)S(1)} %constant_dynamic-slice_fusion), channel_id=1, source_target_pairs={{0,2},{1,3},{2,4},{3,5},{4,6},{5,7},{8,10},{9,11},{10,12},{11,13},... | collective-permute-start | bytes 983048 | tf_op jit(solution)/shard_map/ppermute | solution.py:315
  8.5 54.8 %copy-start.11 = (s32[256]{0:T(256)S(1)}, s32[256]{0:T(256)}, u32[]{:S(2)}) copy-start(s32[256]{0:T(256)} %param.13) | copy-start | bytes 3076
  11.0 20.0 %collective-permute-start.1 = (bf16[4,128,640]{2,1,0:T(8,128)(2,1)}, bf16[4,128,640]{2,1,0:T(8,128)(2,1)S(1)}, u32[]{:S(2)}, u32[]{:S(2)}) collective-permute-start(bf16[4,128,640]{2,1,0:T(8,128)(2,1)} %get-tuple-element.29), channel_id=1, source_target_pairs={{0,1},{1,0},{2,3},{3,2},{4,5},{5,4},{6,7},{7,6},{8,9},{9,8},{10,11... | collective-permute-start | bytes 1966088 | tf_op jit(solution)/shard_map/ppermute | solution.py:295
  14.3 10.8 %collective-permute-start.11 = (bf16[640,256]{1,0:T(8,128)(2,1)S(1)}, bf16[640,256]{1,0:T(8,128)(2,1)S(1)}, u32[]{:S(2)}, u32[]{:S(2)}) collective-permute-start(bf16[640,256]{1,0:T(8,128)(2,1)S(1)} %collective-permute-done.9.refs_11_), channel_id=1, source_target_pairs={{2,0},{3,1},{4,2},{5,3},{10,8},{11,9},{12,10},{13,11},{18,16},{19,... | collective-permute-start | bytes 983048 | tf_op jit(solution)/shard_map/ppermute | solution.py:315
  15.6 19.8 %collective-permute-start = (bf16[4,128,640]{2,1,0:T(8,128)(2,1)}, bf16[4,128,640]{2,1,0:T(8,128)(2,1)S(1)}, u32[]{:S(2)}, u32[]{:S(2)}) collective-permute-start(bf16[4,128,640]{2,1,0:T(8,128)(2,1)} %get-tuple-element.28.refs_0_), channel_id=1, source_target_pairs={{0,8},{8,0},{1,9},{9,1},{2,10},{10,2},{3,11},{11,3},{4,12},{12,4},... | collective-permute-start | bytes 1966088 | tf_op jit(solution)/shard_map/ppermute | solution.py:298
  15.6 12.0 %collective-permute-start.10 = (bf16[640,256]{1,0:T(8,128)(2,1)S(1)}, bf16[640,256]{1,0:T(8,128)(2,1)S(1)}, u32[]{:S(2)}, u32[]{:S(2)}) collective-permute-start(bf16[640,256]{1,0:T(8,128)(2,1)S(1)} %collective-permute-done.9.refs_11_), channel_id=1, source_target_pairs={{0,16},{1,17},{2,18},{3,19},{4,20},{5,21},{16,0},{17,1},{18,2},{19... | collective-permute-start | bytes 983048 | tf_op jit(solution)/shard_map/ppermute | solution.py:324
  19.2 10.4 %collective-permute-start.5 = (bf16[640,256]{1,0:T(8,128)(2,1)S(1)}, bf16[640,256]{1,0:T(8,128)(2,1)S(1)}, u32[]{:S(2)}, u32[]{:S(2)}) collective-permute-start(bf16[640,256]{1,0:T(8,128)(2,1)S(1)} %collective-permute-done.3.refs_5_), channel_id=1, source_target_pairs={{2,4},{3,5},{4,6},{5,7},{10,12},{11,13},{12,14},{13,15},{18,20},{1... | collective-permute-start | bytes 983048 | tf_op jit(solution)/shard_map/ppermute | solution.py:315
  25.1 6.0 %collective-permute-start.4 = (bf16[640,256]{1,0:T(8,128)(2,1)S(1)}, bf16[640,256]{1,0:T(8,128)(2,1)S(1)}, u32[]{:S(2)}, u32[]{:S(2)}) collective-permute-start(bf16[640,256]{1,0:T(8,128)(2,1)S(1)} %collective-permute-done.3.refs_5_), channel_id=1, source_target_pairs={{2,18},{3,19},{4,20},{5,21},{6,22},{7,23},{18,2},{19,3},{20,4},{21... | collective-permute-start | bytes 983048 | tf_op jit(solution)/shard_map/ppermute | solution.py:324
  27.6 0.7 copy-start.4
  28.4 11.6 %collective-permute-start.13 = (bf16[640,256]{1,0:T(8,128)(2,1)S(1)}, bf16[640,256]{1,0:T(8,128)(2,1)}, u32[]{:S(2)}, u32[]{:S(2)}) collective-permute-start(bf16[640,256]{1,0:T(8,128)(2,1)S(1)} %collective-permute-done.11.refs_13_), channel_id=1, source_target_pairs={{2,0},{3,1},{10,8},{11,9},{18,16},{19,17},{26,24},{27,25}} | collective-permute-start | bytes 983048 | tf_op jit(solution)/shard_map/ppermute | solution.py:315
  29.7 13.9 %collective-permute-start.7 = (bf16[640,256]{1,0:T(8,128)(2,1)S(1)}, bf16[640,256]{1,0:T(8,128)(2,1)}, u32[]{:S(2)}, u32[]{:S(2)}) collective-permute-start(bf16[640,256]{1,0:T(8,128)(2,1)S(1)} %collective-permute-done.5.refs_7_), channel_id=1, source_target_pairs={{4,6},{5,7},{12,14},{13,15},{20,22},{21,23},{28,30},{29,31}} | collective-permute-start | bytes 983048 | tf_op jit(solution)/shard_map/ppermute | solution.py:315
  31.1 19.9 %collective-permute-start.2 = (bf16[4,128,640]{2,1,0:T(8,128)(2,1)S(1)}, bf16[4,128,640]{2,1,0:T(8,128)(2,1)S(1)}, u32[]{:S(2)}, u32[]{:S(2)}) collective-permute-start(bf16[4,128,640]{2,1,0:T(8,128)(2,1)S(1)} %collective-permute-done.1.refs_2_), channel_id=1, source_target_pairs={{0,8},{8,0},{1,9},{9,1},{2,10},{10,2},{3,11},{11,3},{4,12},{12,4},... | collective-permute-start | bytes 1966088 | tf_op jit(solution)/shard_map/ppermute | solution.py:298
  31.1 0.7 copy-start.8
  31.8 13.2 %collective-permute-start.12 = (bf16[640,256]{1,0:T(8,128)(2,1)S(1)}, bf16[640,256]{1,0:T(8,128)(2,1)}, u32[]{:S(2)}, u32[]{:S(2)}) collective-permute-start(bf16[640,256]{1,0:T(8,128)(2,1)S(1)} %collective-permute-done.11.refs_13_), channel_id=1, source_target_pairs={{0,16},{1,17},{2,18},{3,19},{16,0},{17,1},{18,2},{19,3},{8,24},{9,... | collective-permute-start | bytes 983048 | tf_op jit(solution)/shard_map/ppermute | solution.py:324
  35.4 9.6 %collective-permute-start.6 = (bf16[640,256]{1,0:T(8,128)(2,1)S(1)}, bf16[640,256]{1,0:T(8,128)(2,1)}, u32[]{:S(2)}, u32[]{:S(2)}) collective-permute-start(bf16[640,256]{1,0:T(8,128)(2,1)S(1)} %collective-permute-done.5.refs_7_), channel_id=1, source_target_pairs={{4,20},{5,21},{6,22},{7,23},{20,4},{21,5},{22,6},{23,7},{12,28},{1... | collective-permute-start | bytes 983048 | tf_op jit(solution)/shard_map/ppermute | solution.py:324
  36.8 0.7 copy-start.6
  40.0 11.0 %collective-permute-start.14 = (bf16[640,256]{1,0:T(8,128)(2,1)}, bf16[640,256]{1,0:T(8,128)(2,1)}, u32[]{:S(2)}, u32[]{:S(2)}) collective-permute-start(bf16[640,256]{1,0:T(8,128)(2,1)} %collective-permute-done.13.refs_15_), channel_id=1, source_target_pairs={{0,16},{1,17},{16,0},{17,1},{8,24},{9,25},{24,8},{25,9}} | collective-permute-start | bytes 983048 | tf_op jit(solution)/shard_map/ppermute | solution.py:324
  43.5 7.4 %collective-permute-start.8 = (bf16[640,256]{1,0:T(8,128)(2,1)}, bf16[640,256]{1,0:T(8,128)(2,1)}, u32[]{:S(2)}, u32[]{:S(2)}) collective-permute-start(bf16[640,256]{1,0:T(8,128)(2,1)} %collective-permute-done.7.refs_9_), channel_id=1, source_target_pairs={{6,22},{7,23},{22,6},{23,7},{14,30},{15,31},{30,14},{31,15}} | collective-permute-start | bytes 983048 | tf_op jit(solution)/shard_map/ppermute | solution.py:324
  50.9 1.1 copy-start.2
  52.0 1.1 copy-start.3
  53.1 1.0 copy-start.5
  54.1 1.0 copy-start.7
  55.1 1.0 copy-start.9
  61.0 59.9 %collective-permute-start.15 = (f32[256,512]{1,0:T(8,128)}, f32[256,512]{1,0:T(8,128)S(1)}, u32[]{:S(2)}, u32[]{:S(2)}) collective-permute-start(f32[256,512]{1,0:T(8,128)} %get-tuple-element.31), channel_id=1, source_target_pairs={{0,1},{1,0},{2,3},{3,2},{4,5},{5,4},{6,7},{7,6},{8,9},{9,8},{10,11... | collective-permute-start | bytes 1572872 | tf_op jit(solution)/shard_map/ppermute | solution.py:295
  64.0 9.7 %collective-permute-start.23 = (s32[1]{0:T(128)}, s32[1]{0:T(128)}, u32[]{:S(2)}, u32[]{:S(2)}) collective-permute-start(s32[1]{0:T(128)} %bitcast.5), channel_id=1, source_target_pairs={{0,7},{1,6},{2,5},{3,4},{4,3},{5,2},{6,1},{7,0},{8,15},{9,14},{10,... | collective-permute-start | bytes 20 | tf_op jit(solution)/shard_map/ppermute | solution.py:295
  69.9 5.3 %collective-permute-start.22 = (s32[1]{0:T(128)}, s32[1]{0:T(128)}, u32[]{:S(2)}, u32[]{:S(2)}) collective-permute-start(s32[1]{0:T(128)} %bitcast.5), channel_id=1, source_target_pairs={{0,6},{1,7},{2,4},{3,5},{4,2},{5,3},{6,0},{7,1},{8,14},{9,15},{10,... | collective-permute-start | bytes 20 | tf_op jit(solution)/shard_map/ppermute | solution.py:295
  69.9 5.9 %collective-permute-start.21 = (s32[1]{0:T(128)}, s32[1]{0:T(128)}, u32[]{:S(2)}, u32[]{:S(2)}) collective-permute-start(s32[1]{0:T(128)} %bitcast.5), channel_id=1, source_target_pairs={{0,5},{1,4},{2,7},{3,6},{4,1},{5,0},{6,3},{7,2},{8,13},{9,12},{10,... | collective-permute-start | bytes 20 | tf_op jit(solution)/shard_map/ppermute | solution.py:295
  69.9 7.3 %collective-permute-start.20 = (s32[1]{0:T(128)}, s32[1]{0:T(128)}, u32[]{:S(2)}, u32[]{:S(2)}) collective-permute-start(s32[1]{0:T(128)} %bitcast.5), channel_id=1, source_target_pairs={{0,4},{1,5},{2,6},{3,7},{4,0},{5,1},{6,2},{7,3},{8,12},{9,13},{10,... | collective-permute-start | bytes 20 | tf_op jit(solution)/shard_map/ppermute | solution.py:295
  73.7 4.5 %collective-permute-start.19 = (s32[1]{0:T(128)}, s32[1]{0:T(128)}, u32[]{:S(2)}, u32[]{:S(2)}) collective-permute-start(s32[1]{0:T(128)} %bitcast.5), channel_id=1, source_target_pairs={{0,3},{1,2},{2,1},{3,0},{4,7},{5,6},{6,5},{7,4},{8,11},{9,10},{10,... | collective-permute-start | bytes 20 | tf_op jit(solution)/shard_map/ppermute | solution.py:295
  75.2 3.7 %collective-permute-start.18 = (s32[1]{0:T(128)}, s32[1]{0:T(128)}, u32[]{:S(2)}, u32[]{:S(2)}) collective-permute-start(s32[1]{0:T(128)} %bitcast.5), channel_id=1, source_target_pairs={{0,2},{1,3},{2,0},{3,1},{4,6},{5,7},{6,4},{7,5},{8,10},{9,11},{10,... | collective-permute-start | bytes 20 | tf_op jit(solution)/shard_map/ppermute | solution.py:295
  75.8 3.7 %collective-permute-start.17 = (s32[1]{0:T(128)}, s32[1]{0:T(128)}, u32[]{:S(2)}, u32[]{:S(2)}) collective-permute-start(s32[1]{0:T(128)} %bitcast.5), channel_id=1, source_target_pairs={{0,1},{1,0},{2,3},{3,2},{4,5},{5,4},{6,7},{7,6},{8,9},{9,8},{10,11... | collective-permute-start | bytes 20 | tf_op jit(solution)/shard_map/ppermute | solution.py:295
  84.6 2.2 %copy-start.1 = (bf16[256,8192]{1,0:T(8,128)(2,1)S(1)}, bf16[256,8192]{1,0:T(8,128)(2,1)}, u32[]{:S(2)}) copy-start(bf16[256,8192]{1,0:T(8,128)(2,1)} %up_ref.1) | copy-start | bytes 12582916
  86.8 10.9 %copy-start = (bf16[128,5120]{1,0:T(8,128)(2,1)S(1)}, bf16[128,5120]{1,0:T(8,128)(2,1)}, u32[]{:S(2)}) copy-start(bf16[128,5120]{1,0:T(8,128)(2,1)} %x_ref.3) | copy-start | bytes 3932164
  86.8 28.4 %copy-start.10 = (bf16[128,1024]{1,0:T(8,128)(2,1)S(1)}, bf16[128,1024]{1,0:T(8,128)(2,1)}, u32[]{:S(2)}) copy-start(bf16[128,1024]{1,0:T(8,128)(2,1)} %g_ref.1) | copy-start | bytes 786436
  94.2 8.3 %collective-permute-start.24 = (bf16[384,128]{1,0:T(8,128)(2,1)S(1)}, bf16[384,128]{1,0:T(8,128)(2,1)S(1)}, u32[]{:S(2)}, u32[]{:S(2)}) collective-permute-start(bf16[384,128]{1,0:T(8,128)(2,1)S(1)} %get-tuple-element.33), channel_id=1, source_target_pairs={{0,1},{1,0},{2,3},{3,2},{4,5},{5,4},{6,7},{7,6},{8,9},{9,8},{10,11... | collective-permute-start | bytes 294920 | tf_op jit(solution)/shard_map/ppermute | solution.py:295
  95.7 7.8 %collective-permute-start.25 = (bf16[384,128]{1,0:T(8,128)(2,1)S(1)}, bf16[384,128]{1,0:T(8,128)(2,1)S(1)}, u32[]{:S(2)}, u32[]{:S(2)}) collective-permute-start(bf16[384,128]{1,0:T(8,128)(2,1)S(1)} %get-tuple-element.34), channel_id=1, source_target_pairs={{0,2},{1,3},{2,0},{3,1},{4,6},{5,7},{6,4},{7,5},{8,10},{9,11},{10,... | collective-permute-start | bytes 294920 | tf_op jit(solution)/shard_map/ppermute | solution.py:295
  97.6 10.1 %collective-permute-start.26 = (bf16[384,128]{1,0:T(8,128)(2,1)S(1)}, bf16[384,128]{1,0:T(8,128)(2,1)S(1)}, u32[]{:S(2)}, u32[]{:S(2)}) collective-permute-start(bf16[384,128]{1,0:T(8,128)(2,1)S(1)} %get-tuple-element.35), channel_id=1, source_target_pairs={{0,3},{1,2},{2,1},{3,0},{4,7},{5,6},{6,5},{7,4},{8,11},{9,10},{10,... | collective-permute-start | bytes 294920 | tf_op jit(solution)/shard_map/ppermute | solution.py:295
  99.5 12.4 %collective-permute-start.27 = (bf16[384,128]{1,0:T(8,128)(2,1)S(1)}, bf16[384,128]{1,0:T(8,128)(2,1)S(1)}, u32[]{:S(2)}, u32[]{:S(2)}) collective-permute-start(bf16[384,128]{1,0:T(8,128)(2,1)S(1)} %get-tuple-element.36), channel_id=1, source_target_pairs={{0,4},{1,5},{2,6},{3,7},{4,0},{5,1},{6,2},{7,3},{8,12},{9,13},{10,... | collective-permute-start | bytes 294920 | tf_op jit(solution)/shard_map/ppermute | solution.py:295
  102.5 11.3 %collective-permute-start.28 = (bf16[384,128]{1,0:T(8,128)(2,1)S(1)}, bf16[384,128]{1,0:T(8,128)(2,1)S(1)}, u32[]{:S(2)}, u32[]{:S(2)}) collective-permute-start(bf16[384,128]{1,0:T(8,128)(2,1)S(1)} %get-tuple-element.37), channel_id=1, source_target_pairs={{0,5},{1,4},{2,7},{3,6},{4,1},{5,0},{6,3},{7,2},{8,13},{9,12},{10,... | collective-permute-start | bytes 294920 | tf_op jit(solution)/shard_map/ppermute | solution.py:295
  103.5 10.3 %collective-permute-start.29 = (bf16[384,128]{1,0:T(8,128)(2,1)S(1)}, bf16[384,128]{1,0:T(8,128)(2,1)S(1)}, u32[]{:S(2)}, u32[]{:S(2)}) collective-permute-start(bf16[384,128]{1,0:T(8,128)(2,1)S(1)} %get-tuple-element.38), channel_id=1, source_target_pairs={{0,6},{1,7},{2,4},{3,5},{4,2},{5,3},{6,0},{7,1},{8,14},{9,15},{10,... | collective-permute-start | bytes 294920 | tf_op jit(solution)/shard_map/ppermute | solution.py:295
  107.7 7.5 %collective-permute-start.30 = (bf16[384,128]{1,0:T(8,128)(2,1)S(1)}, bf16[384,128]{1,0:T(8,128)(2,1)S(1)}, u32[]{:S(2)}, u32[]{:S(2)}) collective-permute-start(bf16[384,128]{1,0:T(8,128)(2,1)S(1)} %get-tuple-element.39), channel_id=1, source_target_pairs={{0,7},{1,6},{2,5},{3,4},{4,3},{5,2},{6,1},{7,0},{8,15},{9,14},{10,... | collective-permute-start | bytes 294920 | tf_op jit(solution)/shard_map/ppermute | solution.py:295
  117.2 7.7 %collective-permute-start.32 = (bf16[384,128]{1,0:T(8,128)(2,1)S(1)}, bf16[384,128]{1,0:T(8,128)(2,1)S(1)}, u32[]{:S(2)}, u32[]{:S(2)}) collective-permute-start(bf16[384,128]{1,0:T(8,128)(2,1)S(1)} %get-tuple-element.42), channel_id=1, source_target_pairs={{0,1},{1,0},{2,3},{3,2},{4,5},{5,4},{6,7},{7,6},{8,9},{9,8},{10,11... | collective-permute-start | bytes 294920 | tf_op jit(solution)/shard_map/ppermute | solution.py:295
  118.3 9.1 %collective-permute-start.33 = (bf16[384,128]{1,0:T(8,128)(2,1)S(1)}, bf16[384,128]{1,0:T(8,128)(2,1)S(1)}, u32[]{:S(2)}, u32[]{:S(2)}) collective-permute-start(bf16[384,128]{1,0:T(8,128)(2,1)S(1)} %get-tuple-element.43), channel_id=1, source_target_pairs={{0,2},{1,3},{2,0},{3,1},{4,6},{5,7},{6,4},{7,5},{8,10},{9,11},{10,... | collective-permute-start | bytes 294920 | tf_op jit(solution)/shard_map/ppermute | solution.py:295
  120.8 4.0 %collective-permute-start.31 = (s32[8]{0:T(128)S(1)}, s32[8]{0:T(128)S(1)}, u32[]{:S(2)}, u32[]{:S(2)}) collective-permute-start(s32[8]{0:T(128)S(1)} %concatenate.15.rows), channel_id=1, source_target_pairs={{0,8},{8,0},{1,9},{9,1},{2,10},{10,2},{3,11},{11,3},{4,12},{12,4},... | collective-permute-start | bytes 104 | tf_op jit(solution)/shard_map/ppermute | solution.py:298
  120.8 8.9 %collective-permute-start.34 = (bf16[384,128]{1,0:T(8,128)(2,1)S(1)}, bf16[384,128]{1,0:T(8,128)(2,1)S(1)}, u32[]{:S(2)}, u32[]{:S(2)}) collective-permute-start(bf16[384,128]{1,0:T(8,128)(2,1)S(1)} %get-tuple-element.44), channel_id=1, source_target_pairs={{0,3},{1,2},{2,1},{3,0},{4,7},{5,6},{6,5},{7,4},{8,11},{9,10},{10,... | collective-permute-start | bytes 294920 | tf_op jit(solution)/shard_map/ppermute | solution.py:295
  120.9 15.7 %collective-permute-start.35 = (bf16[384,128]{1,0:T(8,128)(2,1)S(1)}, bf16[384,128]{1,0:T(8,128)(2,1)S(1)}, u32[]{:S(2)}, u32[]{:S(2)}) collective-permute-start(bf16[384,128]{1,0:T(8,128)(2,1)S(1)} %get-tuple-element.45), channel_id=1, source_target_pairs={{0,4},{1,5},{2,6},{3,7},{4,0},{5,1},{6,2},{7,3},{8,12},{9,13},{10,... | collective-permute-start | bytes 294920 | tf_op jit(solution)/shard_map/ppermute | solution.py:295
  124.9 14.5 %collective-permute-start.36 = (bf16[384,128]{1,0:T(8,128)(2,1)S(1)}, bf16[384,128]{1,0:T(8,128)(2,1)S(1)}, u32[]{:S(2)}, u32[]{:S(2)}) collective-permute-start(bf16[384,128]{1,0:T(8,128)(2,1)S(1)} %get-tuple-element.46), channel_id=1, source_target_pairs={{0,5},{1,4},{2,7},{3,6},{4,1},{5,0},{6,3},{7,2},{8,13},{9,12},{10,... | collective-permute-start | bytes 294920 | tf_op jit(solution)/shard_map/ppermute | solution.py:295
  124.9 14.4 %collective-permute-start.37 = (bf16[384,128]{1,0:T(8,128)(2,1)S(1)}, bf16[384,128]{1,0:T(8,128)(2,1)S(1)}, u32[]{:S(2)}, u32[]{:S(2)}) collective-permute-start(bf16[384,128]{1,0:T(8,128)(2,1)S(1)} %get-tuple-element.47), channel_id=1, source_target_pairs={{0,6},{1,7},{2,4},{3,5},{4,2},{5,3},{6,0},{7,1},{8,14},{9,15},{10,... | collective-permute-start | bytes 294920 | tf_op jit(solution)/shard_map/ppermute | solution.py:295
  127.4 12.5 %collective-permute-start.38 = (bf16[384,128]{1,0:T(8,128)(2,1)S(1)}, bf16[384,128]{1,0:T(8,128)(2,1)S(1)}, u32[]{:S(2)}, u32[]{:S(2)}) collective-permute-start(bf16[384,128]{1,0:T(8,128)(2,1)S(1)} %get-tuple-element.48), channel_id=1, source_target_pairs={{0,7},{1,6},{2,5},{3,4},{4,3},{5,2},{6,1},{7,0},{8,15},{9,14},{10,... | collective-permute-start | bytes 294920 | tf_op jit(solution)/shard_map/ppermute | solution.py:295
  129.7 31.5 %collective-permute-start.16 = (f32[128,512]{1,0:T(8,128)S(1)}, f32[128,512]{1,0:T(8,128)S(1)}, u32[]{:S(2)}, u32[]{:S(2)}) collective-permute-start(f32[128,512]{1,0:T(8,128)S(1)} %get-tuple-element.54), channel_id=1, source_target_pairs={{0,8},{8,0},{1,9},{9,1},{2,10},{10,2},{3,11},{11,3},{4,12},{12,4},... | collective-permute-start | bytes 786440 | tf_op jit(solution)/shard_map/ppermute | solution.py:298
  136.6 3.4 %collective-permute-start.39 = (bf16[384,128]{1,0:T(8,128)(2,1)S(1)}, bf16[384,128]{1,0:T(8,128)(2,1)S(1)}, u32[]{:S(2)}, u32[]{:S(2)}) collective-permute-start(bf16[384,128]{1,0:T(8,128)(2,1)S(1)} %get-tuple-element.41.rest_0_), channel_id=1, source_target_pairs={{0,8},{8,0},{1,9},{9,1},{2,10},{10,2},{3,11},{11,3},{4,12},{12,4},... | collective-permute-start | bytes 294920 | tf_op jit(solution)/shard_map/ppermute | solution.py:298
  139.3 1.3 collective-permute-start.40
  139.3 1.5 collective-permute-start.41
  139.9 1.3 collective-permute-start.42
  139.9 14.9 %collective-permute-start.43 = (bf16[384,128]{1,0:T(8,128)(2,1)S(1)}, bf16[384,128]{1,0:T(8,128)(2,1)S(1)}, u32[]{:S(2)}, u32[]{:S(2)}) collective-permute-start(bf16[384,128]{1,0:T(8,128)(2,1)S(1)} %collective-permute-done.35.rest_4_), channel_id=1, source_target_pairs={{0,8},{8,0},{1,9},{9,1},{2,10},{10,2},{3,11},{11,3},{4,12},{12,4},... | collective-permute-start | bytes 294920 | tf_op jit(solution)/shard_map/ppermute | solution.py:298
  140.6 14.2 %collective-permute-start.44 = (bf16[384,128]{1,0:T(8,128)(2,1)S(1)}, bf16[384,128]{1,0:T(8,128)(2,1)S(1)}, u32[]{:S(2)}, u32[]{:S(2)}) collective-permute-start(bf16[384,128]{1,0:T(8,128)(2,1)S(1)} %collective-permute-done.36.rest_5_), channel_id=1, source_target_pairs={{0,8},{8,0},{1,9},{9,1},{2,10},{10,2},{3,11},{11,3},{4,12},{12,4},... | collective-permute-start | bytes 294920 | tf_op jit(solution)/shard_map/ppermute | solution.py:298
  140.8 14.1 %collective-permute-start.45 = (bf16[384,128]{1,0:T(8,128)(2,1)S(1)}, bf16[384,128]{1,0:T(8,128)(2,1)S(1)}, u32[]{:S(2)}, u32[]{:S(2)}) collective-permute-start(bf16[384,128]{1,0:T(8,128)(2,1)S(1)} %collective-permute-done.37.rest_6_), channel_id=1, source_target_pairs={{0,8},{8,0},{1,9},{9,1},{2,10},{10,2},{3,11},{11,3},{4,12},{12,4},... | collective-permute-start | bytes 294920 | tf_op jit(solution)/shard_map/ppermute | solution.py:298
  141.2 13.7 %collective-permute-start.46 = (bf16[384,128]{1,0:T(8,128)(2,1)S(1)}, bf16[384,128]{1,0:T(8,128)(2,1)S(1)}, u32[]{:S(2)}, u32[]{:S(2)}) collective-permute-start(bf16[384,128]{1,0:T(8,128)(2,1)S(1)} %collective-permute-done.38.rest_7_), channel_id=1, source_target_pairs={{0,8},{8,0},{1,9},{9,1},{2,10},{10,2},{3,11},{11,3},{4,12},{12,4},... | collective-permute-start | bytes 294920 | tf_op jit(solution)/shard_map/ppermute | solution.py:298

commit v2 on v1

--- a/solution.py
+++ b/solution.py
@@ -117,11 +117,11 @@
         xs_ref[k, rows:] = dot(x, odd).astype(jnp.bfloat16)
 
 
-def gather_kernel(count, down_chunks, up_chunks, rows, down_ref, up_ref, *rest):
+def gather_kernel(first, count, down_chunks, up_chunks, rows, down_ref, up_ref, _, *rest):
     outs, (down_buf, up_buf, flat, sems) = rest[:count], rest[count:]
     copies = []
     for s in range(count):
-        start = pl.multiple_of((rows[s] // GROUP_ROWS) * GROUP_ROWS, GROUP_ROWS)
+        start = pl.multiple_of((rows[first + s] // GROUP_ROWS) * GROUP_ROWS, GROUP_ROWS)
         a = pltpu.make_async_copy(down_ref.at[pl.ds(start, GROUP_ROWS)], down_buf.at[s], sems.at[2 * s])
         b = pltpu.make_async_copy(up_ref.at[pl.ds(start, GROUP_ROWS)], up_buf.at[s], sems.at[2 * s + 1])
         a.start()
@@ -129,7 +129,7 @@
         copies.append((a, b))
     step = 8
     for s in range(count):
-        row = rows[s] % GROUP_ROWS
+        row = rows[first + s] % GROUP_ROWS
         upper = row >= 8
         sub = row % 8
         copies[s][0].wait()
@@ -170,7 +170,7 @@
 
 
 def adapter_kernel(count, down_chunks, where, xs_ref, g_ref, *rest):
-    pieces, outs, (lifted_ref, up_panel) = rest[:count], rest[count:2 * count], rest[2 * count:]
+    pieces, outs, (lifted_ref, up_panel) = rest[:count], rest[count + 1:2 * count + 1], rest[2 * count + 1:]
     me = where[0]
     rows = g_ref.shape[0]
     across = g_ref.shape[1] // LANES
@@ -258,25 +258,19 @@
                 copy.wait()
 
 
-def base_kernel(outer, where, x_refs, w_ref, arrivals, own_ref, other_ref, acc):
-    z, half = where[0], where[1]
-    width = arrivals[0][3].shape[1]
-
-    def left(block):
-        return jnp.concatenate([ref[block] for ref in x_refs], axis=0)
-
-    acc[...] = dot(left(z), w_ref[...])
-    for direction, distance, crossed, ref in arrivals:
-        source = z - direction * distance
-
-        @pl.when((source >= 0) & (source < outer))
-        def _():
-            at = pl.multiple_of((half if not crossed else 1 - half) * width, LANES)
-            acc[:, pl.ds(at, width)] += dot(left(source), ref[...])
-
+def base_kernel(*refs):
+    x_refs, w_ref, own_ref, other_ref = refs[:4], refs[4], refs[-2], refs[-1]
+    halves, _, width = w_ref.shape
+    outer, _, depth = x_refs[0].shape
     rows = own_ref.shape[0]
-    own_ref[...] = acc[:rows]
-    other_ref[...] = acc[rows:]
+    total = [0.0] * halves
+    for k in range(outer):
+        left = jnp.concatenate([ref[k] for ref in x_refs], axis=0)
+        for h in range(halves):
+            total[h] += dot(left, w_ref[h, k * depth:(k + 1) * depth, :])
+    for h in range(halves):
+        own_ref[:, h * width:(h + 1) * width] = total[h][:rows]
+        other_ref[:, h * width:(h + 1) * width] = total[h][rows:]
 
 
 def fast_body(tokens, cotangent, frozen_value, down_store, up_store, block_adapter, adapter_slot):
@@ -298,32 +292,15 @@
         return lax.ppermute(value, "dp", [(0, 1), (1, 0)])
 
     row = store_rows(block_adapter, adapter_slot)
-    rows = jnp.concatenate([row] + [exchange(row, s) for s in range(1, group)])
+    asked = [row] + [exchange(row, s) for s in range(1, group)]
+    place = jnp.arange(2 * group, dtype=jnp.int32)
+    rows = sum(jnp.where(place[:group] == s, asked[s], 0) for s in range(group))
     rows_core = other_core(rows)
 
     width = frozen_value.shape[1] // parts
     half = lax.dynamic_slice_in_dim(frozen_value, part * width, width, axis=1)
-    arrivals = []
-    for direction in (1, -1):
-        moving = half
-        for distance in range(1, outer):
-            steps = [
-                (t, t + 2 * direction)
-                for t in range(group)
-                if 0 <= t // 2 + direction < outer and 0 <= t // 2 - direction * (distance - 1) < outer
-            ]
-            moving = lax.ppermute(moving, "tensor", steps)
-            arrivals.append((direction, distance, False, moving))
-            crossing = [
-                (a * group + t, (1 - a) * group + t)
-                for a in range(parts)
-                for t in range(group)
-                if 0 <= t // 2 - direction * distance < outer
-            ]
-            arrivals.append(
-                (direction, distance, True, lax.ppermute(moving, ("parts", "tensor"), crossing))
-            )
-
+    lines = [list(range(0, group, 2)), list(range(1, group, 2))]
+    half = lax.all_gather(half, "tensor", axis_index_groups=lines, axis=0, tiled=True)
     block = jax.ShapeDtypeStruct((outer, token_rows, slice_width), jnp.bfloat16)
     x_mine, x_theirs = pl.pallas_call(
         split_kernel, out_shape=(block, block), in_specs=[SMEM, VMEM], out_specs=(VMEM, VMEM),
@@ -338,21 +315,28 @@
         in_specs=[VMEM], out_specs=VMEM, name="pair_columns", compiler_params=LIMIT,
     )(tokens)
 
-    sent = pl.pallas_call(
-        functools.partial(gather_kernel, group, down_chunks, up_chunks),
-        out_shape=[piece] * group,
-        in_specs=[SMEM, ANY, ANY],
-        out_specs=[VMEM] * group,
-        scratch_shapes=[
-            pltpu.VMEM((group, GROUP_ROWS, down_store.shape[1]), jnp.bfloat16),
-            pltpu.VMEM((group, GROUP_ROWS, up_store.shape[1]), jnp.bfloat16),
-            pltpu.VMEM((down_chunks * 8, LANES), jnp.float32),
-            pltpu.SemaphoreType.DMA((2 * group,)),
-        ],
-        compiler_params=LIMIT,
-        name="pick_panels",
-    )(rows, down_store, up_store)
+    def pick(first, count, after):
+        return pl.pallas_call(
+            functools.partial(gather_kernel, first, count, down_chunks, up_chunks),
+            out_shape=[piece] * count,
+            in_specs=[SMEM, ANY, ANY, ANY],
+            out_specs=[VMEM] * count,
+            scratch_shapes=[
+                pltpu.VMEM((count, GROUP_ROWS, down_store.shape[1]), jnp.bfloat16),
+                pltpu.VMEM((count, GROUP_ROWS, up_store.shape[1]), jnp.bfloat16),
+                pltpu.VMEM((down_chunks * 8, LANES), jnp.float32),
+                pltpu.SemaphoreType.DMA((2 * count,)),
+            ],
+            compiler_params=LIMIT,
+            name="pick_panels",
+        )(rows, down_store, up_store, after)
+
+    sent = pick(0, group // 2, rows)
+    sent += pick(group // 2, group // 2, sent[0])
     panels = [sent[0]] + [exchange(sent[s], s) for s in range(1, group)]
+
+    half, _ = lax.optimization_barrier((half, sent[-1]))
+    projection = lax.all_gather(half, "parts", axis=0)
 
     owned_groups = ADAPTERS // lax.axis_size("dp") // 8
     down_shape = jax.ShapeDtypeStruct((owned_groups, down_chunks, 8, 1, LANES), jnp.float32)
@@ -361,17 +345,17 @@
         zero_kernel, out_shape=(down_shape, up_shape), in_specs=[ANY], out_specs=(ANY, ANY),
         scratch_shapes=[pltpu.VMEM((up_chunks, 8, 1, LANES), jnp.float32), pltpu.SemaphoreType.DMA((2,))],
         compiler_params=LIMIT, name="clear_rows",
-    )(sent[0])
+    )(sent[-1])
 
     results = pl.pallas_call(
         functools.partial(adapter_kernel, group, down_chunks),
         out_shape=[piece] * group + [jax.ShapeDtypeStruct((token_rows, VALUE_OUTPUTS), jnp.float32)],
-        in_specs=[SMEM] + [VMEM] * (2 + group),
+        in_specs=[SMEM] + [VMEM] * (2 + group) + [ANY],
         out_specs=[VMEM] * (group + 1),
         scratch_shapes=[pltpu.VMEM((2 * R, VALUE_OUTPUTS), jnp.float32)],
         compiler_params=LIMIT,
         name="adapter",
-    )(here, xs, cotangent, *panels)
+    )(here, xs, cotangent, *panels, down_zero)
     terms, lifted = results[:group], results[group]
     back = [terms[0]] + [exchange(terms[s], s) for s in range(1, group)]
     back_core = [other_core(term) for term in back]
@@ -395,21 +379,15 @@
     grad_down = grad_down.reshape(owned_groups, down_chunks, 8, LANES).transpose(0, 2, 1, 3)
     grad_up = grad_up.reshape(owned_groups, up_chunks, 8, LANES).transpose(0, 2, 1, 3)
 
-    def base(where, *refs):
-        x_refs, w_ref, got = refs[:4], refs[4], refs[5:5 + len(arrivals)]
-        tagged = [a[:3] + (ref,) for a, ref in zip(arrivals, got)]
-        base_kernel(outer, where, x_refs, w_ref, tagged, *refs[5 + len(arrivals):])
-
     sums = jax.ShapeDtypeStruct((2 * token_rows, frozen_value.shape[1]), jnp.float32)
     own, other = pl.pallas_call(
-        base,
+        base_kernel,
         out_shape=(sums, sums),
-        in_specs=[SMEM] + [VMEM] * (5 + len(arrivals)),
+        in_specs=[VMEM] * 5 + [ANY],
         out_specs=(VMEM, VMEM),
-        scratch_shapes=[pltpu.VMEM((4 * token_rows, frozen_value.shape[1]), jnp.float32)],
         compiler_params=LIMIT,
         name="frozen_part",
-    )(jnp.stack([z, part]), *x_blocks, frozen_value, *[a[3] for a in arrivals])
+    )(*x_blocks, projection, terms[0])
     columns = own + exchange(other, 1)
     kept, gone = columns[:token_rows], columns[token_rows:]
     got = other_core(gone)

time: 164 us -> 158 us (0.963)
  starting transfers between devices: 70.7 us -> 45.1 us
  between operations: 1.61 us -> 15 us
  other arithmetic: 1.73 us -> 7.38 us
  Pallas kernels: 33.3 us -> 35.3 us
    ppermute x12 -> x0, starting transfers between devices: 25.7 us -> none  [the longest x6 14.2 us: fast_body(): lax.ppermute(moving, ('parts', 'tensor'), crossing)]
    ppermute x12 -> x0, waiting for transfers between devices: 16.7 us -> none  [the longest x6 8.87 us: fast_body(): moving = lax.ppermute(moving, 'tensor', steps)]
    ppermute x23, waiting for transfers between devices: 16.9 us -> 32.5 us  [exchange(): return lax.ppermute(value, 'tensor', [(t, t ^ s) for t in range(group)])]
    concatenate x2 -> x0, local copies, waits for them, and re-layouts: 10.2 us -> none  [the longest x1 5.09 us: fast_body(): jnp.concatenate([rows, rows_core])]
    unnamed x24 -> x62, local copies, waits for them, and re-layouts: 9.47 us -> 17.8 us
    add x0 -> x1, other arithmetic: none -> 5.04 us  [fast_body(): sum((jnp.where(place[:group] == s, asked[s], 0) for s in range(group)))]
    pallas_call x2 -> x3, Pallas kernels: 12.3 us -> 13.6 us  [the longest x2 10.4 us: pick(): pl.pallas_call(functools.partial(gather_kernel, first, count, down_chunks...]
  transfers between devices with their start and end apart: 47 -> 37, of which waited for: 14 -> 12; matrix products, arithmetic and copies ran while one was open for 7% -> 5% of each run, Pallas kernels for 18% -> 21%
where the time goes in v2:
time: 158 us; the launch traced here: 156 us
  starting transfers between devices  45.1 us (29%)
  Pallas kernels  35.3 us (22%)
  waiting for transfers between devices  33.9 us (21%)
  local copies, waits for them, and re-layouts  19.3 us (12%)
  between operations  15 us (9%)
  other arithmetic  7.38 us (5%)
    ppermute x23, starting transfers between devices, exchange(): return lax.ppermute(value, 'tensor', [(t, t ^ s) for t in range(group)])  43.3 us
    ppermute x23, waiting for transfers between devices, exchange(): return lax.ppermute(value, 'tensor', [(t, t ^ s) for t in range(group)])  32.5 us
    unnamed x62, local copies, waits for them, and re-layouts  17.8 us
    pallas_call x2, Pallas kernels, pick(): pl.pallas_call(functools.partial(gather_kernel, first, count, down_chunks...  10.4 us
    pallas_call x1, Pallas kernels, fast_body(): pl.pallas_call(zero_kernel, out_shape=(down_shape, up_shape), in_specs=[A...  8.42 us
    pallas_call x1, Pallas kernels, fast_body(): pl.pallas_call(functools.partial(scatter_kernel, 2 * group, down_chunks,...  6.51 us
    add x1, other arithmetic, fast_body(): sum((jnp.where(place[:group] == s, asked[s], 0) for s in range(group)))  5.04 us
  transfers between devices with their start and end apart: 37, of which 12 were waited for; matrix products, arithmetic and copies ran while one was open for 5% of the time, Pallas kernels for 21%

profile of v2, /device:TPU:0, one launch (start us, length us, event | category | flops | bytes accessed | tf_op | source)
XLA Modules:
  0.0 156.0 jit_solution(9012921207280058043)
XLA Ops:
  7.2 1.0 copy-done
  8.3 0.7 constant_dynamic-slice_fusion
  9.7 1.3 fusion.2
  11.0 6.0 %collective-permute-start.9 = (s32[1]{0:T(128)}, s32[1]{0:T(128)}, u32[]{:S(2)}, u32[]{:S(2)}) collective-permute-start(s32[1]{0:T(128)} %bitcast.2), channel_id=1, source_target_pairs={{0,7},{1,6},{2,5},{3,4},{4,3},{5,2},{6,1},{7,0},{8,15},{9,14},{10,... | collective-permute-start | bytes 20 | tf_op jit(solution)/shard_map/ppermute | solution.py:289
  17.2 0.8 collective-permute-start.7
  18.0 1.9 %collective-permute-start.6 = (s32[1]{0:T(128)}, s32[1]{0:T(128)}, u32[]{:S(2)}, u32[]{:S(2)}) collective-permute-start(s32[1]{0:T(128)} %bitcast.2), channel_id=1, source_target_pairs={{0,4},{1,5},{2,6},{3,7},{4,0},{5,1},{6,2},{7,3},{8,12},{9,13},{10,... | collective-permute-start | bytes 20 | tf_op jit(solution)/shard_map/ppermute | solution.py:289
  20.0 2.4 %collective-permute-start.5 = (s32[1]{0:T(128)}, s32[1]{0:T(128)}, u32[]{:S(2)}, u32[]{:S(2)}) collective-permute-start(s32[1]{0:T(128)} %bitcast.2), channel_id=1, source_target_pairs={{0,3},{1,2},{2,1},{3,0},{4,7},{5,6},{6,5},{7,4},{8,11},{9,10},{10,... | collective-permute-start | bytes 20 | tf_op jit(solution)/shard_map/ppermute | solution.py:289
  22.3 0.8 collective-permute-start.4
  23.5 1.0 collective-permute-done.5
  24.5 1.6 %collective-permute-done.4 = s32[1]{0:T(128)} collective-permute-done((s32[1]{0:T(128)}, s32[1]{0:T(128)}, u32[]{:S(2)}, u32[]{:S(2)}) %collective-permute-start.4) | collective-permute-done | bytes 36 | tf_op jit(solution)/shard_map/ppermute | solution.py:289
  26.1 0.8 collective-permute-done.3
  26.9 5.0 %fusion.9.rows._ = s32[8]{0:T(128)S(1)} fusion(s32[16]{0:T(128)S(1)} %iota.22, s32[]{:T(128)} %bitcast.9, s32[]{:T(128)} %bitcast.8, s32[]{:T(128)} %bitcast.7, s32[]{:T(128)} %bitcast.6, s32[]{:T(128)} %bitcast.5, s32[]{:T(128)} %bitcast.4, s32[]{:T(128)} %bitcast.3, s32[]{:T(128)} %fusion.2), kind=kLoop, calls=%fused_computation.19 | loop fusion | flops 184 | bytes 96 | tf_op jit(solution)/shard_map/add | solution.py:297
  31.9 2.2 %copy-done.2 = bf16[256,8192]{1,0:T(8,128)(2,1)S(1)} copy-done((bf16[256,8192]{1,0:T(8,128)(2,1)S(1)}, bf16[256,8192]{1,0:T(8,128)(2,1)}, u32[]{:S(2)}) %copy-start.2) | copy-done | bytes 4194328
  34.2 5.3 %pick_panels.2 = (bf16[384,128]{1,0:T(8,128)(2,1)S(1)}, bf16[384,128]{1,0:T(8,128)(2,1)S(1)}, bf16[384,128]{1,0:T(8,128)(2,1)}, bf16[384,128]{1,0:T(8,128)(2,1)}) custom-call(s32[8]{0:T(128)S(1)} %fusion.9.rows._, bf16[256,40960]{1,0:T(8,128)(2,1)} %down_ref.3, bf16[256,8192]{1,0:T(8,128)(2,1)S(1)} %copy-done.2, s32[8]{0:T(128)S(1)} %fusion.9.rows._), custom_call_target="tpu_custom_call" | custom-call | tf_op jit(solution)/shard_map/pick_panels/pallas_call | solution.py:319
  39.4 5.2 %pick_panels.3 = (bf16[384,128]{1,0:T(8,128)(2,1)}, bf16[384,128]{1,0:T(8,128)(2,1)S(1)}, bf16[384,128]{1,0:T(8,128)(2,1)S(1)}, bf16[384,128]{1,0:T(8,128)(2,1)S(1)}) custom-call(s32[8]{0:T(128)S(1)} %fusion.9.rows._, bf16[256,40960]{1,0:T(8,128)(2,1)} %down_ref.3, bf16[256,8192]{1,0:T(8,128)(2,1)S(1)} %copy-done.2, ...), custom_call_target="tpu_custom_call" | custom-call | tf_op jit(solution)/shard_map/pick_panels/pallas_call | solution.py:319
  44.6 0.6 copy-done.6
  45.2 0.6 copy-done.13
  45.9 0.6 copy-done.15
  46.5 0.6 copy-done.16
  47.2 2.5 %split_tokens.1 = (bf16[4,128,640]{2,1,0:T(8,128)(2,1)}, bf16[4,128,640]{2,1,0:T(8,128)(2,1)}) custom-call(s32[1]{0:T(128)} %bitcast.where, bf16[128,5120]{1,0:T(8,128)(2,1)} %x_ref.3), custom_call_target="tpu_custom_call" | custom-call | tf_op jit(solution)/shard_map/split_tokens/pallas_call | solution.py:305
  50.0 14.1 %collective-permute-done.1.refs_2_ = bf16[4,128,640]{2,1,0:T(8,128)(2,1)S(1)} collective-permute-done((bf16[4,128,640]{2,1,0:T(8,128)(2,1)}, bf16[4,128,640]{2,1,0:T(8,128)(2,1)S(1)}, u32[]{:S(2)}, u32[]{:S(2)}) %collective-permute-start.1) | collective-permute-done | bytes 655392 | tf_op jit(solution)/shard_map/ppermute | solution.py:289
  64.1 1.5 collective-permute-start.10
  65.6 1.2 collective-permute-start.11
  66.8 0.8 collective-permute-start.12
  67.6 1.7 %collective-permute-done.10.rest_1_ = bf16[384,128]{1,0:T(8,128)(2,1)S(1)} collective-permute-done((bf16[384,128]{1,0:T(8,128)(2,1)S(1)}, bf16[384,128]{1,0:T(8,128)(2,1)S(1)}, u32[]{:S(2)}, u32[]{:S(2)}) %collective-permute-start.10) | collective-permute-done | bytes 98336 | tf_op jit(solution)/shard_map/ppermute | solution.py:289
  69.3 0.6 copy-done.11
  70.0 2.2 %collective-permute-start.13 = (bf16[384,128]{1,0:T(8,128)(2,1)}, bf16[384,128]{1,0:T(8,128)(2,1)}, u32[]{:S(2)}, u32[]{:S(2)}) collective-permute-start(bf16[384,128]{1,0:T(8,128)(2,1)} %get-tuple-element.37), channel_id=1, source_target_pairs={{0,4},{1,5},{2,6},{3,7},{4,0},{5,1},{6,2},{7,3},{8,12},{9,13},{10,... | collective-permute-start | bytes 294920 | tf_op jit(solution)/shard_map/ppermute | solution.py:289
  72.2 1.8 %pair_columns.1.xs_ref = bf16[8,256,320]{2,1,0:T(8,128)(2,1)S(1)} custom-call(bf16[128,5120]{1,0:T(8,128)(2,1)S(1)} %copy-done.3), custom_call_target="tpu_custom_call" | custom-call | tf_op jit(solution)/shard_map/pair_columns/pallas_call | solution.py:312
  74.0 2.4 %collective-permute-start.16 = (bf16[384,128]{1,0:T(8,128)(2,1)}, bf16[384,128]{1,0:T(8,128)(2,1)S(1)}, u32[]{:S(2)}, u32[]{:S(2)}) collective-permute-start(bf16[384,128]{1,0:T(8,128)(2,1)} %copy-done.13), channel_id=1, source_target_pairs={{0,7},{1,6},{2,5},{3,4},{4,3},{5,2},{6,1},{7,0},{8,15},{9,14},{10,... | collective-permute-start | bytes 294920 | tf_op jit(solution)/shard_map/ppermute | solution.py:289
  76.4 1.7 %collective-permute-start.14 = (bf16[384,128]{1,0:T(8,128)(2,1)}, bf16[384,128]{1,0:T(8,128)(2,1)S(1)}, u32[]{:S(2)}, u32[]{:S(2)}) collective-permute-start(bf16[384,128]{1,0:T(8,128)(2,1)} %copy-done.16), channel_id=1, source_target_pairs={{0,5},{1,4},{2,7},{3,6},{4,1},{5,0},{6,3},{7,2},{8,13},{9,12},{10,... | collective-permute-start | bytes 294920 | tf_op jit(solution)/shard_map/ppermute | solution.py:289
  78.1 7.1 %collective-permute-start.15 = (bf16[384,128]{1,0:T(8,128)(2,1)}, bf16[384,128]{1,0:T(8,128)(2,1)S(1)}, u32[]{:S(2)}, u32[]{:S(2)}) collective-permute-start(bf16[384,128]{1,0:T(8,128)(2,1)} %copy-done.15), channel_id=1, source_target_pairs={{0,6},{1,7},{2,4},{3,5},{4,2},{5,3},{6,0},{7,1},{8,14},{9,15},{10,... | collective-permute-start | bytes 294920 | tf_op jit(solution)/shard_map/ppermute | solution.py:289
  85.3 0.9 copy-done.14
  86.2 8.4 %clear_rows.1 = (f32[16,320,8,1,128]{4,3,2,1,0:T(1,128)}, f32[16,64,8,1,128]{4,3,2,1,0:T(1,128)}) custom-call(bf16[384,128]{1,0:T(8,128)(2,1)S(1)} %copy-done.14), custom_call_target="tpu_custom_call" | custom-call | tf_op jit(solution)/shard_map/clear_rows/pallas_call | solution.py:344
  94.7 0.9 copy-done.7
  95.5 0.9 copy-done.10
  96.5 0.9 copy-done.12
  97.4 2.5 %adapter.1 = (bf16[384,128]{1,0:T(8,128)(2,1)S(1)}, bf16[384,128]{1,0:T(8,128)(2,1)S(1)}, bf16[384,128]{1,0:T(8,128)(2,1)S(1)}, bf16[384,128]{1,0:T(8,128)(2,1)S...) custom-call(s32[4]{0:T(128)S(1)} %pad_add_fusion.where, ...), custom_call_target="tpu_custom_call" | custom-call | tf_op jit(solution)/shard_map/adapter/pallas_call | solution.py:350
  99.9 0.6 copy-done.8
  100.6 0.6 copy-done.17
  101.2 0.6 copy-done.19
  101.8 0.6 copy-done.21
  102.5 0.6 copy-done.23
  103.1 0.6 copy-done.25
  103.7 0.6 copy-done.27
  104.4 0.6 copy-done.29
  105.0 1.7 %copy-done.4 = bf16[5120,256]{1,0:T(8,128)(2,1)S(1)} copy-done((bf16[5120,256]{1,0:T(8,128)(2,1)S(1)}, bf16[5120,256]{1,0:T(8,128)(2,1)}, u32[]{:S(2)}) %copy-start.4) | copy-done | bytes 2621464
  106.8 0.9 copy-done.9
  107.7 3.1 %frozen_part.1 = (f32[256,512]{1,0:T(8,128)S(1)}, f32[256,512]{1,0:T(8,128)S(1)}) custom-call(bf16[4,128,640]{2,1,0:T(8,128)(2,1)S(1)} %copy-done.5, bf16[4,128,640]{2,1,0:T(8,128)(2,1)} %collective-permute-done.refs_1_, bf16[4,128,640]{2,1,0:T(8,128)(2,1)S(1)} %collective-permute-done.1.refs_2_, bf16[4,128,640]{2,1,0:T(8,128)(2,1)} %collective-permute-done.2.refs_3_, ...), custom_call_target="tpu_custom_call" | custom-call | tf_op jit(solution)/shard_map/frozen_part/pallas_call | solution.py:383
  110.8 2.5 %collective-permute-start.17 = (f32[256,512]{1,0:T(8,128)S(1)}, f32[256,512]{1,0:T(8,128)S(1)}, u32[]{:S(2)}, u32[]{:S(2)}) collective-permute-start(f32[256,512]{1,0:T(8,128)S(1)} %get-tuple-element.43), channel_id=1, source_target_pairs={{0,1},{1,0},{2,3},{3,2},{4,5},{5,4},{6,7},{7,6},{8,9},{9,8},{10,11... | collective-permute-start | bytes 1572872 | tf_op jit(solution)/shard_map/ppermute | solution.py:289
  113.5 3.3 %collective-permute-start.22 = (bf16[384,128]{1,0:T(8,128)(2,1)S(1)}, bf16[384,128]{1,0:T(8,128)(2,1)S(1)}, u32[]{:S(2)}, u32[]{:S(2)}) collective-permute-start(bf16[384,128]{1,0:T(8,128)(2,1)S(1)} %copy-done.26), channel_id=1, source_target_pairs={{0,3},{1,2},{2,1},{3,0},{4,7},{5,6},{6,5},{7,4},{8,11},{9,10},{10,... | collective-permute-start | bytes 294920 | tf_op jit(solution)/shard_map/ppermute | solution.py:289
  116.8 7.5 %collective-permute-done.17 = f32[256,512]{1,0:T(8,128)S(1)} collective-permute-done((f32[256,512]{1,0:T(8,128)S(1)}, f32[256,512]{1,0:T(8,128)S(1)}, u32[]{:S(2)}, u32[]{:S(2)}) %collective-permute-start.17) | collective-permute-done | bytes 524320 | tf_op jit(solution)/shard_map/ppermute | solution.py:289
  124.4 1.4 collective-permute-start.23
  125.9 1.3 collective-permute-start.24
  127.2 0.9 collective-permute-start.25
  128.1 4.1 %collective-permute-start.26 = (bf16[384,128]{1,0:T(8,128)(2,1)S(1)}, bf16[384,128]{1,0:T(8,128)(2,1)S(1)}, u32[]{:S(2)}, u32[]{:S(2)}) collective-permute-start(bf16[384,128]{1,0:T(8,128)(2,1)S(1)} %copy-done.18), channel_id=1, source_target_pairs={{0,7},{1,6},{2,5},{3,4},{4,3},{5,2},{6,1},{7,0},{8,15},{9,14},{10,... | collective-permute-start | bytes 294920 | tf_op jit(solution)/shard_map/ppermute | solution.py:289
  132.2 0.7 fusion.10
  133.0 2.8 %collective-permute-done.23.rest_4_ = bf16[384,128]{1,0:T(8,128)(2,1)S(1)} collective-permute-done((bf16[384,128]{1,0:T(8,128)(2,1)S(1)}, bf16[384,128]{1,0:T(8,128)(2,1)S(1)}, u32[]{:S(2)}, u32[]{:S(2)}) %collective-permute-start.23) | collective-permute-done | bytes 98336 | tf_op jit(solution)/shard_map/ppermute | solution.py:289
  135.7 3.0 %collective-permute-done.24.rest_5_ = bf16[384,128]{1,0:T(8,128)(2,1)S(1)} collective-permute-done((bf16[384,128]{1,0:T(8,128)(2,1)S(1)}, bf16[384,128]{1,0:T(8,128)(2,1)S(1)}, u32[]{:S(2)}, u32[]{:S(2)}) %collective-permute-start.24) | collective-permute-done | bytes 98336 | tf_op jit(solution)/shard_map/ppermute | solution.py:289
  138.7 0.5 collective-permute-start.29
  139.3 0.4 collective-permute-start.31
  140.7 0.6 collective-permute-done.32.rest_13_
  141.4 0.4 collective-permute-done.34.rest_15_
  141.8 6.5 %place_rows.1 = (f32[16,320,8,1,128]{4,3,2,1,0:T(1,128)}, f32[16,64,8,1,128]{4,3,2,1,0:T(1,128)}) custom-call(s32[1]{0:T(128)} %bitcast.14.first_row, s32[16]{0:T(128)S(1)} %pad_add_fusion.1.rows, bf16[384,128]{1,0:T(8,128)(2,1)S(1)} %copy-done.9, ...), custom_call_target="tpu_custom_call", output_to_operand_aliasing={{0}: (18, {}), {1}: (19, {})} | custom-call | tf_op jit(solution)/shard_map/place_rows/pallas_call | solution.py:363
  148.3 0.8 fusion.1
  (91 shorter events, 2.7 us)
Async XLA Ops:
  7.2 1.1 copy-start
  7.2 40.0 %all-gather.4.cloned.1.call-start = ((), (), s32[]{:S(2)}) async-start(), calls=%async_computation | async-start | bytes 1638400 | tf_op jit(solution)/shard_map/all_gather | solution.py:303
  9.0 96.0 %all-gather.6.cloned.1.call-start = ((), (), s32[]{:S(2)}) async-start(), calls=%async_computation.1 | async-start | bytes 3932160 | tf_op jit(solution)/shard_map/all_gather | solution.py:339
  11.0 11.3 %collective-permute-start.9 = (s32[1]{0:T(128)}, s32[1]{0:T(128)}, u32[]{:S(2)}, u32[]{:S(2)}) collective-permute-start(s32[1]{0:T(128)} %bitcast.2), channel_id=1, source_target_pairs={{0,7},{1,6},{2,5},{3,4},{4,3},{5,2},{6,1},{7,0},{8,15},{9,14},{10,... | collective-permute-start | bytes 20 | tf_op jit(solution)/shard_map/ppermute | solution.py:289
  17.0 6.1 %collective-permute-start.8 = (s32[1]{0:T(128)}, s32[1]{0:T(128)}, u32[]{:S(2)}, u32[]{:S(2)}) collective-permute-start(s32[1]{0:T(128)} %bitcast.2), channel_id=1, source_target_pairs={{0,6},{1,7},{2,4},{3,5},{4,2},{5,3},{6,0},{7,1},{8,14},{9,15},{10,... | collective-permute-start | bytes 20 | tf_op jit(solution)/shard_map/ppermute | solution.py:289
  17.2 6.2 %collective-permute-start.7 = (s32[1]{0:T(128)}, s32[1]{0:T(128)}, u32[]{:S(2)}, u32[]{:S(2)}) collective-permute-start(s32[1]{0:T(128)} %bitcast.2), channel_id=1, source_target_pairs={{0,5},{1,4},{2,7},{3,6},{4,1},{5,0},{6,3},{7,2},{8,13},{9,12},{10,... | collective-permute-start | bytes 20 | tf_op jit(solution)/shard_map/ppermute | solution.py:289
  18.0 5.4 %collective-permute-start.6 = (s32[1]{0:T(128)}, s32[1]{0:T(128)}, u32[]{:S(2)}, u32[]{:S(2)}) collective-permute-start(s32[1]{0:T(128)} %bitcast.2), channel_id=1, source_target_pairs={{0,4},{1,5},{2,6},{3,7},{4,0},{5,1},{6,2},{7,3},{8,12},{9,13},{10,... | collective-permute-start | bytes 20 | tf_op jit(solution)/shard_map/ppermute | solution.py:289
  20.0 4.5 %collective-permute-start.5 = (s32[1]{0:T(128)}, s32[1]{0:T(128)}, u32[]{:S(2)}, u32[]{:S(2)}) collective-permute-start(s32[1]{0:T(128)} %bitcast.2), channel_id=1, source_target_pairs={{0,3},{1,2},{2,1},{3,0},{4,7},{5,6},{6,5},{7,4},{8,11},{9,10},{10,... | collective-permute-start | bytes 20 | tf_op jit(solution)/shard_map/ppermute | solution.py:289
  22.3 3.8 %collective-permute-start.4 = (s32[1]{0:T(128)}, s32[1]{0:T(128)}, u32[]{:S(2)}, u32[]{:S(2)}) collective-permute-start(s32[1]{0:T(128)} %bitcast.2), channel_id=1, source_target_pairs={{0,2},{1,3},{2,0},{3,1},{4,6},{5,7},{6,4},{7,5},{8,10},{9,11},{10,... | collective-permute-start | bytes 20 | tf_op jit(solution)/shard_map/ppermute | solution.py:289
  23.1 3.8 %collective-permute-start.3 = (s32[1]{0:T(128)}, s32[1]{0:T(128)}, u32[]{:S(2)}, u32[]{:S(2)}) collective-permute-start(s32[1]{0:T(128)} %bitcast.2), channel_id=1, source_target_pairs={{0,1},{1,0},{2,3},{3,2},{4,5},{5,4},{6,7},{7,6},{8,9},{9,8},{10,11... | collective-permute-start | bytes 20 | tf_op jit(solution)/shard_map/ppermute | solution.py:289
  31.9 2.2 %copy-start.2 = (bf16[256,8192]{1,0:T(8,128)(2,1)S(1)}, bf16[256,8192]{1,0:T(8,128)(2,1)}, u32[]{:S(2)}) copy-start(bf16[256,8192]{1,0:T(8,128)(2,1)} %up_ref.3) | copy-start | bytes 12582916
  39.4 32.7 %copy-start.3 = (bf16[128,5120]{1,0:T(8,128)(2,1)S(1)}, bf16[128,5120]{1,0:T(8,128)(2,1)}, u32[]{:S(2)}) copy-start(bf16[128,5120]{1,0:T(8,128)(2,1)} %x_ref.3) | copy-start | bytes 3932164
  44.6 0.6 copy-start.6
  45.2 0.6 copy-start.13
  45.9 0.6 copy-start.15
  49.7 14.4 %collective-permute-start.1 = (bf16[4,128,640]{2,1,0:T(8,128)(2,1)}, bf16[4,128,640]{2,1,0:T(8,128)(2,1)S(1)}, u32[]{:S(2)}, u32[]{:S(2)}) collective-permute-start(bf16[4,128,640]{2,1,0:T(8,128)(2,1)} %get-tuple-element.30), channel_id=1, source_target_pairs={{0,1},{1,0},{2,3},{3,2},{4,5},{5,4},{6,7},{7,6},{8,9},{9,8},{10,11... | collective-permute-start | bytes 1966088 | tf_op jit(solution)/shard_map/ppermute | solution.py:289
  50.0 55.0 %collective-permute-start = (bf16[4,128,640]{2,1,0:T(8,128)(2,1)}, bf16[4,128,640]{2,1,0:T(8,128)(2,1)}, u32[]{:S(2)}, u32[]{:S(2)}) collective-permute-start(bf16[4,128,640]{2,1,0:T(8,128)(2,1)} %get-tuple-element.29.refs_0_), channel_id=1, source_target_pairs={{0,8},{8,0},{1,9},{9,1},{2,10},{10,2},{3,11},{11,3},{4,12},{12,4},... | collective-permute-start | bytes 1966088 | tf_op jit(solution)/shard_map/ppermute | solution.py:292
  64.1 40.9 %collective-permute-start.2 = (bf16[4,128,640]{2,1,0:T(8,128)(2,1)S(1)}, bf16[4,128,640]{2,1,0:T(8,128)(2,1)}, u32[]{:S(2)}, u32[]{:S(2)}) collective-permute-start(bf16[4,128,640]{2,1,0:T(8,128)(2,1)S(1)} %collective-permute-done.1.refs_2_), channel_id=1, source_target_pairs={{0,8},{8,0},{1,9},{9,1},{2,10},{10,2},{3,11},{11,3},{4,12},{12,4},... | collective-permute-start | bytes 1966088 | tf_op jit(solution)/shard_map/ppermute | solution.py:292
  64.1 5.2 %collective-permute-start.10 = (bf16[384,128]{1,0:T(8,128)(2,1)S(1)}, bf16[384,128]{1,0:T(8,128)(2,1)S(1)}, u32[]{:S(2)}, u32[]{:S(2)}) collective-permute-start(bf16[384,128]{1,0:T(8,128)(2,1)S(1)} %get-tuple-element.34), channel_id=1, source_target_pairs={{0,1},{1,0},{2,3},{3,2},{4,5},{5,4},{6,7},{7,6},{8,9},{9,8},{10,11... | collective-permute-start | bytes 294920 | tf_op jit(solution)/shard_map/ppermute | solution.py:289
  65.6 8.4 %collective-permute-start.11 = (bf16[384,128]{1,0:T(8,128)(2,1)}, bf16[384,128]{1,0:T(8,128)(2,1)}, u32[]{:S(2)}, u32[]{:S(2)}) collective-permute-start(bf16[384,128]{1,0:T(8,128)(2,1)} %get-tuple-element.35), channel_id=1, source_target_pairs={{0,2},{1,3},{2,0},{3,1},{4,6},{5,7},{6,4},{7,5},{8,10},{9,11},{10,... | collective-permute-start | bytes 294920 | tf_op jit(solution)/shard_map/ppermute | solution.py:289
  66.8 9.5 %collective-permute-start.12 = (bf16[384,128]{1,0:T(8,128)(2,1)}, bf16[384,128]{1,0:T(8,128)(2,1)}, u32[]{:S(2)}, u32[]{:S(2)}) collective-permute-start(bf16[384,128]{1,0:T(8,128)(2,1)} %get-tuple-element.36), channel_id=1, source_target_pairs={{0,3},{1,2},{2,1},{3,0},{4,7},{5,6},{6,5},{7,4},{8,11},{9,10},{10,... | collective-permute-start | bytes 294920 | tf_op jit(solution)/shard_map/ppermute | solution.py:289
  69.3 0.6 copy-start.11
  70.0 8.1 %collective-permute-start.13 = (bf16[384,128]{1,0:T(8,128)(2,1)}, bf16[384,128]{1,0:T(8,128)(2,1)}, u32[]{:S(2)}, u32[]{:S(2)}) collective-permute-start(bf16[384,128]{1,0:T(8,128)(2,1)} %get-tuple-element.37), channel_id=1, source_target_pairs={{0,4},{1,5},{2,6},{3,7},{4,0},{5,1},{6,2},{7,3},{8,12},{9,13},{10,... | collective-permute-start | bytes 294920 | tf_op jit(solution)/shard_map/ppermute | solution.py:289
  74.0 20.7 %collective-permute-start.16 = (bf16[384,128]{1,0:T(8,128)(2,1)}, bf16[384,128]{1,0:T(8,128)(2,1)S(1)}, u32[]{:S(2)}, u32[]{:S(2)}) collective-permute-start(bf16[384,128]{1,0:T(8,128)(2,1)} %copy-done.13), channel_id=1, source_target_pairs={{0,7},{1,6},{2,5},{3,4},{4,3},{5,2},{6,1},{7,0},{8,15},{9,14},{10,... | collective-permute-start | bytes 294920 | tf_op jit(solution)/shard_map/ppermute | solution.py:289
  76.4 18.3 %collective-permute-start.14 = (bf16[384,128]{1,0:T(8,128)(2,1)}, bf16[384,128]{1,0:T(8,128)(2,1)S(1)}, u32[]{:S(2)}, u32[]{:S(2)}) collective-permute-start(bf16[384,128]{1,0:T(8,128)(2,1)} %copy-done.16), channel_id=1, source_target_pairs={{0,5},{1,4},{2,7},{3,6},{4,1},{5,0},{6,3},{7,2},{8,13},{9,12},{10,... | collective-permute-start | bytes 294920 | tf_op jit(solution)/shard_map/ppermute | solution.py:289
  78.1 16.5 %collective-permute-start.15 = (bf16[384,128]{1,0:T(8,128)(2,1)}, bf16[384,128]{1,0:T(8,128)(2,1)S(1)}, u32[]{:S(2)}, u32[]{:S(2)}) collective-permute-start(bf16[384,128]{1,0:T(8,128)(2,1)} %copy-done.15), channel_id=1, source_target_pairs={{0,6},{1,7},{2,4},{3,5},{4,2},{5,3},{6,0},{7,1},{8,14},{9,15},{10,... | collective-permute-start | bytes 294920 | tf_op jit(solution)/shard_map/ppermute | solution.py:289
  85.3 0.9 copy-start.14
  94.6 0.9 copy-start.7
  95.5 0.9 copy-start.10
  96.5 0.9 copy-start.12
  97.4 7.6 %copy-start.5 = (bf16[4,128,640]{2,1,0:T(8,128)(2,1)S(1)}, bf16[4,128,640]{2,1,0:T(8,128)(2,1)}, u32[]{:S(2)}) copy-start(bf16[4,128,640]{2,1,0:T(8,128)(2,1)} %get-tuple-element.29.refs_0_) | copy-start | bytes 1966084
  99.9 0.6 copy-start.8
  100.6 0.6 copy-start.17
  101.2 0.6 copy-start.19
  101.8 0.6 copy-start.21
  103.7 0.6 copy-start.27
  105.0 1.7 %copy-start.4 = (bf16[5120,256]{1,0:T(8,128)(2,1)S(1)}, bf16[5120,256]{1,0:T(8,128)(2,1)}, u32[]{:S(2)}) copy-start(bf16[5120,256]{1,0:T(8,128)(2,1)} %all-gather.6.cloned.1.call-done) | copy-start | bytes 7864324
  106.8 0.9 copy-start.9
  107.7 5.7 %copy-start.30 = (bf16[384,128]{1,0:T(8,128)(2,1)S(1)}, bf16[384,128]{1,0:T(8,128)(2,1)}, u32[]{:S(2)}) copy-start(bf16[384,128]{1,0:T(8,128)(2,1)} %copy-done.29) | copy-start | bytes 294916
  107.7 5.8 %copy-start.28 = (bf16[384,128]{1,0:T(8,128)(2,1)S(1)}, bf16[384,128]{1,0:T(8,128)(2,1)}, u32[]{:S(2)}) copy-start(bf16[384,128]{1,0:T(8,128)(2,1)} %copy-done.27) | copy-start | bytes 294916
  107.7 5.9 %copy-start.26 = (bf16[384,128]{1,0:T(8,128)(2,1)S(1)}, bf16[384,128]{1,0:T(8,128)(2,1)}, u32[]{:S(2)}) copy-start(bf16[384,128]{1,0:T(8,128)(2,1)} %copy-done.25) | copy-start | bytes 294916
  107.7 16.7 %copy-start.24 = (bf16[384,128]{1,0:T(8,128)(2,1)S(1)}, bf16[384,128]{1,0:T(8,128)(2,1)}, u32[]{:S(2)}) copy-start(bf16[384,128]{1,0:T(8,128)(2,1)} %copy-done.23) | copy-start | bytes 294916
  107.7 18.2 %copy-start.22 = (bf16[384,128]{1,0:T(8,128)(2,1)S(1)}, bf16[384,128]{1,0:T(8,128)(2,1)}, u32[]{:S(2)}) copy-start(bf16[384,128]{1,0:T(8,128)(2,1)} %copy-done.21) | copy-start | bytes 294916
  107.7 19.5 %copy-start.20 = (bf16[384,128]{1,0:T(8,128)(2,1)S(1)}, bf16[384,128]{1,0:T(8,128)(2,1)}, u32[]{:S(2)}) copy-start(bf16[384,128]{1,0:T(8,128)(2,1)} %copy-done.19) | copy-start | bytes 294916
  107.7 20.5 %copy-start.18 = (bf16[384,128]{1,0:T(8,128)(2,1)S(1)}, bf16[384,128]{1,0:T(8,128)(2,1)}, u32[]{:S(2)}) copy-start(bf16[384,128]{1,0:T(8,128)(2,1)} %copy-done.17) | copy-start | bytes 294916
  110.8 13.5 %collective-permute-start.17 = (f32[256,512]{1,0:T(8,128)S(1)}, f32[256,512]{1,0:T(8,128)S(1)}, u32[]{:S(2)}, u32[]{:S(2)}) collective-permute-start(f32[256,512]{1,0:T(8,128)S(1)} %get-tuple-element.43), channel_id=1, source_target_pairs={{0,1},{1,0},{2,3},{3,2},{4,5},{5,4},{6,7},{7,6},{8,9},{9,8},{10,11... | collective-permute-start | bytes 1572872 | tf_op jit(solution)/shard_map/ppermute | solution.py:289
  113.3 13.9 %collective-permute-start.20 = (bf16[384,128]{1,0:T(8,128)(2,1)S(1)}, bf16[384,128]{1,0:T(8,128)(2,1)S(1)}, u32[]{:S(2)}, u32[]{:S(2)}) collective-permute-start(bf16[384,128]{1,0:T(8,128)(2,1)S(1)} %copy-done.30), channel_id=1, source_target_pairs={{0,1},{1,0},{2,3},{3,2},{4,5},{5,4},{6,7},{7,6},{8,9},{9,8},{10,11... | collective-permute-start | bytes 294920 | tf_op jit(solution)/shard_map/ppermute | solution.py:289
  113.4 14.7 %collective-permute-start.21 = (bf16[384,128]{1,0:T(8,128)(2,1)S(1)}, bf16[384,128]{1,0:T(8,128)(2,1)S(1)}, u32[]{:S(2)}, u32[]{:S(2)}) collective-permute-start(bf16[384,128]{1,0:T(8,128)(2,1)S(1)} %copy-done.28), channel_id=1, source_target_pairs={{0,2},{1,3},{2,0},{3,1},{4,6},{5,7},{6,4},{7,5},{8,10},{9,11},{10,... | collective-permute-start | bytes 294920 | tf_op jit(solution)/shard_map/ppermute | solution.py:289
  113.4 12.5 %collective-permute-start.19 = (s32[8]{0:T(128)S(1)}, s32[8]{0:T(128)S(1)}, u32[]{:S(2)}, u32[]{:S(2)}) collective-permute-start(s32[8]{0:T(128)S(1)} %fusion.9.rows._), channel_id=1, source_target_pairs={{0,8},{8,0},{1,9},{9,1},{2,10},{10,2},{3,11},{11,3},{4,12},{12,4},... | collective-permute-start | bytes 104 | tf_op jit(solution)/shard_map/ppermute | solution.py:292
  113.5 19.4 %collective-permute-start.22 = (bf16[384,128]{1,0:T(8,128)(2,1)S(1)}, bf16[384,128]{1,0:T(8,128)(2,1)S(1)}, u32[]{:S(2)}, u32[]{:S(2)}) collective-permute-start(bf16[384,128]{1,0:T(8,128)(2,1)S(1)} %copy-done.26), channel_id=1, source_target_pairs={{0,3},{1,2},{2,1},{3,0},{4,7},{5,6},{6,5},{7,4},{8,11},{9,10},{10,... | collective-permute-start | bytes 294920 | tf_op jit(solution)/shard_map/ppermute | solution.py:289
  124.4 11.3 %collective-permute-start.23 = (bf16[384,128]{1,0:T(8,128)(2,1)S(1)}, bf16[384,128]{1,0:T(8,128)(2,1)S(1)}, u32[]{:S(2)}, u32[]{:S(2)}) collective-permute-start(bf16[384,128]{1,0:T(8,128)(2,1)S(1)} %copy-done.24), channel_id=1, source_target_pairs={{0,4},{1,5},{2,6},{3,7},{4,0},{5,1},{6,2},{7,3},{8,12},{9,13},{10,... | collective-permute-start | bytes 294920 | tf_op jit(solution)/shard_map/ppermute | solution.py:289
  125.9 12.8 %collective-permute-start.24 = (bf16[384,128]{1,0:T(8,128)(2,1)S(1)}, bf16[384,128]{1,0:T(8,128)(2,1)S(1)}, u32[]{:S(2)}, u32[]{:S(2)}) collective-permute-start(bf16[384,128]{1,0:T(8,128)(2,1)S(1)} %copy-done.22), channel_id=1, source_target_pairs={{0,5},{1,4},{2,7},{3,6},{4,1},{5,0},{6,3},{7,2},{8,13},{9,12},{10,... | collective-permute-start | bytes 294920 | tf_op jit(solution)/shard_map/ppermute | solution.py:289
  127.2 11.5 %collective-permute-start.25 = (bf16[384,128]{1,0:T(8,128)(2,1)S(1)}, bf16[384,128]{1,0:T(8,128)(2,1)S(1)}, u32[]{:S(2)}, u32[]{:S(2)}) collective-permute-start(bf16[384,128]{1,0:T(8,128)(2,1)S(1)} %copy-done.20), channel_id=1, source_target_pairs={{0,6},{1,7},{2,4},{3,5},{4,2},{5,3},{6,0},{7,1},{8,14},{9,15},{10,... | collective-permute-start | bytes 294920 | tf_op jit(solution)/shard_map/ppermute | solution.py:289
  128.1 11.1 %collective-permute-start.26 = (bf16[384,128]{1,0:T(8,128)(2,1)S(1)}, bf16[384,128]{1,0:T(8,128)(2,1)S(1)}, u32[]{:S(2)}, u32[]{:S(2)}) collective-permute-start(bf16[384,128]{1,0:T(8,128)(2,1)S(1)} %copy-done.18), channel_id=1, source_target_pairs={{0,7},{1,6},{2,5},{3,4},{4,3},{5,2},{6,1},{7,0},{8,15},{9,14},{10,... | collective-permute-start | bytes 294920 | tf_op jit(solution)/shard_map/ppermute | solution.py:289
  133.0 15.4 %collective-permute-start.18 = (f32[128,512]{1,0:T(8,128)}, f32[128,512]{1,0:T(8,128)S(1)}, u32[]{:S(2)}, u32[]{:S(2)}) collective-permute-start(f32[128,512]{1,0:T(8,128)} %get-tuple-element.56), channel_id=1, source_target_pairs={{0,8},{8,0},{1,9},{9,1},{2,10},{10,2},{3,11},{11,3},{4,12},{12,4},... | collective-permute-start | bytes 786440 | tf_op jit(solution)/shard_map/ppermute | solution.py:292
  135.7 3.6 %collective-permute-start.27 = (bf16[384,128]{1,0:T(8,128)(2,1)S(1)}, bf16[384,128]{1,0:T(8,128)(2,1)S(1)}, u32[]{:S(2)}, u32[]{:S(2)}) collective-permute-start(bf16[384,128]{1,0:T(8,128)(2,1)S(1)} %copy-done.9), channel_id=1, source_target_pairs={{0,8},{8,0},{1,9},{9,1},{2,10},{10,2},{3,11},{11,3},{4,12},{12,4},... | collective-permute-start | bytes 294920 | tf_op jit(solution)/shard_map/ppermute | solution.py:292
  138.7 1.3 collective-permute-start.28
  138.7 1.5 collective-permute-start.29
  139.2 1.3 collective-permute-start.30
  139.3 1.5 collective-permute-start.31
  140.0 1.3 collective-permute-start.32
  140.1 1.3 collective-permute-start.33
  140.5 1.3 collective-permute-start.34
  141.8 7.3 %copy-start.1 = (bf16[640,512]{1,0:T(8,128)(2,1)S(1)}, bf16[640,512]{1,0:T(8,128)(2,1)}, u32[]{:S(2)}) copy-start(bf16[640,512]{1,0:T(8,128)(2,1)} %param.9) | copy-start | bytes 1966084
  (4 other events, 2.5 us)
Sparse Core Ops, SparseCore 0:
  10.2 35.3 all-gather.3
  47.3 39.3 all-gather.5

commit v3 on v2

--- a/solution.py
+++ b/solution.py
@@ -18,7 +18,8 @@
 VMEM = pl.BlockSpec(memory_space=pltpu.VMEM)
 SMEM = pl.BlockSpec(memory_space=pltpu.SMEM)
 ANY = pl.BlockSpec(memory_space=pl.ANY)
-LIMIT = pltpu.CompilerParams(vmem_limit_bytes=40 * 1024 * 1024)
+LIMIT = pltpu.CompilerParams(vmem_limit_bytes=16 * 1024 * 1024)
+WIDE = pltpu.CompilerParams(vmem_limit_bytes=60 * 1024 * 1024)
 
 
 def dot(a, b):
@@ -117,23 +118,29 @@
         xs_ref[k, rows:] = dot(x, odd).astype(jnp.bfloat16)
 
 
-def gather_kernel(first, count, down_chunks, up_chunks, rows, down_ref, up_ref, _, *rest):
-    outs, (down_buf, up_buf, flat, sems) = rest[:count], rest[count:]
+def gather_kernel(first, count, down_chunks, up_chunks, *refs):
+    asked, (down_ref, up_ref, _) = refs[:first + count], refs[first + count:first + count + 3]
+    outs, rows_ref = refs[first + count + 3:-8], refs[-8]
+    down_buf, up_buf, flat, built, rows, sems, row_sem = refs[-7:]
+    for s in range(first + count):
+        pltpu.make_async_copy(asked[s], rows.at[s], row_sem).start()
+    for s in range(first + count):
+        pltpu.make_async_copy(asked[s], rows.at[s], row_sem).wait()
     copies = []
     for s in range(count):
-        start = pl.multiple_of((rows[first + s] // GROUP_ROWS) * GROUP_ROWS, GROUP_ROWS)
-        a = pltpu.make_async_copy(down_ref.at[pl.ds(start, GROUP_ROWS)], down_buf.at[s], sems.at[2 * s])
-        b = pltpu.make_async_copy(up_ref.at[pl.ds(start, GROUP_ROWS)], up_buf.at[s], sems.at[2 * s + 1])
+        start = pl.multiple_of((rows[first + s, 0] // GROUP_ROWS) * GROUP_ROWS, GROUP_ROWS)
+        a = pltpu.make_async_copy(down_ref.at[pl.ds(start, GROUP_ROWS)], down_buf.at[s], sems.at[3 * s])
+        b = pltpu.make_async_copy(up_ref.at[pl.ds(start, GROUP_ROWS)], up_buf.at[s], sems.at[3 * s + 1])
         a.start()
         b.start()
-        copies.append((a, b))
-    step = 8
+        copies.append((a, b, pltpu.make_async_copy(built.at[s], outs[s], sems.at[3 * s + 2])))
+    for s in range(first + count):
+        rows_ref[s] = rows[s, 0]
+    step = 16
     for s in range(count):
-        row = rows[first + s] % GROUP_ROWS
+        row = rows[first + s, 0] % GROUP_ROWS
         upper = row >= 8
         sub = row % 8
-        copies[s][0].wait()
-        copies[s][1].wait()
 
         def pick(buf, lane):
             tile = buf[s, :, pl.ds(pl.multiple_of(lane, LANES), LANES)].astype(jnp.float32)
@@ -145,13 +152,18 @@
                 flat[pl.ds(pl.multiple_of(j * 8, 8), 8), :] = pick(down_buf, j * LANES)
             return carry
 
+        copies[s][0].wait()
         lax.fori_loop(0, down_chunks // step, some, 0)
-        outs[s][:down_chunks] = flat[pl.ds(sub, down_chunks, stride=8), :].astype(jnp.bfloat16)
+        built[s, :down_chunks] = flat[pl.ds(sub, down_chunks, stride=8), :].astype(jnp.bfloat16)
         across = up_chunks // 8
+        copies[s][1].wait()
         for j in range(up_chunks):
             place = (j % across) * 8 + j // across
             flat[place * 8:place * 8 + 8, :] = pick(up_buf, j * LANES)
-        outs[s][down_chunks:] = flat[pl.ds(sub, up_chunks, stride=8), :].astype(jnp.bfloat16)
+        built[s, down_chunks:] = flat[pl.ds(sub, up_chunks, stride=8), :].astype(jnp.bfloat16)
+        copies[s][2].start()
+    for s in range(count):
+        copies[s][2].wait()
 
 
 def zero_kernel(after_ref, down_ref, up_ref, zeros, sems):
@@ -170,17 +182,23 @@
 
 
 def adapter_kernel(count, down_chunks, where, xs_ref, g_ref, *rest):
-    pieces, outs, (lifted_ref, up_panel) = rest[:count], rest[count + 1:2 * count + 1], rest[2 * count + 1:]
+    sources, targets = rest[:count], rest[count + 1:2 * count + 1]
+    lifted_ref, up_panel, pieces, outs, sems = rest[2 * count + 1:]
+    arriving = [pltpu.make_async_copy(sources[s], pieces.at[s], sems.at[0, s]) for s in range(count)]
+    leaving = [pltpu.make_async_copy(outs.at[s], targets[s], sems.at[1, s]) for s in range(count)]
+    for copy in arriving:
+        copy.start()
     me = where[0]
     rows = g_ref.shape[0]
     across = g_ref.shape[1] // LANES
     total = jnp.zeros((2 * rows, LANES), jnp.float32)
     for s in range(count):
         owner = me ^ s
-        total += dot(xs_ref[owner], pieces[s][:down_chunks])
+        arriving[s].wait()
+        total += dot(xs_ref[owner], pieces[s, :down_chunks])
         at = pl.multiple_of(owner * 8, 8)
         for c in range(across):
-            block = pieces[s][down_chunks + 8 * c:down_chunks + 8 * c + 8, :].astype(jnp.float32)
+            block = pieces[s, down_chunks + 8 * c:down_chunks + 8 * c + 8, :].astype(jnp.float32)
             up_panel[pl.ds(at, 8), c * LANES:(c + 1) * LANES] = block
             up_panel[pl.ds(R + at, 8), c * LANES:(c + 1) * LANES] = block
     panel = up_panel[...].astype(jnp.bfloat16)
@@ -197,80 +215,91 @@
     up_panel[...] = up_term
     for s in range(count):
         owner = me ^ s
-        outs[s][:down_chunks] = t_dot(xs_ref[owner], diagonal).astype(jnp.bfloat16)
+        outs[s, :down_chunks] = t_dot(xs_ref[owner], diagonal).astype(jnp.bfloat16)
         at = pl.multiple_of(owner * 8, 8)
         rows_here = up_panel[pl.ds(at, 8), :]
         up_part = jnp.concatenate(
             [rows_here[:, c * LANES:(c + 1) * LANES] for c in range(across)], axis=0
         )
-        outs[s][down_chunks:] = up_part.astype(jnp.bfloat16)
-
-
-def scatter_kernel(count, down_chunks, up_chunks, first_row, rows, *rest):
-    pieces = rest[:count]
+        outs[s, down_chunks:] = up_part.astype(jnp.bfloat16)
+        leaving[s].start()
+    for copy in leaving:
+        copy.wait()
+
+
+def scatter_kernel(count, down_chunks, up_chunks, first_row, rows_here, rows_core, *rest):
+    sources = rest[:count]
     down_out, up_out = rest[count + 2:count + 4]
-    down_sum, up_sum, ordered, sem = rest[count + 4:]
+    pieces, down_sum, up_sum, ordered, arrived, sem = rest[count + 4:]
     owned_rows = down_out.shape[0] * 8
     across = up_chunks // 8
-    slots = []
+    rows = [(rows_here if b < count // 2 else rows_core)[b % (count // 2)] - first_row[0] for b in range(count)]
+    arriving = [pltpu.make_async_copy(sources[b], pieces.at[b], arrived.at[b]) for b in range(count)]
+    for copy in arriving:
+        copy.start()
+    owned = [(row >= 0) & (row < owned_rows) for row in rows]
+    slots, final = [], []
     for b in range(count):
-        slot = jnp.int32(b)
+        slot, last = jnp.int32(b), jnp.bool_(True)
         for e in range(b - 1, -1, -1):
             slot = jnp.where(rows[e] == rows[b], e, slot)
+        for e in range(b + 1, count):
+            last = last & (rows[e] != rows[b])
         slots.append(slot)
-        down = pieces[b][:down_chunks].astype(jnp.float32).reshape(down_chunks, 1, LANES)
-        for c in range(across):
-            ordered[pl.ds(c, 8, stride=across), :] = pieces[b][
-                down_chunks + 8 * c:down_chunks + 8 * c + 8
-            ].astype(jnp.float32)
-        up = ordered[...].reshape(up_chunks, 1, LANES)
-
-        @pl.when(slot == b)
+        final.append(last)
+
+    def copies(b):
+        return (
+            pltpu.make_async_copy(down_sum.at[slots[b]], down_out.at[rows[b] // 8, :, rows[b] % 8], sem),
+            pltpu.make_async_copy(up_sum.at[slots[b]], up_out.at[rows[b] // 8, :, rows[b] % 8], sem),
+        )
+
+    for b in range(count):
+        arriving[b].wait()
+
+        @pl.when(owned[b])
         def _():
-            down_sum[b] = down
-            up_sum[b] = up
-
-        @pl.when(slot != b)
-        def _():
-            down_sum[slot] += down
-            up_sum[slot] += up
-
-    def copies(b):
-        local = rows[b] - first_row[0]
-        return (
-            pltpu.make_async_copy(down_sum.at[b], down_out.at[local // 8, :, local % 8], sem),
-            pltpu.make_async_copy(up_sum.at[b], up_out.at[local // 8, :, local % 8], sem),
-        )
-
-    def mine(b):
-        local = rows[b] - first_row[0]
-        return (slots[b] == b) & (local >= 0) & (local < owned_rows)
+            slot = slots[b]
+            down = pieces[b, :down_chunks].astype(jnp.float32).reshape(down_chunks, 1, LANES)
+            for c in range(across):
+                ordered[pl.ds(c, 8, stride=across), :] = pieces[
+                    b, down_chunks + 8 * c:down_chunks + 8 * c + 8
+                ].astype(jnp.float32)
+            up = ordered[...].reshape(up_chunks, 1, LANES)
+
+            @pl.when(slot == b)
+            def _():
+                down_sum[b] = down
+                up_sum[b] = up
+
+            @pl.when(slot != b)
+            def _():
+                down_sum[slot] += down
+                up_sum[slot] += up
+
+            @pl.when(final[b])
+            def _():
+                for copy in copies(b):
+                    copy.start()
 
     for b in range(count):
-        @pl.when(mine(b))
-        def _():
-            for copy in copies(b):
-                copy.start()
-    for b in range(count):
-        @pl.when(mine(b))
+        @pl.when(owned[b] & final[b])
         def _():
             for copy in copies(b):
                 copy.wait()
 
 
 def base_kernel(*refs):
-    x_refs, w_ref, own_ref, other_ref = refs[:4], refs[4], refs[-2], refs[-1]
-    halves, _, width = w_ref.shape
+    x_refs, w_refs, own_ref, other_ref = refs[:4], refs[4:6], refs[-2], refs[-1]
     outer, _, depth = x_refs[0].shape
-    rows = own_ref.shape[0]
-    total = [0.0] * halves
-    for k in range(outer):
-        left = jnp.concatenate([ref[k] for ref in x_refs], axis=0)
-        for h in range(halves):
-            total[h] += dot(left, w_ref[h, k * depth:(k + 1) * depth, :])
-    for h in range(halves):
-        own_ref[:, h * width:(h + 1) * width] = total[h][:rows]
-        other_ref[:, h * width:(h + 1) * width] = total[h][rows:]
+    rows, width = own_ref.shape[0], w_refs[0].shape[1]
+    for h, w_ref in enumerate(w_refs):
+        total = 0.0
+        for k in range(outer):
+            left = jnp.concatenate([ref[k] for ref in x_refs], axis=0)
+            total += dot(left, w_ref[k * depth:(k + 1) * depth, :])
+        own_ref[:, h * width:(h + 1) * width] = total[:rows]
+        other_ref[:, h * width:(h + 1) * width] = total[rows:]
 
 
 def fast_body(tokens, cotangent, frozen_value, down_store, up_store, block_adapter, adapter_slot):
@@ -291,23 +320,24 @@
     def other_core(value):
         return lax.ppermute(value, "dp", [(0, 1), (1, 0)])
 
-    row = store_rows(block_adapter, adapter_slot)
+    def other_part(value):
+        return lax.ppermute(value, "parts", [(a, parts - 1 - a) for a in range(parts)])
+
+    row = jnp.broadcast_to(store_rows(block_adapter, adapter_slot), (LANES,))
     asked = [row] + [exchange(row, s) for s in range(1, group)]
-    place = jnp.arange(2 * group, dtype=jnp.int32)
-    rows = sum(jnp.where(place[:group] == s, asked[s], 0) for s in range(group))
-    rows_core = other_core(rows)
 
     width = frozen_value.shape[1] // parts
     half = lax.dynamic_slice_in_dim(frozen_value, part * width, width, axis=1)
     lines = [list(range(0, group, 2)), list(range(1, group, 2))]
     half = lax.all_gather(half, "tensor", axis_index_groups=lines, axis=0, tiled=True)
+
     block = jax.ShapeDtypeStruct((outer, token_rows, slice_width), jnp.bfloat16)
     x_mine, x_theirs = pl.pallas_call(
         split_kernel, out_shape=(block, block), in_specs=[SMEM, VMEM], out_specs=(VMEM, VMEM),
         name="split_tokens",
     )(x[None], tokens)
     x_far = exchange(x_theirs, 1)
-    x_blocks = (x_mine, other_core(x_mine), x_far, other_core(x_far))
+    y_mine = other_part(x_mine)
 
     xs = pl.pallas_call(
         interleave_kernel,
@@ -318,25 +348,29 @@
     def pick(first, count, after):
         return pl.pallas_call(
             functools.partial(gather_kernel, first, count, down_chunks, up_chunks),
-            out_shape=[piece] * count,
-            in_specs=[SMEM, ANY, ANY, ANY],
-            out_specs=[VMEM] * count,
+            out_shape=[piece] * count + [jax.ShapeDtypeStruct((first + count,), jnp.int32)],
+            in_specs=[ANY] * (first + count + 3),
+            out_specs=[ANY] * count + [SMEM],
             scratch_shapes=[
                 pltpu.VMEM((count, GROUP_ROWS, down_store.shape[1]), jnp.bfloat16),
                 pltpu.VMEM((count, GROUP_ROWS, up_store.shape[1]), jnp.bfloat16),
                 pltpu.VMEM((down_chunks * 8, LANES), jnp.float32),
-                pltpu.SemaphoreType.DMA((2 * count,)),
+                pltpu.VMEM((count, down_chunks + up_chunks, LANES), jnp.bfloat16),
+                pltpu.SMEM((first + count, LANES), jnp.int32),
+                pltpu.SemaphoreType.DMA((3 * count,)),
+                pltpu.SemaphoreType.DMA(()),
             ],
-            compiler_params=LIMIT,
+            compiler_params=WIDE,
             name="pick_panels",
-        )(rows, down_store, up_store, after)
-
-    sent = pick(0, group // 2, rows)
-    sent += pick(group // 2, group // 2, sent[0])
+        )(*asked[:first + count], down_store, up_store, after)
+
+    *sent, _ = pick(0, group // 2, row)
+    *more, rows = pick(group // 2, group // 2, sent[0])
+    sent += more
     panels = [sent[0]] + [exchange(sent[s], s) for s in range(1, group)]
-
-    half, _ = lax.optimization_barrier((half, sent[-1]))
-    projection = lax.all_gather(half, "parts", axis=0)
+    rows_core = other_core(rows)
+    x_far, _ = lax.optimization_barrier((x_far, panels[2]))
+    x_blocks = (x_mine, y_mine, x_far, other_part(x_far))
 
     owned_groups = ADAPTERS // lax.axis_size("dp") // 8
     down_shape = jax.ShapeDtypeStruct((owned_groups, down_chunks, 8, 1, LANES), jnp.float32)
@@ -344,15 +378,20 @@
     down_zero, up_zero = pl.pallas_call(
         zero_kernel, out_shape=(down_shape, up_shape), in_specs=[ANY], out_specs=(ANY, ANY),
         scratch_shapes=[pltpu.VMEM((up_chunks, 8, 1, LANES), jnp.float32), pltpu.SemaphoreType.DMA((2,))],
-        compiler_params=LIMIT, name="clear_rows",
+        compiler_params=WIDE, name="clear_rows",
     )(sent[-1])
 
     results = pl.pallas_call(
         functools.partial(adapter_kernel, group, down_chunks),
         out_shape=[piece] * group + [jax.ShapeDtypeStruct((token_rows, VALUE_OUTPUTS), jnp.float32)],
-        in_specs=[SMEM] + [VMEM] * (2 + group) + [ANY],
-        out_specs=[VMEM] * (group + 1),
-        scratch_shapes=[pltpu.VMEM((2 * R, VALUE_OUTPUTS), jnp.float32)],
+        in_specs=[SMEM] + [VMEM] * 2 + [ANY] * (group + 1),
+        out_specs=[ANY] * group + [VMEM],
+        scratch_shapes=[
+            pltpu.VMEM((2 * R, VALUE_OUTPUTS), jnp.float32),
+            pltpu.VMEM((group,) + piece.shape, jnp.bfloat16),
+            pltpu.VMEM((group,) + piece.shape, jnp.bfloat16),
+            pltpu.SemaphoreType.DMA((2, group)),
+        ],
         compiler_params=LIMIT,
         name="adapter",
     )(here, xs, cotangent, *panels, down_zero)
@@ -363,37 +402,50 @@
     grad_down, grad_up = pl.pallas_call(
         functools.partial(scatter_kernel, 2 * group, down_chunks, up_chunks),
         out_shape=(down_shape, up_shape),
-        in_specs=[SMEM, SMEM] + [VMEM] * (2 * group) + [ANY, ANY],
+        in_specs=[SMEM] * 3 + [ANY] * (2 * group + 2),
         out_specs=(ANY, ANY),
-        input_output_aliases={2 + 2 * group: 0, 3 + 2 * group: 1},
+        input_output_aliases={3 + 2 * group: 0, 4 + 2 * group: 1},
         scratch_shapes=[
+            pltpu.VMEM((2 * group,) + piece.shape, jnp.bfloat16),
             pltpu.VMEM((2 * group, down_chunks, 1, LANES), jnp.float32),
             pltpu.VMEM((2 * group, up_chunks, 1, LANES), jnp.float32),
             pltpu.VMEM((up_chunks, LANES), jnp.float32),
+            pltpu.SemaphoreType.DMA((2 * group,)),
             pltpu.SemaphoreType.DMA(()),
         ],
-        compiler_params=LIMIT,
+        compiler_params=WIDE,
         name="place_rows",
-    )((core * (ADAPTERS // lax.axis_size("dp")))[None], jnp.concatenate([rows, rows_core]), *back, *back_core,
+    )((core * (ADAPTERS // lax.axis_size("dp")))[None], rows, rows_core, *back, *back_core,
       down_zero, up_zero)
     grad_down = grad_down.reshape(owned_groups, down_chunks, 8, LANES).transpose(0, 2, 1, 3)
     grad_up = grad_up.reshape(owned_groups, up_chunks, 8, LANES).transpose(0, 2, 1, 3)
 
-    sums = jax.ShapeDtypeStruct((2 * token_rows, frozen_value.shape[1]), jnp.float32)
+    half, _ = lax.optimization_barrier((half, panels[-1]))
+    both = (half, other_core(half))
+    sums = jax.ShapeDtypeStruct((2 * token_rows, parts * width), jnp.float32)
     own, other = pl.pallas_call(
         base_kernel,
         out_shape=(sums, sums),
-        in_specs=[VMEM] * 5 + [ANY],
+        in_specs=[VMEM] * 6 + [ANY],
         out_specs=(VMEM, VMEM),
         compiler_params=LIMIT,
         name="frozen_part",
-    )(*x_blocks, projection, terms[0])
+    )(*x_blocks, *both, terms[0])
     columns = own + exchange(other, 1)
     kept, gone = columns[:token_rows], columns[token_rows:]
-    got = other_core(gone)
-    frozen_output = jnp.where(
-        core == 0, jnp.concatenate([kept, got], axis=1), jnp.concatenate([got, kept], axis=1)
-    )
+    got = other_part(gone)
+    quarters = [[c[:, :width], c[:, width:]] for c in (kept, got)]
+
+    def pick_quarter(c, a):
+        first = quarters[a][0] if c == 0 else quarters[a][1]
+        second = quarters[a][1] if c == 0 else quarters[a][0]
+        return jnp.where(core == 0, first, second)
+
+    def columns_of(c):
+        low, high = pick_quarter(c, 0), pick_quarter(c, 1)
+        return jnp.where(part == 0, low, high), jnp.where(part == 0, high, low)
+
+    frozen_output = jnp.concatenate(columns_of(0) + columns_of(1), axis=1)
     mixed = (frozen_output + lifted).astype(jnp.bfloat16)
     return mixed, grad_down.reshape(owned_groups * 8, -1), grad_up.reshape(owned_groups * 8, -1)
 

time: 158 us -> 145 us (0.918)
  local copies, waits for them, and re-layouts: 19.3 us -> 12.7 us
  starting transfers between devices: 45.1 us -> 38.5 us
  other arithmetic: 7.38 us -> 2.28 us
  Pallas kernels: 35.3 us -> 39.9 us
    ppermute x23, starting transfers between devices: 43.3 us -> 34.4 us  [exchange(): return lax.ppermute(value, 'tensor', [(t, t ^ s) for t in range(group)])]
    unnamed x62 -> x76, local copies, waits for them, and re-layouts: 17.8 us -> 11.3 us
    add x1 -> x0, other arithmetic: 5.04 us -> none  [fast_body(): sum((jnp.where(place[:group] == s, asked[s], 0) for s in range(group)))]
    pallas_call x1, Pallas kernels: 2.52 us -> 6.37 us  [fast_body(): pl.pallas_call(functools.partial(adapter_kernel, group, down_chunks), out...]
    all_gather x1, waiting for transfers between devices: 0.01 us -> 2.74 us  [fast_body(): lax.all_gather(half, 'tensor', axis_index_groups=lines, axis=0, tiled=True)]
    ppermute x23, waiting for transfers between devices: 32.5 us -> 29.9 us  [exchange(): return lax.ppermute(value, 'tensor', [(t, t ^ s) for t in range(group)])]
    ppermute x0 -> x3, starting transfers between devices: none -> 2.37 us  [other_part(): lax.ppermute(value, 'parts', [(a, parts - 1 - a) for a in range(parts)])]
  transfers between devices with their start and end apart: 37 -> 37, of which waited for: 12 -> 15; matrix products, arithmetic and copies ran while one was open for 5% -> 1% of each run, Pallas kernels for 21% -> 25%
where the time goes in v3:
time: 145 us; the launch traced here: 144 us
  Pallas kernels  39.9 us (28%)
  starting transfers between devices  38.5 us (27%)
  waiting for transfers between devices  35.2 us (24%)
  between operations  15.2 us (10%)
  local copies, waits for them, and re-layouts  12.7 us (9%)
  other arithmetic  2.28 us (2%)
    ppermute x23, starting transfers between devices, exchange(): return lax.ppermute(value, 'tensor', [(t, t ^ s) for t in range(group)])  34.4 us
    ppermute x23, waiting for transfers between devices, exchange(): return lax.ppermute(value, 'tensor', [(t, t ^ s) for t in range(group)])  29.9 us
    unnamed x76, local copies, waits for them, and re-layouts  11.3 us
    pallas_call x2, Pallas kernels, pick(): pl.pallas_call(functools.partial(gather_kernel, first, count, down_chunks...  11.1 us
    pallas_call x1, Pallas kernels, fast_body(): pl.pallas_call(zero_kernel, out_shape=(down_shape, up_shape), in_specs=[A...  8.42 us
    pallas_call x1, Pallas kernels, fast_body(): pl.pallas_call(functools.partial(adapter_kernel, group, down_chunks), out...  6.37 us
    pallas_call x1, Pallas kernels, fast_body(): pl.pallas_call(functools.partial(scatter_kernel, 2 * group, down_chunks,...  6.08 us
    pallas_call x1, Pallas kernels, fast_body(): pl.pallas_call(base_kernel, out_shape=(sums, sums), in_specs=[VMEM] * 6 +...  3.7 us
  transfers between devices with their start and end apart: 37, of which 15 were waited for; matrix products, arithmetic and copies ran while one was open for 1% of the time, Pallas kernels for 25%

profile of v3, /device:TPU:0, one launch (start us, length us, event | category | flops | bytes accessed | tf_op | source)
XLA Modules:
  0.0 143.9 jit_solution(1505337040178020849)
XLA Ops:
  7.2 1.0 copy-done
  8.3 0.7 constant_dynamic-slice_fusion
  9.7 1.3 fusion.1
  11.0 0.6 broadcast_in_dim.20.refs_0_.refs_6_
  11.7 3.0 %collective-permute-start.2 = (s32[128]{0:T(128)S(1)}, s32[128]{0:T(128)S(1)}, u32[]{:S(2)}, u32[]{:S(2)}) collective-permute-start(s32[128]{0:T(128)S(1)} %broadcast_in_dim.20.refs_0_.refs_6_), channel_id=1, source_target_pairs={{0,1},{1,0},{2,3},{3,2},{4,5},{5,4},{6,7},{7,6},{8,9},{9,8},{10,11... | collective-permute-start | bytes 1544 | tf_op jit(solution)/shard_map/ppermute | solution.py:318
  14.7 1.6 %collective-permute-start.3 = (s32[128]{0:T(128)S(1)}, s32[128]{0:T(128)S(1)}, u32[]{:S(2)}, u32[]{:S(2)}) collective-permute-start(s32[128]{0:T(128)S(1)} %broadcast_in_dim.20.refs_0_.refs_6_), channel_id=1, source_target_pairs={{0,2},{1,3},{2,0},{3,1},{4,6},{5,7},{6,4},{7,5},{8,10},{9,11},{10,... | collective-permute-start | bytes 1544 | tf_op jit(solution)/shard_map/ppermute | solution.py:318
  16.2 3.0 %collective-permute-start.7 = (s32[128]{0:T(128)S(1)}, s32[128]{0:T(128)S(1)}, u32[]{:S(2)}, u32[]{:S(2)}) collective-permute-start(s32[128]{0:T(128)S(1)} %broadcast_in_dim.20.refs_0_.refs_6_), channel_id=1, source_target_pairs={{0,4},{1,5},{2,6},{3,7},{4,0},{5,1},{6,2},{7,3},{8,12},{9,13},{10,... | collective-permute-start | bytes 1544 | tf_op jit(solution)/shard_map/ppermute | solution.py:318
  19.3 1.3 collective-permute-start.8
  20.5 3.6 %collective-permute-start.9 = (s32[128]{0:T(128)S(1)}, s32[128]{0:T(128)S(1)}, u32[]{:S(2)}, u32[]{:S(2)}) collective-permute-start(s32[128]{0:T(128)S(1)} %broadcast_in_dim.20.refs_0_.refs_6_), channel_id=1, source_target_pairs={{0,6},{1,7},{2,4},{3,5},{4,2},{5,3},{6,0},{7,1},{8,14},{9,15},{10,... | collective-permute-start | bytes 1544 | tf_op jit(solution)/shard_map/ppermute | solution.py:318
  24.2 0.4 copy-done.28
  24.6 0.6 copy-done.29
  25.2 5.5 %pick_panels.2 = (bf16[384,128]{1,0:T(8,128)(2,1)}, bf16[384,128]{1,0:T(8,128)(2,1)}, bf16[384,128]{1,0:T(8,128)(2,1)}, bf16[384,128]{1,0:T(8,128)(2,1)}, s32[4]{0:T(128)}) custom-call(s32[128]{0:T(128)} %copy-done.26, s32[128]{0:T(128)} %copy-done.27, s32[128]{0:T(128)} %copy-done.28, s32[128]{0:T(128)} %copy-done.29, bf16[256,40960]{1,0:T(8,128)(2,1)} %refs_8_.1, ...), custom_call_target="tpu_custom_call" | custom-call | tf_op jit(solution)/shard_map/pick_panels/pallas_call | solution.py:349
  30.7 0.5 copy-done.32
  31.3 5.6 %pick_panels.3 = (bf16[384,128]{1,0:T(8,128)(2,1)}, bf16[384,128]{1,0:T(8,128)(2,1)}, bf16[384,128]{1,0:T(8,128)(2,1)}, bf16[384,128]{1,0:T(8,128)(2,1)}, s32[8]{0:T(128)}) custom-call(s32[128]{0:T(128)} %copy-done.26, s32[128]{0:T(128)} %copy-done.27, s32[128]{0:T(128)} %copy-done.28, s32[128]{0:T(128)} %copy-done.29, s32[128]{0:T(128)} %copy-done.32, ...), custom_call_target="tpu_custom_call" | custom-call | tf_op jit(solution)/shard_map/pick_panels/pallas_call | solution.py:349
  37.0 5.3 %collective-permute-start.11 = (bf16[384,128]{1,0:T(8,128)(2,1)}, bf16[384,128]{1,0:T(8,128)(2,1)S(1)}, u32[]{:S(2)}, u32[]{:S(2)}) collective-permute-start(bf16[384,128]{1,0:T(8,128)(2,1)} %get-tuple-element.36.after_ref), channel_id=1, source_target_pairs={{0,7},{1,6},{2,5},{3,4},{4,3},{5,2},{6,1},{7,0},{8,15},{9,14},{10,... | collective-permute-start | bytes 294920 | tf_op jit(solution)/shard_map/ppermute | solution.py:318
  42.3 2.5 %split_tokens.1 = (bf16[4,128,640]{2,1,0:T(8,128)(2,1)}, bf16[4,128,640]{2,1,0:T(8,128)(2,1)}) custom-call(s32[1]{0:T(128)} %bitcast.where, bf16[128,5120]{1,0:T(8,128)(2,1)} %x_ref.3), custom_call_target="tpu_custom_call" | custom-call | tf_op jit(solution)/shard_map/split_tokens/pallas_call | solution.py:335
  44.8 0.5 collective-permute-start.1
  45.3 1.9 %collective-permute-done.11.rest_7_ = bf16[384,128]{1,0:T(8,128)(2,1)S(1)} collective-permute-done((bf16[384,128]{1,0:T(8,128)(2,1)}, bf16[384,128]{1,0:T(8,128)(2,1)S(1)}, u32[]{:S(2)}, u32[]{:S(2)}) %collective-permute-start.11) | collective-permute-done | bytes 98336 | tf_op jit(solution)/shard_map/ppermute | solution.py:318
  47.2 2.7 %all-gather.2.cloned.1.call-done.refs_4_ = bf16[2560,256]{1,0:T(8,128)(2,1)} async-done(((bf16[640,256]{1,0:T(8,128)(2,1)}), bf16[2560,256]{1,0:T(8,128)(2,1)}) %all-gather.2.cloned.1.call-update) | async-done | bytes 1310736 | tf_op jit(solution)/shard_map/all_gather | solution.py:332
  49.9 0.4 collective-permute-start.5
  50.4 1.3 collective-permute-start
  51.7 3.5 %collective-permute-done.5.rest_2_ = bf16[384,128]{1,0:T(8,128)(2,1)S(1)} collective-permute-done((bf16[384,128]{1,0:T(8,128)(2,1)S(1)}, bf16[384,128]{1,0:T(8,128)(2,1)S(1)}, u32[]{:S(2)}, u32[]{:S(2)}) %collective-permute-start.5) | collective-permute-done | bytes 98336 | tf_op jit(solution)/shard_map/ppermute | solution.py:318
  55.2 4.5 %collective-permute-done.1.refs_2_ = bf16[4,128,640]{2,1,0:T(8,128)(2,1)} collective-permute-done((bf16[4,128,640]{2,1,0:T(8,128)(2,1)}, bf16[4,128,640]{2,1,0:T(8,128)(2,1)}, u32[]{:S(2)}, u32[]{:S(2)}) %collective-permute-start.1) | collective-permute-done | bytes 655392 | tf_op jit(solution)/shard_map/ppermute | solution.py:318
  59.7 1.0 collective-permute-start.6
  60.7 1.2 collective-permute-start.13
  61.9 3.4 %collective-permute-done.13.rest_1_ = bf16[384,128]{1,0:T(8,128)(2,1)S(1)} collective-permute-done((bf16[384,128]{1,0:T(8,128)(2,1)S(1)}, bf16[384,128]{1,0:T(8,128)(2,1)S(1)}, u32[]{:S(2)}, u32[]{:S(2)}) %collective-permute-start.13) | collective-permute-done | bytes 98336 | tf_op jit(solution)/shard_map/ppermute | solution.py:318
  65.4 1.8 %pair_columns.1.xs_ref = bf16[8,256,320]{2,1,0:T(8,128)(2,1)S(1)} custom-call(bf16[128,5120]{1,0:T(8,128)(2,1)S(1)} %copy-done.3), custom_call_target="tpu_custom_call" | custom-call | tf_op jit(solution)/shard_map/pair_columns/pallas_call | solution.py:342
  67.2 1.6 %collective-permute-done.14.rest_3_ = bf16[384,128]{1,0:T(8,128)(2,1)} collective-permute-done((bf16[384,128]{1,0:T(8,128)(2,1)}, bf16[384,128]{1,0:T(8,128)(2,1)}, u32[]{:S(2)}, u32[]{:S(2)}) %collective-permute-start.14) | collective-permute-done | bytes 98336 | tf_op jit(solution)/shard_map/ppermute | solution.py:318
  68.8 2.0 %collective-permute-start.16 = (bf16[384,128]{1,0:T(8,128)(2,1)}, bf16[384,128]{1,0:T(8,128)(2,1)S(1)}, u32[]{:S(2)}, u32[]{:S(2)}) collective-permute-start(bf16[384,128]{1,0:T(8,128)(2,1)} %get-tuple-element.41), channel_id=1, source_target_pairs={{0,5},{1,4},{2,7},{3,6},{4,1},{5,0},{6,3},{7,2},{8,13},{9,12},{10,... | collective-permute-start | bytes 294920 | tf_op jit(solution)/shard_map/ppermute | solution.py:318
  70.8 4.6 %collective-permute-done.15.rest_4_ = bf16[384,128]{1,0:T(8,128)(2,1)} collective-permute-done((bf16[384,128]{1,0:T(8,128)(2,1)}, bf16[384,128]{1,0:T(8,128)(2,1)}, u32[]{:S(2)}, u32[]{:S(2)}) %collective-permute-start.15) | collective-permute-done | bytes 98336 | tf_op jit(solution)/shard_map/ppermute | solution.py:318
  75.4 1.1 collective-permute-start.17
  76.5 0.1 pad_add_fusion.where
  76.5 8.4 %clear_rows.1 = (f32[16,320,8,1,128]{4,3,2,1,0:T(1,128)}, f32[16,64,8,1,128]{4,3,2,1,0:T(1,128)}) custom-call(bf16[384,128]{1,0:T(8,128)(2,1)} %get-tuple-element.36.after_ref), custom_call_target="tpu_custom_call" | custom-call | tf_op jit(solution)/shard_map/clear_rows/pallas_call | solution.py:378
  85.0 7.0 %copy-done.2 = f32[16,320,8,1,128]{4,3,2,1,0:T(1,128)S(1)} copy-done((f32[16,320,8,1,128]{4,3,2,1,0:T(1,128)S(1)}, f32[16,320,8,1,128]{4,3,2,1,0:T(1,128)}, u32[]{:S(2)}) %copy-start.2) | copy-done | bytes 20971544
  92.0 0.9 copy-done.10
  92.9 6.4 %adapter.1 = (bf16[384,128]{1,0:T(8,128)(2,1)S(1)}, bf16[384,128]{1,0:T(8,128)(2,1)S(1)}, bf16[384,128]{1,0:T(8,128)(2,1)S(1)}, bf16[384,128]{1,0:T(8,128)(2,1)S...) custom-call(s32[4]{0:T(128)S(1)} %pad_add_fusion.where, ...), custom_call_target="tpu_custom_call" | custom-call | tf_op jit(solution)/shard_map/adapter/pallas_call | solution.py:384
  99.3 3.7 %frozen_part.1 = (f32[256,512]{1,0:T(8,128)S(1)}, f32[256,512]{1,0:T(8,128)S(1)}) custom-call(bf16[4,128,640]{2,1,0:T(8,128)(2,1)S(1)} %copy-done.5, bf16[4,128,640]{2,1,0:T(8,128)(2,1)} %collective-permute-done.refs_1_, bf16[4,128,640]{2,1,0:T(8,128)(2,1)} %collective-permute-done.1.refs_2_, bf16[4,128,640]{2,1,0:T(8,128)(2,1)} %collective-permute-done.6.refs_3_, ...), custom_call_target="tpu_custom_call" | custom-call | tf_op jit(solution)/shard_map/frozen_part/pallas_call | solution.py:426
  103.0 2.3 %collective-permute-start.18 = (f32[256,512]{1,0:T(8,128)S(1)}, f32[256,512]{1,0:T(8,128)S(1)}, u32[]{:S(2)}, u32[]{:S(2)}) collective-permute-start(f32[256,512]{1,0:T(8,128)S(1)} %get-tuple-element.46), channel_id=1, source_target_pairs={{0,1},{1,0},{2,3},{3,2},{4,5},{5,4},{6,7},{7,6},{8,9},{9,8},{10,11... | collective-permute-start | bytes 1572872 | tf_op jit(solution)/shard_map/ppermute | solution.py:318
  105.3 0.1 collective-permute-start.21
  105.4 3.4 %collective-permute-start.23 = (bf16[384,128]{1,0:T(8,128)(2,1)S(1)}, bf16[384,128]{1,0:T(8,128)(2,1)S(1)}, u32[]{:S(2)}, u32[]{:S(2)}) collective-permute-start(bf16[384,128]{1,0:T(8,128)(2,1)S(1)} %get-tuple-element.51), channel_id=1, source_target_pairs={{0,3},{1,2},{2,1},{3,0},{4,7},{5,6},{6,5},{7,4},{8,11},{9,10},{10,... | collective-permute-start | bytes 294920 | tf_op jit(solution)/shard_map/ppermute | solution.py:318
  108.8 1.1 collective-permute-done.20.rows_core
  109.9 0.3 collective-permute-start.24
  110.2 4.4 %collective-permute-done.21.rest_1_ = bf16[384,128]{1,0:T(8,128)(2,1)S(1)} collective-permute-done((bf16[384,128]{1,0:T(8,128)(2,1)S(1)}, bf16[384,128]{1,0:T(8,128)(2,1)S(1)}, u32[]{:S(2)}, u32[]{:S(2)}) %collective-permute-start.21) | collective-permute-done | bytes 98336 | tf_op jit(solution)/shard_map/ppermute | solution.py:318
  114.6 2.6 %collective-permute-start.26 = (bf16[384,128]{1,0:T(8,128)(2,1)S(1)}, bf16[384,128]{1,0:T(8,128)(2,1)S(1)}, u32[]{:S(2)}, u32[]{:S(2)}) collective-permute-start(bf16[384,128]{1,0:T(8,128)(2,1)S(1)} %get-tuple-element.54), channel_id=1, source_target_pairs={{0,6},{1,7},{2,4},{3,5},{4,2},{5,3},{6,0},{7,1},{8,14},{9,15},{10,... | collective-permute-start | bytes 294920 | tf_op jit(solution)/shard_map/ppermute | solution.py:318
  117.2 2.7 %collective-permute-start.27 = (bf16[384,128]{1,0:T(8,128)(2,1)S(1)}, bf16[384,128]{1,0:T(8,128)(2,1)S(1)}, u32[]{:S(2)}, u32[]{:S(2)}) collective-permute-start(bf16[384,128]{1,0:T(8,128)(2,1)S(1)} %get-tuple-element.55), channel_id=1, source_target_pairs={{0,7},{1,6},{2,5},{3,4},{4,3},{5,2},{6,1},{7,0},{8,15},{9,14},{10,... | collective-permute-start | bytes 294920 | tf_op jit(solution)/shard_map/ppermute | solution.py:318
  120.0 0.1 add.16
  120.1 0.1 collective-permute-start.19
  120.2 2.5 %collective-permute-done.24.rest_4_ = bf16[384,128]{1,0:T(8,128)(2,1)S(1)} collective-permute-done((bf16[384,128]{1,0:T(8,128)(2,1)S(1)}, bf16[384,128]{1,0:T(8,128)(2,1)S(1)}, u32[]{:S(2)}, u32[]{:S(2)}) %collective-permute-start.24) | collective-permute-done | bytes 98336 | tf_op jit(solution)/shard_map/ppermute | solution.py:318
  122.7 3.4 %collective-permute-done.25.rest_5_ = bf16[384,128]{1,0:T(8,128)(2,1)S(1)} collective-permute-done((bf16[384,128]{1,0:T(8,128)(2,1)S(1)}, bf16[384,128]{1,0:T(8,128)(2,1)S(1)}, u32[]{:S(2)}, u32[]{:S(2)}) %collective-permute-start.25) | collective-permute-done | bytes 98336 | tf_op jit(solution)/shard_map/ppermute | solution.py:318
  126.1 0.5 collective-permute-start.30
  126.6 0.1 collective-permute-start.31
  126.7 0.4 collective-permute-start.32
  127.1 0.3 collective-permute-done.29.rest_9_
  127.4 0.2 collective-permute-start.33
  127.6 0.4 collective-permute-start.34
  127.9 0.2 collective-permute-start.35
  128.1 0.6 collective-permute-done.33.rest_13_
  128.7 0.2 collective-permute-done.34.rest_14_
  128.9 0.4 collective-permute-done.35.rest_15_
  129.2 0.1 copy-done.23
  129.4 0.1 copy-done.24
  129.5 0.5 copy-done.25
  130.1 6.1 %place_rows.1 = (f32[16,320,8,1,128]{4,3,2,1,0:T(1,128)}, f32[16,64,8,1,128]{4,3,2,1,0:T(1,128)}) custom-call(s32[1]{0:T(128)} %bitcast.5.first_row, s32[8]{0:T(128)} %get-tuple-element.48.rows_here, s32[8]{0:T(128)} %copy-done.31, bf16[384,128]{1,0:T(8,128)(2,1)} %copy-done.7, ...), custom_call_target="tpu_custom_call", output_to_operand_aliasing={{0}: (19, {}), {1}: (20, {})} | custom-call | tf_op jit(solution)/shard_map/place_rows/pallas_call | solution.py:402
  136.3 0.8 fusion
  (103 shorter events, 0.5 us)
Async XLA Ops:
  7.2 42.8 %all-gather.2.cloned.1.call-start = ((), (), s32[]{:S(2)}) async-start(), calls=%async_computation | async-start | bytes 1638400 | tf_op jit(solution)/shard_map/all_gather | solution.py:332
  11.6 12.5 %copy-start.26 = (s32[128]{0:T(128)}, s32[128]{0:T(128)S(1)}, u32[]{:S(2)}) copy-start(s32[128]{0:T(128)S(1)} %broadcast_in_dim.20.refs_0_.refs_6_) | copy-start | bytes 1540
  11.7 8.9 %collective-permute-start.2 = (s32[128]{0:T(128)S(1)}, s32[128]{0:T(128)S(1)}, u32[]{:S(2)}, u32[]{:S(2)}) collective-permute-start(s32[128]{0:T(128)S(1)} %broadcast_in_dim.20.refs_0_.refs_6_), channel_id=1, source_target_pairs={{0,1},{1,0},{2,3},{3,2},{4,5},{5,4},{6,7},{7,6},{8,9},{9,8},{10,11... | collective-permute-start | bytes 1544 | tf_op jit(solution)/shard_map/ppermute | solution.py:318
  14.7 9.5 %collective-permute-start.3 = (s32[128]{0:T(128)S(1)}, s32[128]{0:T(128)S(1)}, u32[]{:S(2)}, u32[]{:S(2)}) collective-permute-start(s32[128]{0:T(128)S(1)} %broadcast_in_dim.20.refs_0_.refs_6_), channel_id=1, source_target_pairs={{0,2},{1,3},{2,0},{3,1},{4,6},{5,7},{6,4},{7,5},{8,10},{9,11},{10,... | collective-permute-start | bytes 1544 | tf_op jit(solution)/shard_map/ppermute | solution.py:318
  16.2 7.9 %collective-permute-start.4 = (s32[128]{0:T(128)S(1)}, s32[128]{0:T(128)S(1)}, u32[]{:S(2)}, u32[]{:S(2)}) collective-permute-start(s32[128]{0:T(128)S(1)} %broadcast_in_dim.20.refs_0_.refs_6_), channel_id=1, source_target_pairs={{0,3},{1,2},{2,1},{3,0},{4,7},{5,6},{6,5},{7,4},{8,11},{9,10},{10,... | collective-permute-start | bytes 1544 | tf_op jit(solution)/shard_map/ppermute | solution.py:318
  16.2 14.4 %collective-permute-start.7 = (s32[128]{0:T(128)S(1)}, s32[128]{0:T(128)S(1)}, u32[]{:S(2)}, u32[]{:S(2)}) collective-permute-start(s32[128]{0:T(128)S(1)} %broadcast_in_dim.20.refs_0_.refs_6_), channel_id=1, source_target_pairs={{0,4},{1,5},{2,6},{3,7},{4,0},{5,1},{6,2},{7,3},{8,12},{9,13},{10,... | collective-permute-start | bytes 1544 | tf_op jit(solution)/shard_map/ppermute | solution.py:318
  19.3 11.4 %collective-permute-start.8 = (s32[128]{0:T(128)S(1)}, s32[128]{0:T(128)S(1)}, u32[]{:S(2)}, u32[]{:S(2)}) collective-permute-start(s32[128]{0:T(128)S(1)} %broadcast_in_dim.20.refs_0_.refs_6_), channel_id=1, source_target_pairs={{0,5},{1,4},{2,7},{3,6},{4,1},{5,0},{6,3},{7,2},{8,13},{9,12},{10,... | collective-permute-start | bytes 1544 | tf_op jit(solution)/shard_map/ppermute | solution.py:318
  20.5 3.7 %copy-start.27 = (s32[128]{0:T(128)}, s32[128]{0:T(128)S(1)}, u32[]{:S(2)}) copy-start(s32[128]{0:T(128)S(1)} %collective-permute-done.2.refs_1_) | copy-start | bytes 1540
  20.5 10.2 %collective-permute-start.9 = (s32[128]{0:T(128)S(1)}, s32[128]{0:T(128)S(1)}, u32[]{:S(2)}, u32[]{:S(2)}) collective-permute-start(s32[128]{0:T(128)S(1)} %broadcast_in_dim.20.refs_0_.refs_6_), channel_id=1, source_target_pairs={{0,6},{1,7},{2,4},{3,5},{4,2},{5,3},{6,0},{7,1},{8,14},{9,15},{10,... | collective-permute-start | bytes 1544 | tf_op jit(solution)/shard_map/ppermute | solution.py:318
  24.1 6.6 %collective-permute-start.10 = (s32[128]{0:T(128)S(1)}, s32[128]{0:T(128)S(1)}, u32[]{:S(2)}, u32[]{:S(2)}) collective-permute-start(s32[128]{0:T(128)S(1)} %broadcast_in_dim.20.refs_0_.refs_6_), channel_id=1, source_target_pairs={{0,7},{1,6},{2,5},{3,4},{4,3},{5,2},{6,1},{7,0},{8,15},{9,14},{10,... | collective-permute-start | bytes 1544 | tf_op jit(solution)/shard_map/ppermute | solution.py:318
  31.3 18.6 %copy-start.37 = (bf16[384,128]{1,0:T(8,128)(2,1)S(1)}, bf16[384,128]{1,0:T(8,128)(2,1)}, u32[]{:S(2)}) copy-start(bf16[384,128]{1,0:T(8,128)(2,1)} %get-tuple-element.33) | copy-start | bytes 294916
  31.3 29.4 %copy-start.36 = (bf16[384,128]{1,0:T(8,128)(2,1)S(1)}, bf16[384,128]{1,0:T(8,128)(2,1)}, u32[]{:S(2)}) copy-start(bf16[384,128]{1,0:T(8,128)(2,1)} %get-tuple-element.38) | copy-start | bytes 294916
  31.3 34.0 %copy-start.3 = (bf16[128,5120]{1,0:T(8,128)(2,1)S(1)}, bf16[128,5120]{1,0:T(8,128)(2,1)}, u32[]{:S(2)}) copy-start(bf16[128,5120]{1,0:T(8,128)(2,1)} %x_ref.3) | copy-start | bytes 3932164
  37.0 48.0 %copy-start.6 = (bf16[384,128]{1,0:T(8,128)(2,1)S(1)}, bf16[384,128]{1,0:T(8,128)(2,1)}, u32[]{:S(2)}) copy-start(bf16[384,128]{1,0:T(8,128)(2,1)} %get-tuple-element.35.refs_10_.rest_0_) | copy-start | bytes 294916
  37.0 48.0 %copy-start.8 = (bf16[128,1024]{1,0:T(8,128)(2,1)S(1)}, bf16[128,1024]{1,0:T(8,128)(2,1)}, u32[]{:S(2)}) copy-start(bf16[128,1024]{1,0:T(8,128)(2,1)} %g_ref.1) | copy-start | bytes 786436
  37.0 10.2 %collective-permute-start.11 = (bf16[384,128]{1,0:T(8,128)(2,1)}, bf16[384,128]{1,0:T(8,128)(2,1)S(1)}, u32[]{:S(2)}, u32[]{:S(2)}) collective-permute-start(bf16[384,128]{1,0:T(8,128)(2,1)} %get-tuple-element.36.after_ref), channel_id=1, source_target_pairs={{0,7},{1,6},{2,5},{3,4},{4,3},{5,2},{6,1},{7,0},{8,15},{9,14},{10,... | collective-permute-start | bytes 294920 | tf_op jit(solution)/shard_map/ppermute | solution.py:318
  44.8 14.9 %collective-permute-start.1 = (bf16[4,128,640]{2,1,0:T(8,128)(2,1)}, bf16[4,128,640]{2,1,0:T(8,128)(2,1)}, u32[]{:S(2)}, u32[]{:S(2)}) collective-permute-start(bf16[4,128,640]{2,1,0:T(8,128)(2,1)} %get-tuple-element.32), channel_id=1, source_target_pairs={{0,1},{1,0},{2,3},{3,2},{4,5},{5,4},{6,7},{7,6},{8,9},{9,8},{10,11... | collective-permute-start | bytes 1966088 | tf_op jit(solution)/shard_map/ppermute | solution.py:318
  49.9 49.4 %collective-permute-start.12 = (bf16[2560,256]{1,0:T(8,128)(2,1)}, bf16[2560,256]{1,0:T(8,128)(2,1)}, u32[]{:S(2)}, u32[]{:S(2)}) collective-permute-start(bf16[2560,256]{1,0:T(8,128)(2,1)} %all-gather.2.cloned.1.call-done.refs_4_), channel_id=1, source_target_pairs={{0,8},{8,0},{1,9},{9,1},{2,10},{10,2},{3,11},{11,3},{4,12},{12,4},... | collective-permute-start | bytes 3932168 | tf_op jit(solution)/shard_map/ppermute | solution.py:321
  49.9 5.2 %collective-permute-start.5 = (bf16[384,128]{1,0:T(8,128)(2,1)S(1)}, bf16[384,128]{1,0:T(8,128)(2,1)S(1)}, u32[]{:S(2)}, u32[]{:S(2)}) collective-permute-start(bf16[384,128]{1,0:T(8,128)(2,1)S(1)} %copy-done.37), channel_id=1, source_target_pairs={{0,2},{1,3},{2,0},{3,1},{4,6},{5,7},{6,4},{7,5},{8,10},{9,11},{10,... | collective-permute-start | bytes 294920 | tf_op jit(solution)/shard_map/ppermute | solution.py:318
  50.4 48.9 %collective-permute-start = (bf16[4,128,640]{2,1,0:T(8,128)(2,1)}, bf16[4,128,640]{2,1,0:T(8,128)(2,1)}, u32[]{:S(2)}, u32[]{:S(2)}) collective-permute-start(bf16[4,128,640]{2,1,0:T(8,128)(2,1)} %get-tuple-element.31.refs_0_), channel_id=1, source_target_pairs={{0,16},{16,0},{1,17},{17,1},{2,18},{18,2},{3,19},{19,3},{4,20},{20... | collective-permute-start | bytes 1966088 | tf_op jit(solution)/shard_map/ppermute | solution.py:324
  59.7 39.6 %collective-permute-start.6 = (bf16[4,128,640]{2,1,0:T(8,128)(2,1)}, bf16[4,128,640]{2,1,0:T(8,128)(2,1)}, u32[]{:S(2)}, u32[]{:S(2)}) collective-permute-start(bf16[4,128,640]{2,1,0:T(8,128)(2,1)} %collective-permute-done.1.refs_2_), channel_id=1, source_target_pairs={{0,16},{16,0},{1,17},{17,1},{2,18},{18,2},{3,19},{19,3},{4,20},{20... | collective-permute-start | bytes 1966088 | tf_op jit(solution)/shard_map/ppermute | solution.py:324
  60.7 4.6 %collective-permute-start.13 = (bf16[384,128]{1,0:T(8,128)(2,1)S(1)}, bf16[384,128]{1,0:T(8,128)(2,1)S(1)}, u32[]{:S(2)}, u32[]{:S(2)}) collective-permute-start(bf16[384,128]{1,0:T(8,128)(2,1)S(1)} %copy-done.36), channel_id=1, source_target_pairs={{0,1},{1,0},{2,3},{3,2},{4,5},{5,4},{6,7},{7,6},{8,9},{9,8},{10,11... | collective-permute-start | bytes 294920 | tf_op jit(solution)/shard_map/ppermute | solution.py:318
  61.9 6.9 %collective-permute-start.14 = (bf16[384,128]{1,0:T(8,128)(2,1)}, bf16[384,128]{1,0:T(8,128)(2,1)}, u32[]{:S(2)}, u32[]{:S(2)}) collective-permute-start(bf16[384,128]{1,0:T(8,128)(2,1)} %get-tuple-element.39), channel_id=1, source_target_pairs={{0,3},{1,2},{2,1},{3,0},{4,7},{5,6},{6,5},{7,4},{8,11},{9,10},{10,... | collective-permute-start | bytes 294920 | tf_op jit(solution)/shard_map/ppermute | solution.py:318
  65.3 19.6 %copy-start.9 = (bf16[384,128]{1,0:T(8,128)(2,1)}, bf16[384,128]{1,0:T(8,128)(2,1)S(1)}, u32[]{:S(2)}) copy-start(bf16[384,128]{1,0:T(8,128)(2,1)S(1)} %collective-permute-done.13.rest_1_) | copy-start | bytes 294916
  65.3 10.0 %collective-permute-start.15 = (bf16[384,128]{1,0:T(8,128)(2,1)}, bf16[384,128]{1,0:T(8,128)(2,1)}, u32[]{:S(2)}, u32[]{:S(2)}) collective-permute-start(bf16[384,128]{1,0:T(8,128)(2,1)} %get-tuple-element.40), channel_id=1, source_target_pairs={{0,4},{1,5},{2,6},{3,7},{4,0},{5,1},{6,2},{7,3},{8,12},{9,13},{10,... | collective-permute-start | bytes 294920 | tf_op jit(solution)/shard_map/ppermute | solution.py:318
  68.8 16.2 %collective-permute-start.16 = (bf16[384,128]{1,0:T(8,128)(2,1)}, bf16[384,128]{1,0:T(8,128)(2,1)S(1)}, u32[]{:S(2)}, u32[]{:S(2)}) collective-permute-start(bf16[384,128]{1,0:T(8,128)(2,1)} %get-tuple-element.41), channel_id=1, source_target_pairs={{0,5},{1,4},{2,7},{3,6},{4,1},{5,0},{6,3},{7,2},{8,13},{9,12},{10,... | collective-permute-start | bytes 294920 | tf_op jit(solution)/shard_map/ppermute | solution.py:318
  75.4 9.6 %collective-permute-start.17 = (bf16[384,128]{1,0:T(8,128)(2,1)}, bf16[384,128]{1,0:T(8,128)(2,1)S(1)}, u32[]{:S(2)}, u32[]{:S(2)}) collective-permute-start(bf16[384,128]{1,0:T(8,128)(2,1)} %get-tuple-element.42), channel_id=1, source_target_pairs={{0,6},{1,7},{2,4},{3,5},{4,2},{5,3},{6,0},{7,1},{8,14},{9,15},{10,... | collective-permute-start | bytes 294920 | tf_op jit(solution)/shard_map/ppermute | solution.py:318
  85.0 7.0 %copy-start.2 = (f32[16,320,8,1,128]{4,3,2,1,0:T(1,128)S(1)}, f32[16,320,8,1,128]{4,3,2,1,0:T(1,128)}, u32[]{:S(2)}) copy-start(f32[16,320,8,1,128]{4,3,2,1,0:T(1,128)} %get-tuple-element.43.rest_8_.rest_16_) | copy-start | bytes 62914564
  92.9 6.4 %copy-start.4 = (bf16[2560,256]{1,0:T(8,128)(2,1)S(1)}, bf16[2560,256]{1,0:T(8,128)(2,1)}, u32[]{:S(2)}) copy-start(bf16[2560,256]{1,0:T(8,128)(2,1)} %all-gather.2.cloned.1.call-done.refs_4_) | copy-start | bytes 3932164
  92.9 6.4 %copy-start.5 = (bf16[4,128,640]{2,1,0:T(8,128)(2,1)S(1)}, bf16[4,128,640]{2,1,0:T(8,128)(2,1)}, u32[]{:S(2)}) copy-start(bf16[4,128,640]{2,1,0:T(8,128)(2,1)} %get-tuple-element.31.refs_0_) | copy-start | bytes 1966084
  99.3 30.7 %copy-start.7 = (bf16[384,128]{1,0:T(8,128)(2,1)}, bf16[384,128]{1,0:T(8,128)(2,1)S(1)}, u32[]{:S(2)}) copy-start(bf16[384,128]{1,0:T(8,128)(2,1)S(1)} %get-tuple-element.44.refs_6_.rest_0_) | copy-start | bytes 294916
  99.3 9.5 %copy-start.30 = (s32[8]{0:T(128)S(1)}, s32[8]{0:T(128)}, u32[]{:S(2)}) copy-start(s32[8]{0:T(128)} %get-tuple-element.48.rows_here) | copy-start | bytes 100
  103.0 14.2 %collective-permute-start.18 = (f32[256,512]{1,0:T(8,128)S(1)}, f32[256,512]{1,0:T(8,128)S(1)}, u32[]{:S(2)}, u32[]{:S(2)}) collective-permute-start(f32[256,512]{1,0:T(8,128)S(1)} %get-tuple-element.46), channel_id=1, source_target_pairs={{0,1},{1,0},{2,3},{3,2},{4,5},{5,4},{6,7},{7,6},{8,9},{9,8},{10,11... | collective-permute-start | bytes 1572872 | tf_op jit(solution)/shard_map/ppermute | solution.py:318
  105.3 9.3 %collective-permute-start.21 = (bf16[384,128]{1,0:T(8,128)(2,1)S(1)}, bf16[384,128]{1,0:T(8,128)(2,1)S(1)}, u32[]{:S(2)}, u32[]{:S(2)}) collective-permute-start(bf16[384,128]{1,0:T(8,128)(2,1)S(1)} %get-tuple-element.49), channel_id=1, source_target_pairs={{0,1},{1,0},{2,3},{3,2},{4,5},{5,4},{6,7},{7,6},{8,9},{9,8},{10,11... | collective-permute-start | bytes 294920 | tf_op jit(solution)/shard_map/ppermute | solution.py:318
  105.4 9.2 %collective-permute-start.22 = (bf16[384,128]{1,0:T(8,128)(2,1)S(1)}, bf16[384,128]{1,0:T(8,128)(2,1)S(1)}, u32[]{:S(2)}, u32[]{:S(2)}) collective-permute-start(bf16[384,128]{1,0:T(8,128)(2,1)S(1)} %get-tuple-element.50), channel_id=1, source_target_pairs={{0,2},{1,3},{2,0},{3,1},{4,6},{5,7},{6,4},{7,5},{8,10},{9,11},{10,... | collective-permute-start | bytes 294920 | tf_op jit(solution)/shard_map/ppermute | solution.py:318
  105.4 14.7 %collective-permute-start.23 = (bf16[384,128]{1,0:T(8,128)(2,1)S(1)}, bf16[384,128]{1,0:T(8,128)(2,1)S(1)}, u32[]{:S(2)}, u32[]{:S(2)}) collective-permute-start(bf16[384,128]{1,0:T(8,128)(2,1)S(1)} %get-tuple-element.51), channel_id=1, source_target_pairs={{0,3},{1,2},{2,1},{3,0},{4,7},{5,6},{6,5},{7,4},{8,11},{9,10},{10,... | collective-permute-start | bytes 294920 | tf_op jit(solution)/shard_map/ppermute | solution.py:318
  108.8 1.1 collective-permute-start.20
  109.9 20.1 %copy-start.31 = (s32[8]{0:T(128)}, s32[8]{0:T(128)S(1)}, u32[]{:S(2)}) copy-start(s32[8]{0:T(128)S(1)} %collective-permute-done.20.rows_core) | copy-start | bytes 100
  109.9 12.7 %collective-permute-start.24 = (bf16[384,128]{1,0:T(8,128)(2,1)S(1)}, bf16[384,128]{1,0:T(8,128)(2,1)S(1)}, u32[]{:S(2)}, u32[]{:S(2)}) collective-permute-start(bf16[384,128]{1,0:T(8,128)(2,1)S(1)} %get-tuple-element.52), channel_id=1, source_target_pairs={{0,4},{1,5},{2,6},{3,7},{4,0},{5,1},{6,2},{7,3},{8,12},{9,13},{10,... | collective-permute-start | bytes 294920 | tf_op jit(solution)/shard_map/ppermute | solution.py:318
  114.6 15.4 %copy-start.11 = (bf16[384,128]{1,0:T(8,128)(2,1)}, bf16[384,128]{1,0:T(8,128)(2,1)S(1)}, u32[]{:S(2)}) copy-start(bf16[384,128]{1,0:T(8,128)(2,1)S(1)} %collective-permute-done.21.rest_1_) | copy-start | bytes 294916
  114.6 11.5 %collective-permute-start.25 = (bf16[384,128]{1,0:T(8,128)(2,1)S(1)}, bf16[384,128]{1,0:T(8,128)(2,1)S(1)}, u32[]{:S(2)}, u32[]{:S(2)}) collective-permute-start(bf16[384,128]{1,0:T(8,128)(2,1)S(1)} %get-tuple-element.53), channel_id=1, source_target_pairs={{0,5},{1,4},{2,7},{3,6},{4,1},{5,0},{6,3},{7,2},{8,13},{9,12},{10,... | collective-permute-start | bytes 294920 | tf_op jit(solution)/shard_map/ppermute | solution.py:318
  114.6 15.4 %copy-start.12 = (bf16[384,128]{1,0:T(8,128)(2,1)}, bf16[384,128]{1,0:T(8,128)(2,1)S(1)}, u32[]{:S(2)}) copy-start(bf16[384,128]{1,0:T(8,128)(2,1)S(1)} %collective-permute-done.22.rest_2_) | copy-start | bytes 294916
  114.6 11.5 %collective-permute-start.26 = (bf16[384,128]{1,0:T(8,128)(2,1)S(1)}, bf16[384,128]{1,0:T(8,128)(2,1)S(1)}, u32[]{:S(2)}, u32[]{:S(2)}) collective-permute-start(bf16[384,128]{1,0:T(8,128)(2,1)S(1)} %get-tuple-element.54), channel_id=1, source_target_pairs={{0,6},{1,7},{2,4},{3,5},{4,2},{5,3},{6,0},{7,1},{8,14},{9,15},{10,... | collective-permute-start | bytes 294920 | tf_op jit(solution)/shard_map/ppermute | solution.py:318
  117.2 9.4 %collective-permute-start.27 = (bf16[384,128]{1,0:T(8,128)(2,1)S(1)}, bf16[384,128]{1,0:T(8,128)(2,1)S(1)}, u32[]{:S(2)}, u32[]{:S(2)}) collective-permute-start(bf16[384,128]{1,0:T(8,128)(2,1)S(1)} %get-tuple-element.55), channel_id=1, source_target_pairs={{0,7},{1,6},{2,5},{3,4},{4,3},{5,2},{6,1},{7,0},{8,15},{9,14},{10,... | collective-permute-start | bytes 294920 | tf_op jit(solution)/shard_map/ppermute | solution.py:318
  120.1 9.9 %copy-start.13 = (bf16[384,128]{1,0:T(8,128)(2,1)}, bf16[384,128]{1,0:T(8,128)(2,1)S(1)}, u32[]{:S(2)}) copy-start(bf16[384,128]{1,0:T(8,128)(2,1)S(1)} %collective-permute-done.23.rest_3_) | copy-start | bytes 294916
  120.1 16.1 %collective-permute-start.19 = (f32[128,512]{1,0:T(8,128)S(1)}, f32[128,512]{1,0:T(8,128)S(1)}, u32[]{:S(2)}, u32[]{:S(2)}) collective-permute-start(f32[128,512]{1,0:T(8,128)S(1)} %slice.25), channel_id=1, source_target_pairs={{0,16},{16,0},{1,17},{17,1},{2,18},{18,2},{3,19},{19,3},{4,20},{20... | collective-permute-start | bytes 786440 | tf_op jit(solution)/shard_map/ppermute | solution.py:324
  122.7 7.4 %copy-start.14 = (bf16[384,128]{1,0:T(8,128)(2,1)}, bf16[384,128]{1,0:T(8,128)(2,1)S(1)}, u32[]{:S(2)}) copy-start(bf16[384,128]{1,0:T(8,128)(2,1)S(1)} %collective-permute-done.24.rest_4_) | copy-start | bytes 294916
  122.7 4.0 %collective-permute-start.28 = (bf16[384,128]{1,0:T(8,128)(2,1)S(1)}, bf16[384,128]{1,0:T(8,128)(2,1)S(1)}, u32[]{:S(2)}, u32[]{:S(2)}) collective-permute-start(bf16[384,128]{1,0:T(8,128)(2,1)S(1)} %get-tuple-element.44.refs_6_.rest_0_), channel_id=1, source_target_pairs={{0,8},{8,0},{1,9},{9,1},{2,10},{10,2},{3,11},{11,3},{4,12},{12,4},... | collective-permute-start | bytes 294920 | tf_op jit(solution)/shard_map/ppermute | solution.py:321
  126.1 3.9 %copy-start.15 = (bf16[384,128]{1,0:T(8,128)(2,1)}, bf16[384,128]{1,0:T(8,128)(2,1)S(1)}, u32[]{:S(2)}) copy-start(bf16[384,128]{1,0:T(8,128)(2,1)S(1)} %collective-permute-done.25.rest_5_) | copy-start | bytes 294916
  126.1 1.3 collective-permute-start.29
  126.1 3.9 %copy-start.16 = (bf16[384,128]{1,0:T(8,128)(2,1)}, bf16[384,128]{1,0:T(8,128)(2,1)S(1)}, u32[]{:S(2)}) copy-start(bf16[384,128]{1,0:T(8,128)(2,1)S(1)} %collective-permute-done.26.rest_6_) | copy-start | bytes 294916
  126.1 1.4 %collective-permute-start.30 = (bf16[384,128]{1,0:T(8,128)(2,1)S(1)}, bf16[384,128]{1,0:T(8,128)(2,1)S(1)}, u32[]{:S(2)}, u32[]{:S(2)}) collective-permute-start(bf16[384,128]{1,0:T(8,128)(2,1)S(1)} %collective-permute-done.22.rest_2_), channel_id=1, source_target_pairs={{0,8},{8,0},{1,9},{9,1},{2,10},{10,2},{3,11},{11,3},{4,12},{12,4},... | collective-permute-start | bytes 294920 | tf_op jit(solution)/shard_map/ppermute | solution.py:321
  126.6 3.4 %copy-start.17 = (bf16[384,128]{1,0:T(8,128)(2,1)}, bf16[384,128]{1,0:T(8,128)(2,1)S(1)}, u32[]{:S(2)}) copy-start(bf16[384,128]{1,0:T(8,128)(2,1)S(1)} %collective-permute-done.27.rest_7_) | copy-start | bytes 294916
  126.6 1.3 collective-permute-start.31
  126.7 3.4 %copy-start.18 = (bf16[384,128]{1,0:T(8,128)(2,1)}, bf16[384,128]{1,0:T(8,128)(2,1)S(1)}, u32[]{:S(2)}) copy-start(bf16[384,128]{1,0:T(8,128)(2,1)S(1)} %collective-permute-done.28.rest_8_) | copy-start | bytes 294916
  126.7 1.4 collective-permute-start.32
  127.4 2.7 %copy-start.19 = (bf16[384,128]{1,0:T(8,128)(2,1)}, bf16[384,128]{1,0:T(8,128)(2,1)S(1)}, u32[]{:S(2)}) copy-start(bf16[384,128]{1,0:T(8,128)(2,1)S(1)} %collective-permute-done.29.rest_9_) | copy-start | bytes 294916
  127.4 1.3 collective-permute-start.33
  127.6 2.5 %copy-start.20 = (bf16[384,128]{1,0:T(8,128)(2,1)}, bf16[384,128]{1,0:T(8,128)(2,1)S(1)}, u32[]{:S(2)}) copy-start(bf16[384,128]{1,0:T(8,128)(2,1)S(1)} %collective-permute-done.30.rest_10_) | copy-start | bytes 294916
  127.6 1.3 collective-permute-start.34
  127.9 2.2 %copy-start.21 = (bf16[384,128]{1,0:T(8,128)(2,1)}, bf16[384,128]{1,0:T(8,128)(2,1)S(1)}, u32[]{:S(2)}) copy-start(bf16[384,128]{1,0:T(8,128)(2,1)S(1)} %collective-permute-done.31.rest_11_) | copy-start | bytes 294916
  127.9 1.3 collective-permute-start.35
  128.1 2.0 %copy-start.22 = (bf16[384,128]{1,0:T(8,128)(2,1)}, bf16[384,128]{1,0:T(8,128)(2,1)S(1)}, u32[]{:S(2)}) copy-start(bf16[384,128]{1,0:T(8,128)(2,1)S(1)} %collective-permute-done.32.rest_12_) | copy-start | bytes 294916
  130.1 6.9 %copy-start.1 = (bf16[640,512]{1,0:T(8,128)(2,1)S(1)}, bf16[640,512]{1,0:T(8,128)(2,1)}, u32[]{:S(2)}) copy-start(bf16[640,512]{1,0:T(8,128)(2,1)} %param.9) | copy-start | bytes 1966084
  (11 other events, 7.2 us)
Sparse Core Ops, SparseCore 0:
  10.2 39.7 all-gather.1

commit v4 on v3

--- a/solution.py
+++ b/solution.py
@@ -118,27 +118,27 @@
         xs_ref[k, rows:] = dot(x, odd).astype(jnp.bfloat16)
 
 
-def gather_kernel(first, count, down_chunks, up_chunks, *refs):
-    asked, (down_ref, up_ref, _) = refs[:first + count], refs[first + count:first + count + 3]
-    outs, rows_ref = refs[first + count + 3:-8], refs[-8]
-    down_buf, up_buf, flat, built, rows, sems, row_sem = refs[-7:]
-    for s in range(first + count):
+def gather_kernel(count, down_chunks, up_chunks, where, *refs):
+    asked, (down_ref, up_ref, out_ref, rows_ref) = refs[:count], refs[count:count + 4]
+    down_buf, up_buf, flat, built, rows, sems, row_sem = refs[count + 4:]
+    me = where[0]
+    for s in range(count):
         pltpu.make_async_copy(asked[s], rows.at[s], row_sem).start()
-    for s in range(first + count):
+    for s in range(count):
         pltpu.make_async_copy(asked[s], rows.at[s], row_sem).wait()
     copies = []
     for s in range(count):
-        start = pl.multiple_of((rows[first + s, 0] // GROUP_ROWS) * GROUP_ROWS, GROUP_ROWS)
+        start = pl.multiple_of((rows[s, 0] // GROUP_ROWS) * GROUP_ROWS, GROUP_ROWS)
         a = pltpu.make_async_copy(down_ref.at[pl.ds(start, GROUP_ROWS)], down_buf.at[s], sems.at[3 * s])
         b = pltpu.make_async_copy(up_ref.at[pl.ds(start, GROUP_ROWS)], up_buf.at[s], sems.at[3 * s + 1])
         a.start()
         b.start()
-        copies.append((a, b, pltpu.make_async_copy(built.at[s], outs[s], sems.at[3 * s + 2])))
-    for s in range(first + count):
-        rows_ref[s] = rows[s, 0]
+        copies.append((a, b, pltpu.make_async_copy(built.at[s], out_ref.at[me ^ s], sems.at[3 * s + 2])))
+    for s in range(count):
+        rows_ref[me ^ s] = rows[s, 0]
     step = 16
     for s in range(count):
-        row = rows[first + s, 0] % GROUP_ROWS
+        row = rows[s, 0] % GROUP_ROWS
         upper = row >= 8
         sub = row % 8
 
@@ -166,8 +166,9 @@
         copies[s][2].wait()
 
 
-def zero_kernel(after_ref, down_ref, up_ref, zeros, sems):
+def zero_kernel(after_ref, down_ref, up_ref, done_ref, zeros, sems):
     del after_ref
+    done_ref[0] = 0
     zeros[...] = jnp.zeros_like(zeros)
     part = zeros.shape[0]
     copies = []
@@ -181,26 +182,16 @@
         c.wait()
 
 
-def adapter_kernel(count, down_chunks, where, xs_ref, g_ref, *rest):
-    sources, targets = rest[:count], rest[count + 1:2 * count + 1]
-    lifted_ref, up_panel, pieces, outs, sems = rest[2 * count + 1:]
-    arriving = [pltpu.make_async_copy(sources[s], pieces.at[s], sems.at[0, s]) for s in range(count)]
-    leaving = [pltpu.make_async_copy(outs.at[s], targets[s], sems.at[1, s]) for s in range(count)]
-    for copy in arriving:
-        copy.start()
-    me = where[0]
+def adapter_kernel(count, down_chunks, xs_ref, g_ref, pieces, _, out_ref, lifted_ref, up_panel):
     rows = g_ref.shape[0]
     across = g_ref.shape[1] // LANES
     total = jnp.zeros((2 * rows, LANES), jnp.float32)
-    for s in range(count):
-        owner = me ^ s
-        arriving[s].wait()
-        total += dot(xs_ref[owner], pieces[s, :down_chunks])
-        at = pl.multiple_of(owner * 8, 8)
+    for t in range(count):
+        total += dot(xs_ref[t], pieces[t, :down_chunks])
         for c in range(across):
-            block = pieces[s, down_chunks + 8 * c:down_chunks + 8 * c + 8, :].astype(jnp.float32)
-            up_panel[pl.ds(at, 8), c * LANES:(c + 1) * LANES] = block
-            up_panel[pl.ds(R + at, 8), c * LANES:(c + 1) * LANES] = block
+            block = pieces[t, down_chunks + 8 * c:down_chunks + 8 * c + 8, :].astype(jnp.float32)
+            up_panel[8 * t:8 * t + 8, c * LANES:(c + 1) * LANES] = block
+            up_panel[R + 8 * t:R + 8 * t + 8, c * LANES:(c + 1) * LANES] = block
     panel = up_panel[...].astype(jnp.bfloat16)
     left = lax.broadcasted_iota(jnp.int32, (rows, LANES), 1) < R
     inner = total[:rows] + pltpu.roll(total[rows:], R, 1)
@@ -212,29 +203,22 @@
         [jnp.where(left, inner_grad, 0.0), jnp.where(left, 0.0, inner_grad)], axis=0
     ).astype(jnp.bfloat16)
     up_term = adapter_scale * t_dot(inner, g)
-    up_panel[...] = up_term
-    for s in range(count):
-        owner = me ^ s
-        outs[s, :down_chunks] = t_dot(xs_ref[owner], diagonal).astype(jnp.bfloat16)
-        at = pl.multiple_of(owner * 8, 8)
-        rows_here = up_panel[pl.ds(at, 8), :]
+    for t in range(count):
+        out_ref[t, :down_chunks] = t_dot(xs_ref[t], diagonal).astype(jnp.bfloat16)
         up_part = jnp.concatenate(
-            [rows_here[:, c * LANES:(c + 1) * LANES] for c in range(across)], axis=0
+            [up_term[8 * t:8 * t + 8, c * LANES:(c + 1) * LANES] for c in range(across)], axis=0
         )
-        outs[s, down_chunks:] = up_part.astype(jnp.bfloat16)
-        leaving[s].start()
-    for copy in leaving:
-        copy.wait()
+        out_ref[t, down_chunks:] = up_part.astype(jnp.bfloat16)
 
 
 def scatter_kernel(count, down_chunks, up_chunks, first_row, rows_here, rows_core, *rest):
-    sources = rest[:count]
-    down_out, up_out = rest[count + 2:count + 4]
-    pieces, down_sum, up_sum, ordered, arrived, sem = rest[count + 4:]
+    sources, (down_out, up_out) = rest[:2], rest[4:6]
+    pieces, down_sum, up_sum, ordered, arrived, sem = rest[6:]
+    half = count // 2
     owned_rows = down_out.shape[0] * 8
     across = up_chunks // 8
-    rows = [(rows_here if b < count // 2 else rows_core)[b % (count // 2)] - first_row[0] for b in range(count)]
-    arriving = [pltpu.make_async_copy(sources[b], pieces.at[b], arrived.at[b]) for b in range(count)]
+    rows = [(rows_here if b < half else rows_core)[b % half] - first_row[0] for b in range(count)]
+    arriving = [pltpu.make_async_copy(sources[b // half].at[b % half], pieces.at[b], arrived.at[b]) for b in range(count)]
     for copy in arriving:
         copy.start()
     owned = [(row >= 0) & (row < owned_rows) for row in rows]
@@ -309,10 +293,8 @@
     slice_width = D // group
     down_chunks = down_store.shape[1] // LANES
     up_chunks = up_store.shape[1] // LANES
-    piece = jax.ShapeDtypeStruct((down_chunks + up_chunks, LANES), jnp.bfloat16)
     me, part, core = lax.axis_index("tensor"), lax.axis_index("parts"), lax.axis_index("dp")
-    z, x = me // 2, me % 2
-    here = jnp.stack([me, x, z, part])
+    x = me % 2
 
     def exchange(value, s):
         return lax.ppermute(value, "tensor", [(t, t ^ s) for t in range(group)])
@@ -345,82 +327,49 @@
         in_specs=[VMEM], out_specs=VMEM, name="pair_columns", compiler_params=LIMIT,
     )(tokens)
 
-    def pick(first, count, after):
-        return pl.pallas_call(
-            functools.partial(gather_kernel, first, count, down_chunks, up_chunks),
-            out_shape=[piece] * count + [jax.ShapeDtypeStruct((first + count,), jnp.int32)],
-            in_specs=[ANY] * (first + count + 3),
-            out_specs=[ANY] * count + [SMEM],
-            scratch_shapes=[
-                pltpu.VMEM((count, GROUP_ROWS, down_store.shape[1]), jnp.bfloat16),
-                pltpu.VMEM((count, GROUP_ROWS, up_store.shape[1]), jnp.bfloat16),
-                pltpu.VMEM((down_chunks * 8, LANES), jnp.float32),
-                pltpu.VMEM((count, down_chunks + up_chunks, LANES), jnp.bfloat16),
-                pltpu.SMEM((first + count, LANES), jnp.int32),
-                pltpu.SemaphoreType.DMA((3 * count,)),
-                pltpu.SemaphoreType.DMA(()),
-            ],
-            compiler_params=WIDE,
-            name="pick_panels",
-        )(*asked[:first + count], down_store, up_store, after)
-
-    *sent, _ = pick(0, group // 2, row)
-    *more, rows = pick(group // 2, group // 2, sent[0])
-    sent += more
-    panels = [sent[0]] + [exchange(sent[s], s) for s in range(1, group)]
+    pieces = jax.ShapeDtypeStruct((group, down_chunks + up_chunks, LANES), jnp.bfloat16)
+    sent, rows = pl.pallas_call(
+        functools.partial(gather_kernel, group, down_chunks, up_chunks),
+        out_shape=(pieces, jax.ShapeDtypeStruct((group,), jnp.int32)),
+        in_specs=[SMEM] + [ANY] * (group + 2),
+        out_specs=(ANY, SMEM),
+        scratch_shapes=[
+            pltpu.VMEM((group, GROUP_ROWS, down_store.shape[1]), jnp.bfloat16),
+            pltpu.VMEM((group, GROUP_ROWS, up_store.shape[1]), jnp.bfloat16),
+            pltpu.VMEM((down_chunks * 8, LANES), jnp.float32),
+            pltpu.VMEM(pieces.shape, jnp.bfloat16),
+            pltpu.SMEM((group, LANES), jnp.int32),
+            pltpu.SemaphoreType.DMA((3 * group,)),
+            pltpu.SemaphoreType.DMA(()),
+        ],
+        compiler_params=WIDE,
+        name="pick_panels",
+    )(me[None], *asked, down_store, up_store)
+    panels = lax.all_to_all(sent, "tensor", 0, 0)
     rows_core = other_core(rows)
-    x_far, _ = lax.optimization_barrier((x_far, panels[2]))
+    x_far, _ = lax.optimization_barrier((x_far, sent))
     x_blocks = (x_mine, y_mine, x_far, other_part(x_far))
 
     owned_groups = ADAPTERS // lax.axis_size("dp") // 8
     down_shape = jax.ShapeDtypeStruct((owned_groups, down_chunks, 8, 1, LANES), jnp.float32)
     up_shape = jax.ShapeDtypeStruct((owned_groups, up_chunks, 8, 1, LANES), jnp.float32)
-    down_zero, up_zero = pl.pallas_call(
-        zero_kernel, out_shape=(down_shape, up_shape), in_specs=[ANY], out_specs=(ANY, ANY),
+    down_zero, up_zero, cleared = pl.pallas_call(
+        zero_kernel, out_shape=(down_shape, up_shape, jax.ShapeDtypeStruct((1,), jnp.int32)),
+        in_specs=[ANY], out_specs=(ANY, ANY, SMEM),
         scratch_shapes=[pltpu.VMEM((up_chunks, 8, 1, LANES), jnp.float32), pltpu.SemaphoreType.DMA((2,))],
         compiler_params=WIDE, name="clear_rows",
-    )(sent[-1])
-
-    results = pl.pallas_call(
+    )(sent)
+
+    terms, lifted = pl.pallas_call(
         functools.partial(adapter_kernel, group, down_chunks),
-        out_shape=[piece] * group + [jax.ShapeDtypeStruct((token_rows, VALUE_OUTPUTS), jnp.float32)],
-        in_specs=[SMEM] + [VMEM] * 2 + [ANY] * (group + 1),
-        out_specs=[ANY] * group + [VMEM],
-        scratch_shapes=[
-            pltpu.VMEM((2 * R, VALUE_OUTPUTS), jnp.float32),
-            pltpu.VMEM((group,) + piece.shape, jnp.bfloat16),
-            pltpu.VMEM((group,) + piece.shape, jnp.bfloat16),
-            pltpu.SemaphoreType.DMA((2, group)),
-        ],
+        out_shape=(pieces, jax.ShapeDtypeStruct((token_rows, VALUE_OUTPUTS), jnp.float32)),
+        in_specs=[VMEM] * 3 + [SMEM],
+        out_specs=(VMEM, VMEM),
+        scratch_shapes=[pltpu.VMEM((2 * R, VALUE_OUTPUTS), jnp.float32)],
         compiler_params=LIMIT,
         name="adapter",
-    )(here, xs, cotangent, *panels, down_zero)
-    terms, lifted = results[:group], results[group]
-    back = [terms[0]] + [exchange(terms[s], s) for s in range(1, group)]
-    back_core = [other_core(term) for term in back]
-
-    grad_down, grad_up = pl.pallas_call(
-        functools.partial(scatter_kernel, 2 * group, down_chunks, up_chunks),
-        out_shape=(down_shape, up_shape),
-        in_specs=[SMEM] * 3 + [ANY] * (2 * group + 2),
-        out_specs=(ANY, ANY),
-        input_output_aliases={3 + 2 * group: 0, 4 + 2 * group: 1},
-        scratch_shapes=[
-            pltpu.VMEM((2 * group,) + piece.shape, jnp.bfloat16),
-            pltpu.VMEM((2 * group, down_chunks, 1, LANES), jnp.float32),
-            pltpu.VMEM((2 * group, up_chunks, 1, LANES), jnp.float32),
-            pltpu.VMEM((up_chunks, LANES), jnp.float32),
-            pltpu.SemaphoreType.DMA((2 * group,)),
-            pltpu.SemaphoreType.DMA(()),
-        ],
-        compiler_params=WIDE,
-        name="place_rows",
-    )((core * (ADAPTERS // lax.axis_size("dp")))[None], rows, rows_core, *back, *back_core,
-      down_zero, up_zero)
-    grad_down = grad_down.reshape(owned_groups, down_chunks, 8, LANES).transpose(0, 2, 1, 3)
-    grad_up = grad_up.reshape(owned_groups, up_chunks, 8, LANES).transpose(0, 2, 1, 3)
-
-    half, _ = lax.optimization_barrier((half, panels[-1]))
+    )(xs, cotangent, panels, cleared)
+    half, _ = lax.optimization_barrier((half, panels))
     both = (half, other_core(half))
     sums = jax.ShapeDtypeStruct((2 * token_rows, parts * width), jnp.float32)
     own, other = pl.pallas_call(
@@ -430,8 +379,34 @@
         out_specs=(VMEM, VMEM),
         compiler_params=LIMIT,
         name="frozen_part",
-    )(*x_blocks, *both, terms[0])
-    columns = own + exchange(other, 1)
+    )(*x_blocks, *both, terms)
+    terms, other = lax.optimization_barrier((terms, other))
+    far = exchange(other, 1)
+    back = lax.all_to_all(terms, "tensor", 0, 0)
+    back_core = other_core(back)
+
+    grad_down, grad_up = pl.pallas_call(
+        functools.partial(scatter_kernel, 2 * group, down_chunks, up_chunks),
+        out_shape=(down_shape, up_shape),
+        in_specs=[SMEM] * 3 + [ANY] * 4,
+        out_specs=(ANY, ANY),
+        input_output_aliases={5: 0, 6: 1},
+        scratch_shapes=[
+            pltpu.VMEM((2 * group,) + pieces.shape[1:], jnp.bfloat16),
+            pltpu.VMEM((2 * group, down_chunks, 1, LANES), jnp.float32),
+            pltpu.VMEM((2 * group, up_chunks, 1, LANES), jnp.float32),
+            pltpu.VMEM((up_chunks, LANES), jnp.float32),
+            pltpu.SemaphoreType.DMA((2 * group,)),
+            pltpu.SemaphoreType.DMA(()),
+        ],
+        compiler_params=WIDE,
+        name="place_rows",
+    )((core * (ADAPTERS // lax.axis_size("dp")))[None], rows, rows_core, back, back_core,
+      down_zero, up_zero)
+    grad_down = grad_down.reshape(owned_groups, down_chunks, 8, LANES).transpose(0, 2, 1, 3)
+    grad_up = grad_up.reshape(owned_groups, up_chunks, 8, LANES).transpose(0, 2, 1, 3)
+
+    columns = own + far
     kept, gone = columns[:token_rows], columns[token_rows:]
     got = other_part(gone)
     quarters = [[c[:, :width], c[:, width:]] for c in (kept, got)]

time: 145 us -> 146 us (level)
  waiting for transfers between devices: 35.2 us -> 58.8 us
  starting transfers between devices: 38.5 us -> 29.8 us
  local copies, waits for them, and re-layouts: 12.7 us -> 5.46 us
  Pallas kernels: 39.9 us -> 33 us
    all_to_all x0 -> x2, waiting for transfers between devices: none -> 35 us  [the longest x1 18.3 us: fast_body(): back = lax.all_to_all(terms, 'tensor', 0, 0)]
    ppermute x23 -> x9, waiting for transfers between devices: 29.9 us -> 6.15 us  [exchange(): return lax.ppermute(value, 'tensor', [(t, t ^ s) for t in range(group)])]
    ppermute x23 -> x9, starting transfers between devices: 34.4 us -> 16.5 us  [exchange(): return lax.ppermute(value, 'tensor', [(t, t ^ s) for t in range(group)])]
    ppermute x3, waiting for transfers between devices: 0.01 us -> 17.6 us  [other_part(): lax.ppermute(value, 'parts', [(a, parts - 1 - a) for a in range(parts)])]
    all_to_all x0 -> x2, starting transfers between devices: none -> 7.98 us  [the longest x1 4.42 us: fast_body(): panels = lax.all_to_all(sent, 'tensor', 0, 0)]
    unnamed x76 -> x38, local copies, waits for them, and re-layouts: 11.3 us -> 4.05 us
    pallas_call x1, Pallas kernels: 6.37 us -> 3.01 us  [fast_body(): pl.pallas_call(functools.partial(adapter_kernel, group, down_chunks), out...]
    ppermute x3, starting transfers between devices: 2.37 us -> 5.24 us  [other_part(): lax.ppermute(value, 'parts', [(a, parts - 1 - a) for a in range(parts)])]
  transfers between devices with their start and end apart: 37 -> 18, of which waited for: 15 -> 9; matrix products, arithmetic and copies ran while one was open for 1% -> 3% of each run, Pallas kernels for 25% -> 17%
where the time goes in v4:
time: 146 us; the launch traced here: 145 us
  waiting for transfers between devices  58.8 us (40%)
  Pallas kernels  33 us (23%)
  starting transfers between devices  29.8 us (20%)
  between operations  14.9 us (10%)
  local copies, waits for them, and re-layouts  5.46 us (4%)
  other arithmetic  3.24 us (2%)
    all_to_all x1, waiting for transfers between devices, fast_body(): back = lax.all_to_all(terms, 'tensor', 0, 0)  18.3 us
    ppermute x3, waiting for transfers between devices, other_part(): lax.ppermute(value, 'parts', [(a, parts - 1 - a) for a in range(parts)])  17.6 us
    all_to_all x1, waiting for transfers between devices, fast_body(): panels = lax.all_to_all(sent, 'tensor', 0, 0)  16.7 us
    ppermute x9, starting transfers between devices, exchange(): return lax.ppermute(value, 'tensor', [(t, t ^ s) for t in range(group)])  16.5 us
    pallas_call x1, Pallas kernels, fast_body(): pl.pallas_call(zero_kernel, out_shape=(down_shape, up_shape, jax.ShapeDty...  8.94 us
    pallas_call x1, Pallas kernels, fast_body(): pl.pallas_call(functools.partial(gather_kernel, group, down_chunks, up_ch...  8.65 us
    ppermute x9, waiting for transfers between devices, exchange(): return lax.ppermute(value, 'tensor', [(t, t ^ s) for t in range(group)])  6.15 us
    ppermute x3, starting transfers between devices, other_part(): lax.ppermute(value, 'parts', [(a, parts - 1 - a) for a in range(parts)])  5.24 us
  transfers between devices with their start and end apart: 18, of which 9 were waited for; matrix products, arithmetic and copies ran while one was open for 3% of the time, Pallas kernels for 17%

profile of v4, /device:TPU:0, one launch (start us, length us, event | category | flops | bytes accessed | tf_op | source)
XLA Modules:
  0.0 145.2 jit_solution(17876815883060212190)
XLA Ops:
  7.2 0.0 copy-start
  7.2 0.0 all-gather.2.cloned.1.call-start
  7.2 1.0 copy-done
  8.3 0.7 constant_dynamic-slice_fusion
  9.0 0.0 all-gather.2.cloned.1.call-update
  9.7 1.3 fusion.1
  11.0 0.6 broadcast_in_dim.24.refs_0_
  11.6 0.0 copy-start.10
  11.7 6.0 %collective-permute-start.8 = (s32[128]{0:T(128)S(1)}, s32[128]{0:T(128)S(1)}, u32[]{:S(2)}, u32[]{:S(2)}) collective-permute-start(s32[128]{0:T(128)S(1)} %broadcast_in_dim.24.refs_0_), channel_id=1, source_target_pairs={{0,7},{1,6},{2,5},{3,4},{4,3},{5,2},{6,1},{7,0},{8,15},{9,14},{10,... | collective-permute-start | bytes 1544 | tf_op jit(solution)/shard_map/ppermute | solution.py:300
  17.7 0.2 collective-permute-start.7
  17.9 0.8 collective-permute-start.6
  18.7 2.0 %collective-permute-start.5 = (s32[128]{0:T(128)S(1)}, s32[128]{0:T(128)S(1)}, u32[]{:S(2)}, u32[]{:S(2)}) collective-permute-start(s32[128]{0:T(128)S(1)} %broadcast_in_dim.24.refs_0_), channel_id=1, source_target_pairs={{0,4},{1,5},{2,6},{3,7},{4,0},{5,1},{6,2},{7,3},{8,12},{9,13},{10,... | collective-permute-start | bytes 1544 | tf_op jit(solution)/shard_map/ppermute | solution.py:300
  20.7 2.3 %collective-permute-start.4 = (s32[128]{0:T(128)S(1)}, s32[128]{0:T(128)S(1)}, u32[]{:S(2)}, u32[]{:S(2)}) collective-permute-start(s32[128]{0:T(128)S(1)} %broadcast_in_dim.24.refs_0_), channel_id=1, source_target_pairs={{0,3},{1,2},{2,1},{3,0},{4,7},{5,6},{6,5},{7,4},{8,11},{9,10},{10,... | collective-permute-start | bytes 1544 | tf_op jit(solution)/shard_map/ppermute | solution.py:300
  23.0 0.0 collective-permute-done.8.refs_7_
  23.0 0.8 collective-permute-start.3
  23.8 0.0 collective-permute-done.7.refs_6_
  23.8 0.4 collective-permute-start.2
  24.2 0.0 collective-permute-done.6.refs_5_
  24.2 0.0 collective-permute-done.5.refs_4_
  24.2 0.0 copy-start.14
  24.2 0.9 collective-permute-done.4.refs_3_
  25.2 1.4 collective-permute-done.3.refs_2_
  26.6 0.8 collective-permute-done.2.refs_1_
  27.3 0.0 copy-done.10
  27.3 0.0 copy-done.11
  27.3 0.0 copy-done.12
  27.3 0.0 copy-done.13
  27.4 0.0 copy-done.14
  27.4 0.0 copy-done.15
  27.4 0.0 copy-done.17
  27.4 0.5 copy-done.18
  27.9 8.6 %pick_panels.1 = (bf16[8,384,128]{2,1,0:T(8,128)(2,1)}, s32[8]{0:T(128)}) custom-call(s32[1]{0:T(128)} %bitcast.1.where, s32[128]{0:T(128)} %copy-done.10, s32[128]{0:T(128)} %copy-done.18, s32[128]{0:T(128)} %copy-done.17, s32[128]{0:T(128)} %copy-done.15, s32[128]{0:T(128)} %copy-done.14, s32[128]{0:T(128)} %copy-done.13, s32[128]{0:T(128)} %copy-done.12, ...), custom_call_target="tpu_custom_call" | custom-call | tf_op jit(solution)/shard_map/pick_panels/pallas_call | solution.py:331
  36.6 0.0 copy-start.7
  36.6 4.4 %all-to-all-start = ((bf16[8,384,128]{2,1,0:T(8,128)(2,1)}), bf16[8,384,128]{2,1,0:T(8,128)(2,1)S(1)}, u32[]{:S(2)}, u32[]{:S(2)}) async-start(bf16[8,384,128]{2,1,0:T(8,128)(2,1)} %get-tuple-element.22.after_ref), calls=%async_computation | async-start | bytes 1572864 | tf_op jit(solution)/shard_map/all_to_all | solution.py:348
  41.0 2.5 %split_tokens.1 = (bf16[4,128,640]{2,1,0:T(8,128)(2,1)}, bf16[4,128,640]{2,1,0:T(8,128)(2,1)}) custom-call(s32[1]{0:T(128)} %bitcast.where, bf16[128,5120]{1,0:T(8,128)(2,1)} %x_ref.3), custom_call_target="tpu_custom_call" | custom-call | tf_op jit(solution)/shard_map/split_tokens/pallas_call | solution.py:317
  43.5 2.0 %collective-permute-start.1 = (bf16[4,128,640]{2,1,0:T(8,128)(2,1)}, bf16[4,128,640]{2,1,0:T(8,128)(2,1)}, u32[]{:S(2)}, u32[]{:S(2)}) collective-permute-start(bf16[4,128,640]{2,1,0:T(8,128)(2,1)} %get-tuple-element.21), channel_id=1, source_target_pairs={{0,1},{1,0},{2,3},{3,2},{4,5},{5,4},{6,7},{7,6},{8,9},{9,8},{10,11... | collective-permute-start | bytes 1966088 | tf_op jit(solution)/shard_map/ppermute | solution.py:300
  45.5 16.7 %all-to-all-done.pieces = bf16[8,384,128]{2,1,0:T(8,128)(2,1)S(1)} async-done(((bf16[8,384,128]{2,1,0:T(8,128)(2,1)}), bf16[8,384,128]{2,1,0:T(8,128)(2,1)S(1)}, u32[]{:S(2)}, u32[]{:S(2)}) %all-to-all-start) | async-done | bytes 786464 | tf_op jit(solution)/shard_map/all_to_all | solution.py:348
  62.2 0.0 collective-permute-start.10
  62.2 1.5 %collective-permute-start = (bf16[4,128,640]{2,1,0:T(8,128)(2,1)}, bf16[4,128,640]{2,1,0:T(8,128)(2,1)}, u32[]{:S(2)}, u32[]{:S(2)}) collective-permute-start(bf16[4,128,640]{2,1,0:T(8,128)(2,1)} %get-tuple-element.20.refs_0_), channel_id=1, source_target_pairs={{0,16},{16,0},{1,17},{17,1},{2,18},{18,2},{3,19},{19,3},{4,20},{20... | collective-permute-start | bytes 1966088 | tf_op jit(solution)/shard_map/ppermute | solution.py:306
  63.6 1.2 collective-permute-done.1.refs_2_
  64.8 2.2 %collective-permute-start.9 = (bf16[4,128,640]{2,1,0:T(8,128)(2,1)}, bf16[4,128,640]{2,1,0:T(8,128)(2,1)}, u32[]{:S(2)}, u32[]{:S(2)}) collective-permute-start(bf16[4,128,640]{2,1,0:T(8,128)(2,1)} %collective-permute-done.1.refs_2_), channel_id=1, source_target_pairs={{0,16},{16,0},{1,17},{17,1},{2,18},{18,2},{3,19},{19,3},{4,20},{20... | collective-permute-start | bytes 1966088 | tf_op jit(solution)/shard_map/ppermute | solution.py:306
  67.0 1.8 %pair_columns.1.xs_ref = bf16[8,256,320]{2,1,0:T(8,128)(2,1)S(1)} custom-call(bf16[128,5120]{1,0:T(8,128)(2,1)S(1)} %copy-done.2), custom_call_target="tpu_custom_call" | custom-call | tf_op jit(solution)/shard_map/pair_columns/pallas_call | solution.py:324
  68.8 8.9 %clear_rows.1 = (f32[16,320,8,1,128]{4,3,2,1,0:T(1,128)}, f32[16,64,8,1,128]{4,3,2,1,0:T(1,128)}, s32[1]{0:T(128)}) custom-call(bf16[8,384,128]{2,1,0:T(8,128)(2,1)} %get-tuple-element.22.after_ref), custom_call_target="tpu_custom_call" | custom-call | tf_op jit(solution)/shard_map/clear_rows/pallas_call | solution.py:356
  77.8 3.0 %adapter.1 = (bf16[8,384,128]{2,1,0:T(8,128)(2,1)}, f32[128,1024]{1,0:T(8,128)S(1)}) custom-call(bf16[8,256,320]{2,1,0:T(8,128)(2,1)S(1)} %pair_columns.1.xs_ref, bf16[128,1024]{1,0:T(8,128)(2,1)S(1)} %copy-done.7, bf16[8,384,128]{2,1,0:T(8,128)(2,1)S(1)} %all-to-all-done.pieces, s32[1]{0:T(128)} %get-tuple-element.25._), custom_call_target="tpu_custom_call" | custom-call | tf_op jit(solution)/shard_map/adapter/pallas_call | solution.py:363
  80.8 0.8 copy-done.5
  81.6 0.0 collective-permute-done.refs_1_
  81.6 12.1 %collective-permute-done.9.refs_3_ = bf16[4,128,640]{2,1,0:T(8,128)(2,1)} collective-permute-done((bf16[4,128,640]{2,1,0:T(8,128)(2,1)}, bf16[4,128,640]{2,1,0:T(8,128)(2,1)}, u32[]{:S(2)}, u32[]{:S(2)}) %collective-permute-start.9) | collective-permute-done | bytes 655392 | tf_op jit(solution)/shard_map/ppermute | solution.py:306
  93.7 0.0 collective-permute-done.10.refs_5_
  93.7 1.1 copy-done.4
  94.8 3.7 %frozen_part.1 = (f32[256,512]{1,0:T(8,128)S(1)}, f32[256,512]{1,0:T(8,128)S(1)}) custom-call(bf16[4,128,640]{2,1,0:T(8,128)(2,1)S(1)} %copy-done.4, bf16[4,128,640]{2,1,0:T(8,128)(2,1)} %collective-permute-done.refs_1_, bf16[4,128,640]{2,1,0:T(8,128)(2,1)} %collective-permute-done.1.refs_2_, bf16[4,128,640]{2,1,0:T(8,128)(2,1)} %collective-permute-done.9.refs_3_, ...), custom_call_target="tpu_custom_call" | custom-call | tf_op jit(solution)/shard_map/frozen_part/pallas_call | solution.py:375
  98.5 3.6 %all-to-all-start.1 = ((bf16[8,384,128]{2,1,0:T(8,128)(2,1)}), bf16[8,384,128]{2,1,0:T(8,128)(2,1)S(1)}, u32[]{:S(2)}, u32[]{:S(2)}) async-start(bf16[8,384,128]{2,1,0:T(8,128)(2,1)} %get-tuple-element.32.refs_6_), calls=%async_computation.1 | async-start | bytes 1572864 | tf_op jit(solution)/shard_map/all_to_all | solution.py:385
  102.1 1.9 %collective-permute-start.11 = (f32[256,512]{1,0:T(8,128)S(1)}, f32[256,512]{1,0:T(8,128)}, u32[]{:S(2)}, u32[]{:S(2)}) collective-permute-start(f32[256,512]{1,0:T(8,128)S(1)} %get-tuple-element.29), channel_id=1, source_target_pairs={{0,1},{1,0},{2,3},{3,2},{4,5},{5,4},{6,7},{7,6},{8,9},{9,8},{10,11... | collective-permute-start | bytes 1572872 | tf_op jit(solution)/shard_map/ppermute | solution.py:300
  104.0 18.3 %all-to-all-done.1.rest_0_ = bf16[8,384,128]{2,1,0:T(8,128)(2,1)S(1)} async-done(((bf16[8,384,128]{2,1,0:T(8,128)(2,1)}), bf16[8,384,128]{2,1,0:T(8,128)(2,1)S(1)}, u32[]{:S(2)}, u32[]{:S(2)}) %all-to-all-start.1) | async-done | bytes 786464 | tf_op jit(solution)/shard_map/all_to_all | solution.py:385
  122.4 0.0 collective-permute-start.14
  122.4 1.9 %collective-permute-done.11 = f32[256,512]{1,0:T(8,128)} collective-permute-done((f32[256,512]{1,0:T(8,128)S(1)}, f32[256,512]{1,0:T(8,128)}, u32[]{:S(2)}, u32[]{:S(2)}) %collective-permute-start.11) | collective-permute-done | bytes 524320 | tf_op jit(solution)/shard_map/ppermute | solution.py:300
  124.3 1.1 add.15
  125.4 1.5 %collective-permute-start.12 = (f32[128,512]{1,0:T(8,128)S(1)}, f32[128,512]{1,0:T(8,128)S(1)}, u32[]{:S(2)}, u32[]{:S(2)}) collective-permute-start(f32[128,512]{1,0:T(8,128)S(1)} %slice.25), channel_id=1, source_target_pairs={{0,16},{16,0},{1,17},{17,1},{2,18},{18,2},{3,19},{19,3},{4,20},{20... | collective-permute-start | bytes 786440 | tf_op jit(solution)/shard_map/ppermute | solution.py:306
  127.0 0.0 collective-permute-start.13
  127.0 5.5 %collective-permute-done.12 = f32[128,512]{1,0:T(8,128)S(1)} collective-permute-done((f32[128,512]{1,0:T(8,128)S(1)}, f32[128,512]{1,0:T(8,128)S(1)}, u32[]{:S(2)}, u32[]{:S(2)}) %collective-permute-start.12) | collective-permute-done | bytes 262176 | tf_op jit(solution)/shard_map/ppermute | solution.py:306
  132.6 0.8 fusion
  133.3 0.0 collective-permute-done.13.rows_core
  133.3 0.0 collective-permute-done.14.rest_1_
  133.4 0.5 copy-done.16
  133.9 4.4 %place_rows.1 = (f32[16,320,8,1,128]{4,3,2,1,0:T(1,128)}, f32[16,64,8,1,128]{4,3,2,1,0:T(1,128)}) custom-call(s32[1]{0:T(128)} %bitcast.3.first_row, s32[8]{0:T(128)} %get-tuple-element.31.rows_here, s32[8]{0:T(128)} %copy-done.16, bf16[8,384,128]{2,1,0:T(8,128)(2,1)} %copy-done.8, ...), custom_call_target="tpu_custom_call", output_to_operand_aliasing={{0}: (5, {}), {1}: (6, {})} | custom-call | tf_op jit(solution)/shard_map/place_rows/pallas_call | solution.py:388
  (25 shorter events, 0.1 us)
Async XLA Ops:
  7.2 1.1 copy-start
  7.2 55.0 %all-gather.2.cloned.1.call-start = ((), (), s32[]{:S(2)}) async-start(), calls=%async_computation.2 | async-start | bytes 1638400 | tf_op jit(solution)/shard_map/all_gather | solution.py:314
  11.6 15.7 %copy-start.10 = (s32[128]{0:T(128)}, s32[128]{0:T(128)S(1)}, u32[]{:S(2)}) copy-start(s32[128]{0:T(128)S(1)} %broadcast_in_dim.24.refs_0_) | copy-start | bytes 1540
  11.7 11.3 %collective-permute-start.8 = (s32[128]{0:T(128)S(1)}, s32[128]{0:T(128)S(1)}, u32[]{:S(2)}, u32[]{:S(2)}) collective-permute-start(s32[128]{0:T(128)S(1)} %broadcast_in_dim.24.refs_0_), channel_id=1, source_target_pairs={{0,7},{1,6},{2,5},{3,4},{4,3},{5,2},{6,1},{7,0},{8,15},{9,14},{10,... | collective-permute-start | bytes 1544 | tf_op jit(solution)/shard_map/ppermute | solution.py:300
  17.7 6.1 %collective-permute-start.7 = (s32[128]{0:T(128)S(1)}, s32[128]{0:T(128)S(1)}, u32[]{:S(2)}, u32[]{:S(2)}) collective-permute-start(s32[128]{0:T(128)S(1)} %broadcast_in_dim.24.refs_0_), channel_id=1, source_target_pairs={{0,6},{1,7},{2,4},{3,5},{4,2},{5,3},{6,0},{7,1},{8,14},{9,15},{10,... | collective-permute-start | bytes 1544 | tf_op jit(solution)/shard_map/ppermute | solution.py:300
  17.9 6.3 %collective-permute-start.6 = (s32[128]{0:T(128)S(1)}, s32[128]{0:T(128)S(1)}, u32[]{:S(2)}, u32[]{:S(2)}) collective-permute-start(s32[128]{0:T(128)S(1)} %broadcast_in_dim.24.refs_0_), channel_id=1, source_target_pairs={{0,5},{1,4},{2,7},{3,6},{4,1},{5,0},{6,3},{7,2},{8,13},{9,12},{10,... | collective-permute-start | bytes 1544 | tf_op jit(solution)/shard_map/ppermute | solution.py:300
  18.7 5.5 %collective-permute-start.5 = (s32[128]{0:T(128)S(1)}, s32[128]{0:T(128)S(1)}, u32[]{:S(2)}, u32[]{:S(2)}) collective-permute-start(s32[128]{0:T(128)S(1)} %broadcast_in_dim.24.refs_0_), channel_id=1, source_target_pairs={{0,4},{1,5},{2,6},{3,7},{4,0},{5,1},{6,2},{7,3},{8,12},{9,13},{10,... | collective-permute-start | bytes 1544 | tf_op jit(solution)/shard_map/ppermute | solution.py:300
  20.7 4.4 %collective-permute-start.4 = (s32[128]{0:T(128)S(1)}, s32[128]{0:T(128)S(1)}, u32[]{:S(2)}, u32[]{:S(2)}) collective-permute-start(s32[128]{0:T(128)S(1)} %broadcast_in_dim.24.refs_0_), channel_id=1, source_target_pairs={{0,3},{1,2},{2,1},{3,0},{4,7},{5,6},{6,5},{7,4},{8,11},{9,10},{10,... | collective-permute-start | bytes 1544 | tf_op jit(solution)/shard_map/ppermute | solution.py:300
  23.0 4.3 %copy-start.11 = (s32[128]{0:T(128)}, s32[128]{0:T(128)S(1)}, u32[]{:S(2)}) copy-start(s32[128]{0:T(128)S(1)} %collective-permute-done.8.refs_7_) | copy-start | bytes 1540
  23.0 3.6 %collective-permute-start.3 = (s32[128]{0:T(128)S(1)}, s32[128]{0:T(128)S(1)}, u32[]{:S(2)}, u32[]{:S(2)}) collective-permute-start(s32[128]{0:T(128)S(1)} %broadcast_in_dim.24.refs_0_), channel_id=1, source_target_pairs={{0,2},{1,3},{2,0},{3,1},{4,6},{5,7},{6,4},{7,5},{8,10},{9,11},{10,... | collective-permute-start | bytes 1544 | tf_op jit(solution)/shard_map/ppermute | solution.py:300
  23.8 3.6 %copy-start.12 = (s32[128]{0:T(128)}, s32[128]{0:T(128)S(1)}, u32[]{:S(2)}) copy-start(s32[128]{0:T(128)S(1)} %collective-permute-done.7.refs_6_) | copy-start | bytes 1540
  23.8 3.5 %collective-permute-start.2 = (s32[128]{0:T(128)S(1)}, s32[128]{0:T(128)S(1)}, u32[]{:S(2)}, u32[]{:S(2)}) collective-permute-start(s32[128]{0:T(128)S(1)} %broadcast_in_dim.24.refs_0_), channel_id=1, source_target_pairs={{0,1},{1,0},{2,3},{3,2},{4,5},{5,4},{6,7},{7,6},{8,9},{9,8},{10,11... | collective-permute-start | bytes 1544 | tf_op jit(solution)/shard_map/ppermute | solution.py:300
  24.2 3.1 %copy-start.13 = (s32[128]{0:T(128)}, s32[128]{0:T(128)S(1)}, u32[]{:S(2)}) copy-start(s32[128]{0:T(128)S(1)} %collective-permute-done.6.refs_5_) | copy-start | bytes 1540
  24.2 3.1 %copy-start.14 = (s32[128]{0:T(128)}, s32[128]{0:T(128)S(1)}, u32[]{:S(2)}) copy-start(s32[128]{0:T(128)S(1)} %collective-permute-done.5.refs_4_) | copy-start | bytes 1540
  25.2 2.2 %copy-start.15 = (s32[128]{0:T(128)}, s32[128]{0:T(128)S(1)}, u32[]{:S(2)}) copy-start(s32[128]{0:T(128)S(1)} %collective-permute-done.4.refs_3_) | copy-start | bytes 1540
  26.6 0.8 copy-start.17
  27.3 0.6 copy-start.18
  27.9 39.1 %copy-start.2 = (bf16[128,5120]{1,0:T(8,128)(2,1)S(1)}, bf16[128,5120]{1,0:T(8,128)(2,1)}, u32[]{:S(2)}) copy-start(bf16[128,5120]{1,0:T(8,128)(2,1)} %x_ref.3) | copy-start | bytes 3932164
  36.6 41.2 %copy-start.7 = (bf16[128,1024]{1,0:T(8,128)(2,1)S(1)}, bf16[128,1024]{1,0:T(8,128)(2,1)}, u32[]{:S(2)}) copy-start(bf16[128,1024]{1,0:T(8,128)(2,1)} %g_ref.1) | copy-start | bytes 786436
  36.6 25.6 %all-to-all-start = ((bf16[8,384,128]{2,1,0:T(8,128)(2,1)}), bf16[8,384,128]{2,1,0:T(8,128)(2,1)S(1)}, u32[]{:S(2)}, u32[]{:S(2)}) async-start(bf16[8,384,128]{2,1,0:T(8,128)(2,1)} %get-tuple-element.22.after_ref), calls=%async_computation | async-start | bytes 1572864 | tf_op jit(solution)/shard_map/all_to_all | solution.py:348
  43.5 21.3 %collective-permute-start.1 = (bf16[4,128,640]{2,1,0:T(8,128)(2,1)}, bf16[4,128,640]{2,1,0:T(8,128)(2,1)}, u32[]{:S(2)}, u32[]{:S(2)}) collective-permute-start(bf16[4,128,640]{2,1,0:T(8,128)(2,1)} %get-tuple-element.21), channel_id=1, source_target_pairs={{0,1},{1,0},{2,3},{3,2},{4,5},{5,4},{6,7},{7,6},{8,9},{9,8},{10,11... | collective-permute-start | bytes 1966088 | tf_op jit(solution)/shard_map/ppermute | solution.py:300
  62.2 31.5 %collective-permute-start.10 = (bf16[2560,256]{1,0:T(8,128)(2,1)}, bf16[2560,256]{1,0:T(8,128)(2,1)}, u32[]{:S(2)}, u32[]{:S(2)}) collective-permute-start(bf16[2560,256]{1,0:T(8,128)(2,1)} %all-gather.2.cloned.1.call-done.refs_4_), channel_id=1, source_target_pairs={{0,8},{8,0},{1,9},{9,1},{2,10},{10,2},{3,11},{11,3},{4,12},{12,4},... | collective-permute-start | bytes 3932168 | tf_op jit(solution)/shard_map/ppermute | solution.py:303
  62.2 19.4 %collective-permute-start = (bf16[4,128,640]{2,1,0:T(8,128)(2,1)}, bf16[4,128,640]{2,1,0:T(8,128)(2,1)}, u32[]{:S(2)}, u32[]{:S(2)}) collective-permute-start(bf16[4,128,640]{2,1,0:T(8,128)(2,1)} %get-tuple-element.20.refs_0_), channel_id=1, source_target_pairs={{0,16},{16,0},{1,17},{17,1},{2,18},{18,2},{3,19},{19,3},{4,20},{20... | collective-permute-start | bytes 1966088 | tf_op jit(solution)/shard_map/ppermute | solution.py:306
  64.8 28.9 %collective-permute-start.9 = (bf16[4,128,640]{2,1,0:T(8,128)(2,1)}, bf16[4,128,640]{2,1,0:T(8,128)(2,1)}, u32[]{:S(2)}, u32[]{:S(2)}) collective-permute-start(bf16[4,128,640]{2,1,0:T(8,128)(2,1)} %collective-permute-done.1.refs_2_), channel_id=1, source_target_pairs={{0,16},{16,0},{1,17},{17,1},{2,18},{18,2},{3,19},{19,3},{4,20},{20... | collective-permute-start | bytes 1966088 | tf_op jit(solution)/shard_map/ppermute | solution.py:306
  68.8 24.9 %copy-start.3 = (bf16[2560,256]{1,0:T(8,128)(2,1)S(1)}, bf16[2560,256]{1,0:T(8,128)(2,1)}, u32[]{:S(2)}) copy-start(bf16[2560,256]{1,0:T(8,128)(2,1)} %all-gather.2.cloned.1.call-done.refs_4_) | copy-start | bytes 3932164
  80.8 0.8 copy-start.5
  93.7 1.1 copy-start.4
  94.8 32.2 %copy-start.9 = (s32[8]{0:T(128)S(1)}, s32[8]{0:T(128)}, u32[]{:S(2)}) copy-start(s32[8]{0:T(128)} %get-tuple-element.31.rows_here) | copy-start | bytes 100
  94.8 37.8 %copy-start.6 = (f32[128,1024]{1,0:T(8,128)S(1)}, f32[128,1024]{1,0:T(8,128)}, u32[]{:S(2)}) copy-start(f32[128,1024]{1,0:T(8,128)} %copy-done.5) | copy-start | bytes 1572868
  98.5 23.9 %all-to-all-start.1 = ((bf16[8,384,128]{2,1,0:T(8,128)(2,1)}), bf16[8,384,128]{2,1,0:T(8,128)(2,1)S(1)}, u32[]{:S(2)}, u32[]{:S(2)}) async-start(bf16[8,384,128]{2,1,0:T(8,128)(2,1)} %get-tuple-element.32.refs_6_), calls=%async_computation.1 | async-start | bytes 1572864 | tf_op jit(solution)/shard_map/all_to_all | solution.py:385
  102.1 22.2 %collective-permute-start.11 = (f32[256,512]{1,0:T(8,128)S(1)}, f32[256,512]{1,0:T(8,128)}, u32[]{:S(2)}, u32[]{:S(2)}) collective-permute-start(f32[256,512]{1,0:T(8,128)S(1)} %get-tuple-element.29), channel_id=1, source_target_pairs={{0,1},{1,0},{2,3},{3,2},{4,5},{5,4},{6,7},{7,6},{8,9},{9,8},{10,11... | collective-permute-start | bytes 1572872 | tf_op jit(solution)/shard_map/ppermute | solution.py:300
  122.4 11.0 %copy-start.8 = (bf16[8,384,128]{2,1,0:T(8,128)(2,1)}, bf16[8,384,128]{2,1,0:T(8,128)(2,1)S(1)}, u32[]{:S(2)}) copy-start(bf16[8,384,128]{2,1,0:T(8,128)(2,1)S(1)} %all-to-all-done.1.rest_0_) | copy-start | bytes 2359300
  122.4 11.0 %collective-permute-start.14 = (bf16[8,384,128]{2,1,0:T(8,128)(2,1)S(1)}, bf16[8,384,128]{2,1,0:T(8,128)(2,1)}, u32[]{:S(2)}, u32[]{:S(2)}) collective-permute-start(bf16[8,384,128]{2,1,0:T(8,128)(2,1)S(1)} %all-to-all-done.1.rest_0_), channel_id=1, source_target_pairs={{0,8},{8,0},{1,9},{9,1},{2,10},{10,2},{3,11},{11,3},{4,12},{12,4},... | collective-permute-start | bytes 2359304 | tf_op jit(solution)/shard_map/ppermute | solution.py:303
  125.4 7.1 %collective-permute-start.12 = (f32[128,512]{1,0:T(8,128)S(1)}, f32[128,512]{1,0:T(8,128)S(1)}, u32[]{:S(2)}, u32[]{:S(2)}) collective-permute-start(f32[128,512]{1,0:T(8,128)S(1)} %slice.25), channel_id=1, source_target_pairs={{0,16},{16,0},{1,17},{17,1},{2,18},{18,2},{3,19},{19,3},{4,20},{20... | collective-permute-start | bytes 786440 | tf_op jit(solution)/shard_map/ppermute | solution.py:306
  127.0 6.4 %collective-permute-start.13 = (s32[8]{0:T(128)S(1)}, s32[8]{0:T(128)S(1)}, u32[]{:S(2)}, u32[]{:S(2)}) collective-permute-start(s32[8]{0:T(128)S(1)} %copy-done.9), channel_id=1, source_target_pairs={{0,8},{8,0},{1,9},{9,1},{2,10},{10,2},{3,11},{11,3},{4,12},{12,4},... | collective-permute-start | bytes 104 | tf_op jit(solution)/shard_map/ppermute | solution.py:303
  133.3 0.5 copy-start.16
  133.9 4.5 %copy-start.1 = (bf16[640,512]{1,0:T(8,128)(2,1)S(1)}, bf16[640,512]{1,0:T(8,128)(2,1)}, u32[]{:S(2)}) copy-start(bf16[640,512]{1,0:T(8,128)(2,1)} %param.9) | copy-start | bytes 1966084
Sparse Core Ops, SparseCore 0:
  10.2 36.4 all-gather.1

commit v5 on v4

--- a/solution.py
+++ b/solution.py
@@ -95,7 +95,8 @@
     return mixed, grad_down, grad_up
 
 
-def split_kernel(where, x_ref, mine_ref, theirs_ref):
+def split_kernel(where, x_ref, mine_ref, theirs_ref, done_ref):
+    done_ref[0] = 0
     inner = where[0]
     outer, rows, width = mine_ref.shape
     for k in range(outer):
@@ -118,52 +119,55 @@
         xs_ref[k, rows:] = dot(x, odd).astype(jnp.bfloat16)
 
 
-def gather_kernel(count, down_chunks, up_chunks, where, *refs):
+def gather_kernel(count, down_chunks, up_chunks, where, after, *refs):
+    del after
     asked, (down_ref, up_ref, out_ref, rows_ref) = refs[:count], refs[count:count + 4]
     down_buf, up_buf, flat, built, rows, sems, row_sem = refs[count + 4:]
     me = where[0]
+    across = up_chunks // 8
     for s in range(count):
         pltpu.make_async_copy(asked[s], rows.at[s], row_sem).start()
     for s in range(count):
         pltpu.make_async_copy(asked[s], rows.at[s], row_sem).wait()
-    copies = []
+
+    def copies(s):
+        start = pl.multiple_of((rows[s, 0] // GROUP_ROWS) * GROUP_ROWS, GROUP_ROWS)
+        return (
+            pltpu.make_async_copy(down_ref.at[pl.ds(start, GROUP_ROWS)], down_buf.at[s], sems.at[0, s]),
+            pltpu.make_async_copy(up_ref.at[pl.ds(start, GROUP_ROWS)], up_buf.at[s], sems.at[1, s]),
+            pltpu.make_async_copy(built.at[s], out_ref.at[me ^ s], sems.at[2, s]),
+        )
+
     for s in range(count):
-        start = pl.multiple_of((rows[s, 0] // GROUP_ROWS) * GROUP_ROWS, GROUP_ROWS)
-        a = pltpu.make_async_copy(down_ref.at[pl.ds(start, GROUP_ROWS)], down_buf.at[s], sems.at[3 * s])
-        b = pltpu.make_async_copy(up_ref.at[pl.ds(start, GROUP_ROWS)], up_buf.at[s], sems.at[3 * s + 1])
-        a.start()
-        b.start()
-        copies.append((a, b, pltpu.make_async_copy(built.at[s], out_ref.at[me ^ s], sems.at[3 * s + 2])))
-    for s in range(count):
+        down, up, _ = copies(s)
+        down.start()
+        up.start()
         rows_ref[me ^ s] = rows[s, 0]
-    step = 16
-    for s in range(count):
+
+    def one(s, carry):
         row = rows[s, 0] % GROUP_ROWS
         upper = row >= 8
         sub = row % 8
 
         def pick(buf, lane):
-            tile = buf[s, :, pl.ds(pl.multiple_of(lane, LANES), LANES)].astype(jnp.float32)
+            tile = buf[s, :, lane:lane + LANES].astype(jnp.float32)
             return jnp.where(upper, tile[8:], tile[:8])
 
-        def some(i, carry):
-            for u in range(step):
-                j = i * step + u
-                flat[pl.ds(pl.multiple_of(j * 8, 8), 8), :] = pick(down_buf, j * LANES)
-            return carry
-
-        copies[s][0].wait()
-        lax.fori_loop(0, down_chunks // step, some, 0)
-        built[s, :down_chunks] = flat[pl.ds(sub, down_chunks, stride=8), :].astype(jnp.bfloat16)
-        across = up_chunks // 8
-        copies[s][1].wait()
+        down, up, leave = copies(s)
+        up.wait()
         for j in range(up_chunks):
-            place = (j % across) * 8 + j // across
+            place = down_chunks + (j % across) * 8 + j // across
             flat[place * 8:place * 8 + 8, :] = pick(up_buf, j * LANES)
-        built[s, down_chunks:] = flat[pl.ds(sub, up_chunks, stride=8), :].astype(jnp.bfloat16)
-        copies[s][2].start()
+        down.wait()
+        for j in range(down_chunks):
+            flat[j * 8:j * 8 + 8, :] = pick(down_buf, j * LANES)
+        built[s] = flat[pl.ds(sub, down_chunks + up_chunks, stride=8), :].astype(jnp.bfloat16)
+        leave.start()
+        return carry
+
+    lax.fori_loop(0, count, one, 0)
     for s in range(count):
-        copies[s][2].wait()
+        copies(s)[2].wait()
 
 
 def zero_kernel(after_ref, down_ref, up_ref, done_ref, zeros, sems):
@@ -274,16 +278,16 @@
 
 
 def base_kernel(*refs):
-    x_refs, w_refs, own_ref, other_ref = refs[:4], refs[4:6], refs[-2], refs[-1]
-    outer, _, depth = x_refs[0].shape
-    rows, width = own_ref.shape[0], w_refs[0].shape[1]
+    x_refs, w_refs, out_refs = refs[:4], refs[4:6], refs[-4:]
+    outer, rows, depth = x_refs[0].shape
+    width = w_refs[0].shape[1]
     for h, w_ref in enumerate(w_refs):
         total = 0.0
         for k in range(outer):
             left = jnp.concatenate([ref[k] for ref in x_refs], axis=0)
             total += dot(left, w_ref[k * depth:(k + 1) * depth, :])
-        own_ref[:, h * width:(h + 1) * width] = total[:rows]
-        other_ref[:, h * width:(h + 1) * width] = total[rows:]
+        for b, ref in enumerate(out_refs):
+            ref[:, h * width:(h + 1) * width] = total[b * rows:(b + 1) * rows]
 
 
 def fast_body(tokens, cotangent, frozen_value, down_store, up_store, block_adapter, adapter_slot):
@@ -314,9 +318,10 @@
     half = lax.all_gather(half, "tensor", axis_index_groups=lines, axis=0, tiled=True)
 
     block = jax.ShapeDtypeStruct((outer, token_rows, slice_width), jnp.bfloat16)
-    x_mine, x_theirs = pl.pallas_call(
-        split_kernel, out_shape=(block, block), in_specs=[SMEM, VMEM], out_specs=(VMEM, VMEM),
-        name="split_tokens",
+    token = jax.ShapeDtypeStruct((1,), jnp.int32)
+    x_mine, x_theirs, split = pl.pallas_call(
+        split_kernel, out_shape=(block, block, token), in_specs=[SMEM, VMEM], out_specs=(VMEM, VMEM, SMEM),
+        name="split_tokens", compiler_params=LIMIT,
     )(x[None], tokens)
     x_far = exchange(x_theirs, 1)
     y_mine = other_part(x_mine)
@@ -331,20 +336,20 @@
     sent, rows = pl.pallas_call(
         functools.partial(gather_kernel, group, down_chunks, up_chunks),
         out_shape=(pieces, jax.ShapeDtypeStruct((group,), jnp.int32)),
-        in_specs=[SMEM] + [ANY] * (group + 2),
+        in_specs=[SMEM, SMEM] + [ANY] * (group + 2),
         out_specs=(ANY, SMEM),
         scratch_shapes=[
             pltpu.VMEM((group, GROUP_ROWS, down_store.shape[1]), jnp.bfloat16),
             pltpu.VMEM((group, GROUP_ROWS, up_store.shape[1]), jnp.bfloat16),
-            pltpu.VMEM((down_chunks * 8, LANES), jnp.float32),
+            pltpu.VMEM(((down_chunks + up_chunks) * 8, LANES), jnp.float32),
             pltpu.VMEM(pieces.shape, jnp.bfloat16),
             pltpu.SMEM((group, LANES), jnp.int32),
-            pltpu.SemaphoreType.DMA((3 * group,)),
+            pltpu.SemaphoreType.DMA((3, group)),
             pltpu.SemaphoreType.DMA(()),
         ],
         compiler_params=WIDE,
         name="pick_panels",
-    )(me[None], *asked, down_store, up_store)
+    )(me[None], split, *asked, down_store, up_store)
     panels = lax.all_to_all(sent, "tensor", 0, 0)
     rows_core = other_core(rows)
     x_far, _ = lax.optimization_barrier((x_far, sent))
@@ -354,7 +359,7 @@
     down_shape = jax.ShapeDtypeStruct((owned_groups, down_chunks, 8, 1, LANES), jnp.float32)
     up_shape = jax.ShapeDtypeStruct((owned_groups, up_chunks, 8, 1, LANES), jnp.float32)
     down_zero, up_zero, cleared = pl.pallas_call(
-        zero_kernel, out_shape=(down_shape, up_shape, jax.ShapeDtypeStruct((1,), jnp.int32)),
+        zero_kernel, out_shape=(down_shape, up_shape, token),
         in_specs=[ANY], out_specs=(ANY, ANY, SMEM),
         scratch_shapes=[pltpu.VMEM((up_chunks, 8, 1, LANES), jnp.float32), pltpu.SemaphoreType.DMA((2,))],
         compiler_params=WIDE, name="clear_rows",
@@ -369,19 +374,20 @@
         compiler_params=LIMIT,
         name="adapter",
     )(xs, cotangent, panels, cleared)
-    half, _ = lax.optimization_barrier((half, panels))
+    half, _ = lax.optimization_barrier((half, cleared))
     both = (half, other_core(half))
-    sums = jax.ShapeDtypeStruct((2 * token_rows, parts * width), jnp.float32)
-    own, other = pl.pallas_call(
+    sums = jax.ShapeDtypeStruct((token_rows, parts * width), jnp.float32)
+    own, to_part, to_inner, to_both = pl.pallas_call(
         base_kernel,
-        out_shape=(sums, sums),
+        out_shape=[sums] * 4,
         in_specs=[VMEM] * 6 + [ANY],
-        out_specs=(VMEM, VMEM),
+        out_specs=[VMEM] * 4,
         compiler_params=LIMIT,
         name="frozen_part",
     )(*x_blocks, *both, terms)
-    terms, other = lax.optimization_barrier((terms, other))
-    far = exchange(other, 1)
+    opposite = [(a * group + t, (parts - 1 - a) * group + (t ^ 1)) for a in range(parts) for t in range(group)]
+    kept = own + exchange(to_inner, 1)
+    got = other_part(to_part) + lax.ppermute(to_both, ("parts", "tensor"), opposite)
     back = lax.all_to_all(terms, "tensor", 0, 0)
     back_core = other_core(back)
 
@@ -399,16 +405,13 @@
             pltpu.SemaphoreType.DMA((2 * group,)),
             pltpu.SemaphoreType.DMA(()),
         ],
-        compiler_params=WIDE,
+        compiler_params=LIMIT,
         name="place_rows",
     )((core * (ADAPTERS // lax.axis_size("dp")))[None], rows, rows_core, back, back_core,
       down_zero, up_zero)
     grad_down = grad_down.reshape(owned_groups, down_chunks, 8, LANES).transpose(0, 2, 1, 3)
     grad_up = grad_up.reshape(owned_groups, up_chunks, 8, LANES).transpose(0, 2, 1, 3)
 
-    columns = own + far
-    kept, gone = columns[:token_rows], columns[token_rows:]
-    got = other_part(gone)
     quarters = [[c[:, :width], c[:, width:]] for c in (kept, got)]
 
     def pick_quarter(c, a):

time: 146 us -> 146 us (level)
  waiting for transfers between devices: 58.8 us -> 51.7 us
  local copies, waits for them, and re-layouts: 5.46 us -> 12 us
    ppermute x9, waiting for transfers between devices: 6.15 us -> 28.2 us  [exchange(): return lax.ppermute(value, 'tensor', [(t, t ^ s) for t in range(group)])]
    all_to_all x1, waiting for transfers between devices: 18.3 us -> 0.01 us  [fast_body(): back = lax.all_to_all(terms, 'tensor', 0, 0)]
    all_to_all x1, waiting for transfers between devices: 16.7 us -> 7.73 us  [fast_body(): panels = lax.all_to_all(sent, 'tensor', 0, 0)]
    unnamed x38 -> x44, local copies, waits for them, and re-layouts: 4.05 us -> 10.6 us
    ppermute x3, waiting for transfers between devices: 17.6 us -> 15.6 us  [other_part(): lax.ppermute(value, 'parts', [(a, parts - 1 - a) for a in range(parts)])]
    pallas_call x3, Pallas kernels: 15.2 us -> 13.4 us  [the longest x1 8.94 us: fast_body(): pl.pallas_call(zero_kernel, out_shape=(down_shape, up_shape, token), in_s...]
  transfers between devices with their start and end apart: 18 -> 19, of which waited for: 9 -> 6; matrix products, arithmetic and copies ran while one was open for 3% -> 3% of each run, Pallas kernels for 17% -> 19%
where the time goes in v5:
time: 146 us; the launch traced here: 144 us
  waiting for transfers between devices  51.7 us (35%)
  Pallas kernels  32.9 us (23%)
  starting transfers between devices  28.9 us (20%)
  between operations  14.9 us (10%)
  local copies, waits for them, and re-layouts  12 us (8%)
  other arithmetic  4.19 us (3%)
    ppermute x9, waiting for transfers between devices, exchange(): return lax.ppermute(value, 'tensor', [(t, t ^ s) for t in range(group)])  28.2 us
    ppermute x9, starting transfers between devices, exchange(): return lax.ppermute(value, 'tensor', [(t, t ^ s) for t in range(group)])  15.7 us
    ppermute x3, waiting for transfers between devices, other_part(): lax.ppermute(value, 'parts', [(a, parts - 1 - a) for a in range(parts)])  15.6 us
    unnamed x44, local copies, waits for them, and re-layouts  10.6 us
    pallas_call x1, Pallas kernels, fast_body(): pl.pallas_call(zero_kernel, out_shape=(down_shape, up_shape, token), in_s...  8.94 us
    pallas_call x1, Pallas kernels, fast_body(): pl.pallas_call(functools.partial(gather_kernel, group, down_chunks, up_ch...  8.09 us
    all_to_all x1, waiting for transfers between devices, fast_body(): panels = lax.all_to_all(sent, 'tensor', 0, 0)  7.73 us
    pallas_call x1, Pallas kernels, fast_body(): pl.pallas_call(functools.partial(scatter_kernel, 2 * group, down_chunks,...  5.46 us
  transfers between devices with their start and end apart: 19, of which 6 were waited for; matrix products, arithmetic and copies ran while one was open for 3% of the time, Pallas kernels for 19%

profile of v5, /device:TPU:0, one launch (start us, length us, event | category | flops | bytes accessed | tf_op | source)
XLA Modules:
  0.0 144.5 jit_solution(7536697519425328712)
XLA Ops:
  7.2 0.0 copy-start
  7.2 0.0 all-gather.2.cloned.1.call-start
  7.2 1.0 copy-done
  8.3 0.8 constant_dynamic-slice_fusion
  9.0 0.0 all-gather.2.cloned.1.call-update
  9.7 1.3 fusion.1
  11.0 0.6 broadcast_in_dim.24.refs_0_
  11.7 0.0 copy-start.14
  11.7 3.0 %collective-permute-start.2 = (s32[128]{0:T(128)S(1)}, s32[128]{0:T(128)S(1)}, u32[]{:S(2)}, u32[]{:S(2)}) collective-permute-start(s32[128]{0:T(128)S(1)} %broadcast_in_dim.24.refs_0_), channel_id=1, source_target_pairs={{0,1},{1,0},{2,3},{3,2},{4,5},{5,4},{6,7},{7,6},{8,9},{9,8},{10,11... | collective-permute-start | bytes 1544 | tf_op jit(solution)/shard_map/ppermute | solution.py:304
  14.7 1.6 %collective-permute-start.3 = (s32[128]{0:T(128)S(1)}, s32[128]{0:T(128)S(1)}, u32[]{:S(2)}, u32[]{:S(2)}) collective-permute-start(s32[128]{0:T(128)S(1)} %broadcast_in_dim.24.refs_0_), channel_id=1, source_target_pairs={{0,2},{1,3},{2,0},{3,1},{4,6},{5,7},{6,4},{7,5},{8,10},{9,11},{10,... | collective-permute-start | bytes 1544 | tf_op jit(solution)/shard_map/ppermute | solution.py:304
  16.3 0.0 collective-permute-start.4
  16.3 3.0 %collective-permute-start.5 = (s32[128]{0:T(128)S(1)}, s32[128]{0:T(128)S(1)}, u32[]{:S(2)}, u32[]{:S(2)}) collective-permute-start(s32[128]{0:T(128)S(1)} %broadcast_in_dim.24.refs_0_), channel_id=1, source_target_pairs={{0,4},{1,5},{2,6},{3,7},{4,0},{5,1},{6,2},{7,3},{8,12},{9,13},{10,... | collective-permute-start | bytes 1544 | tf_op jit(solution)/shard_map/ppermute | solution.py:304
  19.3 1.3 collective-permute-start.6
  20.5 0.0 collective-permute-done.2.refs_1_
  20.5 3.6 %collective-permute-start.7 = (s32[128]{0:T(128)S(1)}, s32[128]{0:T(128)S(1)}, u32[]{:S(2)}, u32[]{:S(2)}) collective-permute-start(s32[128]{0:T(128)S(1)} %broadcast_in_dim.24.refs_0_), channel_id=1, source_target_pairs={{0,6},{1,7},{2,4},{3,5},{4,2},{5,3},{6,0},{7,1},{8,14},{9,15},{10,... | collective-permute-start | bytes 1544 | tf_op jit(solution)/shard_map/ppermute | solution.py:304
  24.1 0.0 collective-permute-done.3.refs_2_
  24.1 0.1 collective-permute-start.8
  24.2 1.3 copy-done.2
  25.5 0.5 split_tokens.1
  26.1 0.8 copy-done.5
  26.9 0.8 copy-done.13
  27.7 0.0 collective-permute-done.4.refs_3_
  27.7 0.0 collective-permute-done.5.refs_4_
  27.8 0.0 collective-permute-done.6.refs_5_
  27.8 0.0 copy-start.19
  27.8 0.0 collective-permute-done.7.refs_6_
  27.8 2.7 %collective-permute-done.8.refs_7_ = s32[128]{0:T(128)S(1)} collective-permute-done((s32[128]{0:T(128)S(1)}, s32[128]{0:T(128)S(1)}, u32[]{:S(2)}, u32[]{:S(2)}) %collective-permute-start.8) | collective-permute-done | bytes 544 | tf_op jit(solution)/shard_map/ppermute | solution.py:304
  30.5 0.5 copy-done.21
  31.1 8.1 %pick_panels.1 = (bf16[8,384,128]{2,1,0:T(8,128)(2,1)}, s32[8]{0:T(128)}) custom-call(s32[1]{0:T(128)} %bitcast.1.where, s32[1]{0:T(128)} %get-tuple-element.23.after, s32[128]{0:T(128)} %copy-done.14, s32[128]{0:T(128)} %copy-done.15, s32[128]{0:T(128)} %copy-done.16, s32[128]{0:T(128)} %copy-done.17, s32[128]{0:T(128)} %copy-done.18, s32[128]{0:T(128)} %copy-done.19, ...), custom_call_target="tpu_custom_call" | custom-call | tf_op jit(solution)/shard_map/pick_panels/pallas_call | solution.py:336
  39.1 4.2 %all-to-all-start = ((bf16[8,384,128]{2,1,0:T(8,128)(2,1)}), bf16[8,384,128]{2,1,0:T(8,128)(2,1)}, u32[]{:S(2)}, u32[]{:S(2)}) async-start(bf16[8,384,128]{2,1,0:T(8,128)(2,1)} %get-tuple-element.24.after_ref), calls=%async_computation | async-start | bytes 1572864 | tf_op jit(solution)/shard_map/all_to_all | solution.py:353
  43.4 1.8 %pair_columns.1.xs_ref = bf16[8,256,320]{2,1,0:T(8,128)(2,1)S(1)} custom-call(bf16[128,5120]{1,0:T(8,128)(2,1)S(1)} %copy-done.3), custom_call_target="tpu_custom_call" | custom-call | tf_op jit(solution)/shard_map/pair_columns/pallas_call | solution.py:329
  45.2 8.9 %clear_rows.1 = (f32[16,320,8,1,128]{4,3,2,1,0:T(1,128)}, f32[16,64,8,1,128]{4,3,2,1,0:T(1,128)}, s32[1]{0:T(128)}) custom-call(bf16[8,384,128]{2,1,0:T(8,128)(2,1)} %get-tuple-element.24.after_ref), custom_call_target="tpu_custom_call" | custom-call | tf_op jit(solution)/shard_map/clear_rows/pallas_call | solution.py:361
  54.1 7.7 %all-to-all-done.pieces = bf16[8,384,128]{2,1,0:T(8,128)(2,1)} async-done(((bf16[8,384,128]{2,1,0:T(8,128)(2,1)}), bf16[8,384,128]{2,1,0:T(8,128)(2,1)}, u32[]{:S(2)}, u32[]{:S(2)}) %all-to-all-start) | async-done | bytes 786464 | tf_op jit(solution)/shard_map/all_to_all | solution.py:353
  61.9 0.9 copy-done.11
  62.8 4.1 %adapter.1 = (bf16[8,384,128]{2,1,0:T(8,128)(2,1)}, f32[128,1024]{1,0:T(8,128)S(1)}) custom-call(bf16[8,256,320]{2,1,0:T(8,128)(2,1)S(1)} %pair_columns.1.xs_ref, bf16[128,1024]{1,0:T(8,128)(2,1)S(1)} %copy-done.11, bf16[8,384,128]{2,1,0:T(8,128)(2,1)} %all-to-all-done.pieces, s32[1]{0:T(128)} %get-tuple-element.26._), custom_call_target="tpu_custom_call" | custom-call | tf_op jit(solution)/shard_map/adapter/pallas_call | solution.py:368
  67.0 3.7 %all-to-all-start.1 = ((bf16[8,384,128]{2,1,0:T(8,128)(2,1)}), bf16[8,384,128]{2,1,0:T(8,128)(2,1)S(1)}, u32[]{:S(2)}, u32[]{:S(2)}) async-start(bf16[8,384,128]{2,1,0:T(8,128)(2,1)} %get-tuple-element.28.refs_6_), calls=%async_computation.1 | async-start | bytes 1572864 | tf_op jit(solution)/shard_map/all_to_all | solution.py:391
  70.7 1.9 %collective-permute-start.1 = (bf16[4,128,640]{2,1,0:T(8,128)(2,1)}, bf16[4,128,640]{2,1,0:T(8,128)(2,1)S(1)}, u32[]{:S(2)}, u32[]{:S(2)}) collective-permute-start(bf16[4,128,640]{2,1,0:T(8,128)(2,1)} %copy-done.13), channel_id=1, source_target_pairs={{0,1},{1,0},{2,3},{3,2},{4,5},{5,4},{6,7},{7,6},{8,9},{9,8},{10,11... | collective-permute-start | bytes 1966088 | tf_op jit(solution)/shard_map/ppermute | solution.py:304
  72.6 0.0 collective-permute-start.10
  72.6 1.4 collective-permute-start
  73.9 20.3 %collective-permute-done.1.refs_2_ = bf16[4,128,640]{2,1,0:T(8,128)(2,1)S(1)} collective-permute-done((bf16[4,128,640]{2,1,0:T(8,128)(2,1)}, bf16[4,128,640]{2,1,0:T(8,128)(2,1)S(1)}, u32[]{:S(2)}, u32[]{:S(2)}) %collective-permute-start.1) | collective-permute-done | bytes 655392 | tf_op jit(solution)/shard_map/ppermute | solution.py:304
  94.2 1.6 %collective-permute-start.9 = (bf16[4,128,640]{2,1,0:T(8,128)(2,1)S(1)}, bf16[4,128,640]{2,1,0:T(8,128)(2,1)}, u32[]{:S(2)}, u32[]{:S(2)}) collective-permute-start(bf16[4,128,640]{2,1,0:T(8,128)(2,1)S(1)} %collective-permute-done.1.refs_2_), channel_id=1, source_target_pairs={{0,16},{16,0},{1,17},{17,1},{2,18},{18,2},{3,19},{19,3},{4,20},{20... | collective-permute-start | bytes 1966088 | tf_op jit(solution)/shard_map/ppermute | solution.py:310
  95.9 0.9 copy-done.7
  96.7 0.0 all-to-all-done.1.rest_0_
  96.7 0.0 collective-permute-start.15
  96.7 0.0 collective-permute-done.refs_1_
  96.8 12.3 %collective-permute-done.9.refs_3_ = bf16[4,128,640]{2,1,0:T(8,128)(2,1)} collective-permute-done((bf16[4,128,640]{2,1,0:T(8,128)(2,1)S(1)}, bf16[4,128,640]{2,1,0:T(8,128)(2,1)}, u32[]{:S(2)}, u32[]{:S(2)}) %collective-permute-start.9) | collective-permute-done | bytes 655392 | tf_op jit(solution)/shard_map/ppermute | solution.py:310
  109.1 0.0 collective-permute-done.10.refs_5_
  109.1 1.3 copy-done.4
  110.4 1.1 copy-done.6
  111.5 1.1 copy-done.8
  112.6 3.9 %frozen_part.1 = (f32[128,512]{1,0:T(8,128)S(1)}, f32[128,512]{1,0:T(8,128)}, f32[128,512]{1,0:T(8,128)}, f32[128,512]{1,0:T(8,128)}) custom-call(bf16[4,128,640]{2,1,0:T(8,128)(2,1)S(1)} %copy-done.6, bf16[4,128,640]{2,1,0:T(8,128)(2,1)} %collective-permute-done.refs_1_, bf16[4,128,640]{2,1,0:T(8,128)(2,1)S(1)} %copy-done.8, ...), custom_call_target="tpu_custom_call" | custom-call | tf_op jit(solution)/shard_map/frozen_part/pallas_call | solution.py:380
  116.5 0.7 copy-done.10
  117.2 1.2 collective-permute-start.11
  118.4 1.7 %collective-permute-start.12 = (f32[128,512]{1,0:T(8,128)}, f32[128,512]{1,0:T(8,128)S(1)}, u32[]{:S(2)}, u32[]{:S(2)}) collective-permute-start(f32[128,512]{1,0:T(8,128)} %get-tuple-element.31), channel_id=1, source_target_pairs={{0,16},{16,0},{1,17},{17,1},{2,18},{18,2},{3,19},{19,3},{4,20},{20... | collective-permute-start | bytes 786440 | tf_op jit(solution)/shard_map/ppermute | solution.py:310
  120.1 0.5 collective-permute-start.13
  120.7 0.0 collective-permute-start.14
  120.7 5.3 %collective-permute-done.11 = f32[128,512]{1,0:T(8,128)S(1)} collective-permute-done((f32[128,512]{1,0:T(8,128)}, f32[128,512]{1,0:T(8,128)S(1)}, u32[]{:S(2)}, u32[]{:S(2)}) %collective-permute-start.11) | collective-permute-done | bytes 262176 | tf_op jit(solution)/shard_map/ppermute | solution.py:304
  125.9 1.0 add.18
  126.9 3.3 %collective-permute-done.12 = f32[128,512]{1,0:T(8,128)S(1)} collective-permute-done((f32[128,512]{1,0:T(8,128)}, f32[128,512]{1,0:T(8,128)S(1)}, u32[]{:S(2)}, u32[]{:S(2)}) %collective-permute-start.12) | collective-permute-done | bytes 262176 | tf_op jit(solution)/shard_map/ppermute | solution.py:310
  130.2 0.0 collective-permute-done.13
  130.3 1.8 %fusion = bf16[128,1024]{1,0:T(8,128)(2,1)} fusion(f32[128,1024]{1,0:T(8,128)} %copy-done.9, f32[128,256]{1,0:T(8,128)S(1)} %get-tuple-element.42, f32[128,256]{1,0:T(8,128)S(1)} %get-tuple-element.41, f32[128,256]{1,0:T(8,128)S(1)} %get-tuple-element.40, f32[128,256]{1,0:T(8,128)S(1)} %get-tuple-element.39), kind=kLoop, calls=%fused_computation.1 | loop fusion | flops 655360 | bytes 1310720 | tf_op jit(solution)/shard_map/convert_element_type | solution.py:427
  132.1 0.0 collective-permute-done.14.rows_core
  132.1 0.0 collective-permute-done.15.rest_1_
  132.1 5.5 %place_rows.1 = (f32[16,320,8,1,128]{4,3,2,1,0:T(1,128)}, f32[16,64,8,1,128]{4,3,2,1,0:T(1,128)}) custom-call(s32[1]{0:T(128)} %bitcast.3.first_row, s32[8]{0:T(128)S(1)} %copy-done.12, s32[8]{0:T(128)S(1)} %collective-permute-done.14.rows_core, bf16[8,384,128]{2,1,0:T(8,128)(2,1)S(1)} %all-to-all-done.1.rest_0_, ...), custom_call_target="tpu_custom_call", output_to_operand_aliasing={{0}: (5, {}), {1}: (6, {})} | custom-call | tf_op jit(solution)/shard_map/place_rows/pallas_call | solution.py:394
  (33 shorter events, 0.1 us)
Async XLA Ops:
  7.2 1.1 copy-start
  7.2 65.4 %all-gather.2.cloned.1.call-start = ((), (), s32[]{:S(2)}) async-start(), calls=%async_computation.2 | async-start | bytes 1638400 | tf_op jit(solution)/shard_map/all_gather | solution.py:318
  11.7 18.8 %copy-start.14 = (s32[128]{0:T(128)}, s32[128]{0:T(128)S(1)}, u32[]{:S(2)}) copy-start(s32[128]{0:T(128)S(1)} %broadcast_in_dim.24.refs_0_) | copy-start | bytes 1540
  11.7 8.9 %collective-permute-start.2 = (s32[128]{0:T(128)S(1)}, s32[128]{0:T(128)S(1)}, u32[]{:S(2)}, u32[]{:S(2)}) collective-permute-start(s32[128]{0:T(128)S(1)} %broadcast_in_dim.24.refs_0_), channel_id=1, source_target_pairs={{0,1},{1,0},{2,3},{3,2},{4,5},{5,4},{6,7},{7,6},{8,9},{9,8},{10,11... | collective-permute-start | bytes 1544 | tf_op jit(solution)/shard_map/ppermute | solution.py:304
  14.7 9.5 %collective-permute-start.3 = (s32[128]{0:T(128)S(1)}, s32[128]{0:T(128)S(1)}, u32[]{:S(2)}, u32[]{:S(2)}) collective-permute-start(s32[128]{0:T(128)S(1)} %broadcast_in_dim.24.refs_0_), channel_id=1, source_target_pairs={{0,2},{1,3},{2,0},{3,1},{4,6},{5,7},{6,4},{7,5},{8,10},{9,11},{10,... | collective-permute-start | bytes 1544 | tf_op jit(solution)/shard_map/ppermute | solution.py:304
  16.3 11.5 %collective-permute-start.4 = (s32[128]{0:T(128)S(1)}, s32[128]{0:T(128)S(1)}, u32[]{:S(2)}, u32[]{:S(2)}) collective-permute-start(s32[128]{0:T(128)S(1)} %broadcast_in_dim.24.refs_0_), channel_id=1, source_target_pairs={{0,3},{1,2},{2,1},{3,0},{4,7},{5,6},{6,5},{7,4},{8,11},{9,10},{10,... | collective-permute-start | bytes 1544 | tf_op jit(solution)/shard_map/ppermute | solution.py:304
  16.3 11.5 %collective-permute-start.5 = (s32[128]{0:T(128)S(1)}, s32[128]{0:T(128)S(1)}, u32[]{:S(2)}, u32[]{:S(2)}) collective-permute-start(s32[128]{0:T(128)S(1)} %broadcast_in_dim.24.refs_0_), channel_id=1, source_target_pairs={{0,4},{1,5},{2,6},{3,7},{4,0},{5,1},{6,2},{7,3},{8,12},{9,13},{10,... | collective-permute-start | bytes 1544 | tf_op jit(solution)/shard_map/ppermute | solution.py:304
  19.3 8.5 %collective-permute-start.6 = (s32[128]{0:T(128)S(1)}, s32[128]{0:T(128)S(1)}, u32[]{:S(2)}, u32[]{:S(2)}) collective-permute-start(s32[128]{0:T(128)S(1)} %broadcast_in_dim.24.refs_0_), channel_id=1, source_target_pairs={{0,5},{1,4},{2,7},{3,6},{4,1},{5,0},{6,3},{7,2},{8,13},{9,12},{10,... | collective-permute-start | bytes 1544 | tf_op jit(solution)/shard_map/ppermute | solution.py:304
  20.5 10.0 %copy-start.15 = (s32[128]{0:T(128)}, s32[128]{0:T(128)S(1)}, u32[]{:S(2)}) copy-start(s32[128]{0:T(128)S(1)} %collective-permute-done.2.refs_1_) | copy-start | bytes 1540
  20.5 7.2 %collective-permute-start.7 = (s32[128]{0:T(128)S(1)}, s32[128]{0:T(128)S(1)}, u32[]{:S(2)}, u32[]{:S(2)}) collective-permute-start(s32[128]{0:T(128)S(1)} %broadcast_in_dim.24.refs_0_), channel_id=1, source_target_pairs={{0,6},{1,7},{2,4},{3,5},{4,2},{5,3},{6,0},{7,1},{8,14},{9,15},{10,... | collective-permute-start | bytes 1544 | tf_op jit(solution)/shard_map/ppermute | solution.py:304
  24.1 6.4 %copy-start.16 = (s32[128]{0:T(128)}, s32[128]{0:T(128)S(1)}, u32[]{:S(2)}) copy-start(s32[128]{0:T(128)S(1)} %collective-permute-done.3.refs_2_) | copy-start | bytes 1540
  24.1 6.3 %collective-permute-start.8 = (s32[128]{0:T(128)S(1)}, s32[128]{0:T(128)S(1)}, u32[]{:S(2)}, u32[]{:S(2)}) collective-permute-start(s32[128]{0:T(128)S(1)} %broadcast_in_dim.24.refs_0_), channel_id=1, source_target_pairs={{0,7},{1,6},{2,5},{3,4},{4,3},{5,2},{6,1},{7,0},{8,15},{9,14},{10,... | collective-permute-start | bytes 1544 | tf_op jit(solution)/shard_map/ppermute | solution.py:304
  24.2 1.3 copy-start.2
  26.1 0.8 copy-start.5
  26.9 0.8 copy-start.13
  27.7 2.8 %copy-start.17 = (s32[128]{0:T(128)}, s32[128]{0:T(128)S(1)}, u32[]{:S(2)}) copy-start(s32[128]{0:T(128)S(1)} %collective-permute-done.4.refs_3_) | copy-start | bytes 1540
  27.8 2.8 %copy-start.18 = (s32[128]{0:T(128)}, s32[128]{0:T(128)S(1)}, u32[]{:S(2)}) copy-start(s32[128]{0:T(128)S(1)} %collective-permute-done.5.refs_4_) | copy-start | bytes 1540
  27.8 2.7 %copy-start.19 = (s32[128]{0:T(128)}, s32[128]{0:T(128)S(1)}, u32[]{:S(2)}) copy-start(s32[128]{0:T(128)S(1)} %collective-permute-done.6.refs_5_) | copy-start | bytes 1540
  27.8 2.7 %copy-start.20 = (s32[128]{0:T(128)}, s32[128]{0:T(128)S(1)}, u32[]{:S(2)}) copy-start(s32[128]{0:T(128)S(1)} %collective-permute-done.7.refs_6_) | copy-start | bytes 1540
  30.5 0.6 copy-start.21
  31.0 12.3 %copy-start.3 = (bf16[128,5120]{1,0:T(8,128)(2,1)S(1)}, bf16[128,5120]{1,0:T(8,128)(2,1)}, u32[]{:S(2)}) copy-start(bf16[128,5120]{1,0:T(8,128)(2,1)} %x_ref.3) | copy-start | bytes 3932164
  39.1 22.7 %all-to-all-start = ((bf16[8,384,128]{2,1,0:T(8,128)(2,1)}), bf16[8,384,128]{2,1,0:T(8,128)(2,1)}, u32[]{:S(2)}, u32[]{:S(2)}) async-start(bf16[8,384,128]{2,1,0:T(8,128)(2,1)} %get-tuple-element.24.after_ref), calls=%async_computation | async-start | bytes 1572864 | tf_op jit(solution)/shard_map/all_to_all | solution.py:353
  61.9 1.0 copy-start.11
  67.0 3.7 %copy-start.9 = (f32[128,1024]{1,0:T(8,128)}, f32[128,1024]{1,0:T(8,128)S(1)}, u32[]{:S(2)}) copy-start(f32[128,1024]{1,0:T(8,128)S(1)} %get-tuple-element.33) | copy-start | bytes 1572868
  67.0 53.7 %copy-start.12 = (s32[8]{0:T(128)S(1)}, s32[8]{0:T(128)}, u32[]{:S(2)}) copy-start(s32[8]{0:T(128)} %get-tuple-element.34.rows_here) | copy-start | bytes 100
  67.0 29.8 %all-to-all-start.1 = ((bf16[8,384,128]{2,1,0:T(8,128)(2,1)}), bf16[8,384,128]{2,1,0:T(8,128)(2,1)S(1)}, u32[]{:S(2)}, u32[]{:S(2)}) async-start(bf16[8,384,128]{2,1,0:T(8,128)(2,1)} %get-tuple-element.28.refs_6_), calls=%async_computation.1 | async-start | bytes 1572864 | tf_op jit(solution)/shard_map/all_to_all | solution.py:391
  70.7 23.6 %collective-permute-start.1 = (bf16[4,128,640]{2,1,0:T(8,128)(2,1)}, bf16[4,128,640]{2,1,0:T(8,128)(2,1)S(1)}, u32[]{:S(2)}, u32[]{:S(2)}) collective-permute-start(bf16[4,128,640]{2,1,0:T(8,128)(2,1)} %copy-done.13), channel_id=1, source_target_pairs={{0,1},{1,0},{2,3},{3,2},{4,5},{5,4},{6,7},{7,6},{8,9},{9,8},{10,11... | collective-permute-start | bytes 1966088 | tf_op jit(solution)/shard_map/ppermute | solution.py:304
  72.6 36.5 %collective-permute-start.10 = (bf16[2560,256]{1,0:T(8,128)(2,1)}, bf16[2560,256]{1,0:T(8,128)(2,1)S(1)}, u32[]{:S(2)}, u32[]{:S(2)}) collective-permute-start(bf16[2560,256]{1,0:T(8,128)(2,1)} %all-gather.2.cloned.1.call-done.refs_4_), channel_id=1, source_target_pairs={{0,8},{8,0},{1,9},{9,1},{2,10},{10,2},{3,11},{11,3},{4,12},{12,4},... | collective-permute-start | bytes 3932168 | tf_op jit(solution)/shard_map/ppermute | solution.py:307
  72.6 24.2 %collective-permute-start = (bf16[4,128,640]{2,1,0:T(8,128)(2,1)}, bf16[4,128,640]{2,1,0:T(8,128)(2,1)}, u32[]{:S(2)}, u32[]{:S(2)}) collective-permute-start(bf16[4,128,640]{2,1,0:T(8,128)(2,1)} %copy-done.5), channel_id=1, source_target_pairs={{0,16},{16,0},{1,17},{17,1},{2,18},{18,2},{3,19},{19,3},{4,20},{20... | collective-permute-start | bytes 1966088 | tf_op jit(solution)/shard_map/ppermute | solution.py:310
  94.2 14.8 %collective-permute-start.9 = (bf16[4,128,640]{2,1,0:T(8,128)(2,1)S(1)}, bf16[4,128,640]{2,1,0:T(8,128)(2,1)}, u32[]{:S(2)}, u32[]{:S(2)}) collective-permute-start(bf16[4,128,640]{2,1,0:T(8,128)(2,1)S(1)} %collective-permute-done.1.refs_2_), channel_id=1, source_target_pairs={{0,16},{16,0},{1,17},{17,1},{2,18},{18,2},{3,19},{19,3},{4,20},{20... | collective-permute-start | bytes 1966088 | tf_op jit(solution)/shard_map/ppermute | solution.py:310
  95.9 0.9 copy-start.7
  96.7 35.4 %collective-permute-start.15 = (bf16[8,384,128]{2,1,0:T(8,128)(2,1)S(1)}, bf16[8,384,128]{2,1,0:T(8,128)(2,1)S(1)}, u32[]{:S(2)}, u32[]{:S(2)}) collective-permute-start(bf16[8,384,128]{2,1,0:T(8,128)(2,1)S(1)} %all-to-all-done.1.rest_0_), channel_id=1, source_target_pairs={{0,8},{8,0},{1,9},{9,1},{2,10},{10,2},{3,11},{11,3},{4,12},{12,4},... | collective-permute-start | bytes 2359304 | tf_op jit(solution)/shard_map/ppermute | solution.py:307
  109.1 1.3 copy-start.4
  110.4 1.1 copy-start.6
  111.5 1.1 copy-start.8
  116.5 0.7 copy-start.10
  117.2 8.8 %collective-permute-start.11 = (f32[128,512]{1,0:T(8,128)}, f32[128,512]{1,0:T(8,128)S(1)}, u32[]{:S(2)}, u32[]{:S(2)}) collective-permute-start(f32[128,512]{1,0:T(8,128)} %get-tuple-element.30), channel_id=1, source_target_pairs={{0,1},{1,0},{2,3},{3,2},{4,5},{5,4},{6,7},{7,6},{8,9},{9,8},{10,11... | collective-permute-start | bytes 786440 | tf_op jit(solution)/shard_map/ppermute | solution.py:304
  118.4 11.8 %collective-permute-start.12 = (f32[128,512]{1,0:T(8,128)}, f32[128,512]{1,0:T(8,128)S(1)}, u32[]{:S(2)}, u32[]{:S(2)}) collective-permute-start(f32[128,512]{1,0:T(8,128)} %get-tuple-element.31), channel_id=1, source_target_pairs={{0,16},{16,0},{1,17},{17,1},{2,18},{18,2},{3,19},{19,3},{4,20},{20... | collective-permute-start | bytes 786440 | tf_op jit(solution)/shard_map/ppermute | solution.py:310
  120.1 10.1 %collective-permute-start.13 = (f32[128,512]{1,0:T(8,128)}, f32[128,512]{1,0:T(8,128)S(1)}, u32[]{:S(2)}, u32[]{:S(2)}) collective-permute-start(f32[128,512]{1,0:T(8,128)} %get-tuple-element.32), channel_id=1, source_target_pairs={{0,17},{1,16},{2,19},{3,18},{4,21},{5,20},{6,23},{7,22},{16,1},{17... | collective-permute-start | bytes 786440 | tf_op jit(solution)/shard_map/ppermute | solution.py:390
  120.7 11.5 %collective-permute-start.14 = (s32[8]{0:T(128)S(1)}, s32[8]{0:T(128)S(1)}, u32[]{:S(2)}, u32[]{:S(2)}) collective-permute-start(s32[8]{0:T(128)S(1)} %copy-done.12), channel_id=1, source_target_pairs={{0,8},{8,0},{1,9},{9,1},{2,10},{10,2},{3,11},{11,3},{4,12},{12,4},... | collective-permute-start | bytes 104 | tf_op jit(solution)/shard_map/ppermute | solution.py:307
  132.1 5.5 %copy-start.1 = (bf16[640,512]{1,0:T(8,128)(2,1)S(1)}, bf16[640,512]{1,0:T(8,128)(2,1)}, u32[]{:S(2)}) copy-start(bf16[640,512]{1,0:T(8,128)(2,1)} %param.9) | copy-start | bytes 1966084
Sparse Core Ops, SparseCore 0:
  9.6 35.6 all-gather.1

commit v6 on v5

--- a/solution.py
+++ b/solution.py
@@ -325,6 +325,7 @@
     )(x[None], tokens)
     x_far = exchange(x_theirs, 1)
     y_mine = other_part(x_mine)
+    split, x_far, y_mine = lax.optimization_barrier((split, x_far, y_mine))
 
     xs = pl.pallas_call(
         interleave_kernel,
@@ -352,18 +353,21 @@
     )(me[None], split, *asked, down_store, up_store)
     panels = lax.all_to_all(sent, "tensor", 0, 0)
     rows_core = other_core(rows)
-    x_far, _ = lax.optimization_barrier((x_far, sent))
-    x_blocks = (x_mine, y_mine, x_far, other_part(x_far))
+    x_far, _ = lax.optimization_barrier((x_far, rows))
+    y_far = other_part(x_far)
 
     owned_groups = ADAPTERS // lax.axis_size("dp") // 8
     down_shape = jax.ShapeDtypeStruct((owned_groups, down_chunks, 8, 1, LANES), jnp.float32)
     up_shape = jax.ShapeDtypeStruct((owned_groups, up_chunks, 8, 1, LANES), jnp.float32)
     down_zero, up_zero, cleared = pl.pallas_call(
         zero_kernel, out_shape=(down_shape, up_shape, token),
-        in_specs=[ANY], out_specs=(ANY, ANY, SMEM),
+        in_specs=[SMEM], out_specs=(ANY, ANY, SMEM),
         scratch_shapes=[pltpu.VMEM((up_chunks, 8, 1, LANES), jnp.float32), pltpu.SemaphoreType.DMA((2,))],
-        compiler_params=WIDE, name="clear_rows",
-    )(sent)
+        compiler_params=LIMIT, name="clear_rows",
+    )(rows)
+    half, _ = lax.optimization_barrier((half, cleared))
+    half_core = other_core(half)
+    panels, y_far, half_core = lax.optimization_barrier((panels, y_far, half_core))
 
     terms, lifted = pl.pallas_call(
         functools.partial(adapter_kernel, group, down_chunks),
@@ -374,8 +378,6 @@
         compiler_params=LIMIT,
         name="adapter",
     )(xs, cotangent, panels, cleared)
-    half, _ = lax.optimization_barrier((half, cleared))
-    both = (half, other_core(half))
     sums = jax.ShapeDtypeStruct((token_rows, parts * width), jnp.float32)
     own, to_part, to_inner, to_both = pl.pallas_call(
         base_kernel,
@@ -384,7 +386,7 @@
         out_specs=[VMEM] * 4,
         compiler_params=LIMIT,
         name="frozen_part",
-    )(*x_blocks, *both, terms)
+    )(x_mine, y_mine, x_far, y_far, half, half_core, terms)
     opposite = [(a * group + t, (parts - 1 - a) * group + (t ^ 1)) for a in range(parts) for t in range(group)]
     kept = own + exchange(to_inner, 1)
     got = other_part(to_part) + lax.ppermute(to_both, ("parts", "tensor"), opposite)

time: 146 us -> 142 us (0.973)
  blocking collectives: 0 us -> 25.8 us
  waiting for transfers between devices: 51.7 us -> 30.9 us
  local copies, waits for them, and re-layouts: 12 us -> 7.61 us
  starting transfers between devices: 28.9 us -> 26.3 us
    all_to_all x0 -> x1, blocking collectives: none -> 25.8 us  [fast_body(): back = lax.all_to_all(terms, 'tensor', 0, 0)]
    ppermute x9, waiting for transfers between devices: 28.2 us -> 10.1 us  [exchange(): return lax.ppermute(value, 'tensor', [(t, t ^ s) for t in range(group)])]
    all_to_all x1, waiting for transfers between devices: 7.73 us -> 0.01 us  [fast_body(): panels = lax.all_to_all(sent, 'tensor', 0, 0)]
    ppermute x3, waiting for transfers between devices: 15.6 us -> 20.8 us  [other_part(): lax.ppermute(value, 'parts', [(a, parts - 1 - a) for a in range(parts)])]
    unnamed x44 -> x42, local copies, waits for them, and re-layouts: 10.6 us -> 6.27 us
    all_to_all x1 -> x0, starting transfers between devices: 3.68 us -> none  [fast_body(): back = lax.all_to_all(terms, 'tensor', 0, 0)]
  transfers between devices with their start and end apart: 19 -> 18, of which waited for: 6 -> 7; matrix products, arithmetic and copies ran while one was open for 3% -> 3% of each run, Pallas kernels for 19% -> 17%
where the time goes in v6:
time: 142 us; the launch traced here: 140 us
  Pallas kernels  31.5 us (22%)
  waiting for transfers between devices  30.9 us (22%)
  starting transfers between devices  26.3 us (19%)
  blocking collectives  25.8 us (18%)
  between operations  15 us (11%)
  local copies, waits for them, and re-layouts  7.61 us (5%)
  other arithmetic  3.24 us (2%)
    all_to_all x1, blocking collectives, fast_body(): back = lax.all_to_all(terms, 'tensor', 0, 0)  25.8 us
    ppermute x3, waiting for transfers between devices, other_part(): lax.ppermute(value, 'parts', [(a, parts - 1 - a) for a in range(parts)])  20.8 us
    ppermute x9, starting transfers between devices, exchange(): return lax.ppermute(value, 'tensor', [(t, t ^ s) for t in range(group)])  16.3 us
    ppermute x9, waiting for transfers between devices, exchange(): return lax.ppermute(value, 'tensor', [(t, t ^ s) for t in range(group)])  10.1 us
    pallas_call x1, Pallas kernels, fast_body(): pl.pallas_call(zero_kernel, out_shape=(down_shape, up_shape, token), in_s...  9.48 us
    pallas_call x1, Pallas kernels, fast_body(): pl.pallas_call(functools.partial(gather_kernel, group, down_chunks, up_ch...  8.36 us
    unnamed x42, local copies, waits for them, and re-layouts  6.27 us
    all_to_all x1, starting transfers between devices, fast_body(): panels = lax.all_to_all(sent, 'tensor', 0, 0)  5.23 us
  transfers between devices with their start and end apart: 18, of which 7 were waited for; matrix products, arithmetic and copies ran while one was open for 3% of the time, Pallas kernels for 17%

profile of v6, /device:TPU:0, one launch (start us, length us, event | category | flops | bytes accessed | tf_op | source)
XLA Modules:
  0.0 140.3 jit_solution(3576028936127039224)
XLA Ops:
  7.2 0.0 copy-start
  7.2 0.0 all-gather.2.cloned.1.call-start
  7.2 1.0 copy-done
  8.3 0.8 constant_dynamic-slice_fusion
  9.0 0.0 all-gather.2.cloned.1.call-update
  9.1 0.0 copy-start.2
  9.1 1.3 copy-done.2
  10.4 0.5 split_tokens.1
  10.9 3.0 %collective-permute-start = (bf16[4,128,640]{2,1,0:T(8,128)(2,1)S(1)}, bf16[4,128,640]{2,1,0:T(8,128)(2,1)}, u32[]{:S(2)}, u32[]{:S(2)}) collective-permute-start(bf16[4,128,640]{2,1,0:T(8,128)(2,1)S(1)} %get-tuple-element.29), channel_id=1, source_target_pairs={{0,1},{1,0},{2,3},{3,2},{4,5},{5,4},{6,7},{7,6},{8,9},{9,8},{10,11... | collective-permute-start | bytes 1966088 | tf_op jit(solution)/shard_map/ppermute | solution.py:304
  13.9 1.5 %collective-permute-start.1 = (bf16[4,128,640]{2,1,0:T(8,128)(2,1)S(1)}, bf16[4,128,640]{2,1,0:T(8,128)(2,1)S(1)}, u32[]{:S(2)}, u32[]{:S(2)}) collective-permute-start(bf16[4,128,640]{2,1,0:T(8,128)(2,1)S(1)} %get-tuple-element.27.refs_0_), channel_id=1, source_target_pairs={{0,16},{16,0},{1,17},{17,1},{2,18},{18,2},{3,19},{19,3},{4,20},{20... | collective-permute-start | bytes 1966088 | tf_op jit(solution)/shard_map/ppermute | solution.py:310
  16.1 1.3 fusion.1
  17.4 0.6 broadcast_in_dim.24.refs_0_
  18.0 0.0 copy-start.13
  18.0 3.6 %collective-permute-start.8 = (s32[128]{0:T(128)S(1)}, s32[128]{0:T(128)S(1)}, u32[]{:S(2)}, u32[]{:S(2)}) collective-permute-start(s32[128]{0:T(128)S(1)} %broadcast_in_dim.24.refs_0_), channel_id=1, source_target_pairs={{0,7},{1,6},{2,5},{3,4},{4,3},{5,2},{6,1},{7,0},{8,15},{9,14},{10,... | collective-permute-start | bytes 1544 | tf_op jit(solution)/shard_map/ppermute | solution.py:304
  21.6 0.2 collective-permute-start.7
  21.9 1.7 %collective-permute-start.6 = (s32[128]{0:T(128)S(1)}, s32[128]{0:T(128)S(1)}, u32[]{:S(2)}, u32[]{:S(2)}) collective-permute-start(s32[128]{0:T(128)S(1)} %broadcast_in_dim.24.refs_0_), channel_id=1, source_target_pairs={{0,5},{1,4},{2,7},{3,6},{4,1},{5,0},{6,3},{7,2},{8,13},{9,12},{10,... | collective-permute-start | bytes 1544 | tf_op jit(solution)/shard_map/ppermute | solution.py:304
  23.6 0.7 collective-permute-done.8.refs_7_
  24.3 1.4 %collective-permute-start.5 = (s32[128]{0:T(128)S(1)}, s32[128]{0:T(128)S(1)}, u32[]{:S(2)}, u32[]{:S(2)}) collective-permute-start(s32[128]{0:T(128)S(1)} %broadcast_in_dim.24.refs_0_), channel_id=1, source_target_pairs={{0,4},{1,5},{2,6},{3,7},{4,0},{5,1},{6,2},{7,3},{8,12},{9,13},{10,... | collective-permute-start | bytes 1544 | tf_op jit(solution)/shard_map/ppermute | solution.py:304
  25.7 1.3 collective-permute-done.7.refs_6_
  27.0 1.6 %collective-permute-start.4 = (s32[128]{0:T(128)S(1)}, s32[128]{0:T(128)S(1)}, u32[]{:S(2)}, u32[]{:S(2)}) collective-permute-start(s32[128]{0:T(128)S(1)} %broadcast_in_dim.24.refs_0_), channel_id=1, source_target_pairs={{0,3},{1,2},{2,1},{3,0},{4,7},{5,6},{6,5},{7,4},{8,11},{9,10},{10,... | collective-permute-start | bytes 1544 | tf_op jit(solution)/shard_map/ppermute | solution.py:304
  28.6 0.2 collective-permute-done.refs_2_
  28.8 1.8 %collective-permute-start.3 = (s32[128]{0:T(128)S(1)}, s32[128]{0:T(128)S(1)}, u32[]{:S(2)}, u32[]{:S(2)}) collective-permute-start(s32[128]{0:T(128)S(1)} %broadcast_in_dim.24.refs_0_), channel_id=1, source_target_pairs={{0,2},{1,3},{2,0},{3,1},{4,6},{5,7},{6,4},{7,5},{8,10},{9,11},{10,... | collective-permute-start | bytes 1544 | tf_op jit(solution)/shard_map/ppermute | solution.py:304
  30.6 0.0 collective-permute-done.1.refs_1_
  30.6 0.8 copy-done.5
  31.5 1.5 %collective-permute-start.2 = (s32[128]{0:T(128)S(1)}, s32[128]{0:T(128)S(1)}, u32[]{:S(2)}, u32[]{:S(2)}) collective-permute-start(s32[128]{0:T(128)S(1)} %broadcast_in_dim.24.refs_0_), channel_id=1, source_target_pairs={{0,1},{1,0},{2,3},{3,2},{4,5},{5,4},{6,7},{7,6},{8,9},{9,8},{10,11... | collective-permute-start | bytes 1544 | tf_op jit(solution)/shard_map/ppermute | solution.py:304
  33.0 0.0 collective-permute-done.6.refs_5_
  33.0 0.0 collective-permute-done.5.refs_4_
  33.0 0.0 collective-permute-done.4.refs_3_
  33.0 0.0 collective-permute-done.3.refs_2_
  33.0 2.0 %collective-permute-done.2.refs_1_ = s32[128]{0:T(128)S(1)} collective-permute-done((s32[128]{0:T(128)S(1)}, s32[128]{0:T(128)S(1)}, u32[]{:S(2)}, u32[]{:S(2)}) %collective-permute-start.2) | collective-permute-done | bytes 544 | tf_op jit(solution)/shard_map/ppermute | solution.py:304
  35.1 0.5 copy-done.20
  35.6 8.4 %pick_panels.1 = (bf16[8,384,128]{2,1,0:T(8,128)(2,1)}, s32[8]{0:T(128)}) custom-call(s32[1]{0:T(128)} %bitcast.1.where, s32[1]{0:T(128)} %get-tuple-element.32.after, s32[128]{0:T(128)} %copy-done.13, s32[128]{0:T(128)} %copy-done.20, s32[128]{0:T(128)} %copy-done.19, s32[128]{0:T(128)} %copy-done.18, s32[128]{0:T(128)} %copy-done.17, s32[128]{0:T(128)} %copy-done.16, ...), custom_call_target="tpu_custom_call" | custom-call | tf_op jit(solution)/shard_map/pick_panels/pallas_call | solution.py:337
  43.9 5.2 %all-to-all-start = ((bf16[8,384,128]{2,1,0:T(8,128)(2,1)}), bf16[8,384,128]{2,1,0:T(8,128)(2,1)}, u32[]{:S(2)}, u32[]{:S(2)}) async-start(bf16[8,384,128]{2,1,0:T(8,128)(2,1)} %get-tuple-element.35), calls=%async_computation | async-start | bytes 1572864 | tf_op jit(solution)/shard_map/all_to_all | solution.py:354
  49.2 0.6 copy-done.11
  49.8 9.5 %clear_rows.1 = (f32[16,320,8,1,128]{4,3,2,1,0:T(1,128)}, f32[16,64,8,1,128]{4,3,2,1,0:T(1,128)}, s32[1]{0:T(128)}) custom-call(s32[8]{0:T(128)S(1)} %copy-done.11), custom_call_target="tpu_custom_call" | custom-call | tf_op jit(solution)/shard_map/clear_rows/pallas_call | solution.py:362
  59.3 0.0 all-gather.2.cloned.1.call-done.refs_4_
  59.3 0.1 collective-permute-start.10
  59.4 1.1 collective-permute-start.9
  60.5 1.8 %pair_columns.1.xs_ref = bf16[8,256,320]{2,1,0:T(8,128)(2,1)S(1)} custom-call(bf16[128,5120]{1,0:T(8,128)(2,1)S(1)} %copy-done.3), custom_call_target="tpu_custom_call" | custom-call | tf_op jit(solution)/shard_map/pair_columns/pallas_call | solution.py:330
  62.3 14.5 %collective-permute-done.9.refs_3_ = bf16[4,128,640]{2,1,0:T(8,128)(2,1)S(1)} collective-permute-done((bf16[4,128,640]{2,1,0:T(8,128)(2,1)}, bf16[4,128,640]{2,1,0:T(8,128)(2,1)S(1)}, u32[]{:S(2)}, u32[]{:S(2)}) %collective-permute-start.9) | collective-permute-done | bytes 655392 | tf_op jit(solution)/shard_map/ppermute | solution.py:310
  76.8 0.9 copy-done.7
  77.6 0.0 all-to-all-done.pieces
  77.6 0.0 collective-permute-done.10.refs_5_
  77.6 0.0 copy-start.10
  77.6 1.0 copy-done.10
  78.7 3.2 %adapter.1 = (bf16[8,384,128]{2,1,0:T(8,128)(2,1)S(1)}, f32[128,1024]{1,0:T(8,128)S(1)}) custom-call(bf16[8,256,320]{2,1,0:T(8,128)(2,1)S(1)} %pair_columns.1.xs_ref, bf16[128,1024]{1,0:T(8,128)(2,1)S(1)} %copy-done.10, bf16[8,384,128]{2,1,0:T(8,128)(2,1)} %all-to-all-done.pieces, s32[1]{0:T(128)} %get-tuple-element.36._), custom_call_target="tpu_custom_call" | custom-call | tf_op jit(solution)/shard_map/adapter/pallas_call | solution.py:372
  81.9 0.0 copy-start.9
  81.9 0.0 copy-start.12
  81.9 25.8 %all_to_all.10.rest_0_ = bf16[8,384,128]{2,1,0:T(8,128)(2,1)S(1)} all-to-all(bf16[8,384,128]{2,1,0:T(8,128)(2,1)S(1)} %get-tuple-element.41.refs_6_), channel_id=1, replica_groups=mesh['parts'=2,'dp'=2,'tensor'=8] {'tensor'}, dimensions={0} | all-to-all | bytes 1572864 | tf_op jit(solution)/shard_map/all_to_all | solution.py:393
  107.7 0.0 collective-permute-start.15
  107.7 0.0 copy-done.4
  107.7 4.0 %frozen_part.1 = (f32[128,512]{1,0:T(8,128)S(1)}, f32[128,512]{1,0:T(8,128)}, f32[128,512]{1,0:T(8,128)}, f32[128,512]{1,0:T(8,128)S(1)}) custom-call(bf16[4,128,640]{2,1,0:T(8,128)(2,1)S(1)} %get-tuple-element.27.refs_0_, bf16[4,128,640]{2,1,0:T(8,128)(2,1)S(1)} %copy-done.6, bf16[4,128,640]{2,1,0:T(8,128)(2,1)} %collective-permute-done.refs_2_, ...), custom_call_target="tpu_custom_call" | custom-call | tf_op jit(solution)/shard_map/frozen_part/pallas_call | solution.py:382
  111.8 1.5 %collective-permute-start.11 = (f32[128,512]{1,0:T(8,128)}, f32[128,512]{1,0:T(8,128)S(1)}, u32[]{:S(2)}, u32[]{:S(2)}) collective-permute-start(f32[128,512]{1,0:T(8,128)} %get-tuple-element.43), channel_id=1, source_target_pairs={{0,1},{1,0},{2,3},{3,2},{4,5},{5,4},{6,7},{7,6},{8,9},{9,8},{10,11... | collective-permute-start | bytes 786440 | tf_op jit(solution)/shard_map/ppermute | solution.py:304
  113.2 1.0 collective-permute-start.12
  114.3 1.0 collective-permute-start.13
  115.3 0.0 collective-permute-start.14
  115.3 5.8 %collective-permute-done.11 = f32[128,512]{1,0:T(8,128)S(1)} collective-permute-done((f32[128,512]{1,0:T(8,128)}, f32[128,512]{1,0:T(8,128)S(1)}, u32[]{:S(2)}, u32[]{:S(2)}) %collective-permute-start.11) | collective-permute-done | bytes 262176 | tf_op jit(solution)/shard_map/ppermute | solution.py:304
  121.1 6.4 %collective-permute-done.12 = f32[128,512]{1,0:T(8,128)S(1)} collective-permute-done((f32[128,512]{1,0:T(8,128)}, f32[128,512]{1,0:T(8,128)S(1)}, u32[]{:S(2)}, u32[]{:S(2)}) %collective-permute-start.12) | collective-permute-done | bytes 262176 | tf_op jit(solution)/shard_map/ppermute | solution.py:310
  127.5 0.0 collective-permute-done.13
  127.6 1.8 %fusion = bf16[128,1024]{1,0:T(8,128)(2,1)} fusion(f32[128,1024]{1,0:T(8,128)} %copy-done.9, f32[128,256]{1,0:T(8,128)S(1)} %get-tuple-element.54, f32[128,256]{1,0:T(8,128)S(1)} %get-tuple-element.53, f32[128,256]{1,0:T(8,128)S(1)} %get-tuple-element.52, f32[128,256]{1,0:T(8,128)S(1)} %get-tuple-element.51), kind=kLoop, calls=%fused_computation.1 | loop fusion | flops 655360 | bytes 1310720 | tf_op jit(solution)/shard_map/convert_element_type | solution.py:429
  129.4 0.0 collective-permute-done.14.rows_core
  129.4 0.0 collective-permute-done.15.rest_1_
  129.4 4.0 %place_rows.1 = (f32[16,320,8,1,128]{4,3,2,1,0:T(1,128)}, f32[16,64,8,1,128]{4,3,2,1,0:T(1,128)}) custom-call(s32[1]{0:T(128)} %bitcast.3.first_row, s32[8]{0:T(128)S(1)} %copy-done.12, s32[8]{0:T(128)S(1)} %collective-permute-done.14.rows_core, bf16[8,384,128]{2,1,0:T(8,128)(2,1)S(1)} %all_to_all.10.rest_0_, ...), custom_call_target="tpu_custom_call", output_to_operand_aliasing={{0}: (5, {}), {1}: (6, {})} | custom-call | tf_op jit(solution)/shard_map/place_rows/pallas_call | solution.py:396
  133.4 0.0 copy-done.1
  (30 shorter events, 0.2 us)
Async XLA Ops:
  7.2 1.1 copy-start
  7.2 52.1 %all-gather.2.cloned.1.call-start = ((), (), s32[]{:S(2)}) async-start(), calls=%async_computation.2 | async-start | bytes 1638400 | tf_op jit(solution)/shard_map/all_gather | solution.py:318
  9.1 1.3 copy-start.2
  10.9 17.9 %collective-permute-start = (bf16[4,128,640]{2,1,0:T(8,128)(2,1)S(1)}, bf16[4,128,640]{2,1,0:T(8,128)(2,1)}, u32[]{:S(2)}, u32[]{:S(2)}) collective-permute-start(bf16[4,128,640]{2,1,0:T(8,128)(2,1)S(1)} %get-tuple-element.29), channel_id=1, source_target_pairs={{0,1},{1,0},{2,3},{3,2},{4,5},{5,4},{6,7},{7,6},{8,9},{9,8},{10,11... | collective-permute-start | bytes 1966088 | tf_op jit(solution)/shard_map/ppermute | solution.py:304
  13.9 16.7 %collective-permute-start.1 = (bf16[4,128,640]{2,1,0:T(8,128)(2,1)S(1)}, bf16[4,128,640]{2,1,0:T(8,128)(2,1)S(1)}, u32[]{:S(2)}, u32[]{:S(2)}) collective-permute-start(bf16[4,128,640]{2,1,0:T(8,128)(2,1)S(1)} %get-tuple-element.27.refs_0_), channel_id=1, source_target_pairs={{0,16},{16,0},{1,17},{17,1},{2,18},{18,2},{3,19},{19,3},{4,20},{20... | collective-permute-start | bytes 1966088 | tf_op jit(solution)/shard_map/ppermute | solution.py:310
  18.0 17.0 %copy-start.13 = (s32[128]{0:T(128)}, s32[128]{0:T(128)S(1)}, u32[]{:S(2)}) copy-start(s32[128]{0:T(128)S(1)} %broadcast_in_dim.24.refs_0_) | copy-start | bytes 1540
  18.0 6.3 %collective-permute-start.8 = (s32[128]{0:T(128)S(1)}, s32[128]{0:T(128)S(1)}, u32[]{:S(2)}, u32[]{:S(2)}) collective-permute-start(s32[128]{0:T(128)S(1)} %broadcast_in_dim.24.refs_0_), channel_id=1, source_target_pairs={{0,7},{1,6},{2,5},{3,4},{4,3},{5,2},{6,1},{7,0},{8,15},{9,14},{10,... | collective-permute-start | bytes 1544 | tf_op jit(solution)/shard_map/ppermute | solution.py:304
  21.6 5.3 %collective-permute-start.7 = (s32[128]{0:T(128)S(1)}, s32[128]{0:T(128)S(1)}, u32[]{:S(2)}, u32[]{:S(2)}) collective-permute-start(s32[128]{0:T(128)S(1)} %broadcast_in_dim.24.refs_0_), channel_id=1, source_target_pairs={{0,6},{1,7},{2,4},{3,5},{4,2},{5,3},{6,0},{7,1},{8,14},{9,15},{10,... | collective-permute-start | bytes 1544 | tf_op jit(solution)/shard_map/ppermute | solution.py:304
  21.9 11.1 %collective-permute-start.6 = (s32[128]{0:T(128)S(1)}, s32[128]{0:T(128)S(1)}, u32[]{:S(2)}, u32[]{:S(2)}) collective-permute-start(s32[128]{0:T(128)S(1)} %broadcast_in_dim.24.refs_0_), channel_id=1, source_target_pairs={{0,5},{1,4},{2,7},{3,6},{4,1},{5,0},{6,3},{7,2},{8,13},{9,12},{10,... | collective-permute-start | bytes 1544 | tf_op jit(solution)/shard_map/ppermute | solution.py:304
  24.3 10.7 %copy-start.14 = (s32[128]{0:T(128)}, s32[128]{0:T(128)S(1)}, u32[]{:S(2)}) copy-start(s32[128]{0:T(128)S(1)} %collective-permute-done.8.refs_7_) | copy-start | bytes 1540
  24.3 8.7 %collective-permute-start.5 = (s32[128]{0:T(128)S(1)}, s32[128]{0:T(128)S(1)}, u32[]{:S(2)}, u32[]{:S(2)}) collective-permute-start(s32[128]{0:T(128)S(1)} %broadcast_in_dim.24.refs_0_), channel_id=1, source_target_pairs={{0,4},{1,5},{2,6},{3,7},{4,0},{5,1},{6,2},{7,3},{8,12},{9,13},{10,... | collective-permute-start | bytes 1544 | tf_op jit(solution)/shard_map/ppermute | solution.py:304
  27.0 8.0 %copy-start.15 = (s32[128]{0:T(128)}, s32[128]{0:T(128)S(1)}, u32[]{:S(2)}) copy-start(s32[128]{0:T(128)S(1)} %collective-permute-done.7.refs_6_) | copy-start | bytes 1540
  27.0 6.0 %collective-permute-start.4 = (s32[128]{0:T(128)S(1)}, s32[128]{0:T(128)S(1)}, u32[]{:S(2)}, u32[]{:S(2)}) collective-permute-start(s32[128]{0:T(128)S(1)} %broadcast_in_dim.24.refs_0_), channel_id=1, source_target_pairs={{0,3},{1,2},{2,1},{3,0},{4,7},{5,6},{6,5},{7,4},{8,11},{9,10},{10,... | collective-permute-start | bytes 1544 | tf_op jit(solution)/shard_map/ppermute | solution.py:304
  28.8 4.2 %collective-permute-start.3 = (s32[128]{0:T(128)S(1)}, s32[128]{0:T(128)S(1)}, u32[]{:S(2)}, u32[]{:S(2)}) collective-permute-start(s32[128]{0:T(128)S(1)} %broadcast_in_dim.24.refs_0_), channel_id=1, source_target_pairs={{0,2},{1,3},{2,0},{3,1},{4,6},{5,7},{6,4},{7,5},{8,10},{9,11},{10,... | collective-permute-start | bytes 1544 | tf_op jit(solution)/shard_map/ppermute | solution.py:304
  30.6 0.9 copy-start.5
  31.5 3.5 %collective-permute-start.2 = (s32[128]{0:T(128)S(1)}, s32[128]{0:T(128)S(1)}, u32[]{:S(2)}, u32[]{:S(2)}) collective-permute-start(s32[128]{0:T(128)S(1)} %broadcast_in_dim.24.refs_0_), channel_id=1, source_target_pairs={{0,1},{1,0},{2,3},{3,2},{4,5},{5,4},{6,7},{7,6},{8,9},{9,8},{10,11... | collective-permute-start | bytes 1544 | tf_op jit(solution)/shard_map/ppermute | solution.py:304
  33.0 2.1 %copy-start.16 = (s32[128]{0:T(128)}, s32[128]{0:T(128)S(1)}, u32[]{:S(2)}) copy-start(s32[128]{0:T(128)S(1)} %collective-permute-done.6.refs_5_) | copy-start | bytes 1540
  33.0 2.1 %copy-start.17 = (s32[128]{0:T(128)}, s32[128]{0:T(128)S(1)}, u32[]{:S(2)}) copy-start(s32[128]{0:T(128)S(1)} %collective-permute-done.5.refs_4_) | copy-start | bytes 1540
  33.0 2.1 %copy-start.18 = (s32[128]{0:T(128)}, s32[128]{0:T(128)S(1)}, u32[]{:S(2)}) copy-start(s32[128]{0:T(128)S(1)} %collective-permute-done.4.refs_3_) | copy-start | bytes 1540
  33.0 2.0 %copy-start.19 = (s32[128]{0:T(128)}, s32[128]{0:T(128)S(1)}, u32[]{:S(2)}) copy-start(s32[128]{0:T(128)S(1)} %collective-permute-done.3.refs_2_) | copy-start | bytes 1540
  35.0 0.5 copy-start.20
  35.6 24.9 %copy-start.3 = (bf16[128,5120]{1,0:T(8,128)(2,1)S(1)}, bf16[128,5120]{1,0:T(8,128)(2,1)}, u32[]{:S(2)}) copy-start(bf16[128,5120]{1,0:T(8,128)(2,1)} %x_ref.3) | copy-start | bytes 3932164
  43.9 33.7 %all-to-all-start = ((bf16[8,384,128]{2,1,0:T(8,128)(2,1)}), bf16[8,384,128]{2,1,0:T(8,128)(2,1)}, u32[]{:S(2)}, u32[]{:S(2)}) async-start(bf16[8,384,128]{2,1,0:T(8,128)(2,1)} %get-tuple-element.35), calls=%async_computation | async-start | bytes 1572864 | tf_op jit(solution)/shard_map/all_to_all | solution.py:354
  49.2 0.6 copy-start.11
  59.3 18.3 %collective-permute-start.10 = (bf16[2560,256]{1,0:T(8,128)(2,1)}, bf16[2560,256]{1,0:T(8,128)(2,1)}, u32[]{:S(2)}, u32[]{:S(2)}) collective-permute-start(bf16[2560,256]{1,0:T(8,128)(2,1)} %all-gather.2.cloned.1.call-done.refs_4_), channel_id=1, source_target_pairs={{0,8},{8,0},{1,9},{9,1},{2,10},{10,2},{3,11},{11,3},{4,12},{12,4},... | collective-permute-start | bytes 3932168 | tf_op jit(solution)/shard_map/ppermute | solution.py:307
  59.4 17.4 %collective-permute-start.9 = (bf16[4,128,640]{2,1,0:T(8,128)(2,1)}, bf16[4,128,640]{2,1,0:T(8,128)(2,1)S(1)}, u32[]{:S(2)}, u32[]{:S(2)}) collective-permute-start(bf16[4,128,640]{2,1,0:T(8,128)(2,1)} %collective-permute-done.refs_2_), channel_id=1, source_target_pairs={{0,16},{16,0},{1,17},{17,1},{2,18},{18,2},{3,19},{19,3},{4,20},{20... | collective-permute-start | bytes 1966088 | tf_op jit(solution)/shard_map/ppermute | solution.py:310
  62.3 45.4 %copy-start.4 = (bf16[2560,256]{1,0:T(8,128)(2,1)S(1)}, bf16[2560,256]{1,0:T(8,128)(2,1)}, u32[]{:S(2)}) copy-start(bf16[2560,256]{1,0:T(8,128)(2,1)} %all-gather.2.cloned.1.call-done.refs_4_) | copy-start | bytes 3932164
  76.7 0.9 copy-start.7
  77.6 30.1 %copy-start.6 = (bf16[4,128,640]{2,1,0:T(8,128)(2,1)S(1)}, bf16[4,128,640]{2,1,0:T(8,128)(2,1)}, u32[]{:S(2)}) copy-start(bf16[4,128,640]{2,1,0:T(8,128)(2,1)} %copy-done.5) | copy-start | bytes 1966084
  77.6 30.1 %copy-start.8 = (bf16[4,128,640]{2,1,0:T(8,128)(2,1)S(1)}, bf16[4,128,640]{2,1,0:T(8,128)(2,1)}, u32[]{:S(2)}) copy-start(bf16[4,128,640]{2,1,0:T(8,128)(2,1)} %copy-done.7) | copy-start | bytes 1966084
  77.6 1.1 copy-start.10
  81.9 29.9 %copy-start.9 = (f32[128,1024]{1,0:T(8,128)}, f32[128,1024]{1,0:T(8,128)S(1)}, u32[]{:S(2)}) copy-start(f32[128,1024]{1,0:T(8,128)S(1)} %get-tuple-element.46) | copy-start | bytes 1572868
  81.9 33.3 %copy-start.12 = (s32[8]{0:T(128)S(1)}, s32[8]{0:T(128)}, u32[]{:S(2)}) copy-start(s32[8]{0:T(128)} %get-tuple-element.33.after_ref.rows_here) | copy-start | bytes 100
  107.7 21.7 %collective-permute-start.15 = (bf16[8,384,128]{2,1,0:T(8,128)(2,1)S(1)}, bf16[8,384,128]{2,1,0:T(8,128)(2,1)}, u32[]{:S(2)}, u32[]{:S(2)}) collective-permute-start(bf16[8,384,128]{2,1,0:T(8,128)(2,1)S(1)} %all_to_all.10.rest_0_), channel_id=1, source_target_pairs={{0,8},{8,0},{1,9},{9,1},{2,10},{10,2},{3,11},{11,3},{4,12},{12,4},... | collective-permute-start | bytes 2359304 | tf_op jit(solution)/shard_map/ppermute | solution.py:307
  111.8 9.3 %collective-permute-start.11 = (f32[128,512]{1,0:T(8,128)}, f32[128,512]{1,0:T(8,128)S(1)}, u32[]{:S(2)}, u32[]{:S(2)}) collective-permute-start(f32[128,512]{1,0:T(8,128)} %get-tuple-element.43), channel_id=1, source_target_pairs={{0,1},{1,0},{2,3},{3,2},{4,5},{5,4},{6,7},{7,6},{8,9},{9,8},{10,11... | collective-permute-start | bytes 786440 | tf_op jit(solution)/shard_map/ppermute | solution.py:304
  113.2 14.3 %collective-permute-start.12 = (f32[128,512]{1,0:T(8,128)}, f32[128,512]{1,0:T(8,128)S(1)}, u32[]{:S(2)}, u32[]{:S(2)}) collective-permute-start(f32[128,512]{1,0:T(8,128)} %get-tuple-element.44), channel_id=1, source_target_pairs={{0,16},{16,0},{1,17},{17,1},{2,18},{18,2},{3,19},{19,3},{4,20},{20... | collective-permute-start | bytes 786440 | tf_op jit(solution)/shard_map/ppermute | solution.py:310
  114.3 13.2 %collective-permute-start.13 = (f32[128,512]{1,0:T(8,128)S(1)}, f32[128,512]{1,0:T(8,128)S(1)}, u32[]{:S(2)}, u32[]{:S(2)}) collective-permute-start(f32[128,512]{1,0:T(8,128)S(1)} %get-tuple-element.45), channel_id=1, source_target_pairs={{0,17},{1,16},{2,19},{3,18},{4,21},{5,20},{6,23},{7,22},{16,1},{17... | collective-permute-start | bytes 786440 | tf_op jit(solution)/shard_map/ppermute | solution.py:392
  115.3 14.1 %collective-permute-start.14 = (s32[8]{0:T(128)S(1)}, s32[8]{0:T(128)S(1)}, u32[]{:S(2)}, u32[]{:S(2)}) collective-permute-start(s32[8]{0:T(128)S(1)} %copy-done.12), channel_id=1, source_target_pairs={{0,8},{8,0},{1,9},{9,1},{2,10},{10,2},{3,11},{11,3},{4,12},{12,4},... | collective-permute-start | bytes 104 | tf_op jit(solution)/shard_map/ppermute | solution.py:307
  129.4 4.1 %copy-start.1 = (bf16[640,512]{1,0:T(8,128)(2,1)S(1)}, bf16[640,512]{1,0:T(8,128)(2,1)}, u32[]{:S(2)}) copy-start(bf16[640,512]{1,0:T(8,128)(2,1)} %param.9) | copy-start | bytes 1966084
Sparse Core Ops, SparseCore 0:
  9.6 35.4 all-gather.1

commit v7 on v6

--- a/solution.py
+++ b/solution.py
@@ -12,7 +12,7 @@
 R = 64
 ADAPTERS = 256
 LANES = 128
-GROUP_ROWS = 16
+TILE_ROWS = 8
 
 adapter_scale = 2.0
 VMEM = pl.BlockSpec(memory_space=pltpu.VMEM)
@@ -20,6 +20,10 @@
 ANY = pl.BlockSpec(memory_space=pl.ANY)
 LIMIT = pltpu.CompilerParams(vmem_limit_bytes=16 * 1024 * 1024)
 WIDE = pltpu.CompilerParams(vmem_limit_bytes=60 * 1024 * 1024)
+
+
+def cost(flops=0, read=0):
+    return pl.CostEstimate(flops=flops, bytes_accessed=read, transcendentals=0)
 
 
 def dot(a, b):
@@ -119,55 +123,42 @@
         xs_ref[k, rows:] = dot(x, odd).astype(jnp.bfloat16)
 
 
-def gather_kernel(count, down_chunks, up_chunks, where, after, *refs):
+def gather_kernel(after, asked, down_ref, up_ref, out_ref, rows_ref, down_buf, up_buf, flat, built, sems):
     del after
-    asked, (down_ref, up_ref, out_ref, rows_ref) = refs[:count], refs[count:count + 4]
-    down_buf, up_buf, flat, built, rows, sems, row_sem = refs[count + 4:]
-    me = where[0]
+    count, down_chunks, up_chunks = down_buf.shape[0], down_buf.shape[1], up_buf.shape[1]
     across = up_chunks // 8
-    for s in range(count):
-        pltpu.make_async_copy(asked[s], rows.at[s], row_sem).start()
-    for s in range(count):
-        pltpu.make_async_copy(asked[s], rows.at[s], row_sem).wait()
-
-    def copies(s):
-        start = pl.multiple_of((rows[s, 0] // GROUP_ROWS) * GROUP_ROWS, GROUP_ROWS)
+
+    def copies(t):
+        tile = asked[t, 0] // TILE_ROWS
         return (
-            pltpu.make_async_copy(down_ref.at[pl.ds(start, GROUP_ROWS)], down_buf.at[s], sems.at[0, s]),
-            pltpu.make_async_copy(up_ref.at[pl.ds(start, GROUP_ROWS)], up_buf.at[s], sems.at[1, s]),
-            pltpu.make_async_copy(built.at[s], out_ref.at[me ^ s], sems.at[2, s]),
+            pltpu.make_async_copy(down_ref.at[tile], down_buf.at[t], sems.at[0, t]),
+            pltpu.make_async_copy(up_ref.at[tile], up_buf.at[t], sems.at[1, t]),
+            pltpu.make_async_copy(built.at[t], out_ref.at[t], sems.at[2, t]),
         )
 
-    for s in range(count):
-        down, up, _ = copies(s)
+    for t in range(count):
+        down, up, _ = copies(t)
         down.start()
         up.start()
-        rows_ref[me ^ s] = rows[s, 0]
-
-    def one(s, carry):
-        row = rows[s, 0] % GROUP_ROWS
-        upper = row >= 8
-        sub = row % 8
-
-        def pick(buf, lane):
-            tile = buf[s, :, lane:lane + LANES].astype(jnp.float32)
-            return jnp.where(upper, tile[8:], tile[:8])
-
-        down, up, leave = copies(s)
+        rows_ref[t] = asked[t, 0]
+
+    def one(t, carry):
+        down, up, leave = copies(t)
         up.wait()
         for j in range(up_chunks):
             place = down_chunks + (j % across) * 8 + j // across
-            flat[place * 8:place * 8 + 8, :] = pick(up_buf, j * LANES)
+            flat[place * 8:place * 8 + 8, :] = up_buf[t, j].astype(jnp.float32)
         down.wait()
         for j in range(down_chunks):
-            flat[j * 8:j * 8 + 8, :] = pick(down_buf, j * LANES)
-        built[s] = flat[pl.ds(sub, down_chunks + up_chunks, stride=8), :].astype(jnp.bfloat16)
+            flat[j * 8:j * 8 + 8, :] = down_buf[t, j].astype(jnp.float32)
+        sub = asked[t, 0] % TILE_ROWS
+        built[t] = flat[pl.ds(sub, down_chunks + up_chunks, stride=8), :].astype(jnp.bfloat16)
         leave.start()
         return carry
 
     lax.fori_loop(0, count, one, 0)
-    for s in range(count):
-        copies(s)[2].wait()
+    for t in range(count):
+        copies(t)[2].wait()
 
 
 def zero_kernel(after_ref, down_ref, up_ref, done_ref, zeros, sems):
@@ -277,15 +268,15 @@
                 copy.wait()
 
 
-def base_kernel(*refs):
-    x_refs, w_refs, out_refs = refs[:4], refs[4:6], refs[-4:]
-    outer, rows, depth = x_refs[0].shape
-    width = w_refs[0].shape[1]
-    for h, w_ref in enumerate(w_refs):
+def base_kernel(where, *refs):
+    x_refs, out_refs = refs[:4], refs[-4:]
+    outer, rows, _ = x_refs[0].shape
+    width = refs[4].shape[1]
+    for h in range(2):
         total = 0.0
         for k in range(outer):
-            left = jnp.concatenate([ref[k] for ref in x_refs], axis=0)
-            total += dot(left, w_ref[k * depth:(k + 1) * depth, :])
+            left = jnp.concatenate([ref[where[0] ^ k] for ref in x_refs], axis=0)
+            total += dot(left, refs[4 + h * outer + k][...])
         for b, ref in enumerate(out_refs):
             ref[:, h * width:(h + 1) * width] = total[b * rows:(b + 1) * rows]
 
@@ -298,7 +289,7 @@
     down_chunks = down_store.shape[1] // LANES
     up_chunks = up_store.shape[1] // LANES
     me, part, core = lax.axis_index("tensor"), lax.axis_index("parts"), lax.axis_index("dp")
-    x = me % 2
+    z, x = me // 2, me % 2
 
     def exchange(value, s):
         return lax.ppermute(value, "tensor", [(t, t ^ s) for t in range(group)])
@@ -309,13 +300,12 @@
     def other_part(value):
         return lax.ppermute(value, "parts", [(a, parts - 1 - a) for a in range(parts)])
 
-    row = jnp.broadcast_to(store_rows(block_adapter, adapter_slot), (LANES,))
-    asked = [row] + [exchange(row, s) for s in range(1, group)]
+    row = store_rows(block_adapter, adapter_slot)
+    asked = lax.all_to_all(jnp.broadcast_to(row, (group, LANES)), "tensor", 0, 0)
 
     width = frozen_value.shape[1] // parts
     half = lax.dynamic_slice_in_dim(frozen_value, part * width, width, axis=1)
-    lines = [list(range(0, group, 2)), list(range(1, group, 2))]
-    half = lax.all_gather(half, "tensor", axis_index_groups=lines, axis=0, tiled=True)
+    quarter = [half] + [exchange(half, 2 * k) for k in range(1, outer)]
 
     block = jax.ShapeDtypeStruct((outer, token_rows, slice_width), jnp.bfloat16)
     token = jax.ShapeDtypeStruct((1,), jnp.int32)
@@ -325,35 +315,38 @@
     )(x[None], tokens)
     x_far = exchange(x_theirs, 1)
     y_mine = other_part(x_mine)
-    split, x_far, y_mine = lax.optimization_barrier((split, x_far, y_mine))
-
     xs = pl.pallas_call(
         interleave_kernel,
         out_shape=jax.ShapeDtypeStruct((group, 2 * token_rows, slice_width // 2), jnp.bfloat16),
         in_specs=[VMEM], out_specs=VMEM, name="pair_columns", compiler_params=LIMIT,
+        cost_estimate=cost(flops=2 << 30, read=4 << 20),
     )(tokens)
 
+    split, x_far, y_mine, xs = lax.optimization_barrier((split, x_far, y_mine, xs))
     pieces = jax.ShapeDtypeStruct((group, down_chunks + up_chunks, LANES), jnp.bfloat16)
+    def tiles(store):
+        view = store.reshape(store.shape[0] // TILE_ROWS, TILE_ROWS, store.shape[1] // LANES, LANES)
+        return view.transpose(0, 2, 1, 3)
+
     sent, rows = pl.pallas_call(
-        functools.partial(gather_kernel, group, down_chunks, up_chunks),
+        gather_kernel,
         out_shape=(pieces, jax.ShapeDtypeStruct((group,), jnp.int32)),
-        in_specs=[SMEM, SMEM] + [ANY] * (group + 2),
+        in_specs=[SMEM, SMEM, ANY, ANY],
         out_specs=(ANY, SMEM),
         scratch_shapes=[
-            pltpu.VMEM((group, GROUP_ROWS, down_store.shape[1]), jnp.bfloat16),
-            pltpu.VMEM((group, GROUP_ROWS, up_store.shape[1]), jnp.bfloat16),
+            pltpu.VMEM((group, down_chunks, TILE_ROWS, LANES), jnp.bfloat16),
+            pltpu.VMEM((group, up_chunks, TILE_ROWS, LANES), jnp.bfloat16),
             pltpu.VMEM(((down_chunks + up_chunks) * 8, LANES), jnp.float32),
             pltpu.VMEM(pieces.shape, jnp.bfloat16),
-            pltpu.SMEM((group, LANES), jnp.int32),
             pltpu.SemaphoreType.DMA((3, group)),
-            pltpu.SemaphoreType.DMA(()),
         ],
         compiler_params=WIDE,
+        cost_estimate=cost(read=40 << 20),
         name="pick_panels",
-    )(me[None], split, *asked, down_store, up_store)
+    )(split, asked, tiles(down_store), tiles(up_store))
     panels = lax.all_to_all(sent, "tensor", 0, 0)
     rows_core = other_core(rows)
-    x_far, _ = lax.optimization_barrier((x_far, rows))
+    x_far, quarter, _ = lax.optimization_barrier((x_far, quarter, rows))
     y_far = other_part(x_far)
 
     owned_groups = ADAPTERS // lax.axis_size("dp") // 8
@@ -363,11 +356,10 @@
         zero_kernel, out_shape=(down_shape, up_shape, token),
         in_specs=[SMEM], out_specs=(ANY, ANY, SMEM),
         scratch_shapes=[pltpu.VMEM((up_chunks, 8, 1, LANES), jnp.float32), pltpu.SemaphoreType.DMA((2,))],
-        compiler_params=LIMIT, name="clear_rows",
+        compiler_params=LIMIT, cost_estimate=cost(read=28 << 20), name="clear_rows",
     )(rows)
-    half, _ = lax.optimization_barrier((half, cleared))
-    half_core = other_core(half)
-    panels, y_far, half_core = lax.optimization_barrier((panels, y_far, half_core))
+    quarter_core = [other_core(w) for w in quarter]
+    panels, y_far, quarter_core = lax.optimization_barrier((panels, y_far, quarter_core))
 
     terms, lifted = pl.pallas_call(
         functools.partial(adapter_kernel, group, down_chunks),
@@ -376,21 +368,22 @@
         out_specs=(VMEM, VMEM),
         scratch_shapes=[pltpu.VMEM((2 * R, VALUE_OUTPUTS), jnp.float32)],
         compiler_params=LIMIT,
+        cost_estimate=cost(flops=3 << 30, read=8 << 20),
         name="adapter",
     )(xs, cotangent, panels, cleared)
     sums = jax.ShapeDtypeStruct((token_rows, parts * width), jnp.float32)
     own, to_part, to_inner, to_both = pl.pallas_call(
         base_kernel,
         out_shape=[sums] * 4,
-        in_specs=[VMEM] * 6 + [ANY],
+        in_specs=[SMEM] + [VMEM] * (4 + 2 * outer) + [ANY],
         out_specs=[VMEM] * 4,
         compiler_params=LIMIT,
+        cost_estimate=cost(flops=4 << 30, read=8 << 20),
         name="frozen_part",
-    )(x_mine, y_mine, x_far, y_far, half, half_core, terms)
+    )(z[None], x_mine, y_mine, x_far, y_far, *quarter, *quarter_core, terms)
     opposite = [(a * group + t, (parts - 1 - a) * group + (t ^ 1)) for a in range(parts) for t in range(group)]
-    kept = own + exchange(to_inner, 1)
-    got = other_part(to_part) + lax.ppermute(to_both, ("parts", "tensor"), opposite)
     back = lax.all_to_all(terms, "tensor", 0, 0)
+    back, own = lax.optimization_barrier((back, own))
     back_core = other_core(back)
 
     grad_down, grad_up = pl.pallas_call(
@@ -408,12 +401,15 @@
             pltpu.SemaphoreType.DMA(()),
         ],
         compiler_params=LIMIT,
+        cost_estimate=cost(read=16 << 20),
         name="place_rows",
     )((core * (ADAPTERS // lax.axis_size("dp")))[None], rows, rows_core, back, back_core,
       down_zero, up_zero)
     grad_down = grad_down.reshape(owned_groups, down_chunks, 8, LANES).transpose(0, 2, 1, 3)
     grad_up = grad_up.reshape(owned_groups, up_chunks, 8, LANES).transpose(0, 2, 1, 3)
 
+    kept = own + exchange(to_inner, 1)
+    got = other_part(to_part) + lax.ppermute(to_both, ("parts", "tensor"), opposite)
     quarters = [[c[:, :width], c[:, width:]] for c in (kept, got)]
 
     def pick_quarter(c, a):

time: 142 us -> 152 us (1.070)
  waiting for transfers between devices: 30.9 us -> 65.7 us
  blocking collectives: 25.8 us -> 0 us
  local copies, waits for them, and re-layouts: 7.61 us -> 24.3 us
  between operations: 15 us -> 1.66 us
  Pallas kernels: 31.5 us -> 28.6 us
  starting transfers between devices: 26.3 us -> 28.5 us
    ppermute x9 -> x5, waiting for transfers between devices: 10.1 us -> 45 us  [exchange(): return lax.ppermute(value, 'tensor', [(t, t ^ s) for t in range(group)])]
    all_to_all x1 -> x0, blocking collectives: 25.8 us -> none  [fast_body(): back = lax.all_to_all(terms, 'tensor', 0, 0)]
    unnamed x42 -> x62, local copies, waits for them, and re-layouts: 6.27 us -> 23 us
    ppermute x3, waiting for transfers between devices: 20.8 us -> 12.3 us  [other_part(): lax.ppermute(value, 'parts', [(a, parts - 1 - a) for a in range(parts)])]
    all_to_all x0 -> x2, waiting for transfers between devices: none -> 8.44 us  [the longest x1 8.44 us: fast_body(): back = lax.all_to_all(terms, 'tensor', 0, 0)]
    all_to_all x0 -> x2, starting transfers between devices: none -> 8.43 us  [the longest x1 4.88 us: fast_body(): lax.all_to_all(jnp.broadcast_to(row, (group, LANES)), 'tensor', 0, 0)]
    ppermute x9 -> x5, starting transfers between devices: 16.3 us -> 8.12 us  [exchange(): return lax.ppermute(value, 'tensor', [(t, t ^ s) for t in range(group)])]
    pallas_call x2, Pallas kernels: 12.4 us -> 7.55 us  [the longest x1 5.76 us: fast_body(): pl.pallas_call(gather_kernel, out_shape=(pieces, jax.ShapeDtypeStruct((gr...]
  transfers between devices with their start and end apart: 18 -> 18, of which waited for: 7 -> 7; matrix products, arithmetic and copies ran while one was open for 3% -> 2% of each run, Pallas kernels for 17% -> 9%
where the time goes in v7:
time: 152 us; the launch traced here: 151 us
  waiting for transfers between devices  65.7 us (43%)
  Pallas kernels  28.6 us (19%)
  starting transfers between devices  28.5 us (19%)
  local copies, waits for them, and re-layouts  24.3 us (16%)
  other arithmetic  2.27 us (1%)
  between operations  1.66 us (1%)
    ppermute x5, waiting for transfers between devices, exchange(): return lax.ppermute(value, 'tensor', [(t, t ^ s) for t in range(group)])  45 us
    unnamed x62, local copies, waits for them, and re-layouts  23 us
    ppermute x3, waiting for transfers between devices, other_part(): lax.ppermute(value, 'parts', [(a, parts - 1 - a) for a in range(parts)])  12.3 us
    pallas_call x1, Pallas kernels, fast_body(): pl.pallas_call(zero_kernel, out_shape=(down_shape, up_shape, token), in_s...  9.48 us
    all_to_all x1, waiting for transfers between devices, fast_body(): back = lax.all_to_all(terms, 'tensor', 0, 0)  8.44 us
    ppermute x5, starting transfers between devices, exchange(): return lax.ppermute(value, 'tensor', [(t, t ^ s) for t in range(group)])  8.12 us
    pallas_call x1, Pallas kernels, fast_body(): pl.pallas_call(gather_kernel, out_shape=(pieces, jax.ShapeDtypeStruct((gr...  5.76 us
    pallas_call x1, Pallas kernels, fast_body(): pl.pallas_call(functools.partial(scatter_kernel, 2 * group, down_chunks,...  5.76 us
  transfers between devices with their start and end apart: 18, of which 7 were waited for; matrix products, arithmetic and copies ran while one was open for 2% of the time, Pallas kernels for 9%

profile of v7, /device:TPU:0, one launch (start us, length us, event | category | flops | bytes accessed | tf_op | source)
XLA Modules:
  0.0 151.0 jit_solution(3534353618288391211)
XLA Ops:
  0.6 0.0 copy-start
  0.7 0.0 copy-start.2
  0.7 1.4 copy-done.2
  2.0 0.9 split_tokens.1
  3.0 3.0 %collective-permute-start = (bf16[4,128,640]{2,1,0:T(8,128)(2,1)}, bf16[4,128,640]{2,1,0:T(8,128)(2,1)S(1)}, u32[]{:S(2)}, u32[]{:S(2)}) collective-permute-start(bf16[4,128,640]{2,1,0:T(8,128)(2,1)} %get-tuple-element.37), channel_id=1, source_target_pairs={{0,1},{1,0},{2,3},{3,2},{4,5},{5,4},{6,7},{7,6},{8,9},{9,8},{10,11... | collective-permute-start | bytes 1966088 | tf_op jit(solution)/shard_map/ppermute | solution.py:295
  6.0 1.5 %collective-permute-start.1 = (bf16[4,128,640]{2,1,0:T(8,128)(2,1)S(1)}, bf16[4,128,640]{2,1,0:T(8,128)(2,1)S(1)}, u32[]{:S(2)}, u32[]{:S(2)}) collective-permute-start(bf16[4,128,640]{2,1,0:T(8,128)(2,1)S(1)} %get-tuple-element.38.refs_0_), channel_id=1, source_target_pairs={{0,16},{16,0},{1,17},{17,1},{2,18},{18,2},{3,19},{19,3},{4,20},{20... | collective-permute-start | bytes 1966088 | tf_op jit(solution)/shard_map/ppermute | solution.py:301
  8.2 1.4 fusion.1
  9.6 1.3 broadcast_in_dim.23
  10.8 4.9 %all-to-all-start = ((s32[8,1,128]{2,1,0:T(1,128)}), s32[8,1,128]{2,1,0:T(1,128)S(1)}, u32[]{:S(2)}, u32[]{:S(2)}) async-start(s32[8,1,128]{2,1,0:T(1,128)} %broadcast_in_dim.23), calls=%async_computation | async-start | bytes 8192 | tf_op jit(solution)/shard_map/all_to_all | solution.py:304
  15.7 1.3 copy-done.3
  17.0 1.8 %pair_columns.1.xs_ref = bf16[8,256,320]{2,1,0:T(8,128)(2,1)S(1)} custom-call(bf16[128,5120]{1,0:T(8,128)(2,1)S(1)} %copy-done.3), custom_call_target="tpu_custom_call" | custom-call | flops 2147483648 | bytes 4194304 | tf_op jit(solution)/shard_map/pair_columns/pallas_call | solution.py:318
  18.8 1.2 copy-done.28
  20.0 1.0 collective-permute-done.refs_2_
  21.0 1.2 collective-permute-done.1.refs_1_
  22.2 0.6 copy-done.30
  22.8 5.8 %pick_panels.1 = (bf16[8,384,128]{2,1,0:T(8,128)(2,1)}, s32[8]{0:T(128)}) custom-call(s32[1]{0:T(128)} %get-tuple-element.40.after, s32[8,128]{1,0:T(8,128)} %bitcast.26, bf16[32,320,8,128]{3,2,1,0:T(8,128)(2,1)} %bitcast.22, bf16[32,64,8,128]{3,2,1,0:T(8,128)(2,1)} %bitcast.24), custom_call_target="tpu_custom_call" | custom-call | bytes 41943040 | tf_op jit(solution)/shard_map/pick_panels/pallas_call | solution.py:331
  28.6 5.0 %all-to-all-start.1 = ((bf16[8,384,128]{2,1,0:T(8,128)(2,1)}), bf16[8,384,128]{2,1,0:T(8,128)(2,1)S(1)}, u32[]{:S(2)}, u32[]{:S(2)}) async-start(bf16[8,384,128]{2,1,0:T(8,128)(2,1)} %get-tuple-element.41), calls=%async_computation.1 | async-start | bytes 1572864 | tf_op jit(solution)/shard_map/all_to_all | solution.py:347
  33.6 3.9 %collective-permute-start.4 = (bf16[640,256]{1,0:T(8,128)(2,1)S(1)}, bf16[640,256]{1,0:T(8,128)(2,1)S(1)}, u32[]{:S(2)}, u32[]{:S(2)}) collective-permute-start(bf16[640,256]{1,0:T(8,128)(2,1)S(1)} %constant_dynamic-slice_fusion.refs_4_), channel_id=1, source_target_pairs={{0,6},{1,7},{2,4},{3,5},{4,2},{5,3},{6,0},{7,1},{8,14},{9,15},{10,... | collective-permute-start | bytes 983048 | tf_op jit(solution)/shard_map/ppermute | solution.py:295
  37.5 0.0 collective-permute-start.3
  37.5 0.6 collective-permute-start.2
  38.1 20.8 %collective-permute-done.4.refs_7_ = bf16[640,256]{1,0:T(8,128)(2,1)S(1)} collective-permute-done((bf16[640,256]{1,0:T(8,128)(2,1)S(1)}, bf16[640,256]{1,0:T(8,128)(2,1)S(1)}, u32[]{:S(2)}, u32[]{:S(2)}) %collective-permute-start.4) | collective-permute-done | bytes 327712 | tf_op jit(solution)/shard_map/ppermute | solution.py:295
  58.9 22.0 %collective-permute-done.3.refs_6_ = bf16[640,256]{1,0:T(8,128)(2,1)S(1)} collective-permute-done((bf16[640,256]{1,0:T(8,128)(2,1)S(1)}, bf16[640,256]{1,0:T(8,128)(2,1)S(1)}, u32[]{:S(2)}, u32[]{:S(2)}) %collective-permute-start.3) | collective-permute-done | bytes 327712 | tf_op jit(solution)/shard_map/ppermute | solution.py:295
  80.9 0.0 collective-permute-done.2.refs_5_
  80.9 1.5 %collective-permute-start.5 = (bf16[4,128,640]{2,1,0:T(8,128)(2,1)S(1)}, bf16[4,128,640]{2,1,0:T(8,128)(2,1)S(1)}, u32[]{:S(2)}, u32[]{:S(2)}) collective-permute-start(bf16[4,128,640]{2,1,0:T(8,128)(2,1)S(1)} %collective-permute-done.refs_2_), channel_id=1, source_target_pairs={{0,16},{16,0},{1,17},{17,1},{2,18},{18,2},{3,19},{19,3},{4,20},{20... | collective-permute-start | bytes 1966088 | tf_op jit(solution)/shard_map/ppermute | solution.py:301
  82.5 0.0 collective-permute-start.6
  82.5 0.5 collective-permute-start.7
  83.0 0.7 copy-done.14
  83.7 0.0 collective-permute-start.8
  83.7 0.7 copy-done.12
  84.4 0.5 collective-permute-start.9
  84.9 0.7 copy-done.4
  85.6 9.5 %clear_rows.1 = (f32[16,320,8,1,128]{4,3,2,1,0:T(1,128)}, f32[16,64,8,1,128]{4,3,2,1,0:T(1,128)}, s32[1]{0:T(128)}) custom-call(s32[8]{0:T(128)S(1)} %copy-done.4), custom_call_target="tpu_custom_call" | custom-call | bytes 29360128 | tf_op jit(solution)/shard_map/clear_rows/pallas_call | solution.py:355
  95.1 0.0 collective-permute-done.6.refs_8_
  95.1 0.7 copy-done.16
  95.8 0.7 copy-done.18
  96.6 0.7 copy-done.20
  97.3 0.7 copy-done.22
  98.1 0.9 copy-done.10
  98.9 0.9 copy-done.24
  99.9 1.4 copy-done.29
  101.3 3.0 %adapter.1 = (bf16[8,384,128]{2,1,0:T(8,128)(2,1)}, f32[128,1024]{1,0:T(8,128)S(1)}) custom-call(bf16[8,256,320]{2,1,0:T(8,128)(2,1)S(1)} %copy-done.29, bf16[128,1024]{1,0:T(8,128)(2,1)S(1)} %copy-done.24, bf16[8,384,128]{2,1,0:T(8,128)(2,1)S(1)} %all-to-all-done.1.pieces, s32[1]{0:T(128)} %get-tuple-element.50._), custom_call_target="tpu_custom_call" | custom-call | flops 3221225472 | bytes 8388608 | tf_op jit(solution)/shard_map/adapter/pallas_call | solution.py:364
  104.3 3.6 %all-to-all-start.2 = ((bf16[8,384,128]{2,1,0:T(8,128)(2,1)}), bf16[8,384,128]{2,1,0:T(8,128)(2,1)S(1)}, u32[]{:S(2)}, u32[]{:S(2)}) async-start(bf16[8,384,128]{2,1,0:T(8,128)(2,1)} %get-tuple-element.51.refs_12_), calls=%async_computation.2 | async-start | bytes 1572864 | tf_op jit(solution)/shard_map/all_to_all | solution.py:385
  107.9 1.1 copy-done.7
  109.0 1.1 copy-done.9
  110.1 1.1 copy-done.11
  111.2 1.0 copy-done.15
  112.2 1.0 copy-done.17
  113.1 1.0 copy-done.19
  114.1 1.0 copy-done.21
  115.1 1.0 copy-done.23
  116.0 1.8 %frozen_part.1 = (f32[128,512]{1,0:T(8,128)S(1)}, f32[128,512]{1,0:T(8,128)S(1)}, f32[128,512]{1,0:T(8,128)S(1)}, f32[128,512]{1,0:T(8,128)S(1)}) custom-call(s32[1]{0:T(128)} %bitcast.7.where, bf16[4,128,640]{2,1,0:T(8,128)(2,1)S(1)} %get-tuple-element.38.refs_0_, bf16[4,128,640]{2,1,0:T(8,128)(2,1)S(1)} %copy-done.9, bf16[4,128,640]{2,1,0:T(8,128)(2,1)S(1)} %copy-done.7, ...), custom_call_target="tpu_custom_call" | custom-call | flops 4294967296 | bytes 8388608 | tf_op jit(solution)/shard_map/frozen_part/pallas_call | solution.py:375
  117.8 0.0 copy-start.25
  117.9 0.7 copy-done.25
  118.6 0.7 copy-done.26
  119.2 0.7 copy-done.27
  120.0 8.4 %all-to-all-done.2.rest_0_ = bf16[8,384,128]{2,1,0:T(8,128)(2,1)S(1)} async-done(((bf16[8,384,128]{2,1,0:T(8,128)(2,1)}), bf16[8,384,128]{2,1,0:T(8,128)(2,1)S(1)}, u32[]{:S(2)}, u32[]{:S(2)}) %all-to-all-start.2) | async-done | bytes 786464 | tf_op jit(solution)/shard_map/all_to_all | solution.py:385
  128.4 0.0 collective-permute-start.14
  128.4 0.5 collective-permute-start.11
  128.9 2.4 %collective-permute-start.12 = (f32[128,512]{1,0:T(8,128)}, f32[128,512]{1,0:T(8,128)S(1)}, u32[]{:S(2)}, u32[]{:S(2)}) collective-permute-start(f32[128,512]{1,0:T(8,128)} %copy-done.26), channel_id=1, source_target_pairs={{0,17},{1,16},{2,19},{3,18},{4,21},{5,20},{6,23},{7,22},{16,1},{17... | collective-permute-start | bytes 786440 | tf_op jit(solution)/shard_map/ppermute | solution.py:412
  131.3 0.6 collective-permute-start.10
  131.9 11.1 %collective-permute-done.11 = f32[128,512]{1,0:T(8,128)S(1)} collective-permute-done((f32[128,512]{1,0:T(8,128)}, f32[128,512]{1,0:T(8,128)S(1)}, u32[]{:S(2)}, u32[]{:S(2)}) %collective-permute-start.11) | collective-permute-done | bytes 262176 | tf_op jit(solution)/shard_map/ppermute | solution.py:301
  143.0 1.2 collective-permute-done.10
  144.3 0.8 fusion
  145.1 5.8 %place_rows.1 = (f32[16,320,8,1,128]{4,3,2,1,0:T(1,128)}, f32[16,64,8,1,128]{4,3,2,1,0:T(1,128)}) custom-call(s32[1]{0:T(128)} %bitcast.8.first_row, s32[8]{0:T(128)S(1)} %copy-done.5, s32[8]{0:T(128)S(1)} %collective-permute-done.13.rows_core, bf16[8,384,128]{2,1,0:T(8,128)(2,1)S(1)} %all-to-all-done.2.rest_0_, ...), custom_call_target="tpu_custom_call", output_to_operand_aliasing={{0}: (5, {}), {1}: (6, {})} | custom-call | bytes 16777216 | tf_op jit(solution)/shard_map/place_rows/pallas_call | solution.py:389
  (48 shorter events, 0.2 us)
Async XLA Ops:
  0.6 32.9 %copy-start = (bf16[640,512]{1,0:T(8,128)(2,1)S(1)}, bf16[640,512]{1,0:T(8,128)(2,1)}, u32[]{:S(2)}) copy-start(bf16[640,512]{1,0:T(8,128)(2,1)} %param.9) | copy-start | bytes 1966084
  0.7 1.4 copy-start.2
  3.0 18.0 %collective-permute-start = (bf16[4,128,640]{2,1,0:T(8,128)(2,1)}, bf16[4,128,640]{2,1,0:T(8,128)(2,1)S(1)}, u32[]{:S(2)}, u32[]{:S(2)}) collective-permute-start(bf16[4,128,640]{2,1,0:T(8,128)(2,1)} %get-tuple-element.37), channel_id=1, source_target_pairs={{0,1},{1,0},{2,3},{3,2},{4,5},{5,4},{6,7},{7,6},{8,9},{9,8},{10,11... | collective-permute-start | bytes 1966088 | tf_op jit(solution)/shard_map/ppermute | solution.py:295
  6.0 16.2 %collective-permute-start.1 = (bf16[4,128,640]{2,1,0:T(8,128)(2,1)S(1)}, bf16[4,128,640]{2,1,0:T(8,128)(2,1)S(1)}, u32[]{:S(2)}, u32[]{:S(2)}) collective-permute-start(bf16[4,128,640]{2,1,0:T(8,128)(2,1)S(1)} %get-tuple-element.38.refs_0_), channel_id=1, source_target_pairs={{0,16},{16,0},{1,17},{17,1},{2,18},{18,2},{3,19},{19,3},{4,20},{20... | collective-permute-start | bytes 1966088 | tf_op jit(solution)/shard_map/ppermute | solution.py:301
  10.8 11.4 %all-to-all-start = ((s32[8,1,128]{2,1,0:T(1,128)}), s32[8,1,128]{2,1,0:T(1,128)S(1)}, u32[]{:S(2)}, u32[]{:S(2)}) async-start(s32[8,1,128]{2,1,0:T(1,128)} %broadcast_in_dim.23), calls=%async_computation | async-start | bytes 8192 | tf_op jit(solution)/shard_map/all_to_all | solution.py:304
  15.7 1.3 copy-start.3
  18.8 1.2 copy-start.28
  21.0 60.0 %copy-start.6 = (bf16[4,128,640]{2,1,0:T(8,128)(2,1)}, bf16[4,128,640]{2,1,0:T(8,128)(2,1)S(1)}, u32[]{:S(2)}) copy-start(bf16[4,128,640]{2,1,0:T(8,128)(2,1)S(1)} %collective-permute-done.refs_2_) | copy-start | bytes 1966084
  22.2 6.4 %copy-start.8 = (bf16[4,128,640]{2,1,0:T(8,128)(2,1)}, bf16[4,128,640]{2,1,0:T(8,128)(2,1)S(1)}, u32[]{:S(2)}) copy-start(bf16[4,128,640]{2,1,0:T(8,128)(2,1)S(1)} %collective-permute-done.1.refs_1_) | copy-start | bytes 1966084
  22.2 0.6 copy-start.30
  28.6 70.3 %all-to-all-start.1 = ((bf16[8,384,128]{2,1,0:T(8,128)(2,1)}), bf16[8,384,128]{2,1,0:T(8,128)(2,1)S(1)}, u32[]{:S(2)}, u32[]{:S(2)}) async-start(bf16[8,384,128]{2,1,0:T(8,128)(2,1)} %get-tuple-element.41), calls=%async_computation.1 | async-start | bytes 1572864 | tf_op jit(solution)/shard_map/all_to_all | solution.py:347
  33.6 25.3 %collective-permute-start.4 = (bf16[640,256]{1,0:T(8,128)(2,1)S(1)}, bf16[640,256]{1,0:T(8,128)(2,1)S(1)}, u32[]{:S(2)}, u32[]{:S(2)}) collective-permute-start(bf16[640,256]{1,0:T(8,128)(2,1)S(1)} %constant_dynamic-slice_fusion.refs_4_), channel_id=1, source_target_pairs={{0,6},{1,7},{2,4},{3,5},{4,2},{5,3},{6,0},{7,1},{8,14},{9,15},{10,... | collective-permute-start | bytes 983048 | tf_op jit(solution)/shard_map/ppermute | solution.py:295
  37.5 43.5 %collective-permute-start.3 = (bf16[640,256]{1,0:T(8,128)(2,1)S(1)}, bf16[640,256]{1,0:T(8,128)(2,1)S(1)}, u32[]{:S(2)}, u32[]{:S(2)}) collective-permute-start(bf16[640,256]{1,0:T(8,128)(2,1)S(1)} %constant_dynamic-slice_fusion.refs_4_), channel_id=1, source_target_pairs={{0,4},{1,5},{2,6},{3,7},{4,0},{5,1},{6,2},{7,3},{8,12},{9,13},{10,... | collective-permute-start | bytes 983048 | tf_op jit(solution)/shard_map/ppermute | solution.py:295
  37.5 43.5 %collective-permute-start.2 = (bf16[640,256]{1,0:T(8,128)(2,1)S(1)}, bf16[640,256]{1,0:T(8,128)(2,1)S(1)}, u32[]{:S(2)}, u32[]{:S(2)}) collective-permute-start(bf16[640,256]{1,0:T(8,128)(2,1)S(1)} %constant_dynamic-slice_fusion.refs_4_), channel_id=1, source_target_pairs={{0,2},{1,3},{2,0},{3,1},{4,6},{5,7},{6,4},{7,5},{8,10},{9,11},{10,... | collective-permute-start | bytes 983048 | tf_op jit(solution)/shard_map/ppermute | solution.py:295
  80.9 17.1 %collective-permute-start.5 = (bf16[4,128,640]{2,1,0:T(8,128)(2,1)S(1)}, bf16[4,128,640]{2,1,0:T(8,128)(2,1)S(1)}, u32[]{:S(2)}, u32[]{:S(2)}) collective-permute-start(bf16[4,128,640]{2,1,0:T(8,128)(2,1)S(1)} %collective-permute-done.refs_2_), channel_id=1, source_target_pairs={{0,16},{16,0},{1,17},{17,1},{2,18},{18,2},{3,19},{19,3},{4,20},{20... | collective-permute-start | bytes 1966088 | tf_op jit(solution)/shard_map/ppermute | solution.py:301
  82.5 12.6 %collective-permute-start.6 = (bf16[640,256]{1,0:T(8,128)(2,1)S(1)}, bf16[640,256]{1,0:T(8,128)(2,1)S(1)}, u32[]{:S(2)}, u32[]{:S(2)}) collective-permute-start(bf16[640,256]{1,0:T(8,128)(2,1)S(1)} %constant_dynamic-slice_fusion.refs_4_), channel_id=1, source_target_pairs={{0,8},{8,0},{1,9},{9,1},{2,10},{10,2},{3,11},{11,3},{4,12},{12,4},... | collective-permute-start | bytes 983048 | tf_op jit(solution)/shard_map/ppermute | solution.py:298
  82.5 13.4 %collective-permute-start.7 = (bf16[640,256]{1,0:T(8,128)(2,1)S(1)}, bf16[640,256]{1,0:T(8,128)(2,1)S(1)}, u32[]{:S(2)}, u32[]{:S(2)}) collective-permute-start(bf16[640,256]{1,0:T(8,128)(2,1)S(1)} %collective-permute-done.2.refs_5_), channel_id=1, source_target_pairs={{0,8},{8,0},{1,9},{9,1},{2,10},{10,2},{3,11},{11,3},{4,12},{12,4},... | collective-permute-start | bytes 983048 | tf_op jit(solution)/shard_map/ppermute | solution.py:298
  83.0 0.7 copy-start.14
  83.7 12.9 %collective-permute-start.8 = (bf16[640,256]{1,0:T(8,128)(2,1)S(1)}, bf16[640,256]{1,0:T(8,128)(2,1)S(1)}, u32[]{:S(2)}, u32[]{:S(2)}) collective-permute-start(bf16[640,256]{1,0:T(8,128)(2,1)S(1)} %collective-permute-done.3.refs_6_), channel_id=1, source_target_pairs={{0,8},{8,0},{1,9},{9,1},{2,10},{10,2},{3,11},{11,3},{4,12},{12,4},... | collective-permute-start | bytes 983048 | tf_op jit(solution)/shard_map/ppermute | solution.py:298
  83.7 0.7 copy-start.12
  84.4 12.9 %collective-permute-start.9 = (bf16[640,256]{1,0:T(8,128)(2,1)S(1)}, bf16[640,256]{1,0:T(8,128)(2,1)S(1)}, u32[]{:S(2)}, u32[]{:S(2)}) collective-permute-start(bf16[640,256]{1,0:T(8,128)(2,1)S(1)} %collective-permute-done.4.refs_7_), channel_id=1, source_target_pairs={{0,8},{8,0},{1,9},{9,1},{2,10},{10,2},{3,11},{11,3},{4,12},{12,4},... | collective-permute-start | bytes 983048 | tf_op jit(solution)/shard_map/ppermute | solution.py:298
  84.9 0.7 copy-start.4
  95.1 0.7 copy-start.16
  95.8 0.7 copy-start.18
  96.6 0.7 copy-start.20
  97.3 0.7 copy-start.22
  98.1 0.9 copy-start.10
  98.9 1.0 copy-start.24
  99.9 1.4 copy-start.29
  101.3 6.6 %copy-start.13 = (bf16[640,256]{1,0:T(8,128)(2,1)S(1)}, bf16[640,256]{1,0:T(8,128)(2,1)}, u32[]{:S(2)}) copy-start(bf16[640,256]{1,0:T(8,128)(2,1)} %copy-done.12) | copy-start | bytes 983044
  104.3 24.1 %all-to-all-start.2 = ((bf16[8,384,128]{2,1,0:T(8,128)(2,1)}), bf16[8,384,128]{2,1,0:T(8,128)(2,1)S(1)}, u32[]{:S(2)}, u32[]{:S(2)}) async-start(bf16[8,384,128]{2,1,0:T(8,128)(2,1)} %get-tuple-element.51.refs_12_), calls=%async_computation.2 | async-start | bytes 1572864 | tf_op jit(solution)/shard_map/all_to_all | solution.py:385
  107.9 1.1 copy-start.7
  109.0 1.1 copy-start.9
  110.1 1.1 copy-start.11
  111.2 1.0 copy-start.15
  112.1 1.0 copy-start.17
  113.1 1.0 copy-start.19
  114.1 1.0 copy-start.21
  115.1 1.0 copy-start.23
  116.0 15.9 %copy-start.5 = (s32[8]{0:T(128)S(1)}, s32[8]{0:T(128)}, u32[]{:S(2)}) copy-start(s32[8]{0:T(128)} %get-tuple-element.43.after_ref.rows_here) | copy-start | bytes 100
  117.8 0.7 copy-start.25
  118.6 0.7 copy-start.26
  119.2 0.7 copy-start.27
  128.4 16.6 %collective-permute-start.14 = (bf16[8,384,128]{2,1,0:T(8,128)(2,1)S(1)}, bf16[8,384,128]{2,1,0:T(8,128)(2,1)S(1)}, u32[]{:S(2)}, u32[]{:S(2)}) collective-permute-start(bf16[8,384,128]{2,1,0:T(8,128)(2,1)S(1)} %all-to-all-done.2.rest_0_), channel_id=1, source_target_pairs={{0,8},{8,0},{1,9},{9,1},{2,10},{10,2},{3,11},{11,3},{4,12},{12,4},... | collective-permute-start | bytes 2359304 | tf_op jit(solution)/shard_map/ppermute | solution.py:298
  128.4 14.5 %collective-permute-start.11 = (f32[128,512]{1,0:T(8,128)}, f32[128,512]{1,0:T(8,128)S(1)}, u32[]{:S(2)}, u32[]{:S(2)}) collective-permute-start(f32[128,512]{1,0:T(8,128)} %copy-done.27), channel_id=1, source_target_pairs={{0,16},{16,0},{1,17},{17,1},{2,18},{18,2},{3,19},{19,3},{4,20},{20... | collective-permute-start | bytes 786440 | tf_op jit(solution)/shard_map/ppermute | solution.py:301
  128.9 14.0 %collective-permute-start.12 = (f32[128,512]{1,0:T(8,128)}, f32[128,512]{1,0:T(8,128)S(1)}, u32[]{:S(2)}, u32[]{:S(2)}) collective-permute-start(f32[128,512]{1,0:T(8,128)} %copy-done.26), channel_id=1, source_target_pairs={{0,17},{1,16},{2,19},{3,18},{4,21},{5,20},{6,23},{7,22},{16,1},{17... | collective-permute-start | bytes 786440 | tf_op jit(solution)/shard_map/ppermute | solution.py:412
  131.3 12.9 %collective-permute-start.10 = (f32[128,512]{1,0:T(8,128)}, f32[128,512]{1,0:T(8,128)S(1)}, u32[]{:S(2)}, u32[]{:S(2)}) collective-permute-start(f32[128,512]{1,0:T(8,128)} %copy-done.25), channel_id=1, source_target_pairs={{0,1},{1,0},{2,3},{3,2},{4,5},{5,4},{6,7},{7,6},{8,9},{9,8},{10,11... | collective-permute-start | bytes 786440 | tf_op jit(solution)/shard_map/ppermute | solution.py:295
  131.9 13.1 %collective-permute-start.13 = (s32[8]{0:T(128)S(1)}, s32[8]{0:T(128)S(1)}, u32[]{:S(2)}, u32[]{:S(2)}) collective-permute-start(s32[8]{0:T(128)S(1)} %copy-done.5), channel_id=1, source_target_pairs={{0,8},{8,0},{1,9},{9,1},{2,10},{10,2},{3,11},{11,3},{4,12},{12,4},... | collective-permute-start | bytes 104 | tf_op jit(solution)/shard_map/ppermute | solution.py:298
  145.0 5.8 %copy-start.1 = (bf16[640,512]{1,0:T(8,128)(2,1)S(1)}, bf16[640,512]{1,0:T(8,128)(2,1)}, u32[]{:S(2)}) copy-start(bf16[640,512]{1,0:T(8,128)(2,1)} %param.9) | copy-start | bytes 1966084

commit v8 on v7

--- a/solution.py
+++ b/solution.py
@@ -99,8 +99,11 @@
     return mixed, grad_down, grad_up
 
 
-def split_kernel(where, x_ref, mine_ref, theirs_ref, done_ref):
-    done_ref[0] = 0
+def row_kernel(block_ref, slot_ref, out_ref):
+    out_ref[...] = jnp.full(out_ref.shape, slot_ref[block_ref[0]], jnp.int32)
+
+
+def split_kernel(where, x_ref, mine_ref, theirs_ref):
     inner = where[0]
     outer, rows, width = mine_ref.shape
     for k in range(outer):
@@ -123,13 +126,12 @@
         xs_ref[k, rows:] = dot(x, odd).astype(jnp.bfloat16)
 
 
-def gather_kernel(after, asked, down_ref, up_ref, out_ref, rows_ref, down_buf, up_buf, flat, built, sems):
-    del after
+def gather_kernel(asked, down_ref, up_ref, out_ref, rows_ref, down_buf, up_buf, flat, built, sems):
     count, down_chunks, up_chunks = down_buf.shape[0], down_buf.shape[1], up_buf.shape[1]
     across = up_chunks // 8
 
     def copies(t):
-        tile = asked[t, 0] // TILE_ROWS
+        tile = asked[t, 0, 0] // TILE_ROWS
         return (
             pltpu.make_async_copy(down_ref.at[tile], down_buf.at[t], sems.at[0, t]),
             pltpu.make_async_copy(up_ref.at[tile], up_buf.at[t], sems.at[1, t]),
@@ -140,7 +142,7 @@
         down, up, _ = copies(t)
         down.start()
         up.start()
-        rows_ref[t] = asked[t, 0]
+        rows_ref[t] = asked[t, 0, 0]
 
     def one(t, carry):
         down, up, leave = copies(t)
@@ -151,7 +153,7 @@
         down.wait()
         for j in range(down_chunks):
             flat[j * 8:j * 8 + 8, :] = down_buf[t, j].astype(jnp.float32)
-        sub = asked[t, 0] % TILE_ROWS
+        sub = asked[t, 0, 0] % TILE_ROWS
         built[t] = flat[pl.ds(sub, down_chunks + up_chunks, stride=8), :].astype(jnp.bfloat16)
         leave.start()
         return carry
@@ -300,8 +302,12 @@
     def other_part(value):
         return lax.ppermute(value, "parts", [(a, parts - 1 - a) for a in range(parts)])
 
-    row = store_rows(block_adapter, adapter_slot)
-    asked = lax.all_to_all(jnp.broadcast_to(row, (group, LANES)), "tensor", 0, 0)
+    row = pl.pallas_call(
+        row_kernel, out_shape=jax.ShapeDtypeStruct((group, 1, LANES), jnp.int32),
+        in_specs=[SMEM, SMEM], out_specs=VMEM, name="own_row",
+    )(block_adapter, adapter_slot)
+    asked = lax.all_to_all(row, "tensor", 0, 0)
+    split_from, row = lax.optimization_barrier((tokens, row))
 
     width = frozen_value.shape[1] // parts
     half = lax.dynamic_slice_in_dim(frozen_value, part * width, width, axis=1)
@@ -309,20 +315,12 @@
 
     block = jax.ShapeDtypeStruct((outer, token_rows, slice_width), jnp.bfloat16)
     token = jax.ShapeDtypeStruct((1,), jnp.int32)
-    x_mine, x_theirs, split = pl.pallas_call(
-        split_kernel, out_shape=(block, block, token), in_specs=[SMEM, VMEM], out_specs=(VMEM, VMEM, SMEM),
+    x_mine, x_theirs = pl.pallas_call(
+        split_kernel, out_shape=(block, block), in_specs=[SMEM, VMEM], out_specs=(VMEM, VMEM),
         name="split_tokens", compiler_params=LIMIT,
-    )(x[None], tokens)
+    )(x[None], split_from)
     x_far = exchange(x_theirs, 1)
     y_mine = other_part(x_mine)
-    xs = pl.pallas_call(
-        interleave_kernel,
-        out_shape=jax.ShapeDtypeStruct((group, 2 * token_rows, slice_width // 2), jnp.bfloat16),
-        in_specs=[VMEM], out_specs=VMEM, name="pair_columns", compiler_params=LIMIT,
-        cost_estimate=cost(flops=2 << 30, read=4 << 20),
-    )(tokens)
-
-    split, x_far, y_mine, xs = lax.optimization_barrier((split, x_far, y_mine, xs))
     pieces = jax.ShapeDtypeStruct((group, down_chunks + up_chunks, LANES), jnp.bfloat16)
     def tiles(store):
         view = store.reshape(store.shape[0] // TILE_ROWS, TILE_ROWS, store.shape[1] // LANES, LANES)
@@ -331,7 +329,7 @@
     sent, rows = pl.pallas_call(
         gather_kernel,
         out_shape=(pieces, jax.ShapeDtypeStruct((group,), jnp.int32)),
-        in_specs=[SMEM, SMEM, ANY, ANY],
+        in_specs=[SMEM, ANY, ANY],
         out_specs=(ANY, SMEM),
         scratch_shapes=[
             pltpu.VMEM((group, down_chunks, TILE_ROWS, LANES), jnp.bfloat16),
@@ -343,11 +341,19 @@
         compiler_params=WIDE,
         cost_estimate=cost(read=40 << 20),
         name="pick_panels",
-    )(split, asked, tiles(down_store), tiles(up_store))
+    )(asked, tiles(down_store), tiles(up_store))
+    sent, quarter = lax.optimization_barrier((sent, quarter))
     panels = lax.all_to_all(sent, "tensor", 0, 0)
     rows_core = other_core(rows)
-    x_far, quarter, _ = lax.optimization_barrier((x_far, quarter, rows))
+    x_far, y_mine, picked = lax.optimization_barrier((x_far, y_mine, rows))
     y_far = other_part(x_far)
+    pair_from, _ = lax.optimization_barrier((tokens, rows))
+    xs = pl.pallas_call(
+        interleave_kernel,
+        out_shape=jax.ShapeDtypeStruct((group, 2 * token_rows, slice_width // 2), jnp.bfloat16),
+        in_specs=[VMEM], out_specs=VMEM, name="pair_columns", compiler_params=LIMIT,
+        cost_estimate=cost(flops=2 << 30, read=4 << 20),
+    )(pair_from)
 
     owned_groups = ADAPTERS // lax.axis_size("dp") // 8
     down_shape = jax.ShapeDtypeStruct((owned_groups, down_chunks, 8, 1, LANES), jnp.float32)
@@ -357,7 +363,7 @@
         in_specs=[SMEM], out_specs=(ANY, ANY, SMEM),
         scratch_shapes=[pltpu.VMEM((up_chunks, 8, 1, LANES), jnp.float32), pltpu.SemaphoreType.DMA((2,))],
         compiler_params=LIMIT, cost_estimate=cost(read=28 << 20), name="clear_rows",
-    )(rows)
+    )(picked)
     quarter_core = [other_core(w) for w in quarter]
     panels, y_far, quarter_core = lax.optimization_barrier((panels, y_far, quarter_core))
 
@@ -383,7 +389,8 @@
     )(z[None], x_mine, y_mine, x_far, y_far, *quarter, *quarter_core, terms)
     opposite = [(a * group + t, (parts - 1 - a) * group + (t ^ 1)) for a in range(parts) for t in range(group)]
     back = lax.all_to_all(terms, "tensor", 0, 0)
-    back, own = lax.optimization_barrier((back, own))
+    arrived = (exchange(to_inner, 1), other_part(to_part), lax.ppermute(to_both, ("parts", "tensor"), opposite))
+    back, arrived = lax.optimization_barrier((back, arrived))
     back_core = other_core(back)
 
     grad_down, grad_up = pl.pallas_call(
@@ -408,8 +415,7 @@
     grad_down = grad_down.reshape(owned_groups, down_chunks, 8, LANES).transpose(0, 2, 1, 3)
     grad_up = grad_up.reshape(owned_groups, up_chunks, 8, LANES).transpose(0, 2, 1, 3)
 
-    kept = own + exchange(to_inner, 1)
-    got = other_part(to_part) + lax.ppermute(to_both, ("parts", "tensor"), opposite)
+    kept, got = own + arrived[0], arrived[1] + arrived[2]
     quarters = [[c[:, :width], c[:, width:]] for c in (kept, got)]
 
     def pick_quarter(c, a):

time: 152 us -> 133 us (0.88)
  waiting for transfers between devices: 65.7 us -> 32.7 us
  blocking collectives: 0 us -> 26.4 us
  local copies, waits for them, and re-layouts: 24.3 us -> 15.5 us
  starting transfers between devices: 28.5 us -> 24.3 us
  Pallas kernels: 28.6 us -> 30.5 us
    all_to_all x0 -> x1, blocking collectives: none -> 26.4 us  [fast_body(): asked = lax.all_to_all(row, 'tensor', 0, 0)]
    ppermute x5, waiting for transfers between devices: 45 us -> 27.2 us  [exchange(): return lax.ppermute(value, 'tensor', [(t, t ^ s) for t in range(group)])]
    ppermute x3, waiting for transfers between devices: 12.3 us -> 0.01 us  [other_part(): lax.ppermute(value, 'parts', [(a, parts - 1 - a) for a in range(parts)])]
    all_to_all x1, waiting for transfers between devices: 8.44 us -> 0.01 us  [fast_body(): back = lax.all_to_all(terms, 'tensor', 0, 0)]
    unnamed x62 -> x42, local copies, waits for them, and re-layouts: 23 us -> 15.5 us
    all_to_all x1 -> x0, starting transfers between devices: 4.88 us -> none  [fast_body(): lax.all_to_all(jnp.broadcast_to(row, (group, LANES)), 'tensor', 0, 0)]
    ppermute x1, waiting for transfers between devices: 0.01 us -> 4.56 us  [fast_body(): lax.ppermute(to_both, ('parts', 'tensor'), opposite)]
    ppermute x5, starting transfers between devices: 8.12 us -> 9.92 us  [exchange(): return lax.ppermute(value, 'tensor', [(t, t ^ s) for t in range(group)])]
  transfers between devices with their start and end apart: 18 -> 17, of which waited for: 7 -> 4; matrix products, arithmetic and copies ran while one was open for 2% -> 1% of each run, Pallas kernels for 9% -> 16%
where the time goes in v8:
time: 133 us; the launch traced here: 132 us
  waiting for transfers between devices  32.7 us (25%)
  Pallas kernels  30.5 us (23%)
  blocking collectives  26.4 us (20%)
  starting transfers between devices  24.3 us (18%)
  local copies, waits for them, and re-layouts  15.5 us (12%)
  between operations  1.62 us (1%)
    ppermute x5, waiting for transfers between devices, exchange(): return lax.ppermute(value, 'tensor', [(t, t ^ s) for t in range(group)])  27.2 us
    all_to_all x1, blocking collectives, fast_body(): asked = lax.all_to_all(row, 'tensor', 0, 0)  26.4 us
    unnamed x42, local copies, waits for them, and re-layouts  15.5 us
    ppermute x5, starting transfers between devices, exchange(): return lax.ppermute(value, 'tensor', [(t, t ^ s) for t in range(group)])  9.92 us
    pallas_call x1, Pallas kernels, fast_body(): pl.pallas_call(zero_kernel, out_shape=(down_shape, up_shape, token), in_s...  9.48 us
    pallas_call x1, Pallas kernels, fast_body(): pl.pallas_call(functools.partial(scatter_kernel, 2 * group, down_chunks,...  6.18 us
    pallas_call x1, Pallas kernels, fast_body(): pl.pallas_call(gather_kernel, out_shape=(pieces, jax.ShapeDtypeStruct((gr...  5.7 us
    ppermute x1, waiting for transfers between devices, fast_body(): lax.ppermute(to_both, ('parts', 'tensor'), opposite)  4.56 us
  transfers between devices with their start and end apart: 17, of which 4 were waited for; matrix products, arithmetic and copies ran while one was open for 1% of the time, Pallas kernels for 16%

profile of v8, /device:TPU:0, one launch (start us, length us, event | category | flops | bytes accessed | tf_op | source)
XLA Modules:
  0.0 131.9 jit_solution(15732813072174513719)
XLA Ops:
  0.6 0.0 copy-start
  0.7 1.1 copy-done
  1.8 5.1 %collective-permute-start.4 = (bf16[640,256]{1,0:T(8,128)(2,1)S(1)}, bf16[640,256]{1,0:T(8,128)(2,1)}, u32[]{:S(2)}, u32[]{:S(2)}) collective-permute-start(bf16[640,256]{1,0:T(8,128)(2,1)S(1)} %constant_dynamic-slice_fusion.refs_4_), channel_id=1, source_target_pairs={{0,6},{1,7},{2,4},{3,5},{4,2},{5,3},{6,0},{7,1},{8,14},{9,15},{10,... | collective-permute-start | bytes 983048 | tf_op jit(solution)/shard_map/ppermute | solution.py:297
  6.9 0.0 collective-permute-start.3
  6.9 0.6 collective-permute-start.2
  8.2 1.3 own_row.1
  9.4 26.4 %all_to_all.15.asked = s32[8,1,128]{2,1,0:T(1,128)} all-to-all(s32[8,1,128]{2,1,0:T(1,128)} %own_row.1), channel_id=1, replica_groups=mesh['parts'=2,'dp'=2,'tensor'=8] {'tensor'}, dimensions={0} | all-to-all | bytes 8192 | tf_op jit(solution)/shard_map/all_to_all | solution.py:309
  35.9 5.7 %pick_panels.1 = (bf16[8,384,128]{2,1,0:T(8,128)(2,1)}, s32[8]{0:T(128)}) custom-call(s32[8,1,128]{2,1,0:T(1,128)} %all_to_all.15.asked, bf16[32,320,8,128]{3,2,1,0:T(8,128)(2,1)} %bitcast.20, bf16[32,64,8,128]{3,2,1,0:T(8,128)(2,1)} %bitcast.21), custom_call_target="tpu_custom_call" | custom-call | bytes 41943040 | tf_op jit(solution)/shard_map/pick_panels/pallas_call | solution.py:329
  41.6 0.0 collective-permute-done.4.refs_7_
  41.6 0.0 collective-permute-done.3.refs_6_
  41.6 0.0 collective-permute-done.2.refs_5_
  41.6 3.8 %all-to-all-start.1 = ((bf16[8,384,128]{2,1,0:T(8,128)(2,1)}), bf16[8,384,128]{2,1,0:T(8,128)(2,1)S(1)}, u32[]{:S(2)}, u32[]{:S(2)}) async-start(bf16[8,384,128]{2,1,0:T(8,128)(2,1)} %get-tuple-element.45), calls=%async_computation.1 | async-start | bytes 1572864 | tf_op jit(solution)/shard_map/all_to_all | solution.py:346
  45.4 0.1 split_tokens.1
  45.5 0.0 copy-start.3
  45.5 0.0 copy-start.18
  45.5 2.1 %collective-permute-start = (bf16[4,128,640]{2,1,0:T(8,128)(2,1)S(1)}, bf16[4,128,640]{2,1,0:T(8,128)(2,1)S(1)}, u32[]{:S(2)}, u32[]{:S(2)}) collective-permute-start(bf16[4,128,640]{2,1,0:T(8,128)(2,1)S(1)} %get-tuple-element.40), channel_id=1, source_target_pairs={{0,1},{1,0},{2,3},{3,2},{4,5},{5,4},{6,7},{7,6},{8,9},{9,8},{10,11... | collective-permute-start | bytes 1966088 | tf_op jit(solution)/shard_map/ppermute | solution.py:297
  47.6 1.2 collective-permute-start.1
  48.8 20.1 %collective-permute-done.refs_2_ = bf16[4,128,640]{2,1,0:T(8,128)(2,1)S(1)} collective-permute-done((bf16[4,128,640]{2,1,0:T(8,128)(2,1)S(1)}, bf16[4,128,640]{2,1,0:T(8,128)(2,1)S(1)}, u32[]{:S(2)}, u32[]{:S(2)}) %collective-permute-start) | collective-permute-done | bytes 655392 | tf_op jit(solution)/shard_map/ppermute | solution.py:297
  68.9 0.0 collective-permute-done.1.refs_1_
  68.9 0.9 copy-done.6
  69.8 1.8 %collective-permute-start.5 = (bf16[4,128,640]{2,1,0:T(8,128)(2,1)S(1)}, bf16[4,128,640]{2,1,0:T(8,128)(2,1)S(1)}, u32[]{:S(2)}, u32[]{:S(2)}) collective-permute-start(bf16[4,128,640]{2,1,0:T(8,128)(2,1)S(1)} %collective-permute-done.refs_2_), channel_id=1, source_target_pairs={{0,16},{16,0},{1,17},{17,1},{2,18},{18,2},{3,19},{19,3},{4,20},{20... | collective-permute-start | bytes 1966088 | tf_op jit(solution)/shard_map/ppermute | solution.py:303
  71.6 0.0 collective-permute-start.6
  71.6 0.5 collective-permute-start.7
  72.1 0.0 collective-permute-start.8
  72.1 0.5 collective-permute-start.9
  72.6 1.8 %pair_columns.1.xs_ref = bf16[8,256,320]{2,1,0:T(8,128)(2,1)S(1)} custom-call(bf16[128,5120]{1,0:T(8,128)(2,1)S(1)} %copy-done.2), custom_call_target="tpu_custom_call" | custom-call | flops 2147483648 | bytes 4194304 | tf_op jit(solution)/shard_map/pair_columns/pallas_call | solution.py:351
  74.5 1.2 copy-done.19
  75.6 9.5 %clear_rows.1 = (f32[16,320,8,1,128]{4,3,2,1,0:T(1,128)}, f32[16,64,8,1,128]{4,3,2,1,0:T(1,128)}, s32[1]{0:T(128)}) custom-call(s32[8]{0:T(128)S(1)} %copy-done.3), custom_call_target="tpu_custom_call" | custom-call | bytes 29360128 | tf_op jit(solution)/shard_map/clear_rows/pallas_call | solution.py:361
  85.1 0.0 collective-permute-done.6.refs_8_
  85.1 0.0 copy-start.10
  85.1 0.7 copy-done.10
  85.9 0.0 collective-permute-done.7.refs_9_
  85.9 0.7 copy-done.12
  86.6 0.0 collective-permute-done.8.refs_10_
  86.6 0.7 copy-done.14
  87.3 0.0 collective-permute-done.9.refs_11_
  87.3 0.7 copy-done.16
  88.1 0.0 collective-permute-done.5.refs_3_
  88.1 0.8 copy-done.8
  88.9 0.0 all-to-all-done.1.pieces
  88.9 1.4 %copy-done.20 = bf16[8,256,320]{2,1,0:T(8,128)(2,1)S(1)} copy-done((bf16[8,256,320]{2,1,0:T(8,128)(2,1)S(1)}, bf16[8,256,320]{2,1,0:T(8,128)(2,1)}, u32[]{:S(2)}) %copy-start.20) | copy-done | bytes 1310744
  90.3 3.0 %adapter.1 = (bf16[8,384,128]{2,1,0:T(8,128)(2,1)}, f32[128,1024]{1,0:T(8,128)S(1)}) custom-call(bf16[8,256,320]{2,1,0:T(8,128)(2,1)S(1)} %copy-done.20, bf16[128,1024]{1,0:T(8,128)(2,1)S(1)} %copy-done.18, bf16[8,384,128]{2,1,0:T(8,128)(2,1)S(1)} %all-to-all-done.1.pieces, s32[1]{0:T(128)} %get-tuple-element.58._), custom_call_target="tpu_custom_call" | custom-call | flops 3221225472 | bytes 8388608 | tf_op jit(solution)/shard_map/adapter/pallas_call | solution.py:370
  93.3 4.5 %all-to-all-start.2 = ((bf16[8,384,128]{2,1,0:T(8,128)(2,1)}), bf16[8,384,128]{2,1,0:T(8,128)(2,1)S(1)}, u32[]{:S(2)}, u32[]{:S(2)}) async-start(bf16[8,384,128]{2,1,0:T(8,128)(2,1)} %get-tuple-element.59.refs_12_), calls=%async_computation.2 | async-start | bytes 1572864 | tf_op jit(solution)/shard_map/all_to_all | solution.py:391
  97.9 1.1 copy-done.5
  98.9 1.1 copy-done.7
  100.0 1.1 copy-done.9
  101.1 1.0 copy-done.11
  102.1 1.0 copy-done.13
  103.1 1.0 copy-done.15
  104.0 1.0 copy-done.17
  105.0 3.0 %frozen_part.1 = (f32[128,512]{1,0:T(8,128)S(1)}, f32[128,512]{1,0:T(8,128)S(1)}, f32[128,512]{1,0:T(8,128)S(1)}, f32[128,512]{1,0:T(8,128)S(1)}) custom-call(s32[1]{0:T(128)} %bitcast.where, bf16[4,128,640]{2,1,0:T(8,128)(2,1)S(1)} %get-tuple-element.39.refs_0_, bf16[4,128,640]{2,1,0:T(8,128)(2,1)S(1)} %copy-done.7, bf16[4,128,640]{2,1,0:T(8,128)(2,1)S(1)} %copy-done.5, ...), custom_call_target="tpu_custom_call" | custom-call | flops 4294967296 | bytes 8388608 | tf_op jit(solution)/shard_map/frozen_part/pallas_call | solution.py:381
  108.0 2.1 %collective-permute-start.10 = (f32[128,512]{1,0:T(8,128)S(1)}, f32[128,512]{1,0:T(8,128)S(1)}, u32[]{:S(2)}, u32[]{:S(2)}) collective-permute-start(f32[128,512]{1,0:T(8,128)S(1)} %get-tuple-element.61), channel_id=1, source_target_pairs={{0,1},{1,0},{2,3},{3,2},{4,5},{5,4},{6,7},{7,6},{8,9},{9,8},{10,11... | collective-permute-start | bytes 786440 | tf_op jit(solution)/shard_map/ppermute | solution.py:297
  110.1 0.2 collective-permute-start.11
  110.3 1.4 %collective-permute-start.12 = (f32[128,512]{1,0:T(8,128)S(1)}, f32[128,512]{1,0:T(8,128)S(1)}, u32[]{:S(2)}, u32[]{:S(2)}) collective-permute-start(f32[128,512]{1,0:T(8,128)S(1)} %get-tuple-element.63), channel_id=1, source_target_pairs={{0,17},{1,16},{2,19},{3,18},{4,21},{5,20},{6,23},{7,22},{16,1},{17... | collective-permute-start | bytes 786440 | tf_op jit(solution)/shard_map/ppermute | solution.py:392
  111.6 7.1 %collective-permute-done.10 = f32[128,512]{1,0:T(8,128)S(1)} collective-permute-done((f32[128,512]{1,0:T(8,128)S(1)}, f32[128,512]{1,0:T(8,128)S(1)}, u32[]{:S(2)}, u32[]{:S(2)}) %collective-permute-start.10) | collective-permute-done | bytes 262176 | tf_op jit(solution)/shard_map/ppermute | solution.py:297
  118.7 0.0 collective-permute-done.11
  118.7 4.6 %collective-permute-done.12 = f32[128,512]{1,0:T(8,128)S(1)} collective-permute-done((f32[128,512]{1,0:T(8,128)S(1)}, f32[128,512]{1,0:T(8,128)S(1)}, u32[]{:S(2)}, u32[]{:S(2)}) %collective-permute-start.12) | collective-permute-done | bytes 262176 | tf_op jit(solution)/shard_map/ppermute | solution.py:392
  123.3 0.0 all-to-all-done.2.rest_0_
  123.3 0.0 collective-permute-start.14
  123.3 0.5 collective-permute-start.13
  124.0 0.8 fusion
  124.7 0.9 collective-permute-done.13.rows_core
  125.6 0.0 collective-permute-done.14.rest_1_
  125.6 6.2 %place_rows.1 = (f32[16,320,8,1,128]{4,3,2,1,0:T(1,128)}, f32[16,64,8,1,128]{4,3,2,1,0:T(1,128)}) custom-call(s32[1]{0:T(128)} %bitcast.6.first_row, s32[8]{0:T(128)S(1)} %copy-done.3, s32[8]{0:T(128)S(1)} %collective-permute-done.13.rows_core, bf16[8,384,128]{2,1,0:T(8,128)(2,1)S(1)} %all-to-all-done.2.rest_0_, ...), custom_call_target="tpu_custom_call", output_to_operand_aliasing={{0}: (5, {}), {1}: (6, {})} | custom-call | bytes 16777216 | tf_op jit(solution)/shard_map/place_rows/pallas_call | solution.py:396
  (26 shorter events, 0.2 us)
Async XLA Ops:
  0.6 1.1 copy-start
  1.8 39.8 %collective-permute-start.4 = (bf16[640,256]{1,0:T(8,128)(2,1)S(1)}, bf16[640,256]{1,0:T(8,128)(2,1)}, u32[]{:S(2)}, u32[]{:S(2)}) collective-permute-start(bf16[640,256]{1,0:T(8,128)(2,1)S(1)} %constant_dynamic-slice_fusion.refs_4_), channel_id=1, source_target_pairs={{0,6},{1,7},{2,4},{3,5},{4,2},{5,3},{6,0},{7,1},{8,14},{9,15},{10,... | collective-permute-start | bytes 983048 | tf_op jit(solution)/shard_map/ppermute | solution.py:297
  6.9 34.7 %collective-permute-start.3 = (bf16[640,256]{1,0:T(8,128)(2,1)S(1)}, bf16[640,256]{1,0:T(8,128)(2,1)}, u32[]{:S(2)}, u32[]{:S(2)}) collective-permute-start(bf16[640,256]{1,0:T(8,128)(2,1)S(1)} %constant_dynamic-slice_fusion.refs_4_), channel_id=1, source_target_pairs={{0,4},{1,5},{2,6},{3,7},{4,0},{5,1},{6,2},{7,3},{8,12},{9,13},{10,... | collective-permute-start | bytes 983048 | tf_op jit(solution)/shard_map/ppermute | solution.py:297
  6.9 34.7 %collective-permute-start.2 = (bf16[640,256]{1,0:T(8,128)(2,1)S(1)}, bf16[640,256]{1,0:T(8,128)(2,1)}, u32[]{:S(2)}, u32[]{:S(2)}) collective-permute-start(bf16[640,256]{1,0:T(8,128)(2,1)S(1)} %constant_dynamic-slice_fusion.refs_4_), channel_id=1, source_target_pairs={{0,2},{1,3},{2,0},{3,1},{4,6},{5,7},{6,4},{7,5},{8,10},{9,11},{10,... | collective-permute-start | bytes 983048 | tf_op jit(solution)/shard_map/ppermute | solution.py:297
  35.9 9.5 %copy-start.2 = (bf16[128,5120]{1,0:T(8,128)(2,1)S(1)}, bf16[128,5120]{1,0:T(8,128)(2,1)}, u32[]{:S(2)}) copy-start(bf16[128,5120]{1,0:T(8,128)(2,1)} %x_ref.1) | copy-start | bytes 3932164
  41.6 47.3 %all-to-all-start.1 = ((bf16[8,384,128]{2,1,0:T(8,128)(2,1)}), bf16[8,384,128]{2,1,0:T(8,128)(2,1)S(1)}, u32[]{:S(2)}, u32[]{:S(2)}) async-start(bf16[8,384,128]{2,1,0:T(8,128)(2,1)} %get-tuple-element.45), calls=%async_computation.1 | async-start | bytes 1572864 | tf_op jit(solution)/shard_map/all_to_all | solution.py:346
  45.5 30.1 %copy-start.3 = (s32[8]{0:T(128)S(1)}, s32[8]{0:T(128)}, u32[]{:S(2)}) copy-start(s32[8]{0:T(128)} %get-tuple-element.57.after_ref.rows_here) | copy-start | bytes 100
  45.5 43.4 %copy-start.18 = (bf16[128,1024]{1,0:T(8,128)(2,1)S(1)}, bf16[128,1024]{1,0:T(8,128)(2,1)}, u32[]{:S(2)}) copy-start(bf16[128,1024]{1,0:T(8,128)(2,1)} %g_ref.1) | copy-start | bytes 786436
  45.5 23.4 %collective-permute-start = (bf16[4,128,640]{2,1,0:T(8,128)(2,1)S(1)}, bf16[4,128,640]{2,1,0:T(8,128)(2,1)S(1)}, u32[]{:S(2)}, u32[]{:S(2)}) collective-permute-start(bf16[4,128,640]{2,1,0:T(8,128)(2,1)S(1)} %get-tuple-element.40), channel_id=1, source_target_pairs={{0,1},{1,0},{2,3},{3,2},{4,5},{5,4},{6,7},{7,6},{8,9},{9,8},{10,11... | collective-permute-start | bytes 1966088 | tf_op jit(solution)/shard_map/ppermute | solution.py:297
  47.6 21.3 %collective-permute-start.1 = (bf16[4,128,640]{2,1,0:T(8,128)(2,1)S(1)}, bf16[4,128,640]{2,1,0:T(8,128)(2,1)S(1)}, u32[]{:S(2)}, u32[]{:S(2)}) collective-permute-start(bf16[4,128,640]{2,1,0:T(8,128)(2,1)S(1)} %get-tuple-element.39.refs_0_), channel_id=1, source_target_pairs={{0,16},{16,0},{1,17},{17,1},{2,18},{18,2},{3,19},{19,3},{4,20},{20... | collective-permute-start | bytes 1966088 | tf_op jit(solution)/shard_map/ppermute | solution.py:303
  68.9 18.4 %copy-start.4 = (bf16[4,128,640]{2,1,0:T(8,128)(2,1)}, bf16[4,128,640]{2,1,0:T(8,128)(2,1)S(1)}, u32[]{:S(2)}) copy-start(bf16[4,128,640]{2,1,0:T(8,128)(2,1)S(1)} %collective-permute-done.refs_2_) | copy-start | bytes 1966084
  68.9 0.9 copy-start.6
  69.8 18.3 %collective-permute-start.5 = (bf16[4,128,640]{2,1,0:T(8,128)(2,1)S(1)}, bf16[4,128,640]{2,1,0:T(8,128)(2,1)S(1)}, u32[]{:S(2)}, u32[]{:S(2)}) collective-permute-start(bf16[4,128,640]{2,1,0:T(8,128)(2,1)S(1)} %collective-permute-done.refs_2_), channel_id=1, source_target_pairs={{0,16},{16,0},{1,17},{17,1},{2,18},{18,2},{3,19},{19,3},{4,20},{20... | collective-permute-start | bytes 1966088 | tf_op jit(solution)/shard_map/ppermute | solution.py:303
  71.6 13.5 %collective-permute-start.6 = (bf16[640,256]{1,0:T(8,128)(2,1)S(1)}, bf16[640,256]{1,0:T(8,128)(2,1)S(1)}, u32[]{:S(2)}, u32[]{:S(2)}) collective-permute-start(bf16[640,256]{1,0:T(8,128)(2,1)S(1)} %constant_dynamic-slice_fusion.refs_4_), channel_id=1, source_target_pairs={{0,8},{8,0},{1,9},{9,1},{2,10},{10,2},{3,11},{11,3},{4,12},{12,4},... | collective-permute-start | bytes 983048 | tf_op jit(solution)/shard_map/ppermute | solution.py:300
  71.6 14.2 %collective-permute-start.7 = (bf16[640,256]{1,0:T(8,128)(2,1)}, bf16[640,256]{1,0:T(8,128)(2,1)S(1)}, u32[]{:S(2)}, u32[]{:S(2)}) collective-permute-start(bf16[640,256]{1,0:T(8,128)(2,1)} %collective-permute-done.2.refs_5_), channel_id=1, source_target_pairs={{0,8},{8,0},{1,9},{9,1},{2,10},{10,2},{3,11},{11,3},{4,12},{12,4},... | collective-permute-start | bytes 983048 | tf_op jit(solution)/shard_map/ppermute | solution.py:300
  72.1 14.5 %collective-permute-start.8 = (bf16[640,256]{1,0:T(8,128)(2,1)}, bf16[640,256]{1,0:T(8,128)(2,1)S(1)}, u32[]{:S(2)}, u32[]{:S(2)}) collective-permute-start(bf16[640,256]{1,0:T(8,128)(2,1)} %collective-permute-done.3.refs_6_), channel_id=1, source_target_pairs={{0,8},{8,0},{1,9},{9,1},{2,10},{10,2},{3,11},{11,3},{4,12},{12,4},... | collective-permute-start | bytes 983048 | tf_op jit(solution)/shard_map/ppermute | solution.py:300
  72.1 15.2 %collective-permute-start.9 = (bf16[640,256]{1,0:T(8,128)(2,1)}, bf16[640,256]{1,0:T(8,128)(2,1)S(1)}, u32[]{:S(2)}, u32[]{:S(2)}) collective-permute-start(bf16[640,256]{1,0:T(8,128)(2,1)} %collective-permute-done.4.refs_7_), channel_id=1, source_target_pairs={{0,8},{8,0},{1,9},{9,1},{2,10},{10,2},{3,11},{11,3},{4,12},{12,4},... | collective-permute-start | bytes 983048 | tf_op jit(solution)/shard_map/ppermute | solution.py:300
  74.4 1.2 copy-start.19
  85.1 0.7 copy-start.10
  85.9 0.7 copy-start.12
  86.6 0.7 copy-start.14
  87.3 0.7 copy-start.16
  88.1 0.8 copy-start.8
  88.9 1.4 %copy-start.20 = (bf16[8,256,320]{2,1,0:T(8,128)(2,1)S(1)}, bf16[8,256,320]{2,1,0:T(8,128)(2,1)}, u32[]{:S(2)}) copy-start(bf16[8,256,320]{2,1,0:T(8,128)(2,1)} %copy-done.19) | copy-start | bytes 3932164
  93.3 30.0 %all-to-all-start.2 = ((bf16[8,384,128]{2,1,0:T(8,128)(2,1)}), bf16[8,384,128]{2,1,0:T(8,128)(2,1)S(1)}, u32[]{:S(2)}, u32[]{:S(2)}) async-start(bf16[8,384,128]{2,1,0:T(8,128)(2,1)} %get-tuple-element.59.refs_12_), calls=%async_computation.2 | async-start | bytes 1572864 | tf_op jit(solution)/shard_map/all_to_all | solution.py:391
  97.9 1.1 copy-start.5
  98.9 1.1 copy-start.7
  100.0 1.1 copy-start.9
  101.1 1.0 copy-start.11
  102.1 1.0 copy-start.13
  103.1 1.0 copy-start.15
  104.0 1.0 copy-start.17
  108.0 10.7 %collective-permute-start.10 = (f32[128,512]{1,0:T(8,128)S(1)}, f32[128,512]{1,0:T(8,128)S(1)}, u32[]{:S(2)}, u32[]{:S(2)}) collective-permute-start(f32[128,512]{1,0:T(8,128)S(1)} %get-tuple-element.61), channel_id=1, source_target_pairs={{0,1},{1,0},{2,3},{3,2},{4,5},{5,4},{6,7},{7,6},{8,9},{9,8},{10,11... | collective-permute-start | bytes 786440 | tf_op jit(solution)/shard_map/ppermute | solution.py:297
  110.1 8.7 %collective-permute-start.11 = (f32[128,512]{1,0:T(8,128)S(1)}, f32[128,512]{1,0:T(8,128)S(1)}, u32[]{:S(2)}, u32[]{:S(2)}) collective-permute-start(f32[128,512]{1,0:T(8,128)S(1)} %get-tuple-element.62), channel_id=1, source_target_pairs={{0,16},{16,0},{1,17},{17,1},{2,18},{18,2},{3,19},{19,3},{4,20},{20... | collective-permute-start | bytes 786440 | tf_op jit(solution)/shard_map/ppermute | solution.py:303
  110.3 13.0 %collective-permute-start.12 = (f32[128,512]{1,0:T(8,128)S(1)}, f32[128,512]{1,0:T(8,128)S(1)}, u32[]{:S(2)}, u32[]{:S(2)}) collective-permute-start(f32[128,512]{1,0:T(8,128)S(1)} %get-tuple-element.63), channel_id=1, source_target_pairs={{0,17},{1,16},{2,19},{3,18},{4,21},{5,20},{6,23},{7,22},{16,1},{17... | collective-permute-start | bytes 786440 | tf_op jit(solution)/shard_map/ppermute | solution.py:392
  123.3 2.3 %collective-permute-start.14 = (bf16[8,384,128]{2,1,0:T(8,128)(2,1)S(1)}, bf16[8,384,128]{2,1,0:T(8,128)(2,1)S(1)}, u32[]{:S(2)}, u32[]{:S(2)}) collective-permute-start(bf16[8,384,128]{2,1,0:T(8,128)(2,1)S(1)} %all-to-all-done.2.rest_0_), channel_id=1, source_target_pairs={{0,8},{8,0},{1,9},{9,1},{2,10},{10,2},{3,11},{11,3},{4,12},{12,4},... | collective-permute-start | bytes 2359304 | tf_op jit(solution)/shard_map/ppermute | solution.py:300
  123.3 2.3 %collective-permute-start.13 = (s32[8]{0:T(128)S(1)}, s32[8]{0:T(128)S(1)}, u32[]{:S(2)}, u32[]{:S(2)}) collective-permute-start(s32[8]{0:T(128)S(1)} %copy-done.3), channel_id=1, source_target_pairs={{0,8},{8,0},{1,9},{9,1},{2,10},{10,2},{3,11},{11,3},{4,12},{12,4},... | collective-permute-start | bytes 104 | tf_op jit(solution)/shard_map/ppermute | solution.py:300
  125.6 6.2 %copy-start.1 = (bf16[640,512]{1,0:T(8,128)(2,1)S(1)}, bf16[640,512]{1,0:T(8,128)(2,1)}, u32[]{:S(2)}) copy-start(bf16[640,512]{1,0:T(8,128)(2,1)} %param.9) | copy-start | bytes 1966084

commit v9 on v8

--- a/solution.py
+++ b/solution.py
@@ -179,16 +179,36 @@
         c.wait()
 
 
-def adapter_kernel(count, down_chunks, xs_ref, g_ref, pieces, _, out_ref, lifted_ref, up_panel):
+def adapter_kernel(
+    count, down_chunks, xs_from, g_from, pieces_from, after, out_to, lifted_ref,
+    up_panel, xs_ref, g_ref, pieces, out_ref, sems,
+):
+    del after
     rows = g_ref.shape[0]
     across = g_ref.shape[1] // LANES
+    fetch_g = pltpu.make_async_copy(g_from, g_ref, sems.at[3, 0])
+    fetch = [
+        (
+            pltpu.make_async_copy(pieces_from.at[t], pieces.at[t], sems.at[0, t]),
+            pltpu.make_async_copy(xs_from.at[t], xs_ref.at[t], sems.at[1, t]),
+        )
+        for t in range(count)
+    ]
+    leave = [pltpu.make_async_copy(out_ref.at[t], out_to.at[t], sems.at[2, t]) for t in range(count)]
+    for panel_copy, x_copy in fetch:
+        panel_copy.start()
+        x_copy.start()
+    fetch_g.start()
     total = jnp.zeros((2 * rows, LANES), jnp.float32)
     for t in range(count):
+        for copy in fetch[t]:
+            copy.wait()
         total += dot(xs_ref[t], pieces[t, :down_chunks])
         for c in range(across):
             block = pieces[t, down_chunks + 8 * c:down_chunks + 8 * c + 8, :].astype(jnp.float32)
             up_panel[8 * t:8 * t + 8, c * LANES:(c + 1) * LANES] = block
             up_panel[R + 8 * t:R + 8 * t + 8, c * LANES:(c + 1) * LANES] = block
+    fetch_g.wait()
     panel = up_panel[...].astype(jnp.bfloat16)
     left = lax.broadcasted_iota(jnp.int32, (rows, LANES), 1) < R
     inner = total[:rows] + pltpu.roll(total[rows:], R, 1)
@@ -206,6 +226,9 @@
             [up_term[8 * t:8 * t + 8, c * LANES:(c + 1) * LANES] for c in range(across)], axis=0
         )
         out_ref[t, down_chunks:] = up_part.astype(jnp.bfloat16)
+        leave[t].start()
+    for copy in leave:
+        copy.wait()
 
 
 def scatter_kernel(count, down_chunks, up_chunks, first_row, rows_here, rows_core, *rest):
@@ -271,14 +294,22 @@
 
 
 def base_kernel(where, *refs):
-    x_refs, out_refs = refs[:4], refs[-4:]
-    outer, rows, _ = x_refs[0].shape
-    width = refs[4].shape[1]
+    x_from, w_from, out_refs = refs[:4], refs[4:-8], refs[-7:-3]
+    x_buf, w_buf, sems = refs[-3:]
+    outer, rows, _ = x_from[0].shape
+    width = w_buf.shape[2]
+    fetch_x = [pltpu.make_async_copy(ref, x_buf.at[b], sems.at[0, b]) for b, ref in enumerate(x_from)]
+    fetch_w = [pltpu.make_async_copy(ref, w_buf.at[b], sems.at[1, b]) for b, ref in enumerate(w_from)]
+    for copy in fetch_x + fetch_w:
+        copy.start()
+    for copy in fetch_x:
+        copy.wait()
     for h in range(2):
         total = 0.0
         for k in range(outer):
-            left = jnp.concatenate([ref[where[0] ^ k] for ref in x_refs], axis=0)
-            total += dot(left, refs[4 + h * outer + k][...])
+            fetch_w[h * outer + k].wait()
+            left = jnp.concatenate([x_buf[b, where[k]] for b in range(4)], axis=0)
+            total += dot(left, w_buf[h * outer + k])
         for b, ref in enumerate(out_refs):
             ref[:, h * width:(h + 1) * width] = total[b * rows:(b + 1) * rows]
 
@@ -307,11 +338,11 @@
         in_specs=[SMEM, SMEM], out_specs=VMEM, name="own_row",
     )(block_adapter, adapter_slot)
     asked = lax.all_to_all(row, "tensor", 0, 0)
-    split_from, row = lax.optimization_barrier((tokens, row))
 
     width = frozen_value.shape[1] // parts
     half = lax.dynamic_slice_in_dim(frozen_value, part * width, width, axis=1)
-    quarter = [half] + [exchange(half, 2 * k) for k in range(1, outer)]
+    split_from, half, asked = lax.optimization_barrier((tokens, half, asked))
+    near = exchange(half, 2)
 
     block = jax.ShapeDtypeStruct((outer, token_rows, slice_width), jnp.bfloat16)
     token = jax.ShapeDtypeStruct((1,), jnp.int32)
@@ -342,11 +373,14 @@
         cost_estimate=cost(read=40 << 20),
         name="pick_panels",
     )(asked, tiles(down_store), tiles(up_store))
-    sent, quarter = lax.optimization_barrier((sent, quarter))
+    sent, near, half, x_far, y_mine = lax.optimization_barrier((sent, near, half, x_far, y_mine))
     panels = lax.all_to_all(sent, "tensor", 0, 0)
     rows_core = other_core(rows)
-    x_far, y_mine, picked = lax.optimization_barrier((x_far, y_mine, rows))
     y_far = other_part(x_far)
+    middle = [(t, t ^ 6) for t in range(group) if t // 2 in (1, 2)]
+    ends = [(t, t ^ 2) for t in range(group) if t // 2 in (1, 2)]
+    passed = [lax.ppermute(w, "tensor", middle) for w in (half, near)]
+    early_core = [other_core(w) for w in (half, near)]
     pair_from, _ = lax.optimization_barrier((tokens, rows))
     xs = pl.pallas_call(
         interleave_kernel,
@@ -363,30 +397,46 @@
         in_specs=[SMEM], out_specs=(ANY, ANY, SMEM),
         scratch_shapes=[pltpu.VMEM((up_chunks, 8, 1, LANES), jnp.float32), pltpu.SemaphoreType.DMA((2,))],
         compiler_params=LIMIT, cost_estimate=cost(read=28 << 20), name="clear_rows",
-    )(picked)
-    quarter_core = [other_core(w) for w in quarter]
-    panels, y_far, quarter_core = lax.optimization_barrier((panels, y_far, quarter_core))
+    )(rows)
+    panels, passed, y_far, early_core = lax.optimization_barrier((panels, passed, y_far, early_core))
 
     terms, lifted = pl.pallas_call(
         functools.partial(adapter_kernel, group, down_chunks),
         out_shape=(pieces, jax.ShapeDtypeStruct((token_rows, VALUE_OUTPUTS), jnp.float32)),
-        in_specs=[VMEM] * 3 + [SMEM],
-        out_specs=(VMEM, VMEM),
-        scratch_shapes=[pltpu.VMEM((2 * R, VALUE_OUTPUTS), jnp.float32)],
-        compiler_params=LIMIT,
+        in_specs=[ANY] * 3 + [SMEM],
+        out_specs=(ANY, VMEM),
+        scratch_shapes=[
+            pltpu.VMEM((2 * R, VALUE_OUTPUTS), jnp.float32),
+            pltpu.VMEM(xs.shape, jnp.bfloat16),
+            pltpu.VMEM(cotangent.shape, jnp.bfloat16),
+            pltpu.VMEM(pieces.shape, jnp.bfloat16),
+            pltpu.VMEM(pieces.shape, jnp.bfloat16),
+            pltpu.SemaphoreType.DMA((4, group)),
+        ],
+        compiler_params=WIDE,
         cost_estimate=cost(flops=3 << 30, read=8 << 20),
         name="adapter",
     )(xs, cotangent, panels, cleared)
+    _, passed = lax.optimization_barrier((terms, passed))
+    inside = (z == 1) | (z == 2)
+    far = [jnp.where(inside, w, lax.ppermute(w, "tensor", ends)) for w in passed]
+    quarters = [half, near] + far + early_core + [other_core(w) for w in far]
+    source = jnp.stack([z, z ^ 1, jnp.where(z < 2, 2, 1), jnp.where(z < 2, 3, 0)])
     sums = jax.ShapeDtypeStruct((token_rows, parts * width), jnp.float32)
     own, to_part, to_inner, to_both = pl.pallas_call(
         base_kernel,
         out_shape=[sums] * 4,
-        in_specs=[SMEM] + [VMEM] * (4 + 2 * outer) + [ANY],
+        in_specs=[SMEM] + [ANY] * (5 + 2 * outer),
         out_specs=[VMEM] * 4,
-        compiler_params=LIMIT,
+        scratch_shapes=[
+            pltpu.VMEM((4,) + block.shape, jnp.bfloat16),
+            pltpu.VMEM((2 * outer, slice_width, width), jnp.bfloat16),
+            pltpu.SemaphoreType.DMA((2, 2 * outer)),
+        ],
+        compiler_params=WIDE,
         cost_estimate=cost(flops=4 << 30, read=8 << 20),
         name="frozen_part",
-    )(z[None], x_mine, y_mine, x_far, y_far, *quarter, *quarter_core, terms)
+    )(source, x_mine, y_mine, x_far, y_far, *quarters, terms)
     opposite = [(a * group + t, (parts - 1 - a) * group + (t ^ 1)) for a in range(parts) for t in range(group)]
     back = lax.all_to_all(terms, "tensor", 0, 0)
     arrived = (exchange(to_inner, 1), other_part(to_part), lax.ppermute(to_both, ("parts", "tensor"), opposite))

time: 133 us -> 136 us (1.023)
  blocking collectives: 26.4 us -> 0 us
  waiting for transfers between devices: 32.7 us -> 48.9 us
  starting transfers between devices: 24.3 us -> 37.9 us
  local copies, waits for them, and re-layouts: 15.5 us -> 5.61 us
  Pallas kernels: 30.5 us -> 38.7 us
  other arithmetic: 0.89 us -> 2.56 us
    all_to_all x1 -> x0, blocking collectives: 26.4 us -> none  [fast_body(): asked = lax.all_to_all(row, 'tensor', 0, 0)]
    ppermute x0 -> x4, waiting for transfers between devices: none -> 19.3 us  [the longest x2 19.3 us: fast_body(): lax.ppermute(w, 'tensor', ends)]
    ppermute x5 -> x3, waiting for transfers between devices: 27.2 us -> 12.6 us  [exchange(): return lax.ppermute(value, 'tensor', [(t, t ^ s) for t in range(group)])]
    unnamed x42 -> x38, local copies, waits for them, and re-layouts: 15.5 us -> 5.58 us
    all_to_all x1, starting transfers between devices: 4.54 us -> 14.1 us  [fast_body(): back = lax.all_to_all(terms, 'tensor', 0, 0)]
    all_to_all x0 -> x1, starting transfers between devices: none -> 7.25 us  [fast_body(): asked = lax.all_to_all(row, 'tensor', 0, 0)]
    ppermute x5 -> x3, starting transfers between devices: 9.92 us -> 3.05 us  [exchange(): return lax.ppermute(value, 'tensor', [(t, t ^ s) for t in range(group)])]
    ppermute x3, waiting for transfers between devices: 0.01 us -> 6.74 us  [other_part(): lax.ppermute(value, 'parts', [(a, parts - 1 - a) for a in range(parts)])]
  transfers between devices with their start and end apart: 17 -> 20, of which waited for: 4 -> 10; matrix products, arithmetic and copies ran while one was open for 1% -> 2% of each run, Pallas kernels for 16% -> 18%
where the time goes in v9:
time: 136 us; the launch traced here: 135 us
  waiting for transfers between devices  48.9 us (36%)
  Pallas kernels  38.7 us (28%)
  starting transfers between devices  37.9 us (28%)
  local copies, waits for them, and re-layouts  5.61 us (4%)
  other arithmetic  2.56 us (2%)
  between operations  1.87 us (1%)
    ppermute x2, waiting for transfers between devices, fast_body(): lax.ppermute(w, 'tensor', ends)  19.3 us
    all_to_all x1, starting transfers between devices, fast_body(): back = lax.all_to_all(terms, 'tensor', 0, 0)  14.1 us
    ppermute x3, waiting for transfers between devices, exchange(): return lax.ppermute(value, 'tensor', [(t, t ^ s) for t in range(group)])  12.6 us
    pallas_call x1, Pallas kernels, fast_body(): pl.pallas_call(zero_kernel, out_shape=(down_shape, up_shape, token), in_s...  9.48 us
    pallas_call x1, Pallas kernels, fast_body(): pl.pallas_call(base_kernel, out_shape=[sums] * 4, in_specs=[SMEM] + [ANY]...  7.27 us
    all_to_all x1, starting transfers between devices, fast_body(): asked = lax.all_to_all(row, 'tensor', 0, 0)  7.25 us
    pallas_call x1, Pallas kernels, fast_body(): pl.pallas_call(functools.partial(scatter_kernel, 2 * group, down_chunks,...  7.06 us
    ppermute x3, waiting for transfers between devices, other_part(): lax.ppermute(value, 'parts', [(a, parts - 1 - a) for a in range(parts)])  6.74 us
  transfers between devices with their start and end apart: 20, of which 10 were waited for; matrix products, arithmetic and copies ran while one was open for 2% of the time, Pallas kernels for 18%

profile of v9, /device:TPU:0, one launch (start us, length us, event | category | flops | bytes accessed | tf_op | source)
XLA Modules:
  0.0 135.5 jit_solution(827737223816691579)
XLA Ops:
  0.6 0.0 copy-start
  1.4 1.3 own_row.1
  2.6 7.3 %all-to-all-start = ((s32[8,1,128]{2,1,0:T(1,128)}), s32[8,1,128]{2,1,0:T(1,128)S(1)}, u32[]{:S(2)}, u32[]{:S(2)}) async-start(s32[8,1,128]{2,1,0:T(1,128)} %own_row.1), calls=%async_computation | async-start | bytes 8192 | tf_op jit(solution)/shard_map/all_to_all | solution.py:340
  10.0 6.3 %all-to-all-done.asked = s32[8,1,128]{2,1,0:T(1,128)S(1)} async-done(((s32[8,1,128]{2,1,0:T(1,128)}), s32[8,1,128]{2,1,0:T(1,128)S(1)}, u32[]{:S(2)}, u32[]{:S(2)}) %all-to-all-start) | async-done | bytes 4128 | tf_op jit(solution)/shard_map/all_to_all | solution.py:340
  16.3 1.3 copy-done.2
  17.6 0.1 split_tokens.1
  17.7 0.6 collective-permute-start.1
  18.3 1.5 %collective-permute-start.2 = (bf16[4,128,640]{2,1,0:T(8,128)(2,1)S(1)}, bf16[4,128,640]{2,1,0:T(8,128)(2,1)}, u32[]{:S(2)}, u32[]{:S(2)}) collective-permute-start(bf16[4,128,640]{2,1,0:T(8,128)(2,1)S(1)} %get-tuple-element.40.refs_0_), channel_id=1, source_target_pairs={{0,16},{16,0},{1,17},{17,1},{2,18},{18,2},{3,19},{19,3},{4,20},{20... | collective-permute-start | bytes 1966088 | tf_op jit(solution)/shard_map/ppermute | solution.py:334
  19.9 0.6 collective-permute-start
  20.4 0.0 copy-done.13
  20.4 5.7 %pick_panels.1 = (bf16[8,384,128]{2,1,0:T(8,128)(2,1)}, s32[8]{0:T(128)}) custom-call(s32[8,1,128]{2,1,0:T(1,128)} %copy-done.13, bf16[32,320,8,128]{3,2,1,0:T(8,128)(2,1)} %bitcast.23, bf16[32,64,8,128]{3,2,1,0:T(8,128)(2,1)} %bitcast.24), custom_call_target="tpu_custom_call" | custom-call | bytes 41943040 | tf_op jit(solution)/shard_map/pick_panels/pallas_call | solution.py:360
  26.2 0.0 copy-done.6
  26.2 1.1 collective-permute-done.refs_5_
  27.3 5.6 %collective-permute-done.1.refs_2_ = bf16[4,128,640]{2,1,0:T(8,128)(2,1)} collective-permute-done((bf16[4,128,640]{2,1,0:T(8,128)(2,1)S(1)}, bf16[4,128,640]{2,1,0:T(8,128)(2,1)}, u32[]{:S(2)}, u32[]{:S(2)}) %collective-permute-start.1) | collective-permute-done | bytes 655392 | tf_op jit(solution)/shard_map/ppermute | solution.py:328
  32.9 0.3 collective-permute-done.2.refs_1_
  33.2 3.5 %all-to-all-start.1 = ((bf16[8,384,128]{2,1,0:T(8,128)(2,1)}), bf16[8,384,128]{2,1,0:T(8,128)(2,1)S(1)}, u32[]{:S(2)}, u32[]{:S(2)}) async-start(bf16[8,384,128]{2,1,0:T(8,128)(2,1)} %get-tuple-element.47), calls=%async_computation.1 | async-start | bytes 1572864 | tf_op jit(solution)/shard_map/all_to_all | solution.py:377
  36.8 1.6 %collective-permute-start.5 = (bf16[4,128,640]{2,1,0:T(8,128)(2,1)}, bf16[4,128,640]{2,1,0:T(8,128)(2,1)}, u32[]{:S(2)}, u32[]{:S(2)}) collective-permute-start(bf16[4,128,640]{2,1,0:T(8,128)(2,1)} %collective-permute-done.1.refs_2_), channel_id=1, source_target_pairs={{0,16},{16,0},{1,17},{17,1},{2,18},{18,2},{3,19},{19,3},{4,20},{20... | collective-permute-start | bytes 1966088 | tf_op jit(solution)/shard_map/ppermute | solution.py:334
  38.4 0.0 collective-permute-start.6
  38.4 0.7 collective-permute-start.3
  39.0 0.6 collective-permute-start.7
  39.6 0.7 collective-permute-start.4
  40.3 0.6 copy-done.4
  40.9 9.5 %clear_rows.1 = (f32[16,320,8,1,128]{4,3,2,1,0:T(1,128)}, f32[16,64,8,1,128]{4,3,2,1,0:T(1,128)}, s32[1]{0:T(128)}) custom-call(s32[8]{0:T(128)S(1)} %copy-done.4), custom_call_target="tpu_custom_call" | custom-call | bytes 29360128 | tf_op jit(solution)/shard_map/clear_rows/pallas_call | solution.py:395
  50.4 1.8 %pair_columns.1.xs_from = bf16[8,256,320]{2,1,0:T(8,128)(2,1)S(1)} custom-call(bf16[128,5120]{1,0:T(8,128)(2,1)S(1)} %copy-done.3), custom_call_target="tpu_custom_call" | custom-call | flops 2147483648 | bytes 4194304 | tf_op jit(solution)/shard_map/pair_columns/pallas_call | solution.py:385
  52.2 1.2 copy-done.7
  53.4 0.0 collective-permute-done.6.refs_8_
  53.4 0.0 collective-permute-done.3
  53.4 0.0 collective-permute-done.7.refs_9_
  53.4 0.0 copy-start.16
  53.4 0.0 collective-permute-done.4
  53.4 0.7 copy-done.15
  54.1 0.1 copy-done.16
  54.2 0.0 collective-permute-done.5.refs_3_
  54.2 3.0 %all-to-all-done.1.pieces_from = bf16[8,384,128]{2,1,0:T(8,128)(2,1)S(1)} async-done(((bf16[8,384,128]{2,1,0:T(8,128)(2,1)}), bf16[8,384,128]{2,1,0:T(8,128)(2,1)S(1)}, u32[]{:S(2)}, u32[]{:S(2)}) %all-to-all-start.1) | async-done | bytes 786464 | tf_op jit(solution)/shard_map/all_to_all | solution.py:377
  57.2 0.9 copy-done.8
  58.1 5.9 %adapter.1 = (bf16[8,384,128]{2,1,0:T(8,128)(2,1)}, f32[128,1024]{1,0:T(8,128)}) custom-call(bf16[8,256,320]{2,1,0:T(8,128)(2,1)} %copy-done.7, bf16[128,1024]{1,0:T(8,128)(2,1)} %g_from.1, bf16[8,384,128]{2,1,0:T(8,128)(2,1)} %copy-done.8, s32[1]{0:T(128)} %get-tuple-element.54.after), custom_call_target="tpu_custom_call" | custom-call | flops 3221225472 | bytes 8388608 | tf_op jit(solution)/shard_map/adapter/pallas_call | solution.py:403
  64.0 1.3 collective-permute-start.8
  65.3 1.3 collective-permute-start.9
  66.7 14.1 %all-to-all-start.2 = ((bf16[8,384,128]{2,1,0:T(8,128)(2,1)}), bf16[8,384,128]{2,1,0:T(8,128)(2,1)S(1)}, u32[]{:S(2)}, u32[]{:S(2)}) async-start(bf16[8,384,128]{2,1,0:T(8,128)(2,1)} %get-tuple-element.55.refs_12_), calls=%async_computation.2 | async-start | bytes 1572864 | tf_op jit(solution)/shard_map/all_to_all | solution.py:441
  80.8 6.9 %collective-permute-done.8 = bf16[640,256]{1,0:T(8,128)(2,1)S(1)} collective-permute-done((bf16[640,256]{1,0:T(8,128)(2,1)S(1)}, bf16[640,256]{1,0:T(8,128)(2,1)S(1)}, u32[]{:S(2)}, u32[]{:S(2)}) %collective-permute-start.8) | collective-permute-done | bytes 327712 | tf_op jit(solution)/shard_map/ppermute | solution.py:422
  87.7 0.0 copy-start.10
  87.7 0.1 collective-permute-start.10
  87.7 12.5 %collective-permute-done.9 = bf16[640,256]{1,0:T(8,128)(2,1)S(1)} collective-permute-done((bf16[640,256]{1,0:T(8,128)(2,1)S(1)}, bf16[640,256]{1,0:T(8,128)(2,1)S(1)}, u32[]{:S(2)}, u32[]{:S(2)}) %collective-permute-start.9) | collective-permute-done | bytes 327712 | tf_op jit(solution)/shard_map/ppermute | solution.py:422
  100.3 0.1 collective-permute-start.11
  100.4 0.7 pad_add_fusion.where
  101.0 0.0 collective-permute-done.10.refs_10_
  101.0 0.9 collective-permute-done.11.refs_11_
  102.0 0.0 copy-done.10
  102.0 0.7 copy-done.18
  102.7 7.3 %frozen_part.1 = (f32[128,512]{1,0:T(8,128)}, f32[128,512]{1,0:T(8,128)}, f32[128,512]{1,0:T(8,128)}, f32[128,512]{1,0:T(8,128)}) custom-call(s32[4]{0:T(128)} %pad_add_fusion.where, bf16[4,128,640]{2,1,0:T(8,128)(2,1)} %copy-done.6, bf16[4,128,640]{2,1,0:T(8,128)(2,1)} %collective-permute-done.2.refs_1_, ...), custom_call_target="tpu_custom_call" | custom-call | flops 4294967296 | bytes 8388608 | tf_op jit(solution)/shard_map/frozen_part/pallas_call | solution.py:426
  110.0 1.8 %collective-permute-start.12 = (f32[128,512]{1,0:T(8,128)}, f32[128,512]{1,0:T(8,128)S(1)}, u32[]{:S(2)}, u32[]{:S(2)}) collective-permute-start(f32[128,512]{1,0:T(8,128)} %get-tuple-element.63), channel_id=1, source_target_pairs={{0,1},{1,0},{2,3},{3,2},{4,5},{5,4},{6,7},{7,6},{8,9},{9,8},{10,11... | collective-permute-start | bytes 786440 | tf_op jit(solution)/shard_map/ppermute | solution.py:328
  111.8 1.5 %collective-permute-start.13 = (f32[128,512]{1,0:T(8,128)}, f32[128,512]{1,0:T(8,128)S(1)}, u32[]{:S(2)}, u32[]{:S(2)}) collective-permute-start(f32[128,512]{1,0:T(8,128)} %get-tuple-element.64), channel_id=1, source_target_pairs={{0,16},{16,0},{1,17},{17,1},{2,18},{18,2},{3,19},{19,3},{4,20},{20... | collective-permute-start | bytes 786440 | tf_op jit(solution)/shard_map/ppermute | solution.py:334
  113.4 0.2 collective-permute-start.14
  113.5 5.9 %collective-permute-done.12 = f32[128,512]{1,0:T(8,128)S(1)} collective-permute-done((f32[128,512]{1,0:T(8,128)}, f32[128,512]{1,0:T(8,128)S(1)}, u32[]{:S(2)}, u32[]{:S(2)}) %collective-permute-start.12) | collective-permute-done | bytes 262176 | tf_op jit(solution)/shard_map/ppermute | solution.py:328
  119.4 6.5 %collective-permute-done.13 = f32[128,512]{1,0:T(8,128)S(1)} collective-permute-done((f32[128,512]{1,0:T(8,128)}, f32[128,512]{1,0:T(8,128)S(1)}, u32[]{:S(2)}, u32[]{:S(2)}) %collective-permute-start.13) | collective-permute-done | bytes 262176 | tf_op jit(solution)/shard_map/ppermute | solution.py:334
  125.8 0.0 collective-permute-done.14
  125.8 0.0 all-to-all-done.2.rest_0_
  125.9 0.0 collective-permute-start.16
  125.9 0.5 collective-permute-start.15
  126.4 1.0 add.19
  127.5 0.8 fusion
  128.2 0.0 collective-permute-done.15.rows_core
  128.2 0.0 collective-permute-done.16.rest_1_
  128.2 7.1 %place_rows.1 = (f32[16,320,8,1,128]{4,3,2,1,0:T(1,128)}, f32[16,64,8,1,128]{4,3,2,1,0:T(1,128)}) custom-call(s32[1]{0:T(128)} %bitcast.9.first_row, s32[8]{0:T(128)S(1)} %copy-done.5, s32[8]{0:T(128)S(1)} %collective-permute-done.15.rows_core, bf16[8,384,128]{2,1,0:T(8,128)(2,1)S(1)} %all-to-all-done.2.rest_0_, ...), custom_call_target="tpu_custom_call", output_to_operand_aliasing={{0}: (5, {}), {1}: (6, {})} | custom-call | bytes 16777216 | tf_op jit(solution)/shard_map/place_rows/pallas_call | solution.py:446
  (30 shorter events, 0.2 us)
Async XLA Ops:
  0.6 9.3 %copy-start = (bf16[640,512]{1,0:T(8,128)(2,1)S(1)}, bf16[640,512]{1,0:T(8,128)(2,1)}, u32[]{:S(2)}) copy-start(bf16[640,512]{1,0:T(8,128)(2,1)} %param.9) | copy-start | bytes 1966084
  2.6 13.6 %all-to-all-start = ((s32[8,1,128]{2,1,0:T(1,128)}), s32[8,1,128]{2,1,0:T(1,128)S(1)}, u32[]{:S(2)}, u32[]{:S(2)}) async-start(s32[8,1,128]{2,1,0:T(1,128)} %own_row.1), calls=%async_computation | async-start | bytes 8192 | tf_op jit(solution)/shard_map/all_to_all | solution.py:340
  9.9 28.4 %copy-start.12 = (bf16[640,256]{1,0:T(8,128)(2,1)}, bf16[640,256]{1,0:T(8,128)(2,1)S(1)}, u32[]{:S(2)}) copy-start(bf16[640,256]{1,0:T(8,128)(2,1)S(1)} %constant_dynamic-slice_fusion.refs_4_) | copy-start | bytes 983044
  16.3 4.2 %copy-start.13 = (s32[8,1,128]{2,1,0:T(1,128)}, s32[8,1,128]{2,1,0:T(1,128)S(1)}, u32[]{:S(2)}) copy-start(s32[8,1,128]{2,1,0:T(1,128)S(1)} %all-to-all-done.asked) | copy-start | bytes 12292
  16.3 1.3 copy-start.2
  17.7 8.5 %copy-start.6 = (bf16[4,128,640]{2,1,0:T(8,128)(2,1)}, bf16[4,128,640]{2,1,0:T(8,128)(2,1)S(1)}, u32[]{:S(2)}) copy-start(bf16[4,128,640]{2,1,0:T(8,128)(2,1)S(1)} %get-tuple-element.40.refs_0_) | copy-start | bytes 1966084
  17.7 15.2 %collective-permute-start.1 = (bf16[4,128,640]{2,1,0:T(8,128)(2,1)S(1)}, bf16[4,128,640]{2,1,0:T(8,128)(2,1)}, u32[]{:S(2)}, u32[]{:S(2)}) collective-permute-start(bf16[4,128,640]{2,1,0:T(8,128)(2,1)S(1)} %get-tuple-element.44), channel_id=1, source_target_pairs={{0,1},{1,0},{2,3},{3,2},{4,5},{5,4},{6,7},{7,6},{8,9},{9,8},{10,11... | collective-permute-start | bytes 1966088 | tf_op jit(solution)/shard_map/ppermute | solution.py:328
  18.3 14.9 %collective-permute-start.2 = (bf16[4,128,640]{2,1,0:T(8,128)(2,1)S(1)}, bf16[4,128,640]{2,1,0:T(8,128)(2,1)}, u32[]{:S(2)}, u32[]{:S(2)}) collective-permute-start(bf16[4,128,640]{2,1,0:T(8,128)(2,1)S(1)} %get-tuple-element.40.refs_0_), channel_id=1, source_target_pairs={{0,16},{16,0},{1,17},{17,1},{2,18},{18,2},{3,19},{19,3},{4,20},{20... | collective-permute-start | bytes 1966088 | tf_op jit(solution)/shard_map/ppermute | solution.py:334
  19.9 7.5 %collective-permute-start = (bf16[640,256]{1,0:T(8,128)(2,1)S(1)}, bf16[640,256]{1,0:T(8,128)(2,1)S(1)}, u32[]{:S(2)}, u32[]{:S(2)}) collective-permute-start(bf16[640,256]{1,0:T(8,128)(2,1)S(1)} %constant_dynamic-slice_fusion.refs_4_), channel_id=1, source_target_pairs={{0,2},{1,3},{2,0},{3,1},{4,6},{5,7},{6,4},{7,5},{8,10},{9,11},{10,... | collective-permute-start | bytes 983048 | tf_op jit(solution)/shard_map/ppermute | solution.py:328
  20.4 29.9 %copy-start.3 = (bf16[128,5120]{1,0:T(8,128)(2,1)S(1)}, bf16[128,5120]{1,0:T(8,128)(2,1)}, u32[]{:S(2)}) copy-start(bf16[128,5120]{1,0:T(8,128)(2,1)} %x_ref.1) | copy-start | bytes 3932164
  27.3 24.9 %copy-start.14 = (bf16[640,256]{1,0:T(8,128)(2,1)}, bf16[640,256]{1,0:T(8,128)(2,1)S(1)}, u32[]{:S(2)}) copy-start(bf16[640,256]{1,0:T(8,128)(2,1)S(1)} %collective-permute-done.refs_5_) | copy-start | bytes 983044
  33.2 24.0 %all-to-all-start.1 = ((bf16[8,384,128]{2,1,0:T(8,128)(2,1)}), bf16[8,384,128]{2,1,0:T(8,128)(2,1)S(1)}, u32[]{:S(2)}, u32[]{:S(2)}) async-start(bf16[8,384,128]{2,1,0:T(8,128)(2,1)} %get-tuple-element.47), calls=%async_computation.1 | async-start | bytes 1572864 | tf_op jit(solution)/shard_map/all_to_all | solution.py:377
  36.8 17.5 %collective-permute-start.5 = (bf16[4,128,640]{2,1,0:T(8,128)(2,1)}, bf16[4,128,640]{2,1,0:T(8,128)(2,1)}, u32[]{:S(2)}, u32[]{:S(2)}) collective-permute-start(bf16[4,128,640]{2,1,0:T(8,128)(2,1)} %collective-permute-done.1.refs_2_), channel_id=1, source_target_pairs={{0,16},{16,0},{1,17},{17,1},{2,18},{18,2},{3,19},{19,3},{4,20},{20... | collective-permute-start | bytes 1966088 | tf_op jit(solution)/shard_map/ppermute | solution.py:334
  38.4 15.0 %collective-permute-start.6 = (bf16[640,256]{1,0:T(8,128)(2,1)S(1)}, bf16[640,256]{1,0:T(8,128)(2,1)S(1)}, u32[]{:S(2)}, u32[]{:S(2)}) collective-permute-start(bf16[640,256]{1,0:T(8,128)(2,1)S(1)} %constant_dynamic-slice_fusion.refs_4_), channel_id=1, source_target_pairs={{0,8},{8,0},{1,9},{9,1},{2,10},{10,2},{3,11},{11,3},{4,12},{12,4},... | collective-permute-start | bytes 983048 | tf_op jit(solution)/shard_map/ppermute | solution.py:331
  38.4 15.0 %collective-permute-start.3 = (bf16[640,256]{1,0:T(8,128)(2,1)S(1)}, bf16[640,256]{1,0:T(8,128)(2,1)S(1)}, u32[]{:S(2)}, u32[]{:S(2)}) collective-permute-start(bf16[640,256]{1,0:T(8,128)(2,1)S(1)} %constant_dynamic-slice_fusion.refs_4_), channel_id=1, source_target_pairs={{2,4},{3,5},{4,2},{5,3},{10,12},{11,13},{12,10},{13,11},{18,20},{1... | collective-permute-start | bytes 983048 | tf_op jit(solution)/shard_map/ppermute | solution.py:382
  39.0 14.4 %collective-permute-start.7 = (bf16[640,256]{1,0:T(8,128)(2,1)S(1)}, bf16[640,256]{1,0:T(8,128)(2,1)S(1)}, u32[]{:S(2)}, u32[]{:S(2)}) collective-permute-start(bf16[640,256]{1,0:T(8,128)(2,1)S(1)} %collective-permute-done.refs_5_), channel_id=1, source_target_pairs={{0,8},{8,0},{1,9},{9,1},{2,10},{10,2},{3,11},{11,3},{4,12},{12,4},... | collective-permute-start | bytes 983048 | tf_op jit(solution)/shard_map/ppermute | solution.py:331
  39.6 13.8 %collective-permute-start.4 = (bf16[640,256]{1,0:T(8,128)(2,1)S(1)}, bf16[640,256]{1,0:T(8,128)(2,1)S(1)}, u32[]{:S(2)}, u32[]{:S(2)}) collective-permute-start(bf16[640,256]{1,0:T(8,128)(2,1)S(1)} %collective-permute-done.refs_5_), channel_id=1, source_target_pairs={{2,4},{3,5},{4,2},{5,3},{10,12},{11,13},{12,10},{13,11},{18,20},{1... | collective-permute-start | bytes 983048 | tf_op jit(solution)/shard_map/ppermute | solution.py:382
  40.3 0.6 copy-start.4
  52.2 1.2 copy-start.7
  53.4 0.7 copy-start.15
  53.4 0.8 copy-start.16
  57.2 0.9 copy-start.8
  64.0 23.6 %collective-permute-start.8 = (bf16[640,256]{1,0:T(8,128)(2,1)S(1)}, bf16[640,256]{1,0:T(8,128)(2,1)S(1)}, u32[]{:S(2)}, u32[]{:S(2)}) collective-permute-start(bf16[640,256]{1,0:T(8,128)(2,1)S(1)} %collective-permute-done.3), channel_id=1, source_target_pairs={{2,0},{3,1},{4,6},{5,7},{10,8},{11,9},{12,14},{13,15},{18,16},{19,... | collective-permute-start | bytes 983048 | tf_op jit(solution)/shard_map/ppermute | solution.py:422
  65.3 34.9 %collective-permute-start.9 = (bf16[640,256]{1,0:T(8,128)(2,1)S(1)}, bf16[640,256]{1,0:T(8,128)(2,1)S(1)}, u32[]{:S(2)}, u32[]{:S(2)}) collective-permute-start(bf16[640,256]{1,0:T(8,128)(2,1)S(1)} %collective-permute-done.4), channel_id=1, source_target_pairs={{2,0},{3,1},{4,6},{5,7},{10,8},{11,9},{12,14},{13,15},{18,16},{19,... | collective-permute-start | bytes 983048 | tf_op jit(solution)/shard_map/ppermute | solution.py:422
  66.7 59.2 %all-to-all-start.2 = ((bf16[8,384,128]{2,1,0:T(8,128)(2,1)}), bf16[8,384,128]{2,1,0:T(8,128)(2,1)S(1)}, u32[]{:S(2)}, u32[]{:S(2)}) async-start(bf16[8,384,128]{2,1,0:T(8,128)(2,1)} %get-tuple-element.55.refs_12_), calls=%async_computation.2 | async-start | bytes 1572864 | tf_op jit(solution)/shard_map/all_to_all | solution.py:441
  87.7 14.3 %copy-start.10 = (bf16[640,256]{1,0:T(8,128)(2,1)}, bf16[640,256]{1,0:T(8,128)(2,1)S(1)}, u32[]{:S(2)}) copy-start(bf16[640,256]{1,0:T(8,128)(2,1)S(1)} %broadcast_select_fusion.1.refs_6_) | copy-start | bytes 983044
  87.7 13.3 %collective-permute-start.10 = (bf16[640,256]{1,0:T(8,128)(2,1)S(1)}, bf16[640,256]{1,0:T(8,128)(2,1)S(1)}, u32[]{:S(2)}, u32[]{:S(2)}) collective-permute-start(bf16[640,256]{1,0:T(8,128)(2,1)S(1)} %broadcast_select_fusion.1.refs_6_), channel_id=1, source_target_pairs={{0,8},{8,0},{1,9},{9,1},{2,10},{10,2},{3,11},{11,3},{4,12},{12,4},... | collective-permute-start | bytes 983048 | tf_op jit(solution)/shard_map/ppermute | solution.py:331
  100.3 1.7 %copy-start.11 = (bf16[640,256]{1,0:T(8,128)(2,1)}, bf16[640,256]{1,0:T(8,128)(2,1)S(1)}, u32[]{:S(2)}) copy-start(bf16[640,256]{1,0:T(8,128)(2,1)S(1)} %broadcast_select_fusion.refs_7_) | copy-start | bytes 983044
  100.3 1.7 %collective-permute-start.11 = (bf16[640,256]{1,0:T(8,128)(2,1)S(1)}, bf16[640,256]{1,0:T(8,128)(2,1)S(1)}, u32[]{:S(2)}, u32[]{:S(2)}) collective-permute-start(bf16[640,256]{1,0:T(8,128)(2,1)S(1)} %broadcast_select_fusion.refs_7_), channel_id=1, source_target_pairs={{0,8},{8,0},{1,9},{9,1},{2,10},{10,2},{3,11},{11,3},{4,12},{12,4},... | collective-permute-start | bytes 983048 | tf_op jit(solution)/shard_map/ppermute | solution.py:331
  101.0 24.9 %copy-start.5 = (s32[8]{0:T(128)S(1)}, s32[8]{0:T(128)}, u32[]{:S(2)}) copy-start(s32[8]{0:T(128)} %get-tuple-element.51.after_ref.rows_here) | copy-start | bytes 100
  101.0 26.5 %copy-start.9 = (f32[128,1024]{1,0:T(8,128)S(1)}, f32[128,1024]{1,0:T(8,128)}, u32[]{:S(2)}) copy-start(f32[128,1024]{1,0:T(8,128)} %get-tuple-element.69) | copy-start | bytes 1572868
  101.0 0.9 copy-start.17
  102.0 0.7 copy-start.18
  110.0 9.4 %collective-permute-start.12 = (f32[128,512]{1,0:T(8,128)}, f32[128,512]{1,0:T(8,128)S(1)}, u32[]{:S(2)}, u32[]{:S(2)}) collective-permute-start(f32[128,512]{1,0:T(8,128)} %get-tuple-element.63), channel_id=1, source_target_pairs={{0,1},{1,0},{2,3},{3,2},{4,5},{5,4},{6,7},{7,6},{8,9},{9,8},{10,11... | collective-permute-start | bytes 786440 | tf_op jit(solution)/shard_map/ppermute | solution.py:328
  111.8 14.0 %collective-permute-start.13 = (f32[128,512]{1,0:T(8,128)}, f32[128,512]{1,0:T(8,128)S(1)}, u32[]{:S(2)}, u32[]{:S(2)}) collective-permute-start(f32[128,512]{1,0:T(8,128)} %get-tuple-element.64), channel_id=1, source_target_pairs={{0,16},{16,0},{1,17},{17,1},{2,18},{18,2},{3,19},{19,3},{4,20},{20... | collective-permute-start | bytes 786440 | tf_op jit(solution)/shard_map/ppermute | solution.py:334
  113.4 12.5 %collective-permute-start.14 = (f32[128,512]{1,0:T(8,128)}, f32[128,512]{1,0:T(8,128)S(1)}, u32[]{:S(2)}, u32[]{:S(2)}) collective-permute-start(f32[128,512]{1,0:T(8,128)} %get-tuple-element.65), channel_id=1, source_target_pairs={{0,17},{1,16},{2,19},{3,18},{4,21},{5,20},{6,23},{7,22},{16,1},{17... | collective-permute-start | bytes 786440 | tf_op jit(solution)/shard_map/ppermute | solution.py:442
  125.9 2.4 %collective-permute-start.16 = (bf16[8,384,128]{2,1,0:T(8,128)(2,1)S(1)}, bf16[8,384,128]{2,1,0:T(8,128)(2,1)S(1)}, u32[]{:S(2)}, u32[]{:S(2)}) collective-permute-start(bf16[8,384,128]{2,1,0:T(8,128)(2,1)S(1)} %all-to-all-done.2.rest_0_), channel_id=1, source_target_pairs={{0,8},{8,0},{1,9},{9,1},{2,10},{10,2},{3,11},{11,3},{4,12},{12,4},... | collective-permute-start | bytes 2359304 | tf_op jit(solution)/shard_map/ppermute | solution.py:331
  125.9 2.4 %collective-permute-start.15 = (s32[8]{0:T(128)S(1)}, s32[8]{0:T(128)S(1)}, u32[]{:S(2)}, u32[]{:S(2)}) collective-permute-start(s32[8]{0:T(128)S(1)} %copy-done.5), channel_id=1, source_target_pairs={{0,8},{8,0},{1,9},{9,1},{2,10},{10,2},{3,11},{11,3},{4,12},{12,4},... | collective-permute-start | bytes 104 | tf_op jit(solution)/shard_map/ppermute | solution.py:331
  128.2 7.1 %copy-start.1 = (bf16[640,512]{1,0:T(8,128)(2,1)S(1)}, bf16[640,512]{1,0:T(8,128)(2,1)}, u32[]{:S(2)}) copy-start(bf16[640,512]{1,0:T(8,128)(2,1)} %param.9) | copy-start | bytes 1966084

commit v10 on v8

--- a/solution.py
+++ b/solution.py
@@ -271,16 +271,31 @@
 
 
 def base_kernel(where, *refs):
-    x_refs, out_refs = refs[:4], refs[-4:]
-    outer, rows, _ = x_refs[0].shape
-    width = refs[4].shape[1]
+    x_from, w_from, out_refs = refs[:4], refs[4:-8], refs[-7:-3]
+    x_buf, w_buf, sems = refs[-3:]
+    outer, _, rows, depth = x_buf.shape
+    width = w_buf.shape[2]
+    fetch_x = [
+        [pltpu.make_async_copy(ref.at[where[k]], x_buf.at[k, b], sems.at[k, b]) for b, ref in enumerate(x_from)]
+        for k in range(outer)
+    ]
+    fetch_w = [
+        [pltpu.make_async_copy(w_from[h * outer + k], w_buf.at[h * outer + k], sems.at[k, 4 + h]) for h in range(2)]
+        for k in range(outer)
+    ]
+    for k in range(outer):
+        for copy in fetch_x[k] + fetch_w[k]:
+            copy.start()
+    total = [0.0, 0.0]
+    for k in range(outer):
+        for copy in fetch_x[k] + fetch_w[k]:
+            copy.wait()
+        left = x_buf[k].reshape(4 * rows, depth)
+        for h in range(2):
+            total[h] += dot(left, w_buf[h * outer + k])
     for h in range(2):
-        total = 0.0
-        for k in range(outer):
-            left = jnp.concatenate([ref[where[0] ^ k] for ref in x_refs], axis=0)
-            total += dot(left, refs[4 + h * outer + k][...])
         for b, ref in enumerate(out_refs):
-            ref[:, h * width:(h + 1) * width] = total[b * rows:(b + 1) * rows]
+            ref[:, h * width:(h + 1) * width] = total[h][b * rows:(b + 1) * rows]
 
 
 def fast_body(tokens, cotangent, frozen_value, down_store, up_store, block_adapter, adapter_slot):
@@ -307,20 +322,19 @@
         in_specs=[SMEM, SMEM], out_specs=VMEM, name="own_row",
     )(block_adapter, adapter_slot)
     asked = lax.all_to_all(row, "tensor", 0, 0)
-    split_from, row = lax.optimization_barrier((tokens, row))
 
     width = frozen_value.shape[1] // parts
     half = lax.dynamic_slice_in_dim(frozen_value, part * width, width, axis=1)
-    quarter = [half] + [exchange(half, 2 * k) for k in range(1, outer)]
-
     block = jax.ShapeDtypeStruct((outer, token_rows, slice_width), jnp.bfloat16)
     token = jax.ShapeDtypeStruct((1,), jnp.int32)
     x_mine, x_theirs = pl.pallas_call(
         split_kernel, out_shape=(block, block), in_specs=[SMEM, VMEM], out_specs=(VMEM, VMEM),
         name="split_tokens", compiler_params=LIMIT,
-    )(x[None], split_from)
+    )(x[None], tokens)
+    x_mine, x_theirs, half, asked = lax.optimization_barrier((x_mine, x_theirs, half, asked))
     x_far = exchange(x_theirs, 1)
     y_mine = other_part(x_mine)
+    quarter = [half] + [exchange(half, 2 * k) for k in range(1, outer - 1)]
     pieces = jax.ShapeDtypeStruct((group, down_chunks + up_chunks, LANES), jnp.bfloat16)
     def tiles(store):
         view = store.reshape(store.shape[0] // TILE_ROWS, TILE_ROWS, store.shape[1] // LANES, LANES)
@@ -342,19 +356,12 @@
         cost_estimate=cost(read=40 << 20),
         name="pick_panels",
     )(asked, tiles(down_store), tiles(up_store))
-    sent, quarter = lax.optimization_barrier((sent, quarter))
+    sent, rows, quarter, x_far, y_mine = lax.optimization_barrier((sent, rows, quarter, x_far, y_mine))
     panels = lax.all_to_all(sent, "tensor", 0, 0)
     rows_core = other_core(rows)
-    x_far, y_mine, picked = lax.optimization_barrier((x_far, y_mine, rows))
     y_far = other_part(x_far)
-    pair_from, _ = lax.optimization_barrier((tokens, rows))
-    xs = pl.pallas_call(
-        interleave_kernel,
-        out_shape=jax.ShapeDtypeStruct((group, 2 * token_rows, slice_width // 2), jnp.bfloat16),
-        in_specs=[VMEM], out_specs=VMEM, name="pair_columns", compiler_params=LIMIT,
-        cost_estimate=cost(flops=2 << 30, read=4 << 20),
-    )(pair_from)
-
+    last = exchange(quarter[0], 2 * (outer - 1))
+    quarter_core = [other_core(w) for w in quarter]
     owned_groups = ADAPTERS // lax.axis_size("dp") // 8
     down_shape = jax.ShapeDtypeStruct((owned_groups, down_chunks, 8, 1, LANES), jnp.float32)
     up_shape = jax.ShapeDtypeStruct((owned_groups, up_chunks, 8, 1, LANES), jnp.float32)
@@ -363,9 +370,15 @@
         in_specs=[SMEM], out_specs=(ANY, ANY, SMEM),
         scratch_shapes=[pltpu.VMEM((up_chunks, 8, 1, LANES), jnp.float32), pltpu.SemaphoreType.DMA((2,))],
         compiler_params=LIMIT, cost_estimate=cost(read=28 << 20), name="clear_rows",
-    )(picked)
-    quarter_core = [other_core(w) for w in quarter]
-    panels, y_far, quarter_core = lax.optimization_barrier((panels, y_far, quarter_core))
+    )(rows)
+    pair_from, _ = lax.optimization_barrier((tokens, cleared))
+    xs = pl.pallas_call(
+        interleave_kernel,
+        out_shape=jax.ShapeDtypeStruct((group, 2 * token_rows, slice_width // 2), jnp.bfloat16),
+        in_specs=[VMEM], out_specs=VMEM, name="pair_columns", compiler_params=LIMIT,
+        cost_estimate=cost(flops=2 << 30, read=4 << 20),
+    )(pair_from)
+    panels, last, y_far, quarter_core = lax.optimization_barrier((panels, last, y_far, quarter_core))
 
     terms, lifted = pl.pallas_call(
         functools.partial(adapter_kernel, group, down_chunks),
@@ -377,16 +390,24 @@
         cost_estimate=cost(flops=3 << 30, read=8 << 20),
         name="adapter",
     )(xs, cotangent, panels, cleared)
+    _, last = lax.optimization_barrier((terms, last))
+    quarters = quarter + [last] + quarter_core + [other_core(last)]
+    source = jnp.stack([z ^ k for k in range(outer)])
     sums = jax.ShapeDtypeStruct((token_rows, parts * width), jnp.float32)
     own, to_part, to_inner, to_both = pl.pallas_call(
         base_kernel,
         out_shape=[sums] * 4,
-        in_specs=[SMEM] + [VMEM] * (4 + 2 * outer) + [ANY],
+        in_specs=[SMEM] + [ANY] * (5 + 2 * outer),
         out_specs=[VMEM] * 4,
-        compiler_params=LIMIT,
+        scratch_shapes=[
+            pltpu.VMEM((outer, 4, token_rows, slice_width), jnp.bfloat16),
+            pltpu.VMEM((2 * outer, slice_width, width), jnp.bfloat16),
+            pltpu.SemaphoreType.DMA((outer, 6)),
+        ],
+        compiler_params=WIDE,
         cost_estimate=cost(flops=4 << 30, read=8 << 20),
         name="frozen_part",
-    )(z[None], x_mine, y_mine, x_far, y_far, *quarter, *quarter_core, terms)
+    )(source, x_mine, y_mine, x_far, y_far, *quarters, terms)
     opposite = [(a * group + t, (parts - 1 - a) * group + (t ^ 1)) for a in range(parts) for t in range(group)]
     back = lax.all_to_all(terms, "tensor", 0, 0)
     arrived = (exchange(to_inner, 1), other_part(to_part), lax.ppermute(to_both, ("parts", "tensor"), opposite))

time: 133 us -> 115 us (0.86)
  the two profiles are of different devices: /device:TPU:0 before, /device:TPU:9 now
where the time goes in v10:
time: 115 us
  waiting for transfers between devices  41.3 us (36%)
  Pallas kernels  33.9 us (29%)
  starting transfers between devices  28.5 us (25%)
  local copies, waits for them, and re-layouts  7.02 us (6%)
  other arithmetic  2.5 us (2%)
  between operations  1.72 us (1%)
    ppermute x5, waiting for transfers between devices, exchange(): return lax.ppermute(value, 'tensor', [(t, t ^ s) for t in range(group)])  32.7 us
    pallas_call x1, Pallas kernels, fast_body(): pl.pallas_call(zero_kernel, out_shape=(down_shape, up_shape, token), in_s...  9.48 us
    all_to_all x1, starting transfers between devices, fast_body(): panels = lax.all_to_all(sent, 'tensor', 0, 0)  7.68 us
    pallas_call x1, Pallas kernels, fast_body(): pl.pallas_call(functools.partial(scatter_kernel, 2 * group, down_chunks,...  7.51 us
    unnamed x40, local copies, waits for them, and re-layouts  7 us
    all_to_all x1, starting transfers between devices, fast_body(): asked = lax.all_to_all(row, 'tensor', 0, 0)  5.69 us
    ppermute x1, waiting for transfers between devices, fast_body(): lax.ppermute(to_both, ('parts', 'tensor'), opposite)  5.56 us
    pallas_call x1, Pallas kernels, fast_body(): pl.pallas_call(base_kernel, out_shape=[sums] * 4, in_specs=[SMEM] + [ANY]...  5.43 us
  transfers between devices with their start and end apart: 18, of which 6 were waited for; matrix products, arithmetic and copies ran while one was open for 2% of the time, Pallas kernels for 19%

profile of v10, /device:TPU:9, one launch (start us, length us, event | category | flops | bytes accessed | tf_op | source)
XLA Modules:
  0.0 115.0 jit_solution(4688516639103204011)
XLA Ops:
  0.6 0.0 copy-start
  1.4 1.3 %own_row.1 = s32[8,1,128]{2,1,0:T(1,128)} custom-call(s32[1]{0:T(128)S(6)} %copy.14.block_ref, s32[256]{0:T(256)} %slot_ref.1), custom_call_target="tpu_custom_call" | custom-call | tf_op jit(solution)/shard_map/own_row/pallas_call | solution.py:320
  2.6 5.7 %all-to-all-start = ((s32[8,1,128]{2,1,0:T(1,128)}), s32[8,1,128]{2,1,0:T(1,128)S(1)}, u32[]{:S(2)}, u32[]{:S(2)}) async-start(s32[8,1,128]{2,1,0:T(1,128)} %own_row.1), calls=%async_computation | async-start | bytes 8192 | tf_op jit(solution)/shard_map/all_to_all | solution.py:324
  8.3 0.0 copy-done
  8.4 0.0 copy-start.10
  8.4 0.0 copy-start.2
  8.4 1.4 %copy-done.2 = bf16[128,5120]{1,0:T(8,128)(2,1)S(1)} copy-done((bf16[128,5120]{1,0:T(8,128)(2,1)S(1)}, bf16[128,5120]{1,0:T(8,128)(2,1)}, u32[]{:S(2)}) %copy-start.2) | copy-done | bytes 1310744
  9.8 0.1 split_tokens.1
  9.9 0.0 copy-start.6
  9.9 2.4 %all-to-all-done.asked = s32[8,1,128]{2,1,0:T(1,128)S(1)} async-done(((s32[8,1,128]{2,1,0:T(1,128)}), s32[8,1,128]{2,1,0:T(1,128)S(1)}, u32[]{:S(2)}, u32[]{:S(2)}) %all-to-all-start) | async-done | bytes 4128 | tf_op jit(solution)/shard_map/all_to_all | solution.py:324
  12.4 0.3 collective-permute-start.2
  12.7 1.2 %collective-permute-start.3 = (bf16[4,128,640]{2,1,0:T(8,128)(2,1)S(1)}, bf16[4,128,640]{2,1,0:T(8,128)(2,1)}, u32[]{:S(2)}, u32[]{:S(2)}) collective-permute-start(bf16[4,128,640]{2,1,0:T(8,128)(2,1)S(1)} %get-tuple-element.43.refs_0_), channel_id=1, source_target_pairs={{0,16},{16,0},{1,17},{17,1},{2,18},{18,2},{3,19},{19,3},{4,20},{20... | collective-permute-start | bytes 1966088 | tf_op jit(solution)/shard_map/ppermute | solution.py:318
  13.9 0.6 collective-permute-start.1
  14.5 0.8 collective-permute-start
  15.4 0.0 copy-done.11
  15.4 5.2 %pick_panels.1 = (bf16[8,384,128]{2,1,0:T(8,128)(2,1)}, s32[8]{0:T(128)}) custom-call(s32[8,1,128]{2,1,0:T(1,128)} %copy-done.11, bf16[32,320,8,128]{3,2,1,0:T(8,128)(2,1)} %bitcast.23, bf16[32,64,8,128]{3,2,1,0:T(8,128)(2,1)} %bitcast.24), custom_call_target="tpu_custom_call" | custom-call | bytes 41943040 | tf_op jit(solution)/shard_map/pick_panels/pallas_call | solution.py:343
  20.6 0.0 copy-done.6
  20.6 7.8 %collective-permute-done.1.refs_6_ = bf16[640,256]{1,0:T(8,128)(2,1)S(1)} collective-permute-done((bf16[640,256]{1,0:T(8,128)(2,1)S(1)}, bf16[640,256]{1,0:T(8,128)(2,1)S(1)}, u32[]{:S(2)}, u32[]{:S(2)}) %collective-permute-start.1) | collective-permute-done | bytes 327712 | tf_op jit(solution)/shard_map/ppermute | solution.py:312
  28.4 0.0 collective-permute-done.refs_5_
  28.4 0.0 collective-permute-done.2.refs_2_
  28.4 0.0 collective-permute-done.3.refs_1_
  28.4 0.7 copy-done.12
  29.1 0.1 copy-done.13
  29.3 7.7 %all-to-all-start.1 = ((bf16[8,384,128]{2,1,0:T(8,128)(2,1)}), bf16[8,384,128]{2,1,0:T(8,128)(2,1)S(1)}, u32[]{:S(2)}, u32[]{:S(2)}) async-start(bf16[8,384,128]{2,1,0:T(8,128)(2,1)} %get-tuple-element.51), calls=%async_computation.1 | async-start | bytes 1572864 | tf_op jit(solution)/shard_map/all_to_all | solution.py:360
  36.9 0.2 collective-permute-start.5
  37.2 1.1 collective-permute-start.7
  38.2 0.0 collective-permute-start.8
  38.2 0.5 collective-permute-start.6
  38.7 1.2 %collective-permute-start.4 = (bf16[640,256]{1,0:T(8,128)(2,1)S(1)}, bf16[640,256]{1,0:T(8,128)(2,1)S(1)}, u32[]{:S(2)}, u32[]{:S(2)}) collective-permute-start(bf16[640,256]{1,0:T(8,128)(2,1)S(1)} %constant_dynamic-slice_fusion.refs_4_), channel_id=1, source_target_pairs={{0,6},{1,7},{2,4},{3,5},{4,2},{5,3},{6,0},{7,1},{8,14},{9,15},{10,... | collective-permute-start | bytes 983048 | tf_op jit(solution)/shard_map/ppermute | solution.py:312
  39.9 0.7 copy-done.4
  40.6 9.5 %clear_rows.1 = (f32[16,320,8,1,128]{4,3,2,1,0:T(1,128)}, f32[16,64,8,1,128]{4,3,2,1,0:T(1,128)}, s32[1]{0:T(128)}) custom-call(s32[8]{0:T(128)S(1)} %copy-done.4), custom_call_target="tpu_custom_call" | custom-call | bytes 29360128 | tf_op jit(solution)/shard_map/clear_rows/pallas_call | solution.py:368
  50.1 1.8 %pair_columns.1.xs_ref = bf16[8,256,320]{2,1,0:T(8,128)(2,1)S(1)} custom-call(bf16[128,5120]{1,0:T(8,128)(2,1)S(1)} %copy-done.3), custom_call_target="tpu_custom_call" | custom-call | flops 2147483648 | bytes 4194304 | tf_op jit(solution)/shard_map/pair_columns/pallas_call | solution.py:375
  51.9 0.0 copy-start.8
  51.9 1.2 %copy-done.8 = bf16[8,256,320]{2,1,0:T(8,128)(2,1)} copy-done((bf16[8,256,320]{2,1,0:T(8,128)(2,1)}, bf16[8,256,320]{2,1,0:T(8,128)(2,1)S(1)}, u32[]{:S(2)}) %copy-start.8) | copy-done | bytes 1310744
  53.1 0.0 collective-permute-done.7.refs_9_
  53.1 0.0 collective-permute-done.8.refs_10_
  53.1 0.0 collective-permute-done.6.refs_8_
  53.1 16.4 %collective-permute-done.4.refs_7_ = bf16[640,256]{1,0:T(8,128)(2,1)S(1)} collective-permute-done((bf16[640,256]{1,0:T(8,128)(2,1)S(1)}, bf16[640,256]{1,0:T(8,128)(2,1)S(1)}, u32[]{:S(2)}, u32[]{:S(2)}) %collective-permute-start.4) | collective-permute-done | bytes 327712 | tf_op jit(solution)/shard_map/ppermute | solution.py:312
  69.6 0.0 copy-done.15
  69.6 0.7 copy-done.17
  70.3 0.0 collective-permute-done.5.refs_3_
  70.3 0.0 all-to-all-done.1.pieces
  70.3 1.4 %copy-done.9 = bf16[8,256,320]{2,1,0:T(8,128)(2,1)S(1)} copy-done((bf16[8,256,320]{2,1,0:T(8,128)(2,1)S(1)}, bf16[8,256,320]{2,1,0:T(8,128)(2,1)}, u32[]{:S(2)}) %copy-start.9) | copy-done | bytes 1310744
  71.7 3.1 %adapter.1 = (bf16[8,384,128]{2,1,0:T(8,128)(2,1)}, f32[128,1024]{1,0:T(8,128)S(1)}) custom-call(bf16[8,256,320]{2,1,0:T(8,128)(2,1)S(1)} %copy-done.9, bf16[128,1024]{1,0:T(8,128)(2,1)S(1)} %copy-done.7, bf16[8,384,128]{2,1,0:T(8,128)(2,1)S(1)} %all-to-all-done.1.pieces, s32[1]{0:T(128)} %get-tuple-element.57._), custom_call_target="tpu_custom_call" | custom-call | flops 3221225472 | bytes 8388608 | tf_op jit(solution)/shard_map/adapter/pallas_call | solution.py:383
  74.8 4.5 %all-to-all-start.2 = ((bf16[8,384,128]{2,1,0:T(8,128)(2,1)}), bf16[8,384,128]{2,1,0:T(8,128)(2,1)S(1)}, u32[]{:S(2)}, u32[]{:S(2)}) async-start(bf16[8,384,128]{2,1,0:T(8,128)(2,1)} %get-tuple-element.60.refs_12_), calls=%async_computation.2 | async-start | bytes 1572864 | tf_op jit(solution)/shard_map/all_to_all | solution.py:412
  79.3 1.0 collective-permute-start.9
  80.3 0.7 pad_add_fusion.where
  81.0 0.6 collective-permute-done.9.refs_11_
  81.6 0.7 copy-done.19
  82.3 5.4 %frozen_part.1 = (f32[128,512]{1,0:T(8,128)}, f32[128,512]{1,0:T(8,128)}, f32[128,512]{1,0:T(8,128)}, f32[128,512]{1,0:T(8,128)}) custom-call(s32[4]{0:T(128)} %pad_add_fusion.where, bf16[4,128,640]{2,1,0:T(8,128)(2,1)} %copy-done.6, bf16[4,128,640]{2,1,0:T(8,128)(2,1)} %collective-permute-done.3.refs_1_, ...), custom_call_target="tpu_custom_call" | custom-call | flops 4294967296 | bytes 8388608 | tf_op jit(solution)/shard_map/frozen_part/pallas_call | solution.py:397
  87.8 1.2 %collective-permute-start.10 = (f32[128,512]{1,0:T(8,128)}, f32[128,512]{1,0:T(8,128)S(1)}, u32[]{:S(2)}, u32[]{:S(2)}) collective-permute-start(f32[128,512]{1,0:T(8,128)} %get-tuple-element.67), channel_id=1, source_target_pairs={{0,1},{1,0},{2,3},{3,2},{4,5},{5,4},{6,7},{7,6},{8,9},{9,8},{10,11... | collective-permute-start | bytes 786440 | tf_op jit(solution)/shard_map/ppermute | solution.py:312
  89.0 0.2 collective-permute-start.11
  89.2 1.2 %collective-permute-start.12 = (f32[128,512]{1,0:T(8,128)}, f32[128,512]{1,0:T(8,128)S(1)}, u32[]{:S(2)}, u32[]{:S(2)}) collective-permute-start(f32[128,512]{1,0:T(8,128)} %get-tuple-element.69), channel_id=1, source_target_pairs={{0,17},{1,16},{2,19},{3,18},{4,21},{5,20},{6,23},{7,22},{16,1},{17... | collective-permute-start | bytes 786440 | tf_op jit(solution)/shard_map/ppermute | solution.py:413
  90.5 8.5 %collective-permute-done.10 = f32[128,512]{1,0:T(8,128)S(1)} collective-permute-done((f32[128,512]{1,0:T(8,128)}, f32[128,512]{1,0:T(8,128)S(1)}, u32[]{:S(2)}, u32[]{:S(2)}) %collective-permute-start.10) | collective-permute-done | bytes 262176 | tf_op jit(solution)/shard_map/ppermute | solution.py:312
  98.9 0.0 collective-permute-done.11
  98.9 5.6 %collective-permute-done.12 = f32[128,512]{1,0:T(8,128)S(1)} collective-permute-done((f32[128,512]{1,0:T(8,128)}, f32[128,512]{1,0:T(8,128)S(1)}, u32[]{:S(2)}, u32[]{:S(2)}) %collective-permute-start.12) | collective-permute-done | bytes 262176 | tf_op jit(solution)/shard_map/ppermute | solution.py:413
  104.5 0.0 all-to-all-done.2.rest_0_
  104.5 0.8 collective-permute-start.14
  105.3 0.1 collective-permute-start.13
  105.4 1.0 add.19
  106.5 0.8 fusion
  107.3 0.0 collective-permute-done.13.rows_core
  107.3 0.0 collective-permute-done.14.rest_1_
  107.3 7.5 %place_rows.1 = (f32[16,320,8,1,128]{4,3,2,1,0:T(1,128)}, f32[16,64,8,1,128]{4,3,2,1,0:T(1,128)}) custom-call(s32[1]{0:T(128)} %bitcast.9.first_row, s32[8]{0:T(128)S(1)} %copy-done.5, s32[8]{0:T(128)S(1)} %collective-permute-done.13.rows_core, bf16[8,384,128]{2,1,0:T(8,128)(2,1)S(1)} %all-to-all-done.2.rest_0_, ...), custom_call_target="tpu_custom_call", output_to_operand_aliasing={{0}: (5, {}), {1}: (6, {})} | custom-call | bytes 16777216 | tf_op jit(solution)/shard_map/place_rows/pallas_call | solution.py:417
  (26 shorter events, 0.1 us)
Async XLA Ops:
  0.6 7.7 %copy-start = (bf16[640,512]{1,0:T(8,128)(2,1)S(1)}, bf16[640,512]{1,0:T(8,128)(2,1)}, u32[]{:S(2)}) copy-start(bf16[640,512]{1,0:T(8,128)(2,1)} %param.9) | copy-start | bytes 1966084
  2.6 9.7 %all-to-all-start = ((s32[8,1,128]{2,1,0:T(1,128)}), s32[8,1,128]{2,1,0:T(1,128)S(1)}, u32[]{:S(2)}, u32[]{:S(2)}) async-start(s32[8,1,128]{2,1,0:T(1,128)} %own_row.1), calls=%async_computation | async-start | bytes 8192 | tf_op jit(solution)/shard_map/all_to_all | solution.py:324
  8.4 30.4 %copy-start.10 = (bf16[640,256]{1,0:T(8,128)(2,1)}, bf16[640,256]{1,0:T(8,128)(2,1)S(1)}, u32[]{:S(2)}) copy-start(bf16[640,256]{1,0:T(8,128)(2,1)S(1)} %constant_dynamic-slice_fusion.refs_4_) | copy-start | bytes 983044
  8.4 1.4 %copy-start.2 = (bf16[128,5120]{1,0:T(8,128)(2,1)S(1)}, bf16[128,5120]{1,0:T(8,128)(2,1)}, u32[]{:S(2)}) copy-start(bf16[128,5120]{1,0:T(8,128)(2,1)} %x_ref.2) | copy-start | bytes 3932164
  9.9 10.7 %copy-start.6 = (bf16[4,128,640]{2,1,0:T(8,128)(2,1)}, bf16[4,128,640]{2,1,0:T(8,128)(2,1)S(1)}, u32[]{:S(2)}) copy-start(bf16[4,128,640]{2,1,0:T(8,128)(2,1)S(1)} %get-tuple-element.43.refs_0_) | copy-start | bytes 1966084
  12.4 3.0 %copy-start.11 = (s32[8,1,128]{2,1,0:T(1,128)}, s32[8,1,128]{2,1,0:T(1,128)S(1)}, u32[]{:S(2)}) copy-start(s32[8,1,128]{2,1,0:T(1,128)S(1)} %all-to-all-done.asked) | copy-start | bytes 12292
  12.4 16.0 %collective-permute-start.2 = (bf16[4,128,640]{2,1,0:T(8,128)(2,1)S(1)}, bf16[4,128,640]{2,1,0:T(8,128)(2,1)}, u32[]{:S(2)}, u32[]{:S(2)}) collective-permute-start(bf16[4,128,640]{2,1,0:T(8,128)(2,1)S(1)} %get-tuple-element.48), channel_id=1, source_target_pairs={{0,1},{1,0},{2,3},{3,2},{4,5},{5,4},{6,7},{7,6},{8,9},{9,8},{10,11... | collective-permute-start | bytes 1966088 | tf_op jit(solution)/shard_map/ppermute | solution.py:312
  12.7 15.7 %collective-permute-start.3 = (bf16[4,128,640]{2,1,0:T(8,128)(2,1)S(1)}, bf16[4,128,640]{2,1,0:T(8,128)(2,1)}, u32[]{:S(2)}, u32[]{:S(2)}) collective-permute-start(bf16[4,128,640]{2,1,0:T(8,128)(2,1)S(1)} %get-tuple-element.43.refs_0_), channel_id=1, source_target_pairs={{0,16},{16,0},{1,17},{17,1},{2,18},{18,2},{3,19},{19,3},{4,20},{20... | collective-permute-start | bytes 1966088 | tf_op jit(solution)/shard_map/ppermute | solution.py:318
  13.9 14.5 %collective-permute-start.1 = (bf16[640,256]{1,0:T(8,128)(2,1)S(1)}, bf16[640,256]{1,0:T(8,128)(2,1)S(1)}, u32[]{:S(2)}, u32[]{:S(2)}) collective-permute-start(bf16[640,256]{1,0:T(8,128)(2,1)S(1)} %constant_dynamic-slice_fusion.refs_4_), channel_id=1, source_target_pairs={{0,4},{1,5},{2,6},{3,7},{4,0},{5,1},{6,2},{7,3},{8,12},{9,13},{10,... | collective-permute-start | bytes 983048 | tf_op jit(solution)/shard_map/ppermute | solution.py:312
  14.5 13.9 %collective-permute-start = (bf16[640,256]{1,0:T(8,128)(2,1)S(1)}, bf16[640,256]{1,0:T(8,128)(2,1)S(1)}, u32[]{:S(2)}, u32[]{:S(2)}) collective-permute-start(bf16[640,256]{1,0:T(8,128)(2,1)S(1)} %constant_dynamic-slice_fusion.refs_4_), channel_id=1, source_target_pairs={{0,2},{1,3},{2,0},{3,1},{4,6},{5,7},{6,4},{7,5},{8,10},{9,11},{10,... | collective-permute-start | bytes 983048 | tf_op jit(solution)/shard_map/ppermute | solution.py:312
  15.4 34.7 %copy-start.3 = (bf16[128,5120]{1,0:T(8,128)(2,1)S(1)}, bf16[128,5120]{1,0:T(8,128)(2,1)}, u32[]{:S(2)}) copy-start(bf16[128,5120]{1,0:T(8,128)(2,1)} %x_ref.2) | copy-start | bytes 3932164
  28.4 0.7 copy-start.12
  28.4 0.8 copy-start.13
  29.1 41.2 %copy-start.7 = (bf16[128,1024]{1,0:T(8,128)(2,1)S(1)}, bf16[128,1024]{1,0:T(8,128)(2,1)}, u32[]{:S(2)}) copy-start(bf16[128,1024]{1,0:T(8,128)(2,1)} %g_ref.1) | copy-start | bytes 786436
  29.3 41.1 %all-to-all-start.1 = ((bf16[8,384,128]{2,1,0:T(8,128)(2,1)}), bf16[8,384,128]{2,1,0:T(8,128)(2,1)S(1)}, u32[]{:S(2)}, u32[]{:S(2)}) async-start(bf16[8,384,128]{2,1,0:T(8,128)(2,1)} %get-tuple-element.51), calls=%async_computation.1 | async-start | bytes 1572864 | tf_op jit(solution)/shard_map/all_to_all | solution.py:360
  36.9 33.4 %collective-permute-start.5 = (bf16[4,128,640]{2,1,0:T(8,128)(2,1)}, bf16[4,128,640]{2,1,0:T(8,128)(2,1)}, u32[]{:S(2)}, u32[]{:S(2)}) collective-permute-start(bf16[4,128,640]{2,1,0:T(8,128)(2,1)} %collective-permute-done.2.refs_2_), channel_id=1, source_target_pairs={{0,16},{16,0},{1,17},{17,1},{2,18},{18,2},{3,19},{19,3},{4,20},{20... | collective-permute-start | bytes 1966088 | tf_op jit(solution)/shard_map/ppermute | solution.py:318
  37.2 15.9 %collective-permute-start.7 = (bf16[640,256]{1,0:T(8,128)(2,1)}, bf16[640,256]{1,0:T(8,128)(2,1)S(1)}, u32[]{:S(2)}, u32[]{:S(2)}) collective-permute-start(bf16[640,256]{1,0:T(8,128)(2,1)} %copy-done.13), channel_id=1, source_target_pairs={{0,8},{8,0},{1,9},{9,1},{2,10},{10,2},{3,11},{11,3},{4,12},{12,4},... | collective-permute-start | bytes 983048 | tf_op jit(solution)/shard_map/ppermute | solution.py:315
  38.2 14.9 %collective-permute-start.8 = (bf16[640,256]{1,0:T(8,128)(2,1)}, bf16[640,256]{1,0:T(8,128)(2,1)S(1)}, u32[]{:S(2)}, u32[]{:S(2)}) collective-permute-start(bf16[640,256]{1,0:T(8,128)(2,1)} %copy-done.12), channel_id=1, source_target_pairs={{0,8},{8,0},{1,9},{9,1},{2,10},{10,2},{3,11},{11,3},{4,12},{12,4},... | collective-permute-start | bytes 983048 | tf_op jit(solution)/shard_map/ppermute | solution.py:315
  38.2 14.9 %collective-permute-start.6 = (bf16[640,256]{1,0:T(8,128)(2,1)S(1)}, bf16[640,256]{1,0:T(8,128)(2,1)S(1)}, u32[]{:S(2)}, u32[]{:S(2)}) collective-permute-start(bf16[640,256]{1,0:T(8,128)(2,1)S(1)} %constant_dynamic-slice_fusion.refs_4_), channel_id=1, source_target_pairs={{0,8},{8,0},{1,9},{9,1},{2,10},{10,2},{3,11},{11,3},{4,12},{12,4},... | collective-permute-start | bytes 983048 | tf_op jit(solution)/shard_map/ppermute | solution.py:315
  38.7 30.8 %collective-permute-start.4 = (bf16[640,256]{1,0:T(8,128)(2,1)S(1)}, bf16[640,256]{1,0:T(8,128)(2,1)S(1)}, u32[]{:S(2)}, u32[]{:S(2)}) collective-permute-start(bf16[640,256]{1,0:T(8,128)(2,1)S(1)} %constant_dynamic-slice_fusion.refs_4_), channel_id=1, source_target_pairs={{0,6},{1,7},{2,4},{3,5},{4,2},{5,3},{6,0},{7,1},{8,14},{9,15},{10,... | collective-permute-start | bytes 983048 | tf_op jit(solution)/shard_map/ppermute | solution.py:312
  39.9 0.7 copy-start.4
  51.9 1.2 %copy-start.8 = (bf16[8,256,320]{2,1,0:T(8,128)(2,1)}, bf16[8,256,320]{2,1,0:T(8,128)(2,1)S(1)}, u32[]{:S(2)}) copy-start(bf16[8,256,320]{2,1,0:T(8,128)(2,1)S(1)} %pair_columns.1.xs_ref) | copy-start | bytes 3932164
  53.1 17.2 %copy-start.14 = (bf16[640,256]{1,0:T(8,128)(2,1)}, bf16[640,256]{1,0:T(8,128)(2,1)S(1)}, u32[]{:S(2)}) copy-start(bf16[640,256]{1,0:T(8,128)(2,1)S(1)} %collective-permute-done.7.refs_9_) | copy-start | bytes 983044
  53.1 16.5 %copy-start.15 = (bf16[640,256]{1,0:T(8,128)(2,1)}, bf16[640,256]{1,0:T(8,128)(2,1)S(1)}, u32[]{:S(2)}) copy-start(bf16[640,256]{1,0:T(8,128)(2,1)S(1)} %collective-permute-done.8.refs_10_) | copy-start | bytes 983044
  53.1 16.4 %copy-start.16 = (bf16[640,256]{1,0:T(8,128)(2,1)}, bf16[640,256]{1,0:T(8,128)(2,1)S(1)}, u32[]{:S(2)}) copy-start(bf16[640,256]{1,0:T(8,128)(2,1)S(1)} %collective-permute-done.6.refs_8_) | copy-start | bytes 983044
  69.6 0.7 copy-start.17
  70.3 1.4 %copy-start.9 = (bf16[8,256,320]{2,1,0:T(8,128)(2,1)S(1)}, bf16[8,256,320]{2,1,0:T(8,128)(2,1)}, u32[]{:S(2)}) copy-start(bf16[8,256,320]{2,1,0:T(8,128)(2,1)} %copy-done.8) | copy-start | bytes 3932164
  71.7 7.6 %copy-start.18 = (bf16[640,256]{1,0:T(8,128)(2,1)S(1)}, bf16[640,256]{1,0:T(8,128)(2,1)}, u32[]{:S(2)}) copy-start(bf16[640,256]{1,0:T(8,128)(2,1)} %copy-done.17) | copy-start | bytes 983044
  74.8 29.7 %all-to-all-start.2 = ((bf16[8,384,128]{2,1,0:T(8,128)(2,1)}), bf16[8,384,128]{2,1,0:T(8,128)(2,1)S(1)}, u32[]{:S(2)}, u32[]{:S(2)}) async-start(bf16[8,384,128]{2,1,0:T(8,128)(2,1)} %get-tuple-element.60.refs_12_), calls=%async_computation.2 | async-start | bytes 1572864 | tf_op jit(solution)/shard_map/all_to_all | solution.py:412
  79.3 2.3 %collective-permute-start.9 = (bf16[640,256]{1,0:T(8,128)(2,1)S(1)}, bf16[640,256]{1,0:T(8,128)(2,1)S(1)}, u32[]{:S(2)}, u32[]{:S(2)}) collective-permute-start(bf16[640,256]{1,0:T(8,128)(2,1)S(1)} %copy-done.18), channel_id=1, source_target_pairs={{0,8},{8,0},{1,9},{9,1},{2,10},{10,2},{3,11},{11,3},{4,12},{12,4},... | collective-permute-start | bytes 983048 | tf_op jit(solution)/shard_map/ppermute | solution.py:315
  81.0 24.3 %copy-start.5 = (s32[8]{0:T(128)S(1)}, s32[8]{0:T(128)}, u32[]{:S(2)}) copy-start(s32[8]{0:T(128)} %get-tuple-element.56.after_ref.rows_here) | copy-start | bytes 100
  81.6 0.7 copy-start.19
  87.8 11.2 %collective-permute-start.10 = (f32[128,512]{1,0:T(8,128)}, f32[128,512]{1,0:T(8,128)S(1)}, u32[]{:S(2)}, u32[]{:S(2)}) collective-permute-start(f32[128,512]{1,0:T(8,128)} %get-tuple-element.67), channel_id=1, source_target_pairs={{0,1},{1,0},{2,3},{3,2},{4,5},{5,4},{6,7},{7,6},{8,9},{9,8},{10,11... | collective-permute-start | bytes 786440 | tf_op jit(solution)/shard_map/ppermute | solution.py:312
  89.0 9.9 %collective-permute-start.11 = (f32[128,512]{1,0:T(8,128)}, f32[128,512]{1,0:T(8,128)S(1)}, u32[]{:S(2)}, u32[]{:S(2)}) collective-permute-start(f32[128,512]{1,0:T(8,128)} %get-tuple-element.68), channel_id=1, source_target_pairs={{0,16},{16,0},{1,17},{17,1},{2,18},{18,2},{3,19},{19,3},{4,20},{20... | collective-permute-start | bytes 786440 | tf_op jit(solution)/shard_map/ppermute | solution.py:318
  89.2 15.3 %collective-permute-start.12 = (f32[128,512]{1,0:T(8,128)}, f32[128,512]{1,0:T(8,128)S(1)}, u32[]{:S(2)}, u32[]{:S(2)}) collective-permute-start(f32[128,512]{1,0:T(8,128)} %get-tuple-element.69), channel_id=1, source_target_pairs={{0,17},{1,16},{2,19},{3,18},{4,21},{5,20},{6,23},{7,22},{16,1},{17... | collective-permute-start | bytes 786440 | tf_op jit(solution)/shard_map/ppermute | solution.py:413
  104.5 2.8 %collective-permute-start.14 = (bf16[8,384,128]{2,1,0:T(8,128)(2,1)S(1)}, bf16[8,384,128]{2,1,0:T(8,128)(2,1)S(1)}, u32[]{:S(2)}, u32[]{:S(2)}) collective-permute-start(bf16[8,384,128]{2,1,0:T(8,128)(2,1)S(1)} %all-to-all-done.2.rest_0_), channel_id=1, source_target_pairs={{0,8},{8,0},{1,9},{9,1},{2,10},{10,2},{3,11},{11,3},{4,12},{12,4},... | collective-permute-start | bytes 2359304 | tf_op jit(solution)/shard_map/ppermute | solution.py:315
  105.3 1.9 %collective-permute-start.13 = (s32[8]{0:T(128)S(1)}, s32[8]{0:T(128)S(1)}, u32[]{:S(2)}, u32[]{:S(2)}) collective-permute-start(s32[8]{0:T(128)S(1)} %copy-done.5), channel_id=1, source_target_pairs={{0,8},{8,0},{1,9},{9,1},{2,10},{10,2},{3,11},{11,3},{4,12},{12,4},... | collective-permute-start | bytes 104 | tf_op jit(solution)/shard_map/ppermute | solution.py:315
  107.3 7.5 %copy-start.1 = (bf16[640,512]{1,0:T(8,128)(2,1)S(1)}, bf16[640,512]{1,0:T(8,128)(2,1)}, u32[]{:S(2)}) copy-start(bf16[640,512]{1,0:T(8,128)(2,1)} %param.9) | copy-start | bytes 1966084

commit v11 on v10

--- a/solution.py
+++ b/solution.py
@@ -113,8 +113,9 @@
         theirs_ref[k] = x_ref[:, pl.ds(other, width)]
 
 
-def interleave_kernel(x_ref, xs_ref):
+def interleave_kernel(x_ref, out_ref, xs_ref, sems):
     group, rows2, half = xs_ref.shape
+    leave = [pltpu.make_async_copy(xs_ref.at[k], out_ref.at[k], sems.at[k]) for k in range(group)]
     rows, width = rows2 // 2, 2 * half
     source = lax.broadcasted_iota(jnp.int32, (width, half), 0)
     target = lax.broadcasted_iota(jnp.int32, (width, half), 1)
@@ -124,6 +125,9 @@
         x = x_ref[:, k * width:(k + 1) * width]
         xs_ref[k, :rows] = dot(x, even).astype(jnp.bfloat16)
         xs_ref[k, rows:] = dot(x, odd).astype(jnp.bfloat16)
+        leave[k].start()
+    for copy in leave:
+        copy.wait()
 
 
 def gather_kernel(asked, down_ref, up_ref, out_ref, rows_ref, down_buf, up_buf, flat, built, sems):
@@ -216,9 +220,12 @@
     across = up_chunks // 8
     rows = [(rows_here if b < half else rows_core)[b % half] - first_row[0] for b in range(count)]
     arriving = [pltpu.make_async_copy(sources[b // half].at[b % half], pieces.at[b], arrived.at[b]) for b in range(count)]
-    for copy in arriving:
-        copy.start()
     owned = [(row >= 0) & (row < owned_rows) for row in rows]
+    for b in range(count):
+        @pl.when(owned[b])
+        def _():
+            arriving[b].start()
+
     slots, final = [], []
     for b in range(count):
         slot, last = jnp.int32(b), jnp.bool_(True)
@@ -231,22 +238,21 @@
 
     def copies(b):
         return (
-            pltpu.make_async_copy(down_sum.at[slots[b]], down_out.at[rows[b] // 8, :, rows[b] % 8], sem),
-            pltpu.make_async_copy(up_sum.at[slots[b]], up_out.at[rows[b] // 8, :, rows[b] % 8], sem),
+            pltpu.make_async_copy(down_sum.at[slots[b]], down_out.at[rows[b] // 8, :, rows[b] % 8, 0], sem),
+            pltpu.make_async_copy(up_sum.at[slots[b]], up_out.at[rows[b] // 8, :, rows[b] % 8, 0], sem),
         )
 
     for b in range(count):
-        arriving[b].wait()
-
         @pl.when(owned[b])
         def _():
+            arriving[b].wait()
             slot = slots[b]
-            down = pieces[b, :down_chunks].astype(jnp.float32).reshape(down_chunks, 1, LANES)
+            down = pieces[b, :down_chunks].astype(jnp.float32)
             for c in range(across):
                 ordered[pl.ds(c, 8, stride=across), :] = pieces[
                     b, down_chunks + 8 * c:down_chunks + 8 * c + 8
                 ].astype(jnp.float32)
-            up = ordered[...].reshape(up_chunks, 1, LANES)
+            up = ordered[...]
 
             @pl.when(slot == b)
             def _():
@@ -295,7 +301,7 @@
             total[h] += dot(left, w_buf[h * outer + k])
     for h in range(2):
         for b, ref in enumerate(out_refs):
-            ref[:, h * width:(h + 1) * width] = total[h][b * rows:(b + 1) * rows]
+            ref[:, h * width:(h + 1) * width] = total[h][b * rows:(b + 1) * rows].astype(ref.dtype)
 
 
 def fast_body(tokens, cotangent, frozen_value, down_store, up_store, block_adapter, adapter_slot):
@@ -322,19 +328,25 @@
         in_specs=[SMEM, SMEM], out_specs=VMEM, name="own_row",
     )(block_adapter, adapter_slot)
     asked = lax.all_to_all(row, "tensor", 0, 0)
+    split_from, half_from, row = lax.optimization_barrier((tokens, frozen_value, row))
 
     width = frozen_value.shape[1] // parts
-    half = lax.dynamic_slice_in_dim(frozen_value, part * width, width, axis=1)
+    half = lax.dynamic_slice_in_dim(half_from, part * width, width, axis=1)
     block = jax.ShapeDtypeStruct((outer, token_rows, slice_width), jnp.bfloat16)
     token = jax.ShapeDtypeStruct((1,), jnp.int32)
     x_mine, x_theirs = pl.pallas_call(
         split_kernel, out_shape=(block, block), in_specs=[SMEM, VMEM], out_specs=(VMEM, VMEM),
         name="split_tokens", compiler_params=LIMIT,
-    )(x[None], tokens)
-    x_mine, x_theirs, half, asked = lax.optimization_barrier((x_mine, x_theirs, half, asked))
+    )(x[None], split_from)
     x_far = exchange(x_theirs, 1)
     y_mine = other_part(x_mine)
-    quarter = [half] + [exchange(half, 2 * k) for k in range(1, outer - 1)]
+    middle = [(t, t ^ 6) for t in range(group) if t // 2 in (1, 2)]
+    ends = [(t, t ^ 2) for t in range(group) if t // 2 in (1, 2)]
+    near = exchange(half, 2)
+    over = lax.ppermute(half, "tensor", middle)
+    near, over, asked = lax.optimization_barrier((near, over, asked))
+    over_near = lax.ppermute(near, "tensor", middle)
+    passed = lax.ppermute(over, "tensor", ends)
     pieces = jax.ShapeDtypeStruct((group, down_chunks + up_chunks, LANES), jnp.bfloat16)
     def tiles(store):
         view = store.reshape(store.shape[0] // TILE_ROWS, TILE_ROWS, store.shape[1] // LANES, LANES)
@@ -356,11 +368,15 @@
         cost_estimate=cost(read=40 << 20),
         name="pick_panels",
     )(asked, tiles(down_store), tiles(up_store))
-    sent, rows, quarter, x_far, y_mine = lax.optimization_barrier((sent, rows, quarter, x_far, y_mine))
+    sent, rows, x_far, y_mine, half, near, over, over_near, passed = lax.optimization_barrier(
+        (sent, rows, x_far, y_mine, half, near, over, over_near, passed)
+    )
     panels = lax.all_to_all(sent, "tensor", 0, 0)
     rows_core = other_core(rows)
     y_far = other_part(x_far)
-    last = exchange(quarter[0], 2 * (outer - 1))
+    inside = (z == 1) | (z == 2)
+    passed_near = lax.ppermute(over_near, "tensor", ends)
+    quarter = [half, near, jnp.where(inside, over, passed)]
     quarter_core = [other_core(w) for w in quarter]
     owned_groups = ADAPTERS // lax.axis_size("dp") // 8
     down_shape = jax.ShapeDtypeStruct((owned_groups, down_chunks, 8, 1, LANES), jnp.float32)
@@ -375,10 +391,14 @@
     xs = pl.pallas_call(
         interleave_kernel,
         out_shape=jax.ShapeDtypeStruct((group, 2 * token_rows, slice_width // 2), jnp.bfloat16),
-        in_specs=[VMEM], out_specs=VMEM, name="pair_columns", compiler_params=LIMIT,
+        in_specs=[VMEM], out_specs=ANY, name="pair_columns", compiler_params=WIDE,
+        scratch_shapes=[
+            pltpu.VMEM((group, 2 * token_rows, slice_width // 2), jnp.bfloat16),
+            pltpu.SemaphoreType.DMA((group,)),
+        ],
         cost_estimate=cost(flops=2 << 30, read=4 << 20),
     )(pair_from)
-    panels, last, y_far, quarter_core = lax.optimization_barrier((panels, last, y_far, quarter_core))
+    panels, passed_near, y_far, quarter_core = lax.optimization_barrier((panels, passed_near, y_far, quarter_core))
 
     terms, lifted = pl.pallas_call(
         functools.partial(adapter_kernel, group, down_chunks),
@@ -390,13 +410,14 @@
         cost_estimate=cost(flops=3 << 30, read=8 << 20),
         name="adapter",
     )(xs, cotangent, panels, cleared)
-    _, last = lax.optimization_barrier((terms, last))
+    _, passed_near = lax.optimization_barrier((terms, passed_near))
+    last = jnp.where(inside, over_near, passed_near)
     quarters = quarter + [last] + quarter_core + [other_core(last)]
-    source = jnp.stack([z ^ k for k in range(outer)])
-    sums = jax.ShapeDtypeStruct((token_rows, parts * width), jnp.float32)
+    source = jnp.stack([z, z ^ 1, jnp.where(z < 2, 2, 1), jnp.where(z < 2, 3, 0)])
+    sums = [jax.ShapeDtypeStruct((token_rows, parts * width), kind) for kind in (jnp.float32,) + (jnp.bfloat16,) * 3]
     own, to_part, to_inner, to_both = pl.pallas_call(
         base_kernel,
-        out_shape=[sums] * 4,
+        out_shape=sums,
         in_specs=[SMEM] + [ANY] * (5 + 2 * outer),
         out_specs=[VMEM] * 4,
         scratch_shapes=[
@@ -422,8 +443,8 @@
         input_output_aliases={5: 0, 6: 1},
         scratch_shapes=[
             pltpu.VMEM((2 * group,) + pieces.shape[1:], jnp.bfloat16),
-            pltpu.VMEM((2 * group, down_chunks, 1, LANES), jnp.float32),
-            pltpu.VMEM((2 * group, up_chunks, 1, LANES), jnp.float32),
+            pltpu.VMEM((2 * group, down_chunks, LANES), jnp.float32),
+            pltpu.VMEM((2 * group, up_chunks, LANES), jnp.float32),
             pltpu.VMEM((up_chunks, LANES), jnp.float32),
             pltpu.SemaphoreType.DMA((2 * group,)),
             pltpu.SemaphoreType.DMA(()),
@@ -436,6 +457,7 @@
     grad_down = grad_down.reshape(owned_groups, down_chunks, 8, LANES).transpose(0, 2, 1, 3)
     grad_up = grad_up.reshape(owned_groups, up_chunks, 8, LANES).transpose(0, 2, 1, 3)
 
+    arrived = [a.astype(jnp.float32) for a in arrived]
     kept, got = own + arrived[0], arrived[1] + arrived[2]
     quarters = [[c[:, :width], c[:, width:]] for c in (kept, got)]
 

time: 115 us -> 99.1 us (0.86)
  the two profiles are of different devices: /device:TPU:9 before, /device:TPU:0 now
where the time goes in v11:
time: 99.1 us; the launch traced here: 98 us
  Pallas kernels  30.9 us (31%)
  starting transfers between devices  28.2 us (28%)
  waiting for transfers between devices  16.8 us (17%)
  blocking collectives  13 us (13%)
  local copies, waits for them, and re-layouts  4.96 us (5%)
  other arithmetic  2.48 us (3%)
  between operations  1.61 us (2%)
    all_to_all x1, blocking collectives, fast_body(): asked = lax.all_to_all(row, 'tensor', 0, 0)  13 us
    ppermute x3, starting transfers between devices, exchange(): return lax.ppermute(value, 'tensor', [(t, t ^ s) for t in range(group)])  9.54 us
    pallas_call x1, Pallas kernels, fast_body(): pl.pallas_call(zero_kernel, out_shape=(down_shape, up_shape, token), in_s...  9.48 us
    pallas_call x1, Pallas kernels, fast_body(): pl.pallas_call(base_kernel, out_shape=sums, in_specs=[SMEM] + [ANY] * (5...  5.29 us
    pallas_call x1, Pallas kernels, fast_body(): pl.pallas_call(gather_kernel, out_shape=(pieces, jax.ShapeDtypeStruct((gr...  5.12 us
    unnamed x32, local copies, waits for them, and re-layouts  4.94 us
    all_to_all x1, starting transfers between devices, fast_body(): back = lax.all_to_all(terms, 'tensor', 0, 0)  4.53 us
    ppermute x3, waiting for transfers between devices, exchange(): return lax.ppermute(value, 'tensor', [(t, t ^ s) for t in range(group)])  4.5 us
  transfers between devices with their start and end apart: 19, of which 6 were waited for; matrix products, arithmetic and copies ran while one was open for 3% of the time, Pallas kernels for 24%

profile of v11, /device:TPU:0, one launch (start us, length us, event | category | flops | bytes accessed | tf_op | source)
XLA Modules:
  0.0 98.0 jit_solution(15494416051686661988)
XLA Ops:
  0.6 0.0 copy-start
  1.4 1.3 %own_row.1 = s32[8,1,128]{2,1,0:T(1,128)} custom-call(s32[1]{0:T(128)S(6)} %copy.14.block_ref, s32[256]{0:T(256)} %slot_ref.1), custom_call_target="tpu_custom_call" | custom-call | tf_op jit(solution)/shard_map/own_row/pallas_call | solution.py:326
  2.6 0.0 copy-done
  2.7 0.0 copy-start.10
  2.7 0.7 collective-permute-start.1
  3.4 5.9 %collective-permute-start = (bf16[640,256]{1,0:T(8,128)(2,1)S(1)}, bf16[640,256]{1,0:T(8,128)(2,1)S(1)}, u32[]{:S(2)}, u32[]{:S(2)}) collective-permute-start(bf16[640,256]{1,0:T(8,128)(2,1)S(1)} %constant_dynamic-slice_fusion.refs_4_), channel_id=1, source_target_pairs={{0,2},{1,3},{2,0},{3,1},{4,6},{5,7},{6,4},{7,5},{8,10},{9,11},{10,... | collective-permute-start | bytes 983048 | tf_op jit(solution)/shard_map/ppermute | solution.py:318
  9.3 1.3 %copy-done.2 = bf16[128,5120]{1,0:T(8,128)(2,1)S(1)} copy-done((bf16[128,5120]{1,0:T(8,128)(2,1)S(1)}, bf16[128,5120]{1,0:T(8,128)(2,1)}, u32[]{:S(2)}) %copy-start.2) | copy-done | bytes 1310744
  10.6 0.1 split_tokens.1
  10.7 0.0 copy-start.5
  10.7 1.6 %collective-permute-start.2 = (bf16[4,128,640]{2,1,0:T(8,128)(2,1)S(1)}, bf16[4,128,640]{2,1,0:T(8,128)(2,1)}, u32[]{:S(2)}, u32[]{:S(2)}) collective-permute-start(bf16[4,128,640]{2,1,0:T(8,128)(2,1)S(1)} %get-tuple-element.50), channel_id=1, source_target_pairs={{0,1},{1,0},{2,3},{3,2},{4,5},{5,4},{6,7},{7,6},{8,9},{9,8},{10,11... | collective-permute-start | bytes 1966088 | tf_op jit(solution)/shard_map/ppermute | solution.py:318
  12.3 1.5 %collective-permute-start.3 = (bf16[4,128,640]{2,1,0:T(8,128)(2,1)S(1)}, bf16[4,128,640]{2,1,0:T(8,128)(2,1)}, u32[]{:S(2)}, u32[]{:S(2)}) collective-permute-start(bf16[4,128,640]{2,1,0:T(8,128)(2,1)S(1)} %get-tuple-element.45.refs_0_), channel_id=1, source_target_pairs={{0,16},{16,0},{1,17},{17,1},{2,18},{18,2},{3,19},{19,3},{4,20},{20... | collective-permute-start | bytes 1966088 | tf_op jit(solution)/shard_map/ppermute | solution.py:324
  13.8 13.0 %all_to_all.15.asked = s32[8,1,128]{2,1,0:T(1,128)} all-to-all(s32[8,1,128]{2,1,0:T(1,128)} %own_row.1), channel_id=1, replica_groups=mesh['parts'=2,'dp'=2,'tensor'=8] {'tensor'}, dimensions={0} | all-to-all | bytes 8192 | tf_op jit(solution)/shard_map/all_to_all | solution.py:330
  26.8 0.0 collective-permute-done.1
  26.8 0.0 collective-permute-done.refs_5_
  26.8 0.7 collective-permute-start.4
  27.5 1.3 %collective-permute-start.5 = (bf16[640,256]{1,0:T(8,128)(2,1)S(1)}, bf16[640,256]{1,0:T(8,128)(2,1)S(1)}, u32[]{:S(2)}, u32[]{:S(2)}) collective-permute-start(bf16[640,256]{1,0:T(8,128)(2,1)S(1)} %collective-permute-done.1), channel_id=1, source_target_pairs={{2,0},{3,1},{4,6},{5,7},{10,8},{11,9},{12,14},{13,15},{18,16},{19,... | collective-permute-start | bytes 983048 | tf_op jit(solution)/shard_map/ppermute | solution.py:349
  28.8 5.1 %pick_panels.1 = (bf16[8,384,128]{2,1,0:T(8,128)(2,1)}, s32[8]{0:T(128)}) custom-call(s32[8,1,128]{2,1,0:T(1,128)} %all_to_all.15.asked, bf16[32,320,8,128]{3,2,1,0:T(8,128)(2,1)} %bitcast.23, bf16[32,64,8,128]{3,2,1,0:T(8,128)(2,1)} %bitcast.24), custom_call_target="tpu_custom_call" | custom-call | bytes 41943040 | tf_op jit(solution)/shard_map/pick_panels/pallas_call | solution.py:355
  33.9 0.0 copy-done.5
  34.0 0.0 collective-permute-done.4
  34.0 3.4 %collective-permute-done.5 = bf16[640,256]{1,0:T(8,128)(2,1)S(1)} collective-permute-done((bf16[640,256]{1,0:T(8,128)(2,1)S(1)}, bf16[640,256]{1,0:T(8,128)(2,1)S(1)}, u32[]{:S(2)}, u32[]{:S(2)}) %collective-permute-start.5) | collective-permute-done | bytes 327712 | tf_op jit(solution)/shard_map/ppermute | solution.py:349
  37.4 0.0 collective-permute-done.2.refs_2_
  37.4 0.0 collective-permute-done.3.refs_1_
  37.4 4.3 %all-to-all-start.1 = ((bf16[8,384,128]{2,1,0:T(8,128)(2,1)}), bf16[8,384,128]{2,1,0:T(8,128)(2,1)S(1)}, u32[]{:S(2)}, u32[]{:S(2)}) async-start(bf16[8,384,128]{2,1,0:T(8,128)(2,1)} %get-tuple-element.55), calls=%async_computation.1 | async-start | bytes 1572864 | tf_op jit(solution)/shard_map/all_to_all | solution.py:374
  41.7 1.5 %collective-permute-start.7 = (bf16[4,128,640]{2,1,0:T(8,128)(2,1)}, bf16[4,128,640]{2,1,0:T(8,128)(2,1)}, u32[]{:S(2)}, u32[]{:S(2)}) collective-permute-start(bf16[4,128,640]{2,1,0:T(8,128)(2,1)} %collective-permute-done.2.refs_2_), channel_id=1, source_target_pairs={{0,16},{16,0},{1,17},{17,1},{2,18},{18,2},{3,19},{19,3},{4,20},{20... | collective-permute-start | bytes 1966088 | tf_op jit(solution)/shard_map/ppermute | solution.py:324
  43.3 0.0 copy-start.8
  43.3 0.1 collective-permute-start.10
  43.4 1.3 %collective-permute-start.6 = (bf16[640,256]{1,0:T(8,128)(2,1)S(1)}, bf16[640,256]{1,0:T(8,128)(2,1)S(1)}, u32[]{:S(2)}, u32[]{:S(2)}) collective-permute-start(bf16[640,256]{1,0:T(8,128)(2,1)S(1)} %collective-permute-done.4), channel_id=1, source_target_pairs={{2,0},{3,1},{4,6},{5,7},{10,8},{11,9},{12,14},{13,15},{18,16},{19,... | collective-permute-start | bytes 983048 | tf_op jit(solution)/shard_map/ppermute | solution.py:378
  44.7 0.0 copy-done.10
  44.7 0.6 collective-permute-start.8
  45.2 0.1 collective-permute-start.9
  45.3 0.6 copy-done.3
  45.9 9.5 %clear_rows.1 = (f32[16,320,8,1,128]{4,3,2,1,0:T(1,128)}, f32[16,64,8,1,128]{4,3,2,1,0:T(1,128)}, s32[1]{0:T(128)}) custom-call(s32[8]{0:T(128)S(1)} %copy-done.3), custom_call_target="tpu_custom_call" | custom-call | bytes 29360128 | tf_op jit(solution)/shard_map/clear_rows/pallas_call | solution.py:384
  55.4 3.9 %pair_columns.1.xs_ref = bf16[8,256,320]{2,1,0:T(8,128)(2,1)} custom-call(bf16[128,5120]{1,0:T(8,128)(2,1)} %x_ref.1), custom_call_target="tpu_custom_call" | custom-call | flops 2147483648 | bytes 4194304 | tf_op jit(solution)/shard_map/pair_columns/pallas_call | solution.py:391
  59.3 0.0 collective-permute-done.10.refs_10_
  59.3 3.2 %collective-permute-done.6 = bf16[640,256]{1,0:T(8,128)(2,1)S(1)} collective-permute-done((bf16[640,256]{1,0:T(8,128)(2,1)S(1)}, bf16[640,256]{1,0:T(8,128)(2,1)S(1)}, u32[]{:S(2)}, u32[]{:S(2)}) %collective-permute-start.6) | collective-permute-done | bytes 327712 | tf_op jit(solution)/shard_map/ppermute | solution.py:378
  62.5 0.0 collective-permute-done.8.refs_8_
  62.5 0.0 collective-permute-done.9.refs_9_
  62.6 0.0 collective-permute-done.7.refs_3_
  62.6 0.7 copy-done.13
  63.3 0.1 copy-done.14
  63.4 0.0 all-to-all-done.1.pieces
  63.4 1.4 %copy-done.7 = bf16[8,256,320]{2,1,0:T(8,128)(2,1)S(1)} copy-done((bf16[8,256,320]{2,1,0:T(8,128)(2,1)S(1)}, bf16[8,256,320]{2,1,0:T(8,128)(2,1)}, u32[]{:S(2)}) %copy-start.7) | copy-done | bytes 1310744
  64.8 3.0 %adapter.1 = (bf16[8,384,128]{2,1,0:T(8,128)(2,1)}, f32[128,1024]{1,0:T(8,128)S(1)}) custom-call(bf16[8,256,320]{2,1,0:T(8,128)(2,1)S(1)} %copy-done.7, bf16[128,1024]{1,0:T(8,128)(2,1)S(1)} %copy-done.6, bf16[8,384,128]{2,1,0:T(8,128)(2,1)S(1)} %all-to-all-done.1.pieces, s32[1]{0:T(128)} %get-tuple-element.63._), custom_call_target="tpu_custom_call" | custom-call | flops 3221225472 | bytes 8388608 | tf_op jit(solution)/shard_map/adapter/pallas_call | solution.py:403
  67.8 0.0 copy-done.8
  67.8 4.5 %all-to-all-start.2 = ((bf16[8,384,128]{2,1,0:T(8,128)(2,1)}), bf16[8,384,128]{2,1,0:T(8,128)(2,1)S(1)}, u32[]{:S(2)}, u32[]{:S(2)}) async-start(bf16[8,384,128]{2,1,0:T(8,128)(2,1)} %get-tuple-element.66.refs_12_), calls=%async_computation.2 | async-start | bytes 1572864 | tf_op jit(solution)/shard_map/all_to_all | solution.py:433
  72.4 0.1 collective-permute-start.11
  72.5 0.6 pad_add_fusion.where
  73.1 1.0 %collective-permute-done.11.refs_11_ = bf16[640,256]{1,0:T(8,128)(2,1)S(1)} collective-permute-done((bf16[640,256]{1,0:T(8,128)(2,1)S(1)}, bf16[640,256]{1,0:T(8,128)(2,1)S(1)}, u32[]{:S(2)}, u32[]{:S(2)}) %collective-permute-start.11) | collective-permute-done | bytes 327712 | tf_op jit(solution)/shard_map/ppermute | solution.py:321
  74.1 0.7 copy-done.15
  74.8 5.3 %frozen_part.1 = (f32[128,512]{1,0:T(8,128)}, bf16[128,512]{1,0:T(8,128)(2,1)}, bf16[128,512]{1,0:T(8,128)(2,1)}, bf16[128,512]{1,0:T(8,128)(2,1)}) custom-call(s32[4]{0:T(128)} %pad_add_fusion.where, bf16[4,128,640]{2,1,0:T(8,128)(2,1)} %copy-done.5, bf16[4,128,640]{2,1,0:T(8,128)(2,1)} %collective-permute-done.3.refs_1_, ...), custom_call_target="tpu_custom_call" | custom-call | flops 4294967296 | bytes 8388608 | tf_op jit(solution)/shard_map/frozen_part/pallas_call | solution.py:418
  80.1 2.1 %collective-permute-start.12 = (bf16[128,512]{1,0:T(8,128)(2,1)}, bf16[128,512]{1,0:T(8,128)(2,1)S(1)}, u32[]{:S(2)}, u32[]{:S(2)}) collective-permute-start(bf16[128,512]{1,0:T(8,128)(2,1)} %get-tuple-element.73), channel_id=1, source_target_pairs={{0,1},{1,0},{2,3},{3,2},{4,5},{5,4},{6,7},{7,6},{8,9},{9,8},{10,11... | collective-permute-start | bytes 393224 | tf_op jit(solution)/shard_map/ppermute | solution.py:318
  82.2 0.5 collective-permute-start.13
  82.7 1.0 %collective-permute-start.14 = (bf16[128,512]{1,0:T(8,128)(2,1)}, bf16[128,512]{1,0:T(8,128)(2,1)S(1)}, u32[]{:S(2)}, u32[]{:S(2)}) collective-permute-start(bf16[128,512]{1,0:T(8,128)(2,1)} %get-tuple-element.75), channel_id=1, source_target_pairs={{0,17},{1,16},{2,19},{3,18},{4,21},{5,20},{6,23},{7,22},{16,1},{17... | collective-permute-start | bytes 393224 | tf_op jit(solution)/shard_map/ppermute | solution.py:434
  83.7 4.5 %collective-permute-done.12 = bf16[128,512]{1,0:T(8,128)(2,1)S(1)} collective-permute-done((bf16[128,512]{1,0:T(8,128)(2,1)}, bf16[128,512]{1,0:T(8,128)(2,1)S(1)}, u32[]{:S(2)}, u32[]{:S(2)}) %collective-permute-start.12) | collective-permute-done | bytes 131104 | tf_op jit(solution)/shard_map/ppermute | solution.py:318
  88.2 0.0 collective-permute-done.13
  88.2 2.9 %collective-permute-done.14 = bf16[128,512]{1,0:T(8,128)(2,1)S(1)} collective-permute-done((bf16[128,512]{1,0:T(8,128)(2,1)}, bf16[128,512]{1,0:T(8,128)(2,1)S(1)}, u32[]{:S(2)}, u32[]{:S(2)}) %collective-permute-start.14) | collective-permute-done | bytes 131104 | tf_op jit(solution)/shard_map/ppermute | solution.py:434
  91.2 1.7 %all-to-all-done.2.rest_0_ = bf16[8,384,128]{2,1,0:T(8,128)(2,1)S(1)} async-done(((bf16[8,384,128]{2,1,0:T(8,128)(2,1)}), bf16[8,384,128]{2,1,0:T(8,128)(2,1)S(1)}, u32[]{:S(2)}, u32[]{:S(2)}) %all-to-all-start.2) | async-done | bytes 786464 | tf_op jit(solution)/shard_map/all_to_all | solution.py:433
  92.9 0.0 collective-permute-start.16
  92.9 0.5 collective-permute-start.15
  93.4 1.0 %convert_add_fusion = (f32[128,512]{1,0:T(8,128)S(1)}, f32[128,512]{1,0:T(8,128)S(1)}) fusion(bf16[128,512]{1,0:T(8,128)(2,1)S(1)} %collective-permute-done.14, bf16[128,512]{1,0:T(8,128)(2,1)S(1)} %collective-permute-done.13, f32[128,512]{1,0:T(8,128)} %get-tuple-element.72, bf16[128,512]{1,0:T(8,128)(2,1)S(1)} %collective-permute-done.12), kind=kLoop, calls=%fused_computation.4 | loop fusion | flops 327680 | bytes 1179648 | tf_op jit(solution)/shard_map/add | solution.py:461
  94.5 0.8 fusion
  95.2 0.0 collective-permute-done.15.rows_core
  95.2 0.0 collective-permute-done.16.rest_1_
  95.2 2.7 %place_rows.1 = (f32[16,320,8,1,128]{4,3,2,1,0:T(1,128)}, f32[16,64,8,1,128]{4,3,2,1,0:T(1,128)}) custom-call(s32[1]{0:T(128)} %bitcast.9.first_row, s32[8]{0:T(128)S(1)} %copy-done.4, s32[8]{0:T(128)S(1)} %collective-permute-done.15.rows_core, bf16[8,384,128]{2,1,0:T(8,128)(2,1)S(1)} %all-to-all-done.2.rest_0_, ...), custom_call_target="tpu_custom_call", output_to_operand_aliasing={{0}: (5, {}), {1}: (6, {})} | custom-call | bytes 16777216 | tf_op jit(solution)/shard_map/place_rows/pallas_call | solution.py:438
  (22 shorter events, 0.2 us)
Async XLA Ops:
  0.6 2.0 %copy-start = (bf16[640,512]{1,0:T(8,128)(2,1)S(1)}, bf16[640,512]{1,0:T(8,128)(2,1)}, u32[]{:S(2)}) copy-start(bf16[640,512]{1,0:T(8,128)(2,1)} %param.9) | copy-start | bytes 1966084
  2.7 42.0 %copy-start.10 = (bf16[640,256]{1,0:T(8,128)(2,1)}, bf16[640,256]{1,0:T(8,128)(2,1)S(1)}, u32[]{:S(2)}) copy-start(bf16[640,256]{1,0:T(8,128)(2,1)S(1)} %constant_dynamic-slice_fusion.refs_4_) | copy-start | bytes 983044
  2.7 24.1 %collective-permute-start.1 = (bf16[640,256]{1,0:T(8,128)(2,1)S(1)}, bf16[640,256]{1,0:T(8,128)(2,1)S(1)}, u32[]{:S(2)}, u32[]{:S(2)}) collective-permute-start(bf16[640,256]{1,0:T(8,128)(2,1)S(1)} %constant_dynamic-slice_fusion.refs_4_), channel_id=1, source_target_pairs={{2,4},{3,5},{4,2},{5,3},{10,12},{11,13},{12,10},{13,11},{18,20},{1... | collective-permute-start | bytes 983048 | tf_op jit(solution)/shard_map/ppermute | solution.py:346
  3.4 23.5 %collective-permute-start = (bf16[640,256]{1,0:T(8,128)(2,1)S(1)}, bf16[640,256]{1,0:T(8,128)(2,1)S(1)}, u32[]{:S(2)}, u32[]{:S(2)}) collective-permute-start(bf16[640,256]{1,0:T(8,128)(2,1)S(1)} %constant_dynamic-slice_fusion.refs_4_), channel_id=1, source_target_pairs={{0,2},{1,3},{2,0},{3,1},{4,6},{5,7},{6,4},{7,5},{8,10},{9,11},{10,... | collective-permute-start | bytes 983048 | tf_op jit(solution)/shard_map/ppermute | solution.py:318
  9.3 1.3 %copy-start.2 = (bf16[128,5120]{1,0:T(8,128)(2,1)S(1)}, bf16[128,5120]{1,0:T(8,128)(2,1)}, u32[]{:S(2)}) copy-start(bf16[128,5120]{1,0:T(8,128)(2,1)} %x_ref.1) | copy-start | bytes 3932164
  10.7 23.3 %copy-start.5 = (bf16[4,128,640]{2,1,0:T(8,128)(2,1)}, bf16[4,128,640]{2,1,0:T(8,128)(2,1)S(1)}, u32[]{:S(2)}) copy-start(bf16[4,128,640]{2,1,0:T(8,128)(2,1)S(1)} %get-tuple-element.45.refs_0_) | copy-start | bytes 1966084
  10.7 26.7 %collective-permute-start.2 = (bf16[4,128,640]{2,1,0:T(8,128)(2,1)S(1)}, bf16[4,128,640]{2,1,0:T(8,128)(2,1)}, u32[]{:S(2)}, u32[]{:S(2)}) collective-permute-start(bf16[4,128,640]{2,1,0:T(8,128)(2,1)S(1)} %get-tuple-element.50), channel_id=1, source_target_pairs={{0,1},{1,0},{2,3},{3,2},{4,5},{5,4},{6,7},{7,6},{8,9},{9,8},{10,11... | collective-permute-start | bytes 1966088 | tf_op jit(solution)/shard_map/ppermute | solution.py:318
  12.3 25.1 %collective-permute-start.3 = (bf16[4,128,640]{2,1,0:T(8,128)(2,1)S(1)}, bf16[4,128,640]{2,1,0:T(8,128)(2,1)}, u32[]{:S(2)}, u32[]{:S(2)}) collective-permute-start(bf16[4,128,640]{2,1,0:T(8,128)(2,1)S(1)} %get-tuple-element.45.refs_0_), channel_id=1, source_target_pairs={{0,16},{16,0},{1,17},{17,1},{2,18},{18,2},{3,19},{19,3},{4,20},{20... | collective-permute-start | bytes 1966088 | tf_op jit(solution)/shard_map/ppermute | solution.py:324
  26.8 18.4 %copy-start.11 = (bf16[640,256]{1,0:T(8,128)(2,1)}, bf16[640,256]{1,0:T(8,128)(2,1)S(1)}, u32[]{:S(2)}) copy-start(bf16[640,256]{1,0:T(8,128)(2,1)S(1)} %collective-permute-done.refs_5_) | copy-start | bytes 983044
  26.8 7.1 %collective-permute-start.4 = (bf16[640,256]{1,0:T(8,128)(2,1)S(1)}, bf16[640,256]{1,0:T(8,128)(2,1)S(1)}, u32[]{:S(2)}, u32[]{:S(2)}) collective-permute-start(bf16[640,256]{1,0:T(8,128)(2,1)S(1)} %collective-permute-done.refs_5_), channel_id=1, source_target_pairs={{2,4},{3,5},{4,2},{5,3},{10,12},{11,13},{12,10},{13,11},{18,20},{1... | collective-permute-start | bytes 983048 | tf_op jit(solution)/shard_map/ppermute | solution.py:348
  27.5 9.9 %collective-permute-start.5 = (bf16[640,256]{1,0:T(8,128)(2,1)S(1)}, bf16[640,256]{1,0:T(8,128)(2,1)S(1)}, u32[]{:S(2)}, u32[]{:S(2)}) collective-permute-start(bf16[640,256]{1,0:T(8,128)(2,1)S(1)} %collective-permute-done.1), channel_id=1, source_target_pairs={{2,0},{3,1},{4,6},{5,7},{10,8},{11,9},{12,14},{13,15},{18,16},{19,... | collective-permute-start | bytes 983048 | tf_op jit(solution)/shard_map/ppermute | solution.py:349
  37.4 26.0 %all-to-all-start.1 = ((bf16[8,384,128]{2,1,0:T(8,128)(2,1)}), bf16[8,384,128]{2,1,0:T(8,128)(2,1)S(1)}, u32[]{:S(2)}, u32[]{:S(2)}) async-start(bf16[8,384,128]{2,1,0:T(8,128)(2,1)} %get-tuple-element.55), calls=%async_computation.1 | async-start | bytes 1572864 | tf_op jit(solution)/shard_map/all_to_all | solution.py:374
  41.7 20.9 %collective-permute-start.7 = (bf16[4,128,640]{2,1,0:T(8,128)(2,1)}, bf16[4,128,640]{2,1,0:T(8,128)(2,1)}, u32[]{:S(2)}, u32[]{:S(2)}) collective-permute-start(bf16[4,128,640]{2,1,0:T(8,128)(2,1)} %collective-permute-done.2.refs_2_), channel_id=1, source_target_pairs={{0,16},{16,0},{1,17},{17,1},{2,18},{18,2},{3,19},{19,3},{4,20},{20... | collective-permute-start | bytes 1966088 | tf_op jit(solution)/shard_map/ppermute | solution.py:324
  43.2 20.2 %copy-start.6 = (bf16[128,1024]{1,0:T(8,128)(2,1)S(1)}, bf16[128,1024]{1,0:T(8,128)(2,1)}, u32[]{:S(2)}) copy-start(bf16[128,1024]{1,0:T(8,128)(2,1)} %g_ref.1) | copy-start | bytes 786436
  43.3 24.5 %copy-start.8 = (bf16[640,256]{1,0:T(8,128)(2,1)}, bf16[640,256]{1,0:T(8,128)(2,1)S(1)}, u32[]{:S(2)}) copy-start(bf16[640,256]{1,0:T(8,128)(2,1)S(1)} %broadcast_select_fusion.1.refs_6_) | copy-start | bytes 983044
  43.3 16.0 %collective-permute-start.10 = (bf16[640,256]{1,0:T(8,128)(2,1)S(1)}, bf16[640,256]{1,0:T(8,128)(2,1)S(1)}, u32[]{:S(2)}, u32[]{:S(2)}) collective-permute-start(bf16[640,256]{1,0:T(8,128)(2,1)S(1)} %broadcast_select_fusion.1.refs_6_), channel_id=1, source_target_pairs={{0,8},{8,0},{1,9},{9,1},{2,10},{10,2},{3,11},{11,3},{4,12},{12,4},... | collective-permute-start | bytes 983048 | tf_op jit(solution)/shard_map/ppermute | solution.py:321
  43.4 19.2 %collective-permute-start.6 = (bf16[640,256]{1,0:T(8,128)(2,1)S(1)}, bf16[640,256]{1,0:T(8,128)(2,1)S(1)}, u32[]{:S(2)}, u32[]{:S(2)}) collective-permute-start(bf16[640,256]{1,0:T(8,128)(2,1)S(1)} %collective-permute-done.4), channel_id=1, source_target_pairs={{2,0},{3,1},{4,6},{5,7},{10,8},{11,9},{12,14},{13,15},{18,16},{19,... | collective-permute-start | bytes 983048 | tf_op jit(solution)/shard_map/ppermute | solution.py:378
  44.7 17.9 %collective-permute-start.8 = (bf16[640,256]{1,0:T(8,128)(2,1)S(1)}, bf16[640,256]{1,0:T(8,128)(2,1)S(1)}, u32[]{:S(2)}, u32[]{:S(2)}) collective-permute-start(bf16[640,256]{1,0:T(8,128)(2,1)S(1)} %constant_dynamic-slice_fusion.refs_4_), channel_id=1, source_target_pairs={{0,8},{8,0},{1,9},{9,1},{2,10},{10,2},{3,11},{11,3},{4,12},{12,4},... | collective-permute-start | bytes 983048 | tf_op jit(solution)/shard_map/ppermute | solution.py:321
  45.2 17.3 %collective-permute-start.9 = (bf16[640,256]{1,0:T(8,128)(2,1)S(1)}, bf16[640,256]{1,0:T(8,128)(2,1)S(1)}, u32[]{:S(2)}, u32[]{:S(2)}) collective-permute-start(bf16[640,256]{1,0:T(8,128)(2,1)S(1)} %collective-permute-done.refs_5_), channel_id=1, source_target_pairs={{0,8},{8,0},{1,9},{9,1},{2,10},{10,2},{3,11},{11,3},{4,12},{12,4},... | collective-permute-start | bytes 983048 | tf_op jit(solution)/shard_map/ppermute | solution.py:321
  45.3 0.6 copy-start.3
  59.3 3.2 %copy-start.12 = (bf16[640,256]{1,0:T(8,128)(2,1)}, bf16[640,256]{1,0:T(8,128)(2,1)S(1)}, u32[]{:S(2)}) copy-start(bf16[640,256]{1,0:T(8,128)(2,1)S(1)} %collective-permute-done.10.refs_10_) | copy-start | bytes 983044
  62.5 0.7 copy-start.13
  62.6 0.8 copy-start.14
  63.4 1.4 %copy-start.7 = (bf16[8,256,320]{2,1,0:T(8,128)(2,1)S(1)}, bf16[8,256,320]{2,1,0:T(8,128)(2,1)}, u32[]{:S(2)}) copy-start(bf16[8,256,320]{2,1,0:T(8,128)(2,1)} %pair_columns.1.xs_ref) | copy-start | bytes 3932164
  67.8 25.0 %all-to-all-start.2 = ((bf16[8,384,128]{2,1,0:T(8,128)(2,1)}), bf16[8,384,128]{2,1,0:T(8,128)(2,1)S(1)}, u32[]{:S(2)}, u32[]{:S(2)}) async-start(bf16[8,384,128]{2,1,0:T(8,128)(2,1)} %get-tuple-element.66.refs_12_), calls=%async_computation.2 | async-start | bytes 1572864 | tf_op jit(solution)/shard_map/all_to_all | solution.py:433
  72.4 1.7 %copy-start.9 = (bf16[640,256]{1,0:T(8,128)(2,1)}, bf16[640,256]{1,0:T(8,128)(2,1)S(1)}, u32[]{:S(2)}) copy-start(bf16[640,256]{1,0:T(8,128)(2,1)S(1)} %broadcast_select_fusion.refs_7_) | copy-start | bytes 983044
  72.4 1.7 %collective-permute-start.11 = (bf16[640,256]{1,0:T(8,128)(2,1)S(1)}, bf16[640,256]{1,0:T(8,128)(2,1)S(1)}, u32[]{:S(2)}, u32[]{:S(2)}) collective-permute-start(bf16[640,256]{1,0:T(8,128)(2,1)S(1)} %broadcast_select_fusion.refs_7_), channel_id=1, source_target_pairs={{0,8},{8,0},{1,9},{9,1},{2,10},{10,2},{3,11},{11,3},{4,12},{12,4},... | collective-permute-start | bytes 983048 | tf_op jit(solution)/shard_map/ppermute | solution.py:321
  73.1 19.8 %copy-start.4 = (s32[8]{0:T(128)S(1)}, s32[8]{0:T(128)}, u32[]{:S(2)}) copy-start(s32[8]{0:T(128)} %get-tuple-element.62.after_ref.rows_here) | copy-start | bytes 100
  74.1 0.7 copy-start.15
  80.1 8.1 %collective-permute-start.12 = (bf16[128,512]{1,0:T(8,128)(2,1)}, bf16[128,512]{1,0:T(8,128)(2,1)S(1)}, u32[]{:S(2)}, u32[]{:S(2)}) collective-permute-start(bf16[128,512]{1,0:T(8,128)(2,1)} %get-tuple-element.73), channel_id=1, source_target_pairs={{0,1},{1,0},{2,3},{3,2},{4,5},{5,4},{6,7},{7,6},{8,9},{9,8},{10,11... | collective-permute-start | bytes 393224 | tf_op jit(solution)/shard_map/ppermute | solution.py:318
  82.2 6.0 %collective-permute-start.13 = (bf16[128,512]{1,0:T(8,128)(2,1)}, bf16[128,512]{1,0:T(8,128)(2,1)S(1)}, u32[]{:S(2)}, u32[]{:S(2)}) collective-permute-start(bf16[128,512]{1,0:T(8,128)(2,1)} %get-tuple-element.74), channel_id=1, source_target_pairs={{0,16},{16,0},{1,17},{17,1},{2,18},{18,2},{3,19},{19,3},{4,20},{20... | collective-permute-start | bytes 393224 | tf_op jit(solution)/shard_map/ppermute | solution.py:324
  82.7 8.4 %collective-permute-start.14 = (bf16[128,512]{1,0:T(8,128)(2,1)}, bf16[128,512]{1,0:T(8,128)(2,1)S(1)}, u32[]{:S(2)}, u32[]{:S(2)}) collective-permute-start(bf16[128,512]{1,0:T(8,128)(2,1)} %get-tuple-element.75), channel_id=1, source_target_pairs={{0,17},{1,16},{2,19},{3,18},{4,21},{5,20},{6,23},{7,22},{16,1},{17... | collective-permute-start | bytes 393224 | tf_op jit(solution)/shard_map/ppermute | solution.py:434
  92.9 2.4 %collective-permute-start.16 = (bf16[8,384,128]{2,1,0:T(8,128)(2,1)S(1)}, bf16[8,384,128]{2,1,0:T(8,128)(2,1)S(1)}, u32[]{:S(2)}, u32[]{:S(2)}) collective-permute-start(bf16[8,384,128]{2,1,0:T(8,128)(2,1)S(1)} %all-to-all-done.2.rest_0_), channel_id=1, source_target_pairs={{0,8},{8,0},{1,9},{9,1},{2,10},{10,2},{3,11},{11,3},{4,12},{12,4},... | collective-permute-start | bytes 2359304 | tf_op jit(solution)/shard_map/ppermute | solution.py:321
  92.9 2.3 %collective-permute-start.15 = (s32[8]{0:T(128)S(1)}, s32[8]{0:T(128)S(1)}, u32[]{:S(2)}, u32[]{:S(2)}) collective-permute-start(s32[8]{0:T(128)S(1)} %copy-done.4), channel_id=1, source_target_pairs={{0,8},{8,0},{1,9},{9,1},{2,10},{10,2},{3,11},{11,3},{4,12},{12,4},... | collective-permute-start | bytes 104 | tf_op jit(solution)/shard_map/ppermute | solution.py:321
  95.2 2.7 %copy-start.1 = (bf16[640,512]{1,0:T(8,128)(2,1)S(1)}, bf16[640,512]{1,0:T(8,128)(2,1)}, u32[]{:S(2)}) copy-start(bf16[640,512]{1,0:T(8,128)(2,1)} %param.9) | copy-start | bytes 1966084

commit v12 on v11

--- a/solution.py
+++ b/solution.py
@@ -103,14 +103,15 @@
     out_ref[...] = jnp.full(out_ref.shape, slot_ref[block_ref[0]], jnp.int32)
 
 
-def split_kernel(where, x_ref, mine_ref, theirs_ref):
+def split_kernel(where, x_ref, mine_ref, *theirs_refs):
     inner = where[0]
     outer, rows, width = mine_ref.shape
+    each = outer // len(theirs_refs)
     for k in range(outer):
         own = pl.multiple_of((2 * k + inner) * width, LANES)
         other = pl.multiple_of((2 * k + 1 - inner) * width, LANES)
         mine_ref[k] = x_ref[:, pl.ds(own, width)]
-        theirs_ref[k] = x_ref[:, pl.ds(other, width)]
+        theirs_refs[k // each][k % each] = x_ref[:, pl.ds(other, width)]
 
 
 def interleave_kernel(x_ref, out_ref, xs_ref, sems):
@@ -277,14 +278,24 @@
 
 
 def base_kernel(where, *refs):
-    x_from, w_from, out_refs = refs[:4], refs[4:-8], refs[-7:-3]
+    whole, halves, w_from, out_refs = refs[:2], refs[2:6], refs[6:-8], refs[-7:-3]
     x_buf, w_buf, sems = refs[-3:]
     outer, _, rows, depth = x_buf.shape
     width = w_buf.shape[2]
+    each = outer // 2
     fetch_x = [
-        [pltpu.make_async_copy(ref.at[where[k]], x_buf.at[k, b], sems.at[k, b]) for b, ref in enumerate(x_from)]
+        [pltpu.make_async_copy(ref.at[where[k]], x_buf.at[k, b], sems.at[k, b]) for b, ref in enumerate(whole)]
         for k in range(outer)
     ]
+
+    def fetch_half(k, b, begin):
+        for h in range(2):
+            @pl.when(where[k] // each == h)
+            def _():
+                source = halves[2 * b + h].at[where[k] % each]
+                copy = pltpu.make_async_copy(source, x_buf.at[k, 2 + b], sems.at[k, 2 + b])
+                copy.start() if begin else copy.wait()
+
     fetch_w = [
         [pltpu.make_async_copy(w_from[h * outer + k], w_buf.at[h * outer + k], sems.at[k, 4 + h]) for h in range(2)]
         for k in range(outer)
@@ -292,10 +303,14 @@
     for k in range(outer):
         for copy in fetch_x[k] + fetch_w[k]:
             copy.start()
+        for b in range(2):
+            fetch_half(k, b, True)
     total = [0.0, 0.0]
     for k in range(outer):
         for copy in fetch_x[k] + fetch_w[k]:
             copy.wait()
+        for b in range(2):
+            fetch_half(k, b, False)
         left = x_buf[k].reshape(4 * rows, depth)
         for h in range(2):
             total[h] += dot(left, w_buf[h * outer + k])
@@ -334,17 +349,19 @@
     half = lax.dynamic_slice_in_dim(half_from, part * width, width, axis=1)
     block = jax.ShapeDtypeStruct((outer, token_rows, slice_width), jnp.bfloat16)
     token = jax.ShapeDtypeStruct((1,), jnp.int32)
-    x_mine, x_theirs = pl.pallas_call(
-        split_kernel, out_shape=(block, block), in_specs=[SMEM, VMEM], out_specs=(VMEM, VMEM),
+    some = jax.ShapeDtypeStruct((outer // 2, token_rows, slice_width), jnp.bfloat16)
+    x_mine, *x_theirs = pl.pallas_call(
+        split_kernel, out_shape=(block, some, some), in_specs=[SMEM, VMEM], out_specs=[VMEM] * 3,
         name="split_tokens", compiler_params=LIMIT,
     )(x[None], split_from)
-    x_far = exchange(x_theirs, 1)
+    x_far = [exchange(x_theirs[0], 1)]
     y_mine = other_part(x_mine)
     middle = [(t, t ^ 6) for t in range(group) if t // 2 in (1, 2)]
     ends = [(t, t ^ 2) for t in range(group) if t // 2 in (1, 2)]
     near = exchange(half, 2)
     over = lax.ppermute(half, "tensor", middle)
-    near, over, asked = lax.optimization_barrier((near, over, asked))
+    near, over, asked, x_theirs = lax.optimization_barrier((near, over, asked, x_theirs))
+    x_far.append(exchange(x_theirs[1], 1))
     over_near = lax.ppermute(near, "tensor", middle)
     passed = lax.ppermute(over, "tensor", ends)
     pieces = jax.ShapeDtypeStruct((group, down_chunks + up_chunks, LANES), jnp.bfloat16)
@@ -373,7 +390,7 @@
     )
     panels = lax.all_to_all(sent, "tensor", 0, 0)
     rows_core = other_core(rows)
-    y_far = other_part(x_far)
+    y_far = [other_part(part_of) for part_of in x_far]
     inside = (z == 1) | (z == 2)
     passed_near = lax.ppermute(over_near, "tensor", ends)
     quarter = [half, near, jnp.where(inside, over, passed)]
@@ -418,7 +435,7 @@
     own, to_part, to_inner, to_both = pl.pallas_call(
         base_kernel,
         out_shape=sums,
-        in_specs=[SMEM] + [ANY] * (5 + 2 * outer),
+        in_specs=[SMEM] + [ANY] * (7 + 2 * outer),
         out_specs=[VMEM] * 4,
         scratch_shapes=[
             pltpu.VMEM((outer, 4, token_rows, slice_width), jnp.bfloat16),
@@ -428,7 +445,7 @@
         compiler_params=WIDE,
         cost_estimate=cost(flops=4 << 30, read=8 << 20),
         name="frozen_part",
-    )(source, x_mine, y_mine, x_far, y_far, *quarters, terms)
+    )(source, x_mine, y_mine, *x_far, *y_far, *quarters, terms)
     opposite = [(a * group + t, (parts - 1 - a) * group + (t ^ 1)) for a in range(parts) for t in range(group)]
     back = lax.all_to_all(terms, "tensor", 0, 0)
     arrived = (exchange(to_inner, 1), other_part(to_part), lax.ppermute(to_both, ("parts", "tensor"), opposite))

time: 99.1 us -> 97.2 us (0.981)
  blocking collectives: 13 us -> 0 us
  starting transfers between devices: 28.2 us -> 35.8 us
  waiting for transfers between devices: 16.8 us -> 18.6 us
  local copies, waits for them, and re-layouts: 4.96 us -> 6.45 us
    all_to_all x1 -> x0, blocking collectives: 13 us -> none  [fast_body(): asked = lax.all_to_all(row, 'tensor', 0, 0)]
    all_to_all x0 -> x1, waiting for transfers between devices: none -> 4.37 us  [fast_body(): asked = lax.all_to_all(row, 'tensor', 0, 0)]
    all_to_all x0 -> x1, starting transfers between devices: none -> 3.55 us  [fast_body(): asked = lax.all_to_all(row, 'tensor', 0, 0)]
    ppermute x1, waiting for transfers between devices: 3.41 us -> 1.14 us  [fast_body(): passed = lax.ppermute(over, 'tensor', ends)]
    all_to_all x1, starting transfers between devices: 4.53 us -> 6.09 us  [fast_body(): back = lax.all_to_all(terms, 'tensor', 0, 0)]
    unnamed x32 -> x38, local copies, waits for them, and re-layouts: 4.94 us -> 6.43 us
    ppermute x1, waiting for transfers between devices: 3.2 us -> 1.79 us  [fast_body(): passed_near = lax.ppermute(over_near, 'tensor', ends)]
    ppermute x3 -> x4, waiting for transfers between devices: 4.5 us -> 5.84 us  [exchange(): return lax.ppermute(value, 'tensor', [(t, t ^ s) for t in range(group)])]
  transfers between devices with their start and end apart: 19 -> 22, of which waited for: 6 -> 8; matrix products, arithmetic and copies ran while one was open for 3% -> 3% of each run, Pallas kernels for 24% -> 25%
where the time goes in v12:
time: 97.2 us; the launch traced here: 96.6 us
  starting transfers between devices  35.8 us (37%)
  Pallas kernels  31.5 us (32%)
  waiting for transfers between devices  18.6 us (19%)
  local copies, waits for them, and re-layouts  6.45 us (7%)
  other arithmetic  2.55 us (3%)
  between operations  1.66 us (2%)
    ppermute x4, starting transfers between devices, exchange(): return lax.ppermute(value, 'tensor', [(t, t ^ s) for t in range(group)])  10.6 us
    pallas_call x1, Pallas kernels, fast_body(): pl.pallas_call(zero_kernel, out_shape=(down_shape, up_shape, token), in_s...  9.48 us
    unnamed x38, local copies, waits for them, and re-layouts  6.43 us
    all_to_all x1, starting transfers between devices, fast_body(): back = lax.all_to_all(terms, 'tensor', 0, 0)  6.09 us
    ppermute x4, waiting for transfers between devices, exchange(): return lax.ppermute(value, 'tensor', [(t, t ^ s) for t in range(group)])  5.84 us
    pallas_call x1, Pallas kernels, fast_body(): pl.pallas_call(base_kernel, out_shape=sums, in_specs=[SMEM] + [ANY] * (7...  5.26 us
    all_to_all x1, starting transfers between devices, fast_body(): panels = lax.all_to_all(sent, 'tensor', 0, 0)  5.17 us
    pallas_call x1, Pallas kernels, fast_body(): pl.pallas_call(gather_kernel, out_shape=(pieces, jax.ShapeDtypeStruct((gr...  5.12 us
  transfers between devices with their start and end apart: 22, of which 8 were waited for; matrix products, arithmetic and copies ran while one was open for 3% of the time, Pallas kernels for 25%

profile of v12, /device:TPU:0, one launch (start us, length us, event | category | flops | bytes accessed | tf_op | source)
XLA Modules:
  0.0 96.6 jit_solution(9116406350627055501)
XLA Ops:
  0.6 0.0 copy-start
  1.4 1.3 %own_row.1 = s32[8,1,128]{2,1,0:T(1,128)} custom-call(s32[1]{0:T(128)S(6)} %copy.14.block_ref, s32[256]{0:T(256)} %slot_ref.1), custom_call_target="tpu_custom_call" | custom-call | tf_op jit(solution)/shard_map/own_row/pallas_call | solution.py:341
  2.7 0.7 collective-permute-start.1
  3.4 5.9 %collective-permute-start = (bf16[640,256]{1,0:T(8,128)(2,1)S(1)}, bf16[640,256]{1,0:T(8,128)(2,1)}, u32[]{:S(2)}, u32[]{:S(2)}) collective-permute-start(bf16[640,256]{1,0:T(8,128)(2,1)S(1)} %constant_dynamic-slice_fusion.refs_6_), channel_id=1, source_target_pairs={{0,2},{1,3},{2,0},{3,1},{4,6},{5,7},{6,4},{7,5},{8,10},{9,11},{10,... | collective-permute-start | bytes 983048 | tf_op jit(solution)/shard_map/ppermute | solution.py:333
  9.3 1.3 %copy-done.2 = bf16[128,5120]{1,0:T(8,128)(2,1)S(1)} copy-done((bf16[128,5120]{1,0:T(8,128)(2,1)S(1)}, bf16[128,5120]{1,0:T(8,128)(2,1)}, u32[]{:S(2)}) %copy-start.2) | copy-done | bytes 1310744
  10.6 0.1 split_tokens.1
  10.7 0.0 copy-start.5
  10.7 1.6 %collective-permute-start.4 = (bf16[4,128,640]{2,1,0:T(8,128)(2,1)S(1)}, bf16[4,128,640]{2,1,0:T(8,128)(2,1)S(1)}, u32[]{:S(2)}, u32[]{:S(2)}) collective-permute-start(bf16[4,128,640]{2,1,0:T(8,128)(2,1)S(1)} %get-tuple-element.49.refs_0_), channel_id=1, source_target_pairs={{0,16},{16,0},{1,17},{17,1},{2,18},{18,2},{3,19},{19,3},{4,20},{20... | collective-permute-start | bytes 1966088 | tf_op jit(solution)/shard_map/ppermute | solution.py:339
  12.3 3.6 %all-to-all-start = ((s32[8,1,128]{2,1,0:T(1,128)}), s32[8,1,128]{2,1,0:T(1,128)S(1)}, u32[]{:S(2)}, u32[]{:S(2)}) async-start(s32[8,1,128]{2,1,0:T(1,128)} %own_row.1), calls=%async_computation | async-start | bytes 8192 | tf_op jit(solution)/shard_map/all_to_all | solution.py:345
  15.8 2.0 %collective-permute-start.2 = (bf16[2,128,640]{2,1,0:T(8,128)(2,1)S(1)}, bf16[2,128,640]{2,1,0:T(8,128)(2,1)}, u32[]{:S(2)}, u32[]{:S(2)}) collective-permute-start(bf16[2,128,640]{2,1,0:T(8,128)(2,1)S(1)} %get-tuple-element.51), channel_id=1, source_target_pairs={{0,1},{1,0},{2,3},{3,2},{4,5},{5,4},{6,7},{7,6},{8,9},{9,8},{10,11... | collective-permute-start | bytes 983048 | tf_op jit(solution)/shard_map/ppermute | solution.py:333
  17.9 4.4 %all-to-all-done.asked = s32[8,1,128]{2,1,0:T(1,128)S(1)} async-done(((s32[8,1,128]{2,1,0:T(1,128)}), s32[8,1,128]{2,1,0:T(1,128)S(1)}, u32[]{:S(2)}, u32[]{:S(2)}) %all-to-all-start) | async-done | bytes 4128 | tf_op jit(solution)/shard_map/all_to_all | solution.py:345
  22.2 0.0 collective-permute-done.1
  22.2 0.0 collective-permute-done.refs_7_
  22.2 0.6 collective-permute-start.3
  22.9 0.7 collective-permute-start.5
  23.5 1.3 %collective-permute-start.6 = (bf16[640,256]{1,0:T(8,128)(2,1)S(1)}, bf16[640,256]{1,0:T(8,128)(2,1)S(1)}, u32[]{:S(2)}, u32[]{:S(2)}) collective-permute-start(bf16[640,256]{1,0:T(8,128)(2,1)S(1)} %collective-permute-done.1), channel_id=1, source_target_pairs={{2,0},{3,1},{4,6},{5,7},{10,8},{11,9},{12,14},{13,15},{18,16},{19,... | collective-permute-start | bytes 983048 | tf_op jit(solution)/shard_map/ppermute | solution.py:366
  24.8 5.1 %pick_panels.1 = (bf16[8,384,128]{2,1,0:T(8,128)(2,1)}, s32[8]{0:T(128)}) custom-call(s32[8,1,128]{2,1,0:T(1,128)} %copy-done.11, bf16[32,320,8,128]{3,2,1,0:T(8,128)(2,1)} %bitcast.23, bf16[32,64,8,128]{3,2,1,0:T(8,128)(2,1)} %bitcast.24), custom_call_target="tpu_custom_call" | custom-call | bytes 41943040 | tf_op jit(solution)/shard_map/pick_panels/pallas_call | solution.py:372
  30.0 0.0 collective-permute-done.2.refs_2_
  30.0 1.4 %collective-permute-done.3.refs_3_ = bf16[2,128,640]{2,1,0:T(8,128)(2,1)S(1)} collective-permute-done((bf16[2,128,640]{2,1,0:T(8,128)(2,1)S(1)}, bf16[2,128,640]{2,1,0:T(8,128)(2,1)S(1)}, u32[]{:S(2)}, u32[]{:S(2)}) %collective-permute-start.3) | collective-permute-done | bytes 327712 | tf_op jit(solution)/shard_map/ppermute | solution.py:333
  31.4 0.0 collective-permute-done.5
  31.4 1.1 %collective-permute-done.6 = bf16[640,256]{1,0:T(8,128)(2,1)S(1)} collective-permute-done((bf16[640,256]{1,0:T(8,128)(2,1)S(1)}, bf16[640,256]{1,0:T(8,128)(2,1)S(1)}, u32[]{:S(2)}, u32[]{:S(2)}) %collective-permute-start.6) | collective-permute-done | bytes 327712 | tf_op jit(solution)/shard_map/ppermute | solution.py:366
  32.5 0.0 collective-permute-done.4.refs_1_
  32.5 0.8 copy-done.12
  33.3 5.2 %all-to-all-start.1 = ((bf16[8,384,128]{2,1,0:T(8,128)(2,1)}), bf16[8,384,128]{2,1,0:T(8,128)(2,1)S(1)}, u32[]{:S(2)}, u32[]{:S(2)}) async-start(bf16[8,384,128]{2,1,0:T(8,128)(2,1)} %get-tuple-element.62), calls=%async_computation.1 | async-start | bytes 1572864 | tf_op jit(solution)/shard_map/all_to_all | solution.py:391
  38.6 0.1 collective-permute-start.12
  38.7 0.6 collective-permute-start.8
  39.2 1.5 %collective-permute-start.9 = (bf16[2,128,640]{2,1,0:T(8,128)(2,1)}, bf16[2,128,640]{2,1,0:T(8,128)(2,1)S(1)}, u32[]{:S(2)}, u32[]{:S(2)}) collective-permute-start(bf16[2,128,640]{2,1,0:T(8,128)(2,1)} %copy-done.13), channel_id=1, source_target_pairs={{0,16},{16,0},{1,17},{17,1},{2,18},{18,2},{3,19},{19,3},{4,20},{20... | collective-permute-start | bytes 983048 | tf_op jit(solution)/shard_map/ppermute | solution.py:339
  40.7 1.3 %collective-permute-start.7 = (bf16[640,256]{1,0:T(8,128)(2,1)S(1)}, bf16[640,256]{1,0:T(8,128)(2,1)S(1)}, u32[]{:S(2)}, u32[]{:S(2)}) collective-permute-start(bf16[640,256]{1,0:T(8,128)(2,1)S(1)} %collective-permute-done.5), channel_id=1, source_target_pairs={{2,0},{3,1},{4,6},{5,7},{10,8},{11,9},{12,14},{13,15},{18,16},{19,... | collective-permute-start | bytes 983048 | tf_op jit(solution)/shard_map/ppermute | solution.py:395
  42.0 0.1 collective-permute-start.10
  42.1 0.0 collective-permute-done.12.refs_12_
  42.1 0.7 copy-done.14
  42.9 0.5 collective-permute-start.11
  43.4 0.7 copy-done.3
  44.0 9.5 %clear_rows.1 = (f32[16,320,8,1,128]{4,3,2,1,0:T(1,128)}, f32[16,64,8,1,128]{4,3,2,1,0:T(1,128)}, s32[1]{0:T(128)}) custom-call(s32[8]{0:T(128)S(1)} %copy-done.3), custom_call_target="tpu_custom_call" | custom-call | bytes 29360128 | tf_op jit(solution)/shard_map/clear_rows/pallas_call | solution.py:401
  53.5 3.9 %pair_columns.1.xs_ref = bf16[8,256,320]{2,1,0:T(8,128)(2,1)} custom-call(bf16[128,5120]{1,0:T(8,128)(2,1)} %x_ref.1), custom_call_target="tpu_custom_call" | custom-call | flops 2147483648 | bytes 4194304 | tf_op jit(solution)/shard_map/pair_columns/pallas_call | solution.py:408
  57.4 0.0 collective-permute-done.8.refs_4_
  57.4 0.0 collective-permute-done.9.refs_5_
  57.4 1.8 %collective-permute-done.7 = bf16[640,256]{1,0:T(8,128)(2,1)S(1)} collective-permute-done((bf16[640,256]{1,0:T(8,128)(2,1)S(1)}, bf16[640,256]{1,0:T(8,128)(2,1)S(1)}, u32[]{:S(2)}, u32[]{:S(2)}) %collective-permute-start.7) | collective-permute-done | bytes 327712 | tf_op jit(solution)/shard_map/ppermute | solution.py:395
  59.2 0.0 collective-permute-done.10.refs_10_
  59.2 0.0 collective-permute-done.11.refs_11_
  59.3 0.7 copy-done.17
  59.9 0.0 all-to-all-done.1.pieces
  59.9 1.4 %copy-done.7 = bf16[8,256,320]{2,1,0:T(8,128)(2,1)S(1)} copy-done((bf16[8,256,320]{2,1,0:T(8,128)(2,1)S(1)}, bf16[8,256,320]{2,1,0:T(8,128)(2,1)}, u32[]{:S(2)}) %copy-start.7) | copy-done | bytes 1310744
  61.4 3.0 %adapter.1 = (bf16[8,384,128]{2,1,0:T(8,128)(2,1)}, f32[128,1024]{1,0:T(8,128)S(1)}) custom-call(bf16[8,256,320]{2,1,0:T(8,128)(2,1)S(1)} %copy-done.7, bf16[128,1024]{1,0:T(8,128)(2,1)S(1)} %copy-done.6, bf16[8,384,128]{2,1,0:T(8,128)(2,1)S(1)} %all-to-all-done.1.pieces, s32[1]{0:T(128)} %get-tuple-element.71._), custom_call_target="tpu_custom_call" | custom-call | flops 3221225472 | bytes 8388608 | tf_op jit(solution)/shard_map/adapter/pallas_call | solution.py:420
  64.3 6.1 %all-to-all-start.2 = ((bf16[8,384,128]{2,1,0:T(8,128)(2,1)}), bf16[8,384,128]{2,1,0:T(8,128)(2,1)S(1)}, u32[]{:S(2)}, u32[]{:S(2)}) async-start(bf16[8,384,128]{2,1,0:T(8,128)(2,1)} %get-tuple-element.74.refs_14_), calls=%async_computation.2 | async-start | bytes 1572864 | tf_op jit(solution)/shard_map/all_to_all | solution.py:450
  70.5 0.1 collective-permute-start.13
  70.6 0.7 pad_add_fusion.where
  71.2 0.9 collective-permute-done.13.refs_13_
  72.2 0.7 copy-done.18
  72.9 5.3 %frozen_part.1 = (f32[128,512]{1,0:T(8,128)}, bf16[128,512]{1,0:T(8,128)(2,1)}, bf16[128,512]{1,0:T(8,128)(2,1)}, bf16[128,512]{1,0:T(8,128)(2,1)}) custom-call(s32[4]{0:T(128)} %pad_add_fusion.where, bf16[4,128,640]{2,1,0:T(8,128)(2,1)} %copy-done.5, bf16[4,128,640]{2,1,0:T(8,128)(2,1)} %copy-done.12, bf16[2,128,640]{2,1,0:T(8,128)(2,1)} %collective-permute-done.2.refs_2_, ...), custom_call_target="tpu_custom_call" | custom-call | flops 4294967296 | bytes 8388608 | tf_op jit(solution)/shard_map/frozen_part/pallas_call | solution.py:435
  78.2 2.1 %collective-permute-start.14 = (bf16[128,512]{1,0:T(8,128)(2,1)}, bf16[128,512]{1,0:T(8,128)(2,1)S(1)}, u32[]{:S(2)}, u32[]{:S(2)}) collective-permute-start(bf16[128,512]{1,0:T(8,128)(2,1)} %get-tuple-element.81), channel_id=1, source_target_pairs={{0,1},{1,0},{2,3},{3,2},{4,5},{5,4},{6,7},{7,6},{8,9},{9,8},{10,11... | collective-permute-start | bytes 393224 | tf_op jit(solution)/shard_map/ppermute | solution.py:333
  80.3 0.5 collective-permute-start.15
  80.8 1.0 %collective-permute-start.16 = (bf16[128,512]{1,0:T(8,128)(2,1)}, bf16[128,512]{1,0:T(8,128)(2,1)S(1)}, u32[]{:S(2)}, u32[]{:S(2)}) collective-permute-start(bf16[128,512]{1,0:T(8,128)(2,1)} %get-tuple-element.83), channel_id=1, source_target_pairs={{0,17},{1,16},{2,19},{3,18},{4,21},{5,20},{6,23},{7,22},{16,1},{17... | collective-permute-start | bytes 393224 | tf_op jit(solution)/shard_map/ppermute | solution.py:451
  81.8 4.5 %collective-permute-done.14 = bf16[128,512]{1,0:T(8,128)(2,1)S(1)} collective-permute-done((bf16[128,512]{1,0:T(8,128)(2,1)}, bf16[128,512]{1,0:T(8,128)(2,1)S(1)}, u32[]{:S(2)}, u32[]{:S(2)}) %collective-permute-start.14) | collective-permute-done | bytes 131104 | tf_op jit(solution)/shard_map/ppermute | solution.py:333
  86.3 0.0 collective-permute-done.15
  86.3 2.9 %collective-permute-done.16 = bf16[128,512]{1,0:T(8,128)(2,1)S(1)} collective-permute-done((bf16[128,512]{1,0:T(8,128)(2,1)}, bf16[128,512]{1,0:T(8,128)(2,1)S(1)}, u32[]{:S(2)}, u32[]{:S(2)}) %collective-permute-start.16) | collective-permute-done | bytes 131104 | tf_op jit(solution)/shard_map/ppermute | solution.py:451
  89.1 1.7 %all-to-all-done.2.rest_0_ = bf16[8,384,128]{2,1,0:T(8,128)(2,1)S(1)} async-done(((bf16[8,384,128]{2,1,0:T(8,128)(2,1)}), bf16[8,384,128]{2,1,0:T(8,128)(2,1)S(1)}, u32[]{:S(2)}, u32[]{:S(2)}) %all-to-all-start.2) | async-done | bytes 786464 | tf_op jit(solution)/shard_map/all_to_all | solution.py:450
  90.8 0.0 collective-permute-start.18
  90.8 0.5 collective-permute-start.17
  91.3 1.0 %convert_add_fusion = (f32[128,512]{1,0:T(8,128)S(1)}, f32[128,512]{1,0:T(8,128)S(1)}) fusion(bf16[128,512]{1,0:T(8,128)(2,1)S(1)} %collective-permute-done.16, bf16[128,512]{1,0:T(8,128)(2,1)S(1)} %collective-permute-done.15, f32[128,512]{1,0:T(8,128)} %get-tuple-element.80, bf16[128,512]{1,0:T(8,128)(2,1)S(1)} %collective-permute-done.14), kind=kLoop, calls=%fused_computation.4 | loop fusion | flops 327680 | bytes 1179648 | tf_op jit(solution)/shard_map/add | solution.py:478
  92.4 0.8 fusion
  93.2 0.0 collective-permute-done.17.rows_core
  93.2 0.0 collective-permute-done.18.rest_1_
  93.2 3.4 %place_rows.1 = (f32[16,320,8,1,128]{4,3,2,1,0:T(1,128)}, f32[16,64,8,1,128]{4,3,2,1,0:T(1,128)}) custom-call(s32[1]{0:T(128)} %bitcast.9.first_row, s32[8]{0:T(128)S(1)} %copy-done.4, s32[8]{0:T(128)S(1)} %collective-permute-done.17.rows_core, bf16[8,384,128]{2,1,0:T(8,128)(2,1)S(1)} %all-to-all-done.2.rest_0_, ...), custom_call_target="tpu_custom_call", output_to_operand_aliasing={{0}: (5, {}), {1}: (6, {})} | custom-call | bytes 16777216 | tf_op jit(solution)/shard_map/place_rows/pallas_call | solution.py:455
  (33 shorter events, 0.2 us)
Async XLA Ops:
  0.6 2.0 %copy-start = (bf16[640,512]{1,0:T(8,128)(2,1)S(1)}, bf16[640,512]{1,0:T(8,128)(2,1)}, u32[]{:S(2)}) copy-start(bf16[640,512]{1,0:T(8,128)(2,1)} %param.9) | copy-start | bytes 1966084
  2.7 39.4 %copy-start.10 = (bf16[640,256]{1,0:T(8,128)(2,1)}, bf16[640,256]{1,0:T(8,128)(2,1)S(1)}, u32[]{:S(2)}) copy-start(bf16[640,256]{1,0:T(8,128)(2,1)S(1)} %constant_dynamic-slice_fusion.refs_6_) | copy-start | bytes 983044
  2.7 19.6 %collective-permute-start.1 = (bf16[640,256]{1,0:T(8,128)(2,1)S(1)}, bf16[640,256]{1,0:T(8,128)(2,1)S(1)}, u32[]{:S(2)}, u32[]{:S(2)}) collective-permute-start(bf16[640,256]{1,0:T(8,128)(2,1)S(1)} %constant_dynamic-slice_fusion.refs_6_), channel_id=1, source_target_pairs={{2,4},{3,5},{4,2},{5,3},{10,12},{11,13},{12,10},{13,11},{18,20},{1... | collective-permute-start | bytes 983048 | tf_op jit(solution)/shard_map/ppermute | solution.py:362
  3.4 18.9 %collective-permute-start = (bf16[640,256]{1,0:T(8,128)(2,1)S(1)}, bf16[640,256]{1,0:T(8,128)(2,1)}, u32[]{:S(2)}, u32[]{:S(2)}) collective-permute-start(bf16[640,256]{1,0:T(8,128)(2,1)S(1)} %constant_dynamic-slice_fusion.refs_6_), channel_id=1, source_target_pairs={{0,2},{1,3},{2,0},{3,1},{4,6},{5,7},{6,4},{7,5},{8,10},{9,11},{10,... | collective-permute-start | bytes 983048 | tf_op jit(solution)/shard_map/ppermute | solution.py:333
  9.3 1.3 %copy-start.2 = (bf16[128,5120]{1,0:T(8,128)(2,1)S(1)}, bf16[128,5120]{1,0:T(8,128)(2,1)}, u32[]{:S(2)}) copy-start(bf16[128,5120]{1,0:T(8,128)(2,1)} %x_ref.1) | copy-start | bytes 3932164
  10.7 19.3 %copy-start.5 = (bf16[4,128,640]{2,1,0:T(8,128)(2,1)}, bf16[4,128,640]{2,1,0:T(8,128)(2,1)S(1)}, u32[]{:S(2)}) copy-start(bf16[4,128,640]{2,1,0:T(8,128)(2,1)S(1)} %get-tuple-element.49.refs_0_) | copy-start | bytes 1966084
  10.7 21.8 %collective-permute-start.4 = (bf16[4,128,640]{2,1,0:T(8,128)(2,1)S(1)}, bf16[4,128,640]{2,1,0:T(8,128)(2,1)S(1)}, u32[]{:S(2)}, u32[]{:S(2)}) collective-permute-start(bf16[4,128,640]{2,1,0:T(8,128)(2,1)S(1)} %get-tuple-element.49.refs_0_), channel_id=1, source_target_pairs={{0,16},{16,0},{1,17},{17,1},{2,18},{18,2},{3,19},{19,3},{4,20},{20... | collective-permute-start | bytes 1966088 | tf_op jit(solution)/shard_map/ppermute | solution.py:339
  12.3 9.9 %all-to-all-start = ((s32[8,1,128]{2,1,0:T(1,128)}), s32[8,1,128]{2,1,0:T(1,128)S(1)}, u32[]{:S(2)}, u32[]{:S(2)}) async-start(s32[8,1,128]{2,1,0:T(1,128)} %own_row.1), calls=%async_computation | async-start | bytes 8192 | tf_op jit(solution)/shard_map/all_to_all | solution.py:345
  15.8 14.1 %collective-permute-start.2 = (bf16[2,128,640]{2,1,0:T(8,128)(2,1)S(1)}, bf16[2,128,640]{2,1,0:T(8,128)(2,1)}, u32[]{:S(2)}, u32[]{:S(2)}) collective-permute-start(bf16[2,128,640]{2,1,0:T(8,128)(2,1)S(1)} %get-tuple-element.51), channel_id=1, source_target_pairs={{0,1},{1,0},{2,3},{3,2},{4,5},{5,4},{6,7},{7,6},{8,9},{9,8},{10,11... | collective-permute-start | bytes 983048 | tf_op jit(solution)/shard_map/ppermute | solution.py:333
  22.2 2.6 %copy-start.11 = (s32[8,1,128]{2,1,0:T(1,128)}, s32[8,1,128]{2,1,0:T(1,128)S(1)}, u32[]{:S(2)}) copy-start(s32[8,1,128]{2,1,0:T(1,128)S(1)} %all-to-all-done.asked) | copy-start | bytes 12292
  22.2 9.1 %collective-permute-start.3 = (bf16[2,128,640]{2,1,0:T(8,128)(2,1)S(1)}, bf16[2,128,640]{2,1,0:T(8,128)(2,1)S(1)}, u32[]{:S(2)}, u32[]{:S(2)}) collective-permute-start(bf16[2,128,640]{2,1,0:T(8,128)(2,1)S(1)} %get-tuple-element.56), channel_id=1, source_target_pairs={{0,1},{1,0},{2,3},{3,2},{4,5},{5,4},{6,7},{7,6},{8,9},{9,8},{10,11... | collective-permute-start | bytes 983048 | tf_op jit(solution)/shard_map/ppermute | solution.py:333
  22.9 8.5 %collective-permute-start.5 = (bf16[640,256]{1,0:T(8,128)(2,1)}, bf16[640,256]{1,0:T(8,128)(2,1)S(1)}, u32[]{:S(2)}, u32[]{:S(2)}) collective-permute-start(bf16[640,256]{1,0:T(8,128)(2,1)} %collective-permute-done.refs_7_), channel_id=1, source_target_pairs={{2,4},{3,5},{4,2},{5,3},{10,12},{11,13},{12,10},{13,11},{18,20},{1... | collective-permute-start | bytes 983048 | tf_op jit(solution)/shard_map/ppermute | solution.py:365
  23.5 9.0 %collective-permute-start.6 = (bf16[640,256]{1,0:T(8,128)(2,1)S(1)}, bf16[640,256]{1,0:T(8,128)(2,1)S(1)}, u32[]{:S(2)}, u32[]{:S(2)}) collective-permute-start(bf16[640,256]{1,0:T(8,128)(2,1)S(1)} %collective-permute-done.1), channel_id=1, source_target_pairs={{2,0},{3,1},{4,6},{5,7},{10,8},{11,9},{12,14},{13,15},{18,16},{19,... | collective-permute-start | bytes 983048 | tf_op jit(solution)/shard_map/ppermute | solution.py:366
  31.4 1.1 %copy-start.13 = (bf16[2,128,640]{2,1,0:T(8,128)(2,1)}, bf16[2,128,640]{2,1,0:T(8,128)(2,1)S(1)}, u32[]{:S(2)}) copy-start(bf16[2,128,640]{2,1,0:T(8,128)(2,1)S(1)} %collective-permute-done.3.refs_3_) | copy-start | bytes 983044
  32.5 0.8 copy-start.12
  33.3 26.6 %all-to-all-start.1 = ((bf16[8,384,128]{2,1,0:T(8,128)(2,1)}), bf16[8,384,128]{2,1,0:T(8,128)(2,1)S(1)}, u32[]{:S(2)}, u32[]{:S(2)}) async-start(bf16[8,384,128]{2,1,0:T(8,128)(2,1)} %get-tuple-element.62), calls=%async_computation.1 | async-start | bytes 1572864 | tf_op jit(solution)/shard_map/all_to_all | solution.py:391
  38.5 21.4 %copy-start.6 = (bf16[128,1024]{1,0:T(8,128)(2,1)S(1)}, bf16[128,1024]{1,0:T(8,128)(2,1)}, u32[]{:S(2)}) copy-start(bf16[128,1024]{1,0:T(8,128)(2,1)} %g_ref.1) | copy-start | bytes 786436
  38.6 25.8 %copy-start.8 = (bf16[640,256]{1,0:T(8,128)(2,1)}, bf16[640,256]{1,0:T(8,128)(2,1)S(1)}, u32[]{:S(2)}) copy-start(bf16[640,256]{1,0:T(8,128)(2,1)S(1)} %broadcast_select_fusion.1.refs_8_) | copy-start | bytes 983044
  38.6 3.6 %collective-permute-start.12 = (bf16[640,256]{1,0:T(8,128)(2,1)S(1)}, bf16[640,256]{1,0:T(8,128)(2,1)S(1)}, u32[]{:S(2)}, u32[]{:S(2)}) collective-permute-start(bf16[640,256]{1,0:T(8,128)(2,1)S(1)} %broadcast_select_fusion.1.refs_8_), channel_id=1, source_target_pairs={{0,8},{8,0},{1,9},{9,1},{2,10},{10,2},{3,11},{11,3},{4,12},{12,4},... | collective-permute-start | bytes 983048 | tf_op jit(solution)/shard_map/ppermute | solution.py:336
  38.7 18.7 %collective-permute-start.8 = (bf16[2,128,640]{2,1,0:T(8,128)(2,1)}, bf16[2,128,640]{2,1,0:T(8,128)(2,1)S(1)}, u32[]{:S(2)}, u32[]{:S(2)}) collective-permute-start(bf16[2,128,640]{2,1,0:T(8,128)(2,1)} %collective-permute-done.2.refs_2_), channel_id=1, source_target_pairs={{0,16},{16,0},{1,17},{17,1},{2,18},{18,2},{3,19},{19,3},{4,20},{20... | collective-permute-start | bytes 983048 | tf_op jit(solution)/shard_map/ppermute | solution.py:339
  39.2 18.2 %collective-permute-start.9 = (bf16[2,128,640]{2,1,0:T(8,128)(2,1)}, bf16[2,128,640]{2,1,0:T(8,128)(2,1)S(1)}, u32[]{:S(2)}, u32[]{:S(2)}) collective-permute-start(bf16[2,128,640]{2,1,0:T(8,128)(2,1)} %copy-done.13), channel_id=1, source_target_pairs={{0,16},{16,0},{1,17},{17,1},{2,18},{18,2},{3,19},{19,3},{4,20},{20... | collective-permute-start | bytes 983048 | tf_op jit(solution)/shard_map/ppermute | solution.py:339
  40.7 18.5 %collective-permute-start.7 = (bf16[640,256]{1,0:T(8,128)(2,1)S(1)}, bf16[640,256]{1,0:T(8,128)(2,1)S(1)}, u32[]{:S(2)}, u32[]{:S(2)}) collective-permute-start(bf16[640,256]{1,0:T(8,128)(2,1)S(1)} %collective-permute-done.5), channel_id=1, source_target_pairs={{2,0},{3,1},{4,6},{5,7},{10,8},{11,9},{12,14},{13,15},{18,16},{19,... | collective-permute-start | bytes 983048 | tf_op jit(solution)/shard_map/ppermute | solution.py:395
  42.0 17.2 %collective-permute-start.10 = (bf16[640,256]{1,0:T(8,128)(2,1)S(1)}, bf16[640,256]{1,0:T(8,128)(2,1)S(1)}, u32[]{:S(2)}, u32[]{:S(2)}) collective-permute-start(bf16[640,256]{1,0:T(8,128)(2,1)S(1)} %constant_dynamic-slice_fusion.refs_6_), channel_id=1, source_target_pairs={{0,8},{8,0},{1,9},{9,1},{2,10},{10,2},{3,11},{11,3},{4,12},{12,4},... | collective-permute-start | bytes 983048 | tf_op jit(solution)/shard_map/ppermute | solution.py:336
  42.1 0.7 copy-start.14
  42.9 16.4 %collective-permute-start.11 = (bf16[640,256]{1,0:T(8,128)(2,1)}, bf16[640,256]{1,0:T(8,128)(2,1)}, u32[]{:S(2)}, u32[]{:S(2)}) collective-permute-start(bf16[640,256]{1,0:T(8,128)(2,1)} %collective-permute-done.refs_7_), channel_id=1, source_target_pairs={{0,8},{8,0},{1,9},{9,1},{2,10},{10,2},{3,11},{11,3},{4,12},{12,4},... | collective-permute-start | bytes 983048 | tf_op jit(solution)/shard_map/ppermute | solution.py:336
  43.4 0.7 copy-start.3
  57.4 1.8 %copy-start.15 = (bf16[2,128,640]{2,1,0:T(8,128)(2,1)}, bf16[2,128,640]{2,1,0:T(8,128)(2,1)S(1)}, u32[]{:S(2)}) copy-start(bf16[2,128,640]{2,1,0:T(8,128)(2,1)S(1)} %collective-permute-done.8.refs_4_) | copy-start | bytes 983044
  57.4 1.8 %copy-start.16 = (bf16[2,128,640]{2,1,0:T(8,128)(2,1)}, bf16[2,128,640]{2,1,0:T(8,128)(2,1)S(1)}, u32[]{:S(2)}) copy-start(bf16[2,128,640]{2,1,0:T(8,128)(2,1)S(1)} %collective-permute-done.9.refs_5_) | copy-start | bytes 983044
  59.2 0.7 copy-start.17
  59.9 1.4 %copy-start.7 = (bf16[8,256,320]{2,1,0:T(8,128)(2,1)S(1)}, bf16[8,256,320]{2,1,0:T(8,128)(2,1)}, u32[]{:S(2)}) copy-start(bf16[8,256,320]{2,1,0:T(8,128)(2,1)} %pair_columns.1.xs_ref) | copy-start | bytes 3932164
  64.3 26.5 %all-to-all-start.2 = ((bf16[8,384,128]{2,1,0:T(8,128)(2,1)}), bf16[8,384,128]{2,1,0:T(8,128)(2,1)S(1)}, u32[]{:S(2)}, u32[]{:S(2)}) async-start(bf16[8,384,128]{2,1,0:T(8,128)(2,1)} %get-tuple-element.74.refs_14_), calls=%async_computation.2 | async-start | bytes 1572864 | tf_op jit(solution)/shard_map/all_to_all | solution.py:450
  70.5 1.7 %copy-start.9 = (bf16[640,256]{1,0:T(8,128)(2,1)}, bf16[640,256]{1,0:T(8,128)(2,1)S(1)}, u32[]{:S(2)}) copy-start(bf16[640,256]{1,0:T(8,128)(2,1)S(1)} %broadcast_select_fusion.refs_9_) | copy-start | bytes 983044
  70.5 1.7 %collective-permute-start.13 = (bf16[640,256]{1,0:T(8,128)(2,1)S(1)}, bf16[640,256]{1,0:T(8,128)(2,1)S(1)}, u32[]{:S(2)}, u32[]{:S(2)}) collective-permute-start(bf16[640,256]{1,0:T(8,128)(2,1)S(1)} %broadcast_select_fusion.refs_9_), channel_id=1, source_target_pairs={{0,8},{8,0},{1,9},{9,1},{2,10},{10,2},{3,11},{11,3},{4,12},{12,4},... | collective-permute-start | bytes 983048 | tf_op jit(solution)/shard_map/ppermute | solution.py:336
  71.2 19.6 %copy-start.4 = (s32[8]{0:T(128)S(1)}, s32[8]{0:T(128)}, u32[]{:S(2)}) copy-start(s32[8]{0:T(128)} %get-tuple-element.70.after_ref.rows_here) | copy-start | bytes 100
  72.2 0.7 copy-start.18
  78.2 8.1 %collective-permute-start.14 = (bf16[128,512]{1,0:T(8,128)(2,1)}, bf16[128,512]{1,0:T(8,128)(2,1)S(1)}, u32[]{:S(2)}, u32[]{:S(2)}) collective-permute-start(bf16[128,512]{1,0:T(8,128)(2,1)} %get-tuple-element.81), channel_id=1, source_target_pairs={{0,1},{1,0},{2,3},{3,2},{4,5},{5,4},{6,7},{7,6},{8,9},{9,8},{10,11... | collective-permute-start | bytes 393224 | tf_op jit(solution)/shard_map/ppermute | solution.py:333
  80.3 6.0 %collective-permute-start.15 = (bf16[128,512]{1,0:T(8,128)(2,1)}, bf16[128,512]{1,0:T(8,128)(2,1)S(1)}, u32[]{:S(2)}, u32[]{:S(2)}) collective-permute-start(bf16[128,512]{1,0:T(8,128)(2,1)} %get-tuple-element.82), channel_id=1, source_target_pairs={{0,16},{16,0},{1,17},{17,1},{2,18},{18,2},{3,19},{19,3},{4,20},{20... | collective-permute-start | bytes 393224 | tf_op jit(solution)/shard_map/ppermute | solution.py:339
  80.8 8.4 %collective-permute-start.16 = (bf16[128,512]{1,0:T(8,128)(2,1)}, bf16[128,512]{1,0:T(8,128)(2,1)S(1)}, u32[]{:S(2)}, u32[]{:S(2)}) collective-permute-start(bf16[128,512]{1,0:T(8,128)(2,1)} %get-tuple-element.83), channel_id=1, source_target_pairs={{0,17},{1,16},{2,19},{3,18},{4,21},{5,20},{6,23},{7,22},{16,1},{17... | collective-permute-start | bytes 393224 | tf_op jit(solution)/shard_map/ppermute | solution.py:451
  90.8 2.3 %collective-permute-start.18 = (bf16[8,384,128]{2,1,0:T(8,128)(2,1)S(1)}, bf16[8,384,128]{2,1,0:T(8,128)(2,1)S(1)}, u32[]{:S(2)}, u32[]{:S(2)}) collective-permute-start(bf16[8,384,128]{2,1,0:T(8,128)(2,1)S(1)} %all-to-all-done.2.rest_0_), channel_id=1, source_target_pairs={{0,8},{8,0},{1,9},{9,1},{2,10},{10,2},{3,11},{11,3},{4,12},{12,4},... | collective-permute-start | bytes 2359304 | tf_op jit(solution)/shard_map/ppermute | solution.py:336
  90.8 2.3 %collective-permute-start.17 = (s32[8]{0:T(128)S(1)}, s32[8]{0:T(128)S(1)}, u32[]{:S(2)}, u32[]{:S(2)}) collective-permute-start(s32[8]{0:T(128)S(1)} %copy-done.4), channel_id=1, source_target_pairs={{0,8},{8,0},{1,9},{9,1},{2,10},{10,2},{3,11},{11,3},{4,12},{12,4},... | collective-permute-start | bytes 104 | tf_op jit(solution)/shard_map/ppermute | solution.py:336
  93.2 3.4 %copy-start.1 = (bf16[640,512]{1,0:T(8,128)(2,1)S(1)}, bf16[640,512]{1,0:T(8,128)(2,1)}, u32[]{:S(2)}) copy-start(bf16[640,512]{1,0:T(8,128)(2,1)} %param.9) | copy-start | bytes 1966084

commit v13 on v12

--- a/solution.py
+++ b/solution.py
@@ -356,11 +356,21 @@
     )(x[None], split_from)
     x_far = [exchange(x_theirs[0], 1)]
     y_mine = other_part(x_mine)
+    xs = pl.pallas_call(
+        interleave_kernel,
+        out_shape=jax.ShapeDtypeStruct((group, 2 * token_rows, slice_width // 2), jnp.bfloat16),
+        in_specs=[VMEM], out_specs=ANY, name="pair_columns", compiler_params=WIDE,
+        scratch_shapes=[
+            pltpu.VMEM((group, 2 * token_rows, slice_width // 2), jnp.bfloat16),
+            pltpu.SemaphoreType.DMA((group,)),
+        ],
+        cost_estimate=cost(),
+    )(split_from)
     middle = [(t, t ^ 6) for t in range(group) if t // 2 in (1, 2)]
     ends = [(t, t ^ 2) for t in range(group) if t // 2 in (1, 2)]
     near = exchange(half, 2)
     over = lax.ppermute(half, "tensor", middle)
-    near, over, asked, x_theirs = lax.optimization_barrier((near, over, asked, x_theirs))
+    near, over, asked, x_theirs, xs = lax.optimization_barrier((near, over, asked, x_theirs, xs))
     x_far.append(exchange(x_theirs[1], 1))
     over_near = lax.ppermute(near, "tensor", middle)
     passed = lax.ppermute(over, "tensor", ends)
@@ -404,17 +414,6 @@
         scratch_shapes=[pltpu.VMEM((up_chunks, 8, 1, LANES), jnp.float32), pltpu.SemaphoreType.DMA((2,))],
         compiler_params=LIMIT, cost_estimate=cost(read=28 << 20), name="clear_rows",
     )(rows)
-    pair_from, _ = lax.optimization_barrier((tokens, cleared))
-    xs = pl.pallas_call(
-        interleave_kernel,
-        out_shape=jax.ShapeDtypeStruct((group, 2 * token_rows, slice_width // 2), jnp.bfloat16),
-        in_specs=[VMEM], out_specs=ANY, name="pair_columns", compiler_params=WIDE,
-        scratch_shapes=[
-            pltpu.VMEM((group, 2 * token_rows, slice_width // 2), jnp.bfloat16),
-            pltpu.SemaphoreType.DMA((group,)),
-        ],
-        cost_estimate=cost(flops=2 << 30, read=4 << 20),
-    )(pair_from)
     panels, passed_near, y_far, quarter_core = lax.optimization_barrier((panels, passed_near, y_far, quarter_core))
 
     terms, lifted = pl.pallas_call(

time: 97.2 us -> 94.6 us (0.973)
  starting transfers between devices: 35.8 us -> 33.3 us
  other arithmetic: 2.55 us -> 4.49 us
  waiting for transfers between devices: 18.6 us -> 17 us
    all_to_all x1, waiting for transfers between devices: 4.37 us -> 0.49 us  [fast_body(): asked = lax.all_to_all(row, 'tensor', 0, 0)]
    ppermute x4, waiting for transfers between devices: 0.01 us -> 2.51 us  [other_part(): lax.ppermute(value, 'parts', [(a, parts - 1 - a) for a in range(parts)])]
    ppermute x1, waiting for transfers between devices: 1.14 us -> 2.51 us  [fast_body(): passed = lax.ppermute(over, 'tensor', ends)]
    all_to_all x1, starting transfers between devices: 6.09 us -> 4.82 us  [fast_body(): back = lax.all_to_all(terms, 'tensor', 0, 0)]
    all_to_all x1, starting transfers between devices: 5.17 us -> 3.93 us  [fast_body(): panels = lax.all_to_all(sent, 'tensor', 0, 0)]
    all_to_all x1, waiting for transfers between devices: 1.67 us -> 0.45 us  [fast_body(): back = lax.all_to_all(terms, 'tensor', 0, 0)]
    select_n x1, other arithmetic: 0.04 us -> 1.01 us  [fast_body(): last = jnp.where(inside, over_near, passed_near)]
    select_n x1, other arithmetic: 0.04 us -> 1.01 us  [fast_body(): quarter = [half, near, jnp.where(inside, over, passed)]]
  transfers between devices with their start and end apart: 22 -> 22, of which waited for: 8 -> 9; matrix products, arithmetic and copies ran while one was open for 3% -> 5% of each run, Pallas kernels for 25% -> 26%
where the time goes in v13:
time: 94.6 us; the launch traced here: 94 us
  starting transfers between devices  33.3 us (35%)
  Pallas kernels  31.6 us (33%)
  waiting for transfers between devices  17 us (18%)
  local copies, waits for them, and re-layouts  5.98 us (6%)
  other arithmetic  4.49 us (5%)
  between operations  1.66 us (2%)
    ppermute x4, starting transfers between devices, exchange(): return lax.ppermute(value, 'tensor', [(t, t ^ s) for t in range(group)])  10.6 us
    pallas_call x1, Pallas kernels, fast_body(): pl.pallas_call(zero_kernel, out_shape=(down_shape, up_shape, token), in_s...  9.48 us
    unnamed x38, local copies, waits for them, and re-layouts  5.95 us
    ppermute x4, waiting for transfers between devices, exchange(): return lax.ppermute(value, 'tensor', [(t, t ^ s) for t in range(group)])  5.8 us
    pallas_call x1, Pallas kernels, fast_body(): pl.pallas_call(gather_kernel, out_shape=(pieces, jax.ShapeDtypeStruct((gr...  5.55 us
    pallas_call x1, Pallas kernels, fast_body(): pl.pallas_call(base_kernel, out_shape=sums, in_specs=[SMEM] + [ANY] * (7...  5.26 us
    all_to_all x1, starting transfers between devices, fast_body(): back = lax.all_to_all(terms, 'tensor', 0, 0)  4.82 us
    ppermute x4, starting transfers between devices, other_part(): lax.ppermute(value, 'parts', [(a, parts - 1 - a) for a in range(parts)])  4.18 us
  transfers between devices with their start and end apart: 22, of which 9 were waited for; matrix products, arithmetic and copies ran while one was open for 5% of the time, Pallas kernels for 26%

profile of v13, /device:TPU:0, one launch (start us, length us, event | category | flops | bytes accessed | tf_op | source)
XLA Modules:
  0.0 94.0 jit_solution(13277976215155454275)
XLA Ops:
  0.6 0.0 copy-start
  1.4 1.3 %own_row.1 = s32[8,1,128]{2,1,0:T(1,128)} custom-call(s32[1]{0:T(128)S(6)} %copy.14.block_ref, s32[256]{0:T(256)} %slot_ref.1), custom_call_target="tpu_custom_call" | custom-call | tf_op jit(solution)/shard_map/own_row/pallas_call | solution.py:341
  2.7 0.7 collective-permute-start.1
  3.4 5.9 %collective-permute-start = (bf16[640,256]{1,0:T(8,128)(2,1)S(1)}, bf16[640,256]{1,0:T(8,128)(2,1)}, u32[]{:S(2)}, u32[]{:S(2)}) collective-permute-start(bf16[640,256]{1,0:T(8,128)(2,1)S(1)} %constant_dynamic-slice_fusion.refs_6_), channel_id=1, source_target_pairs={{0,2},{1,3},{2,0},{3,1},{4,6},{5,7},{6,4},{7,5},{8,10},{9,11},{10,... | collective-permute-start | bytes 983048 | tf_op jit(solution)/shard_map/ppermute | solution.py:333
  9.3 1.3 %copy-done.2 = bf16[128,5120]{1,0:T(8,128)(2,1)S(1)} copy-done((bf16[128,5120]{1,0:T(8,128)(2,1)S(1)}, bf16[128,5120]{1,0:T(8,128)(2,1)}, u32[]{:S(2)}) %copy-start.2) | copy-done | bytes 1310744
  10.6 0.1 split_tokens.1
  10.7 1.6 %collective-permute-start.4 = (bf16[4,128,640]{2,1,0:T(8,128)(2,1)S(1)}, bf16[4,128,640]{2,1,0:T(8,128)(2,1)}, u32[]{:S(2)}, u32[]{:S(2)}) collective-permute-start(bf16[4,128,640]{2,1,0:T(8,128)(2,1)S(1)} %get-tuple-element.49.refs_0_), channel_id=1, source_target_pairs={{0,16},{16,0},{1,17},{17,1},{2,18},{18,2},{3,19},{19,3},{4,20},{20... | collective-permute-start | bytes 1966088 | tf_op jit(solution)/shard_map/ppermute | solution.py:339
  12.3 3.6 %all-to-all-start = ((s32[8,1,128]{2,1,0:T(1,128)}), s32[8,1,128]{2,1,0:T(1,128)S(1)}, u32[]{:S(2)}, u32[]{:S(2)}) async-start(s32[8,1,128]{2,1,0:T(1,128)} %own_row.1), calls=%async_computation | async-start | bytes 8192 | tf_op jit(solution)/shard_map/all_to_all | solution.py:345
  15.8 2.0 %collective-permute-start.2 = (bf16[2,128,640]{2,1,0:T(8,128)(2,1)S(1)}, bf16[2,128,640]{2,1,0:T(8,128)(2,1)}, u32[]{:S(2)}, u32[]{:S(2)}) collective-permute-start(bf16[2,128,640]{2,1,0:T(8,128)(2,1)S(1)} %get-tuple-element.51), channel_id=1, source_target_pairs={{0,1},{1,0},{2,3},{3,2},{4,5},{5,4},{6,7},{7,6},{8,9},{9,8},{10,11... | collective-permute-start | bytes 983048 | tf_op jit(solution)/shard_map/ppermute | solution.py:333
  17.9 3.9 %pair_columns.1.xs_ref = bf16[8,256,320]{2,1,0:T(8,128)(2,1)} custom-call(bf16[128,5120]{1,0:T(8,128)(2,1)} %x_ref.1), custom_call_target="tpu_custom_call" | custom-call | tf_op jit(solution)/shard_map/pair_columns/pallas_call | solution.py:359
  21.7 0.5 all-to-all-done.asked
  22.2 0.0 collective-permute-done.1
  22.2 0.0 collective-permute-done.refs_7_
  22.2 0.6 collective-permute-start.3
  22.9 0.7 collective-permute-start.5
  23.5 1.3 %collective-permute-start.6 = (bf16[640,256]{1,0:T(8,128)(2,1)S(1)}, bf16[640,256]{1,0:T(8,128)(2,1)S(1)}, u32[]{:S(2)}, u32[]{:S(2)}) collective-permute-start(bf16[640,256]{1,0:T(8,128)(2,1)S(1)} %collective-permute-done.1), channel_id=1, source_target_pairs={{2,0},{3,1},{4,6},{5,7},{10,8},{11,9},{12,14},{13,15},{18,16},{19,... | collective-permute-start | bytes 983048 | tf_op jit(solution)/shard_map/ppermute | solution.py:376
  24.9 5.6 %pick_panels.1 = (bf16[8,384,128]{2,1,0:T(8,128)(2,1)}, s32[8]{0:T(128)}) custom-call(s32[8,1,128]{2,1,0:T(1,128)} %copy-done.13, bf16[32,320,8,128]{3,2,1,0:T(8,128)(2,1)} %bitcast.23, bf16[32,64,8,128]{3,2,1,0:T(8,128)(2,1)} %bitcast.24), custom_call_target="tpu_custom_call" | custom-call | bytes 41943040 | tf_op jit(solution)/shard_map/pick_panels/pallas_call | solution.py:382
  30.4 0.0 collective-permute-done.2.refs_2_
  30.4 0.0 collective-permute-done.4.refs_1_
  30.5 1.0 %collective-permute-done.3.refs_3_ = bf16[2,128,640]{2,1,0:T(8,128)(2,1)} collective-permute-done((bf16[2,128,640]{2,1,0:T(8,128)(2,1)S(1)}, bf16[2,128,640]{2,1,0:T(8,128)(2,1)}, u32[]{:S(2)}, u32[]{:S(2)}) %collective-permute-start.3) | collective-permute-done | bytes 327712 | tf_op jit(solution)/shard_map/ppermute | solution.py:333
  31.5 0.0 collective-permute-done.5
  31.5 2.5 %collective-permute-done.6 = bf16[640,256]{1,0:T(8,128)(2,1)S(1)} collective-permute-done((bf16[640,256]{1,0:T(8,128)(2,1)S(1)}, bf16[640,256]{1,0:T(8,128)(2,1)S(1)}, u32[]{:S(2)}, u32[]{:S(2)}) %collective-permute-start.6) | collective-permute-done | bytes 327712 | tf_op jit(solution)/shard_map/ppermute | solution.py:376
  34.0 0.7 copy-done.9
  34.7 3.9 %all-to-all-start.1 = ((bf16[8,384,128]{2,1,0:T(8,128)(2,1)}), bf16[8,384,128]{2,1,0:T(8,128)(2,1)S(1)}, u32[]{:S(2)}, u32[]{:S(2)}) async-start(bf16[8,384,128]{2,1,0:T(8,128)(2,1)} %get-tuple-element.62), calls=%async_computation.1 | async-start | bytes 1572864 | tf_op jit(solution)/shard_map/all_to_all | solution.py:401
  38.6 1.0 %broadcast_select_fusion.1.refs_8_ = bf16[640,256]{1,0:T(8,128)(2,1)S(1)} fusion(bf16[640,256]{1,0:T(8,128)(2,1)S(1)} %collective-permute-done.1, bf16[640,256]{1,0:T(8,128)(2,1)} %copy-done.9, pred[]{:T(512)S(6)} %or.3), kind=kLoop, calls=%fused_computation.3 | loop fusion | flops 163840 | bytes 983041 | tf_op jit(solution)/shard_map/jit(_where)/select_n | solution.py:406
  39.7 0.1 collective-permute-start.12
  39.7 0.6 collective-permute-start.8
  40.3 1.5 %collective-permute-start.9 = (bf16[2,128,640]{2,1,0:T(8,128)(2,1)}, bf16[2,128,640]{2,1,0:T(8,128)(2,1)S(1)}, u32[]{:S(2)}, u32[]{:S(2)}) collective-permute-start(bf16[2,128,640]{2,1,0:T(8,128)(2,1)} %collective-permute-done.3.refs_3_), channel_id=1, source_target_pairs={{0,16},{16,0},{1,17},{17,1},{2,18},{18,2},{3,19},{19,3},{4,20},{20... | collective-permute-start | bytes 983048 | tf_op jit(solution)/shard_map/ppermute | solution.py:339
  41.8 1.3 %collective-permute-start.7 = (bf16[640,256]{1,0:T(8,128)(2,1)S(1)}, bf16[640,256]{1,0:T(8,128)(2,1)S(1)}, u32[]{:S(2)}, u32[]{:S(2)}) collective-permute-start(bf16[640,256]{1,0:T(8,128)(2,1)S(1)} %collective-permute-done.5), channel_id=1, source_target_pairs={{2,0},{3,1},{4,6},{5,7},{10,8},{11,9},{12,14},{13,15},{18,16},{19,... | collective-permute-start | bytes 983048 | tf_op jit(solution)/shard_map/ppermute | solution.py:405
  43.1 0.1 collective-permute-start.10
  43.2 0.0 collective-permute-done.12.refs_12_
  43.2 0.7 copy-done.14
  43.9 0.5 collective-permute-start.11
  44.4 0.7 copy-done.4
  45.1 9.5 %clear_rows.1 = (f32[16,320,8,1,128]{4,3,2,1,0:T(1,128)}, f32[16,64,8,1,128]{4,3,2,1,0:T(1,128)}, s32[1]{0:T(128)}) custom-call(s32[8]{0:T(128)S(1)} %copy-done.4), custom_call_target="tpu_custom_call" | custom-call | bytes 29360128 | tf_op jit(solution)/shard_map/clear_rows/pallas_call | solution.py:411
  54.6 0.0 collective-permute-done.8.refs_4_
  54.6 2.5 %collective-permute-done.9.refs_5_ = bf16[2,128,640]{2,1,0:T(8,128)(2,1)S(1)} collective-permute-done((bf16[2,128,640]{2,1,0:T(8,128)(2,1)}, bf16[2,128,640]{2,1,0:T(8,128)(2,1)S(1)}, u32[]{:S(2)}, u32[]{:S(2)}) %collective-permute-start.9) | collective-permute-done | bytes 327712 | tf_op jit(solution)/shard_map/ppermute | solution.py:339
  57.1 1.8 %collective-permute-done.7 = bf16[640,256]{1,0:T(8,128)(2,1)S(1)} collective-permute-done((bf16[640,256]{1,0:T(8,128)(2,1)S(1)}, bf16[640,256]{1,0:T(8,128)(2,1)S(1)}, u32[]{:S(2)}, u32[]{:S(2)}) %collective-permute-start.7) | collective-permute-done | bytes 327712 | tf_op jit(solution)/shard_map/ppermute | solution.py:405
  58.9 0.0 collective-permute-done.10.refs_10_
  58.9 0.7 copy-done.17
  59.7 0.0 collective-permute-done.11.refs_11_
  59.7 0.0 all-to-all-done.1.pieces
  59.7 0.1 copy-done.10
  59.7 0.9 %copy-done.7 = bf16[128,1024]{1,0:T(8,128)(2,1)S(1)} copy-done((bf16[128,1024]{1,0:T(8,128)(2,1)S(1)}, bf16[128,1024]{1,0:T(8,128)(2,1)}, u32[]{:S(2)}) %copy-start.7) | copy-done | bytes 262168
  60.7 3.0 %adapter.1 = (bf16[8,384,128]{2,1,0:T(8,128)(2,1)}, f32[128,1024]{1,0:T(8,128)S(1)}) custom-call(bf16[8,256,320]{2,1,0:T(8,128)(2,1)S(1)} %copy-done.3, bf16[128,1024]{1,0:T(8,128)(2,1)S(1)} %copy-done.7, bf16[8,384,128]{2,1,0:T(8,128)(2,1)S(1)} %all-to-all-done.1.pieces, s32[1]{0:T(128)} %get-tuple-element.73._), custom_call_target="tpu_custom_call" | custom-call | flops 3221225472 | bytes 8388608 | tf_op jit(solution)/shard_map/adapter/pallas_call | solution.py:419
  63.7 4.8 %all-to-all-start.2 = ((bf16[8,384,128]{2,1,0:T(8,128)(2,1)}), bf16[8,384,128]{2,1,0:T(8,128)(2,1)S(1)}, u32[]{:S(2)}, u32[]{:S(2)}) async-start(bf16[8,384,128]{2,1,0:T(8,128)(2,1)} %get-tuple-element.74.refs_14_), calls=%async_computation.2 | async-start | bytes 1572864 | tf_op jit(solution)/shard_map/all_to_all | solution.py:449
  68.5 1.0 %broadcast_select_fusion.refs_9_ = bf16[640,256]{1,0:T(8,128)(2,1)S(1)} fusion(bf16[640,256]{1,0:T(8,128)(2,1)S(1)} %collective-permute-done.5, bf16[640,256]{1,0:T(8,128)(2,1)} %copy-done.10, pred[]{:T(512)S(6)} %or.3), kind=kLoop, calls=%fused_computation.2 | loop fusion | flops 163840 | bytes 983041 | tf_op jit(solution)/shard_map/jit(_where)/select_n | solution.py:430
  69.5 0.1 collective-permute-start.13
  69.6 0.7 pad_add_fusion.where
  70.3 0.9 %collective-permute-done.13.refs_13_ = bf16[640,256]{1,0:T(8,128)(2,1)S(1)} collective-permute-done((bf16[640,256]{1,0:T(8,128)(2,1)S(1)}, bf16[640,256]{1,0:T(8,128)(2,1)S(1)}, u32[]{:S(2)}, u32[]{:S(2)}) %collective-permute-start.13) | collective-permute-done | bytes 327712 | tf_op jit(solution)/shard_map/ppermute | solution.py:336
  71.2 0.7 copy-done.18
  72.0 5.3 %frozen_part.1 = (f32[128,512]{1,0:T(8,128)}, bf16[128,512]{1,0:T(8,128)(2,1)}, bf16[128,512]{1,0:T(8,128)(2,1)}, bf16[128,512]{1,0:T(8,128)(2,1)}) custom-call(s32[4]{0:T(128)} %pad_add_fusion.where, bf16[4,128,640]{2,1,0:T(8,128)(2,1)} %copy-done.6, bf16[4,128,640]{2,1,0:T(8,128)(2,1)} %collective-permute-done.4.refs_1_, ...), custom_call_target="tpu_custom_call" | custom-call | flops 4294967296 | bytes 8388608 | tf_op jit(solution)/shard_map/frozen_part/pallas_call | solution.py:434
  77.2 2.1 %collective-permute-start.14 = (bf16[128,512]{1,0:T(8,128)(2,1)}, bf16[128,512]{1,0:T(8,128)(2,1)S(1)}, u32[]{:S(2)}, u32[]{:S(2)}) collective-permute-start(bf16[128,512]{1,0:T(8,128)(2,1)} %get-tuple-element.81), channel_id=1, source_target_pairs={{0,1},{1,0},{2,3},{3,2},{4,5},{5,4},{6,7},{7,6},{8,9},{9,8},{10,11... | collective-permute-start | bytes 393224 | tf_op jit(solution)/shard_map/ppermute | solution.py:333
  79.3 0.5 collective-permute-start.15
  79.8 1.0 %collective-permute-start.16 = (bf16[128,512]{1,0:T(8,128)(2,1)}, bf16[128,512]{1,0:T(8,128)(2,1)S(1)}, u32[]{:S(2)}, u32[]{:S(2)}) collective-permute-start(bf16[128,512]{1,0:T(8,128)(2,1)} %get-tuple-element.83), channel_id=1, source_target_pairs={{0,17},{1,16},{2,19},{3,18},{4,21},{5,20},{6,23},{7,22},{16,1},{17... | collective-permute-start | bytes 393224 | tf_op jit(solution)/shard_map/ppermute | solution.py:450
  80.8 4.8 %collective-permute-done.14 = bf16[128,512]{1,0:T(8,128)(2,1)S(1)} collective-permute-done((bf16[128,512]{1,0:T(8,128)(2,1)}, bf16[128,512]{1,0:T(8,128)(2,1)S(1)}, u32[]{:S(2)}, u32[]{:S(2)}) %collective-permute-start.14) | collective-permute-done | bytes 131104 | tf_op jit(solution)/shard_map/ppermute | solution.py:333
  85.6 0.0 collective-permute-done.15
  85.6 2.5 %collective-permute-done.16 = bf16[128,512]{1,0:T(8,128)(2,1)S(1)} collective-permute-done((bf16[128,512]{1,0:T(8,128)(2,1)}, bf16[128,512]{1,0:T(8,128)(2,1)S(1)}, u32[]{:S(2)}, u32[]{:S(2)}) %collective-permute-start.16) | collective-permute-done | bytes 131104 | tf_op jit(solution)/shard_map/ppermute | solution.py:450
  88.1 0.5 all-to-all-done.2.rest_0_
  88.6 0.5 collective-permute-start.17
  89.1 1.0 %convert_add_fusion = (f32[128,512]{1,0:T(8,128)S(1)}, f32[128,512]{1,0:T(8,128)S(1)}) fusion(bf16[128,512]{1,0:T(8,128)(2,1)S(1)} %collective-permute-done.16, bf16[128,512]{1,0:T(8,128)(2,1)S(1)} %collective-permute-done.15, f32[128,512]{1,0:T(8,128)} %get-tuple-element.80, bf16[128,512]{1,0:T(8,128)(2,1)S(1)} %collective-permute-done.14), kind=kLoop, calls=%fused_computation.4 | loop fusion | flops 327680 | bytes 1179648 | tf_op jit(solution)/shard_map/add | solution.py:477
  90.1 0.8 fusion
  90.9 0.0 collective-permute-done.17.rows_core
  90.9 3.1 %place_rows.1 = (f32[16,320,8,1,128]{4,3,2,1,0:T(1,128)}, f32[16,64,8,1,128]{4,3,2,1,0:T(1,128)}) custom-call(s32[1]{0:T(128)} %bitcast.9.first_row, s32[8]{0:T(128)S(1)} %copy-done.5, s32[8]{0:T(128)S(1)} %collective-permute-done.17.rows_core, bf16[8,384,128]{2,1,0:T(8,128)(2,1)S(1)} %all-to-all-done.2.rest_0_, ...), custom_call_target="tpu_custom_call", output_to_operand_aliasing={{0}: (5, {}), {1}: (6, {})} | custom-call | bytes 16777216 | tf_op jit(solution)/shard_map/place_rows/pallas_call | solution.py:454
  (33 shorter events, 0.1 us)
Async XLA Ops:
  0.6 2.0 %copy-start = (bf16[640,512]{1,0:T(8,128)(2,1)S(1)}, bf16[640,512]{1,0:T(8,128)(2,1)}, u32[]{:S(2)}) copy-start(bf16[640,512]{1,0:T(8,128)(2,1)} %param.9) | copy-start | bytes 1966084
  2.7 22.2 %copy-start.12 = (bf16[640,256]{1,0:T(8,128)(2,1)}, bf16[640,256]{1,0:T(8,128)(2,1)S(1)}, u32[]{:S(2)}) copy-start(bf16[640,256]{1,0:T(8,128)(2,1)S(1)} %constant_dynamic-slice_fusion.refs_6_) | copy-start | bytes 983044
  2.7 19.6 %collective-permute-start.1 = (bf16[640,256]{1,0:T(8,128)(2,1)S(1)}, bf16[640,256]{1,0:T(8,128)(2,1)S(1)}, u32[]{:S(2)}, u32[]{:S(2)}) collective-permute-start(bf16[640,256]{1,0:T(8,128)(2,1)S(1)} %constant_dynamic-slice_fusion.refs_6_), channel_id=1, source_target_pairs={{2,4},{3,5},{4,2},{5,3},{10,12},{11,13},{12,10},{13,11},{18,20},{1... | collective-permute-start | bytes 983048 | tf_op jit(solution)/shard_map/ppermute | solution.py:372
  3.4 18.9 %collective-permute-start = (bf16[640,256]{1,0:T(8,128)(2,1)S(1)}, bf16[640,256]{1,0:T(8,128)(2,1)}, u32[]{:S(2)}, u32[]{:S(2)}) collective-permute-start(bf16[640,256]{1,0:T(8,128)(2,1)S(1)} %constant_dynamic-slice_fusion.refs_6_), channel_id=1, source_target_pairs={{0,2},{1,3},{2,0},{3,1},{4,6},{5,7},{6,4},{7,5},{8,10},{9,11},{10,... | collective-permute-start | bytes 983048 | tf_op jit(solution)/shard_map/ppermute | solution.py:333
  9.3 1.3 %copy-start.2 = (bf16[128,5120]{1,0:T(8,128)(2,1)S(1)}, bf16[128,5120]{1,0:T(8,128)(2,1)}, u32[]{:S(2)}) copy-start(bf16[128,5120]{1,0:T(8,128)(2,1)} %x_ref.1) | copy-start | bytes 3932164
  10.7 19.7 %copy-start.6 = (bf16[4,128,640]{2,1,0:T(8,128)(2,1)}, bf16[4,128,640]{2,1,0:T(8,128)(2,1)S(1)}, u32[]{:S(2)}) copy-start(bf16[4,128,640]{2,1,0:T(8,128)(2,1)S(1)} %get-tuple-element.49.refs_0_) | copy-start | bytes 1966084
  10.7 19.7 %collective-permute-start.4 = (bf16[4,128,640]{2,1,0:T(8,128)(2,1)S(1)}, bf16[4,128,640]{2,1,0:T(8,128)(2,1)}, u32[]{:S(2)}, u32[]{:S(2)}) collective-permute-start(bf16[4,128,640]{2,1,0:T(8,128)(2,1)S(1)} %get-tuple-element.49.refs_0_), channel_id=1, source_target_pairs={{0,16},{16,0},{1,17},{17,1},{2,18},{18,2},{3,19},{19,3},{4,20},{20... | collective-permute-start | bytes 1966088 | tf_op jit(solution)/shard_map/ppermute | solution.py:339
  12.3 9.9 %all-to-all-start = ((s32[8,1,128]{2,1,0:T(1,128)}), s32[8,1,128]{2,1,0:T(1,128)S(1)}, u32[]{:S(2)}, u32[]{:S(2)}) async-start(s32[8,1,128]{2,1,0:T(1,128)} %own_row.1), calls=%async_computation | async-start | bytes 8192 | tf_op jit(solution)/shard_map/all_to_all | solution.py:345
  15.8 14.6 %collective-permute-start.2 = (bf16[2,128,640]{2,1,0:T(8,128)(2,1)S(1)}, bf16[2,128,640]{2,1,0:T(8,128)(2,1)}, u32[]{:S(2)}, u32[]{:S(2)}) collective-permute-start(bf16[2,128,640]{2,1,0:T(8,128)(2,1)S(1)} %get-tuple-element.51), channel_id=1, source_target_pairs={{0,1},{1,0},{2,3},{3,2},{4,5},{5,4},{6,7},{7,6},{8,9},{9,8},{10,11... | collective-permute-start | bytes 983048 | tf_op jit(solution)/shard_map/ppermute | solution.py:333
  22.2 2.6 %copy-start.13 = (s32[8,1,128]{2,1,0:T(1,128)}, s32[8,1,128]{2,1,0:T(1,128)S(1)}, u32[]{:S(2)}) copy-start(s32[8,1,128]{2,1,0:T(1,128)S(1)} %all-to-all-done.asked) | copy-start | bytes 12292
  22.2 9.2 %collective-permute-start.3 = (bf16[2,128,640]{2,1,0:T(8,128)(2,1)S(1)}, bf16[2,128,640]{2,1,0:T(8,128)(2,1)}, u32[]{:S(2)}, u32[]{:S(2)}) collective-permute-start(bf16[2,128,640]{2,1,0:T(8,128)(2,1)S(1)} %get-tuple-element.56), channel_id=1, source_target_pairs={{0,1},{1,0},{2,3},{3,2},{4,5},{5,4},{6,7},{7,6},{8,9},{9,8},{10,11... | collective-permute-start | bytes 983048 | tf_op jit(solution)/shard_map/ppermute | solution.py:333
  22.9 8.6 %collective-permute-start.5 = (bf16[640,256]{1,0:T(8,128)(2,1)}, bf16[640,256]{1,0:T(8,128)(2,1)S(1)}, u32[]{:S(2)}, u32[]{:S(2)}) collective-permute-start(bf16[640,256]{1,0:T(8,128)(2,1)} %collective-permute-done.refs_7_), channel_id=1, source_target_pairs={{2,4},{3,5},{4,2},{5,3},{10,12},{11,13},{12,10},{13,11},{18,20},{1... | collective-permute-start | bytes 983048 | tf_op jit(solution)/shard_map/ppermute | solution.py:375
  23.5 10.4 %collective-permute-start.6 = (bf16[640,256]{1,0:T(8,128)(2,1)S(1)}, bf16[640,256]{1,0:T(8,128)(2,1)S(1)}, u32[]{:S(2)}, u32[]{:S(2)}) collective-permute-start(bf16[640,256]{1,0:T(8,128)(2,1)S(1)} %collective-permute-done.1), channel_id=1, source_target_pairs={{2,0},{3,1},{4,6},{5,7},{10,8},{11,9},{12,14},{13,15},{18,16},{19,... | collective-permute-start | bytes 983048 | tf_op jit(solution)/shard_map/ppermute | solution.py:376
  24.9 34.9 %copy-start.3 = (bf16[8,256,320]{2,1,0:T(8,128)(2,1)S(1)}, bf16[8,256,320]{2,1,0:T(8,128)(2,1)}, u32[]{:S(2)}) copy-start(bf16[8,256,320]{2,1,0:T(8,128)(2,1)} %pair_columns.1.xs_ref) | copy-start | bytes 3932164
  34.0 0.7 copy-start.9
  34.7 25.0 %all-to-all-start.1 = ((bf16[8,384,128]{2,1,0:T(8,128)(2,1)}), bf16[8,384,128]{2,1,0:T(8,128)(2,1)S(1)}, u32[]{:S(2)}, u32[]{:S(2)}) async-start(bf16[8,384,128]{2,1,0:T(8,128)(2,1)} %get-tuple-element.62), calls=%async_computation.1 | async-start | bytes 1572864 | tf_op jit(solution)/shard_map/all_to_all | solution.py:401
  39.7 20.0 %copy-start.8 = (bf16[640,256]{1,0:T(8,128)(2,1)}, bf16[640,256]{1,0:T(8,128)(2,1)S(1)}, u32[]{:S(2)}) copy-start(bf16[640,256]{1,0:T(8,128)(2,1)S(1)} %broadcast_select_fusion.1.refs_8_) | copy-start | bytes 983044
  39.7 3.5 %collective-permute-start.12 = (bf16[640,256]{1,0:T(8,128)(2,1)S(1)}, bf16[640,256]{1,0:T(8,128)(2,1)S(1)}, u32[]{:S(2)}, u32[]{:S(2)}) collective-permute-start(bf16[640,256]{1,0:T(8,128)(2,1)S(1)} %broadcast_select_fusion.1.refs_8_), channel_id=1, source_target_pairs={{0,8},{8,0},{1,9},{9,1},{2,10},{10,2},{3,11},{11,3},{4,12},{12,4},... | collective-permute-start | bytes 983048 | tf_op jit(solution)/shard_map/ppermute | solution.py:336
  39.7 14.8 %collective-permute-start.8 = (bf16[2,128,640]{2,1,0:T(8,128)(2,1)}, bf16[2,128,640]{2,1,0:T(8,128)(2,1)S(1)}, u32[]{:S(2)}, u32[]{:S(2)}) collective-permute-start(bf16[2,128,640]{2,1,0:T(8,128)(2,1)} %collective-permute-done.2.refs_2_), channel_id=1, source_target_pairs={{0,16},{16,0},{1,17},{17,1},{2,18},{18,2},{3,19},{19,3},{4,20},{20... | collective-permute-start | bytes 983048 | tf_op jit(solution)/shard_map/ppermute | solution.py:339
  40.3 16.8 %collective-permute-start.9 = (bf16[2,128,640]{2,1,0:T(8,128)(2,1)}, bf16[2,128,640]{2,1,0:T(8,128)(2,1)S(1)}, u32[]{:S(2)}, u32[]{:S(2)}) collective-permute-start(bf16[2,128,640]{2,1,0:T(8,128)(2,1)} %collective-permute-done.3.refs_3_), channel_id=1, source_target_pairs={{0,16},{16,0},{1,17},{17,1},{2,18},{18,2},{3,19},{19,3},{4,20},{20... | collective-permute-start | bytes 983048 | tf_op jit(solution)/shard_map/ppermute | solution.py:339
  41.8 17.1 %collective-permute-start.7 = (bf16[640,256]{1,0:T(8,128)(2,1)S(1)}, bf16[640,256]{1,0:T(8,128)(2,1)S(1)}, u32[]{:S(2)}, u32[]{:S(2)}) collective-permute-start(bf16[640,256]{1,0:T(8,128)(2,1)S(1)} %collective-permute-done.5), channel_id=1, source_target_pairs={{2,0},{3,1},{4,6},{5,7},{10,8},{11,9},{12,14},{13,15},{18,16},{19,... | collective-permute-start | bytes 983048 | tf_op jit(solution)/shard_map/ppermute | solution.py:405
  43.1 15.8 %collective-permute-start.10 = (bf16[640,256]{1,0:T(8,128)(2,1)}, bf16[640,256]{1,0:T(8,128)(2,1)S(1)}, u32[]{:S(2)}, u32[]{:S(2)}) collective-permute-start(bf16[640,256]{1,0:T(8,128)(2,1)} %copy-done.12), channel_id=1, source_target_pairs={{0,8},{8,0},{1,9},{9,1},{2,10},{10,2},{3,11},{11,3},{4,12},{12,4},... | collective-permute-start | bytes 983048 | tf_op jit(solution)/shard_map/ppermute | solution.py:336
  43.2 0.7 copy-start.14
  43.9 15.7 %collective-permute-start.11 = (bf16[640,256]{1,0:T(8,128)(2,1)}, bf16[640,256]{1,0:T(8,128)(2,1)}, u32[]{:S(2)}, u32[]{:S(2)}) collective-permute-start(bf16[640,256]{1,0:T(8,128)(2,1)} %collective-permute-done.refs_7_), channel_id=1, source_target_pairs={{0,8},{8,0},{1,9},{9,1},{2,10},{10,2},{3,11},{11,3},{4,12},{12,4},... | collective-permute-start | bytes 983048 | tf_op jit(solution)/shard_map/ppermute | solution.py:336
  44.4 0.7 copy-start.4
  54.6 4.3 %copy-start.15 = (bf16[2,128,640]{2,1,0:T(8,128)(2,1)}, bf16[2,128,640]{2,1,0:T(8,128)(2,1)S(1)}, u32[]{:S(2)}) copy-start(bf16[2,128,640]{2,1,0:T(8,128)(2,1)S(1)} %collective-permute-done.8.refs_4_) | copy-start | bytes 983044
  57.1 1.8 %copy-start.16 = (bf16[2,128,640]{2,1,0:T(8,128)(2,1)}, bf16[2,128,640]{2,1,0:T(8,128)(2,1)S(1)}, u32[]{:S(2)}) copy-start(bf16[2,128,640]{2,1,0:T(8,128)(2,1)S(1)} %collective-permute-done.9.refs_5_) | copy-start | bytes 983044
  58.9 0.8 copy-start.10
  58.9 0.7 copy-start.17
  59.7 1.0 %copy-start.7 = (bf16[128,1024]{1,0:T(8,128)(2,1)S(1)}, bf16[128,1024]{1,0:T(8,128)(2,1)}, u32[]{:S(2)}) copy-start(bf16[128,1024]{1,0:T(8,128)(2,1)} %g_ref.1) | copy-start | bytes 786436
  63.7 24.9 %all-to-all-start.2 = ((bf16[8,384,128]{2,1,0:T(8,128)(2,1)}), bf16[8,384,128]{2,1,0:T(8,128)(2,1)S(1)}, u32[]{:S(2)}, u32[]{:S(2)}) async-start(bf16[8,384,128]{2,1,0:T(8,128)(2,1)} %get-tuple-element.74.refs_14_), calls=%async_computation.2 | async-start | bytes 1572864 | tf_op jit(solution)/shard_map/all_to_all | solution.py:449
  69.5 1.7 %copy-start.11 = (bf16[640,256]{1,0:T(8,128)(2,1)}, bf16[640,256]{1,0:T(8,128)(2,1)S(1)}, u32[]{:S(2)}) copy-start(bf16[640,256]{1,0:T(8,128)(2,1)S(1)} %broadcast_select_fusion.refs_9_) | copy-start | bytes 983044
  69.5 1.7 %collective-permute-start.13 = (bf16[640,256]{1,0:T(8,128)(2,1)S(1)}, bf16[640,256]{1,0:T(8,128)(2,1)S(1)}, u32[]{:S(2)}, u32[]{:S(2)}) collective-permute-start(bf16[640,256]{1,0:T(8,128)(2,1)S(1)} %broadcast_select_fusion.refs_9_), channel_id=1, source_target_pairs={{0,8},{8,0},{1,9},{9,1},{2,10},{10,2},{3,11},{11,3},{4,12},{12,4},... | collective-permute-start | bytes 983048 | tf_op jit(solution)/shard_map/ppermute | solution.py:336
  70.3 18.3 %copy-start.5 = (s32[8]{0:T(128)S(1)}, s32[8]{0:T(128)}, u32[]{:S(2)}) copy-start(s32[8]{0:T(128)} %get-tuple-element.72.after_ref.rows_here) | copy-start | bytes 100
  71.2 0.7 copy-start.18
  77.2 8.4 %collective-permute-start.14 = (bf16[128,512]{1,0:T(8,128)(2,1)}, bf16[128,512]{1,0:T(8,128)(2,1)S(1)}, u32[]{:S(2)}, u32[]{:S(2)}) collective-permute-start(bf16[128,512]{1,0:T(8,128)(2,1)} %get-tuple-element.81), channel_id=1, source_target_pairs={{0,1},{1,0},{2,3},{3,2},{4,5},{5,4},{6,7},{7,6},{8,9},{9,8},{10,11... | collective-permute-start | bytes 393224 | tf_op jit(solution)/shard_map/ppermute | solution.py:333
  79.3 6.3 %collective-permute-start.15 = (bf16[128,512]{1,0:T(8,128)(2,1)}, bf16[128,512]{1,0:T(8,128)(2,1)S(1)}, u32[]{:S(2)}, u32[]{:S(2)}) collective-permute-start(bf16[128,512]{1,0:T(8,128)(2,1)} %get-tuple-element.82), channel_id=1, source_target_pairs={{0,16},{16,0},{1,17},{17,1},{2,18},{18,2},{3,19},{19,3},{4,20},{20... | collective-permute-start | bytes 393224 | tf_op jit(solution)/shard_map/ppermute | solution.py:339
  79.8 8.3 %collective-permute-start.16 = (bf16[128,512]{1,0:T(8,128)(2,1)}, bf16[128,512]{1,0:T(8,128)(2,1)S(1)}, u32[]{:S(2)}, u32[]{:S(2)}) collective-permute-start(bf16[128,512]{1,0:T(8,128)(2,1)} %get-tuple-element.83), channel_id=1, source_target_pairs={{0,17},{1,16},{2,19},{3,18},{4,21},{5,20},{6,23},{7,22},{16,1},{17... | collective-permute-start | bytes 393224 | tf_op jit(solution)/shard_map/ppermute | solution.py:450
  88.6 2.3 %collective-permute-start.18 = (bf16[8,384,128]{2,1,0:T(8,128)(2,1)S(1)}, bf16[8,384,128]{2,1,0:T(8,128)(2,1)S(1)}, u32[]{:S(2)}, u32[]{:S(2)}) collective-permute-start(bf16[8,384,128]{2,1,0:T(8,128)(2,1)S(1)} %all-to-all-done.2.rest_0_), channel_id=1, source_target_pairs={{0,8},{8,0},{1,9},{9,1},{2,10},{10,2},{3,11},{11,3},{4,12},{12,4},... | collective-permute-start | bytes 2359304 | tf_op jit(solution)/shard_map/ppermute | solution.py:336
  88.6 2.3 %collective-permute-start.17 = (s32[8]{0:T(128)S(1)}, s32[8]{0:T(128)S(1)}, u32[]{:S(2)}, u32[]{:S(2)}) collective-permute-start(s32[8]{0:T(128)S(1)} %copy-done.5), channel_id=1, source_target_pairs={{0,8},{8,0},{1,9},{9,1},{2,10},{10,2},{3,11},{11,3},{4,12},{12,4},... | collective-permute-start | bytes 104 | tf_op jit(solution)/shard_map/ppermute | solution.py:336
  90.9 3.1 %copy-start.1 = (bf16[640,512]{1,0:T(8,128)(2,1)S(1)}, bf16[640,512]{1,0:T(8,128)(2,1)}, u32[]{:S(2)}) copy-start(bf16[640,512]{1,0:T(8,128)(2,1)} %param.9) | copy-start | bytes 1966084

commit v14 on v13

--- a/solution.py
+++ b/solution.py
@@ -103,8 +103,8 @@
     out_ref[...] = jnp.full(out_ref.shape, slot_ref[block_ref[0]], jnp.int32)
 
 
-def split_kernel(where, x_ref, mine_ref, *theirs_refs):
-    inner = where[0]
+def split_kernel(x_ref, mine_ref, *theirs_refs):
+    inner = lax.axis_index("tensor") % 2
     outer, rows, width = mine_ref.shape
     each = outer // len(theirs_refs)
     for k in range(outer):
@@ -213,13 +213,14 @@
         out_ref[t, down_chunks:] = up_part.astype(jnp.bfloat16)
 
 
-def scatter_kernel(count, down_chunks, up_chunks, first_row, rows_here, rows_core, *rest):
+def scatter_kernel(count, down_chunks, up_chunks, rows_here, rows_core, *rest):
     sources, (down_out, up_out) = rest[:2], rest[4:6]
     pieces, down_sum, up_sum, ordered, arrived, sem = rest[6:]
     half = count // 2
     owned_rows = down_out.shape[0] * 8
+    first_row = lax.axis_index("dp") * owned_rows
     across = up_chunks // 8
-    rows = [(rows_here if b < half else rows_core)[b % half] - first_row[0] for b in range(count)]
+    rows = [(rows_here if b < half else rows_core)[b % half] - first_row for b in range(count)]
     arriving = [pltpu.make_async_copy(sources[b // half].at[b % half], pieces.at[b], arrived.at[b]) for b in range(count)]
     owned = [(row >= 0) & (row < owned_rows) for row in rows]
     for b in range(count):
@@ -277,46 +278,44 @@
                 copy.wait()
 
 
-def base_kernel(where, *refs):
+def base_kernel(*refs):
     whole, halves, w_from, out_refs = refs[:2], refs[2:6], refs[6:-8], refs[-7:-3]
     x_buf, w_buf, sems = refs[-3:]
-    outer, _, rows, depth = x_buf.shape
-    width = w_buf.shape[2]
-    each = outer // 2
-    fetch_x = [
-        [pltpu.make_async_copy(ref.at[where[k]], x_buf.at[k, b], sems.at[k, b]) for b, ref in enumerate(whole)]
-        for k in range(outer)
-    ]
-
-    def fetch_half(k, b, begin):
-        for h in range(2):
-            @pl.when(where[k] // each == h)
-            def _():
-                source = halves[2 * b + h].at[where[k] % each]
-                copy = pltpu.make_async_copy(source, x_buf.at[k, 2 + b], sems.at[k, 2 + b])
-                copy.start() if begin else copy.wait()
-
-    fetch_w = [
-        [pltpu.make_async_copy(w_from[h * outer + k], w_buf.at[h * outer + k], sems.at[k, 4 + h]) for h in range(2)]
-        for k in range(outer)
-    ]
+    outer, rows, depth = whole[0].shape
+    width, each = w_from[0].shape[1], outer // 2
+    z = lax.axis_index("tensor") // 2
+    order = [z, z ^ 1, jnp.where(z < 2, 2, 1), jnp.where(z < 2, 3, 0)]
+
+    def fetch(k, begin):
+        columns = pl.ds(k * depth, depth)
+        copies = [
+            pltpu.make_async_copy(ref.at[order[k]], x_buf.at[pl.ds(b * rows, rows), columns], sems.at[k, b])
+            for b, ref in enumerate(whole)
+        ] + [
+            pltpu.make_async_copy(w_from[h * outer + k], w_buf.at[columns, pl.ds(h * width, width)], sems.at[k, 4 + h])
+            for h in range(2)
+        ]
+        for copy in copies:
+            copy.start() if begin else copy.wait()
+        for b in range(2):
+            for h in range(2):
+                @pl.when(order[k] // each == h)
+                def _():
+                    source = halves[2 * b + h].at[order[k] % each]
+                    place = x_buf.at[pl.ds((2 + b) * rows, rows), columns]
+                    copy = pltpu.make_async_copy(source, place, sems.at[k, 2 + b])
+                    copy.start() if begin else copy.wait()
+
     for k in range(outer):
-        for copy in fetch_x[k] + fetch_w[k]:
-            copy.start()
-        for b in range(2):
-            fetch_half(k, b, True)
-    total = [0.0, 0.0]
-    for k in range(outer):
-        for copy in fetch_x[k] + fetch_w[k]:
-            copy.wait()
-        for b in range(2):
-            fetch_half(k, b, False)
-        left = x_buf[k].reshape(4 * rows, depth)
-        for h in range(2):
-            total[h] += dot(left, w_buf[h * outer + k])
-    for h in range(2):
-        for b, ref in enumerate(out_refs):
-            ref[:, h * width:(h + 1) * width] = total[h][b * rows:(b + 1) * rows].astype(ref.dtype)
+        fetch(k, True)
+    total = 0.0
+    for first in range(0, outer, each):
+        for k in range(first, first + each):
+            fetch(k, False)
+        columns = slice(first * depth, (first + each) * depth)
+        total += dot(x_buf[:, columns], w_buf[columns, :])
+    for b, ref in enumerate(out_refs):
+        ref[...] = total[b * rows:(b + 1) * rows].astype(ref.dtype)
 
 
 def fast_body(tokens, cotangent, frozen_value, down_store, up_store, block_adapter, adapter_slot):
@@ -327,7 +326,7 @@
     down_chunks = down_store.shape[1] // LANES
     up_chunks = up_store.shape[1] // LANES
     me, part, core = lax.axis_index("tensor"), lax.axis_index("parts"), lax.axis_index("dp")
-    z, x = me // 2, me % 2
+    z = me // 2
 
     def exchange(value, s):
         return lax.ppermute(value, "tensor", [(t, t ^ s) for t in range(group)])
@@ -351,9 +350,9 @@
     token = jax.ShapeDtypeStruct((1,), jnp.int32)
     some = jax.ShapeDtypeStruct((outer // 2, token_rows, slice_width), jnp.bfloat16)
     x_mine, *x_theirs = pl.pallas_call(
-        split_kernel, out_shape=(block, some, some), in_specs=[SMEM, VMEM], out_specs=[VMEM] * 3,
+        split_kernel, out_shape=(block, some, some), in_specs=[VMEM], out_specs=[VMEM] * 3,
         name="split_tokens", compiler_params=LIMIT,
-    )(x[None], split_from)
+    )(split_from)
     x_far = [exchange(x_theirs[0], 1)]
     y_mine = other_part(x_mine)
     xs = pl.pallas_call(
@@ -364,7 +363,7 @@
             pltpu.VMEM((group, 2 * token_rows, slice_width // 2), jnp.bfloat16),
             pltpu.SemaphoreType.DMA((group,)),
         ],
-        cost_estimate=cost(),
+        cost_estimate=cost(read=128 << 20),
     )(split_from)
     middle = [(t, t ^ 6) for t in range(group) if t // 2 in (1, 2)]
     ends = [(t, t ^ 2) for t in range(group) if t // 2 in (1, 2)]
@@ -429,22 +428,21 @@
     _, passed_near = lax.optimization_barrier((terms, passed_near))
     last = jnp.where(inside, over_near, passed_near)
     quarters = quarter + [last] + quarter_core + [other_core(last)]
-    source = jnp.stack([z, z ^ 1, jnp.where(z < 2, 2, 1), jnp.where(z < 2, 3, 0)])
     sums = [jax.ShapeDtypeStruct((token_rows, parts * width), kind) for kind in (jnp.float32,) + (jnp.bfloat16,) * 3]
     own, to_part, to_inner, to_both = pl.pallas_call(
         base_kernel,
         out_shape=sums,
-        in_specs=[SMEM] + [ANY] * (7 + 2 * outer),
+        in_specs=[ANY] * (7 + 2 * outer),
         out_specs=[VMEM] * 4,
         scratch_shapes=[
-            pltpu.VMEM((outer, 4, token_rows, slice_width), jnp.bfloat16),
-            pltpu.VMEM((2 * outer, slice_width, width), jnp.bfloat16),
+            pltpu.VMEM((4 * token_rows, outer * slice_width), jnp.bfloat16),
+            pltpu.VMEM((outer * slice_width, parts * width), jnp.bfloat16),
             pltpu.SemaphoreType.DMA((outer, 6)),
         ],
         compiler_params=WIDE,
         cost_estimate=cost(flops=4 << 30, read=8 << 20),
         name="frozen_part",
-    )(source, x_mine, y_mine, *x_far, *y_far, *quarters, terms)
+    )(x_mine, y_mine, *x_far, *y_far, *quarters, terms)
     opposite = [(a * group + t, (parts - 1 - a) * group + (t ^ 1)) for a in range(parts) for t in range(group)]
     back = lax.all_to_all(terms, "tensor", 0, 0)
     arrived = (exchange(to_inner, 1), other_part(to_part), lax.ppermute(to_both, ("parts", "tensor"), opposite))
@@ -454,9 +452,9 @@
     grad_down, grad_up = pl.pallas_call(
         functools.partial(scatter_kernel, 2 * group, down_chunks, up_chunks),
         out_shape=(down_shape, up_shape),
-        in_specs=[SMEM] * 3 + [ANY] * 4,
+        in_specs=[SMEM] * 2 + [ANY] * 4,
         out_specs=(ANY, ANY),
-        input_output_aliases={5: 0, 6: 1},
+        input_output_aliases={4: 0, 5: 1},
         scratch_shapes=[
             pltpu.VMEM((2 * group,) + pieces.shape[1:], jnp.bfloat16),
             pltpu.VMEM((2 * group, down_chunks, LANES), jnp.float32),
@@ -468,8 +466,7 @@
         compiler_params=LIMIT,
         cost_estimate=cost(read=16 << 20),
         name="place_rows",
-    )((core * (ADAPTERS // lax.axis_size("dp")))[None], rows, rows_core, back, back_core,
-      down_zero, up_zero)
+    )(rows, rows_core, back, back_core, down_zero, up_zero)
     grad_down = grad_down.reshape(owned_groups, down_chunks, 8, LANES).transpose(0, 2, 1, 3)
     grad_up = grad_up.reshape(owned_groups, up_chunks, 8, LANES).transpose(0, 2, 1, 3)
 

time: 94.6 us -> 94.6 us (level)
  waiting for transfers between devices: 17 us -> 18.6 us
    unnamed x38 -> x36, local copies, waits for them, and re-layouts: 5.95 us -> 5.83 us
  transfers between devices with their start and end apart: 22 -> 22, of which waited for: 9 -> 9; matrix products, arithmetic and copies ran while one was open for 5% -> 4% of each run, Pallas kernels for 26% -> 25%
where the time goes in v14:
time: 94.6 us; the launch traced here: 93.7 us
  starting transfers between devices  32.8 us (35%)
  Pallas kernels  31 us (33%)
  waiting for transfers between devices  18.6 us (20%)
  local copies, waits for them, and re-layouts  5.86 us (6%)
  other arithmetic  3.84 us (4%)
  between operations  1.65 us (2%)
    ppermute x4, starting transfers between devices, exchange(): return lax.ppermute(value, 'tensor', [(t, t ^ s) for t in range(group)])  9.91 us
    pallas_call x1, Pallas kernels, fast_body(): pl.pallas_call(zero_kernel, out_shape=(down_shape, up_shape, token), in_s...  9.48 us
    ppermute x4, waiting for transfers between devices, exchange(): return lax.ppermute(value, 'tensor', [(t, t ^ s) for t in range(group)])  6.18 us
    unnamed x36, local copies, waits for them, and re-layouts  5.83 us
    pallas_call x1, Pallas kernels, fast_body(): pl.pallas_call(gather_kernel, out_shape=(pieces, jax.ShapeDtypeStruct((gr...  5.26 us
    pallas_call x1, Pallas kernels, fast_body(): pl.pallas_call(base_kernel, out_shape=sums, in_specs=[ANY] * (7 + 2 * out...  4.96 us
    all_to_all x1, starting transfers between devices, fast_body(): back = lax.all_to_all(terms, 'tensor', 0, 0)  4.35 us
    ppermute x4, starting transfers between devices, other_part(): lax.ppermute(value, 'parts', [(a, parts - 1 - a) for a in range(parts)])  4.18 us
  transfers between devices with their start and end apart: 22, of which 9 were waited for; matrix products, arithmetic and copies ran while one was open for 4% of the time, Pallas kernels for 25%

profile of v14, /device:TPU:0, one launch (start us, length us, event | category | flops | bytes accessed | tf_op | source)
XLA Modules:
  0.0 93.7 jit_solution(3202295829730089663)
XLA Ops:
  0.6 0.0 copy-start
  1.4 1.3 %own_row.1 = s32[8,1,128]{2,1,0:T(1,128)} custom-call(s32[1]{0:T(128)S(6)} %copy.14.block_ref, s32[256]{0:T(256)} %slot_ref.1), custom_call_target="tpu_custom_call" | custom-call | tf_op jit(solution)/shard_map/own_row/pallas_call | solution.py:340
  2.7 1.4 %collective-permute-start.1 = (bf16[640,256]{1,0:T(8,128)(2,1)S(1)}, bf16[640,256]{1,0:T(8,128)(2,1)}, u32[]{:S(2)}, u32[]{:S(2)}) collective-permute-start(bf16[640,256]{1,0:T(8,128)(2,1)S(1)} %constant_dynamic-slice_fusion.refs_6_), channel_id=1, source_target_pairs={{2,4},{3,5},{4,2},{5,3},{10,12},{11,13},{12,10},{13,11},{18,20},{1... | collective-permute-start | bytes 983048 | tf_op jit(solution)/shard_map/ppermute | solution.py:371
  4.1 5.2 %collective-permute-start = (bf16[640,256]{1,0:T(8,128)(2,1)S(1)}, bf16[640,256]{1,0:T(8,128)(2,1)}, u32[]{:S(2)}, u32[]{:S(2)}) collective-permute-start(bf16[640,256]{1,0:T(8,128)(2,1)S(1)} %constant_dynamic-slice_fusion.refs_6_), channel_id=1, source_target_pairs={{0,2},{1,3},{2,0},{3,1},{4,6},{5,7},{6,4},{7,5},{8,10},{9,11},{10,... | collective-permute-start | bytes 983048 | tf_op jit(solution)/shard_map/ppermute | solution.py:332
  9.3 1.3 %copy-done.2 = bf16[128,5120]{1,0:T(8,128)(2,1)S(1)} copy-done((bf16[128,5120]{1,0:T(8,128)(2,1)S(1)}, bf16[128,5120]{1,0:T(8,128)(2,1)}, u32[]{:S(2)}) %copy-start.2) | copy-done | bytes 1310744
  10.6 0.1 split_tokens.1
  10.7 1.6 %collective-permute-start.4 = (bf16[4,128,640]{2,1,0:T(8,128)(2,1)S(1)}, bf16[4,128,640]{2,1,0:T(8,128)(2,1)}, u32[]{:S(2)}, u32[]{:S(2)}) collective-permute-start(bf16[4,128,640]{2,1,0:T(8,128)(2,1)S(1)} %get-tuple-element.49.refs_0_), channel_id=1, source_target_pairs={{0,16},{16,0},{1,17},{17,1},{2,18},{18,2},{3,19},{19,3},{4,20},{20... | collective-permute-start | bytes 1966088 | tf_op jit(solution)/shard_map/ppermute | solution.py:338
  12.3 3.6 %all-to-all-start = ((s32[8,1,128]{2,1,0:T(1,128)}), s32[8,1,128]{2,1,0:T(1,128)S(1)}, u32[]{:S(2)}, u32[]{:S(2)}) async-start(s32[8,1,128]{2,1,0:T(1,128)} %own_row.1), calls=%async_computation | async-start | bytes 8192 | tf_op jit(solution)/shard_map/all_to_all | solution.py:344
  15.8 2.0 %collective-permute-start.2 = (bf16[2,128,640]{2,1,0:T(8,128)(2,1)S(1)}, bf16[2,128,640]{2,1,0:T(8,128)(2,1)}, u32[]{:S(2)}, u32[]{:S(2)}) collective-permute-start(bf16[2,128,640]{2,1,0:T(8,128)(2,1)S(1)} %get-tuple-element.51), channel_id=1, source_target_pairs={{0,1},{1,0},{2,3},{3,2},{4,5},{5,4},{6,7},{7,6},{8,9},{9,8},{10,11... | collective-permute-start | bytes 983048 | tf_op jit(solution)/shard_map/ppermute | solution.py:332
  17.9 3.9 %pair_columns.1.xs_ref = bf16[8,256,320]{2,1,0:T(8,128)(2,1)} custom-call(bf16[128,5120]{1,0:T(8,128)(2,1)} %x_ref.1), custom_call_target="tpu_custom_call" | custom-call | bytes 134217728 | tf_op jit(solution)/shard_map/pair_columns/pallas_call | solution.py:358
  21.7 0.5 all-to-all-done.asked
  22.2 0.0 collective-permute-done.1
  22.2 0.0 collective-permute-done.refs_7_
  22.2 0.6 collective-permute-start.3
  22.9 0.7 collective-permute-start.5
  23.5 1.3 %collective-permute-start.6 = (bf16[640,256]{1,0:T(8,128)(2,1)}, bf16[640,256]{1,0:T(8,128)(2,1)}, u32[]{:S(2)}, u32[]{:S(2)}) collective-permute-start(bf16[640,256]{1,0:T(8,128)(2,1)} %collective-permute-done.1), channel_id=1, source_target_pairs={{2,0},{3,1},{4,6},{5,7},{10,8},{11,9},{12,14},{13,15},{18,16},{19,... | collective-permute-start | bytes 983048 | tf_op jit(solution)/shard_map/ppermute | solution.py:375
  24.9 5.3 %pick_panels.1 = (bf16[8,384,128]{2,1,0:T(8,128)(2,1)}, s32[8]{0:T(128)}) custom-call(s32[8,1,128]{2,1,0:T(1,128)} %copy-done.12, bf16[32,320,8,128]{3,2,1,0:T(8,128)(2,1)} %bitcast.16, bf16[32,64,8,128]{3,2,1,0:T(8,128)(2,1)} %bitcast.18), custom_call_target="tpu_custom_call" | custom-call | bytes 41943040 | tf_op jit(solution)/shard_map/pick_panels/pallas_call | solution.py:381
  30.1 0.0 collective-permute-done.2.refs_2_
  30.1 0.0 collective-permute-done.4.refs_1_
  30.2 1.3 %collective-permute-done.3.refs_3_ = bf16[2,128,640]{2,1,0:T(8,128)(2,1)} collective-permute-done((bf16[2,128,640]{2,1,0:T(8,128)(2,1)S(1)}, bf16[2,128,640]{2,1,0:T(8,128)(2,1)}, u32[]{:S(2)}, u32[]{:S(2)}) %collective-permute-start.3) | collective-permute-done | bytes 327712 | tf_op jit(solution)/shard_map/ppermute | solution.py:332
  31.5 0.0 collective-permute-done.5
  31.5 2.8 %collective-permute-done.6 = bf16[640,256]{1,0:T(8,128)(2,1)} collective-permute-done((bf16[640,256]{1,0:T(8,128)(2,1)}, bf16[640,256]{1,0:T(8,128)(2,1)}, u32[]{:S(2)}, u32[]{:S(2)}) %collective-permute-start.6) | collective-permute-done | bytes 327712 | tf_op jit(solution)/shard_map/ppermute | solution.py:375
  34.3 3.9 %all-to-all-start.1 = ((bf16[8,384,128]{2,1,0:T(8,128)(2,1)}), bf16[8,384,128]{2,1,0:T(8,128)(2,1)S(1)}, u32[]{:S(2)}, u32[]{:S(2)}) async-start(bf16[8,384,128]{2,1,0:T(8,128)(2,1)} %get-tuple-element.62), calls=%async_computation.1 | async-start | bytes 1572864 | tf_op jit(solution)/shard_map/all_to_all | solution.py:400
  38.2 1.0 %broadcast_select_fusion.1.refs_8_ = bf16[640,256]{1,0:T(8,128)(2,1)S(1)} fusion(bf16[640,256]{1,0:T(8,128)(2,1)} %collective-permute-done.1, bf16[640,256]{1,0:T(8,128)(2,1)} %collective-permute-done.6, pred[]{:T(512)S(6)} %or.3), kind=kLoop, calls=%fused_computation.3 | loop fusion | flops 163840 | bytes 983041 | tf_op jit(solution)/shard_map/jit(_where)/select_n | solution.py:405
  39.2 0.1 collective-permute-start.12
  39.3 0.6 collective-permute-start.8
  39.9 1.5 %collective-permute-start.9 = (bf16[2,128,640]{2,1,0:T(8,128)(2,1)}, bf16[2,128,640]{2,1,0:T(8,128)(2,1)S(1)}, u32[]{:S(2)}, u32[]{:S(2)}) collective-permute-start(bf16[2,128,640]{2,1,0:T(8,128)(2,1)} %collective-permute-done.3.refs_3_), channel_id=1, source_target_pairs={{0,16},{16,0},{1,17},{17,1},{2,18},{18,2},{3,19},{19,3},{4,20},{20... | collective-permute-start | bytes 983048 | tf_op jit(solution)/shard_map/ppermute | solution.py:338
  41.4 1.3 %collective-permute-start.7 = (bf16[640,256]{1,0:T(8,128)(2,1)S(1)}, bf16[640,256]{1,0:T(8,128)(2,1)S(1)}, u32[]{:S(2)}, u32[]{:S(2)}) collective-permute-start(bf16[640,256]{1,0:T(8,128)(2,1)S(1)} %collective-permute-done.5), channel_id=1, source_target_pairs={{2,0},{3,1},{4,6},{5,7},{10,8},{11,9},{12,14},{13,15},{18,16},{19,... | collective-permute-start | bytes 983048 | tf_op jit(solution)/shard_map/ppermute | solution.py:404
  42.7 0.1 collective-permute-start.10
  42.8 0.0 collective-permute-done.12.refs_12_
  42.8 0.7 copy-done.13
  43.6 0.5 collective-permute-start.11
  44.0 0.6 copy-done.4
  44.7 9.5 %clear_rows.1 = (f32[16,320,8,1,128]{4,3,2,1,0:T(1,128)}, f32[16,64,8,1,128]{4,3,2,1,0:T(1,128)}, s32[1]{0:T(128)}) custom-call(s32[8]{0:T(128)S(1)} %copy-done.4), custom_call_target="tpu_custom_call" | custom-call | bytes 29360128 | tf_op jit(solution)/shard_map/clear_rows/pallas_call | solution.py:410
  54.1 0.0 collective-permute-done.8.refs_4_
  54.2 2.5 %collective-permute-done.9.refs_5_ = bf16[2,128,640]{2,1,0:T(8,128)(2,1)S(1)} collective-permute-done((bf16[2,128,640]{2,1,0:T(8,128)(2,1)}, bf16[2,128,640]{2,1,0:T(8,128)(2,1)S(1)}, u32[]{:S(2)}, u32[]{:S(2)}) %collective-permute-start.9) | collective-permute-done | bytes 327712 | tf_op jit(solution)/shard_map/ppermute | solution.py:338
  56.7 1.8 %collective-permute-done.7 = bf16[640,256]{1,0:T(8,128)(2,1)S(1)} collective-permute-done((bf16[640,256]{1,0:T(8,128)(2,1)S(1)}, bf16[640,256]{1,0:T(8,128)(2,1)S(1)}, u32[]{:S(2)}, u32[]{:S(2)}) %collective-permute-start.7) | collective-permute-done | bytes 327712 | tf_op jit(solution)/shard_map/ppermute | solution.py:404
  58.4 0.0 collective-permute-done.10.refs_10_
  58.5 0.7 copy-done.9
  59.2 0.7 copy-done.16
  59.9 0.0 collective-permute-done.11.refs_11_
  59.9 0.0 all-to-all-done.1.pieces
  59.9 0.0 copy-start.7
  59.9 0.9 %copy-done.7 = bf16[128,1024]{1,0:T(8,128)(2,1)S(1)} copy-done((bf16[128,1024]{1,0:T(8,128)(2,1)S(1)}, bf16[128,1024]{1,0:T(8,128)(2,1)}, u32[]{:S(2)}) %copy-start.7) | copy-done | bytes 262168
  60.8 3.0 %adapter.1 = (bf16[8,384,128]{2,1,0:T(8,128)(2,1)}, f32[128,1024]{1,0:T(8,128)S(1)}) custom-call(bf16[8,256,320]{2,1,0:T(8,128)(2,1)S(1)} %copy-done.3, bf16[128,1024]{1,0:T(8,128)(2,1)S(1)} %copy-done.7, bf16[8,384,128]{2,1,0:T(8,128)(2,1)S(1)} %all-to-all-done.1.pieces, s32[1]{0:T(128)} %get-tuple-element.73._), custom_call_target="tpu_custom_call" | custom-call | flops 3221225472 | bytes 8388608 | tf_op jit(solution)/shard_map/adapter/pallas_call | solution.py:418
  63.8 4.3 %all-to-all-start.2 = ((bf16[8,384,128]{2,1,0:T(8,128)(2,1)}), bf16[8,384,128]{2,1,0:T(8,128)(2,1)S(1)}, u32[]{:S(2)}, u32[]{:S(2)}) async-start(bf16[8,384,128]{2,1,0:T(8,128)(2,1)} %get-tuple-element.74.refs_14_), calls=%async_computation.2 | async-start | bytes 1572864 | tf_op jit(solution)/shard_map/all_to_all | solution.py:447
  68.2 1.0 %broadcast_select_fusion.refs_9_ = bf16[640,256]{1,0:T(8,128)(2,1)S(1)} fusion(bf16[640,256]{1,0:T(8,128)(2,1)S(1)} %collective-permute-done.5, bf16[640,256]{1,0:T(8,128)(2,1)} %copy-done.9, pred[]{:T(512)S(6)} %or.3), kind=kLoop, calls=%fused_computation.2 | loop fusion | flops 163840 | bytes 983041 | tf_op jit(solution)/shard_map/jit(_where)/select_n | solution.py:429
  69.2 0.1 collective-permute-start.13
  69.3 1.6 %collective-permute-done.13.refs_13_ = bf16[640,256]{1,0:T(8,128)(2,1)S(1)} collective-permute-done((bf16[640,256]{1,0:T(8,128)(2,1)S(1)}, bf16[640,256]{1,0:T(8,128)(2,1)S(1)}, u32[]{:S(2)}, u32[]{:S(2)}) %collective-permute-start.13) | collective-permute-done | bytes 327712 | tf_op jit(solution)/shard_map/ppermute | solution.py:335
  70.9 0.7 copy-done.17
  71.7 5.0 %frozen_part.1 = (f32[128,512]{1,0:T(8,128)}, bf16[128,512]{1,0:T(8,128)(2,1)}, bf16[128,512]{1,0:T(8,128)(2,1)}, bf16[128,512]{1,0:T(8,128)(2,1)}) custom-call(bf16[4,128,640]{2,1,0:T(8,128)(2,1)} %copy-done.6, bf16[4,128,640]{2,1,0:T(8,128)(2,1)} %collective-permute-done.4.refs_1_, bf16[2,128,640]{2,1,0:T(8,128)(2,1)} %collective-permute-done.2.refs_2_, ...), custom_call_target="tpu_custom_call" | custom-call | flops 4294967296 | bytes 8388608 | tf_op jit(solution)/shard_map/frozen_part/pallas_call | solution.py:432
  76.6 2.1 %collective-permute-start.14 = (bf16[128,512]{1,0:T(8,128)(2,1)}, bf16[128,512]{1,0:T(8,128)(2,1)S(1)}, u32[]{:S(2)}, u32[]{:S(2)}) collective-permute-start(bf16[128,512]{1,0:T(8,128)(2,1)} %get-tuple-element.81), channel_id=1, source_target_pairs={{0,1},{1,0},{2,3},{3,2},{4,5},{5,4},{6,7},{7,6},{8,9},{9,8},{10,11... | collective-permute-start | bytes 393224 | tf_op jit(solution)/shard_map/ppermute | solution.py:332
  78.7 0.5 collective-permute-start.15
  79.2 1.0 %collective-permute-start.16 = (bf16[128,512]{1,0:T(8,128)(2,1)}, bf16[128,512]{1,0:T(8,128)(2,1)S(1)}, u32[]{:S(2)}, u32[]{:S(2)}) collective-permute-start(bf16[128,512]{1,0:T(8,128)(2,1)} %get-tuple-element.83), channel_id=1, source_target_pairs={{0,17},{1,16},{2,19},{3,18},{4,21},{5,20},{6,23},{7,22},{16,1},{17... | collective-permute-start | bytes 393224 | tf_op jit(solution)/shard_map/ppermute | solution.py:448
  80.3 4.9 %collective-permute-done.14 = bf16[128,512]{1,0:T(8,128)(2,1)S(1)} collective-permute-done((bf16[128,512]{1,0:T(8,128)(2,1)}, bf16[128,512]{1,0:T(8,128)(2,1)S(1)}, u32[]{:S(2)}, u32[]{:S(2)}) %collective-permute-start.14) | collective-permute-done | bytes 131104 | tf_op jit(solution)/shard_map/ppermute | solution.py:332
  85.1 0.0 collective-permute-done.15
  85.1 2.5 %collective-permute-done.16 = bf16[128,512]{1,0:T(8,128)(2,1)S(1)} collective-permute-done((bf16[128,512]{1,0:T(8,128)(2,1)}, bf16[128,512]{1,0:T(8,128)(2,1)S(1)}, u32[]{:S(2)}, u32[]{:S(2)}) %collective-permute-start.16) | collective-permute-done | bytes 131104 | tf_op jit(solution)/shard_map/ppermute | solution.py:448
  87.6 0.7 all-to-all-done.2.rest_0_
  88.3 0.0 collective-permute-start.18
  88.3 0.5 collective-permute-start.17
  88.8 1.0 %convert_add_fusion = (f32[128,512]{1,0:T(8,128)S(1)}, f32[128,512]{1,0:T(8,128)S(1)}) fusion(bf16[128,512]{1,0:T(8,128)(2,1)S(1)} %collective-permute-done.16, bf16[128,512]{1,0:T(8,128)(2,1)S(1)} %collective-permute-done.15, f32[128,512]{1,0:T(8,128)} %get-tuple-element.80, bf16[128,512]{1,0:T(8,128)(2,1)S(1)} %collective-permute-done.14), kind=kLoop, calls=%fused_computation.4 | loop fusion | flops 327680 | bytes 1179648 | tf_op jit(solution)/shard_map/add | solution.py:474
  89.8 0.8 fusion
  90.6 0.0 collective-permute-done.17.rows_core
  90.6 3.1 %place_rows.1 = (f32[16,320,8,1,128]{4,3,2,1,0:T(1,128)}, f32[16,64,8,1,128]{4,3,2,1,0:T(1,128)}) custom-call(s32[8]{0:T(128)S(1)} %copy-done.5, s32[8]{0:T(128)S(1)} %collective-permute-done.17.rows_core, bf16[8,384,128]{2,1,0:T(8,128)(2,1)S(1)} %all-to-all-done.2.rest_0_, ...), custom_call_target="tpu_custom_call", output_to_operand_aliasing={{0}: (4, {}), {1}: (5, {})} | custom-call | bytes 16777216 | tf_op jit(solution)/shard_map/place_rows/pallas_call | solution.py:452
  (30 shorter events, 0.1 us)
Async XLA Ops:
  0.6 2.0 %copy-start = (bf16[640,512]{1,0:T(8,128)(2,1)S(1)}, bf16[640,512]{1,0:T(8,128)(2,1)}, u32[]{:S(2)}) copy-start(bf16[640,512]{1,0:T(8,128)(2,1)} %param.9) | copy-start | bytes 1966084
  2.7 40.0 %copy-start.11 = (bf16[640,256]{1,0:T(8,128)(2,1)}, bf16[640,256]{1,0:T(8,128)(2,1)S(1)}, u32[]{:S(2)}) copy-start(bf16[640,256]{1,0:T(8,128)(2,1)S(1)} %constant_dynamic-slice_fusion.refs_6_) | copy-start | bytes 983044
  2.7 19.6 %collective-permute-start.1 = (bf16[640,256]{1,0:T(8,128)(2,1)S(1)}, bf16[640,256]{1,0:T(8,128)(2,1)}, u32[]{:S(2)}, u32[]{:S(2)}) collective-permute-start(bf16[640,256]{1,0:T(8,128)(2,1)S(1)} %constant_dynamic-slice_fusion.refs_6_), channel_id=1, source_target_pairs={{2,4},{3,5},{4,2},{5,3},{10,12},{11,13},{12,10},{13,11},{18,20},{1... | collective-permute-start | bytes 983048 | tf_op jit(solution)/shard_map/ppermute | solution.py:371
  4.1 18.2 %collective-permute-start = (bf16[640,256]{1,0:T(8,128)(2,1)S(1)}, bf16[640,256]{1,0:T(8,128)(2,1)}, u32[]{:S(2)}, u32[]{:S(2)}) collective-permute-start(bf16[640,256]{1,0:T(8,128)(2,1)S(1)} %constant_dynamic-slice_fusion.refs_6_), channel_id=1, source_target_pairs={{0,2},{1,3},{2,0},{3,1},{4,6},{5,7},{6,4},{7,5},{8,10},{9,11},{10,... | collective-permute-start | bytes 983048 | tf_op jit(solution)/shard_map/ppermute | solution.py:332
  9.3 1.3 %copy-start.2 = (bf16[128,5120]{1,0:T(8,128)(2,1)S(1)}, bf16[128,5120]{1,0:T(8,128)(2,1)}, u32[]{:S(2)}) copy-start(bf16[128,5120]{1,0:T(8,128)(2,1)} %x_ref.1) | copy-start | bytes 3932164
  10.7 19.4 %copy-start.6 = (bf16[4,128,640]{2,1,0:T(8,128)(2,1)}, bf16[4,128,640]{2,1,0:T(8,128)(2,1)S(1)}, u32[]{:S(2)}) copy-start(bf16[4,128,640]{2,1,0:T(8,128)(2,1)S(1)} %get-tuple-element.49.refs_0_) | copy-start | bytes 1966084
  10.7 19.4 %collective-permute-start.4 = (bf16[4,128,640]{2,1,0:T(8,128)(2,1)S(1)}, bf16[4,128,640]{2,1,0:T(8,128)(2,1)}, u32[]{:S(2)}, u32[]{:S(2)}) collective-permute-start(bf16[4,128,640]{2,1,0:T(8,128)(2,1)S(1)} %get-tuple-element.49.refs_0_), channel_id=1, source_target_pairs={{0,16},{16,0},{1,17},{17,1},{2,18},{18,2},{3,19},{19,3},{4,20},{20... | collective-permute-start | bytes 1966088 | tf_op jit(solution)/shard_map/ppermute | solution.py:338
  12.3 9.9 %all-to-all-start = ((s32[8,1,128]{2,1,0:T(1,128)}), s32[8,1,128]{2,1,0:T(1,128)S(1)}, u32[]{:S(2)}, u32[]{:S(2)}) async-start(s32[8,1,128]{2,1,0:T(1,128)} %own_row.1), calls=%async_computation | async-start | bytes 8192 | tf_op jit(solution)/shard_map/all_to_all | solution.py:344
  15.8 14.3 %collective-permute-start.2 = (bf16[2,128,640]{2,1,0:T(8,128)(2,1)S(1)}, bf16[2,128,640]{2,1,0:T(8,128)(2,1)}, u32[]{:S(2)}, u32[]{:S(2)}) collective-permute-start(bf16[2,128,640]{2,1,0:T(8,128)(2,1)S(1)} %get-tuple-element.51), channel_id=1, source_target_pairs={{0,1},{1,0},{2,3},{3,2},{4,5},{5,4},{6,7},{7,6},{8,9},{9,8},{10,11... | collective-permute-start | bytes 983048 | tf_op jit(solution)/shard_map/ppermute | solution.py:332
  22.2 2.6 %copy-start.12 = (s32[8,1,128]{2,1,0:T(1,128)}, s32[8,1,128]{2,1,0:T(1,128)S(1)}, u32[]{:S(2)}) copy-start(s32[8,1,128]{2,1,0:T(1,128)S(1)} %all-to-all-done.asked) | copy-start | bytes 12292
  22.2 9.2 %collective-permute-start.3 = (bf16[2,128,640]{2,1,0:T(8,128)(2,1)S(1)}, bf16[2,128,640]{2,1,0:T(8,128)(2,1)}, u32[]{:S(2)}, u32[]{:S(2)}) collective-permute-start(bf16[2,128,640]{2,1,0:T(8,128)(2,1)S(1)} %get-tuple-element.56), channel_id=1, source_target_pairs={{0,1},{1,0},{2,3},{3,2},{4,5},{5,4},{6,7},{7,6},{8,9},{9,8},{10,11... | collective-permute-start | bytes 983048 | tf_op jit(solution)/shard_map/ppermute | solution.py:332
  22.9 8.6 %collective-permute-start.5 = (bf16[640,256]{1,0:T(8,128)(2,1)}, bf16[640,256]{1,0:T(8,128)(2,1)S(1)}, u32[]{:S(2)}, u32[]{:S(2)}) collective-permute-start(bf16[640,256]{1,0:T(8,128)(2,1)} %collective-permute-done.refs_7_), channel_id=1, source_target_pairs={{2,4},{3,5},{4,2},{5,3},{10,12},{11,13},{12,10},{13,11},{18,20},{1... | collective-permute-start | bytes 983048 | tf_op jit(solution)/shard_map/ppermute | solution.py:374
  23.5 10.8 %collective-permute-start.6 = (bf16[640,256]{1,0:T(8,128)(2,1)}, bf16[640,256]{1,0:T(8,128)(2,1)}, u32[]{:S(2)}, u32[]{:S(2)}) collective-permute-start(bf16[640,256]{1,0:T(8,128)(2,1)} %collective-permute-done.1), channel_id=1, source_target_pairs={{2,0},{3,1},{4,6},{5,7},{10,8},{11,9},{12,14},{13,15},{18,16},{19,... | collective-permute-start | bytes 983048 | tf_op jit(solution)/shard_map/ppermute | solution.py:375
  24.8 35.0 %copy-start.3 = (bf16[8,256,320]{2,1,0:T(8,128)(2,1)S(1)}, bf16[8,256,320]{2,1,0:T(8,128)(2,1)}, u32[]{:S(2)}) copy-start(bf16[8,256,320]{2,1,0:T(8,128)(2,1)} %pair_columns.1.xs_ref) | copy-start | bytes 3932164
  34.3 25.6 %all-to-all-start.1 = ((bf16[8,384,128]{2,1,0:T(8,128)(2,1)}), bf16[8,384,128]{2,1,0:T(8,128)(2,1)S(1)}, u32[]{:S(2)}, u32[]{:S(2)}) async-start(bf16[8,384,128]{2,1,0:T(8,128)(2,1)} %get-tuple-element.62), calls=%async_computation.1 | async-start | bytes 1572864 | tf_op jit(solution)/shard_map/all_to_all | solution.py:400
  39.2 3.6 %copy-start.8 = (bf16[640,256]{1,0:T(8,128)(2,1)}, bf16[640,256]{1,0:T(8,128)(2,1)S(1)}, u32[]{:S(2)}) copy-start(bf16[640,256]{1,0:T(8,128)(2,1)S(1)} %broadcast_select_fusion.1.refs_8_) | copy-start | bytes 983044
  39.2 3.6 %collective-permute-start.12 = (bf16[640,256]{1,0:T(8,128)(2,1)S(1)}, bf16[640,256]{1,0:T(8,128)(2,1)S(1)}, u32[]{:S(2)}, u32[]{:S(2)}) collective-permute-start(bf16[640,256]{1,0:T(8,128)(2,1)S(1)} %broadcast_select_fusion.1.refs_8_), channel_id=1, source_target_pairs={{0,8},{8,0},{1,9},{9,1},{2,10},{10,2},{3,11},{11,3},{4,12},{12,4},... | collective-permute-start | bytes 983048 | tf_op jit(solution)/shard_map/ppermute | solution.py:335
  39.3 14.8 %collective-permute-start.8 = (bf16[2,128,640]{2,1,0:T(8,128)(2,1)}, bf16[2,128,640]{2,1,0:T(8,128)(2,1)S(1)}, u32[]{:S(2)}, u32[]{:S(2)}) collective-permute-start(bf16[2,128,640]{2,1,0:T(8,128)(2,1)} %collective-permute-done.2.refs_2_), channel_id=1, source_target_pairs={{0,16},{16,0},{1,17},{17,1},{2,18},{18,2},{3,19},{19,3},{4,20},{20... | collective-permute-start | bytes 983048 | tf_op jit(solution)/shard_map/ppermute | solution.py:338
  39.9 16.8 %collective-permute-start.9 = (bf16[2,128,640]{2,1,0:T(8,128)(2,1)}, bf16[2,128,640]{2,1,0:T(8,128)(2,1)S(1)}, u32[]{:S(2)}, u32[]{:S(2)}) collective-permute-start(bf16[2,128,640]{2,1,0:T(8,128)(2,1)} %collective-permute-done.3.refs_3_), channel_id=1, source_target_pairs={{0,16},{16,0},{1,17},{17,1},{2,18},{18,2},{3,19},{19,3},{4,20},{20... | collective-permute-start | bytes 983048 | tf_op jit(solution)/shard_map/ppermute | solution.py:338
  41.4 17.0 %collective-permute-start.7 = (bf16[640,256]{1,0:T(8,128)(2,1)S(1)}, bf16[640,256]{1,0:T(8,128)(2,1)S(1)}, u32[]{:S(2)}, u32[]{:S(2)}) collective-permute-start(bf16[640,256]{1,0:T(8,128)(2,1)S(1)} %collective-permute-done.5), channel_id=1, source_target_pairs={{2,0},{3,1},{4,6},{5,7},{10,8},{11,9},{12,14},{13,15},{18,16},{19,... | collective-permute-start | bytes 983048 | tf_op jit(solution)/shard_map/ppermute | solution.py:404
  42.7 15.7 %collective-permute-start.10 = (bf16[640,256]{1,0:T(8,128)(2,1)S(1)}, bf16[640,256]{1,0:T(8,128)(2,1)S(1)}, u32[]{:S(2)}, u32[]{:S(2)}) collective-permute-start(bf16[640,256]{1,0:T(8,128)(2,1)S(1)} %constant_dynamic-slice_fusion.refs_6_), channel_id=1, source_target_pairs={{0,8},{8,0},{1,9},{9,1},{2,10},{10,2},{3,11},{11,3},{4,12},{12,4},... | collective-permute-start | bytes 983048 | tf_op jit(solution)/shard_map/ppermute | solution.py:335
  42.8 0.7 copy-start.13
  43.6 16.3 %collective-permute-start.11 = (bf16[640,256]{1,0:T(8,128)(2,1)}, bf16[640,256]{1,0:T(8,128)(2,1)}, u32[]{:S(2)}, u32[]{:S(2)}) collective-permute-start(bf16[640,256]{1,0:T(8,128)(2,1)} %collective-permute-done.refs_7_), channel_id=1, source_target_pairs={{0,8},{8,0},{1,9},{9,1},{2,10},{10,2},{3,11},{11,3},{4,12},{12,4},... | collective-permute-start | bytes 983048 | tf_op jit(solution)/shard_map/ppermute | solution.py:335
  44.0 0.6 copy-start.4
  54.2 4.3 %copy-start.14 = (bf16[2,128,640]{2,1,0:T(8,128)(2,1)}, bf16[2,128,640]{2,1,0:T(8,128)(2,1)S(1)}, u32[]{:S(2)}) copy-start(bf16[2,128,640]{2,1,0:T(8,128)(2,1)S(1)} %collective-permute-done.8.refs_4_) | copy-start | bytes 983044
  56.7 1.8 %copy-start.15 = (bf16[2,128,640]{2,1,0:T(8,128)(2,1)}, bf16[2,128,640]{2,1,0:T(8,128)(2,1)S(1)}, u32[]{:S(2)}) copy-start(bf16[2,128,640]{2,1,0:T(8,128)(2,1)S(1)} %collective-permute-done.9.refs_5_) | copy-start | bytes 983044
  58.4 0.7 copy-start.9
  59.2 0.7 copy-start.16
  59.9 1.0 %copy-start.7 = (bf16[128,1024]{1,0:T(8,128)(2,1)S(1)}, bf16[128,1024]{1,0:T(8,128)(2,1)}, u32[]{:S(2)}) copy-start(bf16[128,1024]{1,0:T(8,128)(2,1)} %g_ref.1) | copy-start | bytes 786436
  63.8 24.4 %all-to-all-start.2 = ((bf16[8,384,128]{2,1,0:T(8,128)(2,1)}), bf16[8,384,128]{2,1,0:T(8,128)(2,1)S(1)}, u32[]{:S(2)}, u32[]{:S(2)}) async-start(bf16[8,384,128]{2,1,0:T(8,128)(2,1)} %get-tuple-element.74.refs_14_), calls=%async_computation.2 | async-start | bytes 1572864 | tf_op jit(solution)/shard_map/all_to_all | solution.py:447
  69.2 1.7 %copy-start.10 = (bf16[640,256]{1,0:T(8,128)(2,1)}, bf16[640,256]{1,0:T(8,128)(2,1)S(1)}, u32[]{:S(2)}) copy-start(bf16[640,256]{1,0:T(8,128)(2,1)S(1)} %broadcast_select_fusion.refs_9_) | copy-start | bytes 983044
  69.2 19.1 %copy-start.5 = (s32[8]{0:T(128)S(1)}, s32[8]{0:T(128)}, u32[]{:S(2)}) copy-start(s32[8]{0:T(128)} %get-tuple-element.72.after_ref.rows_here) | copy-start | bytes 100
  69.2 1.7 %collective-permute-start.13 = (bf16[640,256]{1,0:T(8,128)(2,1)S(1)}, bf16[640,256]{1,0:T(8,128)(2,1)S(1)}, u32[]{:S(2)}, u32[]{:S(2)}) collective-permute-start(bf16[640,256]{1,0:T(8,128)(2,1)S(1)} %broadcast_select_fusion.refs_9_), channel_id=1, source_target_pairs={{0,8},{8,0},{1,9},{9,1},{2,10},{10,2},{3,11},{11,3},{4,12},{12,4},... | collective-permute-start | bytes 983048 | tf_op jit(solution)/shard_map/ppermute | solution.py:335
  70.9 0.7 copy-start.17
  76.6 8.5 %collective-permute-start.14 = (bf16[128,512]{1,0:T(8,128)(2,1)}, bf16[128,512]{1,0:T(8,128)(2,1)S(1)}, u32[]{:S(2)}, u32[]{:S(2)}) collective-permute-start(bf16[128,512]{1,0:T(8,128)(2,1)} %get-tuple-element.81), channel_id=1, source_target_pairs={{0,1},{1,0},{2,3},{3,2},{4,5},{5,4},{6,7},{7,6},{8,9},{9,8},{10,11... | collective-permute-start | bytes 393224 | tf_op jit(solution)/shard_map/ppermute | solution.py:332
  78.7 6.4 %collective-permute-start.15 = (bf16[128,512]{1,0:T(8,128)(2,1)}, bf16[128,512]{1,0:T(8,128)(2,1)S(1)}, u32[]{:S(2)}, u32[]{:S(2)}) collective-permute-start(bf16[128,512]{1,0:T(8,128)(2,1)} %get-tuple-element.82), channel_id=1, source_target_pairs={{0,16},{16,0},{1,17},{17,1},{2,18},{18,2},{3,19},{19,3},{4,20},{20... | collective-permute-start | bytes 393224 | tf_op jit(solution)/shard_map/ppermute | solution.py:338
  79.2 8.4 %collective-permute-start.16 = (bf16[128,512]{1,0:T(8,128)(2,1)}, bf16[128,512]{1,0:T(8,128)(2,1)S(1)}, u32[]{:S(2)}, u32[]{:S(2)}) collective-permute-start(bf16[128,512]{1,0:T(8,128)(2,1)} %get-tuple-element.83), channel_id=1, source_target_pairs={{0,17},{1,16},{2,19},{3,18},{4,21},{5,20},{6,23},{7,22},{16,1},{17... | collective-permute-start | bytes 393224 | tf_op jit(solution)/shard_map/ppermute | solution.py:448
  88.3 2.4 %collective-permute-start.18 = (bf16[8,384,128]{2,1,0:T(8,128)(2,1)S(1)}, bf16[8,384,128]{2,1,0:T(8,128)(2,1)S(1)}, u32[]{:S(2)}, u32[]{:S(2)}) collective-permute-start(bf16[8,384,128]{2,1,0:T(8,128)(2,1)S(1)} %all-to-all-done.2.rest_0_), channel_id=1, source_target_pairs={{0,8},{8,0},{1,9},{9,1},{2,10},{10,2},{3,11},{11,3},{4,12},{12,4},... | collective-permute-start | bytes 2359304 | tf_op jit(solution)/shard_map/ppermute | solution.py:335
  88.3 2.3 %collective-permute-start.17 = (s32[8]{0:T(128)S(1)}, s32[8]{0:T(128)S(1)}, u32[]{:S(2)}, u32[]{:S(2)}) collective-permute-start(s32[8]{0:T(128)S(1)} %copy-done.5), channel_id=1, source_target_pairs={{0,8},{8,0},{1,9},{9,1},{2,10},{10,2},{3,11},{11,3},{4,12},{12,4},... | collective-permute-start | bytes 104 | tf_op jit(solution)/shard_map/ppermute | solution.py:335
  90.6 3.1 %copy-start.1 = (bf16[640,512]{1,0:T(8,128)(2,1)S(1)}, bf16[640,512]{1,0:T(8,128)(2,1)}, u32[]{:S(2)}) copy-start(bf16[640,512]{1,0:T(8,128)(2,1)} %param.9) | copy-start | bytes 1966084

commit v15 on v14

--- a/solution.py
+++ b/solution.py
@@ -131,7 +131,7 @@
         copy.wait()
 
 
-def gather_kernel(asked, down_ref, up_ref, out_ref, rows_ref, down_buf, up_buf, flat, built, sems):
+def gather_kernel(asked, down_ref, up_ref, out_ref, rows_ref, down_buf, up_buf, flats, built, sems):
     count, down_chunks, up_chunks = down_buf.shape[0], down_buf.shape[1], up_buf.shape[1]
     across = up_chunks // 8
 
@@ -149,7 +149,7 @@
         up.start()
         rows_ref[t] = asked[t, 0, 0]
 
-    def one(t, carry):
+    def one(t, flat):
         down, up, leave = copies(t)
         up.wait()
         for j in range(up_chunks):
@@ -161,9 +161,13 @@
         sub = asked[t, 0, 0] % TILE_ROWS
         built[t] = flat[pl.ds(sub, down_chunks + up_chunks, stride=8), :].astype(jnp.bfloat16)
         leave.start()
+
+    def two(i, carry):
+        for u in range(2):
+            one(2 * i + u, flats.at[u])
         return carry
 
-    lax.fori_loop(0, count, one, 0)
+    lax.fori_loop(0, count // 2, two, 0)
     for t in range(count):
         copies(t)[2].wait()
 
@@ -284,27 +288,37 @@
     outer, rows, depth = whole[0].shape
     width, each = w_from[0].shape[1], outer // 2
     z = lax.axis_index("tensor") // 2
+    inside = (z == 1) | (z == 2)
     order = [z, z ^ 1, jnp.where(z < 2, 2, 1), jnp.where(z < 2, 3, 0)]
+    pieces = len(w_from) // 2
 
     def fetch(k, begin):
         columns = pl.ds(k * depth, depth)
-        copies = [
-            pltpu.make_async_copy(ref.at[order[k]], x_buf.at[pl.ds(b * rows, rows), columns], sems.at[k, b])
-            for b, ref in enumerate(whole)
-        ] + [
-            pltpu.make_async_copy(w_from[h * outer + k], w_buf.at[columns, pl.ds(h * width, width)], sems.at[k, 4 + h])
-            for h in range(2)
-        ]
-        for copy in copies:
+
+        def move(source, place, sem):
+            copy = pltpu.make_async_copy(source, place, sem)
             copy.start() if begin else copy.wait()
-        for b in range(2):
+
+        for b, ref in enumerate(whole):
+            move(ref.at[order[k]], x_buf.at[pl.ds(b * rows, rows), columns], sems.at[k, b])
             for h in range(2):
                 @pl.when(order[k] // each == h)
                 def _():
-                    source = halves[2 * b + h].at[order[k] % each]
                     place = x_buf.at[pl.ds((2 + b) * rows, rows), columns]
-                    copy = pltpu.make_async_copy(source, place, sems.at[k, 2 + b])
-                    copy.start() if begin else copy.wait()
+                    move(halves[2 * b + h].at[order[k] % each], place, sems.at[k, 2 + b])
+        for h in range(2):
+            place, sem = w_buf.at[columns, pl.ds(h * width, width)], sems.at[k, 4 + h]
+            if k < 2:
+                move(w_from[h * pieces + k], place, sem)
+                continue
+
+            @pl.when(inside)
+            def _():
+                move(w_from[h * pieces + 2 * k - 2], place, sem)
+
+            @pl.when(jnp.logical_not(inside))
+            def _():
+                move(w_from[h * pieces + 2 * k - 1], place, sem)
 
     for k in range(outer):
         fetch(k, True)
@@ -371,6 +385,7 @@
     over = lax.ppermute(half, "tensor", middle)
     near, over, asked, x_theirs, xs = lax.optimization_barrier((near, over, asked, x_theirs, xs))
     x_far.append(exchange(x_theirs[1], 1))
+    y_far = [other_part(x_far[0])]
     over_near = lax.ppermute(near, "tensor", middle)
     passed = lax.ppermute(over, "tensor", ends)
     pieces = jax.ShapeDtypeStruct((group, down_chunks + up_chunks, LANES), jnp.bfloat16)
@@ -386,7 +401,7 @@
         scratch_shapes=[
             pltpu.VMEM((group, down_chunks, TILE_ROWS, LANES), jnp.bfloat16),
             pltpu.VMEM((group, up_chunks, TILE_ROWS, LANES), jnp.bfloat16),
-            pltpu.VMEM(((down_chunks + up_chunks) * 8, LANES), jnp.float32),
+            pltpu.VMEM((2, (down_chunks + up_chunks) * 8, LANES), jnp.float32),
             pltpu.VMEM(pieces.shape, jnp.bfloat16),
             pltpu.SemaphoreType.DMA((3, group)),
         ],
@@ -394,16 +409,16 @@
         cost_estimate=cost(read=40 << 20),
         name="pick_panels",
     )(asked, tiles(down_store), tiles(up_store))
-    sent, rows, x_far, y_mine, half, near, over, over_near, passed = lax.optimization_barrier(
-        (sent, rows, x_far, y_mine, half, near, over, over_near, passed)
+    sent, rows, x_far, y_far, y_mine, half, near, over, over_near, passed = lax.optimization_barrier(
+        (sent, rows, x_far, y_far, y_mine, half, near, over, over_near, passed)
     )
     panels = lax.all_to_all(sent, "tensor", 0, 0)
     rows_core = other_core(rows)
-    y_far = [other_part(part_of) for part_of in x_far]
-    inside = (z == 1) | (z == 2)
+    y_far.append(other_part(x_far[1]))
     passed_near = lax.ppermute(over_near, "tensor", ends)
-    quarter = [half, near, jnp.where(inside, over, passed)]
+    quarter = [half, near, over, passed, over_near]
     quarter_core = [other_core(w) for w in quarter]
+
     owned_groups = ADAPTERS // lax.axis_size("dp") // 8
     down_shape = jax.ShapeDtypeStruct((owned_groups, down_chunks, 8, 1, LANES), jnp.float32)
     up_shape = jax.ShapeDtypeStruct((owned_groups, up_chunks, 8, 1, LANES), jnp.float32)
@@ -426,13 +441,12 @@
         name="adapter",
     )(xs, cotangent, panels, cleared)
     _, passed_near = lax.optimization_barrier((terms, passed_near))
-    last = jnp.where(inside, over_near, passed_near)
-    quarters = quarter + [last] + quarter_core + [other_core(last)]
+    quarters = quarter + [passed_near] + quarter_core + [other_core(passed_near)]
     sums = [jax.ShapeDtypeStruct((token_rows, parts * width), kind) for kind in (jnp.float32,) + (jnp.bfloat16,) * 3]
     own, to_part, to_inner, to_both = pl.pallas_call(
         base_kernel,
         out_shape=sums,
-        in_specs=[ANY] * (7 + 2 * outer),
+        in_specs=[ANY] * (7 + len(quarters)),
         out_specs=[VMEM] * 4,
         scratch_shapes=[
             pltpu.VMEM((4 * token_rows, outer * slice_width), jnp.bfloat16),

time: 94.6 us -> 99 us (1.047)
  waiting for transfers between devices: 18.6 us -> 22.3 us
  other arithmetic: 3.84 us -> 1.81 us
  starting transfers between devices: 32.8 us -> 34.7 us
    ppermute x4, waiting for transfers between devices: 2.52 us -> 7.8 us  [other_part(): lax.ppermute(value, 'parts', [(a, parts - 1 - a) for a in range(parts)])]
    ppermute x1, waiting for transfers between devices: 2.82 us -> 0.28 us  [fast_body(): passed = lax.ppermute(over, 'tensor', ends)]
    select_n x2 -> x0, other arithmetic: 2.02 us -> none  [the longest x1 1.01 us: fast_body(): quarter = [half, near, jnp.where(inside, over, passed)]]
    all_to_all x1, starting transfers between devices: 4.35 us -> 6.31 us  [fast_body(): back = lax.all_to_all(terms, 'tensor', 0, 0)]
    all_to_all x1, waiting for transfers between devices: 0.51 us -> 2.45 us  [fast_body(): asked = lax.all_to_all(row, 'tensor', 0, 0)]
    ppermute x4, waiting for transfers between devices: 6.18 us -> 4.35 us  [exchange(): return lax.ppermute(value, 'tensor', [(t, t ^ s) for t in range(group)])]
    ppermute x1, waiting for transfers between devices: 2.46 us -> 3.98 us  [fast_body(): lax.ppermute(to_both, ('parts', 'tensor'), opposite)]
    ppermute x1, starting transfers between devices: 1.03 us -> 0.03 us  [fast_body(): lax.ppermute(to_both, ('parts', 'tensor'), opposite)]
  transfers between devices with their start and end apart: 22 -> 24, of which waited for: 9 -> 9; matrix products, arithmetic and copies ran while one was open for 4% -> 2% of each run, Pallas kernels for 25% -> 24%
where the time goes in v15:
time: 99 us; the launch traced here: 98.2 us
  starting transfers between devices  34.7 us (35%)
  Pallas kernels  31.1 us (31%)
  waiting for transfers between devices  22.3 us (23%)
  local copies, waits for them, and re-layouts  6.69 us (7%)
  other arithmetic  1.81 us (2%)
  between operations  1.65 us (2%)
    ppermute x4, starting transfers between devices, exchange(): return lax.ppermute(value, 'tensor', [(t, t ^ s) for t in range(group)])  10.1 us
    pallas_call x1, Pallas kernels, fast_body(): pl.pallas_call(zero_kernel, out_shape=(down_shape, up_shape, token), in_s...  9.48 us
    ppermute x4, waiting for transfers between devices, other_part(): lax.ppermute(value, 'parts', [(a, parts - 1 - a) for a in range(parts)])  7.8 us
    unnamed x40, local copies, waits for them, and re-layouts  6.67 us
    all_to_all x1, starting transfers between devices, fast_body(): back = lax.all_to_all(terms, 'tensor', 0, 0)  6.31 us
    pallas_call x1, Pallas kernels, fast_body(): pl.pallas_call(gather_kernel, out_shape=(pieces, jax.ShapeDtypeStruct((gr...  5.25 us
    ppermute x4, starting transfers between devices, other_part(): lax.ppermute(value, 'parts', [(a, parts - 1 - a) for a in range(parts)])  5.16 us
    pallas_call x1, Pallas kernels, fast_body(): pl.pallas_call(base_kernel, out_shape=sums, in_specs=[ANY] * (7 + len(qua...  5.03 us
  transfers between devices with their start and end apart: 24, of which 9 were waited for; matrix products, arithmetic and copies ran while one was open for 2% of the time, Pallas kernels for 24%

profile of v15, /device:TPU:0, one launch (start us, length us, event | category | flops | bytes accessed | tf_op | source)
XLA Modules:
  0.0 98.2 jit_solution(5581489748837231897)
XLA Ops:
  0.6 0.0 copy-start
  1.4 1.3 %own_row.1 = s32[8,1,128]{2,1,0:T(1,128)} custom-call(s32[1]{0:T(128)S(6)} %copy.14.block_ref, s32[256]{0:T(256)} %slot_ref.1), custom_call_target="tpu_custom_call" | custom-call | tf_op jit(solution)/shard_map/own_row/pallas_call | solution.py:354
  2.7 0.7 collective-permute-start.1
  3.4 5.9 %collective-permute-start = (bf16[640,256]{1,0:T(8,128)(2,1)S(1)}, bf16[640,256]{1,0:T(8,128)(2,1)}, u32[]{:S(2)}, u32[]{:S(2)}) collective-permute-start(bf16[640,256]{1,0:T(8,128)(2,1)S(1)} %constant_dynamic-slice_fusion.refs_6_), channel_id=1, source_target_pairs={{0,2},{1,3},{2,0},{3,1},{4,6},{5,7},{6,4},{7,5},{8,10},{9,11},{10,... | collective-permute-start | bytes 983048 | tf_op jit(solution)/shard_map/ppermute | solution.py:346
  9.3 1.3 %copy-done.2 = bf16[128,5120]{1,0:T(8,128)(2,1)S(1)} copy-done((bf16[128,5120]{1,0:T(8,128)(2,1)S(1)}, bf16[128,5120]{1,0:T(8,128)(2,1)}, u32[]{:S(2)}) %copy-start.2) | copy-done | bytes 1310744
  10.6 0.1 split_tokens.1
  10.7 1.6 %collective-permute-start.2 = (bf16[2,128,640]{2,1,0:T(8,128)(2,1)S(1)}, bf16[2,128,640]{2,1,0:T(8,128)(2,1)}, u32[]{:S(2)}, u32[]{:S(2)}) collective-permute-start(bf16[2,128,640]{2,1,0:T(8,128)(2,1)S(1)} %get-tuple-element.54), channel_id=1, source_target_pairs={{0,1},{1,0},{2,3},{3,2},{4,5},{5,4},{6,7},{7,6},{8,9},{9,8},{10,11... | collective-permute-start | bytes 983048 | tf_op jit(solution)/shard_map/ppermute | solution.py:346
  12.3 1.5 %collective-permute-start.5 = (bf16[4,128,640]{2,1,0:T(8,128)(2,1)S(1)}, bf16[4,128,640]{2,1,0:T(8,128)(2,1)}, u32[]{:S(2)}, u32[]{:S(2)}) collective-permute-start(bf16[4,128,640]{2,1,0:T(8,128)(2,1)S(1)} %get-tuple-element.52.refs_0_), channel_id=1, source_target_pairs={{0,16},{16,0},{1,17},{17,1},{2,18},{18,2},{3,19},{19,3},{4,20},{20... | collective-permute-start | bytes 1966088 | tf_op jit(solution)/shard_map/ppermute | solution.py:352
  13.8 3.3 %all-to-all-start = ((s32[8,1,128]{2,1,0:T(1,128)}), s32[8,1,128]{2,1,0:T(1,128)S(1)}, u32[]{:S(2)}, u32[]{:S(2)}) async-start(s32[8,1,128]{2,1,0:T(1,128)} %own_row.1), calls=%async_computation | async-start | bytes 8192 | tf_op jit(solution)/shard_map/all_to_all | solution.py:358
  17.1 3.9 %pair_columns.1.xs_ref = bf16[8,256,320]{2,1,0:T(8,128)(2,1)} custom-call(bf16[128,5120]{1,0:T(8,128)(2,1)} %x_ref.1), custom_call_target="tpu_custom_call" | custom-call | bytes 134217728 | tf_op jit(solution)/shard_map/pair_columns/pallas_call | solution.py:372
  21.0 2.4 %all-to-all-done.asked = s32[8,1,128]{2,1,0:T(1,128)S(1)} async-done(((s32[8,1,128]{2,1,0:T(1,128)}), s32[8,1,128]{2,1,0:T(1,128)S(1)}, u32[]{:S(2)}, u32[]{:S(2)}) %all-to-all-start) | async-done | bytes 4128 | tf_op jit(solution)/shard_map/all_to_all | solution.py:358
  23.4 0.0 collective-permute-done.1.refs_8_
  23.4 0.0 collective-permute-done.refs_7_
  23.4 0.6 collective-permute-start.3
  24.1 0.0 collective-permute-done.2.refs_2_
  24.1 0.5 collective-permute-start.4
  24.6 1.4 %collective-permute-start.6 = (bf16[640,256]{1,0:T(8,128)(2,1)}, bf16[640,256]{1,0:T(8,128)(2,1)}, u32[]{:S(2)}, u32[]{:S(2)}) collective-permute-start(bf16[640,256]{1,0:T(8,128)(2,1)} %collective-permute-done.refs_7_), channel_id=1, source_target_pairs={{2,4},{3,5},{4,2},{5,3},{10,12},{11,13},{12,10},{13,11},{18,20},{1... | collective-permute-start | bytes 983048 | tf_op jit(solution)/shard_map/ppermute | solution.py:389
  26.0 1.3 %collective-permute-start.7 = (bf16[640,256]{1,0:T(8,128)(2,1)S(1)}, bf16[640,256]{1,0:T(8,128)(2,1)}, u32[]{:S(2)}, u32[]{:S(2)}) collective-permute-start(bf16[640,256]{1,0:T(8,128)(2,1)S(1)} %collective-permute-done.1.refs_8_), channel_id=1, source_target_pairs={{2,0},{3,1},{4,6},{5,7},{10,8},{11,9},{12,14},{13,15},{18,16},{19,... | collective-permute-start | bytes 983048 | tf_op jit(solution)/shard_map/ppermute | solution.py:390
  27.3 5.2 %pick_panels.1 = (bf16[8,384,128]{2,1,0:T(8,128)(2,1)}, s32[8]{0:T(128)}) custom-call(s32[8,1,128]{2,1,0:T(1,128)} %copy-done.9, bf16[32,320,8,128]{3,2,1,0:T(8,128)(2,1)} %bitcast.16, bf16[32,64,8,128]{3,2,1,0:T(8,128)(2,1)} %bitcast.18), custom_call_target="tpu_custom_call" | custom-call | bytes 41943040 | tf_op jit(solution)/shard_map/pick_panels/pallas_call | solution.py:396
  32.5 2.4 %collective-permute-done.4.refs_4_ = bf16[2,128,640]{2,1,0:T(8,128)(2,1)S(1)} collective-permute-done((bf16[2,128,640]{2,1,0:T(8,128)(2,1)}, bf16[2,128,640]{2,1,0:T(8,128)(2,1)S(1)}, u32[]{:S(2)}, u32[]{:S(2)}) %collective-permute-start.4) | collective-permute-done | bytes 327712 | tf_op jit(solution)/shard_map/ppermute | solution.py:352
  34.9 0.0 collective-permute-done.5.refs_1_
  34.9 0.0 collective-permute-done.6.refs_10_
  34.9 0.3 collective-permute-done.7.refs_9_
  35.2 0.5 copy-done.11
  35.7 0.1 copy-done.12
  35.8 3.5 %all-to-all-start.1 = ((bf16[8,384,128]{2,1,0:T(8,128)(2,1)}), bf16[8,384,128]{2,1,0:T(8,128)(2,1)S(1)}, u32[]{:S(2)}, u32[]{:S(2)}) async-start(bf16[8,384,128]{2,1,0:T(8,128)(2,1)} %get-tuple-element.65), calls=%async_computation.1 | async-start | bytes 1572864 | tf_op jit(solution)/shard_map/all_to_all | solution.py:415
  39.3 1.6 %collective-permute-start.9 = (bf16[2,128,640]{2,1,0:T(8,128)(2,1)}, bf16[2,128,640]{2,1,0:T(8,128)(2,1)S(1)}, u32[]{:S(2)}, u32[]{:S(2)}) collective-permute-start(bf16[2,128,640]{2,1,0:T(8,128)(2,1)} %copy-done.11), channel_id=1, source_target_pairs={{0,16},{16,0},{1,17},{17,1},{2,18},{18,2},{3,19},{19,3},{4,20},{20... | collective-permute-start | bytes 983048 | tf_op jit(solution)/shard_map/ppermute | solution.py:352
  40.9 0.5 collective-permute-start.11
  41.4 0.0 collective-permute-start.12
  41.5 0.5 collective-permute-start.13
  42.0 5.4 %collective-permute-done.9.refs_5_ = bf16[2,128,640]{2,1,0:T(8,128)(2,1)S(1)} collective-permute-done((bf16[2,128,640]{2,1,0:T(8,128)(2,1)}, bf16[2,128,640]{2,1,0:T(8,128)(2,1)S(1)}, u32[]{:S(2)}, u32[]{:S(2)}) %collective-permute-start.9) | collective-permute-done | bytes 327712 | tf_op jit(solution)/shard_map/ppermute | solution.py:352
  47.4 0.0 collective-permute-start.14
  47.4 0.0 collective-permute-done.10.refs_12_
  47.4 0.7 copy-done.13
  48.1 1.3 %collective-permute-start.8 = (bf16[640,256]{1,0:T(8,128)(2,1)}, bf16[640,256]{1,0:T(8,128)(2,1)}, u32[]{:S(2)}, u32[]{:S(2)}) collective-permute-start(bf16[640,256]{1,0:T(8,128)(2,1)} %collective-permute-done.6.refs_10_), channel_id=1, source_target_pairs={{2,0},{3,1},{4,6},{5,7},{10,8},{11,9},{12,14},{13,15},{18,16},{19,... | collective-permute-start | bytes 983048 | tf_op jit(solution)/shard_map/ppermute | solution.py:418
  49.4 0.7 copy-done.4
  50.1 9.5 %clear_rows.1 = (f32[16,320,8,1,128]{4,3,2,1,0:T(1,128)}, f32[16,64,8,1,128]{4,3,2,1,0:T(1,128)}, s32[1]{0:T(128)}) custom-call(s32[8]{0:T(128)S(1)} %copy-done.4), custom_call_target="tpu_custom_call" | custom-call | bytes 29360128 | tf_op jit(solution)/shard_map/clear_rows/pallas_call | solution.py:425
  59.6 0.0 collective-permute-done.11.refs_13_
  59.6 0.0 collective-permute-done.12.refs_14_
  59.6 0.0 collective-permute-done.14.refs_16_
  59.6 0.7 copy-done.15
  60.3 0.2 copy-done.16
  60.5 0.1 copy-done.17
  60.6 0.8 copy-done.18
  61.3 1.2 %collective-permute-done.8.refs_11_ = bf16[640,256]{1,0:T(8,128)(2,1)} collective-permute-done((bf16[640,256]{1,0:T(8,128)(2,1)}, bf16[640,256]{1,0:T(8,128)(2,1)}, u32[]{:S(2)}, u32[]{:S(2)}) %collective-permute-start.8) | collective-permute-done | bytes 327712 | tf_op jit(solution)/shard_map/ppermute | solution.py:418
  62.6 0.0 all-to-all-done.1.pieces
  62.6 0.0 copy-start.7
  62.6 0.9 copy-done.7
  63.5 3.0 %adapter.1 = (bf16[8,384,128]{2,1,0:T(8,128)(2,1)}, f32[128,1024]{1,0:T(8,128)S(1)}) custom-call(bf16[8,256,320]{2,1,0:T(8,128)(2,1)S(1)} %copy-done.3, bf16[128,1024]{1,0:T(8,128)(2,1)S(1)} %copy-done.7, bf16[8,384,128]{2,1,0:T(8,128)(2,1)S(1)} %all-to-all-done.1.pieces, s32[1]{0:T(128)} %get-tuple-element.77._), custom_call_target="tpu_custom_call" | custom-call | flops 3221225472 | bytes 8388608 | tf_op jit(solution)/shard_map/adapter/pallas_call | solution.py:433
  66.5 6.3 %all-to-all-start.2 = ((bf16[8,384,128]{2,1,0:T(8,128)(2,1)}), bf16[8,384,128]{2,1,0:T(8,128)(2,1)S(1)}, u32[]{:S(2)}, u32[]{:S(2)}) async-start(bf16[8,384,128]{2,1,0:T(8,128)(2,1)} %get-tuple-element.78.refs_18_), calls=%async_computation.2 | async-start | bytes 1572864 | tf_op jit(solution)/shard_map/all_to_all | solution.py:461
  72.8 0.1 collective-permute-start.15
  72.9 1.8 %collective-permute-done.15.refs_17_ = bf16[640,256]{1,0:T(8,128)(2,1)S(1)} collective-permute-done((bf16[640,256]{1,0:T(8,128)(2,1)}, bf16[640,256]{1,0:T(8,128)(2,1)S(1)}, u32[]{:S(2)}, u32[]{:S(2)}) %collective-permute-start.15) | collective-permute-done | bytes 327712 | tf_op jit(solution)/shard_map/ppermute | solution.py:349
  74.7 0.7 copy-done.19
  75.4 5.0 %frozen_part.1 = (f32[128,512]{1,0:T(8,128)}, bf16[128,512]{1,0:T(8,128)(2,1)}, bf16[128,512]{1,0:T(8,128)(2,1)}, bf16[128,512]{1,0:T(8,128)(2,1)}) custom-call(bf16[4,128,640]{2,1,0:T(8,128)(2,1)} %copy-done.6, bf16[4,128,640]{2,1,0:T(8,128)(2,1)} %collective-permute-done.5.refs_1_, bf16[2,128,640]{2,1,0:T(8,128)(2,1)} %collective-permute-done.2.refs_2_, ...), custom_call_target="tpu_custom_call" | custom-call | flops 4294967296 | bytes 8388608 | tf_op jit(solution)/shard_map/frozen_part/pallas_call | solution.py:446
  80.5 2.0 %collective-permute-start.16 = (bf16[128,512]{1,0:T(8,128)(2,1)}, bf16[128,512]{1,0:T(8,128)(2,1)S(1)}, u32[]{:S(2)}, u32[]{:S(2)}) collective-permute-start(bf16[128,512]{1,0:T(8,128)(2,1)} %get-tuple-element.87), channel_id=1, source_target_pairs={{0,1},{1,0},{2,3},{3,2},{4,5},{5,4},{6,7},{7,6},{8,9},{9,8},{10,11... | collective-permute-start | bytes 393224 | tf_op jit(solution)/shard_map/ppermute | solution.py:346
  82.5 1.5 %collective-permute-start.17 = (bf16[128,512]{1,0:T(8,128)(2,1)}, bf16[128,512]{1,0:T(8,128)(2,1)S(1)}, u32[]{:S(2)}, u32[]{:S(2)}) collective-permute-start(bf16[128,512]{1,0:T(8,128)(2,1)} %get-tuple-element.88), channel_id=1, source_target_pairs={{0,16},{16,0},{1,17},{17,1},{2,18},{18,2},{3,19},{19,3},{4,20},{20... | collective-permute-start | bytes 393224 | tf_op jit(solution)/shard_map/ppermute | solution.py:352
  84.0 0.0 collective-permute-start.18
  84.0 4.3 %collective-permute-done.16 = bf16[128,512]{1,0:T(8,128)(2,1)S(1)} collective-permute-done((bf16[128,512]{1,0:T(8,128)(2,1)}, bf16[128,512]{1,0:T(8,128)(2,1)S(1)}, u32[]{:S(2)}, u32[]{:S(2)}) %collective-permute-start.16) | collective-permute-done | bytes 131104 | tf_op jit(solution)/shard_map/ppermute | solution.py:346
  88.4 4.0 %collective-permute-done.18 = bf16[128,512]{1,0:T(8,128)(2,1)S(1)} collective-permute-done((bf16[128,512]{1,0:T(8,128)(2,1)}, bf16[128,512]{1,0:T(8,128)(2,1)S(1)}, u32[]{:S(2)}, u32[]{:S(2)}) %collective-permute-start.18) | collective-permute-done | bytes 131104 | tf_op jit(solution)/shard_map/ppermute | solution.py:462
  92.4 0.3 all-to-all-done.2.rest_0_
  92.7 0.5 collective-permute-start.19
  93.2 1.0 %convert_add_fusion = (f32[128,512]{1,0:T(8,128)S(1)}, f32[128,512]{1,0:T(8,128)S(1)}) fusion(bf16[128,512]{1,0:T(8,128)(2,1)S(1)} %collective-permute-done.18, bf16[128,512]{1,0:T(8,128)(2,1)S(1)} %collective-permute-done.17, f32[128,512]{1,0:T(8,128)} %get-tuple-element.86, bf16[128,512]{1,0:T(8,128)(2,1)S(1)} %collective-permute-done.16), kind=kLoop, calls=%fused_computation.2 | loop fusion | flops 327680 | bytes 1179648 | tf_op jit(solution)/shard_map/add | solution.py:488
  94.3 0.8 fusion
  95.1 3.1 %place_rows.1 = (f32[16,320,8,1,128]{4,3,2,1,0:T(1,128)}, f32[16,64,8,1,128]{4,3,2,1,0:T(1,128)}) custom-call(s32[8]{0:T(128)S(1)} %copy-done.5, s32[8]{0:T(128)S(1)} %collective-permute-done.19.rows_core, bf16[8,384,128]{2,1,0:T(8,128)(2,1)S(1)} %all-to-all-done.2.rest_0_, ...), custom_call_target="tpu_custom_call", output_to_operand_aliasing={{0}: (4, {}), {1}: (5, {})} | custom-call | bytes 16777216 | tf_op jit(solution)/shard_map/place_rows/pallas_call | solution.py:466
  (36 shorter events, 0.1 us)
Async XLA Ops:
  0.6 2.0 %copy-start = (bf16[640,512]{1,0:T(8,128)(2,1)S(1)}, bf16[640,512]{1,0:T(8,128)(2,1)}, u32[]{:S(2)}) copy-start(bf16[640,512]{1,0:T(8,128)(2,1)} %param.9) | copy-start | bytes 1966084
  2.7 38.3 %copy-start.8 = (bf16[640,256]{1,0:T(8,128)(2,1)}, bf16[640,256]{1,0:T(8,128)(2,1)S(1)}, u32[]{:S(2)}) copy-start(bf16[640,256]{1,0:T(8,128)(2,1)S(1)} %constant_dynamic-slice_fusion.refs_6_) | copy-start | bytes 983044
  2.7 20.7 %collective-permute-start.1 = (bf16[640,256]{1,0:T(8,128)(2,1)S(1)}, bf16[640,256]{1,0:T(8,128)(2,1)S(1)}, u32[]{:S(2)}, u32[]{:S(2)}) collective-permute-start(bf16[640,256]{1,0:T(8,128)(2,1)S(1)} %constant_dynamic-slice_fusion.refs_6_), channel_id=1, source_target_pairs={{2,4},{3,5},{4,2},{5,3},{10,12},{11,13},{12,10},{13,11},{18,20},{1... | collective-permute-start | bytes 983048 | tf_op jit(solution)/shard_map/ppermute | solution.py:385
  3.4 20.1 %collective-permute-start = (bf16[640,256]{1,0:T(8,128)(2,1)S(1)}, bf16[640,256]{1,0:T(8,128)(2,1)}, u32[]{:S(2)}, u32[]{:S(2)}) collective-permute-start(bf16[640,256]{1,0:T(8,128)(2,1)S(1)} %constant_dynamic-slice_fusion.refs_6_), channel_id=1, source_target_pairs={{0,2},{1,3},{2,0},{3,1},{4,6},{5,7},{6,4},{7,5},{8,10},{9,11},{10,... | collective-permute-start | bytes 983048 | tf_op jit(solution)/shard_map/ppermute | solution.py:346
  9.3 1.3 %copy-start.2 = (bf16[128,5120]{1,0:T(8,128)(2,1)S(1)}, bf16[128,5120]{1,0:T(8,128)(2,1)}, u32[]{:S(2)}) copy-start(bf16[128,5120]{1,0:T(8,128)(2,1)} %x_ref.1) | copy-start | bytes 3932164
  10.7 21.8 %copy-start.6 = (bf16[4,128,640]{2,1,0:T(8,128)(2,1)}, bf16[4,128,640]{2,1,0:T(8,128)(2,1)S(1)}, u32[]{:S(2)}) copy-start(bf16[4,128,640]{2,1,0:T(8,128)(2,1)S(1)} %get-tuple-element.52.refs_0_) | copy-start | bytes 1966084
  10.7 13.4 %collective-permute-start.2 = (bf16[2,128,640]{2,1,0:T(8,128)(2,1)S(1)}, bf16[2,128,640]{2,1,0:T(8,128)(2,1)}, u32[]{:S(2)}, u32[]{:S(2)}) collective-permute-start(bf16[2,128,640]{2,1,0:T(8,128)(2,1)S(1)} %get-tuple-element.54), channel_id=1, source_target_pairs={{0,1},{1,0},{2,3},{3,2},{4,5},{5,4},{6,7},{7,6},{8,9},{9,8},{10,11... | collective-permute-start | bytes 983048 | tf_op jit(solution)/shard_map/ppermute | solution.py:346
  12.3 22.7 %collective-permute-start.5 = (bf16[4,128,640]{2,1,0:T(8,128)(2,1)S(1)}, bf16[4,128,640]{2,1,0:T(8,128)(2,1)}, u32[]{:S(2)}, u32[]{:S(2)}) collective-permute-start(bf16[4,128,640]{2,1,0:T(8,128)(2,1)S(1)} %get-tuple-element.52.refs_0_), channel_id=1, source_target_pairs={{0,16},{16,0},{1,17},{17,1},{2,18},{18,2},{3,19},{19,3},{4,20},{20... | collective-permute-start | bytes 1966088 | tf_op jit(solution)/shard_map/ppermute | solution.py:352
  13.8 9.6 %all-to-all-start = ((s32[8,1,128]{2,1,0:T(1,128)}), s32[8,1,128]{2,1,0:T(1,128)S(1)}, u32[]{:S(2)}, u32[]{:S(2)}) async-start(s32[8,1,128]{2,1,0:T(1,128)} %own_row.1), calls=%async_computation | async-start | bytes 8192 | tf_op jit(solution)/shard_map/all_to_all | solution.py:358
  23.4 3.8 %copy-start.9 = (s32[8,1,128]{2,1,0:T(1,128)}, s32[8,1,128]{2,1,0:T(1,128)S(1)}, u32[]{:S(2)}) copy-start(s32[8,1,128]{2,1,0:T(1,128)S(1)} %all-to-all-done.asked) | copy-start | bytes 12292
  23.4 9.1 %copy-start.10 = (bf16[640,256]{1,0:T(8,128)(2,1)}, bf16[640,256]{1,0:T(8,128)(2,1)S(1)}, u32[]{:S(2)}) copy-start(bf16[640,256]{1,0:T(8,128)(2,1)S(1)} %collective-permute-done.1.refs_8_) | copy-start | bytes 983044
  23.4 11.5 %collective-permute-start.3 = (bf16[2,128,640]{2,1,0:T(8,128)(2,1)S(1)}, bf16[2,128,640]{2,1,0:T(8,128)(2,1)S(1)}, u32[]{:S(2)}, u32[]{:S(2)}) collective-permute-start(bf16[2,128,640]{2,1,0:T(8,128)(2,1)S(1)} %get-tuple-element.59), channel_id=1, source_target_pairs={{0,1},{1,0},{2,3},{3,2},{4,5},{5,4},{6,7},{7,6},{8,9},{9,8},{10,11... | collective-permute-start | bytes 983048 | tf_op jit(solution)/shard_map/ppermute | solution.py:346
  24.1 10.9 %collective-permute-start.4 = (bf16[2,128,640]{2,1,0:T(8,128)(2,1)}, bf16[2,128,640]{2,1,0:T(8,128)(2,1)S(1)}, u32[]{:S(2)}, u32[]{:S(2)}) collective-permute-start(bf16[2,128,640]{2,1,0:T(8,128)(2,1)} %collective-permute-done.2.refs_2_), channel_id=1, source_target_pairs={{0,16},{16,0},{1,17},{17,1},{2,18},{18,2},{3,19},{19,3},{4,20},{20... | collective-permute-start | bytes 983048 | tf_op jit(solution)/shard_map/ppermute | solution.py:352
  24.6 10.4 %collective-permute-start.6 = (bf16[640,256]{1,0:T(8,128)(2,1)}, bf16[640,256]{1,0:T(8,128)(2,1)}, u32[]{:S(2)}, u32[]{:S(2)}) collective-permute-start(bf16[640,256]{1,0:T(8,128)(2,1)} %collective-permute-done.refs_7_), channel_id=1, source_target_pairs={{2,4},{3,5},{4,2},{5,3},{10,12},{11,13},{12,10},{13,11},{18,20},{1... | collective-permute-start | bytes 983048 | tf_op jit(solution)/shard_map/ppermute | solution.py:389
  26.0 9.3 %collective-permute-start.7 = (bf16[640,256]{1,0:T(8,128)(2,1)S(1)}, bf16[640,256]{1,0:T(8,128)(2,1)}, u32[]{:S(2)}, u32[]{:S(2)}) collective-permute-start(bf16[640,256]{1,0:T(8,128)(2,1)S(1)} %collective-permute-done.1.refs_8_), channel_id=1, source_target_pairs={{2,0},{3,1},{4,6},{5,7},{10,8},{11,9},{12,14},{13,15},{18,16},{19,... | collective-permute-start | bytes 983048 | tf_op jit(solution)/shard_map/ppermute | solution.py:390
  27.3 35.3 %copy-start.3 = (bf16[8,256,320]{2,1,0:T(8,128)(2,1)S(1)}, bf16[8,256,320]{2,1,0:T(8,128)(2,1)}, u32[]{:S(2)}) copy-start(bf16[8,256,320]{2,1,0:T(8,128)(2,1)} %pair_columns.1.xs_ref) | copy-start | bytes 3932164
  34.9 0.8 copy-start.12
  34.9 0.8 copy-start.11
  35.8 26.8 %all-to-all-start.1 = ((bf16[8,384,128]{2,1,0:T(8,128)(2,1)}), bf16[8,384,128]{2,1,0:T(8,128)(2,1)S(1)}, u32[]{:S(2)}, u32[]{:S(2)}) async-start(bf16[8,384,128]{2,1,0:T(8,128)(2,1)} %get-tuple-element.65), calls=%async_computation.1 | async-start | bytes 1572864 | tf_op jit(solution)/shard_map/all_to_all | solution.py:415
  39.3 8.1 %collective-permute-start.9 = (bf16[2,128,640]{2,1,0:T(8,128)(2,1)}, bf16[2,128,640]{2,1,0:T(8,128)(2,1)S(1)}, u32[]{:S(2)}, u32[]{:S(2)}) collective-permute-start(bf16[2,128,640]{2,1,0:T(8,128)(2,1)} %copy-done.11), channel_id=1, source_target_pairs={{0,16},{16,0},{1,17},{17,1},{2,18},{18,2},{3,19},{19,3},{4,20},{20... | collective-permute-start | bytes 983048 | tf_op jit(solution)/shard_map/ppermute | solution.py:352
  40.9 6.4 %collective-permute-start.10 = (bf16[640,256]{1,0:T(8,128)(2,1)S(1)}, bf16[640,256]{1,0:T(8,128)(2,1)S(1)}, u32[]{:S(2)}, u32[]{:S(2)}) collective-permute-start(bf16[640,256]{1,0:T(8,128)(2,1)S(1)} %constant_dynamic-slice_fusion.refs_6_), channel_id=1, source_target_pairs={{0,8},{8,0},{1,9},{9,1},{2,10},{10,2},{3,11},{11,3},{4,12},{12,4},... | collective-permute-start | bytes 983048 | tf_op jit(solution)/shard_map/ppermute | solution.py:349
  40.9 18.6 %collective-permute-start.11 = (bf16[640,256]{1,0:T(8,128)(2,1)}, bf16[640,256]{1,0:T(8,128)(2,1)S(1)}, u32[]{:S(2)}, u32[]{:S(2)}) collective-permute-start(bf16[640,256]{1,0:T(8,128)(2,1)} %collective-permute-done.refs_7_), channel_id=1, source_target_pairs={{0,8},{8,0},{1,9},{9,1},{2,10},{10,2},{3,11},{11,3},{4,12},{12,4},... | collective-permute-start | bytes 983048 | tf_op jit(solution)/shard_map/ppermute | solution.py:349
  41.4 18.1 %collective-permute-start.12 = (bf16[640,256]{1,0:T(8,128)(2,1)}, bf16[640,256]{1,0:T(8,128)(2,1)S(1)}, u32[]{:S(2)}, u32[]{:S(2)}) collective-permute-start(bf16[640,256]{1,0:T(8,128)(2,1)} %copy-done.10), channel_id=1, source_target_pairs={{0,8},{8,0},{1,9},{9,1},{2,10},{10,2},{3,11},{11,3},{4,12},{12,4},... | collective-permute-start | bytes 983048 | tf_op jit(solution)/shard_map/ppermute | solution.py:349
  41.5 18.2 %collective-permute-start.13 = (bf16[640,256]{1,0:T(8,128)(2,1)}, bf16[640,256]{1,0:T(8,128)(2,1)S(1)}, u32[]{:S(2)}, u32[]{:S(2)}) collective-permute-start(bf16[640,256]{1,0:T(8,128)(2,1)} %collective-permute-done.7.refs_9_), channel_id=1, source_target_pairs={{0,8},{8,0},{1,9},{9,1},{2,10},{10,2},{3,11},{11,3},{4,12},{12,4},... | collective-permute-start | bytes 983048 | tf_op jit(solution)/shard_map/ppermute | solution.py:349
  47.4 0.7 copy-start.13
  47.4 12.2 %collective-permute-start.14 = (bf16[640,256]{1,0:T(8,128)(2,1)}, bf16[640,256]{1,0:T(8,128)(2,1)S(1)}, u32[]{:S(2)}, u32[]{:S(2)}) collective-permute-start(bf16[640,256]{1,0:T(8,128)(2,1)} %collective-permute-done.6.refs_10_), channel_id=1, source_target_pairs={{0,8},{8,0},{1,9},{9,1},{2,10},{10,2},{3,11},{11,3},{4,12},{12,4},... | collective-permute-start | bytes 983048 | tf_op jit(solution)/shard_map/ppermute | solution.py:349
  48.1 14.4 %copy-start.14 = (bf16[640,256]{1,0:T(8,128)(2,1)}, bf16[640,256]{1,0:T(8,128)(2,1)S(1)}, u32[]{:S(2)}) copy-start(bf16[640,256]{1,0:T(8,128)(2,1)S(1)} %collective-permute-done.10.refs_12_) | copy-start | bytes 983044
  48.1 14.4 %collective-permute-start.8 = (bf16[640,256]{1,0:T(8,128)(2,1)}, bf16[640,256]{1,0:T(8,128)(2,1)}, u32[]{:S(2)}, u32[]{:S(2)}) collective-permute-start(bf16[640,256]{1,0:T(8,128)(2,1)} %collective-permute-done.6.refs_10_), channel_id=1, source_target_pairs={{2,0},{3,1},{4,6},{5,7},{10,8},{11,9},{12,14},{13,15},{18,16},{19,... | collective-permute-start | bytes 983048 | tf_op jit(solution)/shard_map/ppermute | solution.py:418
  49.4 0.7 copy-start.4
  59.6 0.8 copy-start.15
  59.6 0.9 copy-start.16
  59.6 1.0 copy-start.17
  60.6 0.8 copy-start.18
  62.6 1.0 copy-start.7
  66.5 26.2 %all-to-all-start.2 = ((bf16[8,384,128]{2,1,0:T(8,128)(2,1)}), bf16[8,384,128]{2,1,0:T(8,128)(2,1)S(1)}, u32[]{:S(2)}, u32[]{:S(2)}) async-start(bf16[8,384,128]{2,1,0:T(8,128)(2,1)} %get-tuple-element.78.refs_18_), calls=%async_computation.2 | async-start | bytes 1572864 | tf_op jit(solution)/shard_map/all_to_all | solution.py:461
  72.8 19.9 %copy-start.5 = (s32[8]{0:T(128)S(1)}, s32[8]{0:T(128)}, u32[]{:S(2)}) copy-start(s32[8]{0:T(128)} %get-tuple-element.76.after_ref.rows_here) | copy-start | bytes 100
  72.8 1.9 %collective-permute-start.15 = (bf16[640,256]{1,0:T(8,128)(2,1)}, bf16[640,256]{1,0:T(8,128)(2,1)S(1)}, u32[]{:S(2)}, u32[]{:S(2)}) collective-permute-start(bf16[640,256]{1,0:T(8,128)(2,1)} %collective-permute-done.8.refs_11_), channel_id=1, source_target_pairs={{0,8},{8,0},{1,9},{9,1},{2,10},{10,2},{3,11},{11,3},{4,12},{12,4},... | collective-permute-start | bytes 983048 | tf_op jit(solution)/shard_map/ppermute | solution.py:349
  74.7 0.7 copy-start.19
  80.5 7.9 %collective-permute-start.16 = (bf16[128,512]{1,0:T(8,128)(2,1)}, bf16[128,512]{1,0:T(8,128)(2,1)S(1)}, u32[]{:S(2)}, u32[]{:S(2)}) collective-permute-start(bf16[128,512]{1,0:T(8,128)(2,1)} %get-tuple-element.87), channel_id=1, source_target_pairs={{0,1},{1,0},{2,3},{3,2},{4,5},{5,4},{6,7},{7,6},{8,9},{9,8},{10,11... | collective-permute-start | bytes 393224 | tf_op jit(solution)/shard_map/ppermute | solution.py:346
  82.5 5.9 %collective-permute-start.17 = (bf16[128,512]{1,0:T(8,128)(2,1)}, bf16[128,512]{1,0:T(8,128)(2,1)S(1)}, u32[]{:S(2)}, u32[]{:S(2)}) collective-permute-start(bf16[128,512]{1,0:T(8,128)(2,1)} %get-tuple-element.88), channel_id=1, source_target_pairs={{0,16},{16,0},{1,17},{17,1},{2,18},{18,2},{3,19},{19,3},{4,20},{20... | collective-permute-start | bytes 393224 | tf_op jit(solution)/shard_map/ppermute | solution.py:352
  84.0 8.4 %collective-permute-start.18 = (bf16[128,512]{1,0:T(8,128)(2,1)}, bf16[128,512]{1,0:T(8,128)(2,1)S(1)}, u32[]{:S(2)}, u32[]{:S(2)}) collective-permute-start(bf16[128,512]{1,0:T(8,128)(2,1)} %get-tuple-element.89), channel_id=1, source_target_pairs={{0,17},{1,16},{2,19},{3,18},{4,21},{5,20},{6,23},{7,22},{16,1},{17... | collective-permute-start | bytes 393224 | tf_op jit(solution)/shard_map/ppermute | solution.py:462
  92.7 2.4 %collective-permute-start.20 = (bf16[8,384,128]{2,1,0:T(8,128)(2,1)S(1)}, bf16[8,384,128]{2,1,0:T(8,128)(2,1)S(1)}, u32[]{:S(2)}, u32[]{:S(2)}) collective-permute-start(bf16[8,384,128]{2,1,0:T(8,128)(2,1)S(1)} %all-to-all-done.2.rest_0_), channel_id=1, source_target_pairs={{0,8},{8,0},{1,9},{9,1},{2,10},{10,2},{3,11},{11,3},{4,12},{12,4},... | collective-permute-start | bytes 2359304 | tf_op jit(solution)/shard_map/ppermute | solution.py:349
  92.7 2.3 %collective-permute-start.19 = (s32[8]{0:T(128)S(1)}, s32[8]{0:T(128)S(1)}, u32[]{:S(2)}, u32[]{:S(2)}) collective-permute-start(s32[8]{0:T(128)S(1)} %copy-done.5), channel_id=1, source_target_pairs={{0,8},{8,0},{1,9},{9,1},{2,10},{10,2},{3,11},{11,3},{4,12},{12,4},... | collective-permute-start | bytes 104 | tf_op jit(solution)/shard_map/ppermute | solution.py:349
  95.1 3.2 %copy-start.1 = (bf16[640,512]{1,0:T(8,128)(2,1)S(1)}, bf16[640,512]{1,0:T(8,128)(2,1)}, u32[]{:S(2)}) copy-start(bf16[640,512]{1,0:T(8,128)(2,1)} %param.9) | copy-start | bytes 1966084

commit v16 on v15

--- a/solution.py
+++ b/solution.py
@@ -383,9 +383,12 @@
     ends = [(t, t ^ 2) for t in range(group) if t // 2 in (1, 2)]
     near = exchange(half, 2)
     over = lax.ppermute(half, "tensor", middle)
-    near, over, asked, x_theirs, xs = lax.optimization_barrier((near, over, asked, x_theirs, xs))
+    half_core = other_core(half)
+    near, over, asked, x_theirs, xs, half_core = lax.optimization_barrier(
+        (near, over, asked, x_theirs, xs, half_core)
+    )
+    near_core = other_core(near)
     x_far.append(exchange(x_theirs[1], 1))
-    y_far = [other_part(x_far[0])]
     over_near = lax.ppermute(near, "tensor", middle)
     passed = lax.ppermute(over, "tensor", ends)
     pieces = jax.ShapeDtypeStruct((group, down_chunks + up_chunks, LANES), jnp.bfloat16)
@@ -409,15 +412,14 @@
         cost_estimate=cost(read=40 << 20),
         name="pick_panels",
     )(asked, tiles(down_store), tiles(up_store))
-    sent, rows, x_far, y_far, y_mine, half, near, over, over_near, passed = lax.optimization_barrier(
-        (sent, rows, x_far, y_far, y_mine, half, near, over, over_near, passed)
+    sent, rows, x_far, y_mine, near_core, over, over_near, passed = lax.optimization_barrier(
+        (sent, rows, x_far, y_mine, near_core, over, over_near, passed)
     )
     panels = lax.all_to_all(sent, "tensor", 0, 0)
     rows_core = other_core(rows)
-    y_far.append(other_part(x_far[1]))
+    y_far = [other_part(piece) for piece in x_far]
     passed_near = lax.ppermute(over_near, "tensor", ends)
-    quarter = [half, near, over, passed, over_near]
-    quarter_core = [other_core(w) for w in quarter]
+    middle_core = [other_core(w) for w in (over, passed)]
 
     owned_groups = ADAPTERS // lax.axis_size("dp") // 8
     down_shape = jax.ShapeDtypeStruct((owned_groups, down_chunks, 8, 1, LANES), jnp.float32)
@@ -428,7 +430,7 @@
         scratch_shapes=[pltpu.VMEM((up_chunks, 8, 1, LANES), jnp.float32), pltpu.SemaphoreType.DMA((2,))],
         compiler_params=LIMIT, cost_estimate=cost(read=28 << 20), name="clear_rows",
     )(rows)
-    panels, passed_near, y_far, quarter_core = lax.optimization_barrier((panels, passed_near, y_far, quarter_core))
+    panels, passed_near, y_far, middle_core = lax.optimization_barrier((panels, passed_near, y_far, middle_core))
 
     terms, lifted = pl.pallas_call(
         functools.partial(adapter_kernel, group, down_chunks),
@@ -440,8 +442,9 @@
         cost_estimate=cost(flops=3 << 30, read=8 << 20),
         name="adapter",
     )(xs, cotangent, panels, cleared)
-    _, passed_near = lax.optimization_barrier((terms, passed_near))
-    quarters = quarter + [passed_near] + quarter_core + [other_core(passed_near)]
+    _, over_near, passed_near = lax.optimization_barrier((terms, over_near, passed_near))
+    quarters = [half, near, over, passed, over_near, passed_near, half_core, near_core]
+    quarters += middle_core + [other_core(w) for w in (over_near, passed_near)]
     sums = [jax.ShapeDtypeStruct((token_rows, parts * width), kind) for kind in (jnp.float32,) + (jnp.bfloat16,) * 3]
     own, to_part, to_inner, to_both = pl.pallas_call(
         base_kernel,

time: 99 us -> 98.1 us (level)
  waiting for transfers between devices: 22.3 us -> 19.8 us
  starting transfers between devices: 34.7 us -> 36.7 us
  local copies, waits for them, and re-layouts: 6.69 us -> 5.45 us
    ppermute x4, waiting for transfers between devices: 7.8 us -> 1.44 us  [other_part(): lax.ppermute(value, 'parts', [(a, parts - 1 - a) for a in range(parts)])]
    ppermute x1, waiting for transfers between devices: 1.21 us -> 5.89 us  [fast_body(): passed_near = lax.ppermute(over_near, 'tensor', ends)]
    all_to_all x1, starting transfers between devices: 3.55 us -> 7.3 us  [fast_body(): panels = lax.all_to_all(sent, 'tensor', 0, 0)]
    all_to_all x1, starting transfers between devices: 6.31 us -> 4.49 us  [fast_body(): back = lax.all_to_all(terms, 'tensor', 0, 0)]
    unnamed x40 -> x36, local copies, waits for them, and re-layouts: 6.67 us -> 5.43 us
    ppermute x1, waiting for transfers between devices: 3.98 us -> 2.76 us  [fast_body(): lax.ppermute(to_both, ('parts', 'tensor'), opposite)]
    ppermute x4, starting transfers between devices: 10.1 us -> 8.87 us  [exchange(): return lax.ppermute(value, 'tensor', [(t, t ^ s) for t in range(group)])]
  transfers between devices with their start and end apart: 24 -> 24, of which waited for: 9 -> 9; matrix products, arithmetic and copies ran while one was open for 2% -> 2% of each run, Pallas kernels for 24% -> 25%
where the time goes in v16:
time: 98.1 us; the launch traced here: 97.2 us
  starting transfers between devices  36.7 us (37%)
  Pallas kernels  31.9 us (33%)
  waiting for transfers between devices  19.8 us (20%)
  local copies, waits for them, and re-layouts  5.45 us (6%)
  other arithmetic  1.81 us (2%)
  between operations  1.6 us (2%)
    pallas_call x1, Pallas kernels, fast_body(): pl.pallas_call(zero_kernel, out_shape=(down_shape, up_shape, token), in_s...  9.48 us
    ppermute x4, starting transfers between devices, exchange(): return lax.ppermute(value, 'tensor', [(t, t ^ s) for t in range(group)])  8.87 us
    all_to_all x1, starting transfers between devices, fast_body(): panels = lax.all_to_all(sent, 'tensor', 0, 0)  7.3 us
    ppermute x1, waiting for transfers between devices, fast_body(): passed_near = lax.ppermute(over_near, 'tensor', ends)  5.89 us
    pallas_call x1, Pallas kernels, fast_body(): pl.pallas_call(gather_kernel, out_shape=(pieces, jax.ShapeDtypeStruct((gr...  5.49 us
    unnamed x36, local copies, waits for them, and re-layouts  5.43 us
    pallas_call x1, Pallas kernels, fast_body(): pl.pallas_call(base_kernel, out_shape=sums, in_specs=[ANY] * (7 + len(qua...  5.02 us
    ppermute x4, starting transfers between devices, other_part(): lax.ppermute(value, 'parts', [(a, parts - 1 - a) for a in range(parts)])  4.51 us
  transfers between devices with their start and end apart: 24, of which 9 were waited for; matrix products, arithmetic and copies ran while one was open for 2% of the time, Pallas kernels for 25%

profile of v16, /device:TPU:0, one launch (start us, length us, event | category | flops | bytes accessed | tf_op | source)
XLA Modules:
  0.0 97.2 jit_solution(15414608349802927367)
XLA Ops:
  0.6 0.0 copy-start
  1.4 1.3 %own_row.1 = s32[8,1,128]{2,1,0:T(1,128)} custom-call(s32[1]{0:T(128)S(6)} %copy.14.block_ref, s32[256]{0:T(256)} %slot_ref.1), custom_call_target="tpu_custom_call" | custom-call | tf_op jit(solution)/shard_map/own_row/pallas_call | solution.py:354
  2.7 0.5 collective-permute-start.2
  3.2 1.4 %collective-permute-start.1 = (bf16[640,256]{1,0:T(8,128)(2,1)S(1)}, bf16[640,256]{1,0:T(8,128)(2,1)}, u32[]{:S(2)}, u32[]{:S(2)}) collective-permute-start(bf16[640,256]{1,0:T(8,128)(2,1)S(1)} %constant_dynamic-slice_fusion.refs_6_), channel_id=1, source_target_pairs={{2,4},{3,5},{4,2},{5,3},{10,12},{11,13},{12,10},{13,11},{18,20},{1... | collective-permute-start | bytes 983048 | tf_op jit(solution)/shard_map/ppermute | solution.py:385
  4.6 4.7 %collective-permute-start = (bf16[640,256]{1,0:T(8,128)(2,1)S(1)}, bf16[640,256]{1,0:T(8,128)(2,1)}, u32[]{:S(2)}, u32[]{:S(2)}) collective-permute-start(bf16[640,256]{1,0:T(8,128)(2,1)S(1)} %constant_dynamic-slice_fusion.refs_6_), channel_id=1, source_target_pairs={{0,2},{1,3},{2,0},{3,1},{4,6},{5,7},{6,4},{7,5},{8,10},{9,11},{10,... | collective-permute-start | bytes 983048 | tf_op jit(solution)/shard_map/ppermute | solution.py:346
  9.3 1.3 %copy-done.2 = bf16[128,5120]{1,0:T(8,128)(2,1)S(1)} copy-done((bf16[128,5120]{1,0:T(8,128)(2,1)S(1)}, bf16[128,5120]{1,0:T(8,128)(2,1)}, u32[]{:S(2)}) %copy-start.2) | copy-done | bytes 1310744
  10.7 0.1 split_tokens.1
  10.8 1.6 %collective-permute-start.5 = (bf16[4,128,640]{2,1,0:T(8,128)(2,1)S(1)}, bf16[4,128,640]{2,1,0:T(8,128)(2,1)}, u32[]{:S(2)}, u32[]{:S(2)}) collective-permute-start(bf16[4,128,640]{2,1,0:T(8,128)(2,1)S(1)} %get-tuple-element.49.refs_0_), channel_id=1, source_target_pairs={{0,16},{16,0},{1,17},{17,1},{2,18},{18,2},{3,19},{19,3},{4,20},{20... | collective-permute-start | bytes 1966088 | tf_op jit(solution)/shard_map/ppermute | solution.py:352
  12.4 1.5 %collective-permute-start.3 = (bf16[2,128,640]{2,1,0:T(8,128)(2,1)S(1)}, bf16[2,128,640]{2,1,0:T(8,128)(2,1)S(1)}, u32[]{:S(2)}, u32[]{:S(2)}) collective-permute-start(bf16[2,128,640]{2,1,0:T(8,128)(2,1)S(1)} %get-tuple-element.51), channel_id=1, source_target_pairs={{0,1},{1,0},{2,3},{3,2},{4,5},{5,4},{6,7},{7,6},{8,9},{9,8},{10,11... | collective-permute-start | bytes 983048 | tf_op jit(solution)/shard_map/ppermute | solution.py:346
  13.9 3.3 %all-to-all-start = ((s32[8,1,128]{2,1,0:T(1,128)}), s32[8,1,128]{2,1,0:T(1,128)S(1)}, u32[]{:S(2)}, u32[]{:S(2)}) async-start(s32[8,1,128]{2,1,0:T(1,128)} %own_row.1), calls=%async_computation | async-start | bytes 8192 | tf_op jit(solution)/shard_map/all_to_all | solution.py:358
  17.2 3.9 %pair_columns.1.xs_ref = bf16[8,256,320]{2,1,0:T(8,128)(2,1)} custom-call(bf16[128,5120]{1,0:T(8,128)(2,1)} %x_ref.1), custom_call_target="tpu_custom_call" | custom-call | bytes 134217728 | tf_op jit(solution)/shard_map/pair_columns/pallas_call | solution.py:372
  21.0 2.5 %all-to-all-done.asked = s32[8,1,128]{2,1,0:T(1,128)S(1)} async-done(((s32[8,1,128]{2,1,0:T(1,128)}), s32[8,1,128]{2,1,0:T(1,128)S(1)}, u32[]{:S(2)}, u32[]{:S(2)}) %all-to-all-start) | async-done | bytes 4128 | tf_op jit(solution)/shard_map/all_to_all | solution.py:358
  23.5 0.0 collective-permute-done.2.refs_12_
  23.5 0.0 collective-permute-done.1.refs_8_
  23.5 0.0 collective-permute-done.refs_7_
  23.5 0.6 collective-permute-start.4
  24.1 1.3 %collective-permute-start.8 = (bf16[640,256]{1,0:T(8,128)(2,1)}, bf16[640,256]{1,0:T(8,128)(2,1)}, u32[]{:S(2)}, u32[]{:S(2)}) collective-permute-start(bf16[640,256]{1,0:T(8,128)(2,1)} %collective-permute-done.1.refs_8_), channel_id=1, source_target_pairs={{2,0},{3,1},{4,6},{5,7},{10,8},{11,9},{12,14},{13,15},{18,16},{19,... | collective-permute-start | bytes 983048 | tf_op jit(solution)/shard_map/ppermute | solution.py:393
  25.4 1.4 %collective-permute-start.7 = (bf16[640,256]{1,0:T(8,128)(2,1)}, bf16[640,256]{1,0:T(8,128)(2,1)}, u32[]{:S(2)}, u32[]{:S(2)}) collective-permute-start(bf16[640,256]{1,0:T(8,128)(2,1)} %collective-permute-done.refs_7_), channel_id=1, source_target_pairs={{2,4},{3,5},{4,2},{5,3},{10,12},{11,13},{12,10},{13,11},{18,20},{1... | collective-permute-start | bytes 983048 | tf_op jit(solution)/shard_map/ppermute | solution.py:392
  26.8 0.0 collective-permute-done.3.refs_2_
  26.8 0.0 collective-permute-start.6
  26.8 0.7 copy-done.11
  27.6 5.5 %pick_panels.1 = (bf16[8,384,128]{2,1,0:T(8,128)(2,1)}, s32[8]{0:T(128)}) custom-call(s32[8,1,128]{2,1,0:T(1,128)} %copy-done.9, bf16[32,320,8,128]{3,2,1,0:T(8,128)(2,1)} %bitcast.16, bf16[32,64,8,128]{3,2,1,0:T(8,128)(2,1)} %bitcast.18), custom_call_target="tpu_custom_call" | custom-call | bytes 41943040 | tf_op jit(solution)/shard_map/pick_panels/pallas_call | solution.py:399
  33.1 0.0 collective-permute-done.5.refs_1_
  33.1 0.0 collective-permute-done.4.refs_3_
  33.1 0.8 collective-permute-done.8.refs_9_
  33.9 0.0 collective-permute-done.7.refs_10_
  33.9 0.0 collective-permute-done.6.refs_13_
  33.9 7.3 %all-to-all-start.1 = ((bf16[8,384,128]{2,1,0:T(8,128)(2,1)}), bf16[8,384,128]{2,1,0:T(8,128)(2,1)S(1)}, u32[]{:S(2)}, u32[]{:S(2)}) async-start(bf16[8,384,128]{2,1,0:T(8,128)(2,1)} %get-tuple-element.62), calls=%async_computation.1 | async-start | bytes 1572864 | tf_op jit(solution)/shard_map/all_to_all | solution.py:418
  41.2 0.6 collective-permute-start.10
  41.8 1.5 %collective-permute-start.11 = (bf16[2,128,640]{2,1,0:T(8,128)(2,1)}, bf16[2,128,640]{2,1,0:T(8,128)(2,1)S(1)}, u32[]{:S(2)}, u32[]{:S(2)}) collective-permute-start(bf16[2,128,640]{2,1,0:T(8,128)(2,1)} %collective-permute-done.4.refs_3_), channel_id=1, source_target_pairs={{0,16},{16,0},{1,17},{17,1},{2,18},{18,2},{3,19},{19,3},{4,20},{20... | collective-permute-start | bytes 983048 | tf_op jit(solution)/shard_map/ppermute | solution.py:352
  43.3 1.3 %collective-permute-start.9 = (bf16[640,256]{1,0:T(8,128)(2,1)}, bf16[640,256]{1,0:T(8,128)(2,1)}, u32[]{:S(2)}, u32[]{:S(2)}) collective-permute-start(bf16[640,256]{1,0:T(8,128)(2,1)} %collective-permute-done.7.refs_10_), channel_id=1, source_target_pairs={{2,0},{3,1},{4,6},{5,7},{10,8},{11,9},{12,14},{13,15},{18,16},{19,... | collective-permute-start | bytes 983048 | tf_op jit(solution)/shard_map/ppermute | solution.py:421
  44.6 0.1 collective-permute-start.12
  44.7 0.5 collective-permute-start.13
  45.2 0.6 copy-done.4
  45.8 9.5 %clear_rows.1 = (f32[16,320,8,1,128]{4,3,2,1,0:T(1,128)}, f32[16,64,8,1,128]{4,3,2,1,0:T(1,128)}, s32[1]{0:T(128)}) custom-call(s32[8]{0:T(128)S(1)} %copy-done.4), custom_call_target="tpu_custom_call" | custom-call | bytes 29360128 | tf_op jit(solution)/shard_map/clear_rows/pallas_call | solution.py:427
  55.3 0.0 collective-permute-done.10.refs_4_
  55.3 1.4 %collective-permute-done.11.refs_5_ = bf16[2,128,640]{2,1,0:T(8,128)(2,1)S(1)} collective-permute-done((bf16[2,128,640]{2,1,0:T(8,128)(2,1)}, bf16[2,128,640]{2,1,0:T(8,128)(2,1)S(1)}, u32[]{:S(2)}, u32[]{:S(2)}) %collective-permute-start.11) | collective-permute-done | bytes 327712 | tf_op jit(solution)/shard_map/ppermute | solution.py:352
  56.7 5.9 %collective-permute-done.9.refs_11_ = bf16[640,256]{1,0:T(8,128)(2,1)} collective-permute-done((bf16[640,256]{1,0:T(8,128)(2,1)}, bf16[640,256]{1,0:T(8,128)(2,1)}, u32[]{:S(2)}, u32[]{:S(2)}) %collective-permute-start.9) | collective-permute-done | bytes 327712 | tf_op jit(solution)/shard_map/ppermute | solution.py:421
  62.6 0.7 copy-done.15
  63.4 0.0 collective-permute-done.13.refs_15_
  63.4 0.0 all-to-all-done.1.pieces
  63.4 0.0 copy-start.7
  63.4 0.9 copy-done.7
  64.4 3.0 %adapter.1 = (bf16[8,384,128]{2,1,0:T(8,128)(2,1)}, f32[128,1024]{1,0:T(8,128)S(1)}) custom-call(bf16[8,256,320]{2,1,0:T(8,128)(2,1)S(1)} %copy-done.3, bf16[128,1024]{1,0:T(8,128)(2,1)S(1)} %copy-done.7, bf16[8,384,128]{2,1,0:T(8,128)(2,1)S(1)} %all-to-all-done.1.pieces, s32[1]{0:T(128)} %get-tuple-element.71._), custom_call_target="tpu_custom_call" | custom-call | flops 3221225472 | bytes 8388608 | tf_op jit(solution)/shard_map/adapter/pallas_call | solution.py:435
  67.4 4.5 %all-to-all-start.2 = ((bf16[8,384,128]{2,1,0:T(8,128)(2,1)}), bf16[8,384,128]{2,1,0:T(8,128)(2,1)S(1)}, u32[]{:S(2)}, u32[]{:S(2)}) async-start(bf16[8,384,128]{2,1,0:T(8,128)(2,1)} %get-tuple-element.72.refs_18_), calls=%async_computation.2 | async-start | bytes 1572864 | tf_op jit(solution)/shard_map/all_to_all | solution.py:464
  71.9 0.1 collective-permute-start.14
  71.9 0.5 collective-permute-start.15
  72.4 1.3 %collective-permute-done.14.refs_16_ = bf16[640,256]{1,0:T(8,128)(2,1)S(1)} collective-permute-done((bf16[640,256]{1,0:T(8,128)(2,1)}, bf16[640,256]{1,0:T(8,128)(2,1)S(1)}, u32[]{:S(2)}, u32[]{:S(2)}) %collective-permute-start.14) | collective-permute-done | bytes 327712 | tf_op jit(solution)/shard_map/ppermute | solution.py:349
  73.8 0.5 collective-permute-done.15.refs_17_
  74.2 0.2 copy-done.16
  74.5 0.7 copy-done.17
  75.2 5.0 %frozen_part.1 = (f32[128,512]{1,0:T(8,128)}, bf16[128,512]{1,0:T(8,128)(2,1)}, bf16[128,512]{1,0:T(8,128)(2,1)}, bf16[128,512]{1,0:T(8,128)(2,1)}) custom-call(bf16[4,128,640]{2,1,0:T(8,128)(2,1)} %copy-done.6, bf16[4,128,640]{2,1,0:T(8,128)(2,1)} %collective-permute-done.5.refs_1_, bf16[2,128,640]{2,1,0:T(8,128)(2,1)} %copy-done.11, ...), custom_call_target="tpu_custom_call" | custom-call | flops 4294967296 | bytes 8388608 | tf_op jit(solution)/shard_map/frozen_part/pallas_call | solution.py:449
  80.3 2.0 %collective-permute-start.16 = (bf16[128,512]{1,0:T(8,128)(2,1)}, bf16[128,512]{1,0:T(8,128)(2,1)S(1)}, u32[]{:S(2)}, u32[]{:S(2)}) collective-permute-start(bf16[128,512]{1,0:T(8,128)(2,1)} %get-tuple-element.81), channel_id=1, source_target_pairs={{0,1},{1,0},{2,3},{3,2},{4,5},{5,4},{6,7},{7,6},{8,9},{9,8},{10,11... | collective-permute-start | bytes 393224 | tf_op jit(solution)/shard_map/ppermute | solution.py:346
  82.3 0.8 collective-permute-start.17
  83.1 0.7 collective-permute-start.18
  83.8 4.3 %collective-permute-done.16 = bf16[128,512]{1,0:T(8,128)(2,1)S(1)} collective-permute-done((bf16[128,512]{1,0:T(8,128)(2,1)}, bf16[128,512]{1,0:T(8,128)(2,1)S(1)}, u32[]{:S(2)}, u32[]{:S(2)}) %collective-permute-start.16) | collective-permute-done | bytes 131104 | tf_op jit(solution)/shard_map/ppermute | solution.py:346
  88.1 2.8 %collective-permute-done.18 = bf16[128,512]{1,0:T(8,128)(2,1)S(1)} collective-permute-done((bf16[128,512]{1,0:T(8,128)(2,1)}, bf16[128,512]{1,0:T(8,128)(2,1)S(1)}, u32[]{:S(2)}, u32[]{:S(2)}) %collective-permute-start.18) | collective-permute-done | bytes 131104 | tf_op jit(solution)/shard_map/ppermute | solution.py:465
  90.8 0.4 all-to-all-done.2.rest_0_
  91.2 0.5 collective-permute-start.19
  91.7 1.0 %convert_add_fusion = (f32[128,512]{1,0:T(8,128)S(1)}, f32[128,512]{1,0:T(8,128)S(1)}) fusion(bf16[128,512]{1,0:T(8,128)(2,1)S(1)} %collective-permute-done.18, bf16[128,512]{1,0:T(8,128)(2,1)S(1)} %collective-permute-done.17, f32[128,512]{1,0:T(8,128)} %get-tuple-element.80, bf16[128,512]{1,0:T(8,128)(2,1)S(1)} %collective-permute-done.16), kind=kLoop, calls=%fused_computation.2 | loop fusion | flops 327680 | bytes 1179648 | tf_op jit(solution)/shard_map/add | solution.py:491
  92.8 0.8 fusion
  93.6 0.0 collective-permute-done.19.rows_core
  93.6 0.0 collective-permute-done.20.rest_1_
  93.6 3.6 %place_rows.1 = (f32[16,320,8,1,128]{4,3,2,1,0:T(1,128)}, f32[16,64,8,1,128]{4,3,2,1,0:T(1,128)}) custom-call(s32[8]{0:T(128)S(1)} %copy-done.5, s32[8]{0:T(128)S(1)} %collective-permute-done.19.rows_core, bf16[8,384,128]{2,1,0:T(8,128)(2,1)S(1)} %all-to-all-done.2.rest_0_, ...), custom_call_target="tpu_custom_call", output_to_operand_aliasing={{0}: (4, {}), {1}: (5, {})} | custom-call | bytes 16777216 | tf_op jit(solution)/shard_map/place_rows/pallas_call | solution.py:469
  (32 shorter events, 0.1 us)
Async XLA Ops:
  0.6 2.0 %copy-start = (bf16[640,512]{1,0:T(8,128)(2,1)S(1)}, bf16[640,512]{1,0:T(8,128)(2,1)}, u32[]{:S(2)}) copy-start(bf16[640,512]{1,0:T(8,128)(2,1)} %param.9) | copy-start | bytes 1966084
  2.7 30.4 %copy-start.8 = (bf16[640,256]{1,0:T(8,128)(2,1)}, bf16[640,256]{1,0:T(8,128)(2,1)S(1)}, u32[]{:S(2)}) copy-start(bf16[640,256]{1,0:T(8,128)(2,1)S(1)} %constant_dynamic-slice_fusion.refs_6_) | copy-start | bytes 983044
  2.7 20.8 %collective-permute-start.2 = (bf16[640,256]{1,0:T(8,128)(2,1)S(1)}, bf16[640,256]{1,0:T(8,128)(2,1)S(1)}, u32[]{:S(2)}, u32[]{:S(2)}) collective-permute-start(bf16[640,256]{1,0:T(8,128)(2,1)S(1)} %constant_dynamic-slice_fusion.refs_6_), channel_id=1, source_target_pairs={{0,8},{8,0},{1,9},{9,1},{2,10},{10,2},{3,11},{11,3},{4,12},{12,4},... | collective-permute-start | bytes 983048 | tf_op jit(solution)/shard_map/ppermute | solution.py:349
  3.2 20.3 %collective-permute-start.1 = (bf16[640,256]{1,0:T(8,128)(2,1)S(1)}, bf16[640,256]{1,0:T(8,128)(2,1)}, u32[]{:S(2)}, u32[]{:S(2)}) collective-permute-start(bf16[640,256]{1,0:T(8,128)(2,1)S(1)} %constant_dynamic-slice_fusion.refs_6_), channel_id=1, source_target_pairs={{2,4},{3,5},{4,2},{5,3},{10,12},{11,13},{12,10},{13,11},{18,20},{1... | collective-permute-start | bytes 983048 | tf_op jit(solution)/shard_map/ppermute | solution.py:385
  4.6 18.9 %collective-permute-start = (bf16[640,256]{1,0:T(8,128)(2,1)S(1)}, bf16[640,256]{1,0:T(8,128)(2,1)}, u32[]{:S(2)}, u32[]{:S(2)}) collective-permute-start(bf16[640,256]{1,0:T(8,128)(2,1)S(1)} %constant_dynamic-slice_fusion.refs_6_), channel_id=1, source_target_pairs={{0,2},{1,3},{2,0},{3,1},{4,6},{5,7},{6,4},{7,5},{8,10},{9,11},{10,... | collective-permute-start | bytes 983048 | tf_op jit(solution)/shard_map/ppermute | solution.py:346
  9.3 1.3 %copy-start.2 = (bf16[128,5120]{1,0:T(8,128)(2,1)S(1)}, bf16[128,5120]{1,0:T(8,128)(2,1)}, u32[]{:S(2)}) copy-start(bf16[128,5120]{1,0:T(8,128)(2,1)} %x_ref.1) | copy-start | bytes 3932164
  10.8 22.3 %copy-start.6 = (bf16[4,128,640]{2,1,0:T(8,128)(2,1)}, bf16[4,128,640]{2,1,0:T(8,128)(2,1)S(1)}, u32[]{:S(2)}) copy-start(bf16[4,128,640]{2,1,0:T(8,128)(2,1)S(1)} %get-tuple-element.49.refs_0_) | copy-start | bytes 1966084
  10.8 22.3 %collective-permute-start.5 = (bf16[4,128,640]{2,1,0:T(8,128)(2,1)S(1)}, bf16[4,128,640]{2,1,0:T(8,128)(2,1)}, u32[]{:S(2)}, u32[]{:S(2)}) collective-permute-start(bf16[4,128,640]{2,1,0:T(8,128)(2,1)S(1)} %get-tuple-element.49.refs_0_), channel_id=1, source_target_pairs={{0,16},{16,0},{1,17},{17,1},{2,18},{18,2},{3,19},{19,3},{4,20},{20... | collective-permute-start | bytes 1966088 | tf_op jit(solution)/shard_map/ppermute | solution.py:352
  12.4 14.5 %collective-permute-start.3 = (bf16[2,128,640]{2,1,0:T(8,128)(2,1)S(1)}, bf16[2,128,640]{2,1,0:T(8,128)(2,1)S(1)}, u32[]{:S(2)}, u32[]{:S(2)}) collective-permute-start(bf16[2,128,640]{2,1,0:T(8,128)(2,1)S(1)} %get-tuple-element.51), channel_id=1, source_target_pairs={{0,1},{1,0},{2,3},{3,2},{4,5},{5,4},{6,7},{7,6},{8,9},{9,8},{10,11... | collective-permute-start | bytes 983048 | tf_op jit(solution)/shard_map/ppermute | solution.py:346
  13.9 9.6 %all-to-all-start = ((s32[8,1,128]{2,1,0:T(1,128)}), s32[8,1,128]{2,1,0:T(1,128)S(1)}, u32[]{:S(2)}, u32[]{:S(2)}) async-start(s32[8,1,128]{2,1,0:T(1,128)} %own_row.1), calls=%async_computation | async-start | bytes 8192 | tf_op jit(solution)/shard_map/all_to_all | solution.py:358
  23.5 4.1 %copy-start.9 = (s32[8,1,128]{2,1,0:T(1,128)}, s32[8,1,128]{2,1,0:T(1,128)S(1)}, u32[]{:S(2)}) copy-start(s32[8,1,128]{2,1,0:T(1,128)S(1)} %all-to-all-done.asked) | copy-start | bytes 12292
  23.5 9.6 %copy-start.10 = (bf16[640,256]{1,0:T(8,128)(2,1)}, bf16[640,256]{1,0:T(8,128)(2,1)S(1)}, u32[]{:S(2)}) copy-start(bf16[640,256]{1,0:T(8,128)(2,1)S(1)} %collective-permute-done.2.refs_12_) | copy-start | bytes 983044
  23.5 9.6 %collective-permute-start.4 = (bf16[2,128,640]{2,1,0:T(8,128)(2,1)S(1)}, bf16[2,128,640]{2,1,0:T(8,128)(2,1)}, u32[]{:S(2)}, u32[]{:S(2)}) collective-permute-start(bf16[2,128,640]{2,1,0:T(8,128)(2,1)S(1)} %get-tuple-element.56), channel_id=1, source_target_pairs={{0,1},{1,0},{2,3},{3,2},{4,5},{5,4},{6,7},{7,6},{8,9},{9,8},{10,11... | collective-permute-start | bytes 983048 | tf_op jit(solution)/shard_map/ppermute | solution.py:346
  24.1 9.7 %collective-permute-start.8 = (bf16[640,256]{1,0:T(8,128)(2,1)}, bf16[640,256]{1,0:T(8,128)(2,1)}, u32[]{:S(2)}, u32[]{:S(2)}) collective-permute-start(bf16[640,256]{1,0:T(8,128)(2,1)} %collective-permute-done.1.refs_8_), channel_id=1, source_target_pairs={{2,0},{3,1},{4,6},{5,7},{10,8},{11,9},{12,14},{13,15},{18,16},{19,... | collective-permute-start | bytes 983048 | tf_op jit(solution)/shard_map/ppermute | solution.py:393
  25.4 8.5 %collective-permute-start.7 = (bf16[640,256]{1,0:T(8,128)(2,1)}, bf16[640,256]{1,0:T(8,128)(2,1)}, u32[]{:S(2)}, u32[]{:S(2)}) collective-permute-start(bf16[640,256]{1,0:T(8,128)(2,1)} %collective-permute-done.refs_7_), channel_id=1, source_target_pairs={{2,4},{3,5},{4,2},{5,3},{10,12},{11,13},{12,10},{13,11},{18,20},{1... | collective-permute-start | bytes 983048 | tf_op jit(solution)/shard_map/ppermute | solution.py:392
  26.8 0.7 copy-start.11
  26.8 7.1 %collective-permute-start.6 = (bf16[640,256]{1,0:T(8,128)(2,1)}, bf16[640,256]{1,0:T(8,128)(2,1)}, u32[]{:S(2)}, u32[]{:S(2)}) collective-permute-start(bf16[640,256]{1,0:T(8,128)(2,1)} %collective-permute-done.refs_7_), channel_id=1, source_target_pairs={{0,8},{8,0},{1,9},{9,1},{2,10},{10,2},{3,11},{11,3},{4,12},{12,4},... | collective-permute-start | bytes 983048 | tf_op jit(solution)/shard_map/ppermute | solution.py:349
  27.6 13.6 %copy-start.12 = (bf16[2,128,640]{2,1,0:T(8,128)(2,1)S(1)}, bf16[2,128,640]{2,1,0:T(8,128)(2,1)}, u32[]{:S(2)}) copy-start(bf16[2,128,640]{2,1,0:T(8,128)(2,1)} %copy-done.11) | copy-start | bytes 983044
  27.6 35.8 %copy-start.3 = (bf16[8,256,320]{2,1,0:T(8,128)(2,1)S(1)}, bf16[8,256,320]{2,1,0:T(8,128)(2,1)}, u32[]{:S(2)}) copy-start(bf16[8,256,320]{2,1,0:T(8,128)(2,1)} %pair_columns.1.xs_ref) | copy-start | bytes 3932164
  33.9 29.5 %all-to-all-start.1 = ((bf16[8,384,128]{2,1,0:T(8,128)(2,1)}), bf16[8,384,128]{2,1,0:T(8,128)(2,1)S(1)}, u32[]{:S(2)}, u32[]{:S(2)}) async-start(bf16[8,384,128]{2,1,0:T(8,128)(2,1)} %get-tuple-element.62), calls=%async_computation.1 | async-start | bytes 1572864 | tf_op jit(solution)/shard_map/all_to_all | solution.py:418
  41.2 14.1 %collective-permute-start.10 = (bf16[2,128,640]{2,1,0:T(8,128)(2,1)S(1)}, bf16[2,128,640]{2,1,0:T(8,128)(2,1)S(1)}, u32[]{:S(2)}, u32[]{:S(2)}) collective-permute-start(bf16[2,128,640]{2,1,0:T(8,128)(2,1)S(1)} %copy-done.12), channel_id=1, source_target_pairs={{0,16},{16,0},{1,17},{17,1},{2,18},{18,2},{3,19},{19,3},{4,20},{20... | collective-permute-start | bytes 983048 | tf_op jit(solution)/shard_map/ppermute | solution.py:352
  41.8 15.0 %collective-permute-start.11 = (bf16[2,128,640]{2,1,0:T(8,128)(2,1)}, bf16[2,128,640]{2,1,0:T(8,128)(2,1)S(1)}, u32[]{:S(2)}, u32[]{:S(2)}) collective-permute-start(bf16[2,128,640]{2,1,0:T(8,128)(2,1)} %collective-permute-done.4.refs_3_), channel_id=1, source_target_pairs={{0,16},{16,0},{1,17},{17,1},{2,18},{18,2},{3,19},{19,3},{4,20},{20... | collective-permute-start | bytes 983048 | tf_op jit(solution)/shard_map/ppermute | solution.py:352
  43.3 19.3 %collective-permute-start.9 = (bf16[640,256]{1,0:T(8,128)(2,1)}, bf16[640,256]{1,0:T(8,128)(2,1)}, u32[]{:S(2)}, u32[]{:S(2)}) collective-permute-start(bf16[640,256]{1,0:T(8,128)(2,1)} %collective-permute-done.7.refs_10_), channel_id=1, source_target_pairs={{2,0},{3,1},{4,6},{5,7},{10,8},{11,9},{12,14},{13,15},{18,16},{19,... | collective-permute-start | bytes 983048 | tf_op jit(solution)/shard_map/ppermute | solution.py:421
  44.6 18.0 %collective-permute-start.12 = (bf16[640,256]{1,0:T(8,128)(2,1)}, bf16[640,256]{1,0:T(8,128)(2,1)S(1)}, u32[]{:S(2)}, u32[]{:S(2)}) collective-permute-start(bf16[640,256]{1,0:T(8,128)(2,1)} %collective-permute-done.1.refs_8_), channel_id=1, source_target_pairs={{0,8},{8,0},{1,9},{9,1},{2,10},{10,2},{3,11},{11,3},{4,12},{12,4},... | collective-permute-start | bytes 983048 | tf_op jit(solution)/shard_map/ppermute | solution.py:349
  44.7 18.7 %collective-permute-start.13 = (bf16[640,256]{1,0:T(8,128)(2,1)}, bf16[640,256]{1,0:T(8,128)(2,1)}, u32[]{:S(2)}, u32[]{:S(2)}) collective-permute-start(bf16[640,256]{1,0:T(8,128)(2,1)} %collective-permute-done.8.refs_9_), channel_id=1, source_target_pairs={{0,8},{8,0},{1,9},{9,1},{2,10},{10,2},{3,11},{11,3},{4,12},{12,4},... | collective-permute-start | bytes 983048 | tf_op jit(solution)/shard_map/ppermute | solution.py:349
  45.2 0.6 copy-start.4
  55.3 7.3 %copy-start.13 = (bf16[2,128,640]{2,1,0:T(8,128)(2,1)}, bf16[2,128,640]{2,1,0:T(8,128)(2,1)S(1)}, u32[]{:S(2)}) copy-start(bf16[2,128,640]{2,1,0:T(8,128)(2,1)S(1)} %collective-permute-done.10.refs_4_) | copy-start | bytes 983044
  56.7 5.9 %copy-start.14 = (bf16[2,128,640]{2,1,0:T(8,128)(2,1)}, bf16[2,128,640]{2,1,0:T(8,128)(2,1)S(1)}, u32[]{:S(2)}) copy-start(bf16[2,128,640]{2,1,0:T(8,128)(2,1)S(1)} %collective-permute-done.11.refs_5_) | copy-start | bytes 983044
  62.6 0.8 copy-start.15
  63.4 1.0 copy-start.7
  67.4 23.8 %all-to-all-start.2 = ((bf16[8,384,128]{2,1,0:T(8,128)(2,1)}), bf16[8,384,128]{2,1,0:T(8,128)(2,1)S(1)}, u32[]{:S(2)}, u32[]{:S(2)}) async-start(bf16[8,384,128]{2,1,0:T(8,128)(2,1)} %get-tuple-element.72.refs_18_), calls=%async_computation.2 | async-start | bytes 1572864 | tf_op jit(solution)/shard_map/all_to_all | solution.py:464
  71.9 19.4 %copy-start.5 = (s32[8]{0:T(128)S(1)}, s32[8]{0:T(128)}, u32[]{:S(2)}) copy-start(s32[8]{0:T(128)} %get-tuple-element.70.after_ref.rows_here) | copy-start | bytes 100
  71.9 1.9 %collective-permute-start.14 = (bf16[640,256]{1,0:T(8,128)(2,1)}, bf16[640,256]{1,0:T(8,128)(2,1)S(1)}, u32[]{:S(2)}, u32[]{:S(2)}) collective-permute-start(bf16[640,256]{1,0:T(8,128)(2,1)} %collective-permute-done.7.refs_10_), channel_id=1, source_target_pairs={{0,8},{8,0},{1,9},{9,1},{2,10},{10,2},{3,11},{11,3},{4,12},{12,4},... | collective-permute-start | bytes 983048 | tf_op jit(solution)/shard_map/ppermute | solution.py:349
  71.9 2.3 %collective-permute-start.15 = (bf16[640,256]{1,0:T(8,128)(2,1)}, bf16[640,256]{1,0:T(8,128)(2,1)S(1)}, u32[]{:S(2)}, u32[]{:S(2)}) collective-permute-start(bf16[640,256]{1,0:T(8,128)(2,1)} %collective-permute-done.9.refs_11_), channel_id=1, source_target_pairs={{0,8},{8,0},{1,9},{9,1},{2,10},{10,2},{3,11},{11,3},{4,12},{12,4},... | collective-permute-start | bytes 983048 | tf_op jit(solution)/shard_map/ppermute | solution.py:349
  73.8 0.7 copy-start.16
  74.5 0.7 copy-start.17
  80.3 7.8 %collective-permute-start.16 = (bf16[128,512]{1,0:T(8,128)(2,1)}, bf16[128,512]{1,0:T(8,128)(2,1)S(1)}, u32[]{:S(2)}, u32[]{:S(2)}) collective-permute-start(bf16[128,512]{1,0:T(8,128)(2,1)} %get-tuple-element.81), channel_id=1, source_target_pairs={{0,1},{1,0},{2,3},{3,2},{4,5},{5,4},{6,7},{7,6},{8,9},{9,8},{10,11... | collective-permute-start | bytes 393224 | tf_op jit(solution)/shard_map/ppermute | solution.py:346
  82.3 5.8 %collective-permute-start.17 = (bf16[128,512]{1,0:T(8,128)(2,1)}, bf16[128,512]{1,0:T(8,128)(2,1)S(1)}, u32[]{:S(2)}, u32[]{:S(2)}) collective-permute-start(bf16[128,512]{1,0:T(8,128)(2,1)} %get-tuple-element.82), channel_id=1, source_target_pairs={{0,16},{16,0},{1,17},{17,1},{2,18},{18,2},{3,19},{19,3},{4,20},{20... | collective-permute-start | bytes 393224 | tf_op jit(solution)/shard_map/ppermute | solution.py:352
  83.1 7.7 %collective-permute-start.18 = (bf16[128,512]{1,0:T(8,128)(2,1)}, bf16[128,512]{1,0:T(8,128)(2,1)S(1)}, u32[]{:S(2)}, u32[]{:S(2)}) collective-permute-start(bf16[128,512]{1,0:T(8,128)(2,1)} %get-tuple-element.83), channel_id=1, source_target_pairs={{0,17},{1,16},{2,19},{3,18},{4,21},{5,20},{6,23},{7,22},{16,1},{17... | collective-permute-start | bytes 393224 | tf_op jit(solution)/shard_map/ppermute | solution.py:465
  91.2 2.4 %collective-permute-start.20 = (bf16[8,384,128]{2,1,0:T(8,128)(2,1)S(1)}, bf16[8,384,128]{2,1,0:T(8,128)(2,1)S(1)}, u32[]{:S(2)}, u32[]{:S(2)}) collective-permute-start(bf16[8,384,128]{2,1,0:T(8,128)(2,1)S(1)} %all-to-all-done.2.rest_0_), channel_id=1, source_target_pairs={{0,8},{8,0},{1,9},{9,1},{2,10},{10,2},{3,11},{11,3},{4,12},{12,4},... | collective-permute-start | bytes 2359304 | tf_op jit(solution)/shard_map/ppermute | solution.py:349
  91.2 2.3 %collective-permute-start.19 = (s32[8]{0:T(128)S(1)}, s32[8]{0:T(128)S(1)}, u32[]{:S(2)}, u32[]{:S(2)}) collective-permute-start(s32[8]{0:T(128)S(1)} %copy-done.5), channel_id=1, source_target_pairs={{0,8},{8,0},{1,9},{9,1},{2,10},{10,2},{3,11},{11,3},{4,12},{12,4},... | collective-permute-start | bytes 104 | tf_op jit(solution)/shard_map/ppermute | solution.py:349
  93.6 3.6 %copy-start.1 = (bf16[640,512]{1,0:T(8,128)(2,1)S(1)}, bf16[640,512]{1,0:T(8,128)(2,1)}, u32[]{:S(2)}) copy-start(bf16[640,512]{1,0:T(8,128)(2,1)} %param.9) | copy-start | bytes 1966084

commit v17 on v15

--- a/solution.py
+++ b/solution.py
@@ -99,10 +99,6 @@
     return mixed, grad_down, grad_up
 
 
-def row_kernel(block_ref, slot_ref, out_ref):
-    out_ref[...] = jnp.full(out_ref.shape, slot_ref[block_ref[0]], jnp.int32)
-
-
 def split_kernel(x_ref, mine_ref, *theirs_refs):
     inner = lax.axis_index("tensor") % 2
     outer, rows, width = mine_ref.shape
@@ -131,12 +127,12 @@
         copy.wait()
 
 
-def gather_kernel(asked, down_ref, up_ref, out_ref, rows_ref, down_buf, up_buf, flats, built, sems):
+def gather_kernel(asked, slot_of, down_ref, up_ref, out_ref, rows_ref, down_buf, up_buf, flats, built, sems):
     count, down_chunks, up_chunks = down_buf.shape[0], down_buf.shape[1], up_buf.shape[1]
     across = up_chunks // 8
 
     def copies(t):
-        tile = asked[t, 0, 0] // TILE_ROWS
+        tile = slot_of[asked[t, 0, 0]] // TILE_ROWS
         return (
             pltpu.make_async_copy(down_ref.at[tile], down_buf.at[t], sems.at[0, t]),
             pltpu.make_async_copy(up_ref.at[tile], up_buf.at[t], sems.at[1, t]),
@@ -147,7 +143,7 @@
         down, up, _ = copies(t)
         down.start()
         up.start()
-        rows_ref[t] = asked[t, 0, 0]
+        rows_ref[t] = slot_of[asked[t, 0, 0]]
 
     def one(t, flat):
         down, up, leave = copies(t)
@@ -158,7 +154,7 @@
         down.wait()
         for j in range(down_chunks):
             flat[j * 8:j * 8 + 8, :] = down_buf[t, j].astype(jnp.float32)
-        sub = asked[t, 0, 0] % TILE_ROWS
+        sub = slot_of[asked[t, 0, 0]] % TILE_ROWS
         built[t] = flat[pl.ds(sub, down_chunks + up_chunks, stride=8), :].astype(jnp.bfloat16)
         leave.start()
 
@@ -308,17 +304,17 @@
                     move(halves[2 * b + h].at[order[k] % each], place, sems.at[k, 2 + b])
         for h in range(2):
             place, sem = w_buf.at[columns, pl.ds(h * width, width)], sems.at[k, 4 + h]
-            if k < 2:
+            if k < 3:
                 move(w_from[h * pieces + k], place, sem)
                 continue
 
             @pl.when(inside)
             def _():
-                move(w_from[h * pieces + 2 * k - 2], place, sem)
+                move(w_from[h * pieces + k], place, sem)
 
             @pl.when(jnp.logical_not(inside))
             def _():
-                move(w_from[h * pieces + 2 * k - 1], place, sem)
+                move(w_from[h * pieces + k + 1], place, sem)
 
     for k in range(outer):
         fetch(k, True)
@@ -351,12 +347,9 @@
     def other_part(value):
         return lax.ppermute(value, "parts", [(a, parts - 1 - a) for a in range(parts)])
 
-    row = pl.pallas_call(
-        row_kernel, out_shape=jax.ShapeDtypeStruct((group, 1, LANES), jnp.int32),
-        in_specs=[SMEM, SMEM], out_specs=VMEM, name="own_row",
-    )(block_adapter, adapter_slot)
-    asked = lax.all_to_all(row, "tensor", 0, 0)
-    split_from, half_from, row = lax.optimization_barrier((tokens, frozen_value, row))
+    own = jnp.broadcast_to(block_adapter, (group, 1, LANES))
+    asked = lax.all_to_all(own, "tensor", 0, 0)
+    split_from, half_from, own = lax.optimization_barrier((tokens, frozen_value, own))
 
     width = frozen_value.shape[1] // parts
     half = lax.dynamic_slice_in_dim(half_from, part * width, width, axis=1)
@@ -385,7 +378,6 @@
     over = lax.ppermute(half, "tensor", middle)
     near, over, asked, x_theirs, xs = lax.optimization_barrier((near, over, asked, x_theirs, xs))
     x_far.append(exchange(x_theirs[1], 1))
-    y_far = [other_part(x_far[0])]
     over_near = lax.ppermute(near, "tensor", middle)
     passed = lax.ppermute(over, "tensor", ends)
     pieces = jax.ShapeDtypeStruct((group, down_chunks + up_chunks, LANES), jnp.bfloat16)
@@ -396,7 +388,7 @@
     sent, rows = pl.pallas_call(
         gather_kernel,
         out_shape=(pieces, jax.ShapeDtypeStruct((group,), jnp.int32)),
-        in_specs=[SMEM, ANY, ANY],
+        in_specs=[SMEM, SMEM, ANY, ANY],
         out_specs=(ANY, SMEM),
         scratch_shapes=[
             pltpu.VMEM((group, down_chunks, TILE_ROWS, LANES), jnp.bfloat16),
@@ -408,15 +400,16 @@
         compiler_params=WIDE,
         cost_estimate=cost(read=40 << 20),
         name="pick_panels",
-    )(asked, tiles(down_store), tiles(up_store))
-    sent, rows, x_far, y_far, y_mine, half, near, over, over_near, passed = lax.optimization_barrier(
-        (sent, rows, x_far, y_far, y_mine, half, near, over, over_near, passed)
+    )(asked, adapter_slot, tiles(down_store), tiles(up_store))
+    sent, rows, x_far, y_mine, half, near, over, over_near, passed = lax.optimization_barrier(
+        (sent, rows, x_far, y_mine, half, near, over, over_near, passed)
     )
     panels = lax.all_to_all(sent, "tensor", 0, 0)
     rows_core = other_core(rows)
-    y_far.append(other_part(x_far[1]))
+    y_far = [other_part(piece) for piece in x_far]
     passed_near = lax.ppermute(over_near, "tensor", ends)
-    quarter = [half, near, over, passed, over_near]
+    inside = (z == 1) | (z == 2)
+    quarter = [half, near, jnp.where(inside, over, passed)]
     quarter_core = [other_core(w) for w in quarter]
 
     owned_groups = ADAPTERS // lax.axis_size("dp") // 8
@@ -428,7 +421,7 @@
         scratch_shapes=[pltpu.VMEM((up_chunks, 8, 1, LANES), jnp.float32), pltpu.SemaphoreType.DMA((2,))],
         compiler_params=LIMIT, cost_estimate=cost(read=28 << 20), name="clear_rows",
     )(rows)
-    panels, passed_near, y_far, quarter_core = lax.optimization_barrier((panels, passed_near, y_far, quarter_core))
+    panels, quarter_core = lax.optimization_barrier((panels, quarter_core))
 
     terms, lifted = pl.pallas_call(
         functools.partial(adapter_kernel, group, down_chunks),
@@ -440,10 +433,11 @@
         cost_estimate=cost(flops=3 << 30, read=8 << 20),
         name="adapter",
     )(xs, cotangent, panels, cleared)
-    _, passed_near = lax.optimization_barrier((terms, passed_near))
-    quarters = quarter + [passed_near] + quarter_core + [other_core(passed_near)]
+    _, over_near, passed_near, y_far = lax.optimization_barrier((terms, over_near, passed_near, y_far))
+    last = [over_near, passed_near]
+    quarters = quarter + last + quarter_core + [other_core(w) for w in last]
     sums = [jax.ShapeDtypeStruct((token_rows, parts * width), kind) for kind in (jnp.float32,) + (jnp.bfloat16,) * 3]
-    own, to_part, to_inner, to_both = pl.pallas_call(
+    kept, to_part, to_inner, to_both = pl.pallas_call(
         base_kernel,
         out_shape=sums,
         in_specs=[ANY] * (7 + len(quarters)),
@@ -485,7 +479,7 @@
     grad_up = grad_up.reshape(owned_groups, up_chunks, 8, LANES).transpose(0, 2, 1, 3)
 
     arrived = [a.astype(jnp.float32) for a in arrived]
-    kept, got = own + arrived[0], arrived[1] + arrived[2]
+    kept, got = kept + arrived[0], arrived[1] + arrived[2]
     quarters = [[c[:, :width], c[:, width:]] for c in (kept, got)]
 
     def pick_quarter(c, a):

time: 99 us -> 109 us (1.10)
  waiting for transfers between devices: 22.3 us -> 34.8 us
  Pallas kernels: 31.1 us -> 29.5 us
    ppermute x4, waiting for transfers between devices: 7.8 us -> 14.8 us  [other_part(): lax.ppermute(value, 'parts', [(a, parts - 1 - a) for a in range(parts)])]
    all_to_all x1, waiting for transfers between devices: 0.01 us -> 5.71 us  [fast_body(): panels = lax.all_to_all(sent, 'tensor', 0, 0)]
    ppermute x1, waiting for transfers between devices: 1.21 us -> 5.9 us  [fast_body(): passed_near = lax.ppermute(over_near, 'tensor', ends)]
    ppermute x1, waiting for transfers between devices: 3.98 us -> 0.01 us  [fast_body(): lax.ppermute(to_both, ('parts', 'tensor'), opposite)]
    all_to_all x1, starting transfers between devices: 6.31 us -> 3.55 us  [fast_body(): back = lax.all_to_all(terms, 'tensor', 0, 0)]
    ppermute x1, waiting for transfers between devices: 0.28 us -> 2.61 us  [fast_body(): passed = lax.ppermute(over, 'tensor', ends)]
    all_to_all x1, waiting for transfers between devices: 2.45 us -> 0.5 us  [fast_body(): asked = lax.all_to_all(own, 'tensor', 0, 0)]
    ppermute x1, starting transfers between devices: 0.03 us -> 1.88 us  [fast_body(): lax.ppermute(to_both, ('parts', 'tensor'), opposite)]
  transfers between devices with their start and end apart: 24 -> 23, of which waited for: 9 -> 10; matrix products, arithmetic and copies ran while one was open for 2% -> 2% of each run, Pallas kernels for 24% -> 22%
where the time goes in v17:
time: 109 us; the launch traced here: 107 us
  waiting for transfers between devices  34.8 us (32%)
  starting transfers between devices  33.8 us (31%)
  Pallas kernels  29.5 us (27%)
  local copies, waits for them, and re-layouts  5.81 us (5%)
  other arithmetic  1.85 us (2%)
  between operations  1.66 us (2%)
    ppermute x4, waiting for transfers between devices, other_part(): lax.ppermute(value, 'parts', [(a, parts - 1 - a) for a in range(parts)])  14.8 us
    ppermute x4, starting transfers between devices, exchange(): return lax.ppermute(value, 'tensor', [(t, t ^ s) for t in range(group)])  9.69 us
    pallas_call x1, Pallas kernels, fast_body(): pl.pallas_call(zero_kernel, out_shape=(down_shape, up_shape, token), in_s...  9.48 us
    ppermute x1, waiting for transfers between devices, fast_body(): passed_near = lax.ppermute(over_near, 'tensor', ends)  5.9 us
    all_to_all x1, waiting for transfers between devices, fast_body(): panels = lax.all_to_all(sent, 'tensor', 0, 0)  5.71 us
    pallas_call x1, Pallas kernels, fast_body(): pl.pallas_call(gather_kernel, out_shape=(pieces, jax.ShapeDtypeStruct((gr...  5.28 us
    unnamed x40, local copies, waits for them, and re-layouts  5.19 us
    pallas_call x1, Pallas kernels, fast_body(): pl.pallas_call(base_kernel, out_shape=sums, in_specs=[ANY] * (7 + len(qua...  5.02 us
  transfers between devices with their start and end apart: 23, of which 10 were waited for; matrix products, arithmetic and copies ran while one was open for 2% of the time, Pallas kernels for 22%

profile of v17, /device:TPU:0, one launch (start us, length us, event | category | flops | bytes accessed | tf_op | source)
XLA Modules:
  0.0 107.5 jit_solution(11129411072457733181)
XLA Ops:
  0.6 0.0 copy-start
  1.4 0.6 broadcast_in_dim.2
  2.0 0.7 collective-permute-start.1
  2.7 5.9 %collective-permute-start = (bf16[640,256]{1,0:T(8,128)(2,1)S(1)}, bf16[640,256]{1,0:T(8,128)(2,1)}, u32[]{:S(2)}, u32[]{:S(2)}) collective-permute-start(bf16[640,256]{1,0:T(8,128)(2,1)S(1)} %constant_dynamic-slice_fusion.refs_6_), channel_id=1, source_target_pairs={{0,2},{1,3},{2,0},{3,1},{4,6},{5,7},{6,4},{7,5},{8,10},{9,11},{10,... | collective-permute-start | bytes 983048 | tf_op jit(solution)/shard_map/ppermute | solution.py:342
  8.6 1.3 %copy-done.2 = bf16[128,5120]{1,0:T(8,128)(2,1)S(1)} copy-done((bf16[128,5120]{1,0:T(8,128)(2,1)S(1)}, bf16[128,5120]{1,0:T(8,128)(2,1)}, u32[]{:S(2)}) %copy-start.2) | copy-done | bytes 1310744
  9.9 0.1 split_tokens.1
  10.0 1.6 %collective-permute-start.4 = (bf16[4,128,640]{2,1,0:T(8,128)(2,1)S(1)}, bf16[4,128,640]{2,1,0:T(8,128)(2,1)}, u32[]{:S(2)}, u32[]{:S(2)}) collective-permute-start(bf16[4,128,640]{2,1,0:T(8,128)(2,1)S(1)} %get-tuple-element.49.refs_0_), channel_id=1, source_target_pairs={{0,16},{16,0},{1,17},{17,1},{2,18},{18,2},{3,19},{19,3},{4,20},{20... | collective-permute-start | bytes 1966088 | tf_op jit(solution)/shard_map/ppermute | solution.py:348
  11.6 3.6 %all-to-all-start = ((s32[8,1,128]{2,1,0:T(1,128)}), s32[8,1,128]{2,1,0:T(1,128)S(1)}, u32[]{:S(2)}, u32[]{:S(2)}) async-start(s32[8,1,128]{2,1,0:T(1,128)} %broadcast_in_dim.2), calls=%async_computation | async-start | bytes 8192 | tf_op jit(solution)/shard_map/all_to_all | solution.py:351
  15.2 2.0 %collective-permute-start.2 = (bf16[2,128,640]{2,1,0:T(8,128)(2,1)S(1)}, bf16[2,128,640]{2,1,0:T(8,128)(2,1)}, u32[]{:S(2)}, u32[]{:S(2)}) collective-permute-start(bf16[2,128,640]{2,1,0:T(8,128)(2,1)S(1)} %get-tuple-element.51), channel_id=1, source_target_pairs={{0,1},{1,0},{2,3},{3,2},{4,5},{5,4},{6,7},{7,6},{8,9},{9,8},{10,11... | collective-permute-start | bytes 983048 | tf_op jit(solution)/shard_map/ppermute | solution.py:342
  17.2 3.9 %pair_columns.1.xs_ref = bf16[8,256,320]{2,1,0:T(8,128)(2,1)} custom-call(bf16[128,5120]{1,0:T(8,128)(2,1)} %x_ref.1), custom_call_target="tpu_custom_call" | custom-call | bytes 134217728 | tf_op jit(solution)/shard_map/pair_columns/pallas_call | solution.py:365
  21.0 0.5 all-to-all-done.asked
  21.5 0.0 collective-permute-done.1
  21.5 0.0 collective-permute-done.refs_7_
  21.6 0.6 collective-permute-start.3
  22.2 1.4 %collective-permute-start.5 = (bf16[640,256]{1,0:T(8,128)(2,1)}, bf16[640,256]{1,0:T(8,128)(2,1)}, u32[]{:S(2)}, u32[]{:S(2)}) collective-permute-start(bf16[640,256]{1,0:T(8,128)(2,1)} %collective-permute-done.refs_7_), channel_id=1, source_target_pairs={{2,4},{3,5},{4,2},{5,3},{10,12},{11,13},{12,10},{13,11},{18,20},{1... | collective-permute-start | bytes 983048 | tf_op jit(solution)/shard_map/ppermute | solution.py:381
  23.6 1.3 %collective-permute-start.6 = (bf16[640,256]{1,0:T(8,128)(2,1)S(1)}, bf16[640,256]{1,0:T(8,128)(2,1)S(1)}, u32[]{:S(2)}, u32[]{:S(2)}) collective-permute-start(bf16[640,256]{1,0:T(8,128)(2,1)S(1)} %collective-permute-done.1), channel_id=1, source_target_pairs={{2,0},{3,1},{4,6},{5,7},{10,8},{11,9},{12,14},{13,15},{18,16},{19,... | collective-permute-start | bytes 983048 | tf_op jit(solution)/shard_map/ppermute | solution.py:382
  24.9 5.3 %pick_panels.1 = (bf16[8,384,128]{2,1,0:T(8,128)(2,1)}, s32[8]{0:T(128)}) custom-call(s32[8,1,128]{2,1,0:T(1,128)} %copy-done.10, s32[256]{0:T(256)} %slot_of.1, bf16[32,320,8,128]{3,2,1,0:T(8,128)(2,1)} %bitcast.18, bf16[32,64,8,128]{3,2,1,0:T(8,128)(2,1)} %bitcast.20), custom_call_target="tpu_custom_call" | custom-call | bytes 41943040 | tf_op jit(solution)/shard_map/pick_panels/pallas_call | solution.py:388
  30.2 0.0 collective-permute-done.2.refs_2_
  30.2 0.0 collective-permute-done.4.refs_1_
  30.2 0.5 collective-permute-done.3.refs_3_
  30.7 0.0 collective-permute-done.5.refs_9_
  30.7 2.6 %collective-permute-done.6 = bf16[640,256]{1,0:T(8,128)(2,1)S(1)} collective-permute-done((bf16[640,256]{1,0:T(8,128)(2,1)S(1)}, bf16[640,256]{1,0:T(8,128)(2,1)S(1)}, u32[]{:S(2)}, u32[]{:S(2)}) %collective-permute-start.6) | collective-permute-done | bytes 327712 | tf_op jit(solution)/shard_map/ppermute | solution.py:382
  33.3 4.6 %all-to-all-start.1 = ((bf16[8,384,128]{2,1,0:T(8,128)(2,1)}), bf16[8,384,128]{2,1,0:T(8,128)(2,1)S(1)}, u32[]{:S(2)}, u32[]{:S(2)}) async-start(bf16[8,384,128]{2,1,0:T(8,128)(2,1)} %get-tuple-element.63), calls=%async_computation.1 | async-start | bytes 1572864 | tf_op jit(solution)/shard_map/all_to_all | solution.py:407
  38.0 0.1 collective-permute-start.9
  38.1 0.5 collective-permute-start.7
  38.6 0.1 collective-permute-start.8
  38.6 0.7 copy-done.4
  39.3 9.5 %clear_rows.1 = (f32[16,320,8,1,128]{4,3,2,1,0:T(1,128)}, f32[16,64,8,1,128]{4,3,2,1,0:T(1,128)}, s32[1]{0:T(128)}) custom-call(s32[8]{0:T(128)S(1)} %copy-done.4), custom_call_target="tpu_custom_call" | custom-call | bytes 29360128 | tf_op jit(solution)/shard_map/clear_rows/pallas_call | solution.py:418
  48.8 0.0 collective-permute-done.9.refs_13_
  48.8 0.0 collective-permute-done.7.refs_11_
  48.8 0.8 copy-done.14
  49.6 0.0 collective-permute-done.8.refs_12_
  49.6 5.7 %all-to-all-done.1.pieces = bf16[8,384,128]{2,1,0:T(8,128)(2,1)S(1)} async-done(((bf16[8,384,128]{2,1,0:T(8,128)(2,1)}), bf16[8,384,128]{2,1,0:T(8,128)(2,1)S(1)}, u32[]{:S(2)}, u32[]{:S(2)}) %all-to-all-start.1) | async-done | bytes 786464 | tf_op jit(solution)/shard_map/all_to_all | solution.py:407
  55.3 0.0 copy-start.7
  55.4 0.9 copy-done.7
  56.3 3.0 %adapter.1 = (bf16[8,384,128]{2,1,0:T(8,128)(2,1)}, f32[128,1024]{1,0:T(8,128)S(1)}) custom-call(bf16[8,256,320]{2,1,0:T(8,128)(2,1)S(1)} %copy-done.3, bf16[128,1024]{1,0:T(8,128)(2,1)S(1)} %copy-done.7, bf16[8,384,128]{2,1,0:T(8,128)(2,1)S(1)} %all-to-all-done.1.pieces, s32[1]{0:T(128)} %get-tuple-element.70._), custom_call_target="tpu_custom_call" | custom-call | flops 3221225472 | bytes 8388608 | tf_op jit(solution)/shard_map/adapter/pallas_call | solution.py:426
  59.3 3.5 %all-to-all-start.2 = ((bf16[8,384,128]{2,1,0:T(8,128)(2,1)}), bf16[8,384,128]{2,1,0:T(8,128)(2,1)S(1)}, u32[]{:S(2)}, u32[]{:S(2)}) async-start(bf16[8,384,128]{2,1,0:T(8,128)(2,1)} %get-tuple-element.71.refs_16_), calls=%async_computation.2 | async-start | bytes 1572864 | tf_op jit(solution)/shard_map/all_to_all | solution.py:455
  62.9 0.6 collective-permute-start.11
  63.5 1.5 %collective-permute-start.12 = (bf16[2,128,640]{2,1,0:T(8,128)(2,1)S(1)}, bf16[2,128,640]{2,1,0:T(8,128)(2,1)S(1)}, u32[]{:S(2)}, u32[]{:S(2)}) collective-permute-start(bf16[2,128,640]{2,1,0:T(8,128)(2,1)S(1)} %copy-done.12), channel_id=1, source_target_pairs={{0,16},{16,0},{1,17},{17,1},{2,18},{18,2},{3,19},{19,3},{4,20},{20... | collective-permute-start | bytes 983048 | tf_op jit(solution)/shard_map/ppermute | solution.py:348
  65.0 1.3 %collective-permute-start.10 = (bf16[640,256]{1,0:T(8,128)(2,1)}, bf16[640,256]{1,0:T(8,128)(2,1)S(1)}, u32[]{:S(2)}, u32[]{:S(2)}) collective-permute-start(bf16[640,256]{1,0:T(8,128)(2,1)} %collective-permute-done.5.refs_9_), channel_id=1, source_target_pairs={{2,0},{3,1},{4,6},{5,7},{10,8},{11,9},{12,14},{13,15},{18,16},{19,... | collective-permute-start | bytes 983048 | tf_op jit(solution)/shard_map/ppermute | solution.py:410
  66.3 7.5 %collective-permute-done.11.refs_4_ = bf16[2,128,640]{2,1,0:T(8,128)(2,1)S(1)} collective-permute-done((bf16[2,128,640]{2,1,0:T(8,128)(2,1)}, bf16[2,128,640]{2,1,0:T(8,128)(2,1)S(1)}, u32[]{:S(2)}, u32[]{:S(2)}) %collective-permute-start.11) | collective-permute-done | bytes 327712 | tf_op jit(solution)/shard_map/ppermute | solution.py:348
  73.8 4.4 %collective-permute-done.12.refs_5_ = bf16[2,128,640]{2,1,0:T(8,128)(2,1)S(1)} collective-permute-done((bf16[2,128,640]{2,1,0:T(8,128)(2,1)S(1)}, bf16[2,128,640]{2,1,0:T(8,128)(2,1)S(1)}, u32[]{:S(2)}, u32[]{:S(2)}) %collective-permute-start.12) | collective-permute-done | bytes 327712 | tf_op jit(solution)/shard_map/ppermute | solution.py:348
  78.3 5.9 %collective-permute-done.10.refs_10_ = bf16[640,256]{1,0:T(8,128)(2,1)S(1)} collective-permute-done((bf16[640,256]{1,0:T(8,128)(2,1)}, bf16[640,256]{1,0:T(8,128)(2,1)S(1)}, u32[]{:S(2)}, u32[]{:S(2)}) %collective-permute-start.10) | collective-permute-done | bytes 327712 | tf_op jit(solution)/shard_map/ppermute | solution.py:410
  84.2 0.0 collective-permute-start.13
  84.2 0.5 collective-permute-start.14
  84.7 1.8 %collective-permute-done.13.refs_14_ = bf16[640,256]{1,0:T(8,128)(2,1)S(1)} collective-permute-done((bf16[640,256]{1,0:T(8,128)(2,1)}, bf16[640,256]{1,0:T(8,128)(2,1)S(1)}, u32[]{:S(2)}, u32[]{:S(2)}) %collective-permute-start.13) | collective-permute-done | bytes 327712 | tf_op jit(solution)/shard_map/ppermute | solution.py:345
  86.4 0.0 collective-permute-done.14.refs_15_
  86.5 0.7 copy-done.18
  87.2 0.7 copy-done.19
  87.9 5.0 %frozen_part.1 = (f32[128,512]{1,0:T(8,128)}, bf16[128,512]{1,0:T(8,128)(2,1)}, bf16[128,512]{1,0:T(8,128)(2,1)}, bf16[128,512]{1,0:T(8,128)(2,1)}) custom-call(bf16[4,128,640]{2,1,0:T(8,128)(2,1)} %copy-done.6, bf16[4,128,640]{2,1,0:T(8,128)(2,1)} %collective-permute-done.4.refs_1_, bf16[2,128,640]{2,1,0:T(8,128)(2,1)} %collective-permute-done.2.refs_2_, ...), custom_call_target="tpu_custom_call" | custom-call | flops 4294967296 | bytes 8388608 | tf_op jit(solution)/shard_map/frozen_part/pallas_call | solution.py:440
  92.9 1.2 %collective-permute-start.15 = (bf16[128,512]{1,0:T(8,128)(2,1)}, bf16[128,512]{1,0:T(8,128)(2,1)S(1)}, u32[]{:S(2)}, u32[]{:S(2)}) collective-permute-start(bf16[128,512]{1,0:T(8,128)(2,1)} %get-tuple-element.81), channel_id=1, source_target_pairs={{0,1},{1,0},{2,3},{3,2},{4,5},{5,4},{6,7},{7,6},{8,9},{9,8},{10,11... | collective-permute-start | bytes 393224 | tf_op jit(solution)/shard_map/ppermute | solution.py:342
  94.1 0.5 collective-permute-start.16
  94.6 1.9 %collective-permute-start.17 = (bf16[128,512]{1,0:T(8,128)(2,1)}, bf16[128,512]{1,0:T(8,128)(2,1)S(1)}, u32[]{:S(2)}, u32[]{:S(2)}) collective-permute-start(bf16[128,512]{1,0:T(8,128)(2,1)} %get-tuple-element.83), channel_id=1, source_target_pairs={{0,17},{1,16},{2,19},{3,18},{4,21},{5,20},{6,23},{7,22},{16,1},{17... | collective-permute-start | bytes 393224 | tf_op jit(solution)/shard_map/ppermute | solution.py:456
  96.5 3.0 %collective-permute-done.15 = bf16[128,512]{1,0:T(8,128)(2,1)S(1)} collective-permute-done((bf16[128,512]{1,0:T(8,128)(2,1)}, bf16[128,512]{1,0:T(8,128)(2,1)S(1)}, u32[]{:S(2)}, u32[]{:S(2)}) %collective-permute-start.15) | collective-permute-done | bytes 131104 | tf_op jit(solution)/shard_map/ppermute | solution.py:342
  99.5 2.9 %collective-permute-done.16 = bf16[128,512]{1,0:T(8,128)(2,1)S(1)} collective-permute-done((bf16[128,512]{1,0:T(8,128)(2,1)}, bf16[128,512]{1,0:T(8,128)(2,1)S(1)}, u32[]{:S(2)}, u32[]{:S(2)}) %collective-permute-start.16) | collective-permute-done | bytes 131104 | tf_op jit(solution)/shard_map/ppermute | solution.py:348
  102.3 0.0 collective-permute-done.17
  102.4 0.0 all-to-all-done.2.rest_0_
  102.4 0.0 collective-permute-start.19
  102.4 0.5 collective-permute-start.18
  102.9 1.0 convert_add_fusion
  103.9 0.8 fusion
  104.7 0.0 collective-permute-done.18.rows_core
  104.7 0.0 collective-permute-done.19.rest_1_
  104.7 2.8 %place_rows.1 = (f32[16,320,8,1,128]{4,3,2,1,0:T(1,128)}, f32[16,64,8,1,128]{4,3,2,1,0:T(1,128)}) custom-call(s32[8]{0:T(128)S(1)} %copy-done.5, s32[8]{0:T(128)S(1)} %collective-permute-done.18.rows_core, bf16[8,384,128]{2,1,0:T(8,128)(2,1)S(1)} %all-to-all-done.2.rest_0_, ...), custom_call_target="tpu_custom_call", output_to_operand_aliasing={{0}: (4, {}), {1}: (5, {})} | custom-call | bytes 16777216 | tf_op jit(solution)/shard_map/place_rows/pallas_call | solution.py:460
  (35 shorter events, 0.2 us)
Async XLA Ops:
  0.6 1.3 %copy-start = (bf16[640,512]{1,0:T(8,128)(2,1)S(1)}, bf16[640,512]{1,0:T(8,128)(2,1)}, u32[]{:S(2)}) copy-start(bf16[640,512]{1,0:T(8,128)(2,1)} %param.9) | copy-start | bytes 1966084
  2.0 22.9 %copy-start.9 = (bf16[640,256]{1,0:T(8,128)(2,1)}, bf16[640,256]{1,0:T(8,128)(2,1)S(1)}, u32[]{:S(2)}) copy-start(bf16[640,256]{1,0:T(8,128)(2,1)S(1)} %constant_dynamic-slice_fusion.refs_6_) | copy-start | bytes 983044
  2.0 19.6 %collective-permute-start.1 = (bf16[640,256]{1,0:T(8,128)(2,1)S(1)}, bf16[640,256]{1,0:T(8,128)(2,1)S(1)}, u32[]{:S(2)}, u32[]{:S(2)}) collective-permute-start(bf16[640,256]{1,0:T(8,128)(2,1)S(1)} %constant_dynamic-slice_fusion.refs_6_), channel_id=1, source_target_pairs={{2,4},{3,5},{4,2},{5,3},{10,12},{11,13},{12,10},{13,11},{18,20},{1... | collective-permute-start | bytes 983048 | tf_op jit(solution)/shard_map/ppermute | solution.py:378
  2.7 18.9 %collective-permute-start = (bf16[640,256]{1,0:T(8,128)(2,1)S(1)}, bf16[640,256]{1,0:T(8,128)(2,1)}, u32[]{:S(2)}, u32[]{:S(2)}) collective-permute-start(bf16[640,256]{1,0:T(8,128)(2,1)S(1)} %constant_dynamic-slice_fusion.refs_6_), channel_id=1, source_target_pairs={{0,2},{1,3},{2,0},{3,1},{4,6},{5,7},{6,4},{7,5},{8,10},{9,11},{10,... | collective-permute-start | bytes 983048 | tf_op jit(solution)/shard_map/ppermute | solution.py:342
  8.6 1.3 %copy-start.2 = (bf16[128,5120]{1,0:T(8,128)(2,1)S(1)}, bf16[128,5120]{1,0:T(8,128)(2,1)}, u32[]{:S(2)}) copy-start(bf16[128,5120]{1,0:T(8,128)(2,1)} %x_ref.1) | copy-start | bytes 3932164
  10.0 20.2 %copy-start.6 = (bf16[4,128,640]{2,1,0:T(8,128)(2,1)}, bf16[4,128,640]{2,1,0:T(8,128)(2,1)S(1)}, u32[]{:S(2)}) copy-start(bf16[4,128,640]{2,1,0:T(8,128)(2,1)S(1)} %get-tuple-element.49.refs_0_) | copy-start | bytes 1966084
  10.0 20.2 %collective-permute-start.4 = (bf16[4,128,640]{2,1,0:T(8,128)(2,1)S(1)}, bf16[4,128,640]{2,1,0:T(8,128)(2,1)}, u32[]{:S(2)}, u32[]{:S(2)}) collective-permute-start(bf16[4,128,640]{2,1,0:T(8,128)(2,1)S(1)} %get-tuple-element.49.refs_0_), channel_id=1, source_target_pairs={{0,16},{16,0},{1,17},{17,1},{2,18},{18,2},{3,19},{19,3},{4,20},{20... | collective-permute-start | bytes 1966088 | tf_op jit(solution)/shard_map/ppermute | solution.py:348
  11.6 9.9 %all-to-all-start = ((s32[8,1,128]{2,1,0:T(1,128)}), s32[8,1,128]{2,1,0:T(1,128)S(1)}, u32[]{:S(2)}, u32[]{:S(2)}) async-start(s32[8,1,128]{2,1,0:T(1,128)} %broadcast_in_dim.2), calls=%async_computation | async-start | bytes 8192 | tf_op jit(solution)/shard_map/all_to_all | solution.py:351
  15.2 15.0 %collective-permute-start.2 = (bf16[2,128,640]{2,1,0:T(8,128)(2,1)S(1)}, bf16[2,128,640]{2,1,0:T(8,128)(2,1)}, u32[]{:S(2)}, u32[]{:S(2)}) collective-permute-start(bf16[2,128,640]{2,1,0:T(8,128)(2,1)S(1)} %get-tuple-element.51), channel_id=1, source_target_pairs={{0,1},{1,0},{2,3},{3,2},{4,5},{5,4},{6,7},{7,6},{8,9},{9,8},{10,11... | collective-permute-start | bytes 983048 | tf_op jit(solution)/shard_map/ppermute | solution.py:342
  21.5 3.3 %copy-start.10 = (s32[8,1,128]{2,1,0:T(1,128)}, s32[8,1,128]{2,1,0:T(1,128)S(1)}, u32[]{:S(2)}) copy-start(s32[8,1,128]{2,1,0:T(1,128)S(1)} %all-to-all-done.asked) | copy-start | bytes 12292
  21.6 9.1 %collective-permute-start.3 = (bf16[2,128,640]{2,1,0:T(8,128)(2,1)S(1)}, bf16[2,128,640]{2,1,0:T(8,128)(2,1)S(1)}, u32[]{:S(2)}, u32[]{:S(2)}) collective-permute-start(bf16[2,128,640]{2,1,0:T(8,128)(2,1)S(1)} %get-tuple-element.56), channel_id=1, source_target_pairs={{0,1},{1,0},{2,3},{3,2},{4,5},{5,4},{6,7},{7,6},{8,9},{9,8},{10,11... | collective-permute-start | bytes 983048 | tf_op jit(solution)/shard_map/ppermute | solution.py:342
  22.2 8.5 %collective-permute-start.5 = (bf16[640,256]{1,0:T(8,128)(2,1)}, bf16[640,256]{1,0:T(8,128)(2,1)}, u32[]{:S(2)}, u32[]{:S(2)}) collective-permute-start(bf16[640,256]{1,0:T(8,128)(2,1)} %collective-permute-done.refs_7_), channel_id=1, source_target_pairs={{2,4},{3,5},{4,2},{5,3},{10,12},{11,13},{12,10},{13,11},{18,20},{1... | collective-permute-start | bytes 983048 | tf_op jit(solution)/shard_map/ppermute | solution.py:381
  23.6 9.7 %collective-permute-start.6 = (bf16[640,256]{1,0:T(8,128)(2,1)S(1)}, bf16[640,256]{1,0:T(8,128)(2,1)S(1)}, u32[]{:S(2)}, u32[]{:S(2)}) collective-permute-start(bf16[640,256]{1,0:T(8,128)(2,1)S(1)} %collective-permute-done.1), channel_id=1, source_target_pairs={{2,0},{3,1},{4,6},{5,7},{10,8},{11,9},{12,14},{13,15},{18,16},{19,... | collective-permute-start | bytes 983048 | tf_op jit(solution)/shard_map/ppermute | solution.py:382
  24.9 30.5 %copy-start.3 = (bf16[8,256,320]{2,1,0:T(8,128)(2,1)S(1)}, bf16[8,256,320]{2,1,0:T(8,128)(2,1)}, u32[]{:S(2)}) copy-start(bf16[8,256,320]{2,1,0:T(8,128)(2,1)} %pair_columns.1.xs_ref) | copy-start | bytes 3932164
  30.7 2.6 %copy-start.11 = (bf16[2,128,640]{2,1,0:T(8,128)(2,1)}, bf16[2,128,640]{2,1,0:T(8,128)(2,1)S(1)}, u32[]{:S(2)}) copy-start(bf16[2,128,640]{2,1,0:T(8,128)(2,1)S(1)} %collective-permute-done.3.refs_3_) | copy-start | bytes 983044
  33.3 22.0 %all-to-all-start.1 = ((bf16[8,384,128]{2,1,0:T(8,128)(2,1)}), bf16[8,384,128]{2,1,0:T(8,128)(2,1)S(1)}, u32[]{:S(2)}, u32[]{:S(2)}) async-start(bf16[8,384,128]{2,1,0:T(8,128)(2,1)} %get-tuple-element.63), calls=%async_computation.1 | async-start | bytes 1572864 | tf_op jit(solution)/shard_map/all_to_all | solution.py:407
  38.0 17.4 %copy-start.8 = (bf16[640,256]{1,0:T(8,128)(2,1)}, bf16[640,256]{1,0:T(8,128)(2,1)S(1)}, u32[]{:S(2)}) copy-start(bf16[640,256]{1,0:T(8,128)(2,1)S(1)} %broadcast_select_fusion.refs_8_) | copy-start | bytes 983044
  38.0 10.8 %collective-permute-start.9 = (bf16[640,256]{1,0:T(8,128)(2,1)S(1)}, bf16[640,256]{1,0:T(8,128)(2,1)S(1)}, u32[]{:S(2)}, u32[]{:S(2)}) collective-permute-start(bf16[640,256]{1,0:T(8,128)(2,1)S(1)} %broadcast_select_fusion.refs_8_), channel_id=1, source_target_pairs={{0,8},{8,0},{1,9},{9,1},{2,10},{10,2},{3,11},{11,3},{4,12},{12,4},... | collective-permute-start | bytes 983048 | tf_op jit(solution)/shard_map/ppermute | solution.py:345
  38.1 10.8 %collective-permute-start.7 = (bf16[640,256]{1,0:T(8,128)(2,1)}, bf16[640,256]{1,0:T(8,128)(2,1)S(1)}, u32[]{:S(2)}, u32[]{:S(2)}) collective-permute-start(bf16[640,256]{1,0:T(8,128)(2,1)} %copy-done.9), channel_id=1, source_target_pairs={{0,8},{8,0},{1,9},{9,1},{2,10},{10,2},{3,11},{11,3},{4,12},{12,4},... | collective-permute-start | bytes 983048 | tf_op jit(solution)/shard_map/ppermute | solution.py:345
  38.6 11.1 %collective-permute-start.8 = (bf16[640,256]{1,0:T(8,128)(2,1)}, bf16[640,256]{1,0:T(8,128)(2,1)}, u32[]{:S(2)}, u32[]{:S(2)}) collective-permute-start(bf16[640,256]{1,0:T(8,128)(2,1)} %collective-permute-done.refs_7_), channel_id=1, source_target_pairs={{0,8},{8,0},{1,9},{9,1},{2,10},{10,2},{3,11},{11,3},{4,12},{12,4},... | collective-permute-start | bytes 983048 | tf_op jit(solution)/shard_map/ppermute | solution.py:345
  38.6 0.7 copy-start.4
  48.8 6.5 %copy-start.13 = (bf16[640,256]{1,0:T(8,128)(2,1)}, bf16[640,256]{1,0:T(8,128)(2,1)S(1)}, u32[]{:S(2)}) copy-start(bf16[640,256]{1,0:T(8,128)(2,1)S(1)} %collective-permute-done.9.refs_13_) | copy-start | bytes 983044
  48.8 0.8 copy-start.14
  55.3 1.0 copy-start.7
  56.3 7.2 %copy-start.12 = (bf16[2,128,640]{2,1,0:T(8,128)(2,1)S(1)}, bf16[2,128,640]{2,1,0:T(8,128)(2,1)}, u32[]{:S(2)}) copy-start(bf16[2,128,640]{2,1,0:T(8,128)(2,1)} %copy-done.11) | copy-start | bytes 983044
  59.3 43.0 %all-to-all-start.2 = ((bf16[8,384,128]{2,1,0:T(8,128)(2,1)}), bf16[8,384,128]{2,1,0:T(8,128)(2,1)S(1)}, u32[]{:S(2)}, u32[]{:S(2)}) async-start(bf16[8,384,128]{2,1,0:T(8,128)(2,1)} %get-tuple-element.71.refs_16_), calls=%async_computation.2 | async-start | bytes 1572864 | tf_op jit(solution)/shard_map/all_to_all | solution.py:455
  62.9 39.5 %copy-start.5 = (s32[8]{0:T(128)S(1)}, s32[8]{0:T(128)}, u32[]{:S(2)}) copy-start(s32[8]{0:T(128)} %get-tuple-element.69.after_ref.rows_here) | copy-start | bytes 100
  62.9 10.9 %collective-permute-start.11 = (bf16[2,128,640]{2,1,0:T(8,128)(2,1)}, bf16[2,128,640]{2,1,0:T(8,128)(2,1)S(1)}, u32[]{:S(2)}, u32[]{:S(2)}) collective-permute-start(bf16[2,128,640]{2,1,0:T(8,128)(2,1)} %collective-permute-done.2.refs_2_), channel_id=1, source_target_pairs={{0,16},{16,0},{1,17},{17,1},{2,18},{18,2},{3,19},{19,3},{4,20},{20... | collective-permute-start | bytes 983048 | tf_op jit(solution)/shard_map/ppermute | solution.py:348
  63.5 14.8 %collective-permute-start.12 = (bf16[2,128,640]{2,1,0:T(8,128)(2,1)S(1)}, bf16[2,128,640]{2,1,0:T(8,128)(2,1)S(1)}, u32[]{:S(2)}, u32[]{:S(2)}) collective-permute-start(bf16[2,128,640]{2,1,0:T(8,128)(2,1)S(1)} %copy-done.12), channel_id=1, source_target_pairs={{0,16},{16,0},{1,17},{17,1},{2,18},{18,2},{3,19},{19,3},{4,20},{20... | collective-permute-start | bytes 983048 | tf_op jit(solution)/shard_map/ppermute | solution.py:348
  65.0 19.2 %collective-permute-start.10 = (bf16[640,256]{1,0:T(8,128)(2,1)}, bf16[640,256]{1,0:T(8,128)(2,1)S(1)}, u32[]{:S(2)}, u32[]{:S(2)}) collective-permute-start(bf16[640,256]{1,0:T(8,128)(2,1)} %collective-permute-done.5.refs_9_), channel_id=1, source_target_pairs={{2,0},{3,1},{4,6},{5,7},{10,8},{11,9},{12,14},{13,15},{18,16},{19,... | collective-permute-start | bytes 983048 | tf_op jit(solution)/shard_map/ppermute | solution.py:410
  73.8 12.6 %copy-start.15 = (bf16[2,128,640]{2,1,0:T(8,128)(2,1)}, bf16[2,128,640]{2,1,0:T(8,128)(2,1)S(1)}, u32[]{:S(2)}) copy-start(bf16[2,128,640]{2,1,0:T(8,128)(2,1)S(1)} %collective-permute-done.11.refs_4_) | copy-start | bytes 983044
  78.3 8.2 %copy-start.16 = (bf16[2,128,640]{2,1,0:T(8,128)(2,1)}, bf16[2,128,640]{2,1,0:T(8,128)(2,1)S(1)}, u32[]{:S(2)}) copy-start(bf16[2,128,640]{2,1,0:T(8,128)(2,1)S(1)} %collective-permute-done.12.refs_5_) | copy-start | bytes 983044
  84.2 2.3 %copy-start.17 = (bf16[640,256]{1,0:T(8,128)(2,1)}, bf16[640,256]{1,0:T(8,128)(2,1)S(1)}, u32[]{:S(2)}) copy-start(bf16[640,256]{1,0:T(8,128)(2,1)S(1)} %collective-permute-done.10.refs_10_) | copy-start | bytes 983044
  84.2 2.3 %collective-permute-start.13 = (bf16[640,256]{1,0:T(8,128)(2,1)}, bf16[640,256]{1,0:T(8,128)(2,1)S(1)}, u32[]{:S(2)}, u32[]{:S(2)}) collective-permute-start(bf16[640,256]{1,0:T(8,128)(2,1)} %collective-permute-done.5.refs_9_), channel_id=1, source_target_pairs={{0,8},{8,0},{1,9},{9,1},{2,10},{10,2},{3,11},{11,3},{4,12},{12,4},... | collective-permute-start | bytes 983048 | tf_op jit(solution)/shard_map/ppermute | solution.py:345
  84.2 2.3 %collective-permute-start.14 = (bf16[640,256]{1,0:T(8,128)(2,1)S(1)}, bf16[640,256]{1,0:T(8,128)(2,1)S(1)}, u32[]{:S(2)}, u32[]{:S(2)}) collective-permute-start(bf16[640,256]{1,0:T(8,128)(2,1)S(1)} %collective-permute-done.10.refs_10_), channel_id=1, source_target_pairs={{0,8},{8,0},{1,9},{9,1},{2,10},{10,2},{3,11},{11,3},{4,12},{12,4},... | collective-permute-start | bytes 983048 | tf_op jit(solution)/shard_map/ppermute | solution.py:345
  86.4 0.7 copy-start.18
  87.2 0.7 copy-start.19
  92.9 6.6 %collective-permute-start.15 = (bf16[128,512]{1,0:T(8,128)(2,1)}, bf16[128,512]{1,0:T(8,128)(2,1)S(1)}, u32[]{:S(2)}, u32[]{:S(2)}) collective-permute-start(bf16[128,512]{1,0:T(8,128)(2,1)} %get-tuple-element.81), channel_id=1, source_target_pairs={{0,1},{1,0},{2,3},{3,2},{4,5},{5,4},{6,7},{7,6},{8,9},{9,8},{10,11... | collective-permute-start | bytes 393224 | tf_op jit(solution)/shard_map/ppermute | solution.py:342
  94.1 8.3 %collective-permute-start.16 = (bf16[128,512]{1,0:T(8,128)(2,1)}, bf16[128,512]{1,0:T(8,128)(2,1)S(1)}, u32[]{:S(2)}, u32[]{:S(2)}) collective-permute-start(bf16[128,512]{1,0:T(8,128)(2,1)} %get-tuple-element.82), channel_id=1, source_target_pairs={{0,16},{16,0},{1,17},{17,1},{2,18},{18,2},{3,19},{19,3},{4,20},{20... | collective-permute-start | bytes 393224 | tf_op jit(solution)/shard_map/ppermute | solution.py:348
  94.6 7.8 %collective-permute-start.17 = (bf16[128,512]{1,0:T(8,128)(2,1)}, bf16[128,512]{1,0:T(8,128)(2,1)S(1)}, u32[]{:S(2)}, u32[]{:S(2)}) collective-permute-start(bf16[128,512]{1,0:T(8,128)(2,1)} %get-tuple-element.83), channel_id=1, source_target_pairs={{0,17},{1,16},{2,19},{3,18},{4,21},{5,20},{6,23},{7,22},{16,1},{17... | collective-permute-start | bytes 393224 | tf_op jit(solution)/shard_map/ppermute | solution.py:456
  102.4 2.4 %collective-permute-start.19 = (bf16[8,384,128]{2,1,0:T(8,128)(2,1)S(1)}, bf16[8,384,128]{2,1,0:T(8,128)(2,1)S(1)}, u32[]{:S(2)}, u32[]{:S(2)}) collective-permute-start(bf16[8,384,128]{2,1,0:T(8,128)(2,1)S(1)} %all-to-all-done.2.rest_0_), channel_id=1, source_target_pairs={{0,8},{8,0},{1,9},{9,1},{2,10},{10,2},{3,11},{11,3},{4,12},{12,4},... | collective-permute-start | bytes 2359304 | tf_op jit(solution)/shard_map/ppermute | solution.py:345
  102.4 2.3 %collective-permute-start.18 = (s32[8]{0:T(128)S(1)}, s32[8]{0:T(128)S(1)}, u32[]{:S(2)}, u32[]{:S(2)}) collective-permute-start(s32[8]{0:T(128)S(1)} %copy-done.5), channel_id=1, source_target_pairs={{0,8},{8,0},{1,9},{9,1},{2,10},{10,2},{3,11},{11,3},{4,12},{12,4},... | collective-permute-start | bytes 104 | tf_op jit(solution)/shard_map/ppermute | solution.py:345
  104.7 2.8 %copy-start.1 = (bf16[640,512]{1,0:T(8,128)(2,1)S(1)}, bf16[640,512]{1,0:T(8,128)(2,1)}, u32[]{:S(2)}) copy-start(bf16[640,512]{1,0:T(8,128)(2,1)} %param.9) | copy-start | bytes 1966084

commit v18 on v17

--- a/solution.py
+++ b/solution.py
@@ -408,10 +408,6 @@
     rows_core = other_core(rows)
     y_far = [other_part(piece) for piece in x_far]
     passed_near = lax.ppermute(over_near, "tensor", ends)
-    inside = (z == 1) | (z == 2)
-    quarter = [half, near, jnp.where(inside, over, passed)]
-    quarter_core = [other_core(w) for w in quarter]
-
     owned_groups = ADAPTERS // lax.axis_size("dp") // 8
     down_shape = jax.ShapeDtypeStruct((owned_groups, down_chunks, 8, 1, LANES), jnp.float32)
     up_shape = jax.ShapeDtypeStruct((owned_groups, up_chunks, 8, 1, LANES), jnp.float32)
@@ -421,7 +417,11 @@
         scratch_shapes=[pltpu.VMEM((up_chunks, 8, 1, LANES), jnp.float32), pltpu.SemaphoreType.DMA((2,))],
         compiler_params=LIMIT, cost_estimate=cost(read=28 << 20), name="clear_rows",
     )(rows)
-    panels, quarter_core = lax.optimization_barrier((panels, quarter_core))
+    cleared, half, near, over, passed = lax.optimization_barrier((cleared, half, near, over, passed))
+    inside = (z == 1) | (z == 2)
+    quarter = [half, near, jnp.where(inside, over, passed)]
+    quarter_core = [other_core(w) for w in quarter]
+    panels, quarter_core, passed_near, y_far = lax.optimization_barrier((panels, quarter_core, passed_near, y_far))
 
     terms, lifted = pl.pallas_call(
         functools.partial(adapter_kernel, group, down_chunks),
@@ -433,7 +433,7 @@
         cost_estimate=cost(flops=3 << 30, read=8 << 20),
         name="adapter",
     )(xs, cotangent, panels, cleared)
-    _, over_near, passed_near, y_far = lax.optimization_barrier((terms, over_near, passed_near, y_far))
+    _, over_near, passed_near = lax.optimization_barrier((terms, over_near, passed_near))
     last = [over_near, passed_near]
     quarters = quarter + last + quarter_core + [other_core(w) for w in last]
     sums = [jax.ShapeDtypeStruct((token_rows, parts * width), kind) for kind in (jnp.float32,) + (jnp.bfloat16,) * 3]

time: 109 us -> 92.5 us (0.85)
  waiting for transfers between devices: 34.8 us -> 18.5 us
    ppermute x4, waiting for transfers between devices: 14.8 us -> 2.53 us  [other_part(): lax.ppermute(value, 'parts', [(a, parts - 1 - a) for a in range(parts)])]
    all_to_all x1, waiting for transfers between devices: 5.71 us -> 0.01 us  [fast_body(): panels = lax.all_to_all(sent, 'tensor', 0, 0)]
    unnamed x40 -> x38, local copies, waits for them, and re-layouts: 5.19 us -> 5.61 us
  transfers between devices with their start and end apart: 23 -> 23, of which waited for: 10 -> 9; matrix products, arithmetic and copies ran while one was open for 2% -> 2% of each run, Pallas kernels for 22% -> 26%
where the time goes in v18:
time: 92.5 us; the launch traced here: 91.9 us
  starting transfers between devices  33.8 us (37%)
  Pallas kernels  30 us (32%)
  waiting for transfers between devices  18.5 us (20%)
  local copies, waits for them, and re-layouts  6.23 us (7%)
  other arithmetic  1.85 us (2%)
  between operations  1.62 us (2%)
    ppermute x4, starting transfers between devices, exchange(): return lax.ppermute(value, 'tensor', [(t, t ^ s) for t in range(group)])  10.5 us
    pallas_call x1, Pallas kernels, fast_body(): pl.pallas_call(zero_kernel, out_shape=(down_shape, up_shape, token), in_s...  9.48 us
    ppermute x1, waiting for transfers between devices, fast_body(): passed_near = lax.ppermute(over_near, 'tensor', ends)  6.18 us
    unnamed x38, local copies, waits for them, and re-layouts  5.61 us
    pallas_call x1, Pallas kernels, fast_body(): pl.pallas_call(gather_kernel, out_shape=(pieces, jax.ShapeDtypeStruct((gr...  5.53 us
    pallas_call x1, Pallas kernels, fast_body(): pl.pallas_call(base_kernel, out_shape=sums, in_specs=[ANY] * (7 + len(qua...  5.02 us
    all_to_all x1, starting transfers between devices, fast_body(): panels = lax.all_to_all(sent, 'tensor', 0, 0)  4.64 us
    ppermute x4, waiting for transfers between devices, exchange(): return lax.ppermute(value, 'tensor', [(t, t ^ s) for t in range(group)])  4.42 us
  transfers between devices with their start and end apart: 23, of which 9 were waited for; matrix products, arithmetic and copies ran while one was open for 2% of the time, Pallas kernels for 26%

profile of v18, /device:TPU:0, one launch (start us, length us, event | category | flops | bytes accessed | tf_op | source)
XLA Modules:
  0.0 91.9 jit_solution(12246881604160045996)
XLA Ops:
  0.6 0.0 copy-start
  1.4 0.6 broadcast_in_dim.2
  2.0 0.7 collective-permute-start.1
  2.7 5.9 %collective-permute-start = (bf16[640,256]{1,0:T(8,128)(2,1)S(1)}, bf16[640,256]{1,0:T(8,128)(2,1)}, u32[]{:S(2)}, u32[]{:S(2)}) collective-permute-start(bf16[640,256]{1,0:T(8,128)(2,1)S(1)} %constant_dynamic-slice_fusion.refs_6_), channel_id=1, source_target_pairs={{0,2},{1,3},{2,0},{3,1},{4,6},{5,7},{6,4},{7,5},{8,10},{9,11},{10,... | collective-permute-start | bytes 983048 | tf_op jit(solution)/shard_map/ppermute | solution.py:342
  8.6 1.3 %copy-done.2 = bf16[128,5120]{1,0:T(8,128)(2,1)S(1)} copy-done((bf16[128,5120]{1,0:T(8,128)(2,1)S(1)}, bf16[128,5120]{1,0:T(8,128)(2,1)}, u32[]{:S(2)}) %copy-start.2) | copy-done | bytes 1310744
  9.9 0.1 split_tokens.1
  10.0 1.6 %collective-permute-start.4 = (bf16[4,128,640]{2,1,0:T(8,128)(2,1)S(1)}, bf16[4,128,640]{2,1,0:T(8,128)(2,1)}, u32[]{:S(2)}, u32[]{:S(2)}) collective-permute-start(bf16[4,128,640]{2,1,0:T(8,128)(2,1)S(1)} %get-tuple-element.55.refs_0_), channel_id=1, source_target_pairs={{0,16},{16,0},{1,17},{17,1},{2,18},{18,2},{3,19},{19,3},{4,20},{20... | collective-permute-start | bytes 1966088 | tf_op jit(solution)/shard_map/ppermute | solution.py:348
  11.6 3.6 %all-to-all-start = ((s32[8,1,128]{2,1,0:T(1,128)}), s32[8,1,128]{2,1,0:T(1,128)S(1)}, u32[]{:S(2)}, u32[]{:S(2)}) async-start(s32[8,1,128]{2,1,0:T(1,128)} %broadcast_in_dim.2), calls=%async_computation | async-start | bytes 8192 | tf_op jit(solution)/shard_map/all_to_all | solution.py:351
  15.2 2.0 %collective-permute-start.2 = (bf16[2,128,640]{2,1,0:T(8,128)(2,1)S(1)}, bf16[2,128,640]{2,1,0:T(8,128)(2,1)}, u32[]{:S(2)}, u32[]{:S(2)}) collective-permute-start(bf16[2,128,640]{2,1,0:T(8,128)(2,1)S(1)} %get-tuple-element.57), channel_id=1, source_target_pairs={{0,1},{1,0},{2,3},{3,2},{4,5},{5,4},{6,7},{7,6},{8,9},{9,8},{10,11... | collective-permute-start | bytes 983048 | tf_op jit(solution)/shard_map/ppermute | solution.py:342
  17.2 3.9 %pair_columns.1.xs_ref = bf16[8,256,320]{2,1,0:T(8,128)(2,1)} custom-call(bf16[128,5120]{1,0:T(8,128)(2,1)} %x_ref.1), custom_call_target="tpu_custom_call" | custom-call | bytes 134217728 | tf_op jit(solution)/shard_map/pair_columns/pallas_call | solution.py:365
  21.0 0.5 all-to-all-done.asked
  21.5 0.0 collective-permute-done.1
  21.5 0.0 collective-permute-done.refs_7_
  21.6 0.6 collective-permute-start.3
  22.2 1.4 %collective-permute-start.5 = (bf16[640,256]{1,0:T(8,128)(2,1)}, bf16[640,256]{1,0:T(8,128)(2,1)}, u32[]{:S(2)}, u32[]{:S(2)}) collective-permute-start(bf16[640,256]{1,0:T(8,128)(2,1)} %collective-permute-done.refs_7_), channel_id=1, source_target_pairs={{2,4},{3,5},{4,2},{5,3},{10,12},{11,13},{12,10},{13,11},{18,20},{1... | collective-permute-start | bytes 983048 | tf_op jit(solution)/shard_map/ppermute | solution.py:381
  23.6 1.3 %collective-permute-start.6 = (bf16[640,256]{1,0:T(8,128)(2,1)S(1)}, bf16[640,256]{1,0:T(8,128)(2,1)S(1)}, u32[]{:S(2)}, u32[]{:S(2)}) collective-permute-start(bf16[640,256]{1,0:T(8,128)(2,1)S(1)} %collective-permute-done.1), channel_id=1, source_target_pairs={{2,0},{3,1},{4,6},{5,7},{10,8},{11,9},{12,14},{13,15},{18,16},{19,... | collective-permute-start | bytes 983048 | tf_op jit(solution)/shard_map/ppermute | solution.py:382
  24.9 5.5 %pick_panels.1 = (bf16[8,384,128]{2,1,0:T(8,128)(2,1)}, s32[8]{0:T(128)}) custom-call(s32[8,1,128]{2,1,0:T(1,128)} %copy-done.10, s32[256]{0:T(256)} %slot_of.1, bf16[32,320,8,128]{3,2,1,0:T(8,128)(2,1)} %bitcast.18, bf16[32,64,8,128]{3,2,1,0:T(8,128)(2,1)} %bitcast.20), custom_call_target="tpu_custom_call" | custom-call | bytes 41943040 | tf_op jit(solution)/shard_map/pick_panels/pallas_call | solution.py:388
  30.4 0.0 collective-permute-done.2.refs_2_
  30.5 0.0 collective-permute-done.4.refs_1_
  30.5 0.2 collective-permute-done.3.refs_3_
  30.7 0.0 collective-permute-done.5.refs_9_
  30.7 2.6 %collective-permute-done.6 = bf16[640,256]{1,0:T(8,128)(2,1)S(1)} collective-permute-done((bf16[640,256]{1,0:T(8,128)(2,1)S(1)}, bf16[640,256]{1,0:T(8,128)(2,1)S(1)}, u32[]{:S(2)}, u32[]{:S(2)}) %collective-permute-start.6) | collective-permute-done | bytes 327712 | tf_op jit(solution)/shard_map/ppermute | solution.py:382
  33.3 4.6 %all-to-all-start.1 = ((bf16[8,384,128]{2,1,0:T(8,128)(2,1)}), bf16[8,384,128]{2,1,0:T(8,128)(2,1)S(1)}, u32[]{:S(2)}, u32[]{:S(2)}) async-start(bf16[8,384,128]{2,1,0:T(8,128)(2,1)} %get-tuple-element.68), calls=%async_computation.1 | async-start | bytes 1572864 | tf_op jit(solution)/shard_map/all_to_all | solution.py:407
  37.9 0.5 collective-permute-start.11
  38.4 1.5 %collective-permute-start.12 = (bf16[2,128,640]{2,1,0:T(8,128)(2,1)}, bf16[2,128,640]{2,1,0:T(8,128)(2,1)S(1)}, u32[]{:S(2)}, u32[]{:S(2)}) collective-permute-start(bf16[2,128,640]{2,1,0:T(8,128)(2,1)} %copy-done.11), channel_id=1, source_target_pairs={{0,16},{16,0},{1,17},{17,1},{2,18},{18,2},{3,19},{19,3},{4,20},{20... | collective-permute-start | bytes 983048 | tf_op jit(solution)/shard_map/ppermute | solution.py:348
  40.0 1.3 %collective-permute-start.10 = (bf16[640,256]{1,0:T(8,128)(2,1)}, bf16[640,256]{1,0:T(8,128)(2,1)S(1)}, u32[]{:S(2)}, u32[]{:S(2)}) collective-permute-start(bf16[640,256]{1,0:T(8,128)(2,1)} %collective-permute-done.5.refs_9_), channel_id=1, source_target_pairs={{2,0},{3,1},{4,6},{5,7},{10,8},{11,9},{12,14},{13,15},{18,16},{19,... | collective-permute-start | bytes 983048 | tf_op jit(solution)/shard_map/ppermute | solution.py:410
  41.3 0.7 copy-done.4
  41.9 9.5 %clear_rows.1 = (f32[16,320,8,1,128]{4,3,2,1,0:T(1,128)}, f32[16,64,8,1,128]{4,3,2,1,0:T(1,128)}, s32[1]{0:T(128)}) custom-call(s32[8]{0:T(128)S(1)} %copy-done.4), custom_call_target="tpu_custom_call" | custom-call | bytes 29360128 | tf_op jit(solution)/shard_map/clear_rows/pallas_call | solution.py:414
  51.5 0.1 collective-permute-start.9
  51.5 0.5 collective-permute-start.7
  52.0 0.0 collective-permute-done.11.refs_4_
  52.0 0.1 collective-permute-start.8
  52.1 0.0 collective-permute-done.12.refs_5_
  52.1 6.2 %collective-permute-done.10.refs_10_ = bf16[640,256]{1,0:T(8,128)(2,1)S(1)} collective-permute-done((bf16[640,256]{1,0:T(8,128)(2,1)}, bf16[640,256]{1,0:T(8,128)(2,1)S(1)}, u32[]{:S(2)}, u32[]{:S(2)}) %collective-permute-start.10) | collective-permute-done | bytes 327712 | tf_op jit(solution)/shard_map/ppermute | solution.py:410
  58.3 0.0 collective-permute-done.9.refs_13_
  58.3 0.0 collective-permute-done.7.refs_11_
  58.3 0.7 copy-done.13
  59.1 0.0 collective-permute-done.8.refs_12_
  59.1 0.1 copy-done.15
  59.2 0.6 copy-done.16
  59.8 0.0 all-to-all-done.1.pieces
  59.8 0.9 %copy-done.7 = bf16[128,1024]{1,0:T(8,128)(2,1)S(1)} copy-done((bf16[128,1024]{1,0:T(8,128)(2,1)S(1)}, bf16[128,1024]{1,0:T(8,128)(2,1)}, u32[]{:S(2)}) %copy-start.7) | copy-done | bytes 262168
  60.7 3.0 %adapter.1 = (bf16[8,384,128]{2,1,0:T(8,128)(2,1)}, f32[128,1024]{1,0:T(8,128)S(1)}) custom-call(bf16[8,256,320]{2,1,0:T(8,128)(2,1)S(1)} %copy-done.3, bf16[128,1024]{1,0:T(8,128)(2,1)S(1)} %copy-done.7, bf16[8,384,128]{2,1,0:T(8,128)(2,1)S(1)} %all-to-all-done.1.pieces, s32[1]{0:T(128)} %get-tuple-element.84._), custom_call_target="tpu_custom_call" | custom-call | flops 3221225472 | bytes 8388608 | tf_op jit(solution)/shard_map/adapter/pallas_call | solution.py:426
  63.8 3.5 %all-to-all-start.2 = ((bf16[8,384,128]{2,1,0:T(8,128)(2,1)}), bf16[8,384,128]{2,1,0:T(8,128)(2,1)S(1)}, u32[]{:S(2)}, u32[]{:S(2)}) async-start(bf16[8,384,128]{2,1,0:T(8,128)(2,1)} %get-tuple-element.85.refs_16_), calls=%async_computation.2 | async-start | bytes 1572864 | tf_op jit(solution)/shard_map/all_to_all | solution.py:455
  67.3 0.1 collective-permute-start.13
  67.4 0.5 collective-permute-start.14
  67.9 1.3 %collective-permute-done.13.refs_14_ = bf16[640,256]{1,0:T(8,128)(2,1)S(1)} collective-permute-done((bf16[640,256]{1,0:T(8,128)(2,1)}, bf16[640,256]{1,0:T(8,128)(2,1)S(1)}, u32[]{:S(2)}, u32[]{:S(2)}) %collective-permute-start.13) | collective-permute-done | bytes 327712 | tf_op jit(solution)/shard_map/ppermute | solution.py:345
  69.2 0.3 collective-permute-done.14.refs_15_
  69.5 0.5 copy-done.17
  69.9 0.7 copy-done.18
  70.7 5.0 %frozen_part.1 = (f32[128,512]{1,0:T(8,128)}, bf16[128,512]{1,0:T(8,128)(2,1)}, bf16[128,512]{1,0:T(8,128)(2,1)}, bf16[128,512]{1,0:T(8,128)(2,1)}) custom-call(bf16[4,128,640]{2,1,0:T(8,128)(2,1)} %copy-done.6, bf16[4,128,640]{2,1,0:T(8,128)(2,1)} %collective-permute-done.4.refs_1_, bf16[2,128,640]{2,1,0:T(8,128)(2,1)} %collective-permute-done.2.refs_2_, ...), custom_call_target="tpu_custom_call" | custom-call | flops 4294967296 | bytes 8388608 | tf_op jit(solution)/shard_map/frozen_part/pallas_call | solution.py:440
  75.7 2.0 %collective-permute-start.15 = (bf16[128,512]{1,0:T(8,128)(2,1)}, bf16[128,512]{1,0:T(8,128)(2,1)S(1)}, u32[]{:S(2)}, u32[]{:S(2)}) collective-permute-start(bf16[128,512]{1,0:T(8,128)(2,1)} %get-tuple-element.93), channel_id=1, source_target_pairs={{0,1},{1,0},{2,3},{3,2},{4,5},{5,4},{6,7},{7,6},{8,9},{9,8},{10,11... | collective-permute-start | bytes 393224 | tf_op jit(solution)/shard_map/ppermute | solution.py:342
  77.7 0.4 collective-permute-start.16
  78.1 1.2 %collective-permute-start.17 = (bf16[128,512]{1,0:T(8,128)(2,1)}, bf16[128,512]{1,0:T(8,128)(2,1)S(1)}, u32[]{:S(2)}, u32[]{:S(2)}) collective-permute-start(bf16[128,512]{1,0:T(8,128)(2,1)} %get-tuple-element.95), channel_id=1, source_target_pairs={{0,17},{1,16},{2,19},{3,18},{4,21},{5,20},{6,23},{7,22},{16,1},{17... | collective-permute-start | bytes 393224 | tf_op jit(solution)/shard_map/ppermute | solution.py:456
  79.3 4.2 %collective-permute-done.15 = bf16[128,512]{1,0:T(8,128)(2,1)S(1)} collective-permute-done((bf16[128,512]{1,0:T(8,128)(2,1)}, bf16[128,512]{1,0:T(8,128)(2,1)S(1)}, u32[]{:S(2)}, u32[]{:S(2)}) %collective-permute-start.15) | collective-permute-done | bytes 131104 | tf_op jit(solution)/shard_map/ppermute | solution.py:342
  83.5 2.5 %collective-permute-done.16 = bf16[128,512]{1,0:T(8,128)(2,1)S(1)} collective-permute-done((bf16[128,512]{1,0:T(8,128)(2,1)}, bf16[128,512]{1,0:T(8,128)(2,1)S(1)}, u32[]{:S(2)}, u32[]{:S(2)}) %collective-permute-start.16) | collective-permute-done | bytes 131104 | tf_op jit(solution)/shard_map/ppermute | solution.py:348
  86.0 0.0 collective-permute-done.17
  86.0 0.6 all-to-all-done.2.rest_0_
  86.6 0.0 collective-permute-start.19
  86.6 0.5 collective-permute-start.18
  87.1 1.0 %convert_add_fusion = (f32[128,512]{1,0:T(8,128)S(1)}, f32[128,512]{1,0:T(8,128)S(1)}) fusion(bf16[128,512]{1,0:T(8,128)(2,1)S(1)} %collective-permute-done.17, bf16[128,512]{1,0:T(8,128)(2,1)S(1)} %collective-permute-done.16, f32[128,512]{1,0:T(8,128)} %get-tuple-element.92, bf16[128,512]{1,0:T(8,128)(2,1)S(1)} %collective-permute-done.15), kind=kLoop, calls=%fused_computation.3 | loop fusion | flops 327680 | bytes 1179648 | tf_op jit(solution)/shard_map/add | solution.py:482
  88.2 0.8 fusion
  89.0 0.0 collective-permute-done.18.rows_core
  89.0 2.9 %place_rows.1 = (f32[16,320,8,1,128]{4,3,2,1,0:T(1,128)}, f32[16,64,8,1,128]{4,3,2,1,0:T(1,128)}) custom-call(s32[8]{0:T(128)S(1)} %copy-done.5, s32[8]{0:T(128)S(1)} %collective-permute-done.18.rows_core, bf16[8,384,128]{2,1,0:T(8,128)(2,1)S(1)} %all-to-all-done.2.rest_0_, ...), custom_call_target="tpu_custom_call", output_to_operand_aliasing={{0}: (4, {}), {1}: (5, {})} | custom-call | bytes 16777216 | tf_op jit(solution)/shard_map/place_rows/pallas_call | solution.py:460
  (33 shorter events, 0.2 us)
Async XLA Ops:
  0.6 1.3 %copy-start = (bf16[640,512]{1,0:T(8,128)(2,1)S(1)}, bf16[640,512]{1,0:T(8,128)(2,1)}, u32[]{:S(2)}) copy-start(bf16[640,512]{1,0:T(8,128)(2,1)} %param.9) | copy-start | bytes 1966084
  2.0 22.9 %copy-start.9 = (bf16[640,256]{1,0:T(8,128)(2,1)}, bf16[640,256]{1,0:T(8,128)(2,1)S(1)}, u32[]{:S(2)}) copy-start(bf16[640,256]{1,0:T(8,128)(2,1)S(1)} %constant_dynamic-slice_fusion.refs_6_) | copy-start | bytes 983044
  2.0 19.6 %collective-permute-start.1 = (bf16[640,256]{1,0:T(8,128)(2,1)S(1)}, bf16[640,256]{1,0:T(8,128)(2,1)S(1)}, u32[]{:S(2)}, u32[]{:S(2)}) collective-permute-start(bf16[640,256]{1,0:T(8,128)(2,1)S(1)} %constant_dynamic-slice_fusion.refs_6_), channel_id=1, source_target_pairs={{2,4},{3,5},{4,2},{5,3},{10,12},{11,13},{12,10},{13,11},{18,20},{1... | collective-permute-start | bytes 983048 | tf_op jit(solution)/shard_map/ppermute | solution.py:378
  2.7 18.9 %collective-permute-start = (bf16[640,256]{1,0:T(8,128)(2,1)S(1)}, bf16[640,256]{1,0:T(8,128)(2,1)}, u32[]{:S(2)}, u32[]{:S(2)}) collective-permute-start(bf16[640,256]{1,0:T(8,128)(2,1)S(1)} %constant_dynamic-slice_fusion.refs_6_), channel_id=1, source_target_pairs={{0,2},{1,3},{2,0},{3,1},{4,6},{5,7},{6,4},{7,5},{8,10},{9,11},{10,... | collective-permute-start | bytes 983048 | tf_op jit(solution)/shard_map/ppermute | solution.py:342
  8.6 1.3 %copy-start.2 = (bf16[128,5120]{1,0:T(8,128)(2,1)S(1)}, bf16[128,5120]{1,0:T(8,128)(2,1)}, u32[]{:S(2)}) copy-start(bf16[128,5120]{1,0:T(8,128)(2,1)} %x_ref.1) | copy-start | bytes 3932164
  10.0 20.4 %copy-start.6 = (bf16[4,128,640]{2,1,0:T(8,128)(2,1)}, bf16[4,128,640]{2,1,0:T(8,128)(2,1)S(1)}, u32[]{:S(2)}) copy-start(bf16[4,128,640]{2,1,0:T(8,128)(2,1)S(1)} %get-tuple-element.55.refs_0_) | copy-start | bytes 1966084
  10.0 20.4 %collective-permute-start.4 = (bf16[4,128,640]{2,1,0:T(8,128)(2,1)S(1)}, bf16[4,128,640]{2,1,0:T(8,128)(2,1)}, u32[]{:S(2)}, u32[]{:S(2)}) collective-permute-start(bf16[4,128,640]{2,1,0:T(8,128)(2,1)S(1)} %get-tuple-element.55.refs_0_), channel_id=1, source_target_pairs={{0,16},{16,0},{1,17},{17,1},{2,18},{18,2},{3,19},{19,3},{4,20},{20... | collective-permute-start | bytes 1966088 | tf_op jit(solution)/shard_map/ppermute | solution.py:348
  11.6 9.9 %all-to-all-start = ((s32[8,1,128]{2,1,0:T(1,128)}), s32[8,1,128]{2,1,0:T(1,128)S(1)}, u32[]{:S(2)}, u32[]{:S(2)}) async-start(s32[8,1,128]{2,1,0:T(1,128)} %broadcast_in_dim.2), calls=%async_computation | async-start | bytes 8192 | tf_op jit(solution)/shard_map/all_to_all | solution.py:351
  15.2 15.3 %collective-permute-start.2 = (bf16[2,128,640]{2,1,0:T(8,128)(2,1)S(1)}, bf16[2,128,640]{2,1,0:T(8,128)(2,1)}, u32[]{:S(2)}, u32[]{:S(2)}) collective-permute-start(bf16[2,128,640]{2,1,0:T(8,128)(2,1)S(1)} %get-tuple-element.57), channel_id=1, source_target_pairs={{0,1},{1,0},{2,3},{3,2},{4,5},{5,4},{6,7},{7,6},{8,9},{9,8},{10,11... | collective-permute-start | bytes 983048 | tf_op jit(solution)/shard_map/ppermute | solution.py:342
  21.5 3.3 %copy-start.10 = (s32[8,1,128]{2,1,0:T(1,128)}, s32[8,1,128]{2,1,0:T(1,128)S(1)}, u32[]{:S(2)}) copy-start(s32[8,1,128]{2,1,0:T(1,128)S(1)} %all-to-all-done.asked) | copy-start | bytes 12292
  21.6 9.1 %collective-permute-start.3 = (bf16[2,128,640]{2,1,0:T(8,128)(2,1)S(1)}, bf16[2,128,640]{2,1,0:T(8,128)(2,1)S(1)}, u32[]{:S(2)}, u32[]{:S(2)}) collective-permute-start(bf16[2,128,640]{2,1,0:T(8,128)(2,1)S(1)} %get-tuple-element.62), channel_id=1, source_target_pairs={{0,1},{1,0},{2,3},{3,2},{4,5},{5,4},{6,7},{7,6},{8,9},{9,8},{10,11... | collective-permute-start | bytes 983048 | tf_op jit(solution)/shard_map/ppermute | solution.py:342
  22.2 8.5 %collective-permute-start.5 = (bf16[640,256]{1,0:T(8,128)(2,1)}, bf16[640,256]{1,0:T(8,128)(2,1)}, u32[]{:S(2)}, u32[]{:S(2)}) collective-permute-start(bf16[640,256]{1,0:T(8,128)(2,1)} %collective-permute-done.refs_7_), channel_id=1, source_target_pairs={{2,4},{3,5},{4,2},{5,3},{10,12},{11,13},{12,10},{13,11},{18,20},{1... | collective-permute-start | bytes 983048 | tf_op jit(solution)/shard_map/ppermute | solution.py:381
  23.6 9.7 %collective-permute-start.6 = (bf16[640,256]{1,0:T(8,128)(2,1)S(1)}, bf16[640,256]{1,0:T(8,128)(2,1)S(1)}, u32[]{:S(2)}, u32[]{:S(2)}) collective-permute-start(bf16[640,256]{1,0:T(8,128)(2,1)S(1)} %collective-permute-done.1), channel_id=1, source_target_pairs={{2,0},{3,1},{4,6},{5,7},{10,8},{11,9},{12,14},{13,15},{18,16},{19,... | collective-permute-start | bytes 983048 | tf_op jit(solution)/shard_map/ppermute | solution.py:382
  24.9 34.9 %copy-start.3 = (bf16[8,256,320]{2,1,0:T(8,128)(2,1)S(1)}, bf16[8,256,320]{2,1,0:T(8,128)(2,1)}, u32[]{:S(2)}) copy-start(bf16[8,256,320]{2,1,0:T(8,128)(2,1)} %pair_columns.1.xs_ref) | copy-start | bytes 3932164
  30.7 2.6 %copy-start.11 = (bf16[2,128,640]{2,1,0:T(8,128)(2,1)}, bf16[2,128,640]{2,1,0:T(8,128)(2,1)S(1)}, u32[]{:S(2)}) copy-start(bf16[2,128,640]{2,1,0:T(8,128)(2,1)S(1)} %collective-permute-done.3.refs_3_) | copy-start | bytes 983044
  33.3 26.5 %all-to-all-start.1 = ((bf16[8,384,128]{2,1,0:T(8,128)(2,1)}), bf16[8,384,128]{2,1,0:T(8,128)(2,1)S(1)}, u32[]{:S(2)}, u32[]{:S(2)}) async-start(bf16[8,384,128]{2,1,0:T(8,128)(2,1)} %get-tuple-element.68), calls=%async_computation.1 | async-start | bytes 1572864 | tf_op jit(solution)/shard_map/all_to_all | solution.py:407
  37.9 14.1 %collective-permute-start.11 = (bf16[2,128,640]{2,1,0:T(8,128)(2,1)}, bf16[2,128,640]{2,1,0:T(8,128)(2,1)}, u32[]{:S(2)}, u32[]{:S(2)}) collective-permute-start(bf16[2,128,640]{2,1,0:T(8,128)(2,1)} %collective-permute-done.2.refs_2_), channel_id=1, source_target_pairs={{0,16},{16,0},{1,17},{17,1},{2,18},{18,2},{3,19},{19,3},{4,20},{20... | collective-permute-start | bytes 983048 | tf_op jit(solution)/shard_map/ppermute | solution.py:348
  38.4 13.7 %collective-permute-start.12 = (bf16[2,128,640]{2,1,0:T(8,128)(2,1)}, bf16[2,128,640]{2,1,0:T(8,128)(2,1)S(1)}, u32[]{:S(2)}, u32[]{:S(2)}) collective-permute-start(bf16[2,128,640]{2,1,0:T(8,128)(2,1)} %copy-done.11), channel_id=1, source_target_pairs={{0,16},{16,0},{1,17},{17,1},{2,18},{18,2},{3,19},{19,3},{4,20},{20... | collective-permute-start | bytes 983048 | tf_op jit(solution)/shard_map/ppermute | solution.py:348
  40.0 18.3 %collective-permute-start.10 = (bf16[640,256]{1,0:T(8,128)(2,1)}, bf16[640,256]{1,0:T(8,128)(2,1)S(1)}, u32[]{:S(2)}, u32[]{:S(2)}) collective-permute-start(bf16[640,256]{1,0:T(8,128)(2,1)} %collective-permute-done.5.refs_9_), channel_id=1, source_target_pairs={{2,0},{3,1},{4,6},{5,7},{10,8},{11,9},{12,14},{13,15},{18,16},{19,... | collective-permute-start | bytes 983048 | tf_op jit(solution)/shard_map/ppermute | solution.py:410
  41.2 0.7 copy-start.4
  51.4 7.6 %copy-start.8 = (bf16[640,256]{1,0:T(8,128)(2,1)}, bf16[640,256]{1,0:T(8,128)(2,1)S(1)}, u32[]{:S(2)}) copy-start(bf16[640,256]{1,0:T(8,128)(2,1)S(1)} %broadcast_select_fusion.refs_8_) | copy-start | bytes 983044
  51.5 6.8 %collective-permute-start.9 = (bf16[640,256]{1,0:T(8,128)(2,1)S(1)}, bf16[640,256]{1,0:T(8,128)(2,1)S(1)}, u32[]{:S(2)}, u32[]{:S(2)}) collective-permute-start(bf16[640,256]{1,0:T(8,128)(2,1)S(1)} %broadcast_select_fusion.refs_8_), channel_id=1, source_target_pairs={{0,8},{8,0},{1,9},{9,1},{2,10},{10,2},{3,11},{11,3},{4,12},{12,4},... | collective-permute-start | bytes 983048 | tf_op jit(solution)/shard_map/ppermute | solution.py:345
  51.5 6.8 %collective-permute-start.7 = (bf16[640,256]{1,0:T(8,128)(2,1)}, bf16[640,256]{1,0:T(8,128)(2,1)S(1)}, u32[]{:S(2)}, u32[]{:S(2)}) collective-permute-start(bf16[640,256]{1,0:T(8,128)(2,1)} %copy-done.9), channel_id=1, source_target_pairs={{0,8},{8,0},{1,9},{9,1},{2,10},{10,2},{3,11},{11,3},{4,12},{12,4},... | collective-permute-start | bytes 983048 | tf_op jit(solution)/shard_map/ppermute | solution.py:345
  52.0 7.0 %collective-permute-start.8 = (bf16[640,256]{1,0:T(8,128)(2,1)}, bf16[640,256]{1,0:T(8,128)(2,1)}, u32[]{:S(2)}, u32[]{:S(2)}) collective-permute-start(bf16[640,256]{1,0:T(8,128)(2,1)} %collective-permute-done.refs_7_), channel_id=1, source_target_pairs={{0,8},{8,0},{1,9},{9,1},{2,10},{10,2},{3,11},{11,3},{4,12},{12,4},... | collective-permute-start | bytes 983048 | tf_op jit(solution)/shard_map/ppermute | solution.py:345
  52.1 6.2 %copy-start.12 = (bf16[2,128,640]{2,1,0:T(8,128)(2,1)}, bf16[2,128,640]{2,1,0:T(8,128)(2,1)S(1)}, u32[]{:S(2)}) copy-start(bf16[2,128,640]{2,1,0:T(8,128)(2,1)S(1)} %collective-permute-done.12.refs_5_) | copy-start | bytes 983044
  58.3 0.7 copy-start.13
  58.3 0.9 copy-start.15
  59.1 0.7 copy-start.16
  59.8 1.0 %copy-start.7 = (bf16[128,1024]{1,0:T(8,128)(2,1)S(1)}, bf16[128,1024]{1,0:T(8,128)(2,1)}, u32[]{:S(2)}) copy-start(bf16[128,1024]{1,0:T(8,128)(2,1)} %g_ref.1) | copy-start | bytes 786436
  60.7 6.7 %copy-start.14 = (bf16[640,256]{1,0:T(8,128)(2,1)S(1)}, bf16[640,256]{1,0:T(8,128)(2,1)}, u32[]{:S(2)}) copy-start(bf16[640,256]{1,0:T(8,128)(2,1)} %copy-done.13) | copy-start | bytes 983044
  63.8 22.9 %all-to-all-start.2 = ((bf16[8,384,128]{2,1,0:T(8,128)(2,1)}), bf16[8,384,128]{2,1,0:T(8,128)(2,1)S(1)}, u32[]{:S(2)}, u32[]{:S(2)}) async-start(bf16[8,384,128]{2,1,0:T(8,128)(2,1)} %get-tuple-element.85.refs_16_), calls=%async_computation.2 | async-start | bytes 1572864 | tf_op jit(solution)/shard_map/all_to_all | solution.py:455
  67.3 19.3 %copy-start.5 = (s32[8]{0:T(128)S(1)}, s32[8]{0:T(128)}, u32[]{:S(2)}) copy-start(s32[8]{0:T(128)} %get-tuple-element.69.after_ref.rows_here) | copy-start | bytes 100
  67.3 1.9 %collective-permute-start.13 = (bf16[640,256]{1,0:T(8,128)(2,1)}, bf16[640,256]{1,0:T(8,128)(2,1)S(1)}, u32[]{:S(2)}, u32[]{:S(2)}) collective-permute-start(bf16[640,256]{1,0:T(8,128)(2,1)} %collective-permute-done.5.refs_9_), channel_id=1, source_target_pairs={{0,8},{8,0},{1,9},{9,1},{2,10},{10,2},{3,11},{11,3},{4,12},{12,4},... | collective-permute-start | bytes 983048 | tf_op jit(solution)/shard_map/ppermute | solution.py:345
  67.4 2.1 %collective-permute-start.14 = (bf16[640,256]{1,0:T(8,128)(2,1)S(1)}, bf16[640,256]{1,0:T(8,128)(2,1)S(1)}, u32[]{:S(2)}, u32[]{:S(2)}) collective-permute-start(bf16[640,256]{1,0:T(8,128)(2,1)S(1)} %copy-done.14), channel_id=1, source_target_pairs={{0,8},{8,0},{1,9},{9,1},{2,10},{10,2},{3,11},{11,3},{4,12},{12,4},... | collective-permute-start | bytes 983048 | tf_op jit(solution)/shard_map/ppermute | solution.py:345
  69.2 0.7 copy-start.17
  69.9 0.7 copy-start.18
  75.7 7.8 %collective-permute-start.15 = (bf16[128,512]{1,0:T(8,128)(2,1)}, bf16[128,512]{1,0:T(8,128)(2,1)S(1)}, u32[]{:S(2)}, u32[]{:S(2)}) collective-permute-start(bf16[128,512]{1,0:T(8,128)(2,1)} %get-tuple-element.93), channel_id=1, source_target_pairs={{0,1},{1,0},{2,3},{3,2},{4,5},{5,4},{6,7},{7,6},{8,9},{9,8},{10,11... | collective-permute-start | bytes 393224 | tf_op jit(solution)/shard_map/ppermute | solution.py:342
  77.7 8.3 %collective-permute-start.16 = (bf16[128,512]{1,0:T(8,128)(2,1)}, bf16[128,512]{1,0:T(8,128)(2,1)S(1)}, u32[]{:S(2)}, u32[]{:S(2)}) collective-permute-start(bf16[128,512]{1,0:T(8,128)(2,1)} %get-tuple-element.94), channel_id=1, source_target_pairs={{0,16},{16,0},{1,17},{17,1},{2,18},{18,2},{3,19},{19,3},{4,20},{20... | collective-permute-start | bytes 393224 | tf_op jit(solution)/shard_map/ppermute | solution.py:348
  78.1 7.9 %collective-permute-start.17 = (bf16[128,512]{1,0:T(8,128)(2,1)}, bf16[128,512]{1,0:T(8,128)(2,1)S(1)}, u32[]{:S(2)}, u32[]{:S(2)}) collective-permute-start(bf16[128,512]{1,0:T(8,128)(2,1)} %get-tuple-element.95), channel_id=1, source_target_pairs={{0,17},{1,16},{2,19},{3,18},{4,21},{5,20},{6,23},{7,22},{16,1},{17... | collective-permute-start | bytes 393224 | tf_op jit(solution)/shard_map/ppermute | solution.py:456
  86.6 2.4 %collective-permute-start.19 = (bf16[8,384,128]{2,1,0:T(8,128)(2,1)S(1)}, bf16[8,384,128]{2,1,0:T(8,128)(2,1)S(1)}, u32[]{:S(2)}, u32[]{:S(2)}) collective-permute-start(bf16[8,384,128]{2,1,0:T(8,128)(2,1)S(1)} %all-to-all-done.2.rest_0_), channel_id=1, source_target_pairs={{0,8},{8,0},{1,9},{9,1},{2,10},{10,2},{3,11},{11,3},{4,12},{12,4},... | collective-permute-start | bytes 2359304 | tf_op jit(solution)/shard_map/ppermute | solution.py:345
  86.6 2.3 %collective-permute-start.18 = (s32[8]{0:T(128)S(1)}, s32[8]{0:T(128)S(1)}, u32[]{:S(2)}, u32[]{:S(2)}) collective-permute-start(s32[8]{0:T(128)S(1)} %copy-done.5), channel_id=1, source_target_pairs={{0,8},{8,0},{1,9},{9,1},{2,10},{10,2},{3,11},{11,3},{4,12},{12,4},... | collective-permute-start | bytes 104 | tf_op jit(solution)/shard_map/ppermute | solution.py:345
  89.0 2.9 %copy-start.1 = (bf16[640,512]{1,0:T(8,128)(2,1)S(1)}, bf16[640,512]{1,0:T(8,128)(2,1)}, u32[]{:S(2)}) copy-start(bf16[640,512]{1,0:T(8,128)(2,1)} %param.9) | copy-start | bytes 1966084

commit v19 on v18

--- a/solution.py
+++ b/solution.py
@@ -421,7 +421,7 @@
     inside = (z == 1) | (z == 2)
     quarter = [half, near, jnp.where(inside, over, passed)]
     quarter_core = [other_core(w) for w in quarter]
-    panels, quarter_core, passed_near, y_far = lax.optimization_barrier((panels, quarter_core, passed_near, y_far))
+    panels, quarter_core, y_far = lax.optimization_barrier((panels, quarter_core, y_far))
 
     terms, lifted = pl.pallas_call(
         functools.partial(adapter_kernel, group, down_chunks),
@@ -433,7 +433,7 @@
         cost_estimate=cost(flops=3 << 30, read=8 << 20),
         name="adapter",
     )(xs, cotangent, panels, cleared)
-    _, over_near, passed_near = lax.optimization_barrier((terms, over_near, passed_near))
+    terms, over_near, passed_near = lax.optimization_barrier((terms, over_near, passed_near))
     last = [over_near, passed_near]
     quarters = quarter + last + quarter_core + [other_core(w) for w in last]
     sums = [jax.ShapeDtypeStruct((token_rows, parts * width), kind) for kind in (jnp.float32,) + (jnp.bfloat16,) * 3]

time: 92.5 us -> 95.3 us (1.030)
  starting transfers between devices: 33.8 us -> 36.3 us
  local copies, waits for them, and re-layouts: 6.23 us -> 5.22 us
    ppermute x4, waiting for transfers between devices: 2.53 us -> 0.01 us  [other_part(): lax.ppermute(value, 'parts', [(a, parts - 1 - a) for a in range(parts)])]
    ppermute x1, waiting for transfers between devices: 6.18 us -> 3.71 us  [fast_body(): passed_near = lax.ppermute(over_near, 'tensor', ends)]
    all_to_all x1, starting transfers between devices: 3.55 us -> 6 us  [fast_body(): back = lax.all_to_all(terms, 'tensor', 0, 0)]
    ppermute x1, waiting for transfers between devices: 0.01 us -> 2.35 us  [fast_body(): lax.ppermute(to_both, ('parts', 'tensor'), opposite)]
    all_to_all x1, waiting for transfers between devices: 0.01 us -> 1.86 us  [fast_body(): panels = lax.all_to_all(sent, 'tensor', 0, 0)]
    unnamed x38 -> x36, local copies, waits for them, and re-layouts: 5.61 us -> 4.6 us
  transfers between devices with their start and end apart: 23 -> 23, of which waited for: 9 -> 11; matrix products, arithmetic and copies ran while one was open for 2% -> 2% of each run, Pallas kernels for 26% -> 29%
where the time goes in v19:
time: 95.3 us; the launch traced here: 94.9 us
  starting transfers between devices  36.3 us (38%)
  Pallas kernels  30.6 us (32%)
  waiting for transfers between devices  19.3 us (20%)
  local copies, waits for them, and re-layouts  5.22 us (5%)
  other arithmetic  1.85 us (2%)
  between operations  1.63 us (2%)
    ppermute x4, starting transfers between devices, exchange(): return lax.ppermute(value, 'tensor', [(t, t ^ s) for t in range(group)])  10.5 us
    pallas_call x1, Pallas kernels, fast_body(): pl.pallas_call(zero_kernel, out_shape=(down_shape, up_shape, token), in_s...  9.48 us
    all_to_all x1, starting transfers between devices, fast_body(): back = lax.all_to_all(terms, 'tensor', 0, 0)  6 us
    pallas_call x1, Pallas kernels, fast_body(): pl.pallas_call(gather_kernel, out_shape=(pieces, jax.ShapeDtypeStruct((gr...  5.76 us
    pallas_call x1, Pallas kernels, fast_body(): pl.pallas_call(base_kernel, out_shape=sums, in_specs=[ANY] * (7 + len(qua...  5.01 us
    ppermute x4, waiting for transfers between devices, exchange(): return lax.ppermute(value, 'tensor', [(t, t ^ s) for t in range(group)])  4.98 us
    all_to_all x1, starting transfers between devices, fast_body(): panels = lax.all_to_all(sent, 'tensor', 0, 0)  4.64 us
    unnamed x36, local copies, waits for them, and re-layouts  4.6 us
  transfers between devices with their start and end apart: 23, of which 11 were waited for; matrix products, arithmetic and copies ran while one was open for 2% of the time, Pallas kernels for 29%

profile of v19, /device:TPU:0, one launch (start us, length us, event | category | flops | bytes accessed | tf_op | source)
XLA Modules:
  0.0 94.9 jit_solution(5123584208052246955)
XLA Ops:
  0.6 0.0 copy-start
  1.4 0.6 broadcast_in_dim.2
  2.0 0.7 collective-permute-start.1
  2.7 5.9 %collective-permute-start = (bf16[640,256]{1,0:T(8,128)(2,1)S(1)}, bf16[640,256]{1,0:T(8,128)(2,1)}, u32[]{:S(2)}, u32[]{:S(2)}) collective-permute-start(bf16[640,256]{1,0:T(8,128)(2,1)S(1)} %constant_dynamic-slice_fusion.refs_6_), channel_id=1, source_target_pairs={{0,2},{1,3},{2,0},{3,1},{4,6},{5,7},{6,4},{7,5},{8,10},{9,11},{10,... | collective-permute-start | bytes 983048 | tf_op jit(solution)/shard_map/ppermute | solution.py:342
  8.6 1.3 %copy-done.2 = bf16[128,5120]{1,0:T(8,128)(2,1)S(1)} copy-done((bf16[128,5120]{1,0:T(8,128)(2,1)S(1)}, bf16[128,5120]{1,0:T(8,128)(2,1)}, u32[]{:S(2)}) %copy-start.2) | copy-done | bytes 1310744
  9.9 0.1 split_tokens.1
  10.0 1.6 %collective-permute-start.4 = (bf16[4,128,640]{2,1,0:T(8,128)(2,1)S(1)}, bf16[4,128,640]{2,1,0:T(8,128)(2,1)}, u32[]{:S(2)}, u32[]{:S(2)}) collective-permute-start(bf16[4,128,640]{2,1,0:T(8,128)(2,1)S(1)} %get-tuple-element.55.refs_0_), channel_id=1, source_target_pairs={{0,16},{16,0},{1,17},{17,1},{2,18},{18,2},{3,19},{19,3},{4,20},{20... | collective-permute-start | bytes 1966088 | tf_op jit(solution)/shard_map/ppermute | solution.py:348
  11.6 3.6 %all-to-all-start = ((s32[8,1,128]{2,1,0:T(1,128)}), s32[8,1,128]{2,1,0:T(1,128)S(1)}, u32[]{:S(2)}, u32[]{:S(2)}) async-start(s32[8,1,128]{2,1,0:T(1,128)} %broadcast_in_dim.2), calls=%async_computation | async-start | bytes 8192 | tf_op jit(solution)/shard_map/all_to_all | solution.py:351
  15.2 2.0 %collective-permute-start.2 = (bf16[2,128,640]{2,1,0:T(8,128)(2,1)S(1)}, bf16[2,128,640]{2,1,0:T(8,128)(2,1)}, u32[]{:S(2)}, u32[]{:S(2)}) collective-permute-start(bf16[2,128,640]{2,1,0:T(8,128)(2,1)S(1)} %get-tuple-element.57), channel_id=1, source_target_pairs={{0,1},{1,0},{2,3},{3,2},{4,5},{5,4},{6,7},{7,6},{8,9},{9,8},{10,11... | collective-permute-start | bytes 983048 | tf_op jit(solution)/shard_map/ppermute | solution.py:342
  17.2 3.9 %pair_columns.1.xs_ref = bf16[8,256,320]{2,1,0:T(8,128)(2,1)} custom-call(bf16[128,5120]{1,0:T(8,128)(2,1)} %x_ref.1), custom_call_target="tpu_custom_call" | custom-call | bytes 134217728 | tf_op jit(solution)/shard_map/pair_columns/pallas_call | solution.py:365
  21.1 0.5 all-to-all-done.asked
  21.5 0.0 collective-permute-done.1
  21.5 0.0 collective-permute-done.refs_7_
  21.6 0.6 collective-permute-start.3
  22.2 1.4 %collective-permute-start.5 = (bf16[640,256]{1,0:T(8,128)(2,1)}, bf16[640,256]{1,0:T(8,128)(2,1)}, u32[]{:S(2)}, u32[]{:S(2)}) collective-permute-start(bf16[640,256]{1,0:T(8,128)(2,1)} %collective-permute-done.refs_7_), channel_id=1, source_target_pairs={{2,4},{3,5},{4,2},{5,3},{10,12},{11,13},{12,10},{13,11},{18,20},{1... | collective-permute-start | bytes 983048 | tf_op jit(solution)/shard_map/ppermute | solution.py:381
  23.6 1.3 %collective-permute-start.6 = (bf16[640,256]{1,0:T(8,128)(2,1)S(1)}, bf16[640,256]{1,0:T(8,128)(2,1)S(1)}, u32[]{:S(2)}, u32[]{:S(2)}) collective-permute-start(bf16[640,256]{1,0:T(8,128)(2,1)S(1)} %collective-permute-done.1), channel_id=1, source_target_pairs={{2,0},{3,1},{4,6},{5,7},{10,8},{11,9},{12,14},{13,15},{18,16},{19,... | collective-permute-start | bytes 983048 | tf_op jit(solution)/shard_map/ppermute | solution.py:382
  24.9 5.8 %pick_panels.1 = (bf16[8,384,128]{2,1,0:T(8,128)(2,1)}, s32[8]{0:T(128)}) custom-call(s32[8,1,128]{2,1,0:T(1,128)} %copy-done.10, s32[256]{0:T(256)} %slot_of.1, bf16[32,320,8,128]{3,2,1,0:T(8,128)(2,1)} %bitcast.18, bf16[32,64,8,128]{3,2,1,0:T(8,128)(2,1)} %bitcast.20), custom_call_target="tpu_custom_call" | custom-call | bytes 41943040 | tf_op jit(solution)/shard_map/pick_panels/pallas_call | solution.py:388
  30.7 0.0 collective-permute-done.2.refs_2_
  30.7 0.0 collective-permute-done.4.refs_1_
  30.7 0.0 collective-permute-done.3.refs_3_
  30.7 0.0 collective-permute-done.5.refs_9_
  30.7 2.6 %collective-permute-done.6 = bf16[640,256]{1,0:T(8,128)(2,1)S(1)} collective-permute-done((bf16[640,256]{1,0:T(8,128)(2,1)S(1)}, bf16[640,256]{1,0:T(8,128)(2,1)S(1)}, u32[]{:S(2)}, u32[]{:S(2)}) %collective-permute-start.6) | collective-permute-done | bytes 327712 | tf_op jit(solution)/shard_map/ppermute | solution.py:382
  33.3 4.6 %all-to-all-start.1 = ((bf16[8,384,128]{2,1,0:T(8,128)(2,1)}), bf16[8,384,128]{2,1,0:T(8,128)(2,1)S(1)}, u32[]{:S(2)}, u32[]{:S(2)}) async-start(bf16[8,384,128]{2,1,0:T(8,128)(2,1)} %get-tuple-element.68), calls=%async_computation.1 | async-start | bytes 1572864 | tf_op jit(solution)/shard_map/all_to_all | solution.py:407
  37.9 0.5 collective-permute-start.10
  38.5 1.5 %collective-permute-start.11 = (bf16[2,128,640]{2,1,0:T(8,128)(2,1)}, bf16[2,128,640]{2,1,0:T(8,128)(2,1)S(1)}, u32[]{:S(2)}, u32[]{:S(2)}) collective-permute-start(bf16[2,128,640]{2,1,0:T(8,128)(2,1)} %copy-done.11), channel_id=1, source_target_pairs={{0,16},{16,0},{1,17},{17,1},{2,18},{18,2},{3,19},{19,3},{4,20},{20... | collective-permute-start | bytes 983048 | tf_op jit(solution)/shard_map/ppermute | solution.py:348
  40.0 0.6 copy-done.4
  40.5 9.5 %clear_rows.1 = (f32[16,320,8,1,128]{4,3,2,1,0:T(1,128)}, f32[16,64,8,1,128]{4,3,2,1,0:T(1,128)}, s32[1]{0:T(128)}) custom-call(s32[8]{0:T(128)S(1)} %copy-done.4), custom_call_target="tpu_custom_call" | custom-call | bytes 29360128 | tf_op jit(solution)/shard_map/clear_rows/pallas_call | solution.py:414
  50.1 0.1 collective-permute-start.9
  50.2 0.5 collective-permute-start.7
  50.7 0.1 collective-permute-start.8
  50.7 0.0 collective-permute-done.10.refs_4_
  50.7 1.3 %collective-permute-start.12 = (bf16[640,256]{1,0:T(8,128)(2,1)}, bf16[640,256]{1,0:T(8,128)(2,1)}, u32[]{:S(2)}, u32[]{:S(2)}) collective-permute-start(bf16[640,256]{1,0:T(8,128)(2,1)} %collective-permute-done.5.refs_9_), channel_id=1, source_target_pairs={{2,0},{3,1},{4,6},{5,7},{10,8},{11,9},{12,14},{13,15},{18,16},{19,... | collective-permute-start | bytes 983048 | tf_op jit(solution)/shard_map/ppermute | solution.py:410
  52.0 0.0 collective-permute-done.11.refs_5_
  52.1 0.0 collective-permute-done.9.refs_13_
  52.1 0.4 collective-permute-done.7.refs_11_
  52.5 0.3 copy-done.13
  52.8 0.3 collective-permute-done.8.refs_12_
  53.1 0.4 copy-done.15
  53.5 1.9 %all-to-all-done.1.pieces = bf16[8,384,128]{2,1,0:T(8,128)(2,1)S(1)} async-done(((bf16[8,384,128]{2,1,0:T(8,128)(2,1)}), bf16[8,384,128]{2,1,0:T(8,128)(2,1)S(1)}, u32[]{:S(2)}, u32[]{:S(2)}) %all-to-all-start.1) | async-done | bytes 786464 | tf_op jit(solution)/shard_map/all_to_all | solution.py:407
  55.4 0.9 %copy-done.7 = bf16[128,1024]{1,0:T(8,128)(2,1)S(1)} copy-done((bf16[128,1024]{1,0:T(8,128)(2,1)S(1)}, bf16[128,1024]{1,0:T(8,128)(2,1)}, u32[]{:S(2)}) %copy-start.7) | copy-done | bytes 262168
  56.3 3.0 %adapter.1 = (bf16[8,384,128]{2,1,0:T(8,128)(2,1)}, f32[128,1024]{1,0:T(8,128)S(1)}) custom-call(bf16[8,256,320]{2,1,0:T(8,128)(2,1)S(1)} %copy-done.3, bf16[128,1024]{1,0:T(8,128)(2,1)S(1)} %copy-done.7, bf16[8,384,128]{2,1,0:T(8,128)(2,1)S(1)} %all-to-all-done.1.pieces, s32[1]{0:T(128)} %get-tuple-element.83._), custom_call_target="tpu_custom_call" | custom-call | flops 3221225472 | bytes 8388608 | tf_op jit(solution)/shard_map/adapter/pallas_call | solution.py:426
  59.3 3.7 %collective-permute-done.12.refs_10_ = bf16[640,256]{1,0:T(8,128)(2,1)} collective-permute-done((bf16[640,256]{1,0:T(8,128)(2,1)}, bf16[640,256]{1,0:T(8,128)(2,1)}, u32[]{:S(2)}, u32[]{:S(2)}) %collective-permute-start.12) | collective-permute-done | bytes 327712 | tf_op jit(solution)/shard_map/ppermute | solution.py:410
  63.0 6.0 %all-to-all-start.2 = ((bf16[8,384,128]{2,1,0:T(8,128)(2,1)}), bf16[8,384,128]{2,1,0:T(8,128)(2,1)S(1)}, u32[]{:S(2)}, u32[]{:S(2)}) async-start(bf16[8,384,128]{2,1,0:T(8,128)(2,1)} %get-tuple-element.91.refs_16_), calls=%async_computation.2 | async-start | bytes 1572864 | tf_op jit(solution)/shard_map/all_to_all | solution.py:455
  69.0 0.1 collective-permute-start.13
  69.1 0.5 collective-permute-start.14
  69.6 1.3 %collective-permute-done.13.refs_14_ = bf16[640,256]{1,0:T(8,128)(2,1)S(1)} collective-permute-done((bf16[640,256]{1,0:T(8,128)(2,1)}, bf16[640,256]{1,0:T(8,128)(2,1)S(1)}, u32[]{:S(2)}, u32[]{:S(2)}) %collective-permute-start.13) | collective-permute-done | bytes 327712 | tf_op jit(solution)/shard_map/ppermute | solution.py:345
  70.9 0.5 collective-permute-done.14.refs_15_
  71.4 0.2 copy-done.16
  71.6 0.7 copy-done.17
  72.4 5.0 %frozen_part.1 = (f32[128,512]{1,0:T(8,128)}, bf16[128,512]{1,0:T(8,128)(2,1)}, bf16[128,512]{1,0:T(8,128)(2,1)}, bf16[128,512]{1,0:T(8,128)(2,1)}) custom-call(bf16[4,128,640]{2,1,0:T(8,128)(2,1)} %copy-done.6, bf16[4,128,640]{2,1,0:T(8,128)(2,1)} %collective-permute-done.4.refs_1_, bf16[2,128,640]{2,1,0:T(8,128)(2,1)} %collective-permute-done.2.refs_2_, ...), custom_call_target="tpu_custom_call" | custom-call | flops 4294967296 | bytes 8388608 | tf_op jit(solution)/shard_map/frozen_part/pallas_call | solution.py:440
  77.4 2.0 %collective-permute-start.15 = (bf16[128,512]{1,0:T(8,128)(2,1)}, bf16[128,512]{1,0:T(8,128)(2,1)S(1)}, u32[]{:S(2)}, u32[]{:S(2)}) collective-permute-start(bf16[128,512]{1,0:T(8,128)(2,1)} %get-tuple-element.93), channel_id=1, source_target_pairs={{0,1},{1,0},{2,3},{3,2},{4,5},{5,4},{6,7},{7,6},{8,9},{9,8},{10,11... | collective-permute-start | bytes 393224 | tf_op jit(solution)/shard_map/ppermute | solution.py:342
  79.4 0.5 collective-permute-start.16
  79.9 1.0 %collective-permute-start.17 = (bf16[128,512]{1,0:T(8,128)(2,1)}, bf16[128,512]{1,0:T(8,128)(2,1)S(1)}, u32[]{:S(2)}, u32[]{:S(2)}) collective-permute-start(bf16[128,512]{1,0:T(8,128)(2,1)} %get-tuple-element.95), channel_id=1, source_target_pairs={{0,17},{1,16},{2,19},{3,18},{4,21},{5,20},{6,23},{7,22},{16,1},{17... | collective-permute-start | bytes 393224 | tf_op jit(solution)/shard_map/ppermute | solution.py:456
  80.9 5.0 %collective-permute-done.15 = bf16[128,512]{1,0:T(8,128)(2,1)S(1)} collective-permute-done((bf16[128,512]{1,0:T(8,128)(2,1)}, bf16[128,512]{1,0:T(8,128)(2,1)S(1)}, u32[]{:S(2)}, u32[]{:S(2)}) %collective-permute-start.15) | collective-permute-done | bytes 131104 | tf_op jit(solution)/shard_map/ppermute | solution.py:342
  85.9 0.0 collective-permute-done.16
  85.9 2.4 %collective-permute-done.17 = bf16[128,512]{1,0:T(8,128)(2,1)S(1)} collective-permute-done((bf16[128,512]{1,0:T(8,128)(2,1)}, bf16[128,512]{1,0:T(8,128)(2,1)S(1)}, u32[]{:S(2)}, u32[]{:S(2)}) %collective-permute-start.17) | collective-permute-done | bytes 131104 | tf_op jit(solution)/shard_map/ppermute | solution.py:456
  88.3 0.8 all-to-all-done.2.rest_0_
  89.1 0.0 collective-permute-start.19
  89.1 0.5 collective-permute-start.18
  89.6 1.0 %convert_add_fusion = (f32[128,512]{1,0:T(8,128)S(1)}, f32[128,512]{1,0:T(8,128)S(1)}) fusion(bf16[128,512]{1,0:T(8,128)(2,1)S(1)} %collective-permute-done.17, bf16[128,512]{1,0:T(8,128)(2,1)S(1)} %collective-permute-done.16, f32[128,512]{1,0:T(8,128)} %get-tuple-element.92, bf16[128,512]{1,0:T(8,128)(2,1)S(1)} %collective-permute-done.15), kind=kLoop, calls=%fused_computation.3 | loop fusion | flops 327680 | bytes 1179648 | tf_op jit(solution)/shard_map/add | solution.py:482
  90.7 0.8 fusion
  91.4 0.0 collective-permute-done.18.rows_core
  91.4 0.0 collective-permute-done.19.rest_1_
  91.4 3.4 %place_rows.1 = (f32[16,320,8,1,128]{4,3,2,1,0:T(1,128)}, f32[16,64,8,1,128]{4,3,2,1,0:T(1,128)}) custom-call(s32[8]{0:T(128)S(1)} %copy-done.5, s32[8]{0:T(128)S(1)} %collective-permute-done.18.rows_core, bf16[8,384,128]{2,1,0:T(8,128)(2,1)S(1)} %all-to-all-done.2.rest_0_, ...), custom_call_target="tpu_custom_call", output_to_operand_aliasing={{0}: (4, {}), {1}: (5, {})} | custom-call | bytes 16777216 | tf_op jit(solution)/shard_map/place_rows/pallas_call | solution.py:460
  (31 shorter events, 0.2 us)
Async XLA Ops:
  0.6 1.3 %copy-start = (bf16[640,512]{1,0:T(8,128)(2,1)S(1)}, bf16[640,512]{1,0:T(8,128)(2,1)}, u32[]{:S(2)}) copy-start(bf16[640,512]{1,0:T(8,128)(2,1)} %param.9) | copy-start | bytes 1966084
  2.0 22.9 %copy-start.9 = (bf16[640,256]{1,0:T(8,128)(2,1)}, bf16[640,256]{1,0:T(8,128)(2,1)S(1)}, u32[]{:S(2)}) copy-start(bf16[640,256]{1,0:T(8,128)(2,1)S(1)} %constant_dynamic-slice_fusion.refs_6_) | copy-start | bytes 983044
  2.0 19.6 %collective-permute-start.1 = (bf16[640,256]{1,0:T(8,128)(2,1)S(1)}, bf16[640,256]{1,0:T(8,128)(2,1)S(1)}, u32[]{:S(2)}, u32[]{:S(2)}) collective-permute-start(bf16[640,256]{1,0:T(8,128)(2,1)S(1)} %constant_dynamic-slice_fusion.refs_6_), channel_id=1, source_target_pairs={{2,4},{3,5},{4,2},{5,3},{10,12},{11,13},{12,10},{13,11},{18,20},{1... | collective-permute-start | bytes 983048 | tf_op jit(solution)/shard_map/ppermute | solution.py:378
  2.7 18.9 %collective-permute-start = (bf16[640,256]{1,0:T(8,128)(2,1)S(1)}, bf16[640,256]{1,0:T(8,128)(2,1)}, u32[]{:S(2)}, u32[]{:S(2)}) collective-permute-start(bf16[640,256]{1,0:T(8,128)(2,1)S(1)} %constant_dynamic-slice_fusion.refs_6_), channel_id=1, source_target_pairs={{0,2},{1,3},{2,0},{3,1},{4,6},{5,7},{6,4},{7,5},{8,10},{9,11},{10,... | collective-permute-start | bytes 983048 | tf_op jit(solution)/shard_map/ppermute | solution.py:342
  8.6 1.3 %copy-start.2 = (bf16[128,5120]{1,0:T(8,128)(2,1)S(1)}, bf16[128,5120]{1,0:T(8,128)(2,1)}, u32[]{:S(2)}) copy-start(bf16[128,5120]{1,0:T(8,128)(2,1)} %x_ref.1) | copy-start | bytes 3932164
  10.0 20.7 %copy-start.6 = (bf16[4,128,640]{2,1,0:T(8,128)(2,1)}, bf16[4,128,640]{2,1,0:T(8,128)(2,1)S(1)}, u32[]{:S(2)}) copy-start(bf16[4,128,640]{2,1,0:T(8,128)(2,1)S(1)} %get-tuple-element.55.refs_0_) | copy-start | bytes 1966084
  10.0 20.7 %collective-permute-start.4 = (bf16[4,128,640]{2,1,0:T(8,128)(2,1)S(1)}, bf16[4,128,640]{2,1,0:T(8,128)(2,1)}, u32[]{:S(2)}, u32[]{:S(2)}) collective-permute-start(bf16[4,128,640]{2,1,0:T(8,128)(2,1)S(1)} %get-tuple-element.55.refs_0_), channel_id=1, source_target_pairs={{0,16},{16,0},{1,17},{17,1},{2,18},{18,2},{3,19},{19,3},{4,20},{20... | collective-permute-start | bytes 1966088 | tf_op jit(solution)/shard_map/ppermute | solution.py:348
  11.6 9.9 %all-to-all-start = ((s32[8,1,128]{2,1,0:T(1,128)}), s32[8,1,128]{2,1,0:T(1,128)S(1)}, u32[]{:S(2)}, u32[]{:S(2)}) async-start(s32[8,1,128]{2,1,0:T(1,128)} %broadcast_in_dim.2), calls=%async_computation | async-start | bytes 8192 | tf_op jit(solution)/shard_map/all_to_all | solution.py:351
  15.2 15.5 %collective-permute-start.2 = (bf16[2,128,640]{2,1,0:T(8,128)(2,1)S(1)}, bf16[2,128,640]{2,1,0:T(8,128)(2,1)}, u32[]{:S(2)}, u32[]{:S(2)}) collective-permute-start(bf16[2,128,640]{2,1,0:T(8,128)(2,1)S(1)} %get-tuple-element.57), channel_id=1, source_target_pairs={{0,1},{1,0},{2,3},{3,2},{4,5},{5,4},{6,7},{7,6},{8,9},{9,8},{10,11... | collective-permute-start | bytes 983048 | tf_op jit(solution)/shard_map/ppermute | solution.py:342
  21.5 3.3 %copy-start.10 = (s32[8,1,128]{2,1,0:T(1,128)}, s32[8,1,128]{2,1,0:T(1,128)S(1)}, u32[]{:S(2)}) copy-start(s32[8,1,128]{2,1,0:T(1,128)S(1)} %all-to-all-done.asked) | copy-start | bytes 12292
  21.6 9.1 %collective-permute-start.3 = (bf16[2,128,640]{2,1,0:T(8,128)(2,1)S(1)}, bf16[2,128,640]{2,1,0:T(8,128)(2,1)S(1)}, u32[]{:S(2)}, u32[]{:S(2)}) collective-permute-start(bf16[2,128,640]{2,1,0:T(8,128)(2,1)S(1)} %get-tuple-element.62), channel_id=1, source_target_pairs={{0,1},{1,0},{2,3},{3,2},{4,5},{5,4},{6,7},{7,6},{8,9},{9,8},{10,11... | collective-permute-start | bytes 983048 | tf_op jit(solution)/shard_map/ppermute | solution.py:342
  22.2 8.5 %collective-permute-start.5 = (bf16[640,256]{1,0:T(8,128)(2,1)}, bf16[640,256]{1,0:T(8,128)(2,1)}, u32[]{:S(2)}, u32[]{:S(2)}) collective-permute-start(bf16[640,256]{1,0:T(8,128)(2,1)} %collective-permute-done.refs_7_), channel_id=1, source_target_pairs={{2,4},{3,5},{4,2},{5,3},{10,12},{11,13},{12,10},{13,11},{18,20},{1... | collective-permute-start | bytes 983048 | tf_op jit(solution)/shard_map/ppermute | solution.py:381
  23.6 9.7 %collective-permute-start.6 = (bf16[640,256]{1,0:T(8,128)(2,1)S(1)}, bf16[640,256]{1,0:T(8,128)(2,1)S(1)}, u32[]{:S(2)}, u32[]{:S(2)}) collective-permute-start(bf16[640,256]{1,0:T(8,128)(2,1)S(1)} %collective-permute-done.1), channel_id=1, source_target_pairs={{2,0},{3,1},{4,6},{5,7},{10,8},{11,9},{12,14},{13,15},{18,16},{19,... | collective-permute-start | bytes 983048 | tf_op jit(solution)/shard_map/ppermute | solution.py:382
  24.9 30.5 %copy-start.3 = (bf16[8,256,320]{2,1,0:T(8,128)(2,1)S(1)}, bf16[8,256,320]{2,1,0:T(8,128)(2,1)}, u32[]{:S(2)}) copy-start(bf16[8,256,320]{2,1,0:T(8,128)(2,1)} %pair_columns.1.xs_ref) | copy-start | bytes 3932164
  30.7 2.6 %copy-start.11 = (bf16[2,128,640]{2,1,0:T(8,128)(2,1)}, bf16[2,128,640]{2,1,0:T(8,128)(2,1)S(1)}, u32[]{:S(2)}) copy-start(bf16[2,128,640]{2,1,0:T(8,128)(2,1)S(1)} %collective-permute-done.3.refs_3_) | copy-start | bytes 983044
  33.3 22.0 %all-to-all-start.1 = ((bf16[8,384,128]{2,1,0:T(8,128)(2,1)}), bf16[8,384,128]{2,1,0:T(8,128)(2,1)S(1)}, u32[]{:S(2)}, u32[]{:S(2)}) async-start(bf16[8,384,128]{2,1,0:T(8,128)(2,1)} %get-tuple-element.68), calls=%async_computation.1 | async-start | bytes 1572864 | tf_op jit(solution)/shard_map/all_to_all | solution.py:407
  37.9 12.8 %collective-permute-start.10 = (bf16[2,128,640]{2,1,0:T(8,128)(2,1)}, bf16[2,128,640]{2,1,0:T(8,128)(2,1)S(1)}, u32[]{:S(2)}, u32[]{:S(2)}) collective-permute-start(bf16[2,128,640]{2,1,0:T(8,128)(2,1)} %collective-permute-done.2.refs_2_), channel_id=1, source_target_pairs={{0,16},{16,0},{1,17},{17,1},{2,18},{18,2},{3,19},{19,3},{4,20},{20... | collective-permute-start | bytes 983048 | tf_op jit(solution)/shard_map/ppermute | solution.py:348
  38.5 13.6 %collective-permute-start.11 = (bf16[2,128,640]{2,1,0:T(8,128)(2,1)}, bf16[2,128,640]{2,1,0:T(8,128)(2,1)S(1)}, u32[]{:S(2)}, u32[]{:S(2)}) collective-permute-start(bf16[2,128,640]{2,1,0:T(8,128)(2,1)} %copy-done.11), channel_id=1, source_target_pairs={{0,16},{16,0},{1,17},{17,1},{2,18},{18,2},{3,19},{19,3},{4,20},{20... | collective-permute-start | bytes 983048 | tf_op jit(solution)/shard_map/ppermute | solution.py:348
  40.0 0.6 copy-start.4
  50.1 3.0 %copy-start.8 = (bf16[640,256]{1,0:T(8,128)(2,1)}, bf16[640,256]{1,0:T(8,128)(2,1)S(1)}, u32[]{:S(2)}) copy-start(bf16[640,256]{1,0:T(8,128)(2,1)S(1)} %broadcast_select_fusion.refs_8_) | copy-start | bytes 983044
  50.1 2.0 %collective-permute-start.9 = (bf16[640,256]{1,0:T(8,128)(2,1)S(1)}, bf16[640,256]{1,0:T(8,128)(2,1)S(1)}, u32[]{:S(2)}, u32[]{:S(2)}) collective-permute-start(bf16[640,256]{1,0:T(8,128)(2,1)S(1)} %broadcast_select_fusion.refs_8_), channel_id=1, source_target_pairs={{0,8},{8,0},{1,9},{9,1},{2,10},{10,2},{3,11},{11,3},{4,12},{12,4},... | collective-permute-start | bytes 983048 | tf_op jit(solution)/shard_map/ppermute | solution.py:345
  50.2 2.3 %collective-permute-start.7 = (bf16[640,256]{1,0:T(8,128)(2,1)}, bf16[640,256]{1,0:T(8,128)(2,1)S(1)}, u32[]{:S(2)}, u32[]{:S(2)}) collective-permute-start(bf16[640,256]{1,0:T(8,128)(2,1)} %copy-done.9), channel_id=1, source_target_pairs={{0,8},{8,0},{1,9},{9,1},{2,10},{10,2},{3,11},{11,3},{4,12},{12,4},... | collective-permute-start | bytes 983048 | tf_op jit(solution)/shard_map/ppermute | solution.py:345
  50.7 2.4 %collective-permute-start.8 = (bf16[640,256]{1,0:T(8,128)(2,1)}, bf16[640,256]{1,0:T(8,128)(2,1)}, u32[]{:S(2)}, u32[]{:S(2)}) collective-permute-start(bf16[640,256]{1,0:T(8,128)(2,1)} %collective-permute-done.refs_7_), channel_id=1, source_target_pairs={{0,8},{8,0},{1,9},{9,1},{2,10},{10,2},{3,11},{11,3},{4,12},{12,4},... | collective-permute-start | bytes 983048 | tf_op jit(solution)/shard_map/ppermute | solution.py:345
  50.7 1.7 %copy-start.12 = (bf16[2,128,640]{2,1,0:T(8,128)(2,1)}, bf16[2,128,640]{2,1,0:T(8,128)(2,1)S(1)}, u32[]{:S(2)}) copy-start(bf16[2,128,640]{2,1,0:T(8,128)(2,1)S(1)} %collective-permute-done.10.refs_4_) | copy-start | bytes 983044
  50.7 12.3 %collective-permute-start.12 = (bf16[640,256]{1,0:T(8,128)(2,1)}, bf16[640,256]{1,0:T(8,128)(2,1)}, u32[]{:S(2)}, u32[]{:S(2)}) collective-permute-start(bf16[640,256]{1,0:T(8,128)(2,1)} %collective-permute-done.5.refs_9_), channel_id=1, source_target_pairs={{2,0},{3,1},{4,6},{5,7},{10,8},{11,9},{12,14},{13,15},{18,16},{19,... | collective-permute-start | bytes 983048 | tf_op jit(solution)/shard_map/ppermute | solution.py:410
  52.0 0.7 copy-start.13
  52.1 1.0 %copy-start.14 = (bf16[640,256]{1,0:T(8,128)(2,1)}, bf16[640,256]{1,0:T(8,128)(2,1)S(1)}, u32[]{:S(2)}) copy-start(bf16[640,256]{1,0:T(8,128)(2,1)S(1)} %collective-permute-done.9.refs_13_) | copy-start | bytes 983044
  52.8 0.7 copy-start.15
  55.4 1.0 %copy-start.7 = (bf16[128,1024]{1,0:T(8,128)(2,1)S(1)}, bf16[128,1024]{1,0:T(8,128)(2,1)}, u32[]{:S(2)}) copy-start(bf16[128,1024]{1,0:T(8,128)(2,1)} %g_ref.1) | copy-start | bytes 786436
  63.0 26.1 %all-to-all-start.2 = ((bf16[8,384,128]{2,1,0:T(8,128)(2,1)}), bf16[8,384,128]{2,1,0:T(8,128)(2,1)S(1)}, u32[]{:S(2)}, u32[]{:S(2)}) async-start(bf16[8,384,128]{2,1,0:T(8,128)(2,1)} %get-tuple-element.91.refs_16_), calls=%async_computation.2 | async-start | bytes 1572864 | tf_op jit(solution)/shard_map/all_to_all | solution.py:455
  69.0 20.1 %copy-start.5 = (s32[8]{0:T(128)S(1)}, s32[8]{0:T(128)}, u32[]{:S(2)}) copy-start(s32[8]{0:T(128)} %get-tuple-element.69.after_ref.rows_here) | copy-start | bytes 100
  69.0 1.9 %collective-permute-start.13 = (bf16[640,256]{1,0:T(8,128)(2,1)}, bf16[640,256]{1,0:T(8,128)(2,1)S(1)}, u32[]{:S(2)}, u32[]{:S(2)}) collective-permute-start(bf16[640,256]{1,0:T(8,128)(2,1)} %collective-permute-done.5.refs_9_), channel_id=1, source_target_pairs={{0,8},{8,0},{1,9},{9,1},{2,10},{10,2},{3,11},{11,3},{4,12},{12,4},... | collective-permute-start | bytes 983048 | tf_op jit(solution)/shard_map/ppermute | solution.py:345
  69.1 2.3 %collective-permute-start.14 = (bf16[640,256]{1,0:T(8,128)(2,1)}, bf16[640,256]{1,0:T(8,128)(2,1)S(1)}, u32[]{:S(2)}, u32[]{:S(2)}) collective-permute-start(bf16[640,256]{1,0:T(8,128)(2,1)} %collective-permute-done.12.refs_10_), channel_id=1, source_target_pairs={{0,8},{8,0},{1,9},{9,1},{2,10},{10,2},{3,11},{11,3},{4,12},{12,4},... | collective-permute-start | bytes 983048 | tf_op jit(solution)/shard_map/ppermute | solution.py:345
  70.9 0.7 copy-start.16
  71.6 0.7 copy-start.17
  77.4 8.5 %collective-permute-start.15 = (bf16[128,512]{1,0:T(8,128)(2,1)}, bf16[128,512]{1,0:T(8,128)(2,1)S(1)}, u32[]{:S(2)}, u32[]{:S(2)}) collective-permute-start(bf16[128,512]{1,0:T(8,128)(2,1)} %get-tuple-element.93), channel_id=1, source_target_pairs={{0,1},{1,0},{2,3},{3,2},{4,5},{5,4},{6,7},{7,6},{8,9},{9,8},{10,11... | collective-permute-start | bytes 393224 | tf_op jit(solution)/shard_map/ppermute | solution.py:342
  79.4 6.5 %collective-permute-start.16 = (bf16[128,512]{1,0:T(8,128)(2,1)}, bf16[128,512]{1,0:T(8,128)(2,1)S(1)}, u32[]{:S(2)}, u32[]{:S(2)}) collective-permute-start(bf16[128,512]{1,0:T(8,128)(2,1)} %get-tuple-element.94), channel_id=1, source_target_pairs={{0,16},{16,0},{1,17},{17,1},{2,18},{18,2},{3,19},{19,3},{4,20},{20... | collective-permute-start | bytes 393224 | tf_op jit(solution)/shard_map/ppermute | solution.py:348
  79.9 8.4 %collective-permute-start.17 = (bf16[128,512]{1,0:T(8,128)(2,1)}, bf16[128,512]{1,0:T(8,128)(2,1)S(1)}, u32[]{:S(2)}, u32[]{:S(2)}) collective-permute-start(bf16[128,512]{1,0:T(8,128)(2,1)} %get-tuple-element.95), channel_id=1, source_target_pairs={{0,17},{1,16},{2,19},{3,18},{4,21},{5,20},{6,23},{7,22},{16,1},{17... | collective-permute-start | bytes 393224 | tf_op jit(solution)/shard_map/ppermute | solution.py:456
  89.1 2.4 %collective-permute-start.19 = (bf16[8,384,128]{2,1,0:T(8,128)(2,1)S(1)}, bf16[8,384,128]{2,1,0:T(8,128)(2,1)S(1)}, u32[]{:S(2)}, u32[]{:S(2)}) collective-permute-start(bf16[8,384,128]{2,1,0:T(8,128)(2,1)S(1)} %all-to-all-done.2.rest_0_), channel_id=1, source_target_pairs={{0,8},{8,0},{1,9},{9,1},{2,10},{10,2},{3,11},{11,3},{4,12},{12,4},... | collective-permute-start | bytes 2359304 | tf_op jit(solution)/shard_map/ppermute | solution.py:345
  89.1 2.3 %collective-permute-start.18 = (s32[8]{0:T(128)S(1)}, s32[8]{0:T(128)S(1)}, u32[]{:S(2)}, u32[]{:S(2)}) collective-permute-start(s32[8]{0:T(128)S(1)} %copy-done.5), channel_id=1, source_target_pairs={{0,8},{8,0},{1,9},{9,1},{2,10},{10,2},{3,11},{11,3},{4,12},{12,4},... | collective-permute-start | bytes 104 | tf_op jit(solution)/shard_map/ppermute | solution.py:345
  91.4 3.4 %copy-start.1 = (bf16[640,512]{1,0:T(8,128)(2,1)S(1)}, bf16[640,512]{1,0:T(8,128)(2,1)}, u32[]{:S(2)}) copy-start(bf16[640,512]{1,0:T(8,128)(2,1)} %param.9) | copy-start | bytes 1966084

commit v20 on v19

--- a/solution.py
+++ b/solution.py
@@ -168,14 +168,15 @@
         copies(t)[2].wait()
 
 
-def zero_kernel(after_ref, down_ref, up_ref, done_ref, zeros, sems):
-    del after_ref
+def zero_kernel(half, *refs):
+    down_ref, up_ref, done_ref, zeros, sems = refs[-5:]
     done_ref[0] = 0
     zeros[...] = jnp.zeros_like(zeros)
     part = zeros.shape[0]
+    groups = down_ref.shape[0] // 2
     copies = []
     for ref, sem in ((down_ref, sems.at[0]), (up_ref, sems.at[1])):
-        for g in range(ref.shape[0]):
+        for g in range(half * groups, (half + 1) * groups):
             for c in range(ref.shape[1] // part):
                 copies.append(pltpu.make_async_copy(zeros, ref.at[g, pl.ds(c * part, part)], sem))
     for c in copies:
@@ -411,17 +412,19 @@
     owned_groups = ADAPTERS // lax.axis_size("dp") // 8
     down_shape = jax.ShapeDtypeStruct((owned_groups, down_chunks, 8, 1, LANES), jnp.float32)
     up_shape = jax.ShapeDtypeStruct((owned_groups, up_chunks, 8, 1, LANES), jnp.float32)
-    down_zero, up_zero, cleared = pl.pallas_call(
-        zero_kernel, out_shape=(down_shape, up_shape, token),
-        in_specs=[SMEM], out_specs=(ANY, ANY, SMEM),
-        scratch_shapes=[pltpu.VMEM((up_chunks, 8, 1, LANES), jnp.float32), pltpu.SemaphoreType.DMA((2,))],
-        compiler_params=LIMIT, cost_estimate=cost(read=28 << 20), name="clear_rows",
-    )(rows)
-    cleared, half, near, over, passed = lax.optimization_barrier((cleared, half, near, over, passed))
+    def clear(half, inputs, in_specs, aliases):
+        return pl.pallas_call(
+            functools.partial(zero_kernel, half), out_shape=(down_shape, up_shape, token),
+            in_specs=in_specs, out_specs=(ANY, ANY, SMEM), input_output_aliases=aliases,
+            scratch_shapes=[pltpu.VMEM((up_chunks, 8, 1, LANES), jnp.float32), pltpu.SemaphoreType.DMA((2,))],
+            compiler_params=LIMIT, cost_estimate=cost(read=14 << 20), name="clear_rows",
+        )(*inputs)
+
+    down_zero, up_zero, cleared = clear(0, (rows,), [SMEM], {})
     inside = (z == 1) | (z == 2)
     quarter = [half, near, jnp.where(inside, over, passed)]
     quarter_core = [other_core(w) for w in quarter]
-    panels, quarter_core, y_far = lax.optimization_barrier((panels, quarter_core, y_far))
+    panels, quarter_core = lax.optimization_barrier((panels, quarter_core))
 
     terms, lifted = pl.pallas_call(
         functools.partial(adapter_kernel, group, down_chunks),
@@ -433,7 +436,7 @@
         cost_estimate=cost(flops=3 << 30, read=8 << 20),
         name="adapter",
     )(xs, cotangent, panels, cleared)
-    terms, over_near, passed_near = lax.optimization_barrier((terms, over_near, passed_near))
+    terms, over_near, passed_near, y_far = lax.optimization_barrier((terms, over_near, passed_near, y_far))
     last = [over_near, passed_near]
     quarters = quarter + last + quarter_core + [other_core(w) for w in last]
     sums = [jax.ShapeDtypeStruct((token_rows, parts * width), kind) for kind in (jnp.float32,) + (jnp.bfloat16,) * 3]
@@ -454,7 +457,9 @@
     opposite = [(a * group + t, (parts - 1 - a) * group + (t ^ 1)) for a in range(parts) for t in range(group)]
     back = lax.all_to_all(terms, "tensor", 0, 0)
     arrived = (exchange(to_inner, 1), other_part(to_part), lax.ppermute(to_both, ("parts", "tensor"), opposite))
-    back, arrived = lax.optimization_barrier((back, arrived))
+    down_zero, up_zero, kept = lax.optimization_barrier((down_zero, up_zero, kept))
+    down_zero, up_zero, cleared = clear(1, (down_zero, up_zero), [ANY, ANY], {0: 0, 1: 1})
+    back, arrived, cleared = lax.optimization_barrier((back, arrived, cleared))
     back_core = other_core(back)
 
     grad_down, grad_up = pl.pallas_call(

time: 95.3 us -> 92.3 us (0.969)
  starting transfers between devices: 36.3 us -> 33.8 us
  Pallas kernels: 30.6 us -> 31.7 us
    all_to_all x1, waiting for transfers between devices: 1.86 us -> 7.15 us  [fast_body(): panels = lax.all_to_all(sent, 'tensor', 0, 0)]
    ppermute x1, waiting for transfers between devices: 3.71 us -> 0.01 us  [fast_body(): passed_near = lax.ppermute(over_near, 'tensor', ends)]
    ppermute x4, waiting for transfers between devices: 0.01 us -> 2.59 us  [other_part(): lax.ppermute(value, 'parts', [(a, parts - 1 - a) for a in range(parts)])]
    all_to_all x1, starting transfers between devices: 6 us -> 3.56 us  [fast_body(): back = lax.all_to_all(terms, 'tensor', 0, 0)]
    ppermute x1, waiting for transfers between devices: 2.35 us -> 0.01 us  [fast_body(): lax.ppermute(to_both, ('parts', 'tensor'), opposite)]
    pallas_call x1 -> x2, Pallas kernels: 9.48 us -> 10.9 us  [clear(): pl.pallas_call(functools.partial(zero_kernel, half), out_shape=(down_shap...]
    unnamed x36 -> x34, local copies, waits for them, and re-layouts: 4.6 us -> 3.87 us
  transfers between devices with their start and end apart: 23 -> 23, of which waited for: 11 -> 8; matrix products, arithmetic and copies ran while one was open for 2% -> 1% of each run, Pallas kernels for 29% -> 31%
where the time goes in v20:
time: 92.3 us; the launch traced here: 91.7 us
  starting transfers between devices  33.8 us (37%)
  Pallas kernels  31.7 us (34%)
  waiting for transfers between devices  19.2 us (21%)
  local copies, waits for them, and re-layouts  4.49 us (5%)
  between operations  1.66 us (2%)
    pallas_call x2, Pallas kernels, clear(): pl.pallas_call(functools.partial(zero_kernel, half), out_shape=(down_shap...  10.9 us
    ppermute x4, starting transfers between devices, exchange(): return lax.ppermute(value, 'tensor', [(t, t ^ s) for t in range(group)])  10.5 us
    all_to_all x1, waiting for transfers between devices, fast_body(): panels = lax.all_to_all(sent, 'tensor', 0, 0)  7.15 us
    pallas_call x1, Pallas kernels, fast_body(): pl.pallas_call(gather_kernel, out_shape=(pieces, jax.ShapeDtypeStruct((gr...  5.87 us
    pallas_call x1, Pallas kernels, fast_body(): pl.pallas_call(base_kernel, out_shape=sums, in_specs=[ANY] * (7 + len(qua...  5.01 us
    all_to_all x1, starting transfers between devices, fast_body(): panels = lax.all_to_all(sent, 'tensor', 0, 0)  4.64 us
    ppermute x4, starting transfers between devices, other_part(): lax.ppermute(value, 'parts', [(a, parts - 1 - a) for a in range(parts)])  4.12 us
    ppermute x4, waiting for transfers between devices, exchange(): return lax.ppermute(value, 'tensor', [(t, t ^ s) for t in range(group)])  4.11 us
  transfers between devices with their start and end apart: 23, of which 8 were waited for; matrix products, arithmetic and copies ran while one was open for 1% of the time, Pallas kernels for 31%

profile of v20, /device:TPU:0, one launch (start us, length us, event | category | flops | bytes accessed | tf_op | source)
XLA Modules:
  0.0 91.7 jit_solution(12073408594873245669)
XLA Ops:
  0.6 0.0 copy-start
  1.4 0.6 broadcast_in_dim.2
  2.0 0.7 collective-permute-start.1
  2.7 5.9 %collective-permute-start = (bf16[640,256]{1,0:T(8,128)(2,1)S(1)}, bf16[640,256]{1,0:T(8,128)(2,1)}, u32[]{:S(2)}, u32[]{:S(2)}) collective-permute-start(bf16[640,256]{1,0:T(8,128)(2,1)S(1)} %constant_dynamic-slice_fusion.refs_6_), channel_id=1, source_target_pairs={{0,2},{1,3},{2,0},{3,1},{4,6},{5,7},{6,4},{7,5},{8,10},{9,11},{10,... | collective-permute-start | bytes 983048 | tf_op jit(solution)/shard_map/ppermute | solution.py:343
  8.6 1.3 %copy-done.2 = bf16[128,5120]{1,0:T(8,128)(2,1)S(1)} copy-done((bf16[128,5120]{1,0:T(8,128)(2,1)S(1)}, bf16[128,5120]{1,0:T(8,128)(2,1)}, u32[]{:S(2)}) %copy-start.2) | copy-done | bytes 1310744
  9.9 0.1 split_tokens.1
  10.0 1.6 %collective-permute-start.4 = (bf16[4,128,640]{2,1,0:T(8,128)(2,1)S(1)}, bf16[4,128,640]{2,1,0:T(8,128)(2,1)}, u32[]{:S(2)}, u32[]{:S(2)}) collective-permute-start(bf16[4,128,640]{2,1,0:T(8,128)(2,1)S(1)} %get-tuple-element.62.refs_0_), channel_id=1, source_target_pairs={{0,16},{16,0},{1,17},{17,1},{2,18},{18,2},{3,19},{19,3},{4,20},{20... | collective-permute-start | bytes 1966088 | tf_op jit(solution)/shard_map/ppermute | solution.py:349
  11.6 3.6 %all-to-all-start = ((s32[8,1,128]{2,1,0:T(1,128)}), s32[8,1,128]{2,1,0:T(1,128)S(1)}, u32[]{:S(2)}, u32[]{:S(2)}) async-start(s32[8,1,128]{2,1,0:T(1,128)} %broadcast_in_dim.2), calls=%async_computation | async-start | bytes 8192 | tf_op jit(solution)/shard_map/all_to_all | solution.py:352
  15.2 2.0 %collective-permute-start.2 = (bf16[2,128,640]{2,1,0:T(8,128)(2,1)S(1)}, bf16[2,128,640]{2,1,0:T(8,128)(2,1)}, u32[]{:S(2)}, u32[]{:S(2)}) collective-permute-start(bf16[2,128,640]{2,1,0:T(8,128)(2,1)S(1)} %get-tuple-element.56), channel_id=1, source_target_pairs={{0,1},{1,0},{2,3},{3,2},{4,5},{5,4},{6,7},{7,6},{8,9},{9,8},{10,11... | collective-permute-start | bytes 983048 | tf_op jit(solution)/shard_map/ppermute | solution.py:343
  17.2 3.9 %pair_columns.1.xs_ref = bf16[8,256,320]{2,1,0:T(8,128)(2,1)} custom-call(bf16[128,5120]{1,0:T(8,128)(2,1)} %x_ref.1), custom_call_target="tpu_custom_call" | custom-call | bytes 134217728 | tf_op jit(solution)/shard_map/pair_columns/pallas_call | solution.py:366
  21.1 0.5 all-to-all-done.asked
  21.5 0.0 collective-permute-done.1
  21.5 0.0 collective-permute-done.refs_7_
  21.6 0.6 collective-permute-start.3
  22.2 1.4 %collective-permute-start.5 = (bf16[640,256]{1,0:T(8,128)(2,1)}, bf16[640,256]{1,0:T(8,128)(2,1)}, u32[]{:S(2)}, u32[]{:S(2)}) collective-permute-start(bf16[640,256]{1,0:T(8,128)(2,1)} %collective-permute-done.refs_7_), channel_id=1, source_target_pairs={{2,4},{3,5},{4,2},{5,3},{10,12},{11,13},{12,10},{13,11},{18,20},{1... | collective-permute-start | bytes 983048 | tf_op jit(solution)/shard_map/ppermute | solution.py:382
  23.6 1.3 %collective-permute-start.6 = (bf16[640,256]{1,0:T(8,128)(2,1)S(1)}, bf16[640,256]{1,0:T(8,128)(2,1)S(1)}, u32[]{:S(2)}, u32[]{:S(2)}) collective-permute-start(bf16[640,256]{1,0:T(8,128)(2,1)S(1)} %collective-permute-done.1), channel_id=1, source_target_pairs={{2,0},{3,1},{4,6},{5,7},{10,8},{11,9},{12,14},{13,15},{18,16},{19,... | collective-permute-start | bytes 983048 | tf_op jit(solution)/shard_map/ppermute | solution.py:383
  24.9 5.9 %pick_panels.1 = (bf16[8,384,128]{2,1,0:T(8,128)(2,1)}, s32[8]{0:T(128)}) custom-call(s32[8,1,128]{2,1,0:T(1,128)} %copy-done.11, s32[256]{0:T(256)} %slot_of.1, bf16[32,320,8,128]{3,2,1,0:T(8,128)(2,1)} %bitcast.19, bf16[32,64,8,128]{3,2,1,0:T(8,128)(2,1)} %bitcast.21), custom_call_target="tpu_custom_call" | custom-call | bytes 41943040 | tf_op jit(solution)/shard_map/pick_panels/pallas_call | solution.py:389
  30.8 0.0 collective-permute-done.2.refs_2_
  30.8 0.0 collective-permute-done.4.refs_1_
  30.8 0.0 collective-permute-done.3.refs_3_
  30.8 0.0 collective-permute-done.5.refs_9_
  30.8 2.5 %collective-permute-done.6 = bf16[640,256]{1,0:T(8,128)(2,1)S(1)} collective-permute-done((bf16[640,256]{1,0:T(8,128)(2,1)S(1)}, bf16[640,256]{1,0:T(8,128)(2,1)S(1)}, u32[]{:S(2)}, u32[]{:S(2)}) %collective-permute-start.6) | collective-permute-done | bytes 327712 | tf_op jit(solution)/shard_map/ppermute | solution.py:383
  33.3 4.6 %all-to-all-start.1 = ((bf16[8,384,128]{2,1,0:T(8,128)(2,1)}), bf16[8,384,128]{2,1,0:T(8,128)(2,1)S(1)}, u32[]{:S(2)}, u32[]{:S(2)}) async-start(bf16[8,384,128]{2,1,0:T(8,128)(2,1)} %get-tuple-element.72), calls=%async_computation.1 | async-start | bytes 1572864 | tf_op jit(solution)/shard_map/all_to_all | solution.py:408
  38.0 0.1 collective-permute-start.9
  38.1 0.5 collective-permute-start.7
  38.6 0.1 collective-permute-start.8
  38.7 0.5 collective-permute-start.11
  39.2 1.5 %collective-permute-start.12 = (bf16[2,128,640]{2,1,0:T(8,128)(2,1)}, bf16[2,128,640]{2,1,0:T(8,128)(2,1)}, u32[]{:S(2)}, u32[]{:S(2)}) collective-permute-start(bf16[2,128,640]{2,1,0:T(8,128)(2,1)} %copy-done.12), channel_id=1, source_target_pairs={{0,16},{16,0},{1,17},{17,1},{2,18},{18,2},{3,19},{19,3},{4,20},{20... | collective-permute-start | bytes 983048 | tf_op jit(solution)/shard_map/ppermute | solution.py:349
  40.7 0.0 collective-permute-done.9.refs_13_
  40.7 1.3 %collective-permute-start.10 = (bf16[640,256]{1,0:T(8,128)(2,1)}, bf16[640,256]{1,0:T(8,128)(2,1)}, u32[]{:S(2)}, u32[]{:S(2)}) collective-permute-start(bf16[640,256]{1,0:T(8,128)(2,1)} %collective-permute-done.5.refs_9_), channel_id=1, source_target_pairs={{2,0},{3,1},{4,6},{5,7},{10,8},{11,9},{12,14},{13,15},{18,16},{19,... | collective-permute-start | bytes 983048 | tf_op jit(solution)/shard_map/ppermute | solution.py:411
  42.0 0.6 copy-done.4
  42.6 5.7 %clear_rows.2 = (f32[16,320,8,1,128]{4,3,2,1,0:T(1,128)}, f32[16,64,8,1,128]{4,3,2,1,0:T(1,128)}, s32[1]{0:T(128)}) custom-call(s32[8]{0:T(128)S(1)} %copy-done.4), custom_call_target="tpu_custom_call" | custom-call | bytes 14680064 | tf_op jit(solution)/shard_map/clear_rows/pallas_call | solution.py:416
  48.3 0.0 collective-permute-done.7.refs_11_
  48.3 0.0 collective-permute-done.8.refs_12_
  48.3 7.1 %all-to-all-done.1.pieces = bf16[8,384,128]{2,1,0:T(8,128)(2,1)S(1)} async-done(((bf16[8,384,128]{2,1,0:T(8,128)(2,1)}), bf16[8,384,128]{2,1,0:T(8,128)(2,1)S(1)}, u32[]{:S(2)}, u32[]{:S(2)}) %all-to-all-start.1) | async-done | bytes 786464 | tf_op jit(solution)/shard_map/all_to_all | solution.py:408
  55.5 0.9 %copy-done.7 = bf16[128,1024]{1,0:T(8,128)(2,1)S(1)} copy-done((bf16[128,1024]{1,0:T(8,128)(2,1)S(1)}, bf16[128,1024]{1,0:T(8,128)(2,1)}, u32[]{:S(2)}) %copy-start.7) | copy-done | bytes 262168
  56.4 3.0 %adapter.1 = (bf16[8,384,128]{2,1,0:T(8,128)(2,1)}, f32[128,1024]{1,0:T(8,128)S(1)}) custom-call(bf16[8,256,320]{2,1,0:T(8,128)(2,1)S(1)} %copy-done.3, bf16[128,1024]{1,0:T(8,128)(2,1)S(1)} %copy-done.7, bf16[8,384,128]{2,1,0:T(8,128)(2,1)S(1)} %all-to-all-done.1.pieces, s32[1]{0:T(128)} %get-tuple-element.78._), custom_call_target="tpu_custom_call" | custom-call | flops 3221225472 | bytes 8388608 | tf_op jit(solution)/shard_map/adapter/pallas_call | solution.py:429
  59.4 0.0 collective-permute-done.11.refs_4_
  59.4 0.0 collective-permute-done.12.refs_5_
  59.4 0.0 collective-permute-done.10.refs_10_
  59.4 3.6 %all-to-all-start.2 = ((bf16[8,384,128]{2,1,0:T(8,128)(2,1)}), bf16[8,384,128]{2,1,0:T(8,128)(2,1)S(1)}, u32[]{:S(2)}, u32[]{:S(2)}) async-start(bf16[8,384,128]{2,1,0:T(8,128)(2,1)} %get-tuple-element.88.refs_16_), calls=%async_computation.2 | async-start | bytes 1572864 | tf_op jit(solution)/shard_map/all_to_all | solution.py:458
  63.0 0.1 collective-permute-start.13
  63.1 0.5 collective-permute-start.14
  63.6 1.3 %collective-permute-done.13.refs_14_ = bf16[640,256]{1,0:T(8,128)(2,1)S(1)} collective-permute-done((bf16[640,256]{1,0:T(8,128)(2,1)}, bf16[640,256]{1,0:T(8,128)(2,1)S(1)}, u32[]{:S(2)}, u32[]{:S(2)}) %collective-permute-start.13) | collective-permute-done | bytes 327712 | tf_op jit(solution)/shard_map/ppermute | solution.py:346
  64.9 0.5 collective-permute-done.14.refs_15_
  65.4 0.2 copy-done.15
  65.6 0.7 copy-done.16
  66.4 5.0 %frozen_part.1 = (f32[128,512]{1,0:T(8,128)}, bf16[128,512]{1,0:T(8,128)(2,1)}, bf16[128,512]{1,0:T(8,128)(2,1)}, bf16[128,512]{1,0:T(8,128)(2,1)}) custom-call(bf16[4,128,640]{2,1,0:T(8,128)(2,1)} %copy-done.6, bf16[4,128,640]{2,1,0:T(8,128)(2,1)} %collective-permute-done.4.refs_1_, bf16[2,128,640]{2,1,0:T(8,128)(2,1)} %collective-permute-done.2.refs_2_, ...), custom_call_target="tpu_custom_call" | custom-call | flops 4294967296 | bytes 8388608 | tf_op jit(solution)/shard_map/frozen_part/pallas_call | solution.py:443
  71.4 2.0 %collective-permute-start.15 = (bf16[128,512]{1,0:T(8,128)(2,1)}, bf16[128,512]{1,0:T(8,128)(2,1)S(1)}, u32[]{:S(2)}, u32[]{:S(2)}) collective-permute-start(bf16[128,512]{1,0:T(8,128)(2,1)} %get-tuple-element.91), channel_id=1, source_target_pairs={{0,1},{1,0},{2,3},{3,2},{4,5},{5,4},{6,7},{7,6},{8,9},{9,8},{10,11... | collective-permute-start | bytes 393224 | tf_op jit(solution)/shard_map/ppermute | solution.py:343
  73.3 0.5 collective-permute-start.16
  73.8 1.1 %collective-permute-start.17 = (bf16[128,512]{1,0:T(8,128)(2,1)}, bf16[128,512]{1,0:T(8,128)(2,1)S(1)}, u32[]{:S(2)}, u32[]{:S(2)}) collective-permute-start(bf16[128,512]{1,0:T(8,128)(2,1)} %get-tuple-element.93), channel_id=1, source_target_pairs={{0,17},{1,16},{2,19},{3,18},{4,21},{5,20},{6,23},{7,22},{16,1},{17... | collective-permute-start | bytes 393224 | tf_op jit(solution)/shard_map/ppermute | solution.py:459
  74.9 4.1 %collective-permute-done.15 = bf16[128,512]{1,0:T(8,128)(2,1)S(1)} collective-permute-done((bf16[128,512]{1,0:T(8,128)(2,1)}, bf16[128,512]{1,0:T(8,128)(2,1)S(1)}, u32[]{:S(2)}, u32[]{:S(2)}) %collective-permute-start.15) | collective-permute-done | bytes 131104 | tf_op jit(solution)/shard_map/ppermute | solution.py:343
  79.0 2.6 %collective-permute-done.16 = bf16[128,512]{1,0:T(8,128)(2,1)S(1)} collective-permute-done((bf16[128,512]{1,0:T(8,128)(2,1)}, bf16[128,512]{1,0:T(8,128)(2,1)S(1)}, u32[]{:S(2)}, u32[]{:S(2)}) %collective-permute-start.16) | collective-permute-done | bytes 131104 | tf_op jit(solution)/shard_map/ppermute | solution.py:349
  81.6 0.0 collective-permute-done.17
  81.6 0.6 all-to-all-done.2.rest_0_
  82.2 0.0 collective-permute-start.19
  82.2 0.0 copy-done.5
  82.2 0.5 collective-permute-start.18
  82.7 5.2 %clear_rows.3 = (f32[16,320,8,1,128]{4,3,2,1,0:T(1,128)}, f32[16,64,8,1,128]{4,3,2,1,0:T(1,128)}, s32[1]{0:T(128)}) custom-call(f32[16,320,8,1,128]{4,3,2,1,0:T(1,128)} %get-tuple-element.99.refs_0_, f32[16,64,8,1,128]{4,3,2,1,0:T(1,128)} %get-tuple-element.100.refs_1_), custom_call_target="tpu_custom_call", output_to_operand_aliasing={{0}: (0, {}), {1}: (1, {})} | custom-call | bytes 14680064 | tf_op jit(solution)/shard_map/clear_rows/pallas_call | solution.py:416
  87.9 0.1 convert_add_fusion
  88.0 0.8 fusion
  88.8 0.0 collective-permute-done.18.rows_core
  88.8 0.0 collective-permute-done.19.rest_1_
  88.8 3.0 %place_rows.1 = (f32[16,320,8,1,128]{4,3,2,1,0:T(1,128)}, f32[16,64,8,1,128]{4,3,2,1,0:T(1,128)}) custom-call(s32[8]{0:T(128)S(1)} %copy-done.5, s32[8]{0:T(128)S(1)} %collective-permute-done.18.rows_core, bf16[8,384,128]{2,1,0:T(8,128)(2,1)S(1)} %all-to-all-done.2.rest_0_, ...), custom_call_target="tpu_custom_call", output_to_operand_aliasing={{0}: (4, {}), {1}: (5, {})} | custom-call | bytes 16777216 | tf_op jit(solution)/shard_map/place_rows/pallas_call | solution.py:465
  (30 shorter events, 0.2 us)
Async XLA Ops:
  0.6 1.3 %copy-start = (bf16[640,512]{1,0:T(8,128)(2,1)S(1)}, bf16[640,512]{1,0:T(8,128)(2,1)}, u32[]{:S(2)}) copy-start(bf16[640,512]{1,0:T(8,128)(2,1)} %param.9) | copy-start | bytes 1966084
  2.0 22.9 %copy-start.9 = (bf16[640,256]{1,0:T(8,128)(2,1)}, bf16[640,256]{1,0:T(8,128)(2,1)S(1)}, u32[]{:S(2)}) copy-start(bf16[640,256]{1,0:T(8,128)(2,1)S(1)} %constant_dynamic-slice_fusion.refs_6_) | copy-start | bytes 983044
  2.0 19.6 %collective-permute-start.1 = (bf16[640,256]{1,0:T(8,128)(2,1)S(1)}, bf16[640,256]{1,0:T(8,128)(2,1)S(1)}, u32[]{:S(2)}, u32[]{:S(2)}) collective-permute-start(bf16[640,256]{1,0:T(8,128)(2,1)S(1)} %constant_dynamic-slice_fusion.refs_6_), channel_id=1, source_target_pairs={{2,4},{3,5},{4,2},{5,3},{10,12},{11,13},{12,10},{13,11},{18,20},{1... | collective-permute-start | bytes 983048 | tf_op jit(solution)/shard_map/ppermute | solution.py:379
  2.7 18.9 %collective-permute-start = (bf16[640,256]{1,0:T(8,128)(2,1)S(1)}, bf16[640,256]{1,0:T(8,128)(2,1)}, u32[]{:S(2)}, u32[]{:S(2)}) collective-permute-start(bf16[640,256]{1,0:T(8,128)(2,1)S(1)} %constant_dynamic-slice_fusion.refs_6_), channel_id=1, source_target_pairs={{0,2},{1,3},{2,0},{3,1},{4,6},{5,7},{6,4},{7,5},{8,10},{9,11},{10,... | collective-permute-start | bytes 983048 | tf_op jit(solution)/shard_map/ppermute | solution.py:343
  8.6 1.3 %copy-start.2 = (bf16[128,5120]{1,0:T(8,128)(2,1)S(1)}, bf16[128,5120]{1,0:T(8,128)(2,1)}, u32[]{:S(2)}) copy-start(bf16[128,5120]{1,0:T(8,128)(2,1)} %x_ref.1) | copy-start | bytes 3932164
  10.0 20.8 %copy-start.6 = (bf16[4,128,640]{2,1,0:T(8,128)(2,1)}, bf16[4,128,640]{2,1,0:T(8,128)(2,1)S(1)}, u32[]{:S(2)}) copy-start(bf16[4,128,640]{2,1,0:T(8,128)(2,1)S(1)} %get-tuple-element.62.refs_0_) | copy-start | bytes 1966084
  10.0 20.8 %collective-permute-start.4 = (bf16[4,128,640]{2,1,0:T(8,128)(2,1)S(1)}, bf16[4,128,640]{2,1,0:T(8,128)(2,1)}, u32[]{:S(2)}, u32[]{:S(2)}) collective-permute-start(bf16[4,128,640]{2,1,0:T(8,128)(2,1)S(1)} %get-tuple-element.62.refs_0_), channel_id=1, source_target_pairs={{0,16},{16,0},{1,17},{17,1},{2,18},{18,2},{3,19},{19,3},{4,20},{20... | collective-permute-start | bytes 1966088 | tf_op jit(solution)/shard_map/ppermute | solution.py:349
  11.6 9.9 %all-to-all-start = ((s32[8,1,128]{2,1,0:T(1,128)}), s32[8,1,128]{2,1,0:T(1,128)S(1)}, u32[]{:S(2)}, u32[]{:S(2)}) async-start(s32[8,1,128]{2,1,0:T(1,128)} %broadcast_in_dim.2), calls=%async_computation | async-start | bytes 8192 | tf_op jit(solution)/shard_map/all_to_all | solution.py:352
  15.2 15.6 %collective-permute-start.2 = (bf16[2,128,640]{2,1,0:T(8,128)(2,1)S(1)}, bf16[2,128,640]{2,1,0:T(8,128)(2,1)}, u32[]{:S(2)}, u32[]{:S(2)}) collective-permute-start(bf16[2,128,640]{2,1,0:T(8,128)(2,1)S(1)} %get-tuple-element.56), channel_id=1, source_target_pairs={{0,1},{1,0},{2,3},{3,2},{4,5},{5,4},{6,7},{7,6},{8,9},{9,8},{10,11... | collective-permute-start | bytes 983048 | tf_op jit(solution)/shard_map/ppermute | solution.py:343
  21.5 3.3 %copy-start.11 = (s32[8,1,128]{2,1,0:T(1,128)}, s32[8,1,128]{2,1,0:T(1,128)S(1)}, u32[]{:S(2)}) copy-start(s32[8,1,128]{2,1,0:T(1,128)S(1)} %all-to-all-done.asked) | copy-start | bytes 12292
  21.6 9.3 %collective-permute-start.3 = (bf16[2,128,640]{2,1,0:T(8,128)(2,1)S(1)}, bf16[2,128,640]{2,1,0:T(8,128)(2,1)S(1)}, u32[]{:S(2)}, u32[]{:S(2)}) collective-permute-start(bf16[2,128,640]{2,1,0:T(8,128)(2,1)S(1)} %get-tuple-element.61), channel_id=1, source_target_pairs={{0,1},{1,0},{2,3},{3,2},{4,5},{5,4},{6,7},{7,6},{8,9},{9,8},{10,11... | collective-permute-start | bytes 983048 | tf_op jit(solution)/shard_map/ppermute | solution.py:343
  22.2 8.7 %collective-permute-start.5 = (bf16[640,256]{1,0:T(8,128)(2,1)}, bf16[640,256]{1,0:T(8,128)(2,1)}, u32[]{:S(2)}, u32[]{:S(2)}) collective-permute-start(bf16[640,256]{1,0:T(8,128)(2,1)} %collective-permute-done.refs_7_), channel_id=1, source_target_pairs={{2,4},{3,5},{4,2},{5,3},{10,12},{11,13},{12,10},{13,11},{18,20},{1... | collective-permute-start | bytes 983048 | tf_op jit(solution)/shard_map/ppermute | solution.py:382
  23.6 9.7 %collective-permute-start.6 = (bf16[640,256]{1,0:T(8,128)(2,1)S(1)}, bf16[640,256]{1,0:T(8,128)(2,1)S(1)}, u32[]{:S(2)}, u32[]{:S(2)}) collective-permute-start(bf16[640,256]{1,0:T(8,128)(2,1)S(1)} %collective-permute-done.1), channel_id=1, source_target_pairs={{2,0},{3,1},{4,6},{5,7},{10,8},{11,9},{12,14},{13,15},{18,16},{19,... | collective-permute-start | bytes 983048 | tf_op jit(solution)/shard_map/ppermute | solution.py:383
  24.9 30.6 %copy-start.3 = (bf16[8,256,320]{2,1,0:T(8,128)(2,1)S(1)}, bf16[8,256,320]{2,1,0:T(8,128)(2,1)}, u32[]{:S(2)}) copy-start(bf16[8,256,320]{2,1,0:T(8,128)(2,1)} %pair_columns.1.xs_ref) | copy-start | bytes 3932164
  30.8 2.5 %copy-start.12 = (bf16[2,128,640]{2,1,0:T(8,128)(2,1)}, bf16[2,128,640]{2,1,0:T(8,128)(2,1)S(1)}, u32[]{:S(2)}) copy-start(bf16[2,128,640]{2,1,0:T(8,128)(2,1)S(1)} %collective-permute-done.3.refs_3_) | copy-start | bytes 983044
  33.3 22.1 %all-to-all-start.1 = ((bf16[8,384,128]{2,1,0:T(8,128)(2,1)}), bf16[8,384,128]{2,1,0:T(8,128)(2,1)S(1)}, u32[]{:S(2)}, u32[]{:S(2)}) async-start(bf16[8,384,128]{2,1,0:T(8,128)(2,1)} %get-tuple-element.72), calls=%async_computation.1 | async-start | bytes 1572864 | tf_op jit(solution)/shard_map/all_to_all | solution.py:408
  38.0 2.7 %copy-start.8 = (bf16[640,256]{1,0:T(8,128)(2,1)}, bf16[640,256]{1,0:T(8,128)(2,1)S(1)}, u32[]{:S(2)}) copy-start(bf16[640,256]{1,0:T(8,128)(2,1)S(1)} %broadcast_select_fusion.refs_8_) | copy-start | bytes 983044
  38.0 2.7 %collective-permute-start.9 = (bf16[640,256]{1,0:T(8,128)(2,1)S(1)}, bf16[640,256]{1,0:T(8,128)(2,1)S(1)}, u32[]{:S(2)}, u32[]{:S(2)}) collective-permute-start(bf16[640,256]{1,0:T(8,128)(2,1)S(1)} %broadcast_select_fusion.refs_8_), channel_id=1, source_target_pairs={{0,8},{8,0},{1,9},{9,1},{2,10},{10,2},{3,11},{11,3},{4,12},{12,4},... | collective-permute-start | bytes 983048 | tf_op jit(solution)/shard_map/ppermute | solution.py:346
  38.1 10.2 %collective-permute-start.7 = (bf16[640,256]{1,0:T(8,128)(2,1)}, bf16[640,256]{1,0:T(8,128)(2,1)S(1)}, u32[]{:S(2)}, u32[]{:S(2)}) collective-permute-start(bf16[640,256]{1,0:T(8,128)(2,1)} %copy-done.9), channel_id=1, source_target_pairs={{0,8},{8,0},{1,9},{9,1},{2,10},{10,2},{3,11},{11,3},{4,12},{12,4},... | collective-permute-start | bytes 983048 | tf_op jit(solution)/shard_map/ppermute | solution.py:346
  38.6 9.7 %collective-permute-start.8 = (bf16[640,256]{1,0:T(8,128)(2,1)}, bf16[640,256]{1,0:T(8,128)(2,1)}, u32[]{:S(2)}, u32[]{:S(2)}) collective-permute-start(bf16[640,256]{1,0:T(8,128)(2,1)} %collective-permute-done.refs_7_), channel_id=1, source_target_pairs={{0,8},{8,0},{1,9},{9,1},{2,10},{10,2},{3,11},{11,3},{4,12},{12,4},... | collective-permute-start | bytes 983048 | tf_op jit(solution)/shard_map/ppermute | solution.py:346
  38.7 20.8 %collective-permute-start.11 = (bf16[2,128,640]{2,1,0:T(8,128)(2,1)}, bf16[2,128,640]{2,1,0:T(8,128)(2,1)}, u32[]{:S(2)}, u32[]{:S(2)}) collective-permute-start(bf16[2,128,640]{2,1,0:T(8,128)(2,1)} %collective-permute-done.2.refs_2_), channel_id=1, source_target_pairs={{0,16},{16,0},{1,17},{17,1},{2,18},{18,2},{3,19},{19,3},{4,20},{20... | collective-permute-start | bytes 983048 | tf_op jit(solution)/shard_map/ppermute | solution.py:349
  39.2 20.2 %collective-permute-start.12 = (bf16[2,128,640]{2,1,0:T(8,128)(2,1)}, bf16[2,128,640]{2,1,0:T(8,128)(2,1)}, u32[]{:S(2)}, u32[]{:S(2)}) collective-permute-start(bf16[2,128,640]{2,1,0:T(8,128)(2,1)} %copy-done.12), channel_id=1, source_target_pairs={{0,16},{16,0},{1,17},{17,1},{2,18},{18,2},{3,19},{19,3},{4,20},{20... | collective-permute-start | bytes 983048 | tf_op jit(solution)/shard_map/ppermute | solution.py:349
  40.7 18.7 %copy-start.13 = (bf16[640,256]{1,0:T(8,128)(2,1)}, bf16[640,256]{1,0:T(8,128)(2,1)S(1)}, u32[]{:S(2)}) copy-start(bf16[640,256]{1,0:T(8,128)(2,1)S(1)} %collective-permute-done.9.refs_13_) | copy-start | bytes 983044
  40.7 18.7 %collective-permute-start.10 = (bf16[640,256]{1,0:T(8,128)(2,1)}, bf16[640,256]{1,0:T(8,128)(2,1)}, u32[]{:S(2)}, u32[]{:S(2)}) collective-permute-start(bf16[640,256]{1,0:T(8,128)(2,1)} %collective-permute-done.5.refs_9_), channel_id=1, source_target_pairs={{2,0},{3,1},{4,6},{5,7},{10,8},{11,9},{12,14},{13,15},{18,16},{19,... | collective-permute-start | bytes 983048 | tf_op jit(solution)/shard_map/ppermute | solution.py:411
  42.0 0.6 copy-start.4
  48.3 7.2 %copy-start.14 = (bf16[640,256]{1,0:T(8,128)(2,1)}, bf16[640,256]{1,0:T(8,128)(2,1)S(1)}, u32[]{:S(2)}) copy-start(bf16[640,256]{1,0:T(8,128)(2,1)S(1)} %collective-permute-done.7.refs_11_) | copy-start | bytes 983044
  55.5 1.0 %copy-start.7 = (bf16[128,1024]{1,0:T(8,128)(2,1)S(1)}, bf16[128,1024]{1,0:T(8,128)(2,1)}, u32[]{:S(2)}) copy-start(bf16[128,1024]{1,0:T(8,128)(2,1)} %g_ref.1) | copy-start | bytes 786436
  59.4 22.7 %all-to-all-start.2 = ((bf16[8,384,128]{2,1,0:T(8,128)(2,1)}), bf16[8,384,128]{2,1,0:T(8,128)(2,1)S(1)}, u32[]{:S(2)}, u32[]{:S(2)}) async-start(bf16[8,384,128]{2,1,0:T(8,128)(2,1)} %get-tuple-element.88.refs_16_), calls=%async_computation.2 | async-start | bytes 1572864 | tf_op jit(solution)/shard_map/all_to_all | solution.py:458
  63.0 19.2 %copy-start.5 = (s32[8]{0:T(128)S(1)}, s32[8]{0:T(128)}, u32[]{:S(2)}) copy-start(s32[8]{0:T(128)} %get-tuple-element.65.refs_0_.rows_here) | copy-start | bytes 100
  63.0 1.9 %collective-permute-start.13 = (bf16[640,256]{1,0:T(8,128)(2,1)}, bf16[640,256]{1,0:T(8,128)(2,1)S(1)}, u32[]{:S(2)}, u32[]{:S(2)}) collective-permute-start(bf16[640,256]{1,0:T(8,128)(2,1)} %collective-permute-done.5.refs_9_), channel_id=1, source_target_pairs={{0,8},{8,0},{1,9},{9,1},{2,10},{10,2},{3,11},{11,3},{4,12},{12,4},... | collective-permute-start | bytes 983048 | tf_op jit(solution)/shard_map/ppermute | solution.py:346
  63.1 2.3 %collective-permute-start.14 = (bf16[640,256]{1,0:T(8,128)(2,1)}, bf16[640,256]{1,0:T(8,128)(2,1)S(1)}, u32[]{:S(2)}, u32[]{:S(2)}) collective-permute-start(bf16[640,256]{1,0:T(8,128)(2,1)} %collective-permute-done.10.refs_10_), channel_id=1, source_target_pairs={{0,8},{8,0},{1,9},{9,1},{2,10},{10,2},{3,11},{11,3},{4,12},{12,4},... | collective-permute-start | bytes 983048 | tf_op jit(solution)/shard_map/ppermute | solution.py:346
  64.9 0.7 copy-start.15
  65.6 0.7 copy-start.16
  71.4 7.7 %collective-permute-start.15 = (bf16[128,512]{1,0:T(8,128)(2,1)}, bf16[128,512]{1,0:T(8,128)(2,1)S(1)}, u32[]{:S(2)}, u32[]{:S(2)}) collective-permute-start(bf16[128,512]{1,0:T(8,128)(2,1)} %get-tuple-element.91), channel_id=1, source_target_pairs={{0,1},{1,0},{2,3},{3,2},{4,5},{5,4},{6,7},{7,6},{8,9},{9,8},{10,11... | collective-permute-start | bytes 393224 | tf_op jit(solution)/shard_map/ppermute | solution.py:343
  73.3 8.3 %collective-permute-start.16 = (bf16[128,512]{1,0:T(8,128)(2,1)}, bf16[128,512]{1,0:T(8,128)(2,1)S(1)}, u32[]{:S(2)}, u32[]{:S(2)}) collective-permute-start(bf16[128,512]{1,0:T(8,128)(2,1)} %get-tuple-element.92), channel_id=1, source_target_pairs={{0,16},{16,0},{1,17},{17,1},{2,18},{18,2},{3,19},{19,3},{4,20},{20... | collective-permute-start | bytes 393224 | tf_op jit(solution)/shard_map/ppermute | solution.py:349
  73.8 7.8 %collective-permute-start.17 = (bf16[128,512]{1,0:T(8,128)(2,1)}, bf16[128,512]{1,0:T(8,128)(2,1)S(1)}, u32[]{:S(2)}, u32[]{:S(2)}) collective-permute-start(bf16[128,512]{1,0:T(8,128)(2,1)} %get-tuple-element.93), channel_id=1, source_target_pairs={{0,17},{1,16},{2,19},{3,18},{4,21},{5,20},{6,23},{7,22},{16,1},{17... | collective-permute-start | bytes 393224 | tf_op jit(solution)/shard_map/ppermute | solution.py:459
  82.2 6.6 %collective-permute-start.19 = (bf16[8,384,128]{2,1,0:T(8,128)(2,1)S(1)}, bf16[8,384,128]{2,1,0:T(8,128)(2,1)S(1)}, u32[]{:S(2)}, u32[]{:S(2)}) collective-permute-start(bf16[8,384,128]{2,1,0:T(8,128)(2,1)S(1)} %all-to-all-done.2.rest_0_), channel_id=1, source_target_pairs={{0,8},{8,0},{1,9},{9,1},{2,10},{10,2},{3,11},{11,3},{4,12},{12,4},... | collective-permute-start | bytes 2359304 | tf_op jit(solution)/shard_map/ppermute | solution.py:346
  82.2 6.6 %collective-permute-start.18 = (s32[8]{0:T(128)S(1)}, s32[8]{0:T(128)S(1)}, u32[]{:S(2)}, u32[]{:S(2)}) collective-permute-start(s32[8]{0:T(128)S(1)} %copy-done.5), channel_id=1, source_target_pairs={{0,8},{8,0},{1,9},{9,1},{2,10},{10,2},{3,11},{11,3},{4,12},{12,4},... | collective-permute-start | bytes 104 | tf_op jit(solution)/shard_map/ppermute | solution.py:346
  82.7 5.2 %copy-start.10 = (f32[128,512]{1,0:T(8,128)S(1)}, f32[128,512]{1,0:T(8,128)}, u32[]{:S(2)}) copy-start(f32[128,512]{1,0:T(8,128)} %get-tuple-element.90) | copy-start | bytes 786436
  88.8 3.0 %copy-start.1 = (bf16[640,512]{1,0:T(8,128)(2,1)S(1)}, bf16[640,512]{1,0:T(8,128)(2,1)}, u32[]{:S(2)}) copy-start(bf16[640,512]{1,0:T(8,128)(2,1)} %param.9) | copy-start | bytes 1966084

commit v21 on v20

--- a/solution.py
+++ b/solution.py
@@ -458,8 +458,8 @@
     back = lax.all_to_all(terms, "tensor", 0, 0)
     arrived = (exchange(to_inner, 1), other_part(to_part), lax.ppermute(to_both, ("parts", "tensor"), opposite))
     down_zero, up_zero, kept = lax.optimization_barrier((down_zero, up_zero, kept))
-    down_zero, up_zero, cleared = clear(1, (down_zero, up_zero), [ANY, ANY], {0: 0, 1: 1})
-    back, arrived, cleared = lax.optimization_barrier((back, arrived, cleared))
+    down_zero, up_zero, _ = clear(1, (down_zero, up_zero), [ANY, ANY], {0: 0, 1: 1})
+    back, arrived, down_zero, up_zero = lax.optimization_barrier((back, arrived, down_zero, up_zero))
     back_core = other_core(back)
 
     grad_down, grad_up = pl.pallas_call(

time: 92.3 us -> 91 us (0.986)
  waiting for transfers between devices: 19.2 us -> 14.3 us
  starting transfers between devices: 33.8 us -> 35.9 us
  local copies, waits for them, and re-layouts: 4.49 us -> 6.01 us
    ppermute x4, waiting for transfers between devices: 4.11 us -> 0.16 us  [exchange(): return lax.ppermute(value, 'tensor', [(t, t ^ s) for t in range(group)])]
    all_to_all x1, starting transfers between devices: 3.55 us -> 6.59 us  [fast_body(): asked = lax.all_to_all(own, 'tensor', 0, 0)]
    ppermute x4, starting transfers between devices: 10.5 us -> 7.81 us  [exchange(): return lax.ppermute(value, 'tensor', [(t, t ^ s) for t in range(group)])]
    ppermute x4, waiting for transfers between devices: 2.59 us -> 0.01 us  [other_part(): lax.ppermute(value, 'parts', [(a, parts - 1 - a) for a in range(parts)])]
    ppermute x1, waiting for transfers between devices: 0.01 us -> 1.97 us  [fast_body(): lax.ppermute(to_both, ('parts', 'tensor'), opposite)]
    all_to_all x1, starting transfers between devices: 3.56 us -> 5.39 us  [fast_body(): back = lax.all_to_all(terms, 'tensor', 0, 0)]
    unnamed x34 -> x36, local copies, waits for them, and re-layouts: 3.87 us -> 5.39 us
    all_to_all x1, waiting for transfers between devices: 7.15 us -> 5.74 us  [fast_body(): panels = lax.all_to_all(sent, 'tensor', 0, 0)]
  transfers between devices with their start and end apart: 23 -> 23, of which waited for: 8 -> 9; matrix products, arithmetic and copies ran while one was open for 1% -> 1% of each run, Pallas kernels for 31% -> 31%
where the time goes in v21:
time: 91 us; the launch traced here: 90.7 us
  starting transfers between devices  35.9 us (39%)
  Pallas kernels  31.9 us (35%)
  waiting for transfers between devices  14.3 us (16%)
  local copies, waits for them, and re-layouts  6.01 us (7%)
  between operations  1.61 us (2%)
  other arithmetic  0.91 us (1%)
    pallas_call x2, Pallas kernels, clear(): pl.pallas_call(functools.partial(zero_kernel, half), out_shape=(down_shap...  10.9 us
    ppermute x4, starting transfers between devices, exchange(): return lax.ppermute(value, 'tensor', [(t, t ^ s) for t in range(group)])  7.81 us
    all_to_all x1, starting transfers between devices, fast_body(): asked = lax.all_to_all(own, 'tensor', 0, 0)  6.59 us
    all_to_all x1, waiting for transfers between devices, fast_body(): panels = lax.all_to_all(sent, 'tensor', 0, 0)  5.74 us
    pallas_call x1, Pallas kernels, fast_body(): pl.pallas_call(gather_kernel, out_shape=(pieces, jax.ShapeDtypeStruct((gr...  5.6 us
    all_to_all x1, starting transfers between devices, fast_body(): back = lax.all_to_all(terms, 'tensor', 0, 0)  5.39 us
    unnamed x36, local copies, waits for them, and re-layouts  5.39 us
    pallas_call x1, Pallas kernels, fast_body(): pl.pallas_call(base_kernel, out_shape=sums, in_specs=[ANY] * (7 + len(qua...  5.02 us
  transfers between devices with their start and end apart: 23, of which 9 were waited for; matrix products, arithmetic and copies ran while one was open for 1% of the time, Pallas kernels for 31%

profile of v21, /device:TPU:0, one launch (start us, length us, event | category | flops | bytes accessed | tf_op | source)
XLA Modules:
  0.0 90.7 jit_solution(11079465949079014414)
XLA Ops:
  0.6 0.0 copy-start
  1.4 0.6 broadcast_in_dim.2
  2.0 3.1 %collective-permute-start = (bf16[640,256]{1,0:T(8,128)(2,1)S(1)}, bf16[640,256]{1,0:T(8,128)(2,1)}, u32[]{:S(2)}, u32[]{:S(2)}) collective-permute-start(bf16[640,256]{1,0:T(8,128)(2,1)S(1)} %constant_dynamic-slice_fusion.refs_6_), channel_id=1, source_target_pairs={{0,2},{1,3},{2,0},{3,1},{4,6},{5,7},{6,4},{7,5},{8,10},{9,11},{10,... | collective-permute-start | bytes 983048 | tf_op jit(solution)/shard_map/ppermute | solution.py:343
  5.1 0.7 collective-permute-start.1
  5.8 0.0 copy-start.2
  5.8 1.3 %copy-done.2 = bf16[128,5120]{1,0:T(8,128)(2,1)S(1)} copy-done((bf16[128,5120]{1,0:T(8,128)(2,1)S(1)}, bf16[128,5120]{1,0:T(8,128)(2,1)}, u32[]{:S(2)}) %copy-start.2) | copy-done | bytes 1310744
  7.1 0.1 split_tokens.1
  7.2 1.6 %collective-permute-start.4 = (bf16[4,128,640]{2,1,0:T(8,128)(2,1)S(1)}, bf16[4,128,640]{2,1,0:T(8,128)(2,1)}, u32[]{:S(2)}, u32[]{:S(2)}) collective-permute-start(bf16[4,128,640]{2,1,0:T(8,128)(2,1)S(1)} %get-tuple-element.64.refs_0_), channel_id=1, source_target_pairs={{0,16},{16,0},{1,17},{17,1},{2,18},{18,2},{3,19},{19,3},{4,20},{20... | collective-permute-start | bytes 1966088 | tf_op jit(solution)/shard_map/ppermute | solution.py:349
  8.8 6.6 %all-to-all-start = ((s32[8,1,128]{2,1,0:T(1,128)}), s32[8,1,128]{2,1,0:T(1,128)S(1)}, u32[]{:S(2)}, u32[]{:S(2)}) async-start(s32[8,1,128]{2,1,0:T(1,128)} %broadcast_in_dim.2), calls=%async_computation | async-start | bytes 8192 | tf_op jit(solution)/shard_map/all_to_all | solution.py:352
  15.4 2.0 %collective-permute-start.2 = (bf16[2,128,640]{2,1,0:T(8,128)(2,1)S(1)}, bf16[2,128,640]{2,1,0:T(8,128)(2,1)}, u32[]{:S(2)}, u32[]{:S(2)}) collective-permute-start(bf16[2,128,640]{2,1,0:T(8,128)(2,1)S(1)} %get-tuple-element.58), channel_id=1, source_target_pairs={{0,1},{1,0},{2,3},{3,2},{4,5},{5,4},{6,7},{7,6},{8,9},{9,8},{10,11... | collective-permute-start | bytes 983048 | tf_op jit(solution)/shard_map/ppermute | solution.py:343
  17.4 3.9 %pair_columns.1.xs_ref = bf16[8,256,320]{2,1,0:T(8,128)(2,1)} custom-call(bf16[128,5120]{1,0:T(8,128)(2,1)} %x_ref.1), custom_call_target="tpu_custom_call" | custom-call | bytes 134217728 | tf_op jit(solution)/shard_map/pair_columns/pallas_call | solution.py:366
  21.3 0.5 all-to-all-done.asked
  21.8 0.0 collective-permute-done.refs_7_
  21.8 0.0 collective-permute-done.1
  21.8 0.6 collective-permute-start.3
  22.4 1.4 %collective-permute-start.5 = (bf16[640,256]{1,0:T(8,128)(2,1)}, bf16[640,256]{1,0:T(8,128)(2,1)}, u32[]{:S(2)}, u32[]{:S(2)}) collective-permute-start(bf16[640,256]{1,0:T(8,128)(2,1)} %collective-permute-done.refs_7_), channel_id=1, source_target_pairs={{2,4},{3,5},{4,2},{5,3},{10,12},{11,13},{12,10},{13,11},{18,20},{1... | collective-permute-start | bytes 983048 | tf_op jit(solution)/shard_map/ppermute | solution.py:382
  23.8 1.3 %collective-permute-start.6 = (bf16[640,256]{1,0:T(8,128)(2,1)S(1)}, bf16[640,256]{1,0:T(8,128)(2,1)S(1)}, u32[]{:S(2)}, u32[]{:S(2)}) collective-permute-start(bf16[640,256]{1,0:T(8,128)(2,1)S(1)} %collective-permute-done.1), channel_id=1, source_target_pairs={{2,0},{3,1},{4,6},{5,7},{10,8},{11,9},{12,14},{13,15},{18,16},{19,... | collective-permute-start | bytes 983048 | tf_op jit(solution)/shard_map/ppermute | solution.py:383
  25.1 5.6 %pick_panels.1 = (bf16[8,384,128]{2,1,0:T(8,128)(2,1)}, s32[8]{0:T(128)}) custom-call(s32[8,1,128]{2,1,0:T(1,128)} %copy-done.11, s32[256]{0:T(256)} %slot_of.1, bf16[32,320,8,128]{3,2,1,0:T(8,128)(2,1)} %bitcast.19, bf16[32,64,8,128]{3,2,1,0:T(8,128)(2,1)} %bitcast.21), custom_call_target="tpu_custom_call" | custom-call | bytes 41943040 | tf_op jit(solution)/shard_map/pick_panels/pallas_call | solution.py:389
  30.7 0.0 collective-permute-done.2.refs_2_
  30.7 0.2 collective-permute-done.3.refs_3_
  30.9 0.0 collective-permute-done.4.refs_1_
  30.9 0.0 collective-permute-done.5.refs_9_
  30.9 2.6 %collective-permute-done.6 = bf16[640,256]{1,0:T(8,128)(2,1)S(1)} collective-permute-done((bf16[640,256]{1,0:T(8,128)(2,1)S(1)}, bf16[640,256]{1,0:T(8,128)(2,1)S(1)}, u32[]{:S(2)}, u32[]{:S(2)}) %collective-permute-start.6) | collective-permute-done | bytes 327712 | tf_op jit(solution)/shard_map/ppermute | solution.py:383
  33.5 4.6 %all-to-all-start.1 = ((bf16[8,384,128]{2,1,0:T(8,128)(2,1)}), bf16[8,384,128]{2,1,0:T(8,128)(2,1)S(1)}, u32[]{:S(2)}, u32[]{:S(2)}) async-start(bf16[8,384,128]{2,1,0:T(8,128)(2,1)} %get-tuple-element.74), calls=%async_computation.1 | async-start | bytes 1572864 | tf_op jit(solution)/shard_map/all_to_all | solution.py:408
  38.2 0.0 collective-permute-start.7
  38.2 0.5 collective-permute-start.8
  38.7 0.1 collective-permute-start.9
  38.9 1.3 %collective-permute-start.10 = (bf16[640,256]{1,0:T(8,128)(2,1)}, bf16[640,256]{1,0:T(8,128)(2,1)}, u32[]{:S(2)}, u32[]{:S(2)}) collective-permute-start(bf16[640,256]{1,0:T(8,128)(2,1)} %collective-permute-done.5.refs_9_), channel_id=1, source_target_pairs={{2,0},{3,1},{4,6},{5,7},{10,8},{11,9},{12,14},{13,15},{18,16},{19,... | collective-permute-start | bytes 983048 | tf_op jit(solution)/shard_map/ppermute | solution.py:411
  40.1 0.6 collective-permute-start.11
  40.7 0.0 collective-permute-done.7.refs_11_
  40.7 0.7 copy-done.13
  41.4 1.5 %collective-permute-start.12 = (bf16[2,128,640]{2,1,0:T(8,128)(2,1)}, bf16[2,128,640]{2,1,0:T(8,128)(2,1)}, u32[]{:S(2)}, u32[]{:S(2)}) collective-permute-start(bf16[2,128,640]{2,1,0:T(8,128)(2,1)} %copy-done.12), channel_id=1, source_target_pairs={{0,16},{16,0},{1,17},{17,1},{2,18},{18,2},{3,19},{19,3},{4,20},{20... | collective-permute-start | bytes 983048 | tf_op jit(solution)/shard_map/ppermute | solution.py:349
  42.9 0.7 copy-done.4
  43.6 5.7 %clear_rows.2 = (f32[16,320,8,1,128]{4,3,2,1,0:T(1,128)}, f32[16,64,8,1,128]{4,3,2,1,0:T(1,128)}, s32[1]{0:T(128)}) custom-call(s32[8]{0:T(128)S(1)} %copy-done.4), custom_call_target="tpu_custom_call" | custom-call | bytes 14680064 | tf_op jit(solution)/shard_map/clear_rows/pallas_call | solution.py:416
  49.4 0.7 copy-done.14
  50.1 5.7 %all-to-all-done.1.pieces = bf16[8,384,128]{2,1,0:T(8,128)(2,1)S(1)} async-done(((bf16[8,384,128]{2,1,0:T(8,128)(2,1)}), bf16[8,384,128]{2,1,0:T(8,128)(2,1)S(1)}, u32[]{:S(2)}, u32[]{:S(2)}) %all-to-all-start.1) | async-done | bytes 786464 | tf_op jit(solution)/shard_map/all_to_all | solution.py:408
  55.8 0.0 copy-start.7
  55.8 0.9 %copy-done.7 = bf16[128,1024]{1,0:T(8,128)(2,1)S(1)} copy-done((bf16[128,1024]{1,0:T(8,128)(2,1)S(1)}, bf16[128,1024]{1,0:T(8,128)(2,1)}, u32[]{:S(2)}) %copy-start.7) | copy-done | bytes 262168
  56.8 3.0 %adapter.1 = (bf16[8,384,128]{2,1,0:T(8,128)(2,1)}, f32[128,1024]{1,0:T(8,128)S(1)}) custom-call(bf16[8,256,320]{2,1,0:T(8,128)(2,1)S(1)} %copy-done.3, bf16[128,1024]{1,0:T(8,128)(2,1)S(1)} %copy-done.7, bf16[8,384,128]{2,1,0:T(8,128)(2,1)S(1)} %all-to-all-done.1.pieces, s32[1]{0:T(128)} %get-tuple-element.80._), custom_call_target="tpu_custom_call" | custom-call | flops 3221225472 | bytes 8388608 | tf_op jit(solution)/shard_map/adapter/pallas_call | solution.py:429
  59.8 0.0 collective-permute-done.10.refs_10_
  59.8 0.0 collective-permute-done.11.refs_4_
  59.8 0.0 collective-permute-done.12.refs_5_
  59.8 5.4 %all-to-all-start.2 = ((bf16[8,384,128]{2,1,0:T(8,128)(2,1)}), bf16[8,384,128]{2,1,0:T(8,128)(2,1)S(1)}, u32[]{:S(2)}, u32[]{:S(2)}) async-start(bf16[8,384,128]{2,1,0:T(8,128)(2,1)} %get-tuple-element.90.refs_16_), calls=%async_computation.2 | async-start | bytes 1572864 | tf_op jit(solution)/shard_map/all_to_all | solution.py:458
  65.2 0.0 collective-permute-start.13
  65.2 0.5 collective-permute-start.14
  65.7 1.3 %collective-permute-done.13.refs_14_ = bf16[640,256]{1,0:T(8,128)(2,1)S(1)} collective-permute-done((bf16[640,256]{1,0:T(8,128)(2,1)}, bf16[640,256]{1,0:T(8,128)(2,1)S(1)}, u32[]{:S(2)}, u32[]{:S(2)}) %collective-permute-start.13) | collective-permute-done | bytes 327712 | tf_op jit(solution)/shard_map/ppermute | solution.py:346
  67.0 0.5 collective-permute-done.14.refs_15_
  67.5 0.2 copy-done.16
  67.7 0.7 copy-done.17
  68.5 5.0 %frozen_part.1 = (f32[128,512]{1,0:T(8,128)}, bf16[128,512]{1,0:T(8,128)(2,1)}, bf16[128,512]{1,0:T(8,128)(2,1)}, bf16[128,512]{1,0:T(8,128)(2,1)}) custom-call(bf16[4,128,640]{2,1,0:T(8,128)(2,1)} %copy-done.6, bf16[4,128,640]{2,1,0:T(8,128)(2,1)} %collective-permute-done.4.refs_1_, bf16[2,128,640]{2,1,0:T(8,128)(2,1)} %collective-permute-done.2.refs_2_, ...), custom_call_target="tpu_custom_call" | custom-call | flops 4294967296 | bytes 8388608 | tf_op jit(solution)/shard_map/frozen_part/pallas_call | solution.py:443
  73.5 2.1 %collective-permute-start.15 = (bf16[128,512]{1,0:T(8,128)(2,1)}, bf16[128,512]{1,0:T(8,128)(2,1)S(1)}, u32[]{:S(2)}, u32[]{:S(2)}) collective-permute-start(bf16[128,512]{1,0:T(8,128)(2,1)} %get-tuple-element.93), channel_id=1, source_target_pairs={{0,1},{1,0},{2,3},{3,2},{4,5},{5,4},{6,7},{7,6},{8,9},{9,8},{10,11... | collective-permute-start | bytes 393224 | tf_op jit(solution)/shard_map/ppermute | solution.py:343
  75.6 0.5 collective-permute-start.16
  76.1 1.0 %collective-permute-start.17 = (bf16[128,512]{1,0:T(8,128)(2,1)}, bf16[128,512]{1,0:T(8,128)(2,1)S(1)}, u32[]{:S(2)}, u32[]{:S(2)}) collective-permute-start(bf16[128,512]{1,0:T(8,128)(2,1)} %get-tuple-element.95), channel_id=1, source_target_pairs={{0,17},{1,16},{2,19},{3,18},{4,21},{5,20},{6,23},{7,22},{16,1},{17... | collective-permute-start | bytes 393224 | tf_op jit(solution)/shard_map/ppermute | solution.py:459
  77.1 5.2 %clear_rows.3 = (f32[16,320,8,1,128]{4,3,2,1,0:T(1,128)}, f32[16,64,8,1,128]{4,3,2,1,0:T(1,128)}, s32[1]{0:T(128)}) custom-call(f32[16,320,8,1,128]{4,3,2,1,0:T(1,128)} %get-tuple-element.96.refs_0_, f32[16,64,8,1,128]{4,3,2,1,0:T(1,128)} %get-tuple-element.97.refs_1_), custom_call_target="tpu_custom_call", output_to_operand_aliasing={{0}: (0, {}), {1}: (1, {})} | custom-call | bytes 14680064 | tf_op jit(solution)/shard_map/clear_rows/pallas_call | solution.py:416
  82.3 0.0 collective-permute-done.15
  82.3 2.0 %collective-permute-done.17 = bf16[128,512]{1,0:T(8,128)(2,1)S(1)} collective-permute-done((bf16[128,512]{1,0:T(8,128)(2,1)}, bf16[128,512]{1,0:T(8,128)(2,1)S(1)}, u32[]{:S(2)}, u32[]{:S(2)}) %collective-permute-start.17) | collective-permute-done | bytes 131104 | tf_op jit(solution)/shard_map/ppermute | solution.py:459
  84.3 0.6 all-to-all-done.2.rest_0_
  85.0 0.0 collective-permute-start.19
  85.0 0.5 collective-permute-start.18
  85.5 0.1 convert_add_fusion
  85.6 0.8 fusion
  86.4 0.9 collective-permute-done.18.rows_core
  87.2 0.0 collective-permute-done.19.rest_1_
  87.3 3.5 %place_rows.1 = (f32[16,320,8,1,128]{4,3,2,1,0:T(1,128)}, f32[16,64,8,1,128]{4,3,2,1,0:T(1,128)}) custom-call(s32[8]{0:T(128)S(1)} %copy-done.5, s32[8]{0:T(128)S(1)} %collective-permute-done.18.rows_core, bf16[8,384,128]{2,1,0:T(8,128)(2,1)S(1)} %all-to-all-done.2.rest_0_, ...), custom_call_target="tpu_custom_call", output_to_operand_aliasing={{0}: (4, {}), {1}: (5, {})} | custom-call | bytes 16777216 | tf_op jit(solution)/shard_map/place_rows/pallas_call | solution.py:465
  (32 shorter events, 0.2 us)
Async XLA Ops:
  0.6 1.3 %copy-start = (bf16[640,512]{1,0:T(8,128)(2,1)S(1)}, bf16[640,512]{1,0:T(8,128)(2,1)}, u32[]{:S(2)}) copy-start(bf16[640,512]{1,0:T(8,128)(2,1)} %param.9) | copy-start | bytes 1966084
  2.0 23.1 %copy-start.9 = (bf16[640,256]{1,0:T(8,128)(2,1)}, bf16[640,256]{1,0:T(8,128)(2,1)S(1)}, u32[]{:S(2)}) copy-start(bf16[640,256]{1,0:T(8,128)(2,1)S(1)} %constant_dynamic-slice_fusion.refs_6_) | copy-start | bytes 983044
  2.0 19.8 %collective-permute-start = (bf16[640,256]{1,0:T(8,128)(2,1)S(1)}, bf16[640,256]{1,0:T(8,128)(2,1)}, u32[]{:S(2)}, u32[]{:S(2)}) collective-permute-start(bf16[640,256]{1,0:T(8,128)(2,1)S(1)} %constant_dynamic-slice_fusion.refs_6_), channel_id=1, source_target_pairs={{0,2},{1,3},{2,0},{3,1},{4,6},{5,7},{6,4},{7,5},{8,10},{9,11},{10,... | collective-permute-start | bytes 983048 | tf_op jit(solution)/shard_map/ppermute | solution.py:343
  5.1 16.7 %collective-permute-start.1 = (bf16[640,256]{1,0:T(8,128)(2,1)S(1)}, bf16[640,256]{1,0:T(8,128)(2,1)S(1)}, u32[]{:S(2)}, u32[]{:S(2)}) collective-permute-start(bf16[640,256]{1,0:T(8,128)(2,1)S(1)} %constant_dynamic-slice_fusion.refs_6_), channel_id=1, source_target_pairs={{2,4},{3,5},{4,2},{5,3},{10,12},{11,13},{12,10},{13,11},{18,20},{1... | collective-permute-start | bytes 983048 | tf_op jit(solution)/shard_map/ppermute | solution.py:379
  5.8 1.3 %copy-start.2 = (bf16[128,5120]{1,0:T(8,128)(2,1)S(1)}, bf16[128,5120]{1,0:T(8,128)(2,1)}, u32[]{:S(2)}) copy-start(bf16[128,5120]{1,0:T(8,128)(2,1)} %x_ref.1) | copy-start | bytes 3932164
  7.2 23.5 %copy-start.6 = (bf16[4,128,640]{2,1,0:T(8,128)(2,1)}, bf16[4,128,640]{2,1,0:T(8,128)(2,1)S(1)}, u32[]{:S(2)}) copy-start(bf16[4,128,640]{2,1,0:T(8,128)(2,1)S(1)} %get-tuple-element.64.refs_0_) | copy-start | bytes 1966084
  7.2 23.7 %collective-permute-start.4 = (bf16[4,128,640]{2,1,0:T(8,128)(2,1)S(1)}, bf16[4,128,640]{2,1,0:T(8,128)(2,1)}, u32[]{:S(2)}, u32[]{:S(2)}) collective-permute-start(bf16[4,128,640]{2,1,0:T(8,128)(2,1)S(1)} %get-tuple-element.64.refs_0_), channel_id=1, source_target_pairs={{0,16},{16,0},{1,17},{17,1},{2,18},{18,2},{3,19},{19,3},{4,20},{20... | collective-permute-start | bytes 1966088 | tf_op jit(solution)/shard_map/ppermute | solution.py:349
  8.8 13.0 %all-to-all-start = ((s32[8,1,128]{2,1,0:T(1,128)}), s32[8,1,128]{2,1,0:T(1,128)S(1)}, u32[]{:S(2)}, u32[]{:S(2)}) async-start(s32[8,1,128]{2,1,0:T(1,128)} %broadcast_in_dim.2), calls=%async_computation | async-start | bytes 8192 | tf_op jit(solution)/shard_map/all_to_all | solution.py:352
  15.4 15.4 %collective-permute-start.2 = (bf16[2,128,640]{2,1,0:T(8,128)(2,1)S(1)}, bf16[2,128,640]{2,1,0:T(8,128)(2,1)}, u32[]{:S(2)}, u32[]{:S(2)}) collective-permute-start(bf16[2,128,640]{2,1,0:T(8,128)(2,1)S(1)} %get-tuple-element.58), channel_id=1, source_target_pairs={{0,1},{1,0},{2,3},{3,2},{4,5},{5,4},{6,7},{7,6},{8,9},{9,8},{10,11... | collective-permute-start | bytes 983048 | tf_op jit(solution)/shard_map/ppermute | solution.py:343
  21.8 3.3 %copy-start.11 = (s32[8,1,128]{2,1,0:T(1,128)}, s32[8,1,128]{2,1,0:T(1,128)S(1)}, u32[]{:S(2)}) copy-start(s32[8,1,128]{2,1,0:T(1,128)S(1)} %all-to-all-done.asked) | copy-start | bytes 12292
  21.8 9.1 %collective-permute-start.3 = (bf16[2,128,640]{2,1,0:T(8,128)(2,1)S(1)}, bf16[2,128,640]{2,1,0:T(8,128)(2,1)S(1)}, u32[]{:S(2)}, u32[]{:S(2)}) collective-permute-start(bf16[2,128,640]{2,1,0:T(8,128)(2,1)S(1)} %get-tuple-element.63), channel_id=1, source_target_pairs={{0,1},{1,0},{2,3},{3,2},{4,5},{5,4},{6,7},{7,6},{8,9},{9,8},{10,11... | collective-permute-start | bytes 983048 | tf_op jit(solution)/shard_map/ppermute | solution.py:343
  22.4 8.5 %collective-permute-start.5 = (bf16[640,256]{1,0:T(8,128)(2,1)}, bf16[640,256]{1,0:T(8,128)(2,1)}, u32[]{:S(2)}, u32[]{:S(2)}) collective-permute-start(bf16[640,256]{1,0:T(8,128)(2,1)} %collective-permute-done.refs_7_), channel_id=1, source_target_pairs={{2,4},{3,5},{4,2},{5,3},{10,12},{11,13},{12,10},{13,11},{18,20},{1... | collective-permute-start | bytes 983048 | tf_op jit(solution)/shard_map/ppermute | solution.py:382
  23.8 9.7 %collective-permute-start.6 = (bf16[640,256]{1,0:T(8,128)(2,1)S(1)}, bf16[640,256]{1,0:T(8,128)(2,1)S(1)}, u32[]{:S(2)}, u32[]{:S(2)}) collective-permute-start(bf16[640,256]{1,0:T(8,128)(2,1)S(1)} %collective-permute-done.1), channel_id=1, source_target_pairs={{2,0},{3,1},{4,6},{5,7},{10,8},{11,9},{12,14},{13,15},{18,16},{19,... | collective-permute-start | bytes 983048 | tf_op jit(solution)/shard_map/ppermute | solution.py:383
  25.1 30.7 %copy-start.3 = (bf16[8,256,320]{2,1,0:T(8,128)(2,1)S(1)}, bf16[8,256,320]{2,1,0:T(8,128)(2,1)}, u32[]{:S(2)}) copy-start(bf16[8,256,320]{2,1,0:T(8,128)(2,1)} %pair_columns.1.xs_ref) | copy-start | bytes 3932164
  30.9 2.6 %copy-start.12 = (bf16[2,128,640]{2,1,0:T(8,128)(2,1)}, bf16[2,128,640]{2,1,0:T(8,128)(2,1)S(1)}, u32[]{:S(2)}) copy-start(bf16[2,128,640]{2,1,0:T(8,128)(2,1)S(1)} %collective-permute-done.3.refs_3_) | copy-start | bytes 983044
  33.5 22.3 %all-to-all-start.1 = ((bf16[8,384,128]{2,1,0:T(8,128)(2,1)}), bf16[8,384,128]{2,1,0:T(8,128)(2,1)S(1)}, u32[]{:S(2)}, u32[]{:S(2)}) async-start(bf16[8,384,128]{2,1,0:T(8,128)(2,1)} %get-tuple-element.74), calls=%async_computation.1 | async-start | bytes 1572864 | tf_op jit(solution)/shard_map/all_to_all | solution.py:408
  38.2 2.6 %collective-permute-start.7 = (bf16[640,256]{1,0:T(8,128)(2,1)}, bf16[640,256]{1,0:T(8,128)(2,1)S(1)}, u32[]{:S(2)}, u32[]{:S(2)}) collective-permute-start(bf16[640,256]{1,0:T(8,128)(2,1)} %copy-done.9), channel_id=1, source_target_pairs={{0,8},{8,0},{1,9},{9,1},{2,10},{10,2},{3,11},{11,3},{4,12},{12,4},... | collective-permute-start | bytes 983048 | tf_op jit(solution)/shard_map/ppermute | solution.py:346
  38.2 11.2 %collective-permute-start.8 = (bf16[640,256]{1,0:T(8,128)(2,1)}, bf16[640,256]{1,0:T(8,128)(2,1)S(1)}, u32[]{:S(2)}, u32[]{:S(2)}) collective-permute-start(bf16[640,256]{1,0:T(8,128)(2,1)} %collective-permute-done.refs_7_), channel_id=1, source_target_pairs={{0,8},{8,0},{1,9},{9,1},{2,10},{10,2},{3,11},{11,3},{4,12},{12,4},... | collective-permute-start | bytes 983048 | tf_op jit(solution)/shard_map/ppermute | solution.py:346
  38.7 17.1 %copy-start.8 = (bf16[640,256]{1,0:T(8,128)(2,1)}, bf16[640,256]{1,0:T(8,128)(2,1)S(1)}, u32[]{:S(2)}) copy-start(bf16[640,256]{1,0:T(8,128)(2,1)S(1)} %broadcast_select_fusion.refs_8_) | copy-start | bytes 983044
  38.7 11.4 %collective-permute-start.9 = (bf16[640,256]{1,0:T(8,128)(2,1)S(1)}, bf16[640,256]{1,0:T(8,128)(2,1)S(1)}, u32[]{:S(2)}, u32[]{:S(2)}) collective-permute-start(bf16[640,256]{1,0:T(8,128)(2,1)S(1)} %broadcast_select_fusion.refs_8_), channel_id=1, source_target_pairs={{0,8},{8,0},{1,9},{9,1},{2,10},{10,2},{3,11},{11,3},{4,12},{12,4},... | collective-permute-start | bytes 983048 | tf_op jit(solution)/shard_map/ppermute | solution.py:346
  38.9 20.9 %collective-permute-start.10 = (bf16[640,256]{1,0:T(8,128)(2,1)}, bf16[640,256]{1,0:T(8,128)(2,1)}, u32[]{:S(2)}, u32[]{:S(2)}) collective-permute-start(bf16[640,256]{1,0:T(8,128)(2,1)} %collective-permute-done.5.refs_9_), channel_id=1, source_target_pairs={{2,0},{3,1},{4,6},{5,7},{10,8},{11,9},{12,14},{13,15},{18,16},{19,... | collective-permute-start | bytes 983048 | tf_op jit(solution)/shard_map/ppermute | solution.py:411
  40.1 19.6 %collective-permute-start.11 = (bf16[2,128,640]{2,1,0:T(8,128)(2,1)}, bf16[2,128,640]{2,1,0:T(8,128)(2,1)}, u32[]{:S(2)}, u32[]{:S(2)}) collective-permute-start(bf16[2,128,640]{2,1,0:T(8,128)(2,1)} %collective-permute-done.2.refs_2_), channel_id=1, source_target_pairs={{0,16},{16,0},{1,17},{17,1},{2,18},{18,2},{3,19},{19,3},{4,20},{20... | collective-permute-start | bytes 983048 | tf_op jit(solution)/shard_map/ppermute | solution.py:349
  40.7 0.7 copy-start.13
  41.4 18.4 %collective-permute-start.12 = (bf16[2,128,640]{2,1,0:T(8,128)(2,1)}, bf16[2,128,640]{2,1,0:T(8,128)(2,1)}, u32[]{:S(2)}, u32[]{:S(2)}) collective-permute-start(bf16[2,128,640]{2,1,0:T(8,128)(2,1)} %copy-done.12), channel_id=1, source_target_pairs={{0,16},{16,0},{1,17},{17,1},{2,18},{18,2},{3,19},{19,3},{4,20},{20... | collective-permute-start | bytes 983048 | tf_op jit(solution)/shard_map/ppermute | solution.py:349
  42.9 0.7 copy-start.4
  49.3 0.7 copy-start.14
  50.1 5.7 %copy-start.15 = (bf16[640,256]{1,0:T(8,128)(2,1)}, bf16[640,256]{1,0:T(8,128)(2,1)S(1)}, u32[]{:S(2)}) copy-start(bf16[640,256]{1,0:T(8,128)(2,1)S(1)} %collective-permute-done.9.refs_13_) | copy-start | bytes 983044
  55.8 1.0 %copy-start.7 = (bf16[128,1024]{1,0:T(8,128)(2,1)S(1)}, bf16[128,1024]{1,0:T(8,128)(2,1)}, u32[]{:S(2)}) copy-start(bf16[128,1024]{1,0:T(8,128)(2,1)} %g_ref.1) | copy-start | bytes 786436
  59.8 25.2 %all-to-all-start.2 = ((bf16[8,384,128]{2,1,0:T(8,128)(2,1)}), bf16[8,384,128]{2,1,0:T(8,128)(2,1)S(1)}, u32[]{:S(2)}, u32[]{:S(2)}) async-start(bf16[8,384,128]{2,1,0:T(8,128)(2,1)} %get-tuple-element.90.refs_16_), calls=%async_computation.2 | async-start | bytes 1572864 | tf_op jit(solution)/shard_map/all_to_all | solution.py:458
  65.2 1.8 %collective-permute-start.13 = (bf16[640,256]{1,0:T(8,128)(2,1)}, bf16[640,256]{1,0:T(8,128)(2,1)S(1)}, u32[]{:S(2)}, u32[]{:S(2)}) collective-permute-start(bf16[640,256]{1,0:T(8,128)(2,1)} %collective-permute-done.5.refs_9_), channel_id=1, source_target_pairs={{0,8},{8,0},{1,9},{9,1},{2,10},{10,2},{3,11},{11,3},{4,12},{12,4},... | collective-permute-start | bytes 983048 | tf_op jit(solution)/shard_map/ppermute | solution.py:346
  65.2 2.3 %collective-permute-start.14 = (bf16[640,256]{1,0:T(8,128)(2,1)}, bf16[640,256]{1,0:T(8,128)(2,1)S(1)}, u32[]{:S(2)}, u32[]{:S(2)}) collective-permute-start(bf16[640,256]{1,0:T(8,128)(2,1)} %collective-permute-done.10.refs_10_), channel_id=1, source_target_pairs={{0,8},{8,0},{1,9},{9,1},{2,10},{10,2},{3,11},{11,3},{4,12},{12,4},... | collective-permute-start | bytes 983048 | tf_op jit(solution)/shard_map/ppermute | solution.py:346
  67.0 0.7 copy-start.16
  67.7 0.7 copy-start.17
  73.5 8.8 %collective-permute-start.15 = (bf16[128,512]{1,0:T(8,128)(2,1)}, bf16[128,512]{1,0:T(8,128)(2,1)S(1)}, u32[]{:S(2)}, u32[]{:S(2)}) collective-permute-start(bf16[128,512]{1,0:T(8,128)(2,1)} %get-tuple-element.93), channel_id=1, source_target_pairs={{0,1},{1,0},{2,3},{3,2},{4,5},{5,4},{6,7},{7,6},{8,9},{9,8},{10,11... | collective-permute-start | bytes 393224 | tf_op jit(solution)/shard_map/ppermute | solution.py:343
  75.6 6.7 %collective-permute-start.16 = (bf16[128,512]{1,0:T(8,128)(2,1)}, bf16[128,512]{1,0:T(8,128)(2,1)S(1)}, u32[]{:S(2)}, u32[]{:S(2)}) collective-permute-start(bf16[128,512]{1,0:T(8,128)(2,1)} %get-tuple-element.94), channel_id=1, source_target_pairs={{0,16},{16,0},{1,17},{17,1},{2,18},{18,2},{3,19},{19,3},{4,20},{20... | collective-permute-start | bytes 393224 | tf_op jit(solution)/shard_map/ppermute | solution.py:349
  76.1 8.2 %collective-permute-start.17 = (bf16[128,512]{1,0:T(8,128)(2,1)}, bf16[128,512]{1,0:T(8,128)(2,1)S(1)}, u32[]{:S(2)}, u32[]{:S(2)}) collective-permute-start(bf16[128,512]{1,0:T(8,128)(2,1)} %get-tuple-element.95), channel_id=1, source_target_pairs={{0,17},{1,16},{2,19},{3,18},{4,21},{5,20},{6,23},{7,22},{16,1},{17... | collective-permute-start | bytes 393224 | tf_op jit(solution)/shard_map/ppermute | solution.py:459
  77.1 7.8 %copy-start.5 = (s32[8]{0:T(128)S(1)}, s32[8]{0:T(128)}, u32[]{:S(2)}) copy-start(s32[8]{0:T(128)} %get-tuple-element.67.refs_0_.rows_here) | copy-start | bytes 100
  77.1 8.3 %copy-start.10 = (f32[128,512]{1,0:T(8,128)S(1)}, f32[128,512]{1,0:T(8,128)}, u32[]{:S(2)}) copy-start(f32[128,512]{1,0:T(8,128)} %get-tuple-element.92) | copy-start | bytes 786436
  85.0 2.3 %collective-permute-start.19 = (bf16[8,384,128]{2,1,0:T(8,128)(2,1)S(1)}, bf16[8,384,128]{2,1,0:T(8,128)(2,1)S(1)}, u32[]{:S(2)}, u32[]{:S(2)}) collective-permute-start(bf16[8,384,128]{2,1,0:T(8,128)(2,1)S(1)} %all-to-all-done.2.rest_0_), channel_id=1, source_target_pairs={{0,8},{8,0},{1,9},{9,1},{2,10},{10,2},{3,11},{11,3},{4,12},{12,4},... | collective-permute-start | bytes 2359304 | tf_op jit(solution)/shard_map/ppermute | solution.py:346
  85.0 2.3 %collective-permute-start.18 = (s32[8]{0:T(128)S(1)}, s32[8]{0:T(128)S(1)}, u32[]{:S(2)}, u32[]{:S(2)}) collective-permute-start(s32[8]{0:T(128)S(1)} %copy-done.5), channel_id=1, source_target_pairs={{0,8},{8,0},{1,9},{9,1},{2,10},{10,2},{3,11},{11,3},{4,12},{12,4},... | collective-permute-start | bytes 104 | tf_op jit(solution)/shard_map/ppermute | solution.py:346
  87.3 3.5 %copy-start.1 = (bf16[640,512]{1,0:T(8,128)(2,1)S(1)}, bf16[640,512]{1,0:T(8,128)(2,1)}, u32[]{:S(2)}) copy-start(bf16[640,512]{1,0:T(8,128)(2,1)} %param.9) | copy-start | bytes 1966084

commit v22 on v21

--- a/solution.py
+++ b/solution.py
@@ -402,11 +402,11 @@
         cost_estimate=cost(read=40 << 20),
         name="pick_panels",
     )(asked, adapter_slot, tiles(down_store), tiles(up_store))
-    sent, rows, x_far, y_mine, half, near, over, over_near, passed = lax.optimization_barrier(
-        (sent, rows, x_far, y_mine, half, near, over, over_near, passed)
+    rows_core = other_core(rows)
+    sent, rows, rows_core, x_far, y_mine, half, near, over, over_near, passed = lax.optimization_barrier(
+        (sent, rows, rows_core, x_far, y_mine, half, near, over, over_near, passed)
     )
     panels = lax.all_to_all(sent, "tensor", 0, 0)
-    rows_core = other_core(rows)
     y_far = [other_part(piece) for piece in x_far]
     passed_near = lax.ppermute(over_near, "tensor", ends)
     owned_groups = ADAPTERS // lax.axis_size("dp") // 8

time: 91 us -> 93 us (1.022)
  waiting for transfers between devices: 14.3 us -> 20 us
  starting transfers between devices: 35.9 us -> 34.2 us
  local copies, waits for them, and re-layouts: 6.01 us -> 4.48 us
    all_to_all x1, waiting for transfers between devices: 5.74 us -> 10.3 us  [fast_body(): panels = lax.all_to_all(sent, 'tensor', 0, 0)]
    all_to_all x1, starting transfers between devices: 6.59 us -> 3.55 us  [fast_body(): asked = lax.all_to_all(own, 'tensor', 0, 0)]
    ppermute x4, starting transfers between devices: 7.81 us -> 10.6 us  [exchange(): return lax.ppermute(value, 'tensor', [(t, t ^ s) for t in range(group)])]
    ppermute x7, waiting for transfers between devices: 2.69 us -> 4.49 us  [other_core(): return lax.ppermute(value, 'dp', [(0, 1), (1, 0)])]
    all_to_all x1, starting transfers between devices: 5.39 us -> 3.66 us  [fast_body(): back = lax.all_to_all(terms, 'tensor', 0, 0)]
    unnamed x36 -> x34, local copies, waits for them, and re-layouts: 5.39 us -> 3.87 us
    ppermute x1, waiting for transfers between devices: 2.61 us -> 1.57 us  [fast_body(): passed = lax.ppermute(over, 'tensor', ends)]
where the time goes in v22:
time: 93 us; the launch traced here: 92.6 us
  starting transfers between devices  34.2 us (37%)
  Pallas kernels  31.4 us (34%)
  waiting for transfers between devices  20 us (22%)
  local copies, waits for them, and re-layouts  4.48 us (5%)
  between operations  1.64 us (2%)
  other arithmetic  0.93 us (1%)
    pallas_call x2, Pallas kernels, clear(): pl.pallas_call(functools.partial(zero_kernel, half), out_shape=(down_shap...  10.9 us
    ppermute x4, starting transfers between devices, exchange(): return lax.ppermute(value, 'tensor', [(t, t ^ s) for t in range(group)])  10.6 us
    all_to_all x1, waiting for transfers between devices, fast_body(): panels = lax.all_to_all(sent, 'tensor', 0, 0)  10.3 us
    pallas_call x1, Pallas kernels, fast_body(): pl.pallas_call(gather_kernel, out_shape=(pieces, jax.ShapeDtypeStruct((gr...  5.39 us
    all_to_all x1, starting transfers between devices, fast_body(): panels = lax.all_to_all(sent, 'tensor', 0, 0)  5.33 us
    pallas_call x1, Pallas kernels, fast_body(): pl.pallas_call(base_kernel, out_shape=sums, in_specs=[ANY] * (7 + len(qua...  5.01 us
    ppermute x4, starting transfers between devices, other_part(): lax.ppermute(value, 'parts', [(a, parts - 1 - a) for a in range(parts)])  4.7 us
    ppermute x7, waiting for transfers between devices, other_core(): return lax.ppermute(value, 'dp', [(0, 1), (1, 0)])  4.49 us
  transfers between devices with their start and end apart: 23, of which 9 were waited for; matrix products, arithmetic and copies ran while one was open for 1% of the time, Pallas kernels for 31%

profile of v22, /device:TPU:0, one launch (start us, length us, event | category | flops | bytes accessed | tf_op | source)
XLA Modules:
  0.0 92.6 jit_solution(9034755993230709016)
XLA Ops:
  0.6 0.0 copy-start
  1.4 0.6 broadcast_in_dim.2
  2.0 0.0 copy-start.9
  2.0 0.7 collective-permute-start.1
  2.7 5.9 %collective-permute-start = (bf16[640,256]{1,0:T(8,128)(2,1)S(1)}, bf16[640,256]{1,0:T(8,128)(2,1)}, u32[]{:S(2)}, u32[]{:S(2)}) collective-permute-start(bf16[640,256]{1,0:T(8,128)(2,1)S(1)} %constant_dynamic-slice_fusion.refs_6_), channel_id=1, source_target_pairs={{0,2},{1,3},{2,0},{3,1},{4,6},{5,7},{6,4},{7,5},{8,10},{9,11},{10,... | collective-permute-start | bytes 983048 | tf_op jit(solution)/shard_map/ppermute | solution.py:343
  8.6 1.3 %copy-done.2 = bf16[128,5120]{1,0:T(8,128)(2,1)S(1)} copy-done((bf16[128,5120]{1,0:T(8,128)(2,1)S(1)}, bf16[128,5120]{1,0:T(8,128)(2,1)}, u32[]{:S(2)}) %copy-start.2) | copy-done | bytes 1310744
  9.9 0.1 split_tokens.1
  10.0 1.6 %collective-permute-start.5 = (bf16[4,128,640]{2,1,0:T(8,128)(2,1)S(1)}, bf16[4,128,640]{2,1,0:T(8,128)(2,1)}, u32[]{:S(2)}, u32[]{:S(2)}) collective-permute-start(bf16[4,128,640]{2,1,0:T(8,128)(2,1)S(1)} %get-tuple-element.65.refs_0_), channel_id=1, source_target_pairs={{0,16},{16,0},{1,17},{17,1},{2,18},{18,2},{3,19},{19,3},{4,20},{20... | collective-permute-start | bytes 1966088 | tf_op jit(solution)/shard_map/ppermute | solution.py:349
  11.6 3.6 %all-to-all-start = ((s32[8,1,128]{2,1,0:T(1,128)}), s32[8,1,128]{2,1,0:T(1,128)S(1)}, u32[]{:S(2)}, u32[]{:S(2)}) async-start(s32[8,1,128]{2,1,0:T(1,128)} %broadcast_in_dim.2), calls=%async_computation | async-start | bytes 8192 | tf_op jit(solution)/shard_map/all_to_all | solution.py:352
  15.2 2.0 %collective-permute-start.3 = (bf16[2,128,640]{2,1,0:T(8,128)(2,1)S(1)}, bf16[2,128,640]{2,1,0:T(8,128)(2,1)}, u32[]{:S(2)}, u32[]{:S(2)}) collective-permute-start(bf16[2,128,640]{2,1,0:T(8,128)(2,1)S(1)} %get-tuple-element.59), channel_id=1, source_target_pairs={{0,1},{1,0},{2,3},{3,2},{4,5},{5,4},{6,7},{7,6},{8,9},{9,8},{10,11... | collective-permute-start | bytes 983048 | tf_op jit(solution)/shard_map/ppermute | solution.py:343
  17.2 3.9 %pair_columns.1.xs_ref = bf16[8,256,320]{2,1,0:T(8,128)(2,1)} custom-call(bf16[128,5120]{1,0:T(8,128)(2,1)} %x_ref.1), custom_call_target="tpu_custom_call" | custom-call | bytes 134217728 | tf_op jit(solution)/shard_map/pair_columns/pallas_call | solution.py:366
  21.1 0.5 all-to-all-done.asked
  21.5 0.0 collective-permute-done.1
  21.5 0.0 collective-permute-done.refs_7_
  21.6 0.6 collective-permute-start.4
  22.2 1.4 %collective-permute-start.6 = (bf16[640,256]{1,0:T(8,128)(2,1)}, bf16[640,256]{1,0:T(8,128)(2,1)}, u32[]{:S(2)}, u32[]{:S(2)}) collective-permute-start(bf16[640,256]{1,0:T(8,128)(2,1)} %collective-permute-done.refs_7_), channel_id=1, source_target_pairs={{2,4},{3,5},{4,2},{5,3},{10,12},{11,13},{12,10},{13,11},{18,20},{1... | collective-permute-start | bytes 983048 | tf_op jit(solution)/shard_map/ppermute | solution.py:382
  23.6 1.3 %collective-permute-start.7 = (bf16[640,256]{1,0:T(8,128)(2,1)S(1)}, bf16[640,256]{1,0:T(8,128)(2,1)S(1)}, u32[]{:S(2)}, u32[]{:S(2)}) collective-permute-start(bf16[640,256]{1,0:T(8,128)(2,1)S(1)} %collective-permute-done.1), channel_id=1, source_target_pairs={{2,0},{3,1},{4,6},{5,7},{10,8},{11,9},{12,14},{13,15},{18,16},{19,... | collective-permute-start | bytes 983048 | tf_op jit(solution)/shard_map/ppermute | solution.py:383
  24.9 5.4 %pick_panels.1 = (bf16[8,384,128]{2,1,0:T(8,128)(2,1)}, s32[8]{0:T(128)}) custom-call(s32[8,1,128]{2,1,0:T(1,128)} %copy-done.11, s32[256]{0:T(256)} %slot_of.1, bf16[32,320,8,128]{3,2,1,0:T(8,128)(2,1)} %bitcast.19, bf16[32,64,8,128]{3,2,1,0:T(8,128)(2,1)} %bitcast.21), custom_call_target="tpu_custom_call" | custom-call | bytes 41943040 | tf_op jit(solution)/shard_map/pick_panels/pallas_call | solution.py:389
  30.3 0.0 collective-permute-done.3.refs_2_
  30.3 0.1 collective-permute-start.2
  30.4 1.3 %collective-permute-done.2.rows_core = s32[8]{0:T(128)S(1)} collective-permute-done((s32[8]{0:T(128)}, s32[8]{0:T(128)S(1)}, u32[]{:S(2)}, u32[]{:S(2)}) %collective-permute-start.2) | collective-permute-done | bytes 64 | tf_op jit(solution)/shard_map/ppermute | solution.py:346
  31.7 0.0 collective-permute-done.5.refs_1_
  31.7 0.0 collective-permute-done.4.refs_3_
  31.7 0.0 collective-permute-done.6.refs_9_
  31.7 1.6 %collective-permute-done.7 = bf16[640,256]{1,0:T(8,128)(2,1)S(1)} collective-permute-done((bf16[640,256]{1,0:T(8,128)(2,1)S(1)}, bf16[640,256]{1,0:T(8,128)(2,1)S(1)}, u32[]{:S(2)}, u32[]{:S(2)}) %collective-permute-start.7) | collective-permute-done | bytes 327712 | tf_op jit(solution)/shard_map/ppermute | solution.py:383
  33.3 5.3 %all-to-all-start.1 = ((bf16[8,384,128]{2,1,0:T(8,128)(2,1)}), bf16[8,384,128]{2,1,0:T(8,128)(2,1)S(1)}, u32[]{:S(2)}, u32[]{:S(2)}) async-start(bf16[8,384,128]{2,1,0:T(8,128)(2,1)} %get-tuple-element.75), calls=%async_computation.1 | async-start | bytes 1572864 | tf_op jit(solution)/shard_map/all_to_all | solution.py:409
  38.7 0.1 collective-permute-start.10
  38.8 0.5 collective-permute-start.8
  39.3 0.1 collective-permute-start.9
  39.3 1.1 %collective-permute-start.12 = (bf16[2,128,640]{2,1,0:T(8,128)(2,1)}, bf16[2,128,640]{2,1,0:T(8,128)(2,1)}, u32[]{:S(2)}, u32[]{:S(2)}) collective-permute-start(bf16[2,128,640]{2,1,0:T(8,128)(2,1)} %collective-permute-done.3.refs_2_), channel_id=1, source_target_pairs={{0,16},{16,0},{1,17},{17,1},{2,18},{18,2},{3,19},{19,3},{4,20},{20... | collective-permute-start | bytes 983048 | tf_op jit(solution)/shard_map/ppermute | solution.py:349
  40.4 0.9 collective-permute-start.13
  41.4 0.0 collective-permute-done.10.refs_13_
  41.4 1.3 %collective-permute-start.11 = (bf16[640,256]{1,0:T(8,128)(2,1)}, bf16[640,256]{1,0:T(8,128)(2,1)}, u32[]{:S(2)}, u32[]{:S(2)}) collective-permute-start(bf16[640,256]{1,0:T(8,128)(2,1)} %collective-permute-done.6.refs_9_), channel_id=1, source_target_pairs={{2,0},{3,1},{4,6},{5,7},{10,8},{11,9},{12,14},{13,15},{18,16},{19,... | collective-permute-start | bytes 983048 | tf_op jit(solution)/shard_map/ppermute | solution.py:411
  42.7 0.6 copy-done.4
  43.2 5.7 %clear_rows.2 = (f32[16,320,8,1,128]{4,3,2,1,0:T(1,128)}, f32[16,64,8,1,128]{4,3,2,1,0:T(1,128)}, s32[1]{0:T(128)}) custom-call(s32[8]{0:T(128)S(1)} %copy-done.4), custom_call_target="tpu_custom_call" | custom-call | bytes 14680064 | tf_op jit(solution)/shard_map/clear_rows/pallas_call | solution.py:416
  49.0 0.0 collective-permute-done.8.refs_11_
  49.0 0.0 collective-permute-done.9.refs_12_
  49.0 10.3 %all-to-all-done.1.pieces = bf16[8,384,128]{2,1,0:T(8,128)(2,1)S(1)} async-done(((bf16[8,384,128]{2,1,0:T(8,128)(2,1)}), bf16[8,384,128]{2,1,0:T(8,128)(2,1)S(1)}, u32[]{:S(2)}, u32[]{:S(2)}) %all-to-all-start.1) | async-done | bytes 786464 | tf_op jit(solution)/shard_map/all_to_all | solution.py:409
  59.3 0.9 %copy-done.7 = bf16[128,1024]{1,0:T(8,128)(2,1)S(1)} copy-done((bf16[128,1024]{1,0:T(8,128)(2,1)S(1)}, bf16[128,1024]{1,0:T(8,128)(2,1)}, u32[]{:S(2)}) %copy-start.7) | copy-done | bytes 262168
  60.2 3.0 %adapter.1 = (bf16[8,384,128]{2,1,0:T(8,128)(2,1)}, f32[128,1024]{1,0:T(8,128)S(1)}) custom-call(bf16[8,256,320]{2,1,0:T(8,128)(2,1)S(1)} %copy-done.3, bf16[128,1024]{1,0:T(8,128)(2,1)S(1)} %copy-done.7, bf16[8,384,128]{2,1,0:T(8,128)(2,1)S(1)} %all-to-all-done.1.pieces, s32[1]{0:T(128)} %get-tuple-element.81._), custom_call_target="tpu_custom_call" | custom-call | flops 3221225472 | bytes 8388608 | tf_op jit(solution)/shard_map/adapter/pallas_call | solution.py:429
  63.2 0.0 collective-permute-done.12.refs_4_
  63.2 0.0 collective-permute-done.13.refs_5_
  63.2 0.0 collective-permute-done.11.refs_10_
  63.2 3.7 %all-to-all-start.2 = ((bf16[8,384,128]{2,1,0:T(8,128)(2,1)}), bf16[8,384,128]{2,1,0:T(8,128)(2,1)S(1)}, u32[]{:S(2)}, u32[]{:S(2)}) async-start(bf16[8,384,128]{2,1,0:T(8,128)(2,1)} %get-tuple-element.91.refs_16_), calls=%async_computation.2 | async-start | bytes 1572864 | tf_op jit(solution)/shard_map/all_to_all | solution.py:458
  66.9 0.0 collective-permute-start.14
  66.9 0.5 collective-permute-start.15
  67.4 1.3 %collective-permute-done.14.refs_14_ = bf16[640,256]{1,0:T(8,128)(2,1)S(1)} collective-permute-done((bf16[640,256]{1,0:T(8,128)(2,1)}, bf16[640,256]{1,0:T(8,128)(2,1)S(1)}, u32[]{:S(2)}, u32[]{:S(2)}) %collective-permute-start.14) | collective-permute-done | bytes 327712 | tf_op jit(solution)/shard_map/ppermute | solution.py:346
  68.7 0.5 collective-permute-done.15.refs_15_
  69.2 0.2 copy-done.15
  69.5 0.7 copy-done.16
  70.2 5.0 %frozen_part.1 = (f32[128,512]{1,0:T(8,128)}, bf16[128,512]{1,0:T(8,128)(2,1)}, bf16[128,512]{1,0:T(8,128)(2,1)}, bf16[128,512]{1,0:T(8,128)(2,1)}) custom-call(bf16[4,128,640]{2,1,0:T(8,128)(2,1)} %copy-done.6, bf16[4,128,640]{2,1,0:T(8,128)(2,1)} %collective-permute-done.5.refs_1_, bf16[2,128,640]{2,1,0:T(8,128)(2,1)} %collective-permute-done.3.refs_2_, ...), custom_call_target="tpu_custom_call" | custom-call | flops 4294967296 | bytes 8388608 | tf_op jit(solution)/shard_map/frozen_part/pallas_call | solution.py:443
  75.2 2.1 %collective-permute-start.16 = (bf16[128,512]{1,0:T(8,128)(2,1)}, bf16[128,512]{1,0:T(8,128)(2,1)S(1)}, u32[]{:S(2)}, u32[]{:S(2)}) collective-permute-start(bf16[128,512]{1,0:T(8,128)(2,1)} %get-tuple-element.94), channel_id=1, source_target_pairs={{0,1},{1,0},{2,3},{3,2},{4,5},{5,4},{6,7},{7,6},{8,9},{9,8},{10,11... | collective-permute-start | bytes 393224 | tf_op jit(solution)/shard_map/ppermute | solution.py:343
  77.3 1.1 %collective-permute-start.17 = (bf16[128,512]{1,0:T(8,128)(2,1)}, bf16[128,512]{1,0:T(8,128)(2,1)S(1)}, u32[]{:S(2)}, u32[]{:S(2)}) collective-permute-start(bf16[128,512]{1,0:T(8,128)(2,1)} %get-tuple-element.95), channel_id=1, source_target_pairs={{0,16},{16,0},{1,17},{17,1},{2,18},{18,2},{3,19},{19,3},{4,20},{20... | collective-permute-start | bytes 393224 | tf_op jit(solution)/shard_map/ppermute | solution.py:349
  78.4 0.4 collective-permute-start.18
  78.8 5.2 %clear_rows.3 = (f32[16,320,8,1,128]{4,3,2,1,0:T(1,128)}, f32[16,64,8,1,128]{4,3,2,1,0:T(1,128)}, s32[1]{0:T(128)}) custom-call(f32[16,320,8,1,128]{4,3,2,1,0:T(1,128)} %get-tuple-element.97.refs_0_, f32[16,64,8,1,128]{4,3,2,1,0:T(1,128)} %get-tuple-element.98.refs_1_), custom_call_target="tpu_custom_call", output_to_operand_aliasing={{0}: (0, {}), {1}: (1, {})} | custom-call | bytes 14680064 | tf_op jit(solution)/shard_map/clear_rows/pallas_call | solution.py:416
  84.0 0.0 collective-permute-done.16
  84.0 0.0 collective-permute-done.17
  84.0 2.7 %collective-permute-done.18 = bf16[128,512]{1,0:T(8,128)(2,1)S(1)} collective-permute-done((bf16[128,512]{1,0:T(8,128)(2,1)}, bf16[128,512]{1,0:T(8,128)(2,1)S(1)}, u32[]{:S(2)}, u32[]{:S(2)}) %collective-permute-start.18) | collective-permute-done | bytes 131104 | tf_op jit(solution)/shard_map/ppermute | solution.py:459
  86.7 0.5 all-to-all-done.2.rest_0_
  87.2 0.0 collective-permute-start.19
  87.2 0.1 convert_add_fusion
  87.3 0.8 fusion
  88.1 1.4 %collective-permute-done.19.rest_1_ = bf16[8,384,128]{2,1,0:T(8,128)(2,1)S(1)} collective-permute-done((bf16[8,384,128]{2,1,0:T(8,128)(2,1)S(1)}, bf16[8,384,128]{2,1,0:T(8,128)(2,1)S(1)}, u32[]{:S(2)}, u32[]{:S(2)}) %collective-permute-start.19) | collective-permute-done | bytes 786464 | tf_op jit(solution)/shard_map/ppermute | solution.py:346
  89.5 3.1 %place_rows.1 = (f32[16,320,8,1,128]{4,3,2,1,0:T(1,128)}, f32[16,64,8,1,128]{4,3,2,1,0:T(1,128)}) custom-call(s32[8]{0:T(128)S(1)} %copy-done.5, s32[8]{0:T(128)S(1)} %collective-permute-done.2.rows_core, bf16[8,384,128]{2,1,0:T(8,128)(2,1)S(1)} %all-to-all-done.2.rest_0_, ...), custom_call_target="tpu_custom_call", output_to_operand_aliasing={{0}: (4, {}), {1}: (5, {})} | custom-call | bytes 16777216 | tf_op jit(solution)/shard_map/place_rows/pallas_call | solution.py:465
  (30 shorter events, 0.2 us)
Async XLA Ops:
  0.6 1.3 %copy-start = (bf16[640,512]{1,0:T(8,128)(2,1)S(1)}, bf16[640,512]{1,0:T(8,128)(2,1)}, u32[]{:S(2)}) copy-start(bf16[640,512]{1,0:T(8,128)(2,1)} %param.9) | copy-start | bytes 1966084
  2.0 22.9 %copy-start.9 = (bf16[640,256]{1,0:T(8,128)(2,1)}, bf16[640,256]{1,0:T(8,128)(2,1)S(1)}, u32[]{:S(2)}) copy-start(bf16[640,256]{1,0:T(8,128)(2,1)S(1)} %constant_dynamic-slice_fusion.refs_6_) | copy-start | bytes 983044
  2.0 19.6 %collective-permute-start.1 = (bf16[640,256]{1,0:T(8,128)(2,1)S(1)}, bf16[640,256]{1,0:T(8,128)(2,1)S(1)}, u32[]{:S(2)}, u32[]{:S(2)}) collective-permute-start(bf16[640,256]{1,0:T(8,128)(2,1)S(1)} %constant_dynamic-slice_fusion.refs_6_), channel_id=1, source_target_pairs={{2,4},{3,5},{4,2},{5,3},{10,12},{11,13},{12,10},{13,11},{18,20},{1... | collective-permute-start | bytes 983048 | tf_op jit(solution)/shard_map/ppermute | solution.py:379
  2.7 18.9 %collective-permute-start = (bf16[640,256]{1,0:T(8,128)(2,1)S(1)}, bf16[640,256]{1,0:T(8,128)(2,1)}, u32[]{:S(2)}, u32[]{:S(2)}) collective-permute-start(bf16[640,256]{1,0:T(8,128)(2,1)S(1)} %constant_dynamic-slice_fusion.refs_6_), channel_id=1, source_target_pairs={{0,2},{1,3},{2,0},{3,1},{4,6},{5,7},{6,4},{7,5},{8,10},{9,11},{10,... | collective-permute-start | bytes 983048 | tf_op jit(solution)/shard_map/ppermute | solution.py:343
  8.6 1.3 %copy-start.2 = (bf16[128,5120]{1,0:T(8,128)(2,1)S(1)}, bf16[128,5120]{1,0:T(8,128)(2,1)}, u32[]{:S(2)}) copy-start(bf16[128,5120]{1,0:T(8,128)(2,1)} %x_ref.1) | copy-start | bytes 3932164
  10.0 20.3 %copy-start.6 = (bf16[4,128,640]{2,1,0:T(8,128)(2,1)}, bf16[4,128,640]{2,1,0:T(8,128)(2,1)S(1)}, u32[]{:S(2)}) copy-start(bf16[4,128,640]{2,1,0:T(8,128)(2,1)S(1)} %get-tuple-element.65.refs_0_) | copy-start | bytes 1966084
  10.0 21.7 %collective-permute-start.5 = (bf16[4,128,640]{2,1,0:T(8,128)(2,1)S(1)}, bf16[4,128,640]{2,1,0:T(8,128)(2,1)}, u32[]{:S(2)}, u32[]{:S(2)}) collective-permute-start(bf16[4,128,640]{2,1,0:T(8,128)(2,1)S(1)} %get-tuple-element.65.refs_0_), channel_id=1, source_target_pairs={{0,16},{16,0},{1,17},{17,1},{2,18},{18,2},{3,19},{19,3},{4,20},{20... | collective-permute-start | bytes 1966088 | tf_op jit(solution)/shard_map/ppermute | solution.py:349
  11.6 9.9 %all-to-all-start = ((s32[8,1,128]{2,1,0:T(1,128)}), s32[8,1,128]{2,1,0:T(1,128)S(1)}, u32[]{:S(2)}, u32[]{:S(2)}) async-start(s32[8,1,128]{2,1,0:T(1,128)} %broadcast_in_dim.2), calls=%async_computation | async-start | bytes 8192 | tf_op jit(solution)/shard_map/all_to_all | solution.py:352
  15.2 15.2 %collective-permute-start.3 = (bf16[2,128,640]{2,1,0:T(8,128)(2,1)S(1)}, bf16[2,128,640]{2,1,0:T(8,128)(2,1)}, u32[]{:S(2)}, u32[]{:S(2)}) collective-permute-start(bf16[2,128,640]{2,1,0:T(8,128)(2,1)S(1)} %get-tuple-element.59), channel_id=1, source_target_pairs={{0,1},{1,0},{2,3},{3,2},{4,5},{5,4},{6,7},{7,6},{8,9},{9,8},{10,11... | collective-permute-start | bytes 983048 | tf_op jit(solution)/shard_map/ppermute | solution.py:343
  21.5 3.3 %copy-start.11 = (s32[8,1,128]{2,1,0:T(1,128)}, s32[8,1,128]{2,1,0:T(1,128)S(1)}, u32[]{:S(2)}) copy-start(s32[8,1,128]{2,1,0:T(1,128)S(1)} %all-to-all-done.asked) | copy-start | bytes 12292
  21.6 10.2 %collective-permute-start.4 = (bf16[2,128,640]{2,1,0:T(8,128)(2,1)S(1)}, bf16[2,128,640]{2,1,0:T(8,128)(2,1)S(1)}, u32[]{:S(2)}, u32[]{:S(2)}) collective-permute-start(bf16[2,128,640]{2,1,0:T(8,128)(2,1)S(1)} %get-tuple-element.64), channel_id=1, source_target_pairs={{0,1},{1,0},{2,3},{3,2},{4,5},{5,4},{6,7},{7,6},{8,9},{9,8},{10,11... | collective-permute-start | bytes 983048 | tf_op jit(solution)/shard_map/ppermute | solution.py:343
  22.2 9.6 %collective-permute-start.6 = (bf16[640,256]{1,0:T(8,128)(2,1)}, bf16[640,256]{1,0:T(8,128)(2,1)}, u32[]{:S(2)}, u32[]{:S(2)}) collective-permute-start(bf16[640,256]{1,0:T(8,128)(2,1)} %collective-permute-done.refs_7_), channel_id=1, source_target_pairs={{2,4},{3,5},{4,2},{5,3},{10,12},{11,13},{12,10},{13,11},{18,20},{1... | collective-permute-start | bytes 983048 | tf_op jit(solution)/shard_map/ppermute | solution.py:382
  23.6 9.7 %collective-permute-start.7 = (bf16[640,256]{1,0:T(8,128)(2,1)S(1)}, bf16[640,256]{1,0:T(8,128)(2,1)S(1)}, u32[]{:S(2)}, u32[]{:S(2)}) collective-permute-start(bf16[640,256]{1,0:T(8,128)(2,1)S(1)} %collective-permute-done.1), channel_id=1, source_target_pairs={{2,0},{3,1},{4,6},{5,7},{10,8},{11,9},{12,14},{13,15},{18,16},{19,... | collective-permute-start | bytes 983048 | tf_op jit(solution)/shard_map/ppermute | solution.py:383
  24.9 34.4 %copy-start.3 = (bf16[8,256,320]{2,1,0:T(8,128)(2,1)S(1)}, bf16[8,256,320]{2,1,0:T(8,128)(2,1)}, u32[]{:S(2)}) copy-start(bf16[8,256,320]{2,1,0:T(8,128)(2,1)} %pair_columns.1.xs_ref) | copy-start | bytes 3932164
  30.3 1.4 %collective-permute-start.2 = (s32[8]{0:T(128)}, s32[8]{0:T(128)S(1)}, u32[]{:S(2)}, u32[]{:S(2)}) collective-permute-start(s32[8]{0:T(128)} %get-tuple-element.68.refs_0_.rows_here), channel_id=1, source_target_pairs={{0,8},{8,0},{1,9},{9,1},{2,10},{10,2},{3,11},{11,3},{4,12},{12,4},... | collective-permute-start | bytes 104 | tf_op jit(solution)/shard_map/ppermute | solution.py:346
  31.7 1.6 %copy-start.12 = (bf16[2,128,640]{2,1,0:T(8,128)(2,1)}, bf16[2,128,640]{2,1,0:T(8,128)(2,1)S(1)}, u32[]{:S(2)}) copy-start(bf16[2,128,640]{2,1,0:T(8,128)(2,1)S(1)} %collective-permute-done.4.refs_3_) | copy-start | bytes 983044
  33.3 26.0 %all-to-all-start.1 = ((bf16[8,384,128]{2,1,0:T(8,128)(2,1)}), bf16[8,384,128]{2,1,0:T(8,128)(2,1)S(1)}, u32[]{:S(2)}, u32[]{:S(2)}) async-start(bf16[8,384,128]{2,1,0:T(8,128)(2,1)} %get-tuple-element.75), calls=%async_computation.1 | async-start | bytes 1572864 | tf_op jit(solution)/shard_map/all_to_all | solution.py:409
  38.7 2.7 %copy-start.8 = (bf16[640,256]{1,0:T(8,128)(2,1)}, bf16[640,256]{1,0:T(8,128)(2,1)S(1)}, u32[]{:S(2)}) copy-start(bf16[640,256]{1,0:T(8,128)(2,1)S(1)} %broadcast_select_fusion.refs_8_) | copy-start | bytes 983044
  38.7 2.7 %collective-permute-start.10 = (bf16[640,256]{1,0:T(8,128)(2,1)S(1)}, bf16[640,256]{1,0:T(8,128)(2,1)S(1)}, u32[]{:S(2)}, u32[]{:S(2)}) collective-permute-start(bf16[640,256]{1,0:T(8,128)(2,1)S(1)} %broadcast_select_fusion.refs_8_), channel_id=1, source_target_pairs={{0,8},{8,0},{1,9},{9,1},{2,10},{10,2},{3,11},{11,3},{4,12},{12,4},... | collective-permute-start | bytes 983048 | tf_op jit(solution)/shard_map/ppermute | solution.py:346
  38.8 10.2 %collective-permute-start.8 = (bf16[640,256]{1,0:T(8,128)(2,1)}, bf16[640,256]{1,0:T(8,128)(2,1)S(1)}, u32[]{:S(2)}, u32[]{:S(2)}) collective-permute-start(bf16[640,256]{1,0:T(8,128)(2,1)} %copy-done.9), channel_id=1, source_target_pairs={{0,8},{8,0},{1,9},{9,1},{2,10},{10,2},{3,11},{11,3},{4,12},{12,4},... | collective-permute-start | bytes 983048 | tf_op jit(solution)/shard_map/ppermute | solution.py:346
  39.3 9.7 %collective-permute-start.9 = (bf16[640,256]{1,0:T(8,128)(2,1)}, bf16[640,256]{1,0:T(8,128)(2,1)}, u32[]{:S(2)}, u32[]{:S(2)}) collective-permute-start(bf16[640,256]{1,0:T(8,128)(2,1)} %collective-permute-done.refs_7_), channel_id=1, source_target_pairs={{0,8},{8,0},{1,9},{9,1},{2,10},{10,2},{3,11},{11,3},{4,12},{12,4},... | collective-permute-start | bytes 983048 | tf_op jit(solution)/shard_map/ppermute | solution.py:346
  39.3 23.9 %collective-permute-start.12 = (bf16[2,128,640]{2,1,0:T(8,128)(2,1)}, bf16[2,128,640]{2,1,0:T(8,128)(2,1)}, u32[]{:S(2)}, u32[]{:S(2)}) collective-permute-start(bf16[2,128,640]{2,1,0:T(8,128)(2,1)} %collective-permute-done.3.refs_2_), channel_id=1, source_target_pairs={{0,16},{16,0},{1,17},{17,1},{2,18},{18,2},{3,19},{19,3},{4,20},{20... | collective-permute-start | bytes 983048 | tf_op jit(solution)/shard_map/ppermute | solution.py:349
  40.4 22.8 %collective-permute-start.13 = (bf16[2,128,640]{2,1,0:T(8,128)(2,1)}, bf16[2,128,640]{2,1,0:T(8,128)(2,1)}, u32[]{:S(2)}, u32[]{:S(2)}) collective-permute-start(bf16[2,128,640]{2,1,0:T(8,128)(2,1)} %copy-done.12), channel_id=1, source_target_pairs={{0,16},{16,0},{1,17},{17,1},{2,18},{18,2},{3,19},{19,3},{4,20},{20... | collective-permute-start | bytes 983048 | tf_op jit(solution)/shard_map/ppermute | solution.py:349
  41.4 21.8 %copy-start.13 = (bf16[640,256]{1,0:T(8,128)(2,1)}, bf16[640,256]{1,0:T(8,128)(2,1)S(1)}, u32[]{:S(2)}) copy-start(bf16[640,256]{1,0:T(8,128)(2,1)S(1)} %collective-permute-done.10.refs_13_) | copy-start | bytes 983044
  41.4 21.8 %collective-permute-start.11 = (bf16[640,256]{1,0:T(8,128)(2,1)}, bf16[640,256]{1,0:T(8,128)(2,1)}, u32[]{:S(2)}, u32[]{:S(2)}) collective-permute-start(bf16[640,256]{1,0:T(8,128)(2,1)} %collective-permute-done.6.refs_9_), channel_id=1, source_target_pairs={{2,0},{3,1},{4,6},{5,7},{10,8},{11,9},{12,14},{13,15},{18,16},{19,... | collective-permute-start | bytes 983048 | tf_op jit(solution)/shard_map/ppermute | solution.py:411
  42.7 0.6 copy-start.4
  49.0 10.3 %copy-start.14 = (bf16[640,256]{1,0:T(8,128)(2,1)}, bf16[640,256]{1,0:T(8,128)(2,1)S(1)}, u32[]{:S(2)}) copy-start(bf16[640,256]{1,0:T(8,128)(2,1)S(1)} %collective-permute-done.8.refs_11_) | copy-start | bytes 983044
  59.3 1.0 %copy-start.7 = (bf16[128,1024]{1,0:T(8,128)(2,1)S(1)}, bf16[128,1024]{1,0:T(8,128)(2,1)}, u32[]{:S(2)}) copy-start(bf16[128,1024]{1,0:T(8,128)(2,1)} %g_ref.1) | copy-start | bytes 786436
  63.2 24.0 %all-to-all-start.2 = ((bf16[8,384,128]{2,1,0:T(8,128)(2,1)}), bf16[8,384,128]{2,1,0:T(8,128)(2,1)S(1)}, u32[]{:S(2)}, u32[]{:S(2)}) async-start(bf16[8,384,128]{2,1,0:T(8,128)(2,1)} %get-tuple-element.91.refs_16_), calls=%async_computation.2 | async-start | bytes 1572864 | tf_op jit(solution)/shard_map/all_to_all | solution.py:458
  66.9 1.9 %collective-permute-start.14 = (bf16[640,256]{1,0:T(8,128)(2,1)}, bf16[640,256]{1,0:T(8,128)(2,1)S(1)}, u32[]{:S(2)}, u32[]{:S(2)}) collective-permute-start(bf16[640,256]{1,0:T(8,128)(2,1)} %collective-permute-done.6.refs_9_), channel_id=1, source_target_pairs={{0,8},{8,0},{1,9},{9,1},{2,10},{10,2},{3,11},{11,3},{4,12},{12,4},... | collective-permute-start | bytes 983048 | tf_op jit(solution)/shard_map/ppermute | solution.py:346
  66.9 2.3 %collective-permute-start.15 = (bf16[640,256]{1,0:T(8,128)(2,1)}, bf16[640,256]{1,0:T(8,128)(2,1)S(1)}, u32[]{:S(2)}, u32[]{:S(2)}) collective-permute-start(bf16[640,256]{1,0:T(8,128)(2,1)} %collective-permute-done.11.refs_10_), channel_id=1, source_target_pairs={{0,8},{8,0},{1,9},{9,1},{2,10},{10,2},{3,11},{11,3},{4,12},{12,4},... | collective-permute-start | bytes 983048 | tf_op jit(solution)/shard_map/ppermute | solution.py:346
  68.7 0.7 copy-start.15
  69.5 0.7 copy-start.16
  75.2 8.8 %collective-permute-start.16 = (bf16[128,512]{1,0:T(8,128)(2,1)}, bf16[128,512]{1,0:T(8,128)(2,1)S(1)}, u32[]{:S(2)}, u32[]{:S(2)}) collective-permute-start(bf16[128,512]{1,0:T(8,128)(2,1)} %get-tuple-element.94), channel_id=1, source_target_pairs={{0,1},{1,0},{2,3},{3,2},{4,5},{5,4},{6,7},{7,6},{8,9},{9,8},{10,11... | collective-permute-start | bytes 393224 | tf_op jit(solution)/shard_map/ppermute | solution.py:343
  77.3 6.7 %collective-permute-start.17 = (bf16[128,512]{1,0:T(8,128)(2,1)}, bf16[128,512]{1,0:T(8,128)(2,1)S(1)}, u32[]{:S(2)}, u32[]{:S(2)}) collective-permute-start(bf16[128,512]{1,0:T(8,128)(2,1)} %get-tuple-element.95), channel_id=1, source_target_pairs={{0,16},{16,0},{1,17},{17,1},{2,18},{18,2},{3,19},{19,3},{4,20},{20... | collective-permute-start | bytes 393224 | tf_op jit(solution)/shard_map/ppermute | solution.py:349
  78.4 8.4 %collective-permute-start.18 = (bf16[128,512]{1,0:T(8,128)(2,1)}, bf16[128,512]{1,0:T(8,128)(2,1)S(1)}, u32[]{:S(2)}, u32[]{:S(2)}) collective-permute-start(bf16[128,512]{1,0:T(8,128)(2,1)} %get-tuple-element.96), channel_id=1, source_target_pairs={{0,17},{1,16},{2,19},{3,18},{4,21},{5,20},{6,23},{7,22},{16,1},{17... | collective-permute-start | bytes 393224 | tf_op jit(solution)/shard_map/ppermute | solution.py:459
  78.8 8.4 %copy-start.10 = (f32[128,512]{1,0:T(8,128)S(1)}, f32[128,512]{1,0:T(8,128)}, u32[]{:S(2)}) copy-start(f32[128,512]{1,0:T(8,128)} %get-tuple-element.93) | copy-start | bytes 786436
  78.8 10.7 %copy-start.5 = (s32[8]{0:T(128)S(1)}, s32[8]{0:T(128)}, u32[]{:S(2)}) copy-start(s32[8]{0:T(128)} %get-tuple-element.68.refs_0_.rows_here) | copy-start | bytes 100
  87.2 2.3 %collective-permute-start.19 = (bf16[8,384,128]{2,1,0:T(8,128)(2,1)S(1)}, bf16[8,384,128]{2,1,0:T(8,128)(2,1)S(1)}, u32[]{:S(2)}, u32[]{:S(2)}) collective-permute-start(bf16[8,384,128]{2,1,0:T(8,128)(2,1)S(1)} %all-to-all-done.2.rest_0_), channel_id=1, source_target_pairs={{0,8},{8,0},{1,9},{9,1},{2,10},{10,2},{3,11},{11,3},{4,12},{12,4},... | collective-permute-start | bytes 2359304 | tf_op jit(solution)/shard_map/ppermute | solution.py:346
  89.5 3.1 %copy-start.1 = (bf16[640,512]{1,0:T(8,128)(2,1)S(1)}, bf16[640,512]{1,0:T(8,128)(2,1)}, u32[]{:S(2)}) copy-start(bf16[640,512]{1,0:T(8,128)(2,1)} %param.9) | copy-start | bytes 1966084

commit v23 on v21

--- a/solution.py
+++ b/solution.py
@@ -436,9 +436,10 @@
         cost_estimate=cost(flops=3 << 30, read=8 << 20),
         name="adapter",
     )(xs, cotangent, panels, cleared)
-    terms, over_near, passed_near, y_far = lax.optimization_barrier((terms, over_near, passed_near, y_far))
-    last = [over_near, passed_near]
-    quarters = quarter + last + quarter_core + [other_core(w) for w in last]
+    over_near, cleared = lax.optimization_barrier((over_near, cleared))
+    over_core = other_core(over_near)
+    terms, over_core, passed_near, y_far = lax.optimization_barrier((terms, over_core, passed_near, y_far))
+    quarters = quarter + [over_near, passed_near] + quarter_core + [over_core, other_core(passed_near)]
     sums = [jax.ShapeDtypeStruct((token_rows, parts * width), kind) for kind in (jnp.float32,) + (jnp.bfloat16,) * 3]
     kept, to_part, to_inner, to_both = pl.pallas_call(
         base_kernel,

time: 91 us -> 98 us (1.077); the launches traced: 90.7 us -> 96.5 us
  waiting for transfers between devices: 14.3 us -> 19.9 us
  starting transfers between devices: 35.9 us -> 38.3 us
  Pallas kernels: 31.9 us -> 30.8 us
    ppermute x4, waiting for transfers between devices: 0.01 us -> 4.34 us  [other_part(): lax.ppermute(value, 'parts', [(a, parts - 1 - a) for a in range(parts)])]
    all_to_all x1, starting transfers between devices: 5.39 us -> 7.78 us  [fast_body(): back = lax.all_to_all(terms, 'tensor', 0, 0)]
    pallas_call x1, Pallas kernels: 3.46 us -> 2.44 us  [fast_body(): pl.pallas_call(functools.partial(scatter_kernel, 2 * group, down_chunks,...]
    unnamed x36 -> x34, local copies, waits for them, and re-layouts: 5.39 us -> 4.41 us
  transfers between devices with their start and end apart: 23 -> 23, of which waited for: 9 -> 9; matrix products, arithmetic and copies ran while one was open for 1% -> 1% of each run, Pallas kernels for 31% -> 29%
where the time goes in v23:
time: 98 us; the launch traced here: 96.5 us
  starting transfers between devices  38.3 us (39%)
  Pallas kernels  30.8 us (31%)
  waiting for transfers between devices  19.9 us (20%)
  local copies, waits for them, and re-layouts  5.03 us (5%)
  between operations  1.61 us (2%)
    pallas_call x2, Pallas kernels, clear(): pl.pallas_call(functools.partial(zero_kernel, half), out_shape=(down_shap...  10.9 us
    ppermute x4, starting transfers between devices, exchange(): return lax.ppermute(value, 'tensor', [(t, t ^ s) for t in range(group)])  7.81 us
    all_to_all x1, starting transfers between devices, fast_body(): back = lax.all_to_all(terms, 'tensor', 0, 0)  7.78 us
    all_to_all x1, starting transfers between devices, fast_body(): asked = lax.all_to_all(own, 'tensor', 0, 0)  6.59 us
    all_to_all x1, waiting for transfers between devices, fast_body(): panels = lax.all_to_all(sent, 'tensor', 0, 0)  5.94 us
    pallas_call x1, Pallas kernels, fast_body(): pl.pallas_call(gather_kernel, out_shape=(pieces, jax.ShapeDtypeStruct((gr...  5.53 us
    pallas_call x1, Pallas kernels, fast_body(): pl.pallas_call(base_kernel, out_shape=sums, in_specs=[ANY] * (7 + len(qua...  5.02 us
    all_to_all x1, starting transfers between devices, fast_body(): panels = lax.all_to_all(sent, 'tensor', 0, 0)  4.64 us
  transfers between devices with their start and end apart: 23, of which 9 were waited for; matrix products, arithmetic and copies ran while one was open for 1% of the time, Pallas kernels for 29%

profile of v23, /device:TPU:0, one launch (start us, length us, event | category | flops | bytes accessed | tf_op | source)
XLA Modules:
  0.0 96.5 jit_solution(10380962627195007556)
XLA Ops:
  0.6 0.0 copy-start
  1.4 0.6 broadcast_in_dim.2
  2.0 3.1 %collective-permute-start = (bf16[640,256]{1,0:T(8,128)(2,1)S(1)}, bf16[640,256]{1,0:T(8,128)(2,1)}, u32[]{:S(2)}, u32[]{:S(2)}) collective-permute-start(bf16[640,256]{1,0:T(8,128)(2,1)S(1)} %constant_dynamic-slice_fusion.refs_6_), channel_id=1, source_target_pairs={{0,2},{1,3},{2,0},{3,1},{4,6},{5,7},{6,4},{7,5},{8,10},{9,11},{10,... | collective-permute-start | bytes 983048 | tf_op jit(solution)/shard_map/ppermute | solution.py:343
  5.1 0.7 collective-permute-start.1
  5.8 0.0 copy-start.2
  5.8 1.3 %copy-done.2 = bf16[128,5120]{1,0:T(8,128)(2,1)S(1)} copy-done((bf16[128,5120]{1,0:T(8,128)(2,1)S(1)}, bf16[128,5120]{1,0:T(8,128)(2,1)}, u32[]{:S(2)}) %copy-start.2) | copy-done | bytes 1310744
  7.1 0.1 split_tokens.1
  7.2 1.6 %collective-permute-start.4 = (bf16[4,128,640]{2,1,0:T(8,128)(2,1)S(1)}, bf16[4,128,640]{2,1,0:T(8,128)(2,1)}, u32[]{:S(2)}, u32[]{:S(2)}) collective-permute-start(bf16[4,128,640]{2,1,0:T(8,128)(2,1)S(1)} %get-tuple-element.65.refs_0_), channel_id=1, source_target_pairs={{0,16},{16,0},{1,17},{17,1},{2,18},{18,2},{3,19},{19,3},{4,20},{20... | collective-permute-start | bytes 1966088 | tf_op jit(solution)/shard_map/ppermute | solution.py:349
  8.8 6.6 %all-to-all-start = ((s32[8,1,128]{2,1,0:T(1,128)}), s32[8,1,128]{2,1,0:T(1,128)S(1)}, u32[]{:S(2)}, u32[]{:S(2)}) async-start(s32[8,1,128]{2,1,0:T(1,128)} %broadcast_in_dim.2), calls=%async_computation | async-start | bytes 8192 | tf_op jit(solution)/shard_map/all_to_all | solution.py:352
  15.4 2.0 %collective-permute-start.2 = (bf16[2,128,640]{2,1,0:T(8,128)(2,1)S(1)}, bf16[2,128,640]{2,1,0:T(8,128)(2,1)}, u32[]{:S(2)}, u32[]{:S(2)}) collective-permute-start(bf16[2,128,640]{2,1,0:T(8,128)(2,1)S(1)} %get-tuple-element.59), channel_id=1, source_target_pairs={{0,1},{1,0},{2,3},{3,2},{4,5},{5,4},{6,7},{7,6},{8,9},{9,8},{10,11... | collective-permute-start | bytes 983048 | tf_op jit(solution)/shard_map/ppermute | solution.py:343
  17.4 3.9 %pair_columns.1.xs_ref = bf16[8,256,320]{2,1,0:T(8,128)(2,1)} custom-call(bf16[128,5120]{1,0:T(8,128)(2,1)} %x_ref.1), custom_call_target="tpu_custom_call" | custom-call | bytes 134217728 | tf_op jit(solution)/shard_map/pair_columns/pallas_call | solution.py:366
  21.3 0.5 all-to-all-done.asked
  21.8 0.0 collective-permute-done.refs_7_
  21.8 0.0 collective-permute-done.1
  21.8 0.6 collective-permute-start.3
  22.4 1.4 %collective-permute-start.5 = (bf16[640,256]{1,0:T(8,128)(2,1)}, bf16[640,256]{1,0:T(8,128)(2,1)}, u32[]{:S(2)}, u32[]{:S(2)}) collective-permute-start(bf16[640,256]{1,0:T(8,128)(2,1)} %collective-permute-done.refs_7_), channel_id=1, source_target_pairs={{2,4},{3,5},{4,2},{5,3},{10,12},{11,13},{12,10},{13,11},{18,20},{1... | collective-permute-start | bytes 983048 | tf_op jit(solution)/shard_map/ppermute | solution.py:382
  23.8 1.3 %collective-permute-start.6 = (bf16[640,256]{1,0:T(8,128)(2,1)S(1)}, bf16[640,256]{1,0:T(8,128)(2,1)S(1)}, u32[]{:S(2)}, u32[]{:S(2)}) collective-permute-start(bf16[640,256]{1,0:T(8,128)(2,1)S(1)} %collective-permute-done.1), channel_id=1, source_target_pairs={{2,0},{3,1},{4,6},{5,7},{10,8},{11,9},{12,14},{13,15},{18,16},{19,... | collective-permute-start | bytes 983048 | tf_op jit(solution)/shard_map/ppermute | solution.py:383
  25.1 5.5 %pick_panels.1 = (bf16[8,384,128]{2,1,0:T(8,128)(2,1)}, s32[8]{0:T(128)}) custom-call(s32[8,1,128]{2,1,0:T(1,128)} %copy-done.11, s32[256]{0:T(256)} %slot_of.1, bf16[32,320,8,128]{3,2,1,0:T(8,128)(2,1)} %bitcast.19, bf16[32,64,8,128]{3,2,1,0:T(8,128)(2,1)} %bitcast.21), custom_call_target="tpu_custom_call" | custom-call | bytes 41943040 | tf_op jit(solution)/shard_map/pick_panels/pallas_call | solution.py:389
  30.7 0.0 collective-permute-done.2.refs_2_
  30.7 0.2 collective-permute-done.3.refs_3_
  30.9 0.0 collective-permute-done.4.refs_1_
  30.9 0.0 collective-permute-done.5.refs_9_
  30.9 2.6 %collective-permute-done.6 = bf16[640,256]{1,0:T(8,128)(2,1)S(1)} collective-permute-done((bf16[640,256]{1,0:T(8,128)(2,1)S(1)}, bf16[640,256]{1,0:T(8,128)(2,1)S(1)}, u32[]{:S(2)}, u32[]{:S(2)}) %collective-permute-start.6) | collective-permute-done | bytes 327712 | tf_op jit(solution)/shard_map/ppermute | solution.py:383
  33.5 4.6 %all-to-all-start.1 = ((bf16[8,384,128]{2,1,0:T(8,128)(2,1)}), bf16[8,384,128]{2,1,0:T(8,128)(2,1)S(1)}, u32[]{:S(2)}, u32[]{:S(2)}) async-start(bf16[8,384,128]{2,1,0:T(8,128)(2,1)} %get-tuple-element.75), calls=%async_computation.1 | async-start | bytes 1572864 | tf_op jit(solution)/shard_map/all_to_all | solution.py:408
  38.2 0.0 collective-permute-start.7
  38.2 0.5 collective-permute-start.8
  38.7 0.1 collective-permute-start.9
  38.9 0.6 copy-done.4
  39.5 5.7 %clear_rows.2 = (f32[16,320,8,1,128]{4,3,2,1,0:T(1,128)}, f32[16,64,8,1,128]{4,3,2,1,0:T(1,128)}, s32[1]{0:T(128)}) custom-call(s32[8]{0:T(128)S(1)} %copy-done.4), custom_call_target="tpu_custom_call" | custom-call | bytes 14680064 | tf_op jit(solution)/shard_map/clear_rows/pallas_call | solution.py:416
  45.2 1.3 %collective-permute-start.11 = (bf16[640,256]{1,0:T(8,128)(2,1)}, bf16[640,256]{1,0:T(8,128)(2,1)}, u32[]{:S(2)}, u32[]{:S(2)}) collective-permute-start(bf16[640,256]{1,0:T(8,128)(2,1)} %collective-permute-done.5.refs_9_), channel_id=1, source_target_pairs={{2,0},{3,1},{4,6},{5,7},{10,8},{11,9},{12,14},{13,15},{18,16},{19,... | collective-permute-start | bytes 983048 | tf_op jit(solution)/shard_map/ppermute | solution.py:411
  46.5 0.5 collective-permute-start.10
  47.0 0.0 collective-permute-done.7.refs_11_
  47.0 0.5 collective-permute-start.12
  47.5 0.0 collective-permute-done.8.refs_12_
  47.5 1.5 %collective-permute-start.13 = (bf16[2,128,640]{2,1,0:T(8,128)(2,1)}, bf16[2,128,640]{2,1,0:T(8,128)(2,1)}, u32[]{:S(2)}, u32[]{:S(2)}) collective-permute-start(bf16[2,128,640]{2,1,0:T(8,128)(2,1)} %copy-done.12), channel_id=1, source_target_pairs={{0,16},{16,0},{1,17},{17,1},{2,18},{18,2},{3,19},{19,3},{4,20},{20... | collective-permute-start | bytes 983048 | tf_op jit(solution)/shard_map/ppermute | solution.py:349
  49.1 0.0 collective-permute-done.9.refs_13_
  49.1 0.8 copy-done.15
  49.8 5.9 %all-to-all-done.1.pieces = bf16[8,384,128]{2,1,0:T(8,128)(2,1)S(1)} async-done(((bf16[8,384,128]{2,1,0:T(8,128)(2,1)}), bf16[8,384,128]{2,1,0:T(8,128)(2,1)S(1)}, u32[]{:S(2)}, u32[]{:S(2)}) %all-to-all-start.1) | async-done | bytes 786464 | tf_op jit(solution)/shard_map/all_to_all | solution.py:408
  55.8 0.9 copy-done.7
  56.7 3.0 %adapter.1 = (bf16[8,384,128]{2,1,0:T(8,128)(2,1)}, f32[128,1024]{1,0:T(8,128)S(1)}) custom-call(bf16[8,256,320]{2,1,0:T(8,128)(2,1)S(1)} %copy-done.3, bf16[128,1024]{1,0:T(8,128)(2,1)S(1)} %copy-done.7, bf16[8,384,128]{2,1,0:T(8,128)(2,1)S(1)} %all-to-all-done.1.pieces, s32[1]{0:T(128)} %get-tuple-element.81._), custom_call_target="tpu_custom_call" | custom-call | flops 3221225472 | bytes 8388608 | tf_op jit(solution)/shard_map/adapter/pallas_call | solution.py:429
  59.7 0.0 collective-permute-done.10.refs_14_
  59.7 0.0 collective-permute-done.11.refs_10_
  59.7 0.0 collective-permute-done.12.refs_4_
  59.7 4.3 %collective-permute-done.13.refs_5_ = bf16[2,128,640]{2,1,0:T(8,128)(2,1)} collective-permute-done((bf16[2,128,640]{2,1,0:T(8,128)(2,1)}, bf16[2,128,640]{2,1,0:T(8,128)(2,1)}, u32[]{:S(2)}, u32[]{:S(2)}) %collective-permute-start.13) | collective-permute-done | bytes 327712 | tf_op jit(solution)/shard_map/ppermute | solution.py:349
  64.1 7.8 %all-to-all-start.2 = ((bf16[8,384,128]{2,1,0:T(8,128)(2,1)}), bf16[8,384,128]{2,1,0:T(8,128)(2,1)S(1)}, u32[]{:S(2)}, u32[]{:S(2)}) async-start(bf16[8,384,128]{2,1,0:T(8,128)(2,1)} %get-tuple-element.92.refs_16_), calls=%async_computation.2 | async-start | bytes 1572864 | tf_op jit(solution)/shard_map/all_to_all | solution.py:459
  71.8 0.0 collective-permute-start.14
  71.9 1.8 %collective-permute-done.14.refs_15_ = bf16[640,256]{1,0:T(8,128)(2,1)S(1)} collective-permute-done((bf16[640,256]{1,0:T(8,128)(2,1)}, bf16[640,256]{1,0:T(8,128)(2,1)S(1)}, u32[]{:S(2)}, u32[]{:S(2)}) %collective-permute-start.14) | collective-permute-done | bytes 327712 | tf_op jit(solution)/shard_map/ppermute | solution.py:346
  73.7 0.7 copy-done.16
  74.4 5.0 %frozen_part.1 = (f32[128,512]{1,0:T(8,128)}, bf16[128,512]{1,0:T(8,128)(2,1)}, bf16[128,512]{1,0:T(8,128)(2,1)}, bf16[128,512]{1,0:T(8,128)(2,1)}) custom-call(bf16[4,128,640]{2,1,0:T(8,128)(2,1)} %copy-done.6, bf16[4,128,640]{2,1,0:T(8,128)(2,1)} %collective-permute-done.4.refs_1_, bf16[2,128,640]{2,1,0:T(8,128)(2,1)} %collective-permute-done.2.refs_2_, ...), custom_call_target="tpu_custom_call" | custom-call | flops 4294967296 | bytes 8388608 | tf_op jit(solution)/shard_map/frozen_part/pallas_call | solution.py:444
  79.4 2.1 %collective-permute-start.15 = (bf16[128,512]{1,0:T(8,128)(2,1)}, bf16[128,512]{1,0:T(8,128)(2,1)S(1)}, u32[]{:S(2)}, u32[]{:S(2)}) collective-permute-start(bf16[128,512]{1,0:T(8,128)(2,1)} %get-tuple-element.95), channel_id=1, source_target_pairs={{0,1},{1,0},{2,3},{3,2},{4,5},{5,4},{6,7},{7,6},{8,9},{9,8},{10,11... | collective-permute-start | bytes 393224 | tf_op jit(solution)/shard_map/ppermute | solution.py:343
  81.5 0.5 collective-permute-start.16
  82.0 1.0 %collective-permute-start.17 = (bf16[128,512]{1,0:T(8,128)(2,1)}, bf16[128,512]{1,0:T(8,128)(2,1)S(1)}, u32[]{:S(2)}, u32[]{:S(2)}) collective-permute-start(bf16[128,512]{1,0:T(8,128)(2,1)} %get-tuple-element.97), channel_id=1, source_target_pairs={{0,17},{1,16},{2,19},{3,18},{4,21},{5,20},{6,23},{7,22},{16,1},{17... | collective-permute-start | bytes 393224 | tf_op jit(solution)/shard_map/ppermute | solution.py:460
  83.1 5.2 %clear_rows.3 = (f32[16,320,8,1,128]{4,3,2,1,0:T(1,128)}, f32[16,64,8,1,128]{4,3,2,1,0:T(1,128)}, s32[1]{0:T(128)}) custom-call(f32[16,320,8,1,128]{4,3,2,1,0:T(1,128)} %get-tuple-element.98.refs_0_, f32[16,64,8,1,128]{4,3,2,1,0:T(1,128)} %get-tuple-element.99.refs_1_), custom_call_target="tpu_custom_call", output_to_operand_aliasing={{0}: (0, {}), {1}: (1, {})} | custom-call | bytes 14680064 | tf_op jit(solution)/shard_map/clear_rows/pallas_call | solution.py:416
  88.2 0.0 collective-permute-done.15
  88.3 0.0 collective-permute-done.16
  88.3 2.1 %collective-permute-done.17 = bf16[128,512]{1,0:T(8,128)(2,1)S(1)} collective-permute-done((bf16[128,512]{1,0:T(8,128)(2,1)}, bf16[128,512]{1,0:T(8,128)(2,1)S(1)}, u32[]{:S(2)}, u32[]{:S(2)}) %collective-permute-start.17) | collective-permute-done | bytes 131104 | tf_op jit(solution)/shard_map/ppermute | solution.py:460
  90.4 1.4 %all-to-all-done.2.rest_0_ = bf16[8,384,128]{2,1,0:T(8,128)(2,1)S(1)} async-done(((bf16[8,384,128]{2,1,0:T(8,128)(2,1)}), bf16[8,384,128]{2,1,0:T(8,128)(2,1)S(1)}, u32[]{:S(2)}, u32[]{:S(2)}) %all-to-all-start.2) | async-done | bytes 786464 | tf_op jit(solution)/shard_map/all_to_all | solution.py:459
  91.8 0.0 collective-permute-start.19
  91.8 0.5 collective-permute-start.18
  92.3 0.1 convert_add_fusion
  92.4 0.8 fusion
  93.2 0.9 collective-permute-done.18.rows_core
  94.0 0.0 collective-permute-done.19.rest_1_
  94.1 2.4 %place_rows.1 = (f32[16,320,8,1,128]{4,3,2,1,0:T(1,128)}, f32[16,64,8,1,128]{4,3,2,1,0:T(1,128)}) custom-call(s32[8]{0:T(128)S(1)} %copy-done.5, s32[8]{0:T(128)S(1)} %collective-permute-done.18.rows_core, bf16[8,384,128]{2,1,0:T(8,128)(2,1)S(1)} %all-to-all-done.2.rest_0_, ...), custom_call_target="tpu_custom_call", output_to_operand_aliasing={{0}: (4, {}), {1}: (5, {})} | custom-call | bytes 16777216 | tf_op jit(solution)/shard_map/place_rows/pallas_call | solution.py:466
  (30 shorter events, 0.2 us)
Async XLA Ops:
  0.6 1.3 %copy-start = (bf16[640,512]{1,0:T(8,128)(2,1)S(1)}, bf16[640,512]{1,0:T(8,128)(2,1)}, u32[]{:S(2)}) copy-start(bf16[640,512]{1,0:T(8,128)(2,1)} %param.9) | copy-start | bytes 1966084
  2.0 23.1 %copy-start.9 = (bf16[640,256]{1,0:T(8,128)(2,1)}, bf16[640,256]{1,0:T(8,128)(2,1)S(1)}, u32[]{:S(2)}) copy-start(bf16[640,256]{1,0:T(8,128)(2,1)S(1)} %constant_dynamic-slice_fusion.refs_6_) | copy-start | bytes 983044
  2.0 19.8 %collective-permute-start = (bf16[640,256]{1,0:T(8,128)(2,1)S(1)}, bf16[640,256]{1,0:T(8,128)(2,1)}, u32[]{:S(2)}, u32[]{:S(2)}) collective-permute-start(bf16[640,256]{1,0:T(8,128)(2,1)S(1)} %constant_dynamic-slice_fusion.refs_6_), channel_id=1, source_target_pairs={{0,2},{1,3},{2,0},{3,1},{4,6},{5,7},{6,4},{7,5},{8,10},{9,11},{10,... | collective-permute-start | bytes 983048 | tf_op jit(solution)/shard_map/ppermute | solution.py:343
  5.1 16.7 %collective-permute-start.1 = (bf16[640,256]{1,0:T(8,128)(2,1)S(1)}, bf16[640,256]{1,0:T(8,128)(2,1)S(1)}, u32[]{:S(2)}, u32[]{:S(2)}) collective-permute-start(bf16[640,256]{1,0:T(8,128)(2,1)S(1)} %constant_dynamic-slice_fusion.refs_6_), channel_id=1, source_target_pairs={{2,4},{3,5},{4,2},{5,3},{10,12},{11,13},{12,10},{13,11},{18,20},{1... | collective-permute-start | bytes 983048 | tf_op jit(solution)/shard_map/ppermute | solution.py:379
  5.8 1.3 %copy-start.2 = (bf16[128,5120]{1,0:T(8,128)(2,1)S(1)}, bf16[128,5120]{1,0:T(8,128)(2,1)}, u32[]{:S(2)}) copy-start(bf16[128,5120]{1,0:T(8,128)(2,1)} %x_ref.1) | copy-start | bytes 3932164
  7.2 23.5 %copy-start.6 = (bf16[4,128,640]{2,1,0:T(8,128)(2,1)}, bf16[4,128,640]{2,1,0:T(8,128)(2,1)S(1)}, u32[]{:S(2)}) copy-start(bf16[4,128,640]{2,1,0:T(8,128)(2,1)S(1)} %get-tuple-element.65.refs_0_) | copy-start | bytes 1966084
  7.2 23.7 %collective-permute-start.4 = (bf16[4,128,640]{2,1,0:T(8,128)(2,1)S(1)}, bf16[4,128,640]{2,1,0:T(8,128)(2,1)}, u32[]{:S(2)}, u32[]{:S(2)}) collective-permute-start(bf16[4,128,640]{2,1,0:T(8,128)(2,1)S(1)} %get-tuple-element.65.refs_0_), channel_id=1, source_target_pairs={{0,16},{16,0},{1,17},{17,1},{2,18},{18,2},{3,19},{19,3},{4,20},{20... | collective-permute-start | bytes 1966088 | tf_op jit(solution)/shard_map/ppermute | solution.py:349
  8.8 13.0 %all-to-all-start = ((s32[8,1,128]{2,1,0:T(1,128)}), s32[8,1,128]{2,1,0:T(1,128)S(1)}, u32[]{:S(2)}, u32[]{:S(2)}) async-start(s32[8,1,128]{2,1,0:T(1,128)} %broadcast_in_dim.2), calls=%async_computation | async-start | bytes 8192 | tf_op jit(solution)/shard_map/all_to_all | solution.py:352
  15.4 15.3 %collective-permute-start.2 = (bf16[2,128,640]{2,1,0:T(8,128)(2,1)S(1)}, bf16[2,128,640]{2,1,0:T(8,128)(2,1)}, u32[]{:S(2)}, u32[]{:S(2)}) collective-permute-start(bf16[2,128,640]{2,1,0:T(8,128)(2,1)S(1)} %get-tuple-element.59), channel_id=1, source_target_pairs={{0,1},{1,0},{2,3},{3,2},{4,5},{5,4},{6,7},{7,6},{8,9},{9,8},{10,11... | collective-permute-start | bytes 983048 | tf_op jit(solution)/shard_map/ppermute | solution.py:343
  21.8 3.3 %copy-start.11 = (s32[8,1,128]{2,1,0:T(1,128)}, s32[8,1,128]{2,1,0:T(1,128)S(1)}, u32[]{:S(2)}) copy-start(s32[8,1,128]{2,1,0:T(1,128)S(1)} %all-to-all-done.asked) | copy-start | bytes 12292
  21.8 9.1 %collective-permute-start.3 = (bf16[2,128,640]{2,1,0:T(8,128)(2,1)S(1)}, bf16[2,128,640]{2,1,0:T(8,128)(2,1)S(1)}, u32[]{:S(2)}, u32[]{:S(2)}) collective-permute-start(bf16[2,128,640]{2,1,0:T(8,128)(2,1)S(1)} %get-tuple-element.64), channel_id=1, source_target_pairs={{0,1},{1,0},{2,3},{3,2},{4,5},{5,4},{6,7},{7,6},{8,9},{9,8},{10,11... | collective-permute-start | bytes 983048 | tf_op jit(solution)/shard_map/ppermute | solution.py:343
  22.4 8.5 %collective-permute-start.5 = (bf16[640,256]{1,0:T(8,128)(2,1)}, bf16[640,256]{1,0:T(8,128)(2,1)}, u32[]{:S(2)}, u32[]{:S(2)}) collective-permute-start(bf16[640,256]{1,0:T(8,128)(2,1)} %collective-permute-done.refs_7_), channel_id=1, source_target_pairs={{2,4},{3,5},{4,2},{5,3},{10,12},{11,13},{12,10},{13,11},{18,20},{1... | collective-permute-start | bytes 983048 | tf_op jit(solution)/shard_map/ppermute | solution.py:382
  23.8 9.7 %collective-permute-start.6 = (bf16[640,256]{1,0:T(8,128)(2,1)S(1)}, bf16[640,256]{1,0:T(8,128)(2,1)S(1)}, u32[]{:S(2)}, u32[]{:S(2)}) collective-permute-start(bf16[640,256]{1,0:T(8,128)(2,1)S(1)} %collective-permute-done.1), channel_id=1, source_target_pairs={{2,0},{3,1},{4,6},{5,7},{10,8},{11,9},{12,14},{13,15},{18,16},{19,... | collective-permute-start | bytes 983048 | tf_op jit(solution)/shard_map/ppermute | solution.py:383
  25.1 30.7 %copy-start.3 = (bf16[8,256,320]{2,1,0:T(8,128)(2,1)S(1)}, bf16[8,256,320]{2,1,0:T(8,128)(2,1)}, u32[]{:S(2)}) copy-start(bf16[8,256,320]{2,1,0:T(8,128)(2,1)} %pair_columns.1.xs_ref) | copy-start | bytes 3932164
  30.9 2.6 %copy-start.12 = (bf16[2,128,640]{2,1,0:T(8,128)(2,1)}, bf16[2,128,640]{2,1,0:T(8,128)(2,1)S(1)}, u32[]{:S(2)}) copy-start(bf16[2,128,640]{2,1,0:T(8,128)(2,1)S(1)} %collective-permute-done.3.refs_3_) | copy-start | bytes 983044
  33.5 22.3 %all-to-all-start.1 = ((bf16[8,384,128]{2,1,0:T(8,128)(2,1)}), bf16[8,384,128]{2,1,0:T(8,128)(2,1)S(1)}, u32[]{:S(2)}, u32[]{:S(2)}) async-start(bf16[8,384,128]{2,1,0:T(8,128)(2,1)} %get-tuple-element.75), calls=%async_computation.1 | async-start | bytes 1572864 | tf_op jit(solution)/shard_map/all_to_all | solution.py:408
  38.2 8.8 %collective-permute-start.7 = (bf16[640,256]{1,0:T(8,128)(2,1)}, bf16[640,256]{1,0:T(8,128)(2,1)S(1)}, u32[]{:S(2)}, u32[]{:S(2)}) collective-permute-start(bf16[640,256]{1,0:T(8,128)(2,1)} %copy-done.9), channel_id=1, source_target_pairs={{0,8},{8,0},{1,9},{9,1},{2,10},{10,2},{3,11},{11,3},{4,12},{12,4},... | collective-permute-start | bytes 983048 | tf_op jit(solution)/shard_map/ppermute | solution.py:346
  38.2 9.4 %collective-permute-start.8 = (bf16[640,256]{1,0:T(8,128)(2,1)}, bf16[640,256]{1,0:T(8,128)(2,1)S(1)}, u32[]{:S(2)}, u32[]{:S(2)}) collective-permute-start(bf16[640,256]{1,0:T(8,128)(2,1)} %collective-permute-done.refs_7_), channel_id=1, source_target_pairs={{0,8},{8,0},{1,9},{9,1},{2,10},{10,2},{3,11},{11,3},{4,12},{12,4},... | collective-permute-start | bytes 983048 | tf_op jit(solution)/shard_map/ppermute | solution.py:346
  38.7 10.3 %copy-start.8 = (bf16[640,256]{1,0:T(8,128)(2,1)}, bf16[640,256]{1,0:T(8,128)(2,1)S(1)}, u32[]{:S(2)}) copy-start(bf16[640,256]{1,0:T(8,128)(2,1)S(1)} %broadcast_select_fusion.refs_8_) | copy-start | bytes 983044
  38.7 10.3 %collective-permute-start.9 = (bf16[640,256]{1,0:T(8,128)(2,1)S(1)}, bf16[640,256]{1,0:T(8,128)(2,1)S(1)}, u32[]{:S(2)}, u32[]{:S(2)}) collective-permute-start(bf16[640,256]{1,0:T(8,128)(2,1)S(1)} %broadcast_select_fusion.refs_8_), channel_id=1, source_target_pairs={{0,8},{8,0},{1,9},{9,1},{2,10},{10,2},{3,11},{11,3},{4,12},{12,4},... | collective-permute-start | bytes 983048 | tf_op jit(solution)/shard_map/ppermute | solution.py:346
  38.9 0.6 copy-start.4
  45.2 14.5 %collective-permute-start.11 = (bf16[640,256]{1,0:T(8,128)(2,1)}, bf16[640,256]{1,0:T(8,128)(2,1)}, u32[]{:S(2)}, u32[]{:S(2)}) collective-permute-start(bf16[640,256]{1,0:T(8,128)(2,1)} %collective-permute-done.5.refs_9_), channel_id=1, source_target_pairs={{2,0},{3,1},{4,6},{5,7},{10,8},{11,9},{12,14},{13,15},{18,16},{19,... | collective-permute-start | bytes 983048 | tf_op jit(solution)/shard_map/ppermute | solution.py:411
  46.5 13.2 %collective-permute-start.10 = (bf16[640,256]{1,0:T(8,128)(2,1)}, bf16[640,256]{1,0:T(8,128)(2,1)}, u32[]{:S(2)}, u32[]{:S(2)}) collective-permute-start(bf16[640,256]{1,0:T(8,128)(2,1)} %collective-permute-done.5.refs_9_), channel_id=1, source_target_pairs={{0,8},{8,0},{1,9},{9,1},{2,10},{10,2},{3,11},{11,3},{4,12},{12,4},... | collective-permute-start | bytes 983048 | tf_op jit(solution)/shard_map/ppermute | solution.py:346
  47.0 2.0 %copy-start.13 = (bf16[640,256]{1,0:T(8,128)(2,1)}, bf16[640,256]{1,0:T(8,128)(2,1)S(1)}, u32[]{:S(2)}) copy-start(bf16[640,256]{1,0:T(8,128)(2,1)S(1)} %collective-permute-done.7.refs_11_) | copy-start | bytes 983044
  47.0 12.7 %collective-permute-start.12 = (bf16[2,128,640]{2,1,0:T(8,128)(2,1)}, bf16[2,128,640]{2,1,0:T(8,128)(2,1)}, u32[]{:S(2)}, u32[]{:S(2)}) collective-permute-start(bf16[2,128,640]{2,1,0:T(8,128)(2,1)} %collective-permute-done.2.refs_2_), channel_id=1, source_target_pairs={{0,16},{16,0},{1,17},{17,1},{2,18},{18,2},{3,19},{19,3},{4,20},{20... | collective-permute-start | bytes 983048 | tf_op jit(solution)/shard_map/ppermute | solution.py:349
  47.5 1.5 %copy-start.14 = (bf16[640,256]{1,0:T(8,128)(2,1)}, bf16[640,256]{1,0:T(8,128)(2,1)S(1)}, u32[]{:S(2)}) copy-start(bf16[640,256]{1,0:T(8,128)(2,1)S(1)} %collective-permute-done.8.refs_12_) | copy-start | bytes 983044
  47.5 16.5 %collective-permute-start.13 = (bf16[2,128,640]{2,1,0:T(8,128)(2,1)}, bf16[2,128,640]{2,1,0:T(8,128)(2,1)}, u32[]{:S(2)}, u32[]{:S(2)}) collective-permute-start(bf16[2,128,640]{2,1,0:T(8,128)(2,1)} %copy-done.12), channel_id=1, source_target_pairs={{0,16},{16,0},{1,17},{17,1},{2,18},{18,2},{3,19},{19,3},{4,20},{20... | collective-permute-start | bytes 983048 | tf_op jit(solution)/shard_map/ppermute | solution.py:349
  49.1 0.8 copy-start.15
  55.8 1.0 copy-start.7
  64.1 27.7 %all-to-all-start.2 = ((bf16[8,384,128]{2,1,0:T(8,128)(2,1)}), bf16[8,384,128]{2,1,0:T(8,128)(2,1)S(1)}, u32[]{:S(2)}, u32[]{:S(2)}) async-start(bf16[8,384,128]{2,1,0:T(8,128)(2,1)} %get-tuple-element.92.refs_16_), calls=%async_computation.2 | async-start | bytes 1572864 | tf_op jit(solution)/shard_map/all_to_all | solution.py:459
  71.8 1.8 %collective-permute-start.14 = (bf16[640,256]{1,0:T(8,128)(2,1)}, bf16[640,256]{1,0:T(8,128)(2,1)S(1)}, u32[]{:S(2)}, u32[]{:S(2)}) collective-permute-start(bf16[640,256]{1,0:T(8,128)(2,1)} %collective-permute-done.11.refs_10_), channel_id=1, source_target_pairs={{0,8},{8,0},{1,9},{9,1},{2,10},{10,2},{3,11},{11,3},{4,12},{12,4},... | collective-permute-start | bytes 983048 | tf_op jit(solution)/shard_map/ppermute | solution.py:346
  73.7 0.7 copy-start.16
  79.4 8.8 %collective-permute-start.15 = (bf16[128,512]{1,0:T(8,128)(2,1)}, bf16[128,512]{1,0:T(8,128)(2,1)S(1)}, u32[]{:S(2)}, u32[]{:S(2)}) collective-permute-start(bf16[128,512]{1,0:T(8,128)(2,1)} %get-tuple-element.95), channel_id=1, source_target_pairs={{0,1},{1,0},{2,3},{3,2},{4,5},{5,4},{6,7},{7,6},{8,9},{9,8},{10,11... | collective-permute-start | bytes 393224 | tf_op jit(solution)/shard_map/ppermute | solution.py:343
  81.5 6.7 %collective-permute-start.16 = (bf16[128,512]{1,0:T(8,128)(2,1)}, bf16[128,512]{1,0:T(8,128)(2,1)S(1)}, u32[]{:S(2)}, u32[]{:S(2)}) collective-permute-start(bf16[128,512]{1,0:T(8,128)(2,1)} %get-tuple-element.96), channel_id=1, source_target_pairs={{0,16},{16,0},{1,17},{17,1},{2,18},{18,2},{3,19},{19,3},{4,20},{20... | collective-permute-start | bytes 393224 | tf_op jit(solution)/shard_map/ppermute | solution.py:349
  82.0 8.4 %collective-permute-start.17 = (bf16[128,512]{1,0:T(8,128)(2,1)}, bf16[128,512]{1,0:T(8,128)(2,1)S(1)}, u32[]{:S(2)}, u32[]{:S(2)}) collective-permute-start(bf16[128,512]{1,0:T(8,128)(2,1)} %get-tuple-element.97), channel_id=1, source_target_pairs={{0,17},{1,16},{2,19},{3,18},{4,21},{5,20},{6,23},{7,22},{16,1},{17... | collective-permute-start | bytes 393224 | tf_op jit(solution)/shard_map/ppermute | solution.py:460
  83.1 8.7 %copy-start.5 = (s32[8]{0:T(128)S(1)}, s32[8]{0:T(128)}, u32[]{:S(2)}) copy-start(s32[8]{0:T(128)} %get-tuple-element.68.refs_0_.rows_here) | copy-start | bytes 100
  83.1 9.2 %copy-start.10 = (f32[128,512]{1,0:T(8,128)S(1)}, f32[128,512]{1,0:T(8,128)}, u32[]{:S(2)}) copy-start(f32[128,512]{1,0:T(8,128)} %get-tuple-element.94) | copy-start | bytes 786436
  91.8 2.3 %collective-permute-start.19 = (bf16[8,384,128]{2,1,0:T(8,128)(2,1)S(1)}, bf16[8,384,128]{2,1,0:T(8,128)(2,1)S(1)}, u32[]{:S(2)}, u32[]{:S(2)}) collective-permute-start(bf16[8,384,128]{2,1,0:T(8,128)(2,1)S(1)} %all-to-all-done.2.rest_0_), channel_id=1, source_target_pairs={{0,8},{8,0},{1,9},{9,1},{2,10},{10,2},{3,11},{11,3},{4,12},{12,4},... | collective-permute-start | bytes 2359304 | tf_op jit(solution)/shard_map/ppermute | solution.py:346
  91.8 2.3 %collective-permute-start.18 = (s32[8]{0:T(128)S(1)}, s32[8]{0:T(128)S(1)}, u32[]{:S(2)}, u32[]{:S(2)}) collective-permute-start(s32[8]{0:T(128)S(1)} %copy-done.5), channel_id=1, source_target_pairs={{0,8},{8,0},{1,9},{9,1},{2,10},{10,2},{3,11},{11,3},{4,12},{12,4},... | collective-permute-start | bytes 104 | tf_op jit(solution)/shard_map/ppermute | solution.py:346
  94.1 2.5 %copy-start.1 = (bf16[640,512]{1,0:T(8,128)(2,1)S(1)}, bf16[640,512]{1,0:T(8,128)(2,1)}, u32[]{:S(2)}) copy-start(bf16[640,512]{1,0:T(8,128)(2,1)} %param.9) | copy-start | bytes 1966084
